TPU v7x, 32 devices: a whole 2x2x4 slice. The times are simulated.
32 devices in a mesh: box: 16 (over z, x, core), face: 2 (over y).
Axes of the slice: x: 2, y: 2, z: 4, core: 2. Of those that a mesh axis runs over, the one named last changes fastest.
Arguments:
- leaf_maps: bfloat16 [2, 1, 16, 3, 512, 1536], P(None, None, 'box', None, 'face'), may hold values from -6 to 6
- w_first: bfloat16 [2, 1, 4096, 512], P(None, None, 'box'), may hold values from -0.01171875 to 0.01171875
- w_second: bfloat16 [2, 1, 2048, 512], P(None, None, 'box'), may hold values from -0.01171875 to 0.01171875
- skel_first: int32 [1, 8, 512], replicated, may hold values from 0 to 1023, as said below
- skel_second: int32 [1, 4, 512], replicated, may hold values from 0 to 1023, as said below
Outputs:
- grand_maps: bfloat16 [2, 1, 8192, 1536], P(None, None, ('box', 'face'))
Inputs may be any that keep to these rules, and one draw needn't show every extreme that they name: `skel_first`: each row holds 512 distinct indices, 0 and 1023 among them. `skel_second`: each row holds 512 distinct indices, 0 and 1023 among them.
All inputs are finite; a program needn't handle non-finite values.
Results may differ from a plain program's by a relative error of at most 0.0075.
Values may be sent and summed in bfloat16 or wider, within the bound.
No kernel may reach another device: no remote copies, remote signals or barrier semaphores. Data moves between devices by JAX's collectives and lax.ppermute only.
A program may use at most 64 MiB of HBM per device.

v0:
```python
import jax
import jax.numpy as jnp
from jax import lax
from jax.sharding import PartitionSpec as P

K = 512


def partner(array, axis, bit):
    return lax.ppermute(array, axis, [(i, i ^ 1 << bit) for i in range(lax.axis_size(axis))])


def complex_dot(left_op, right_op):

    def real_dot(first_op, second_op):
        return jnp.einsum("trk,tkc->trc", first_op, second_op, preferred_element_type=jnp.float32)

    real_part = real_dot(left_op[0], right_op[0]) - real_dot(left_op[1], right_op[1])
    imag_part = real_dot(left_op[0], right_op[1]) + real_dot(left_op[1], right_op[0])
    return jnp.stack([real_part, imag_part])


def skeleton_picker(skeleton):
    side_index = jnp.arange(2 * K, dtype=jnp.int32)
    return (side_index[None, :, None] == skeleton[:, None, :]).astype(jnp.bfloat16)


def select_columns(left_cols, right_cols, picker):
    end_cols = jnp.concatenate([left_cols[:, :, :, :K], right_cols[:, :, :, K : 2 * K]], axis=3)
    side_cols = jnp.concatenate([left_cols[:, :, :, 2 * K :], right_cols[:, :, :, 2 * K :]], axis=3)
    picked = jnp.einsum("ptrs,tsk->ptrk", side_cols, picker, preferred_element_type=jnp.float32)
    return jnp.concatenate([end_cols.astype(jnp.float32), picked], axis=3)


def merge_rows(rows_own, iface_own, iface_other, weight_inv, skeleton, parity):
    picker = skeleton_picker(skeleton)
    coupling = lax.dynamic_slice_in_dim(rows_own, (1 - parity) * K, K, 3)
    hidden = complex_dot(coupling, weight_inv).astype(jnp.bfloat16)
    nothing = jnp.zeros_like(rows_own)
    own_left = jnp.where(parity == 0, rows_own, nothing)
    own_right = jnp.where(parity == 1, rows_own, nothing)
    diagonal = select_columns(own_left, own_right, picker)
    left_iface = jnp.where(parity == 0, iface_own, iface_other)
    right_iface = jnp.where(parity == 0, iface_other, iface_own)
    chosen = select_columns(left_iface, right_iface, picker).astype(jnp.bfloat16)
    product = complex_dot(hidden, lax.all_gather(chosen, "face", axis=2, tiled=True))
    return (diagonal - product).astype(jnp.bfloat16)


def select_rows(candidates, cand_index, skeleton):
    picker = (skeleton[:, :, None] == cand_index[None, None, :]).astype(jnp.bfloat16)
    picked_rows = jnp.einsum(
        "tjr,ptrc->jptc", picker, candidates, preferred_element_type=jnp.float32
    )
    picked = lax.psum_scatter(
        picked_rows.astype(jnp.bfloat16).astype(jnp.bfloat16),
        "face",
        scatter_dimension=0,
        tiled=True,
    ).astype(jnp.float32)
    return jnp.transpose(picked, (1, 2, 0, 3)).astype(jnp.bfloat16)


def on_device(leaf_maps, w_first, w_second, skel_first, skel_second):
    box_index = lax.axis_index("box")
    face_index = lax.axis_index("face")
    face_rows = leaf_maps.shape[4]
    leaf_faces = leaf_maps[:, :, 0]
    parity_one = box_index % 2
    first_face = lax.dynamic_index_in_dim(leaf_faces, 2 * parity_one, 2, keepdims=False)
    second_face = lax.dynamic_index_in_dim(leaf_faces, 2 - parity_one, 2, keepdims=False)
    rows_one = jnp.concatenate([first_face, second_face], axis=2)
    iface_one = lax.dynamic_index_in_dim(leaf_faces, 1 - parity_one, 2, keepdims=False)
    iface_sibling, w_half = partner((iface_one, w_first), "box", 0)
    w_one = jnp.where(
        parity_one == 0,
        jnp.concatenate([w_first, w_half], axis=2),
        jnp.concatenate([w_half, w_first], axis=2),
    )
    skel_one = lax.dynamic_index_in_dim(skel_first, box_index // 2, 1, keepdims=False)
    merged_one = merge_rows(rows_one, iface_one, iface_sibling, w_one, skel_one, parity_one)
    end_rows = jnp.where(
        parity_one == 0, merged_one[:, :, :face_rows], merged_one[:, :, face_rows:]
    )
    side_rows = jnp.where(
        parity_one == 0, merged_one[:, :, face_rows:], merged_one[:, :, :face_rows]
    )
    local_rows = face_index * face_rows + jnp.arange(face_rows, dtype=jnp.int32)
    own_pick = select_rows(side_rows, parity_one * K + local_rows, skel_one)
    end_other, pick_other, w_quarter = partner((end_rows, own_pick, w_second), "box", 0)
    side_parent = (own_pick.astype(jnp.float32) + pick_other.astype(jnp.float32)).astype(
        jnp.bfloat16
    )
    parity_two = box_index // 2 % 2
    quarter_role = box_index % 4
    w_pair = jnp.where(
        parity_one == 0,
        jnp.concatenate([w_second, w_quarter], axis=2),
        jnp.concatenate([w_quarter, w_second], axis=2),
    )
    iface_two = jnp.where(parity_one == 1 - parity_two, end_rows, end_other)
    rows_two = jnp.where((quarter_role == 1) | (quarter_role == 2), side_parent, end_rows)
    iface_cousin, w_cousin = partner((iface_two, w_pair), "box", 1)
    w_two = jnp.where(
        parity_two == 0,
        jnp.concatenate([w_pair, w_cousin], axis=2),
        jnp.concatenate([w_cousin, w_pair], axis=2),
    )
    skel_two = lax.dynamic_index_in_dim(skel_second, box_index // 4, 1, keepdims=False)
    return merge_rows(rows_two, iface_two, iface_cousin, w_two, skel_two, parity_two)


def solution(mesh):
    return jax.shard_map(
        on_device,
        mesh=mesh,
        in_specs=(
            P(None, None, "box", None, "face", None),
            P(None, None, "box", None),
            P(None, None, "box", None),
            P(),
            P(),
        ),
        out_specs=P(None, None, ("box", "face"), None),
        check_vma=False,
    )
```

profile of v0, /device:TPU:1, one launch (start us, length us, event | category | flops | bytes accessed | tf_op | source)
XLA Modules:
  0.0 230.9 jit_solution(466118993856727462)
XLA Ops:
  6.5 3.9 %dynamic-slice_bitcast_fusion = (bf16[2,1,256,1536]{3,2,0,1:T(8,128)(2,1)}, bf16[2,1,256,1536]{3,2,0,1:T(8,128)(2,1)S(1)}, bf16[2,1,256,1536]{3,2,0,1:T(8,128)(2,1)S(1)}) fusion(bf16[2,1,1,3,256,1536]{5,4,3,2,1,0:T(8,128)(2,1)} %param.5, s32[]{:T(128)S(6)} %select_n.207, s32[]{:T(128)S(6)} %select_n.198, s32[]{:T(128)S(6)} %select_n.199), kind=kLoop, calls=%fused_computation.44 | loop fusion | bytes 9437196 | tf_op jit(solution)/shard_map/jit(dynamic_index_in_dim)/squeeze | solution.py:73
  10.5 3.7 %collective-permute-done.1 = bf16[2,1,256,1536]{3,2,0,1:T(8,128)(2,1)} collective-permute-done((bf16[2,1,256,1536]{3,2,0,1:T(8,128)(2,1)}, bf16[2,1,256,1536]{3,2,0,1:T(8,128)(2,1)}, u32[]{:S(2)}, u32[]{:S(2)}) %collective-permute-start.1) | collective-permute-done | bytes 1572896 | tf_op jit(solution)/shard_map/ppermute | solution.py:10
  14.2 2.1 broadcast_select_fusion.6
  16.6 0.9 fusion.45
  17.5 1.2 pad_maximum_fusion.1
  19.1 1.0 broadcast_select_fusion.1
  20.0 0.4 slice_bitcast_fusion.12
  20.5 2.6 %fusion.7 = f32[2,1,512,1024]{3,2,0,1:T(8,128)} fusion(bf16[2,512,512]{2,1,0:T(8,128)(2,1)S(1)} %get-tuple-element.17, bf16[2,512,512]{2,1,0:T(8,128)(2,1)S(1)} %get-tuple-element.34), kind=kLoop, calls=%fused_computation.21 | loop fusion | flops 5242880 | bytes 6291456 | tf_op jit(solution)/shard_map/concatenate | solution.py:32
  23.0 2.8 %fusion.20 = f32[2,1,512,512]{3,2,0,1:T(8,128)} fusion(bf16[2,1,512,512]{3,2,0,1:T(8,128)(2,1)S(1)} %get-tuple-element.18, bf16[2,1,512,512]{3,2,0,1:T(8,128)(2,1)S(1)} %get-tuple-element.33, s32[512]{0:T(512)S(1)} %bitcast.180), kind=kOutput, calls=%fused_computation.33 | convolution fusion | flops 1078460416 | bytes 4196352 | tf_op jit(solution)/shard_map/ptrs,tsk->ptrk/dot_general | solution.py:31
  25.8 1.6 maximum_select_fusion
  27.4 0.4 fusion.69
  27.8 0.4 fusion.68
  28.2 0.4 fusion.43
  28.7 0.4 fusion.44
  29.1 36.8 %all-gather.3.cloned.1.call-done = bf16[2,1,512,1536]{3,2,0,1:T(8,128)(2,1)} async-done(((bf16[2,1,256,1536]{3,2,0,1:T(8,128)(2,1)}), bf16[2,1,512,1536]{3,2,0,1:T(8,128)(2,1)}) %all-gather.3.cloned.1.call-update) | async-done | bytes 3145744 | tf_op jit(solution)/shard_map/all_gather | solution.py:46
  65.9 2.5 %fusion.28 = f32[512,1536]{1,0:T(8,128)S(1)} fusion(bf16[512,512]{1,0:T(8,128)(2,1)S(1)} %fusion.43, bf16[2,1,512,1536]{3,2,0,1:T(8,128)(2,1)} %all-gather.3.cloned.1.call-done), kind=kOutput, calls=%fused_computation.56 | convolution fusion | flops 805306368 | bytes 5242880 | tf_op jit(solution)/shard_map/trk,tkc->trc/dot_general | solution.py:16
  68.5 1.0 fusion.29
  69.4 1.0 fusion.1
  70.4 1.0 fusion.2
  71.4 1.2 copy-done.2
  72.6 0.7 copy-done.8
  73.3 1.0 fusion
  74.3 2.6 %fusion.3 = bf16[512,2,1,1536]{3,0,1,2:T(8,128)(2,1)} fusion(pred[]{:T(512)S(6)} %eq.144, bf16[2,1,512,1536]{3,2,0,1:T(8,128)(2,1)S(1)} %fusion, s32[256]{0:T(256)S(1)} %add_add_fusion, s32[512]{0:T(512)S(1)} %bitcast.181), kind=kOutput, calls=%fused_computation.10 | convolution fusion | flops 807796736 | bytes 6294529 | tf_op jit(solution)/shard_map/tjr,ptrc->jptc/dot_general | solution.py:52
  77.2 43.3 %reduce-scatter.2.cloned.1.call-done = bf16[256,2,1,1536]{3,0,1,2:T(8,128)(2,1)} async-done(((bf16[512,2,1,1536]{3,0,1,2:T(8,128)(2,1)}), bf16[256,2,1,1536]{3,0,1,2:T(8,128)(2,1)}) %reduce-scatter.2.cloned.1.call-update) | async-done | bytes 1572880 | tf_op jit(solution)/shard_map/reduce_scatter | solution.py:55
  120.4 0.7 collective-permute-start.2
  121.1 3.4 %collective-permute-done.2 = bf16[2,1,256,1536]{3,2,0,1:T(8,128)(2,1)} collective-permute-done((bf16[2,1,256,1536]{3,2,0,1:T(8,128)(2,1)}, bf16[2,1,256,1536]{3,2,0,1:T(8,128)(2,1)}, u32[]{:S(2)}, u32[]{:S(2)}) %collective-permute-start.2) | collective-permute-done | bytes 1572896 | tf_op jit(solution)/shard_map/ppermute | solution.py:10
  124.5 4.8 %broadcast_select_fusion.9 = (bf16[2,1,256,1536]{3,2,0,1:T(8,128)(2,1)}, bf16[2,1,256,1536]{3,2,0,1:T(8,128)(2,1)}, bf16[2,1,256,1536]{3,2,0,1:T(8,128)(2,1)}) fusion(pred[]{:T(512)S(6)} %eq.141, bf16[2,1,256,1536]{3,2,0,1:T(8,128)(2,1)} %collective-permute-done.2, bf16[256,2,1,1536]{3,0,1,2:T(8,128)(2,1)} %reduce-scatter.2.cloned.1.call-done, pred[]{:T(512)S(6)} %or.3, ...), kind=kLoop, calls=%fused_computation.55 | loop fusion | flops 5505024 | bytes 11010051 | tf_op jit(solution)/shard_map/jit(_where)/select_n | solution.py:40
  129.7 3.2 %collective-permute-done.5 = bf16[2,1,256,1536]{3,2,0,1:T(8,128)(2,1)S(1)} collective-permute-done((bf16[2,1,256,1536]{3,2,0,1:T(8,128)(2,1)}, bf16[2,1,256,1536]{3,2,0,1:T(8,128)(2,1)S(1)}, u32[]{:S(2)}, u32[]{:S(2)}) %collective-permute-start.5) | collective-permute-done | bytes 1572896 | tf_op jit(solution)/shard_map/ppermute | solution.py:10
  132.9 1.6 broadcast_select_fusion.2
  134.6 1.8 collective-permute-start.3
  136.4 0.7 constant_dynamic-slice_fusion
  137.1 33.6 %collective-permute-done.6 = bf16[2,1,256,1536]{3,2,0,1:T(8,128)(2,1)S(1)} collective-permute-done((bf16[2,1,256,1536]{3,2,0,1:T(8,128)(2,1)S(1)}, bf16[2,1,256,1536]{3,2,0,1:T(8,128)(2,1)S(1)}, u32[]{:S(2)}, u32[]{:S(2)}) %collective-permute-start.6) | collective-permute-done | bytes 1572896 | tf_op jit(solution)/shard_map/ppermute | solution.py:10
  171.2 0.9 fusion.48
  172.1 1.3 pad_maximum_fusion.2
  173.4 1.3 maximum_select_fusion.3
  174.8 1.2 fusion.65
  176.0 11.7 %collective-permute-done.4 = bf16[2,1,256,512]{3,2,1,0:T(8,128)(2,1)S(1)} collective-permute-done((bf16[2,1,256,512]{3,2,1,0:T(8,128)(2,1)S(1)}, bf16[2,1,256,512]{3,2,1,0:T(8,128)(2,1)S(1)}, u32[]{:S(2)}, u32[]{:S(2)}) %collective-permute-start.4) | collective-permute-done | bytes 524320 | tf_op jit(solution)/shard_map/ppermute | solution.py:10
  187.7 0.4 maximum_select_fusion.1
  188.3 1.2 copy-done.7
  189.6 1.6 fusion.56
  191.2 0.8 fusion.34
  193.3 24.3 %all-gather.5.cloned.1.call-done = bf16[2,1,512,1536]{3,2,0,1:T(8,128)(2,1)} async-done(((bf16[2,1,256,1536]{3,2,0,1:T(8,128)(2,1)}), bf16[2,1,512,1536]{3,2,0,1:T(8,128)(2,1)}) %all-gather.5.cloned.1.call-update) | async-done | bytes 3145744 | tf_op jit(solution)/shard_map/all_gather | solution.py:46
  217.6 2.1 fusion.30
  220.0 0.6 fusion.31
  220.5 0.6 fusion.5
  221.2 0.6 fusion.6
  221.7 1.0 copy-done.6
  222.7 1.6 fusion.24
  (47 shorter events, 3.7 us)
Async XLA Ops:
  6.5 4.0 %copy-start = (s32[1,8,512]{2,1,0:T(8,128)S(1)}, s32[1,8,512]{2,1,0:T(8,128)}, u32[]{:S(2)}) copy-start(s32[1,8,512]{2,1,0:T(8,128)} %param.8) | copy-start | bytes 49156
  6.5 59.4 %all-gather.3.cloned.1.call-start = ((), (), s32[]{:S(2)}) async-start(), calls=%async_computation.1 | async-start | bytes 4718592 | tf_op jit(solution)/shard_map/all_gather | solution.py:46
  10.4 3.8 %collective-permute-start.1 = (bf16[2,1,256,1536]{3,2,0,1:T(8,128)(2,1)}, bf16[2,1,256,1536]{3,2,0,1:T(8,128)(2,1)}, u32[]{:S(2)}, u32[]{:S(2)}) collective-permute-start(bf16[2,1,256,1536]{3,2,0,1:T(8,128)(2,1)} %get-tuple-element.8), channel_id=1, source_target_pairs={{0,2},{2,0},{4,6},{6,4},{8,10},{10,8},{12,14},{14,12},{16,18},{18,... | collective-permute-start | bytes 4718600 | tf_op jit(solution)/shard_map/ppermute | solution.py:10
  18.7 101.7 %reduce-scatter.2.cloned.1.call-start = ((), (), s32[]{:S(2)}) async-start(), calls=%async_computation.2 | async-start | bytes 4718592 | tf_op jit(solution)/shard_map/reduce_scatter | solution.py:55
  18.8 7.0 %collective-permute-start = (bf16[2,1,256,512]{3,2,1,0:T(8,128)(2,1)}, bf16[2,1,256,512]{3,2,1,0:T(8,128)(2,1)}, u32[]{:S(2)}, u32[]{:S(2)}) collective-permute-start(bf16[2,1,256,512]{3,2,1,0:T(8,128)(2,1)} %param.6), channel_id=1, source_target_pairs={{0,2},{2,0},{4,6},{6,4},{8,10},{10,8},{12,14},{14,12},{16,18},{18,... | collective-permute-start | bytes 1572872 | tf_op jit(solution)/shard_map/ppermute | solution.py:10
  23.0 2.8 %copy-start.10 = (bf16[2,1,256,512]{3,2,1,0:T(8,128)(2,1)S(1)}, bf16[2,1,256,512]{3,2,1,0:T(8,128)(2,1)}, u32[]{:S(2)}) copy-start(bf16[2,1,256,512]{3,2,1,0:T(8,128)(2,1)} %param.6) | copy-start | bytes 1572868
  65.9 2.5 %copy-start.3 = (bf16[2,1,512,1536]{3,2,0,1:T(8,128)(2,1)S(1)}, bf16[2,1,512,1536]{3,2,0,1:T(8,128)(2,1)}, u32[]{:S(2)}) copy-start(bf16[2,1,512,1536]{3,2,0,1:T(8,128)(2,1)} %all-gather.3.cloned.1.call-done) | copy-start | bytes 9437188
  70.4 2.2 copy-start.2
  70.4 2.9 %copy-start.8 = (f32[2,1,512,512]{3,2,0,1:T(8,128)S(1)}, f32[2,1,512,512]{3,2,0,1:T(8,128)}, u32[]{:S(2)}) copy-start(f32[2,1,512,512]{3,2,0,1:T(8,128)} %fusion.20) | copy-start | bytes 6291460
  76.9 140.7 %all-gather.5.cloned.1.call-start = ((), (), s32[]{:S(2)}) async-start(), calls=%async_computation.3 | async-start | bytes 4718592 | tf_op jit(solution)/shard_map/all_gather | solution.py:46
  120.4 4.1 %collective-permute-start.2 = (bf16[2,1,256,1536]{3,2,0,1:T(8,128)(2,1)}, bf16[2,1,256,1536]{3,2,0,1:T(8,128)(2,1)}, u32[]{:S(2)}, u32[]{:S(2)}) collective-permute-start(bf16[2,1,256,1536]{3,2,0,1:T(8,128)(2,1)} %bitcast.177), channel_id=1, source_target_pairs={{0,2},{2,0},{4,6},{6,4},{8,10},{10,8},{12,14},{14,12},{16,18},{18,... | collective-permute-start | bytes 4718600 | tf_op jit(solution)/shard_map/ppermute | solution.py:10
  129.3 3.6 %collective-permute-start.5 = (bf16[2,1,256,1536]{3,2,0,1:T(8,128)(2,1)}, bf16[2,1,256,1536]{3,2,0,1:T(8,128)(2,1)S(1)}, u32[]{:S(2)}, u32[]{:S(2)}) collective-permute-start(bf16[2,1,256,1536]{3,2,0,1:T(8,128)(2,1)} %get-tuple-element.7), channel_id=1, source_target_pairs={{0,2},{2,0},{4,6},{6,4},{8,10},{10,8},{12,14},{14,12},{16,18},{18,... | collective-permute-start | bytes 4718600 | tf_op jit(solution)/shard_map/ppermute | solution.py:10
  129.7 4.9 %copy-start.9 = (bf16[2,1,128,512]{3,2,1,0:T(8,128)(2,1)S(1)}, bf16[2,1,128,512]{3,2,1,0:T(8,128)(2,1)}, u32[]{:S(2)}) copy-start(bf16[2,1,128,512]{3,2,1,0:T(8,128)(2,1)} %param.7) | copy-start | bytes 786436
  134.5 36.2 %collective-permute-start.6 = (bf16[2,1,256,1536]{3,2,0,1:T(8,128)(2,1)S(1)}, bf16[2,1,256,1536]{3,2,0,1:T(8,128)(2,1)S(1)}, u32[]{:S(2)}, u32[]{:S(2)}) collective-permute-start(bf16[2,1,256,1536]{3,2,0,1:T(8,128)(2,1)S(1)} %broadcast_select_fusion.2), channel_id=1, source_target_pairs={{0,4},{2,6},{4,0},{6,2},{8,12},{10,14},{12,8},{14,10},{16,20},{18,... | collective-permute-start | bytes 4718600 | tf_op jit(solution)/shard_map/ppermute | solution.py:10
  134.6 38.8 %collective-permute-start.3 = (bf16[2,1,128,512]{3,2,1,0:T(8,128)(2,1)S(1)}, bf16[2,1,128,512]{3,2,1,0:T(8,128)(2,1)}, u32[]{:S(2)}, u32[]{:S(2)}) collective-permute-start(bf16[2,1,128,512]{3,2,1,0:T(8,128)(2,1)S(1)} %copy-done.9), channel_id=1, source_target_pairs={{0,2},{2,0},{4,6},{6,4},{8,10},{10,8},{12,14},{14,12},{16,18},{18,... | collective-permute-start | bytes 786440 | tf_op jit(solution)/shard_map/ppermute | solution.py:10
  173.4 14.7 %copy-start.5 = (bf16[2,1,256,1536]{3,2,0,1:T(8,128)(2,1)S(1)}, bf16[2,1,256,1536]{3,2,0,1:T(8,128)(2,1)}, u32[]{:S(2)}) copy-start(bf16[2,1,256,1536]{3,2,0,1:T(8,128)(2,1)} %get-tuple-element.6) | copy-start | bytes 4718596
  174.7 13.0 %collective-permute-start.4 = (bf16[2,1,256,512]{3,2,1,0:T(8,128)(2,1)S(1)}, bf16[2,1,256,512]{3,2,1,0:T(8,128)(2,1)S(1)}, u32[]{:S(2)}, u32[]{:S(2)}) collective-permute-start(bf16[2,1,256,512]{3,2,1,0:T(8,128)(2,1)S(1)} %maximum_select_fusion.3), channel_id=1, source_target_pairs={{0,4},{2,6},{4,0},{6,2},{8,12},{10,14},{12,8},{14,10},{16,20},{18,... | collective-permute-start | bytes 1572872 | tf_op jit(solution)/shard_map/ppermute | solution.py:10
  188.1 1.4 copy-start.7
  217.6 2.4 %copy-start.4 = (bf16[2,1,512,1536]{3,2,0,1:T(8,128)(2,1)S(1)}, bf16[2,1,512,1536]{3,2,0,1:T(8,128)(2,1)}, u32[]{:S(2)}) copy-start(bf16[2,1,512,1536]{3,2,0,1:T(8,128)(2,1)} %all-gather.5.cloned.1.call-done) | copy-start | bytes 9437188
  221.1 1.6 copy-start.6
  221.1 3.2 %copy-start.1 = (s32[1,8,512]{2,1,0:T(8,128)S(1)}, s32[1,8,512]{2,1,0:T(8,128)}, u32[]{:S(2)}) copy-start(s32[1,8,512]{2,1,0:T(8,128)} %param.8) | copy-start | bytes 49156
Sparse Core Ops, SparseCore 0:
  18.8 47.0 all-gather.2
  77.0 43.3 reduce-scatter.1
  173.5 44.0 all-gather.4
where the time goes:
time: 232 us; the launch traced here: 231 us
  waiting for transfers between devices  160 us (69%)
  other arithmetic  23.8 us (10%)
  matrix products  20.3 us (9%)
  between operations  13.5 us (6%)
  local copies, waits for them, and re-layouts  9.77 us (4%)
  starting transfers between devices  3.54 us (2%)
    all_gather x2, waiting for transfers between devices, merge_rows(): lax.all_gather(chosen, 'face', axis=2, tiled=True)  61 us
    ppermute x7, waiting for transfers between devices, partner(): lax.ppermute(array, axis, [(i, i ^ 1 << bit) for i in range(lax.axis_size...  55.6 us
    reduce_scatter x1, waiting for transfers between devices, select_rows(): lax.psum_scatter(picked_rows.astype(jnp.bfloat16).astype(jnp.bfloat16), '...  43.3 us
    dot_general x16, matrix products, real_dot(): jnp.einsum('trk,tkc->trc', first_op, second_op, preferred_element_type=jn...  12.3 us
    concatenate x6, other arithmetic, select_columns(): return jnp.concatenate([end_cols.astype(jnp.float32), picked], axis=3)  6.97 us
    select_n x2, other arithmetic, merge_rows(): own_left = jnp.where(parity == 0, rows_own, nothing)  5.81 us
    dot_general x4, matrix products, select_columns(): jnp.einsum('ptrs,tsk->ptrk', side_cols, picker, preferred_element_type=jn...  5.37 us
  transfers between devices with their start and end apart: 10, of which 8 were waited for; matrix products, arithmetic and copies ran while one was open for 9% of the time, Pallas kernels for 0%

commit v1 on v0

v1 whole, which is shorter than its diff:
```python
import jax
import jax.numpy as jnp
from jax import lax
from jax.experimental import pallas as pl
from jax.experimental.pallas import tpu as pltpu
from jax.sharding import PartitionSpec as P

BF16 = jnp.bfloat16
F32 = jnp.float32
VMEM_BYTES = 48 * 1024 * 1024


def dot(first, second):
    return jnp.dot(first, second, preferred_element_type=F32)


def complex_dot(left, right):
    real = dot(left[0], right[0]) - dot(left[1], right[1])
    imag = dot(left[0], right[1]) + dot(left[1], right[0])
    return real, imag


def column_picker(skeleton, offset, count):
    rows = lax.broadcasted_iota(jnp.int32, (count, skeleton.shape[1]), 0) + offset
    return jnp.where(rows == skeleton, 1.0, 0.0).astype(BF16)


def row_picker(skeleton, offset, count):
    cols = lax.broadcasted_iota(jnp.int32, (skeleton.shape[0], count), 1) + offset
    return jnp.where(cols == skeleton, 1.0, 0.0).astype(BF16)


def call(kernel, scalars, inputs, in_specs, out_shapes, scratch=(), flops=0):
    whole = [
        pl.BlockSpec(s.shape, lambda i, sc, n=len(s.shape): (0,) * n) for s in out_shapes
    ]
    specs = [
        pl.BlockSpec(a.shape, lambda i, sc, n=a.ndim: (0,) * n) if s is None else s
        for a, s in zip(inputs, in_specs)
    ]
    moved = sum(s.size * s.dtype.itemsize for s in out_shapes)
    return pl.pallas_call(
        kernel,
        grid_spec=pltpu.PrefetchScalarGridSpec(
            num_scalar_prefetch=1, grid=(1,), in_specs=specs, out_specs=whole,
            scratch_shapes=list(scratch),
        ),
        out_shape=out_shapes,
        compiler_params=pltpu.CompilerParams(vmem_limit_bytes=VMEM_BYTES),
        cost_estimate=pl.CostEstimate(flops=flops, bytes_accessed=2 * moved, transcendentals=0),
    )(scalars, *inputs)


def on_device(leaf_maps, w_first, w_second, skel_first, skel_second):
    box = lax.axis_index("box")
    face = lax.axis_index("face")
    n_box, n_face = lax.axis_size("box"), lax.axis_size("face")
    fr = leaf_maps.shape[4]
    k = leaf_maps.shape[5] // 3
    half = k // 2
    leaf = leaf_maps[:, 0, 0]
    par = box % 2
    par2 = box // 2 % 2
    quarter = box % 4
    scalars = jnp.stack([par, par2, face, quarter]).astype(jnp.int32)

    def box_permute(array, mask, senders=None):
        pairs = [(b, b ^ mask) for b in range(n_box) if senders is None or senders(b)]
        return lax.ppermute(array, "box", pairs)

    def keeper(b):
        return (b & 1) != (b >> 1 & 1)

    def giver(b):
        return not keeper(b)

    def face_permute(array, step, senders=None):
        pairs = [
            (b * n_face + f, b * n_face + (f + n_face - step) % n_face)
            for b in range(n_box) if senders is None or senders(b)
            for f in range(n_face)
        ]
        return lax.ppermute(array, ("box", "face"), pairs)

    skel_one = lax.dynamic_index_in_dim(skel_first[0], box // 2, 0, keepdims=True)
    skel_two = lax.dynamic_index_in_dim(skel_second[0], box // 4, 0, keepdims=True)
    sds = jax.ShapeDtypeStruct

    end_own = lax.dynamic_slice(
        leaf, (0, 1 - par, 0, par * k), (2, 1, fr, k)
    ).reshape(2, fr, k)
    end_far = [face_permute(end_own, s) for s in range(1, n_face)]
    end_sib = box_permute(end_own, 1)

    def side_kernel(sc, rows_ref, skel_ref, out_ref):
        picker = column_picker(skel_ref[...], sc[0] * k, k)
        for t in range(2):
            out_ref[t] = dot(rows_ref[t], picker).astype(BF16)

    (side_own,) = call(
        side_kernel, scalars, [leaf, skel_one],
        [pl.BlockSpec((2, None, fr, k), lambda i, sc: (0, 1 - sc[0], 0, 2)), None],
        [sds((2, fr, k), BF16)], flops=4 * fr * k * k,
    )
    side = side_own + box_permute(side_own, 1)
    side_half = lax.dynamic_slice(side, (0, 0, par * half), (2, fr, half))
    side_far = [face_permute(side_half, s) for s in range(1, n_face)]

    w_one = jnp.roll(w_first[:, 0], -face * fr, axis=2)
    w_one_sib = box_permute(w_one, 1)
    w_two = jnp.roll(w_second[:, 0], -face * fr, axis=2)
    w_two_x = box_permute(w_two, 2)
    w_two_pair = jnp.stack([w_two, w_two_x])
    w_two_sib = box_permute(w_two_pair, 1)

    s_rows = leaf[:, 2]
    s_sib = box_permute(s_rows, 1, giver)
    skel_rows = skel_one.reshape(k, 1)

    def rows_kernel(sc, own_ref, sib_ref, end_ref, skel_ref, skel_col_ref, *outs):
        p, q, f = sc[0], sc[1], sc[2]

        def columns(ref, t, side, block):
            start = pl.multiple_of((side ^ block) * k, k) if block < 2 else 2 * k
            return ref[t, :, pl.ds(start, k)]

        @pl.when(p == q)
        def _():
            picker = column_picker(skel_ref[...], p * k, k)
            for t in range(2):
                outs[0][t, :, :k] = columns(end_ref, t, p, 1)
                outs[0][t, :, k : 2 * k] = columns(end_ref, t, p, 0)
                outs[0][t, :, 2 * k :] = dot(columns(end_ref, t, p, 2), picker).astype(BF16)

        @pl.when(p != q)
        def _():
            pick_own = column_picker(skel_ref[...], p * k, k)
            pick_sib = column_picker(skel_ref[...], (1 - p) * k, k)
            for t in range(2):
                own = [columns(own_ref, t, p, 1), columns(own_ref, t, p, 0),
                       dot(columns(own_ref, t, p, 2), pick_own).astype(BF16)]
                sib = [columns(sib_ref, t, 1 - p, 1), columns(sib_ref, t, 1 - p, 0),
                       dot(columns(sib_ref, t, 1 - p, 2), pick_sib).astype(BF16)]
                for s in range(n_face):
                    start = pl.multiple_of((f + n_face - s) % n_face * fr, fr)
                    slots = skel_col_ref[pl.ds(start, fr), :]
                    take_own = row_picker(slots, p * k + f * fr, fr)
                    take_sib = row_picker(slots, (1 - p) * k + f * fr, fr)
                    for c in range(3):
                        outs[s][t, :, c * k : (c + 1) * k] = (
                            dot(take_own, own[c]) + dot(take_sib, sib[c])
                        ).astype(BF16)

    face_block = (2, None, fr, 3 * k)
    kept = call(
        rows_kernel, scalars, [leaf, s_sib, leaf, skel_one, skel_rows],
        [pl.BlockSpec(face_block, lambda i, sc: (0, 2, 0, 0)), None,
         pl.BlockSpec(face_block, lambda i, sc: (0, sc[0], 0, 0)), None, None],
        [sds((2, fr, 3 * k), BF16)] * n_face, flops=16 * fr * fr * n_face * 3 * k,
    )
    kept_far = [face_permute(kept[s], s, keeper) for s in range(1, n_face)]

    end_sib_far = [box_permute(a, 1) for a in end_far]
    side_sib_far = [box_permute(a, 1) for a in side_far]
    ends_own = [end_own] + end_far
    ends_sib = [end_sib] + end_sib_far

    def side_product(sc, hidden, side_ref, far_refs, sib_refs, acc):
        p = sc[0]
        first = complex_dot([h[:, :fr] for h in hidden], [side_ref[0], side_ref[1]])
        for t in range(2):
            acc[t] -= first[t]
        for s in range(1, n_face):
            part = [h[:, s * fr : (s + 1) * fr] for h in hidden]
            for ref, which in ((far_refs[s - 1], p), (sib_refs[s - 1], 1 - p)):
                term = complex_dot(part, [ref[0], ref[1]])
                cols = pl.ds(pl.multiple_of(which * half, half), half)
                for t in range(2):
                    acc[t, :, cols] -= term[t]

    def block_product(hidden, refs):
        total = None
        for s, ref in enumerate(refs):
            term = complex_dot([h[:, s * fr : (s + 1) * fr] for h in hidden], [ref[0], ref[1]])
            total = term if total is None else [a + b for a, b in zip(total, term)]
        return total

    def weigh(couple_ref, p, own_ref, sib_ref):
        lo = pl.ds(pl.multiple_of(p * half, half), half)
        hi = pl.ds(pl.multiple_of((1 - p) * half, half), half)
        first = complex_dot([couple_ref[0, :, lo], couple_ref[1, :, lo]], [own_ref[0], own_ref[1]])
        second = complex_dot([couple_ref[0, :, hi], couple_ref[1, :, hi]], [sib_ref[0], sib_ref[1]])
        return [(a + b).astype(BF16) for a, b in zip(first, second)]

    nf = n_face - 1

    def iface_kernel(sc, couple_ref, sidecol_ref, w_ref, wsib_ref, skel_ref, skel2_ref, *rest):
        ends = rest[:n_face]
        side_ref = rest[n_face]
        far = rest[n_face + 1 : n_face + 1 + nf]
        sib = rest[n_face + 1 + nf : n_face + 1 + 2 * nf]
        end_out, side_out, acc = rest[n_face + 1 + 2 * nf :]
        p, q = sc[0], sc[1]

        @pl.when(p == q)
        def _():
            end_out[...] = jnp.zeros_like(end_out)
            side_out[...] = jnp.zeros_like(side_out)

        @pl.when(p != q)
        def _():
            hidden = weigh(couple_ref, p, w_ref, wsib_ref)
            ended = block_product(hidden, ends)
            picker = column_picker(skel_ref[...], p * k, k)
            for t in range(2):
                end_out[t] = (-ended[t]).astype(BF16)
                acc[t] = dot(sidecol_ref[t], picker)
            side_product(sc, hidden, side_ref, far, sib, acc)
            picker2 = column_picker(skel2_ref[...], q * k, k)
            for t in range(2):
                side_out[t] = dot(acc[t].astype(BF16), picker2).astype(BF16)

    end_rows = lambda block: pl.BlockSpec((2, None, fr, k), lambda i, sc: (0, sc[0], 0, block(sc)))
    two_end, two_side = call(
        iface_kernel, scalars,
        [leaf, leaf, w_one, w_one_sib, skel_one, skel_two, *ends_sib, side, *side_far, *side_sib_far],
        [end_rows(lambda sc: 1 - sc[0]), end_rows(lambda sc: 2)] + [None] * (5 + n_face + 2 * nf),
        [sds((2, fr, k), BF16)] * 2, [pltpu.VMEM((2, fr, k), F32)],
        flops=8 * fr * k * 3 * k,
    )

    side_x = box_permute(two_side, 3, keeper)
    end_x = box_permute(two_end, 3, keeper)
    two_sides = two_side + side_x
    two_half = lax.dynamic_slice(two_sides, (0, 0, par2 * half), (2, fr, half))
    end_y = [face_permute(two_end, s, keeper) for s in range(1, n_face)]
    half_y = [face_permute(two_half, s, keeper) for s in range(1, n_face)]
    end_xy = [box_permute(a, 3, keeper) for a in end_y]
    half_xy = [box_permute(a, 3, keeper) for a in half_y]
    gathered = [two_end, end_x, two_sides]
    for s in range(nf):
        gathered += [end_y[s], end_xy[s], half_y[s], half_xy[s]]
    forwarded = [box_permute(a, 1, keeper) for a in gathered]

    def level_one_kernel(sc, *rest):
        zs = rest[:n_face]
        skel_col_ref, w_ref, wsib_ref, w2_ref, w2sib_ref, skel2_ref = rest[n_face : n_face + 6]
        rest = rest[n_face + 6 :]
        own_ends, sib_ends = rest[:n_face], rest[n_face : 2 * n_face]
        rest = rest[2 * n_face :]
        side_ref, far, sib = rest[0], rest[1 : 1 + nf], rest[1 + nf : 1 + 2 * nf]
        hid_out, end_out, side_out, couple, acc, w2 = rest[1 + 2 * nf :]
        p, q, f, r = sc[0], sc[1], sc[2], sc[3]
        is_end = p == q

        def rows(t, c):
            total = zs[0][t, :, c * k : (c + 1) * k]
            for z in zs[1:]:
                total = total + z[t, :, c * k : (c + 1) * k]
            return total

        slots = skel_col_ref[pl.ds(pl.multiple_of(f * fr, fr), fr), :]
        right = jnp.where(slots >= k, 1, 0)
        right = jnp.where(is_end, p, right)
        own_side = right == p
        for t in range(2):
            couple[t] = rows(t, 0)
        hidden = weigh(couple, p, w_ref, wsib_ref)
        own = block_product(hidden, own_ends)
        other = block_product(hidden, sib_ends)
        for t in range(2):
            acc[t] = rows(t, 2).astype(F32)
        side_product(sc, hidden, side_ref, far, sib, acc)
        picker2 = column_picker(skel2_ref[...], q * k, k)
        for t in range(2):
            ends = rows(t, 1).astype(F32)
            nothing = jnp.zeros_like(ends)
            own_rows = (jnp.where(own_side, ends, nothing) - own[t]).astype(BF16)
            sib_rows = (jnp.where(own_side, nothing, ends) - other[t]).astype(BF16)
            end_out[t] = jnp.where(is_end, own_rows, sib_rows)
            couple[t] = jnp.where(is_end, sib_rows, own_rows)
            side_out[t] = dot(acc[t].astype(BF16), picker2).astype(BF16)
        blk = k // 4
        for i, (ref, part) in enumerate(((w2_ref, 0), (w2_ref, 1), (w2sib_ref, 0), (w2sib_ref, 1))):
            place = r ^ (part * 2) ^ (i // 2)
            for t in range(2):
                w2[t, pl.ds(pl.multiple_of(place * blk, blk), blk), :] = ref[part, t]
        second = complex_dot([couple[0], couple[1]], [w2[0], w2[1]])
        for t in range(2):
            hid_out[t] = second[t].astype(BF16)

    hid_two, diag_end, diag_side = call(
        level_one_kernel, scalars,
        [kept[0], *kept_far, skel_rows, w_one, w_one_sib, w_two_pair, w_two_sib, skel_two,
         *ends_own, *ends_sib, side, *side_far, *side_sib_far],
        [None] * (n_face + 6 + 2 * n_face + 1 + 2 * nf),
        [sds((2, fr, k), BF16)] * 3,
        [pltpu.VMEM((2, fr, k), BF16), pltpu.VMEM((2, fr, k), F32), pltpu.VMEM((2, k, k), BF16)],
        flops=8 * fr * k * 5 * k,
    )

    def final_kernel(sc, hid_ref, end_ref, side_ref, *rest):
        n = 3 + 4 * nf
        have, sent = rest[:n], rest[n : 2 * n]
        out_ref, acc = rest[2 * n :]
        q = sc[1]
        own_cols = pl.ds(pl.multiple_of(q * k, k), k)
        sib_cols = pl.ds(pl.multiple_of((1 - q) * k, k), k)
        hidden = [hid_ref[0], hid_ref[1]]

        def term(s, i):
            part = [h[:, s * fr : (s + 1) * fr] for h in hidden]
            return complex_dot(part, [have[i][t] + sent[i][t] for t in range(2)])

        own, other, sides = term(0, 0), term(0, 1), term(0, 2)
        for t in range(2):
            acc[t] = side_ref[t].astype(F32) - sides[t]
        for s in range(1, n_face):
            base = 3 + 4 * (s - 1)
            own = [a + b for a, b in zip(own, term(s, base))]
            other = [a + b for a, b in zip(other, term(s, base + 1))]
            for i, which in ((base + 2, q), (base + 3, 1 - q)):
                add = term(s, i)
                cols = pl.ds(pl.multiple_of(which * half, half), half)
                for t in range(2):
                    acc[t, :, cols] -= add[t]
        for t in range(2):
            out_ref[t, 0, :, own_cols] = (end_ref[t].astype(F32) - own[t]).astype(BF16)
            out_ref[t, 0, :, sib_cols] = (-other[t]).astype(BF16)
            out_ref[t, 0, :, 2 * k :] = acc[t].astype(BF16)

    (out,) = call(
        final_kernel, scalars, [hid_two, diag_end, diag_side, *gathered, *forwarded],
        [None] * (3 + 2 * (3 + 4 * nf)),
        [sds((2, 1, fr, 3 * k), BF16)], [pltpu.VMEM((2, fr, k), F32)],
        flops=8 * fr * k * 3 * k,
    )
    return out


def solution(mesh):
    return jax.shard_map(
        on_device,
        mesh=mesh,
        in_specs=(
            P(None, None, "box", None, "face", None),
            P(None, None, "box", None),
            P(None, None, "box", None),
            P(),
            P(),
        ),
        out_specs=P(None, None, ("box", "face"), None),
        check_vma=False,
    )
```

time: 232 us -> 102 us (0.44)
  waiting for transfers between devices: 160 us -> 21.2 us
  starting transfers between devices: 3.54 us -> 37.9 us
  Pallas kernels: 0 us -> 25 us
  matrix products: 20.3 us -> 0 us
  other arithmetic: 23.8 us -> 6.44 us
  between operations: 13.5 us -> 0.5 us
    all_gather x2 -> x0, waiting for transfers between devices: 61 us -> none  [merge_rows(): lax.all_gather(chosen, 'face', axis=2, tiled=True)]
    reduce_scatter x1 -> x0, waiting for transfers between devices: 43.3 us -> none  [select_rows(): lax.psum_scatter(picked_rows.astype(jnp.bfloat16).astype(jnp.bfloat16), '...]
    ppermute x7 -> x24, starting transfers between devices: 3.27 us -> 37.9 us  [the longest x19 28.5 us: box_permute(): return lax.ppermute(array, 'box', pairs)]
    ppermute x7 -> x24, waiting for transfers between devices: 55.6 us -> 21.2 us  [the longest x5 14.2 us: face_permute(): return lax.ppermute(array, ('box', 'face'), pairs)]
    pallas_call x0 -> x5, Pallas kernels: none -> 25 us  [call(): pl.pallas_call(kernel, grid_spec=pltpu.PrefetchScalarGridSpec(num_scalar_...]
    dot_general x21 -> x0, matrix products: 20.3 us -> none  [the longest x16 12.3 us: real_dot(): jnp.einsum('trk,tkc->trc', first_op, second_op, preferred_element_type=jn...]
    select_n x9 -> x0, other arithmetic: 13.1 us -> none  [the longest x2 5.81 us: merge_rows(): own_left = jnp.where(parity == 0, rows_own, nothing)]
    concatenate x8 -> x2, other arithmetic: 8.21 us -> 1.97 us  [the longest x1 1.76 us: on_device(): w_two = jnp.roll(w_second[:, 0], -face * fr, axis=2)]
  transfers between devices with their start and end apart: 10 -> 24, of which waited for: 8 -> 5; matrix products, arithmetic and copies ran while one was open for 9% -> 9% of each run, Pallas kernels for 0% -> 19%
where the time goes in v1:
time: 102 us; the launch traced here: 101 us
  starting transfers between devices  37.9 us (37%)
  Pallas kernels  25 us (25%)
  waiting for transfers between devices  21.2 us (21%)
  local copies, waits for them, and re-layouts  10 us (10%)
  other arithmetic  6.44 us (6%)
    ppermute x19, starting transfers between devices, box_permute(): return lax.ppermute(array, 'box', pairs)  28.5 us
    pallas_call x5, Pallas kernels, call(): pl.pallas_call(kernel, grid_spec=pltpu.PrefetchScalarGridSpec(num_scalar_...  25 us
    ppermute x5, waiting for transfers between devices, face_permute(): return lax.ppermute(array, ('box', 'face'), pairs)  14.2 us
    ppermute x5, starting transfers between devices, face_permute(): return lax.ppermute(array, ('box', 'face'), pairs)  9.46 us
    ppermute x19, waiting for transfers between devices, box_permute(): return lax.ppermute(array, 'box', pairs)  7.04 us
    unnamed x32, local copies, waits for them, and re-layouts  4.61 us
    squeeze x1, local copies, waits for them, and re-layouts, on_device(): s_rows = leaf[:, 2]  2.66 us
  transfers between devices with their start and end apart: 24, of which 5 were waited for; matrix products, arithmetic and copies ran while one was open for 9% of the time, Pallas kernels for 19%

profile of v1, /device:TPU:1, one launch (start us, length us, event | category | flops | bytes accessed | tf_op | source)
XLA Modules:
  0.0 101.1 jit_solution(10040244242223025533)
XLA Ops:
  0.0 2.7 %slice_bitcast_fusion = bf16[2,256,1536]{2,1,0:T(8,128)(2,1)} fusion(bf16[2,3,256,1536]{3,2,1,0:T(8,128)(2,1)} %bitcast.20), kind=kLoop, calls=%fused_computation | loop fusion | bytes 3145728 | tf_op jit(solution)/shard_map/squeeze | solution.py:116
  2.7 1.3 %collective-permute-start = (bf16[2,256,1536]{2,1,0:T(8,128)(2,1)}, bf16[2,256,1536]{2,1,0:T(8,128)(2,1)}, u32[]{:S(2)}, u32[]{:S(2)}) collective-permute-start(bf16[2,256,1536]{2,1,0:T(8,128)(2,1)} %slice_bitcast_fusion), channel_id=1, source_target_pairs={{0,2},{6,4},{8,10},{14,12},{16,18},{22,20},{24,26},{30,28},{1,3},{... | collective-permute-start | bytes 4718600 | tf_op jit(solution)/shard_map/ppermute | solution.py:69
  4.1 0.7 fusion.3
  4.8 2.3 %copy-done.1 = bf16[2,1,1,3,256,1536]{5,4,3,2,1,0:T(8,128)(2,1)S(1)} copy-done((bf16[2,1,1,3,256,1536]{5,4,3,2,1,0:T(8,128)(2,1)S(1)}, bf16[2,1,1,3,256,1536]{5,4,3,2,1,0:T(8,128)(2,1)}, u32[]{:S(2)}) %copy-start.1) | copy-done | bytes 4718616
  7.2 1.0 shard_map.56
  8.2 2.3 %collective-permute-start.8 = (bf16[2,256,512]{2,1,0:T(8,128)(2,1)S(1)}, bf16[2,256,512]{2,1,0:T(8,128)(2,1)}, u32[]{:S(2)}, u32[]{:S(2)}) collective-permute-start(bf16[2,256,512]{2,1,0:T(8,128)(2,1)S(1)} %shard_map.56), channel_id=1, source_target_pairs={{0,2},{2,0},{4,6},{6,4},{8,10},{10,8},{12,14},{14,12},{16,18},{18,... | collective-permute-start | bytes 1572872 | tf_op jit(solution)/shard_map/ppermute | solution.py:69
  10.5 1.1 %dynamic-slice_bitcast_fusion.rest_8_ = bf16[2,256,512]{2,1,0:T(8,128)(2,1)S(1)} fusion(bf16[2,1,1,3,256,1536]{5,4,3,2,1,0:T(8,128)(2,1)} %param.5, s32[]{:T(128)S(6)} %select_n.70, s32[]{:T(128)S(6)} %select_n.71), kind=kLoop, calls=%fused_computation.7 | loop fusion | bytes 1048584 | tf_op jit(solution)/shard_map/reshape | solution.py:91
  11.6 2.1 %collective-permute-start.5 = (bf16[2,256,512]{2,1,0:T(8,128)(2,1)S(1)}, bf16[2,256,512]{2,1,0:T(8,128)(2,1)}, u32[]{:S(2)}, u32[]{:S(2)}) collective-permute-start(bf16[2,256,512]{2,1,0:T(8,128)(2,1)S(1)} %dynamic-slice_bitcast_fusion.rest_8_), channel_id=1, source_target_pairs={{0,1},{1,0},{2,3},{3,2},{4,5},{5,4},{6,7},{7,6},{8,9},{9,8},{10,11... | collective-permute-start | bytes 1572872 | tf_op jit(solution)/shard_map/ppermute | solution.py:83
  13.7 0.3 collective-permute-start.6
  14.0 0.2 fusion.rest_3_.w_ref
  14.2 0.3 collective-permute-start.2
  14.5 1.2 %add.62.rest_12_.rest_2_ = bf16[2,256,512]{2,1,0:T(8,128)(2,1)S(1)} add(bf16[2,256,512]{2,1,0:T(8,128)(2,1)S(1)} %shard_map.56, bf16[2,256,512]{2,1,0:T(8,128)(2,1)} %collective-permute-done.8) | non-fusion elementwise | flops 262144 | bytes 1572864 | tf_op jit(solution)/shard_map/add | solution.py:105
  15.8 1.8 %fusion.1 = bf16[2,128,512]{2,1,0:T(8,128)(2,1)} fusion(s32[]{:T(128)S(6)} %select_n.67, bf16[2,128,512]{2,1,0:T(8,128)(2,1)} %bitcast.26), kind=kLoop, calls=%fused_computation.8 | loop fusion | flops 524288 | bytes 524292 | tf_op jit(solution)/shard_map/jit(_roll_dynamic)/concatenate | solution.py:111
  17.6 0.9 copy.6.skel_col_ref.rest_2_
  18.5 7.6 %collective-permute-done.5.rest_9_ = bf16[2,256,512]{2,1,0:T(8,128)(2,1)} collective-permute-done((bf16[2,256,512]{2,1,0:T(8,128)(2,1)S(1)}, bf16[2,256,512]{2,1,0:T(8,128)(2,1)}, u32[]{:S(2)}, u32[]{:S(2)}) %collective-permute-start.5) | collective-permute-done | bytes 524320 | tf_op jit(solution)/shard_map/ppermute | solution.py:83
  26.1 0.8 collective-permute-start.7
  26.9 1.1 %fusion.5 = bf16[1,2,128,512]{3,2,1,0:T(8,128)(2,1)S(1)} fusion(s32[]{:T(128)S(6)} %select_n.67, bf16[2,128,512]{2,1,0:T(8,128)(2,1)} %bitcast.27), kind=kLoop, calls=%fused_computation.17 | loop fusion | flops 524288 | bytes 524292 | tf_op jit(solution)/shard_map/stack | solution.py:113
  28.0 3.6 %collective-permute-done.9.rest_13_.rest_3_ = bf16[2,256,256]{2,1,0:T(8,128)(2,1)S(1)} collective-permute-done((bf16[2,256,256]{2,1,0:T(8,128)(2,1)S(1)}, bf16[2,256,256]{2,1,0:T(8,128)(2,1)S(1)}, u32[]{:S(2)}, u32[]{:S(2)}) %collective-permute-start.9) | collective-permute-done | bytes 262176 | tf_op jit(solution)/shard_map/ppermute | solution.py:83
  31.6 0.9 collective-permute-start.3
  32.5 1.6 %collective-permute-start.10 = (bf16[2,256,256]{2,1,0:T(8,128)(2,1)S(1)}, bf16[2,256,256]{2,1,0:T(8,128)(2,1)S(1)}, u32[]{:S(2)}, u32[]{:S(2)}) collective-permute-start(bf16[2,256,256]{2,1,0:T(8,128)(2,1)S(1)} %collective-permute-done.9.rest_13_.rest_3_), channel_id=1, source_target_pairs={{0,2},{2,0},{4,6},{6,4},{8,10},{10,8},{12,14},{14,12},{16,18},{18,... | collective-permute-start | bytes 786440 | tf_op jit(solution)/shard_map/ppermute | solution.py:69
  34.1 0.9 copy-done.8
  35.1 6.4 %shard_map.55 = (bf16[2,256,1536]{2,1,0:T(8,128)(2,1)S(1)}, bf16[2,256,1536]{2,1,0:T(8,128)(2,1)}) custom-call(s32[4]{0:T(128)S(1)} %pad_add_fusion.sc, bf16[2,3,256,1536]{3,2,1,0:T(8,128)(2,1)} %bitcast.21, bf16[2,256,1536]{2,1,0:T(8,128)(2,1)} %collective-permute-done.sib_ref, bf16[2,3,256,1536]{3,2,1,0:T(8,128)(2,1)} %bitcast.22, ...), custom_call_target="tpu_custom_call" | custom-call | flops 3221225472 | bytes 6291456 | tf_op jit(solution)/shard_map/pallas_call | solution.py:42
  41.5 3.1 %collective-permute-start.1 = (bf16[2,256,1536]{2,1,0:T(8,128)(2,1)}, bf16[2,256,1536]{2,1,0:T(8,128)(2,1)}, u32[]{:S(2)}, u32[]{:S(2)}) collective-permute-start(bf16[2,256,1536]{2,1,0:T(8,128)(2,1)} %get-tuple-element.13), channel_id=1, source_target_pairs={{2,3},{3,2},{4,5},{5,4},{10,11},{11,10},{12,13},{13,12},{18,19},{1... | collective-permute-start | bytes 4718600 | tf_op jit(solution)/shard_map/ppermute | solution.py:83
  44.7 5.2 %shard_map.58 = (bf16[2,256,512]{2,1,0:T(8,128)(2,1)S(1)}, bf16[2,256,512]{2,1,0:T(8,128)(2,1)}) custom-call(s32[4]{0:T(128)S(1)} %pad_add_fusion.sc, bf16[2,3,256,1536]{3,2,1,0:T(8,128)(2,1)} %bitcast.23, bf16[2,3,256,1536]{3,2,1,0:T(8,128)(2,1)} %bitcast.24, bf16[2,256,512]{2,1,0:T(8,128)(2,1)S(1)} %fusion.rest_3_.w_ref, ...), custom_call_target="tpu_custom_call" | custom-call | flops 1610612736 | bytes 2097152 | tf_op jit(solution)/shard_map/pallas_call | solution.py:42
  49.9 2.1 %collective-permute-start.12 = (bf16[2,256,512]{2,1,0:T(8,128)(2,1)}, bf16[2,256,512]{2,1,0:T(8,128)(2,1)}, u32[]{:S(2)}, u32[]{:S(2)}) collective-permute-start(bf16[2,256,512]{2,1,0:T(8,128)(2,1)} %get-tuple-element.18), channel_id=1, source_target_pairs={{2,4},{4,2},{10,12},{12,10},{18,20},{20,18},{26,28},{28,26},{3,5},... | collective-permute-start | bytes 1572872 | tf_op jit(solution)/shard_map/ppermute | solution.py:69
  52.1 0.8 pad_maximum_fusion.rest_5_
  52.9 1.9 %collective-permute-start.13 = (bf16[2,256,512]{2,1,0:T(8,128)(2,1)S(1)}, bf16[2,256,512]{2,1,0:T(8,128)(2,1)S(1)}, u32[]{:S(2)}, u32[]{:S(2)}) collective-permute-start(bf16[2,256,512]{2,1,0:T(8,128)(2,1)S(1)} %get-tuple-element.17.rest_0_), channel_id=1, source_target_pairs={{2,3},{3,2},{4,5},{5,4},{10,11},{11,10},{12,13},{13,12},{18,19},{1... | collective-permute-start | bytes 1572872 | tf_op jit(solution)/shard_map/ppermute | solution.py:83
  54.8 3.9 %collective-permute-start.11 = (bf16[2,256,512]{2,1,0:T(8,128)(2,1)S(1)}, bf16[2,256,512]{2,1,0:T(8,128)(2,1)S(1)}, u32[]{:S(2)}, u32[]{:S(2)}) collective-permute-start(bf16[2,256,512]{2,1,0:T(8,128)(2,1)S(1)} %get-tuple-element.17.rest_0_), channel_id=1, source_target_pairs={{2,4},{4,2},{10,12},{12,10},{18,20},{20,18},{26,28},{28,26},{3,5},... | collective-permute-start | bytes 1572872 | tf_op jit(solution)/shard_map/ppermute | solution.py:69
  58.8 1.9 %collective-permute-done.12 = bf16[2,256,512]{2,1,0:T(8,128)(2,1)} collective-permute-done((bf16[2,256,512]{2,1,0:T(8,128)(2,1)}, bf16[2,256,512]{2,1,0:T(8,128)(2,1)}, u32[]{:S(2)}, u32[]{:S(2)}) %collective-permute-start.12) | collective-permute-done | bytes 524320 | tf_op jit(solution)/shard_map/ppermute | solution.py:69
  60.7 1.3 %collective-permute-start.17 = (bf16[2,256,512]{2,1,0:T(8,128)(2,1)S(1)}, bf16[2,256,512]{2,1,0:T(8,128)(2,1)S(1)}, u32[]{:S(2)}, u32[]{:S(2)}) collective-permute-start(bf16[2,256,512]{2,1,0:T(8,128)(2,1)S(1)} %get-tuple-element.17.rest_0_), channel_id=1, source_target_pairs={{2,0},{4,6},{10,8},{12,14},{18,16},{20,22},{26,24},{28,30},{3,1},{... | collective-permute-start | bytes 1572872 | tf_op jit(solution)/shard_map/ppermute | solution.py:69
  62.0 1.3 %add.64.rest_2_ = bf16[2,256,512]{2,1,0:T(8,128)(2,1)S(1)} add(bf16[2,256,512]{2,1,0:T(8,128)(2,1)} %get-tuple-element.18, bf16[2,256,512]{2,1,0:T(8,128)(2,1)} %collective-permute-done.12) | non-fusion elementwise | flops 262144 | bytes 1572864 | tf_op jit(solution)/shard_map/add | solution.py:234
  63.4 2.1 %collective-permute-start.15 = (bf16[2,256,256]{2,1,0:T(8,128)(2,1)S(1)}, bf16[2,256,256]{2,1,0:T(8,128)(2,1)S(1)}, u32[]{:S(2)}, u32[]{:S(2)}) collective-permute-start(bf16[2,256,256]{2,1,0:T(8,128)(2,1)S(1)} %constant_dynamic-slice_fusion), channel_id=1, source_target_pairs={{2,3},{3,2},{4,5},{5,4},{10,11},{11,10},{12,13},{13,12},{18,19},{1... | collective-permute-start | bytes 786440 | tf_op jit(solution)/shard_map/ppermute | solution.py:83
  65.6 2.9 %collective-permute-done.13.rest_3_ = bf16[2,256,512]{2,1,0:T(8,128)(2,1)S(1)} collective-permute-done((bf16[2,256,512]{2,1,0:T(8,128)(2,1)S(1)}, bf16[2,256,512]{2,1,0:T(8,128)(2,1)S(1)}, u32[]{:S(2)}, u32[]{:S(2)}) %collective-permute-start.13) | collective-permute-done | bytes 524320 | tf_op jit(solution)/shard_map/ppermute | solution.py:83
  68.5 2.8 %collective-permute-start.14 = (bf16[2,256,512]{2,1,0:T(8,128)(2,1)S(1)}, bf16[2,256,512]{2,1,0:T(8,128)(2,1)S(1)}, u32[]{:S(2)}, u32[]{:S(2)}) collective-permute-start(bf16[2,256,512]{2,1,0:T(8,128)(2,1)S(1)} %collective-permute-done.13.rest_3_), channel_id=1, source_target_pairs={{2,4},{4,2},{10,12},{12,10},{18,20},{20,18},{26,28},{28,26},{3,5},... | collective-permute-start | bytes 1572872 | tf_op jit(solution)/shard_map/ppermute | solution.py:69
  71.3 2.8 %collective-permute-start.16 = (bf16[2,256,256]{2,1,0:T(8,128)(2,1)S(1)}, bf16[2,256,256]{2,1,0:T(8,128)(2,1)S(1)}, u32[]{:S(2)}, u32[]{:S(2)}) collective-permute-start(bf16[2,256,256]{2,1,0:T(8,128)(2,1)S(1)} %collective-permute-done.15.rest_5_), channel_id=1, source_target_pairs={{2,4},{4,2},{10,12},{12,10},{18,20},{20,18},{26,28},{28,26},{3,5},... | collective-permute-start | bytes 786440 | tf_op jit(solution)/shard_map/ppermute | solution.py:69
  74.1 1.3 %collective-permute-start.22 = (bf16[2,256,256]{2,1,0:T(8,128)(2,1)S(1)}, bf16[2,256,256]{2,1,0:T(8,128)(2,1)S(1)}, u32[]{:S(2)}, u32[]{:S(2)}) collective-permute-start(bf16[2,256,256]{2,1,0:T(8,128)(2,1)S(1)} %collective-permute-done.15.rest_5_), channel_id=1, source_target_pairs={{2,0},{4,6},{10,8},{12,14},{18,16},{20,22},{26,24},{28,30},{3,1},{... | collective-permute-start | bytes 786440 | tf_op jit(solution)/shard_map/ppermute | solution.py:69
  75.4 1.3 %collective-permute-start.19 = (bf16[2,256,512]{2,1,0:T(8,128)(2,1)S(1)}, bf16[2,256,512]{2,1,0:T(8,128)(2,1)S(1)}, u32[]{:S(2)}, u32[]{:S(2)}) collective-permute-start(bf16[2,256,512]{2,1,0:T(8,128)(2,1)S(1)} %add.64.rest_2_), channel_id=1, source_target_pairs={{2,0},{4,6},{10,8},{12,14},{18,16},{20,22},{26,24},{28,30},{3,1},{... | collective-permute-start | bytes 1572872 | tf_op jit(solution)/shard_map/ppermute | solution.py:69
  76.7 5.0 %collective-permute-done.16.rest_6_ = bf16[2,256,256]{2,1,0:T(8,128)(2,1)S(1)} collective-permute-done((bf16[2,256,256]{2,1,0:T(8,128)(2,1)S(1)}, bf16[2,256,256]{2,1,0:T(8,128)(2,1)S(1)}, u32[]{:S(2)}, u32[]{:S(2)}) %collective-permute-start.16) | collective-permute-done | bytes 262176 | tf_op jit(solution)/shard_map/ppermute | solution.py:69
  81.8 1.3 %collective-permute-start.18 = (bf16[2,256,512]{2,1,0:T(8,128)(2,1)S(1)}, bf16[2,256,512]{2,1,0:T(8,128)(2,1)S(1)}, u32[]{:S(2)}, u32[]{:S(2)}) collective-permute-start(bf16[2,256,512]{2,1,0:T(8,128)(2,1)S(1)} %collective-permute-done.11.rest_1_), channel_id=1, source_target_pairs={{2,0},{4,6},{10,8},{12,14},{18,16},{20,22},{26,24},{28,30},{3,1},{... | collective-permute-start | bytes 1572872 | tf_op jit(solution)/shard_map/ppermute | solution.py:69
  83.1 1.3 %collective-permute-start.20 = (bf16[2,256,512]{2,1,0:T(8,128)(2,1)S(1)}, bf16[2,256,512]{2,1,0:T(8,128)(2,1)S(1)}, u32[]{:S(2)}, u32[]{:S(2)}) collective-permute-start(bf16[2,256,512]{2,1,0:T(8,128)(2,1)S(1)} %collective-permute-done.13.rest_3_), channel_id=1, source_target_pairs={{2,0},{4,6},{10,8},{12,14},{18,16},{20,22},{26,24},{28,30},{3,1},{... | collective-permute-start | bytes 1572872 | tf_op jit(solution)/shard_map/ppermute | solution.py:69
  84.5 1.3 %collective-permute-start.21 = (bf16[2,256,512]{2,1,0:T(8,128)(2,1)S(1)}, bf16[2,256,512]{2,1,0:T(8,128)(2,1)S(1)}, u32[]{:S(2)}, u32[]{:S(2)}) collective-permute-start(bf16[2,256,512]{2,1,0:T(8,128)(2,1)S(1)} %collective-permute-done.14.rest_4_), channel_id=1, source_target_pairs={{2,0},{4,6},{10,8},{12,14},{18,16},{20,22},{26,24},{28,30},{3,1},{... | collective-permute-start | bytes 1572872 | tf_op jit(solution)/shard_map/ppermute | solution.py:69
  85.8 1.5 %collective-permute-start.23 = (bf16[2,256,256]{2,1,0:T(8,128)(2,1)S(1)}, bf16[2,256,256]{2,1,0:T(8,128)(2,1)S(1)}, u32[]{:S(2)}, u32[]{:S(2)}) collective-permute-start(bf16[2,256,256]{2,1,0:T(8,128)(2,1)S(1)} %collective-permute-done.16.rest_6_), channel_id=1, source_target_pairs={{2,0},{4,6},{10,8},{12,14},{18,16},{20,22},{26,24},{28,30},{3,1},{... | collective-permute-start | bytes 786440 | tf_op jit(solution)/shard_map/ppermute | solution.py:69
  87.3 6.9 %shard_map.57 = (bf16[2,256,512]{2,1,0:T(8,128)(2,1)S(1)}, bf16[2,256,512]{2,1,0:T(8,128)(2,1)S(1)}, bf16[2,256,512]{2,1,0:T(8,128)(2,1)S(1)}) custom-call(s32[4]{0:T(128)S(1)} %pad_add_fusion.sc, bf16[2,256,1536]{2,1,0:T(8,128)(2,1)} %copy-done.10, bf16[2,256,1536]{2,1,0:T(8,128)(2,1)} %collective-permute-done.1.rest_1_, s32[512,1]{1,0:T(8,128)S(1)} %copy-done.9, ...), custom_call_target="tpu_custom_call" | custom-call | flops 2684354560 | bytes 3145728 | tf_op jit(solution)/shard_map/pallas_call | solution.py:42
  94.3 0.7 copy-done.12
  95.0 0.2 copy-done.11
  95.2 0.2 copy-done.13
  95.4 0.2 copy-done.14
  95.6 5.4 %shard_map.59 = bf16[2,1,256,1536]{3,2,1,0:T(8,128)(2,1)} custom-call(s32[4]{0:T(128)S(1)} %pad_add_fusion.sc, bf16[2,256,512]{2,1,0:T(8,128)(2,1)S(1)} %get-tuple-element.14.hid_ref, bf16[2,256,512]{2,1,0:T(8,128)(2,1)S(1)} %get-tuple-element.15.end_ref, bf16[2,256,512]{2,1,0:T(8,128)(2,1)S(1)} %get-tuple-element.16.side_ref, ...), custom_call_target="tpu_custom_call" | custom-call | flops 1610612736 | bytes 3145728 | tf_op jit(solution)/shard_map/pallas_call | solution.py:42
  (51 shorter events, 0.4 us)
Async XLA Ops:
  0.0 26.9 %copy-start = (s32[1,4,512]{2,1,0:T(4,128)S(1)}, s32[1,4,512]{2,1,0:T(4,128)}, u32[]{:S(2)}) copy-start(s32[1,4,512]{2,1,0:T(4,128)} %param.9) | copy-start | bytes 24580
  2.7 29.8 %collective-permute-start = (bf16[2,256,1536]{2,1,0:T(8,128)(2,1)}, bf16[2,256,1536]{2,1,0:T(8,128)(2,1)}, u32[]{:S(2)}, u32[]{:S(2)}) collective-permute-start(bf16[2,256,1536]{2,1,0:T(8,128)(2,1)} %slice_bitcast_fusion), channel_id=1, source_target_pairs={{0,2},{6,4},{8,10},{14,12},{16,18},{22,20},{24,26},{30,28},{1,3},{... | collective-permute-start | bytes 4718600 | tf_op jit(solution)/shard_map/ppermute | solution.py:69
  4.8 2.3 %copy-start.1 = (bf16[2,1,1,3,256,1536]{5,4,3,2,1,0:T(8,128)(2,1)S(1)}, bf16[2,1,1,3,256,1536]{5,4,3,2,1,0:T(8,128)(2,1)}, u32[]{:S(2)}) copy-start(bf16[2,1,1,3,256,1536]{5,4,3,2,1,0:T(8,128)(2,1)} %param.5) | copy-start | bytes 14155780
  7.2 6.9 %copy-start.15 = (bf16[2,1,256,512]{3,2,1,0:T(8,128)(2,1)S(1)}, bf16[2,1,256,512]{3,2,1,0:T(8,128)(2,1)}, u32[]{:S(2)}) copy-start(bf16[2,1,256,512]{3,2,1,0:T(8,128)(2,1)} %param.6) | copy-start | bytes 1572868
  8.2 6.3 %collective-permute-start.8 = (bf16[2,256,512]{2,1,0:T(8,128)(2,1)S(1)}, bf16[2,256,512]{2,1,0:T(8,128)(2,1)}, u32[]{:S(2)}, u32[]{:S(2)}) collective-permute-start(bf16[2,256,512]{2,1,0:T(8,128)(2,1)S(1)} %shard_map.56), channel_id=1, source_target_pairs={{0,2},{2,0},{4,6},{6,4},{8,10},{10,8},{12,14},{14,12},{16,18},{18,... | collective-permute-start | bytes 1572872 | tf_op jit(solution)/shard_map/ppermute | solution.py:69
  11.5 4.2 %copy-start.4 = (bf16[2,256,512]{2,1,0:T(8,128)(2,1)}, bf16[2,256,512]{2,1,0:T(8,128)(2,1)S(1)}, u32[]{:S(2)}) copy-start(bf16[2,256,512]{2,1,0:T(8,128)(2,1)S(1)} %dynamic-slice_bitcast_fusion.rest_8_) | copy-start | bytes 1572868
  11.6 14.5 %collective-permute-start.5 = (bf16[2,256,512]{2,1,0:T(8,128)(2,1)S(1)}, bf16[2,256,512]{2,1,0:T(8,128)(2,1)}, u32[]{:S(2)}, u32[]{:S(2)}) collective-permute-start(bf16[2,256,512]{2,1,0:T(8,128)(2,1)S(1)} %dynamic-slice_bitcast_fusion.rest_8_), channel_id=1, source_target_pairs={{0,1},{1,0},{2,3},{3,2},{4,5},{5,4},{6,7},{7,6},{8,9},{9,8},{10,11... | collective-permute-start | bytes 1572872 | tf_op jit(solution)/shard_map/ppermute | solution.py:83
  13.7 31.0 %collective-permute-start.6 = (bf16[2,256,512]{2,1,0:T(8,128)(2,1)S(1)}, bf16[2,256,512]{2,1,0:T(8,128)(2,1)S(1)}, u32[]{:S(2)}, u32[]{:S(2)}) collective-permute-start(bf16[2,256,512]{2,1,0:T(8,128)(2,1)S(1)} %dynamic-slice_bitcast_fusion.rest_8_), channel_id=1, source_target_pairs={{0,2},{2,0},{4,6},{6,4},{8,10},{10,8},{12,14},{14,12},{16,18},{18,... | collective-permute-start | bytes 1572872 | tf_op jit(solution)/shard_map/ppermute | solution.py:69
  14.2 27.3 %collective-permute-start.2 = (bf16[2,256,512]{2,1,0:T(8,128)(2,1)S(1)}, bf16[2,256,512]{2,1,0:T(8,128)(2,1)S(1)}, u32[]{:S(2)}, u32[]{:S(2)}) collective-permute-start(bf16[2,256,512]{2,1,0:T(8,128)(2,1)S(1)} %fusion.rest_3_.w_ref), channel_id=1, source_target_pairs={{0,2},{2,0},{4,6},{6,4},{8,10},{10,8},{12,14},{14,12},{16,18},{18,... | collective-permute-start | bytes 1572872 | tf_op jit(solution)/shard_map/ppermute | solution.py:69
  15.7 29.1 %copy-start.2 = (bf16[2,256,512]{2,1,0:T(8,128)(2,1)}, bf16[2,256,512]{2,1,0:T(8,128)(2,1)S(1)}, u32[]{:S(2)}) copy-start(bf16[2,256,512]{2,1,0:T(8,128)(2,1)S(1)} %add.62.rest_12_.rest_2_) | copy-start | bytes 1572868
  15.7 15.9 %collective-permute-start.9 = (bf16[2,256,256]{2,1,0:T(8,128)(2,1)S(1)}, bf16[2,256,256]{2,1,0:T(8,128)(2,1)S(1)}, u32[]{:S(2)}, u32[]{:S(2)}) collective-permute-start(bf16[2,256,256]{2,1,0:T(8,128)(2,1)S(1)} %constant_dynamic-slice_fusion.1), channel_id=1, source_target_pairs={{0,1},{1,0},{2,3},{3,2},{4,5},{5,4},{6,7},{7,6},{8,9},{9,8},{10,11... | collective-permute-start | bytes 786440 | tf_op jit(solution)/shard_map/ppermute | solution.py:83
  26.1 18.6 %collective-permute-start.7 = (bf16[2,256,512]{2,1,0:T(8,128)(2,1)}, bf16[2,256,512]{2,1,0:T(8,128)(2,1)S(1)}, u32[]{:S(2)}, u32[]{:S(2)}) collective-permute-start(bf16[2,256,512]{2,1,0:T(8,128)(2,1)} %collective-permute-done.5.rest_9_), channel_id=1, source_target_pairs={{0,2},{2,0},{4,6},{6,4},{8,10},{10,8},{12,14},{14,12},{16,18},{18,... | collective-permute-start | bytes 1572872 | tf_op jit(solution)/shard_map/ppermute | solution.py:69
  31.6 20.5 %collective-permute-start.3 = (bf16[2,128,512]{2,1,0:T(8,128)(2,1)}, bf16[2,128,512]{2,1,0:T(8,128)(2,1)S(1)}, u32[]{:S(2)}, u32[]{:S(2)}) collective-permute-start(bf16[2,128,512]{2,1,0:T(8,128)(2,1)} %fusion.1), channel_id=1, source_target_pairs={{0,4},{2,6},{4,0},{6,2},{8,12},{10,14},{12,8},{14,10},{16,20},{18,... | collective-permute-start | bytes 786440 | tf_op jit(solution)/shard_map/ppermute | solution.py:69
  32.5 12.2 %collective-permute-start.10 = (bf16[2,256,256]{2,1,0:T(8,128)(2,1)S(1)}, bf16[2,256,256]{2,1,0:T(8,128)(2,1)S(1)}, u32[]{:S(2)}, u32[]{:S(2)}) collective-permute-start(bf16[2,256,256]{2,1,0:T(8,128)(2,1)S(1)} %collective-permute-done.9.rest_13_.rest_3_), channel_id=1, source_target_pairs={{0,2},{2,0},{4,6},{6,4},{8,10},{10,8},{12,14},{14,12},{16,18},{18,... | collective-permute-start | bytes 786440 | tf_op jit(solution)/shard_map/ppermute | solution.py:69
  34.1 0.9 copy-start.8
  41.5 8.4 %copy-start.10 = (bf16[2,256,1536]{2,1,0:T(8,128)(2,1)}, bf16[2,256,1536]{2,1,0:T(8,128)(2,1)S(1)}, u32[]{:S(2)}) copy-start(bf16[2,256,1536]{2,1,0:T(8,128)(2,1)S(1)} %get-tuple-element.12.rest_0_) | copy-start | bytes 4718596
  41.5 44.3 %collective-permute-start.1 = (bf16[2,256,1536]{2,1,0:T(8,128)(2,1)}, bf16[2,256,1536]{2,1,0:T(8,128)(2,1)}, u32[]{:S(2)}, u32[]{:S(2)}) collective-permute-start(bf16[2,256,1536]{2,1,0:T(8,128)(2,1)} %get-tuple-element.13), channel_id=1, source_target_pairs={{2,3},{3,2},{4,5},{5,4},{10,11},{11,10},{12,13},{13,12},{18,19},{1... | collective-permute-start | bytes 4718600 | tf_op jit(solution)/shard_map/ppermute | solution.py:83
  44.7 5.2 %copy-start.3 = (bf16[2,256,512]{2,1,0:T(8,128)(2,1)}, bf16[2,256,512]{2,1,0:T(8,128)(2,1)S(1)}, u32[]{:S(2)}) copy-start(bf16[2,256,512]{2,1,0:T(8,128)(2,1)S(1)} %collective-permute-done.7.rest_11_.rest_1_) | copy-start | bytes 1572868
  44.7 5.2 %copy-start.6 = (bf16[2,256,256]{2,1,0:T(8,128)(2,1)}, bf16[2,256,256]{2,1,0:T(8,128)(2,1)S(1)}, u32[]{:S(2)}) copy-start(bf16[2,256,256]{2,1,0:T(8,128)(2,1)S(1)} %collective-permute-done.10.rest_14_.rest_4_) | copy-start | bytes 786436
  49.9 10.8 %collective-permute-start.12 = (bf16[2,256,512]{2,1,0:T(8,128)(2,1)}, bf16[2,256,512]{2,1,0:T(8,128)(2,1)}, u32[]{:S(2)}, u32[]{:S(2)}) collective-permute-start(bf16[2,256,512]{2,1,0:T(8,128)(2,1)} %get-tuple-element.18), channel_id=1, source_target_pairs={{2,4},{4,2},{10,12},{12,10},{18,20},{20,18},{26,28},{28,26},{3,5},... | collective-permute-start | bytes 1572872 | tf_op jit(solution)/shard_map/ppermute | solution.py:69
  52.9 10.5 %collective-permute-start.4 = (bf16[2,2,128,512]{3,2,1,0:T(8,128)(2,1)}, bf16[2,2,128,512]{3,2,1,0:T(8,128)(2,1)}, u32[]{:S(2)}, u32[]{:S(2)}) collective-permute-start(bf16[2,2,128,512]{3,2,1,0:T(8,128)(2,1)} %pad_maximum_fusion.rest_5_), channel_id=1, source_target_pairs={{0,2},{2,0},{4,6},{6,4},{8,10},{10,8},{12,14},{14,12},{16,18},{18,... | collective-permute-start | bytes 1572872 | tf_op jit(solution)/shard_map/ppermute | solution.py:69
  52.9 15.6 %collective-permute-start.13 = (bf16[2,256,512]{2,1,0:T(8,128)(2,1)S(1)}, bf16[2,256,512]{2,1,0:T(8,128)(2,1)S(1)}, u32[]{:S(2)}, u32[]{:S(2)}) collective-permute-start(bf16[2,256,512]{2,1,0:T(8,128)(2,1)S(1)} %get-tuple-element.17.rest_0_), channel_id=1, source_target_pairs={{2,3},{3,2},{4,5},{5,4},{10,11},{11,10},{12,13},{13,12},{18,19},{1... | collective-permute-start | bytes 1572872 | tf_op jit(solution)/shard_map/ppermute | solution.py:83
  54.8 19.3 %collective-permute-start.11 = (bf16[2,256,512]{2,1,0:T(8,128)(2,1)S(1)}, bf16[2,256,512]{2,1,0:T(8,128)(2,1)S(1)}, u32[]{:S(2)}, u32[]{:S(2)}) collective-permute-start(bf16[2,256,512]{2,1,0:T(8,128)(2,1)S(1)} %get-tuple-element.17.rest_0_), channel_id=1, source_target_pairs={{2,4},{4,2},{10,12},{12,10},{18,20},{20,18},{26,28},{28,26},{3,5},... | collective-permute-start | bytes 1572872 | tf_op jit(solution)/shard_map/ppermute | solution.py:69
  58.8 28.5 %copy-start.5 = (bf16[2,256,512]{2,1,0:T(8,128)(2,1)S(1)}, bf16[2,256,512]{2,1,0:T(8,128)(2,1)}, u32[]{:S(2)}) copy-start(bf16[2,256,512]{2,1,0:T(8,128)(2,1)} %copy-done.4) | copy-start | bytes 1572868
  58.8 28.5 %copy-start.7 = (bf16[2,256,256]{2,1,0:T(8,128)(2,1)S(1)}, bf16[2,256,256]{2,1,0:T(8,128)(2,1)}, u32[]{:S(2)}) copy-start(bf16[2,256,256]{2,1,0:T(8,128)(2,1)} %copy-done.6) | copy-start | bytes 786436
  58.8 28.5 %copy-start.9 = (s32[512,1]{1,0:T(8,128)S(1)}, s32[512,1]{1,0:T(8,128)}, u32[]{:S(2)}) copy-start(s32[512,1]{1,0:T(8,128)} %copy.6.skel_col_ref.rest_2_) | copy-start | bytes 6148
  60.7 14.7 %collective-permute-start.17 = (bf16[2,256,512]{2,1,0:T(8,128)(2,1)S(1)}, bf16[2,256,512]{2,1,0:T(8,128)(2,1)S(1)}, u32[]{:S(2)}, u32[]{:S(2)}) collective-permute-start(bf16[2,256,512]{2,1,0:T(8,128)(2,1)S(1)} %get-tuple-element.17.rest_0_), channel_id=1, source_target_pairs={{2,0},{4,6},{10,8},{12,14},{18,16},{20,22},{26,24},{28,30},{3,1},{... | collective-permute-start | bytes 1572872 | tf_op jit(solution)/shard_map/ppermute | solution.py:69
  63.4 7.9 %collective-permute-start.15 = (bf16[2,256,256]{2,1,0:T(8,128)(2,1)S(1)}, bf16[2,256,256]{2,1,0:T(8,128)(2,1)S(1)}, u32[]{:S(2)}, u32[]{:S(2)}) collective-permute-start(bf16[2,256,256]{2,1,0:T(8,128)(2,1)S(1)} %constant_dynamic-slice_fusion), channel_id=1, source_target_pairs={{2,3},{3,2},{4,5},{5,4},{10,11},{11,10},{12,13},{13,12},{18,19},{1... | collective-permute-start | bytes 786440 | tf_op jit(solution)/shard_map/ppermute | solution.py:83
  68.5 16.0 %collective-permute-start.14 = (bf16[2,256,512]{2,1,0:T(8,128)(2,1)S(1)}, bf16[2,256,512]{2,1,0:T(8,128)(2,1)S(1)}, u32[]{:S(2)}, u32[]{:S(2)}) collective-permute-start(bf16[2,256,512]{2,1,0:T(8,128)(2,1)S(1)} %collective-permute-done.13.rest_3_), channel_id=1, source_target_pairs={{2,4},{4,2},{10,12},{12,10},{18,20},{20,18},{26,28},{28,26},{3,5},... | collective-permute-start | bytes 1572872 | tf_op jit(solution)/shard_map/ppermute | solution.py:69
  71.3 10.5 %collective-permute-start.16 = (bf16[2,256,256]{2,1,0:T(8,128)(2,1)S(1)}, bf16[2,256,256]{2,1,0:T(8,128)(2,1)S(1)}, u32[]{:S(2)}, u32[]{:S(2)}) collective-permute-start(bf16[2,256,256]{2,1,0:T(8,128)(2,1)S(1)} %collective-permute-done.15.rest_5_), channel_id=1, source_target_pairs={{2,4},{4,2},{10,12},{12,10},{18,20},{20,18},{26,28},{28,26},{3,5},... | collective-permute-start | bytes 786440 | tf_op jit(solution)/shard_map/ppermute | solution.py:69
  74.1 9.0 %collective-permute-start.22 = (bf16[2,256,256]{2,1,0:T(8,128)(2,1)S(1)}, bf16[2,256,256]{2,1,0:T(8,128)(2,1)S(1)}, u32[]{:S(2)}, u32[]{:S(2)}) collective-permute-start(bf16[2,256,256]{2,1,0:T(8,128)(2,1)S(1)} %collective-permute-done.15.rest_5_), channel_id=1, source_target_pairs={{2,0},{4,6},{10,8},{12,14},{18,16},{20,22},{26,24},{28,30},{3,1},{... | collective-permute-start | bytes 786440 | tf_op jit(solution)/shard_map/ppermute | solution.py:69
  75.4 18.9 %collective-permute-start.19 = (bf16[2,256,512]{2,1,0:T(8,128)(2,1)S(1)}, bf16[2,256,512]{2,1,0:T(8,128)(2,1)S(1)}, u32[]{:S(2)}, u32[]{:S(2)}) collective-permute-start(bf16[2,256,512]{2,1,0:T(8,128)(2,1)S(1)} %add.64.rest_2_), channel_id=1, source_target_pairs={{2,0},{4,6},{10,8},{12,14},{18,16},{20,22},{26,24},{28,30},{3,1},{... | collective-permute-start | bytes 1572872 | tf_op jit(solution)/shard_map/ppermute | solution.py:69
  81.8 12.5 %collective-permute-start.18 = (bf16[2,256,512]{2,1,0:T(8,128)(2,1)S(1)}, bf16[2,256,512]{2,1,0:T(8,128)(2,1)S(1)}, u32[]{:S(2)}, u32[]{:S(2)}) collective-permute-start(bf16[2,256,512]{2,1,0:T(8,128)(2,1)S(1)} %collective-permute-done.11.rest_1_), channel_id=1, source_target_pairs={{2,0},{4,6},{10,8},{12,14},{18,16},{20,22},{26,24},{28,30},{3,1},{... | collective-permute-start | bytes 1572872 | tf_op jit(solution)/shard_map/ppermute | solution.py:69
  83.1 11.2 %collective-permute-start.20 = (bf16[2,256,512]{2,1,0:T(8,128)(2,1)S(1)}, bf16[2,256,512]{2,1,0:T(8,128)(2,1)S(1)}, u32[]{:S(2)}, u32[]{:S(2)}) collective-permute-start(bf16[2,256,512]{2,1,0:T(8,128)(2,1)S(1)} %collective-permute-done.13.rest_3_), channel_id=1, source_target_pairs={{2,0},{4,6},{10,8},{12,14},{18,16},{20,22},{26,24},{28,30},{3,1},{... | collective-permute-start | bytes 1572872 | tf_op jit(solution)/shard_map/ppermute | solution.py:69
  84.5 9.9 %collective-permute-start.21 = (bf16[2,256,512]{2,1,0:T(8,128)(2,1)S(1)}, bf16[2,256,512]{2,1,0:T(8,128)(2,1)S(1)}, u32[]{:S(2)}, u32[]{:S(2)}) collective-permute-start(bf16[2,256,512]{2,1,0:T(8,128)(2,1)S(1)} %collective-permute-done.14.rest_4_), channel_id=1, source_target_pairs={{2,0},{4,6},{10,8},{12,14},{18,16},{20,22},{26,24},{28,30},{3,1},{... | collective-permute-start | bytes 1572872 | tf_op jit(solution)/shard_map/ppermute | solution.py:69
  85.8 8.5 %collective-permute-start.23 = (bf16[2,256,256]{2,1,0:T(8,128)(2,1)S(1)}, bf16[2,256,256]{2,1,0:T(8,128)(2,1)S(1)}, u32[]{:S(2)}, u32[]{:S(2)}) collective-permute-start(bf16[2,256,256]{2,1,0:T(8,128)(2,1)S(1)} %collective-permute-done.16.rest_6_), channel_id=1, source_target_pairs={{2,0},{4,6},{10,8},{12,14},{18,16},{20,22},{26,24},{28,30},{3,1},{... | collective-permute-start | bytes 786440 | tf_op jit(solution)/shard_map/ppermute | solution.py:69
  94.3 0.8 copy-start.12
  94.3 1.0 copy-start.11
  94.3 1.1 %copy-start.13 = (bf16[2,256,512]{2,1,0:T(8,128)(2,1)}, bf16[2,256,512]{2,1,0:T(8,128)(2,1)S(1)}, u32[]{:S(2)}) copy-start(bf16[2,256,512]{2,1,0:T(8,128)(2,1)S(1)} %collective-permute-done.20.rest_10_) | copy-start | bytes 1572868
  94.3 1.3 %copy-start.14 = (bf16[2,256,512]{2,1,0:T(8,128)(2,1)}, bf16[2,256,512]{2,1,0:T(8,128)(2,1)S(1)}, u32[]{:S(2)}) copy-start(bf16[2,256,512]{2,1,0:T(8,128)(2,1)S(1)} %collective-permute-done.21.rest_11_) | copy-start | bytes 1572868

commit v2 on v0

v2 whole, which is shorter than its diff:
```python
import jax
import jax.numpy as jnp
from jax import lax
from jax.experimental import pallas as pl
from jax.experimental.pallas import tpu as pltpu
from jax.sharding import PartitionSpec as P

BF16 = jnp.bfloat16
F32 = jnp.float32
VMEM_BYTES = 28 * 1024 * 1024
ROW_CHUNKS = 2


def dot(first, second):
    return jnp.dot(first, second, preferred_element_type=F32)


def stacked(real, imag):
    return jnp.concatenate(
        [jnp.concatenate([real, -imag], axis=1), jnp.concatenate([imag, real], axis=1)], axis=0
    )


def flat(array):
    return array.reshape(array.shape[0] * array.shape[1], array.shape[2])


def column_picker(index, offset, count):
    rows = lax.broadcasted_iota(jnp.int32, (count, index.shape[1]), 0) + offset
    return jnp.where(rows == index, 1.0, 0.0).astype(BF16)


def row_picker(index, offset, count):
    cols = lax.broadcasted_iota(jnp.int32, (index.shape[0], count), 1) + offset
    return jnp.where(cols == index, 1.0, 0.0).astype(BF16)


def call(kernel, scalars, inputs, out_shapes, specs=None, out_specs=None, scratch=(), flops=0, aliases=None):
    specs = specs or [None] * len(inputs)
    out_specs = out_specs or [None] * len(out_shapes)

    def whole(array, spec):
        if spec is not None:
            return spec
        rank = len(array.shape)
        return pl.BlockSpec(array.shape, lambda i, sc: (0,) * rank)

    moved = sum(s.size * s.dtype.itemsize for s in out_shapes)
    return pl.pallas_call(
        kernel,
        grid_spec=pltpu.PrefetchScalarGridSpec(
            num_scalar_prefetch=1, grid=(1,),
            in_specs=[whole(a, s) for a, s in zip(inputs, specs)],
            out_specs=[whole(a, s) for a, s in zip(out_shapes, out_specs)],
            scratch_shapes=list(scratch),
        ),
        out_shape=out_shapes,
        input_output_aliases=aliases or {},
        compiler_params=pltpu.CompilerParams(vmem_limit_bytes=VMEM_BYTES),
        cost_estimate=pl.CostEstimate(flops=flops, bytes_accessed=2 * moved, transcendentals=0),
    )(scalars, *inputs)


def after(array, *others):
    return lax.optimization_barrier((array, *others))[0]


def on_device(leaf_maps, w_first, w_second, skel_first, skel_second):
    box = lax.axis_index("box")
    face = lax.axis_index("face")
    n_box, n_face = lax.axis_size("box"), lax.axis_size("face")
    nf = n_face - 1
    fr = leaf_maps.shape[4]
    hr = fr // 2
    k = leaf_maps.shape[5] // 3
    half = k // 2
    leaf = leaf_maps[:, 0, 0]
    par = box % 2
    par2 = box // 2 % 2
    scalars = jnp.stack([par, par2, face, box % 4]).astype(jnp.int32)
    sds = jax.ShapeDtypeStruct

    def box_permute(array, mask):
        return lax.ppermute(array, "box", [(b, b ^ mask) for b in range(n_box)])

    def keeper(b):
        return (b & 1) != (b >> 1 & 1)

    def giver(b):
        return not keeper(b)

    def face_permute(array, step, senders=None):
        pairs = [
            (b * n_face + f, b * n_face + (f + n_face - step) % n_face)
            for b in range(n_box) if senders is None or senders(b)
            for f in range(n_face)
        ]
        return lax.ppermute(array, ("box", "face"), pairs)

    def over_face(array, senders=None):
        return [face_permute(array, s, senders) for s in range(1, n_face)]

    skel_one = lax.dynamic_index_in_dim(skel_first[0], box // 2, 0, keepdims=True)
    skel_two = lax.dynamic_index_in_dim(skel_second[0], box // 4, 0, keepdims=True)

    def iface_cols(start):
        return lax.dynamic_slice(leaf, (0, 1 - par, 0, start), (2, 1, fr, k)).reshape(2, fr, k)

    end_own = iface_cols(par * k)
    end_far = over_face(end_own, giver)
    sides_raw = iface_cols(2 * k)
    sides_sib = box_permute(sides_raw, 1)
    end_sib = box_permute(end_own, 1)

    def slots_kernel(sc, own_ref, sib_ref, end_ref, skel_ref, skel2_ref,
                     comp_out, col_out, side_out, keep_out, send_out):
        p, q = sc[0], sc[1]
        rows = lax.broadcasted_iota(jnp.int32, (k, k), 0)
        cols = lax.broadcasted_iota(jnp.int32, (k, k), 1)
        skel = jnp.broadcast_to(skel_ref[...].astype(F32), (k, k))
        column = jnp.sum(jnp.where(rows == cols, skel, 0.0), axis=1, keepdims=True)
        col_out[...] = column.astype(jnp.int32)
        place = skel2_ref[...] - q * k
        taken = jnp.where(rows == place, jnp.broadcast_to(column, (k, k)), 0.0)
        comp = jnp.sum(taken, axis=0, keepdims=True).astype(jnp.int32)
        mine = jnp.logical_and(place >= 0, place < k)
        comp = jnp.where(mine, comp, -1)
        comp_out[...] = comp
        pick_own = column_picker(comp, p * k, k)
        pick_sib = column_picker(comp, (1 - p) * k, k)
        side = dot(flat(own_ref[...]), pick_own) + dot(flat(sib_ref[...]), pick_sib)
        side_out[...] = side.astype(BF16).reshape(2, fr, k)
        couple = pl.ds(pl.multiple_of((1 - p) * k, k), k)
        for ref, h in ((keep_out, p), (send_out, 1 - p)):
            take = pl.ds(pl.multiple_of(h * hr, hr), hr)
            for t in range(2):
                ref[t, :, :k] = end_ref[t, take, couple]
                ref[t, :, k:] = dot(end_ref[t, take, 2 * k :], pick_own).astype(BF16)

    comp, skel_col, side, v_keep, v_send = call(
        slots_kernel, scalars, [leaf, sides_sib, leaf, skel_one, skel_two],
        [sds((1, k), jnp.int32), sds((k, 1), jnp.int32), sds((2, fr, k), BF16),
         sds((2, hr, 2 * k), BF16), sds((2, hr, 2 * k), BF16)],
        specs=[pl.BlockSpec((2, None, fr, k), lambda i, sc: (0, 1 - sc[0], 0, 2)), None,
               pl.BlockSpec((2, None, fr, 3 * k), lambda i, sc: (0, sc[0], 0, 0)), None, None],
        flops=12 * fr * k * k,
    )
    side_far = over_face(side, keeper)
    v_recv = box_permute(v_send, 1)

    w_one = jnp.roll(w_first[:, 0], -face * fr, axis=2)
    w_one_sib = box_permute(w_one, 1)
    w_two = jnp.roll(w_second[:, 0], -face * fr, axis=2)
    w_two_pair = jnp.stack([w_two, box_permute(w_two, 2)])
    w_two_sib = box_permute(w_two_pair, 1)

    s_sib = box_permute(leaf[:, 2], 1)
    cr = fr // ROW_CHUNKS

    def rows_kernel(sc, own_ref, sib_ref, end_ref, comp_ref, col_ref, *outs):
        p, q, f = sc[0], sc[1], sc[2]

        @pl.when(p == q)
        def _():
            picker = column_picker(comp_ref[...], p * k, k)
            for t in range(2):
                outs[0][t, :, : 2 * k] = end_ref[t, :, : 2 * k]
                outs[0][t, :, 2 * k :] = dot(end_ref[t, :, 2 * k :], picker).astype(BF16)

        @pl.when(p != q)
        def _():
            pick_own = column_picker(comp_ref[...], p * k, k)
            pick_sib = column_picker(comp_ref[...], (1 - p) * k, k)
            takes = []
            for s in range(n_face):
                start = pl.multiple_of((f + n_face - s) % n_face * fr, fr)
                slots = col_ref[pl.ds(start, fr), :]
                takes.append([row_picker(slots, p * k + f * fr, fr),
                              row_picker(slots, (1 - p) * k + f * fr, fr)])
            take_own = jnp.concatenate([t[0] for t in takes], axis=0)
            take_sib = jnp.concatenate([t[1] for t in takes], axis=0)
            for t in range(2):
                sides = [dot(ref[t, :, 2 * k :], pick).astype(BF16)
                         for ref, pick in ((own_ref, pick_own), (sib_ref, pick_sib))]
                for c in range(3):
                    cols = slice(c * k, (c + 1) * k)
                    own, sib = sides if c == 2 else (own_ref[t, :, cols], sib_ref[t, :, cols])
                    picked = (dot(take_own, own) + dot(take_sib, sib)).astype(BF16)
                    outs[0][t, :, cols] = picked[:fr]
                    for s in range(1, n_face):
                        for i in range(ROW_CHUNKS):
                            lo = s * fr + i * cr
                            outs[1 + (s - 1) * ROW_CHUNKS + i][t, :, cols] = picked[lo : lo + cr]

    def face_block(which):
        return pl.BlockSpec((2, None, fr, 3 * k), lambda i, sc: (0, which(sc), 0, 0))

    kept, *kept_out = call(
        rows_kernel, scalars, [leaf, s_sib, leaf, comp, skel_col],
        [sds((2, fr, 3 * k), BF16)] + [sds((2, cr, 3 * k), BF16)] * (nf * ROW_CHUNKS),
        specs=[face_block(lambda sc: 2), None, face_block(lambda sc: sc[0]), None, None],
        flops=16 * fr * fr * n_face * 3 * k,
    )

    end_fwd = [box_permute(a, 1) for a in end_far]
    side_fwd = [box_permute(a, 1) for a in side_far]
    rest_far = over_face(after(end_own, *side_far), keeper)
    rest_fwd = [box_permute(a, 1) for a in rest_far]

    def hidden_rows(couple, p, own_ref, sib_ref, m):
        lo = pl.ds(pl.multiple_of(p * half, half), half)
        hi = pl.ds(pl.multiple_of((1 - p) * half, half), half)
        both = dot(stacked(couple(0, lo), couple(1, lo)), flat(own_ref[...]))
        both = both + dot(stacked(couple(0, hi), couple(1, hi)), flat(sib_ref[...]))
        both = both.astype(BF16)
        return both[:m], both[m:]

    def piece(hidden, start, count):
        return stacked(hidden[0][:, start : start + count], hidden[1][:, start : start + count])

    def iface_kernel(sc, keep_ref, recv_ref, own_ref, sib_ref, end_ref, endsib_ref, side_ref,
                     acc_out, hid_out, rows):
        p, q = sc[0], sc[1]

        @pl.when(p == q)
        def _():
            rows[...] = recv_ref[...]

        @pl.when(p != q)
        def _():
            rows[...] = keep_ref[...]

        hidden = hidden_rows(lambda t, c: rows[t, :, c], p, own_ref, sib_ref, hr)
        hid_out[0] = hidden[0]
        hid_out[1] = hidden[1]
        left = piece(hidden, 0, fr)
        is_end = p == q
        ends = jnp.where(is_end, end_ref[...], endsib_ref[...])
        acc_out[:, :, :k] = -dot(left, flat(ends)).reshape(2, hr, k)
        acc_out[:, :, k:] = rows[:, :, k:].astype(F32) - dot(left, flat(side_ref[...])).reshape(2, hr, k)

    v_acc, v_hid = call(
        iface_kernel, scalars, [v_keep, v_recv, w_one, w_one_sib, end_own, end_sib, side],
        [sds((2, hr, 2 * k), F32), sds((2, hr, k), BF16)],
        scratch=[pltpu.VMEM((2, hr, 2 * k), BF16)], flops=8 * hr * k * 2 * k,
    )

    def iface_far_kernel(sc, acc_ref, hid_ref, *rest):
        far, fwd, side_f, side_w = (rest[i * nf : (i + 1) * nf] for i in range(4))
        end_out, side_out = rest[4 * nf :]
        hidden = [hid_ref[0], hid_ref[1]]
        end = acc_ref[:, :, :k]
        side = acc_ref[:, :, k:]
        for s in range(nf):
            left = piece(hidden, (s + 1) * fr, fr)
            end = end - dot(left, flat(far[s][...] + fwd[s][...])).reshape(2, hr, k)
            side = side - dot(left, flat(side_f[s][...] + side_w[s][...])).reshape(2, hr, k)
        end_out[...] = end.astype(BF16)
        side_out[...] = side.astype(BF16)

    two_end, two_side = call(
        iface_far_kernel, scalars, [v_acc, v_hid, *end_far, *end_fwd, *side_far, *side_fwd],
        [sds((2, hr, k), BF16)] * 2, flops=8 * hr * k * k,
    )

    side_x = box_permute(two_side, 2)
    end_y = over_face(two_end)
    end_x = box_permute(two_end, 2)

    def half_slots(array):
        return lax.dynamic_slice(array, (0, 0, par2 * half), (2, hr, half))

    half_y = over_face(half_slots(two_side) + half_slots(side_x))
    end_xy = [box_permute(a, 2) for a in end_y]
    half_xy = [box_permute(a, 2) for a in half_y]

    def join_kernel(sc, end_ref, endx_ref, side_ref, sidex_ref, out_ref):
        q = sc[1]
        out_ref[:, :, pl.ds(pl.multiple_of(q * k, k), k)] = end_ref[...]
        out_ref[:, :, pl.ds(pl.multiple_of((1 - q) * k, k), k)] = endx_ref[...]
        out_ref[:, :, 2 * k :] = side_ref[...] + sidex_ref[...]

    def join_far_kernel(sc, end_ref, endx_ref, side_ref, sidex_ref, out_ref):
        q = sc[1]
        out_ref[:, :, pl.ds(pl.multiple_of(q * k, k), k)] = end_ref[...]
        out_ref[:, :, pl.ds(pl.multiple_of((1 - q) * k, k), k)] = endx_ref[...]
        out_ref[:, :, pl.ds(pl.multiple_of(2 * k + q * half, half), half)] = side_ref[...]
        out_ref[:, :, pl.ds(pl.multiple_of(2 * k + (1 - q) * half, half), half)] = sidex_ref[...]

    two_shape = [sds((2, hr, 3 * k), BF16)]
    two_rows = call(join_kernel, scalars, [two_end, end_x, two_side, side_x], two_shape)
    for s in range(nf):
        two_rows += call(join_far_kernel, scalars, [end_y[s], end_xy[s], half_y[s], half_xy[s]], two_shape)
    two_sib = [box_permute(a, 1) for a in two_rows]

    def gather_kernel(sc, own_ref, sib_ref, side_ref, *rest):
        far, fwd, rfar, rfwd, sfar, sfwd = (rest[i * nf : (i + 1) * nf] for i in range(6))
        out_ref = rest[6 * nf]
        p, q = sc[0], sc[1]

        def block(which):
            return pl.ds(pl.multiple_of(which * k, k), k)

        out_ref[0, :, :, block(p)] = own_ref[...]
        out_ref[0, :, :, block(1 - p)] = sib_ref[...]
        out_ref[0, :, :, 2 * k :] = side_ref[...]
        for s in range(nf):
            out_ref[s + 1, :, :, block(q)] = far[s][...] + fwd[s][...]
            out_ref[s + 1, :, :, block(1 - q)] = rfar[s][...] + rfwd[s][...]
            out_ref[s + 1, :, :, 2 * k :] = sfar[s][...] + sfwd[s][...]

    (iface,) = call(
        gather_kernel, scalars,
        [end_own, end_sib, side, *end_far, *end_fwd, *rest_far, *rest_fwd, *side_far, *side_fwd],
        [sds((n_face, 2, fr, 3 * k), BF16)],
    )

    def keep_kernel(chunk, sc, *refs):
        kept_ref, refs = refs[0], refs[1:]
        far, refs = refs[:nf], refs[nf:]
        col_ref, own_ref, sib_ref, w2_ref, w2sib_ref, iface_ref = refs[:6]
        mine, sibs = refs[6 : 6 + n_face], refs[6 + n_face : 6 + 2 * n_face]
        out_ref, hid, w2 = refs[-3:]
        p, q, f, r = sc[0], sc[1], sc[2], sc[3]
        is_end = p == q

        def rows(t, c):
            total = kept_ref[t, :, c * k : (c + 1) * k]
            for z in far:
                total = total + z[t, :, c * k : (c + 1) * k]
            return total

        slots = col_ref[pl.ds(pl.multiple_of(f * fr + chunk * cr, cr), cr), :]
        right = jnp.where(slots >= k, 1, 0)
        right = jnp.where(is_end, p, right) > 0
        lefts = [rows(t, 0) for t in range(2)]
        rights = [rows(t, 1) for t in range(2)]
        couple = [jnp.where(right, a, b) for a, b in zip(lefts, rights)]

        def columns(t, which):
            return jnp.where(which == 0, couple[t][:, :half], couple[t][:, half:])

        own = stacked(columns(0, p), columns(1, p))
        sib = stacked(columns(0, 1 - p), columns(1, 1 - p))
        both = (dot(own, flat(own_ref[...])) + dot(sib, flat(sib_ref[...]))).astype(BF16)
        hidden = both[:cr], both[cr:]
        nothing = jnp.zeros((cr, k), BF16)
        start = [
            jnp.concatenate([jnp.where(right, nothing, a) for a in lefts], axis=0),
            jnp.concatenate([jnp.where(right, a, nothing) for a in rights], axis=0),
            jnp.concatenate([rows(t, 2) for t in range(2)], axis=0),
        ]
        merged = []
        for c in range(3):
            total = start[c].astype(F32)
            for s in range(n_face):
                total = total - dot(piece(hidden, s * fr, fr), flat(iface_ref[s, :, :, c * k : (c + 1) * k]))
            merged.append(total.astype(BF16))
        is_left = q == 0
        blk = k // 4
        for i, (ref, part) in enumerate(((w2_ref, 0), (w2_ref, 1), (w2sib_ref, 0), (w2sib_ref, 1))):
            place = r ^ (part * 2) ^ (i // 2)
            for t in range(2):
                w2[t, pl.ds(pl.multiple_of(place * blk, blk), blk), :] = ref[part, t]
        couple2 = jnp.where(is_left, merged[1], merged[0])
        second = dot(stacked(couple2[:cr], couple2[cr:]), flat(w2[...])).astype(BF16)
        for s in range(n_face):
            for h in range(2):
                hid[s * 2 + h] = piece((second[:cr], second[cr:]), s * fr + h * hr, hr)
        none = jnp.zeros_like(merged[0])
        first = [jnp.where(is_left, merged[0], none), jnp.where(is_left, none, merged[1]), merged[2]]
        for c in range(3):
            cols = slice(c * k, (c + 1) * k)
            total = first[c].astype(F32)
            for s in range(n_face):
                total = total - dot(hid[s * 2 + p], flat(mine[s][:, :, cols]))
                total = total - dot(hid[s * 2 + 1 - p], flat(sibs[s][:, :, cols]))
            total = total.astype(BF16)
            out_ref[0, 0, :, cols] = total[:cr]
            out_ref[1, 0, :, cols] = total[cr:]

    out = None
    sent = rest_far
    chunks = []
    for i in range(ROW_CHUNKS):
        outgoing = [kept_out[(s - 1) * ROW_CHUNKS + i] for s in range(1, n_face)]
        outgoing = [after(a, *sent) for a in outgoing]
        sent = [face_permute(a, s + 1, keeper) for s, a in enumerate(outgoing)]
        chunks.append(sent)
    for i in range(ROW_CHUNKS):
        inputs = [kept, *chunks[i], skel_col, w_one, w_one_sib, w_two_pair, w_two_sib, iface, *two_rows, *two_sib]
        specs = [pl.BlockSpec((2, cr, 3 * k), lambda g, sc, i=i: (0, i, 0))]
        specs += [None] * (len(inputs) - 1)
        aliases = None
        if out is not None:
            inputs.append(out)
            specs.append(pl.BlockSpec(memory_space=pl.ANY))
            aliases = {len(inputs): 0}
        (out,) = call(
            lambda sc, *refs, i=i: keep_kernel(i, sc, *refs), scalars, inputs,
            [sds((2, 1, fr, 3 * k), BF16)], specs=specs,
            out_specs=[pl.BlockSpec((2, 1, cr, 3 * k), lambda g, sc, i=i: (0, 0, i, 0))],
            scratch=[pltpu.VMEM((2 * n_face, 2 * cr, 2 * hr), BF16), pltpu.VMEM((2, k, k), BF16)],
            flops=8 * cr * k * 8 * k, aliases=aliases,
        )
    return out


def solution(mesh):
    return jax.shard_map(
        on_device,
        mesh=mesh,
        in_specs=(
            P(None, None, "box", None, "face", None),
            P(None, None, "box", None),
            P(None, None, "box", None),
            P(),
            P(),
        ),
        out_specs=P(None, None, ("box", "face"), None),
        check_vma=False,
    )
```

time: 232 us -> 87.2 us (0.38)
  waiting for transfers between devices: 160 us -> 28 us
  Pallas kernels: 0 us -> 25.3 us
  other arithmetic: 23.8 us -> 2.49 us
  matrix products: 20.3 us -> 0 us
  starting transfers between devices: 3.54 us -> 21.6 us
  between operations: 13.5 us -> 0.46 us
    all_gather x2 -> x0, waiting for transfers between devices: 61 us -> none  [merge_rows(): lax.all_gather(chosen, 'face', axis=2, tiled=True)]
    reduce_scatter x1 -> x0, waiting for transfers between devices: 43.3 us -> none  [select_rows(): lax.psum_scatter(picked_rows.astype(jnp.bfloat16).astype(jnp.bfloat16), '...]
    ppermute x7 -> x23, waiting for transfers between devices: 55.6 us -> 28 us  [the longest x7 22.9 us: face_permute(): return lax.ppermute(array, ('box', 'face'), pairs)]
    pallas_call x0 -> x9, Pallas kernels: none -> 25.3 us  [call(): pl.pallas_call(kernel, grid_spec=pltpu.PrefetchScalarGridSpec(num_scalar_...]
    dot_general x21 -> x0, matrix products: 20.3 us -> none  [the longest x16 12.3 us: real_dot(): jnp.einsum('trk,tkc->trc', first_op, second_op, preferred_element_type=jn...]
    ppermute x7 -> x23, starting transfers between devices: 3.27 us -> 21.6 us  [the longest x7 16.5 us: face_permute(): return lax.ppermute(array, ('box', 'face'), pairs)]
    select_n x9 -> x0, other arithmetic: 13.1 us -> none  [the longest x2 5.81 us: merge_rows(): own_left = jnp.where(parity == 0, rows_own, nothing)]
    concatenate x8 -> x2, other arithmetic: 8.21 us -> 1.24 us  [the longest x1 1.05 us: on_device(): w_two = jnp.roll(w_second[:, 0], -face * fr, axis=2)]
  transfers between devices with their start and end apart: 10 -> 23, of which waited for: 8 -> 6; matrix products, arithmetic and copies ran while one was open for 9% -> 7% of each run, Pallas kernels for 0% -> 24%
where the time goes in v2:
time: 87.2 us; the launch traced here: 86.6 us
  waiting for transfers between devices  28 us (32%)
  Pallas kernels  25.3 us (29%)
  starting transfers between devices  21.6 us (25%)
  local copies, waits for them, and re-layouts  8.86 us (10%)
  other arithmetic  2.49 us (3%)
    pallas_call x9, Pallas kernels, call(): pl.pallas_call(kernel, grid_spec=pltpu.PrefetchScalarGridSpec(num_scalar_...  25.3 us
    ppermute x7, waiting for transfers between devices, face_permute(): return lax.ppermute(array, ('box', 'face'), pairs)  22.9 us
    ppermute x7, starting transfers between devices, face_permute(): return lax.ppermute(array, ('box', 'face'), pairs)  16.5 us
    ppermute x16, starting transfers between devices, box_permute(): return lax.ppermute(array, 'box', [(b, b ^ mask) for b in range(n_box)])  5.12 us
    ppermute x16, waiting for transfers between devices, box_permute(): return lax.ppermute(array, 'box', [(b, b ^ mask) for b in range(n_box)])  5.09 us
    unnamed x38, local copies, waits for them, and re-layouts  3.3 us
    squeeze x1, local copies, waits for them, and re-layouts, on_device(): s_sib = box_permute(leaf[:, 2], 1)  2.71 us
    reshape x1, local copies, waits for them, and re-layouts, iface_cols(): lax.dynamic_slice(leaf, (0, 1 - par, 0, start), (2, 1, fr, k))  2.12 us
  transfers between devices with their start and end apart: 23, of which 6 were waited for; matrix products, arithmetic and copies ran while one was open for 7% of the time, Pallas kernels for 24%

profile of v2, /device:TPU:1, one launch (start us, length us, event | category | flops | bytes accessed | tf_op | source)
XLA Modules:
  0.0 86.6 jit_solution(4187962499625926689)
XLA Ops:
  0.0 2.1 %dynamic-slice_bitcast_fusion = (bf16[2,256,512]{2,1,0:T(8,128)(2,1)}, bf16[2,256,512]{2,1,0:T(8,128)(2,1)S(1)}) fusion(bf16[2,1,1,3,256,1536]{5,4,3,2,1,0:T(8,128)(2,1)} %param.5, s32[]{:T(128)S(6)} %select_n.64, s32[]{:T(128)S(6)} %select_n.68), kind=kLoop, calls=%fused_computation.7 | loop fusion | bytes 2097160 | tf_op jit(solution)/shard_map/reshape | solution.py:107
  2.1 0.1 collective-permute-start.1
  2.2 2.7 %slice_bitcast_fusion = bf16[2,256,1536]{2,1,0:T(8,128)(2,1)} fusion(bf16[2,3,256,1536]{3,2,1,0:T(8,128)(2,1)} %bitcast.20), kind=kLoop, calls=%fused_computation | loop fusion | bytes 3145728 | tf_op jit(solution)/shard_map/squeeze | solution.py:157
  4.9 0.5 collective-permute-start
  5.4 0.2 fusion.own_ref.refs_3_
  5.5 0.1 collective-permute-start.6
  5.7 0.7 collective-permute-start.10
  6.4 0.1 pad_add_fusion.sc
  6.5 0.7 fusion.2
  7.2 0.0 collective-permute-done.1.sib_ref
  7.2 0.0 copy-start
  7.2 2.3 %copy-done = bf16[2,1,1,3,256,1536]{5,4,3,2,1,0:T(8,128)(2,1)S(1)} copy-done((bf16[2,1,1,3,256,1536]{5,4,3,2,1,0:T(8,128)(2,1)S(1)}, bf16[2,1,1,3,256,1536]{5,4,3,2,1,0:T(8,128)(2,1)}, u32[]{:S(2)}) %copy-start) | copy-done | bytes 4718616
  9.6 1.8 %shard_map.55 = (s32[1,512]{1,0:T(1,128)S(1)}, s32[512,1]{1,0:T(8,128)S(1)}, bf16[2,256,512]{2,1,0:T(8,128)(2,1)S(1)}, bf16[2,128,1024]{2,1,0:T(8,128)(2,1)S(1)}, bf16[2,128,1024]{2,1,0:T(8,128)(2,1)S(1)}) custom-call(s32[4]{0:T(128)S(1)} %pad_add_fusion.sc, bf16[2,3,256,1536]{3,2,1,0:T(8,128)(2,1)S(1)} %bitcast.21, ...), custom_call_target="tpu_custom_call" | custom-call | flops 805306368 | bytes 3153920 | tf_op jit(solution)/shard_map/pallas_call | solution.py:49
  11.4 4.6 %collective-permute-start.2 = (bf16[2,256,512]{2,1,0:T(8,128)(2,1)S(1)}, bf16[2,256,512]{2,1,0:T(8,128)(2,1)S(1)}, u32[]{:S(2)}, u32[]{:S(2)}) collective-permute-start(bf16[2,256,512]{2,1,0:T(8,128)(2,1)S(1)} %get-tuple-element.25.side_ref), channel_id=1, source_target_pairs={{2,3},{3,2},{4,5},{5,4},{10,11},{11,10},{12,13},{13,12},{18,19},{1... | collective-permute-start | bytes 1572872 | tf_op jit(solution)/shard_map/ppermute | solution.py:98
  16.0 0.4 collective-permute-start.9
  16.4 0.2 collective-permute-start.14
  16.6 1.5 %collective-permute-start.11 = (bf16[2,256,512]{2,1,0:T(8,128)(2,1)S(1)}, bf16[2,256,512]{2,1,0:T(8,128)(2,1)S(1)}, u32[]{:S(2)}, u32[]{:S(2)}) collective-permute-start(bf16[2,256,512]{2,1,0:T(8,128)(2,1)S(1)} %collective-permute-done.10.rest_0_), channel_id=1, source_target_pairs={{0,2},{2,0},{4,6},{6,4},{8,10},{10,8},{12,14},{14,12},{16,18},{18,... | collective-permute-start | bytes 1572872 | tf_op jit(solution)/shard_map/ppermute | solution.py:84
  18.1 4.7 %collective-permute-done.2.rest_4_.rest_2_ = bf16[2,256,512]{2,1,0:T(8,128)(2,1)S(1)} collective-permute-done((bf16[2,256,512]{2,1,0:T(8,128)(2,1)S(1)}, bf16[2,256,512]{2,1,0:T(8,128)(2,1)S(1)}, u32[]{:S(2)}, u32[]{:S(2)}) %collective-permute-start.2) | collective-permute-done | bytes 524320 | tf_op jit(solution)/shard_map/ppermute | solution.py:98
  22.9 3.6 %collective-permute-start.3 = (bf16[2,256,512]{2,1,0:T(8,128)(2,1)}, bf16[2,256,512]{2,1,0:T(8,128)(2,1)}, u32[]{:S(2)}, u32[]{:S(2)}) collective-permute-start(bf16[2,256,512]{2,1,0:T(8,128)(2,1)} %get-tuple-element.26.own_ref.end_ref), channel_id=1, source_target_pairs={{2,3},{3,2},{4,5},{5,4},{10,11},{11,10},{12,13},{13,12},{18,19},{1... | collective-permute-start | bytes 1572872 | tf_op jit(solution)/shard_map/ppermute | solution.py:98
  26.5 2.4 %shard_map.58 = (f32[2,128,1024]{2,1,0:T(8,128)S(1)}, bf16[2,128,512]{2,1,0:T(8,128)(2,1)S(1)}) custom-call(s32[4]{0:T(128)S(1)} %pad_add_fusion.sc, bf16[2,128,1024]{2,1,0:T(8,128)(2,1)S(1)} %get-tuple-element.29.keep_ref, bf16[2,128,1024]{2,1,0:T(8,128)(2,1)S(1)} %collective-permute-done.14.recv_ref, bf16[2,256,512]{2,1,0:T(8,128)(2,1)S(1)} %fusion.own_ref.refs_3_, ...), custom_call_target="tpu_custom_call" | custom-call | flops 536870912 | bytes 2621440 | tf_op jit(solution)/shard_map/pallas_call | solution.py:49
  29.0 1.7 %shard_map.59 = (bf16[2,128,512]{2,1,0:T(8,128)(2,1)}, bf16[2,128,512]{2,1,0:T(8,128)(2,1)}) custom-call(s32[4]{0:T(128)S(1)} %pad_add_fusion.sc, f32[2,128,1024]{2,1,0:T(8,128)S(1)} %get-tuple-element.31.acc_ref, bf16[2,128,512]{2,1,0:T(8,128)(2,1)S(1)} %get-tuple-element.32.hid_ref, bf16[2,256,512]{2,1,0:T(8,128)(2,1)S(1)} %collective-permute-done.10.rest_0_, ...), custom_call_target="tpu_custom_call" | custom-call | flops 268435456 | bytes 1048576 | tf_op jit(solution)/shard_map/pallas_call | solution.py:49
  30.7 0.1 collective-permute-start.16
  30.9 5.3 %shard_map.56 = (bf16[2,256,1536]{2,1,0:T(8,128)(2,1)S(1)}, bf16[2,128,1536]{2,1,0:T(8,128)(2,1)}, bf16[2,128,1536]{2,1,0:T(8,128)(2,1)S(1)}) custom-call(s32[4]{0:T(128)S(1)} %pad_add_fusion.sc, bf16[2,3,256,1536]{3,2,1,0:T(8,128)(2,1)S(1)} %bitcast.25, bf16[2,256,1536]{2,1,0:T(8,128)(2,1)} %collective-permute-done.sib_ref, ...), custom_call_target="tpu_custom_call" | custom-call | flops 3221225472 | bytes 6291456 | tf_op jit(solution)/shard_map/pallas_call | solution.py:49
  36.2 0.9 %copy-done.13 = bf16[2,128,1536]{2,1,0:T(8,128)(2,1)} copy-done((bf16[2,128,1536]{2,1,0:T(8,128)(2,1)}, bf16[2,128,1536]{2,1,0:T(8,128)(2,1)S(1)}, u32[]{:S(2)}) %copy-start.13) | copy-done | bytes 786456
  37.1 3.1 %collective-permute-start.4 = (bf16[2,128,1536]{2,1,0:T(8,128)(2,1)}, bf16[2,128,1536]{2,1,0:T(8,128)(2,1)}, u32[]{:S(2)}, u32[]{:S(2)}) collective-permute-start(bf16[2,128,1536]{2,1,0:T(8,128)(2,1)} %get-tuple-element.27), channel_id=1, source_target_pairs={{2,3},{3,2},{4,5},{5,4},{10,11},{11,10},{12,13},{13,12},{18,19},{1... | collective-permute-start | bytes 2359304 | tf_op jit(solution)/shard_map/ppermute | solution.py:98
  40.3 0.3 collective-permute-start.17
  40.6 1.0 %dynamic-slice_add_fusion = bf16[2,128,256]{2,1,0:T(8,128)(2,1)S(1)} fusion(bf16[2,128,512]{2,1,0:T(8,128)(2,1)} %collective-permute-done.16.sidex_ref, s32[]{:T(128)S(6)} %select_n.71, bf16[2,128,512]{2,1,0:T(8,128)(2,1)} %get-tuple-element.34.side_ref), kind=kLoop, calls=%fused_computation.10 | loop fusion | flops 262144 | bytes 393220 | tf_op jit(solution)/shard_map/add | solution.py:273
  41.6 1.3 %collective-permute-start.19 = (bf16[2,128,256]{2,1,0:T(8,128)(2,1)S(1)}, bf16[2,128,256]{2,1,0:T(8,128)(2,1)S(1)}, u32[]{:S(2)}, u32[]{:S(2)}) collective-permute-start(bf16[2,128,256]{2,1,0:T(8,128)(2,1)S(1)} %dynamic-slice_add_fusion), channel_id=1, source_target_pairs={{0,1},{1,0},{2,3},{3,2},{4,5},{5,4},{6,7},{7,6},{8,9},{9,8},{10,11... | collective-permute-start | bytes 393224 | tf_op jit(solution)/shard_map/ppermute | solution.py:98
  42.9 14.2 %collective-permute-done.17.end_ref = bf16[2,128,512]{2,1,0:T(8,128)(2,1)S(1)} collective-permute-done((bf16[2,128,512]{2,1,0:T(8,128)(2,1)}, bf16[2,128,512]{2,1,0:T(8,128)(2,1)S(1)}, u32[]{:S(2)}, u32[]{:S(2)}) %collective-permute-start.17) | collective-permute-done | bytes 262176 | tf_op jit(solution)/shard_map/ppermute | solution.py:98
  57.1 1.7 %collective-permute-done.19.side_ref = bf16[2,128,256]{2,1,0:T(8,128)(2,1)S(1)} collective-permute-done((bf16[2,128,256]{2,1,0:T(8,128)(2,1)S(1)}, bf16[2,128,256]{2,1,0:T(8,128)(2,1)S(1)}, u32[]{:S(2)}, u32[]{:S(2)}) %collective-permute-start.19) | collective-permute-done | bytes 131104 | tf_op jit(solution)/shard_map/ppermute | solution.py:98
  58.8 1.1 %fusion.1 = bf16[2,128,512]{2,1,0:T(8,128)(2,1)S(1)} fusion(s32[]{:T(128)S(6)} %select_n.70, bf16[2,128,512]{2,1,0:T(8,128)(2,1)} %bitcast.27), kind=kLoop, calls=%fused_computation.9 | loop fusion | flops 524288 | bytes 524292 | tf_op jit(solution)/shard_map/jit(_roll_dynamic)/concatenate | solution.py:153
  59.8 0.0 copy-start.15
  59.8 1.5 %collective-permute-start.7 = (bf16[2,128,512]{2,1,0:T(8,128)(2,1)S(1)}, bf16[2,128,512]{2,1,0:T(8,128)(2,1)S(1)}, u32[]{:S(2)}, u32[]{:S(2)}) collective-permute-start(bf16[2,128,512]{2,1,0:T(8,128)(2,1)S(1)} %fusion.1), channel_id=1, source_target_pairs={{0,4},{2,6},{4,0},{6,2},{8,12},{10,14},{12,8},{14,10},{16,20},{18,... | collective-permute-start | bytes 786440 | tf_op jit(solution)/shard_map/ppermute | solution.py:84
  61.4 1.7 %shard_map.60.refs_8_ = bf16[2,128,1536]{2,1,0:T(8,128)(2,1)S(1)} custom-call(s32[4]{0:T(128)S(1)} %pad_add_fusion.sc, bf16[2,128,512]{2,1,0:T(8,128)(2,1)} %get-tuple-element.33.end_ref, bf16[2,128,512]{2,1,0:T(8,128)(2,1)S(1)} %collective-permute-done.15.endx_ref, bf16[2,128,512]{2,1,0:T(8,128)(2,1)} %get-tuple-element.34.side_ref, ...), custom_call_target="tpu_custom_call" | custom-call | bytes 1572864 | tf_op jit(solution)/shard_map/pallas_call | solution.py:49
  63.2 0.1 collective-permute-start.21
  63.2 2.2 %collective-permute-done.18.endx_ref = bf16[2,128,512]{2,1,0:T(8,128)(2,1)S(1)} collective-permute-done((bf16[2,128,512]{2,1,0:T(8,128)(2,1)S(1)}, bf16[2,128,512]{2,1,0:T(8,128)(2,1)S(1)}, u32[]{:S(2)}, u32[]{:S(2)}) %collective-permute-start.18) | collective-permute-done | bytes 262176 | tf_op jit(solution)/shard_map/ppermute | solution.py:84
  65.5 2.8 %collective-permute-done.20.sidex_ref = bf16[2,128,256]{2,1,0:T(8,128)(2,1)S(1)} collective-permute-done((bf16[2,128,256]{2,1,0:T(8,128)(2,1)S(1)}, bf16[2,128,256]{2,1,0:T(8,128)(2,1)S(1)}, u32[]{:S(2)}, u32[]{:S(2)}) %collective-permute-start.20) | collective-permute-done | bytes 131104 | tf_op jit(solution)/shard_map/ppermute | solution.py:84
  68.3 0.6 shard_map.61.refs_9_
  68.9 0.1 collective-permute-start.22
  69.0 0.1 fusion.4
  69.1 0.5 collective-permute-start.12
  69.6 2.8 %collective-permute-start.5 = (bf16[2,128,1536]{2,1,0:T(8,128)(2,1)S(1)}, bf16[2,128,1536]{2,1,0:T(8,128)(2,1)S(1)}, u32[]{:S(2)}, u32[]{:S(2)}) collective-permute-start(bf16[2,128,1536]{2,1,0:T(8,128)(2,1)S(1)} %copy-done.14), channel_id=1, source_target_pairs={{2,3},{3,2},{4,5},{5,4},{10,11},{11,10},{12,13},{13,12},{18,19},{1... | collective-permute-start | bytes 2359304 | tf_op jit(solution)/shard_map/ppermute | solution.py:98
  72.5 0.1 pad_maximum_fusion.refs_5_
  72.5 0.1 collective-permute-start.8
  72.7 2.0 %shard_map.57.refs_7_ = bf16[2,2,256,1536]{3,2,1,0:T(8,128)(2,1)S(1)} custom-call(s32[4]{0:T(128)S(1)} %pad_add_fusion.sc, bf16[2,256,512]{2,1,0:T(8,128)(2,1)} %get-tuple-element.26.own_ref.end_ref, bf16[2,256,512]{2,1,0:T(8,128)(2,1)S(1)} %copy-done.8, bf16[2,256,512]{2,1,0:T(8,128)(2,1)S(1)} %copy-done.4, bf16[2,256,512]{2,1,0:T(8,128)(2,1)S(1)} %copy-done.2, ...), custom_call_target="tpu_custom_call" | custom-call | bytes 6291456 | tf_op jit(solution)/shard_map/pallas_call | solution.py:49
  74.7 5.4 %shard_map.62.refs_12_ = bf16[2,1,256,1536]{3,2,1,0:T(8,128)(2,1)} custom-call(s32[4]{0:T(128)S(1)} %pad_add_fusion.sc, bf16[2,256,1536]{2,1,0:T(8,128)(2,1)S(1)} %get-tuple-element.22.refs_0_, bf16[2,128,1536]{2,1,0:T(8,128)(2,1)} %collective-permute-done.4.refs_1_, s32[512,1]{1,0:T(8,128)S(1)} %get-tuple-element.21.col_ref.refs_2_, ...), custom_call_target="tpu_custom_call" | custom-call | flops 2147483648 | bytes 3145728 | tf_op jit(solution)/shard_map/pallas_call | solution.py:49
  80.1 2.2 %collective-permute-done.5.refs_1_ = bf16[2,128,1536]{2,1,0:T(8,128)(2,1)S(1)} collective-permute-done((bf16[2,128,1536]{2,1,0:T(8,128)(2,1)S(1)}, bf16[2,128,1536]{2,1,0:T(8,128)(2,1)S(1)}, u32[]{:S(2)}, u32[]{:S(2)}) %collective-permute-start.5) | collective-permute-done | bytes 786464 | tf_op jit(solution)/shard_map/ppermute | solution.py:98
  82.4 4.3 %shard_map.63 = bf16[2,1,256,1536]{3,2,1,0:T(8,128)(2,1)} custom-call(s32[4]{0:T(128)S(1)} %pad_add_fusion.sc, bf16[2,256,1536]{2,1,0:T(8,128)(2,1)S(1)} %get-tuple-element.22.refs_0_, bf16[2,128,1536]{2,1,0:T(8,128)(2,1)S(1)} %collective-permute-done.5.refs_1_, s32[512,1]{1,0:T(8,128)S(1)} %get-tuple-element.21.col_ref.refs_2_, ...), custom_call_target="tpu_custom_call", output_to_operand_aliasing={{}: (13, {})} | custom-call | flops 2147483648 | bytes 3145728 | tf_op jit(solution)/shard_map/pallas_call | solution.py:49
  (55 shorter events, 0.1 us)
Async XLA Ops:
  2.1 5.1 %collective-permute-start.1 = (bf16[2,256,512]{2,1,0:T(8,128)(2,1)S(1)}, bf16[2,256,512]{2,1,0:T(8,128)(2,1)S(1)}, u32[]{:S(2)}, u32[]{:S(2)}) collective-permute-start(bf16[2,256,512]{2,1,0:T(8,128)(2,1)S(1)} %get-tuple-element.36), channel_id=1, source_target_pairs={{0,2},{2,0},{4,6},{6,4},{8,10},{10,8},{12,14},{14,12},{16,18},{18,... | collective-permute-start | bytes 1572872 | tf_op jit(solution)/shard_map/ppermute | solution.py:84
  2.2 3.2 %copy-start.16 = (bf16[2,1,256,512]{3,2,1,0:T(8,128)(2,1)S(1)}, bf16[2,1,256,512]{3,2,1,0:T(8,128)(2,1)}, u32[]{:S(2)}) copy-start(bf16[2,1,256,512]{3,2,1,0:T(8,128)(2,1)} %param.6) | copy-start | bytes 1572868
  4.9 26.0 %collective-permute-start = (bf16[2,256,1536]{2,1,0:T(8,128)(2,1)}, bf16[2,256,1536]{2,1,0:T(8,128)(2,1)}, u32[]{:S(2)}, u32[]{:S(2)}) collective-permute-start(bf16[2,256,1536]{2,1,0:T(8,128)(2,1)} %slice_bitcast_fusion), channel_id=1, source_target_pairs={{0,2},{2,0},{4,6},{6,4},{8,10},{10,8},{12,14},{14,12},{16,18},{18,... | collective-permute-start | bytes 4718600 | tf_op jit(solution)/shard_map/ppermute | solution.py:84
  5.4 25.5 %slice-start = ((s8[4718592]{0:T(1024)(128)(4,1)}), s8[524288]{0:T(1024)(128)(4,1)S(1)}, s32[]{:S(2)}) async-start(s8[4718592]{0:T(1024)(128)(4,1)} %bitcast.23), calls=%async_computation | async-start | bytes 1048576
  5.5 10.9 %collective-permute-start.6 = (bf16[2,256,512]{2,1,0:T(8,128)(2,1)S(1)}, bf16[2,256,512]{2,1,0:T(8,128)(2,1)S(1)}, u32[]{:S(2)}, u32[]{:S(2)}) collective-permute-start(bf16[2,256,512]{2,1,0:T(8,128)(2,1)S(1)} %fusion.own_ref.refs_3_), channel_id=1, source_target_pairs={{0,2},{2,0},{4,6},{6,4},{8,10},{10,8},{12,14},{14,12},{16,18},{18,... | collective-permute-start | bytes 1572872 | tf_op jit(solution)/shard_map/ppermute | solution.py:84
  5.7 10.9 %collective-permute-start.10 = (bf16[2,256,512]{2,1,0:T(8,128)(2,1)}, bf16[2,256,512]{2,1,0:T(8,128)(2,1)S(1)}, u32[]{:S(2)}, u32[]{:S(2)}) collective-permute-start(bf16[2,256,512]{2,1,0:T(8,128)(2,1)} %get-tuple-element.26.own_ref.end_ref), channel_id=1, source_target_pairs={{0,1},{1,0},{6,7},{7,6},{8,9},{9,8},{14,15},{15,14},{16,17},{17,16... | collective-permute-start | bytes 1572872 | tf_op jit(solution)/shard_map/ppermute | solution.py:98
  7.2 2.3 %copy-start = (bf16[2,1,1,3,256,1536]{5,4,3,2,1,0:T(8,128)(2,1)S(1)}, bf16[2,1,1,3,256,1536]{5,4,3,2,1,0:T(8,128)(2,1)}, u32[]{:S(2)}) copy-start(bf16[2,1,1,3,256,1536]{5,4,3,2,1,0:T(8,128)(2,1)} %param.5) | copy-start | bytes 14155780
  9.6 21.3 %slice-start.1 = ((s8[4718592]{0:T(1024)(128)(4,1)}), s8[4194304]{0:T(1024)(128)(4,1)S(1)}, s32[]{:S(2)}) async-start(s8[4718592]{0:T(1024)(128)(4,1)} %bitcast.23), calls=%async_computation.1 | async-start | bytes 8388608
  11.4 17.5 %copy-start.3 = (bf16[2,256,512]{2,1,0:T(8,128)(2,1)}, bf16[2,256,512]{2,1,0:T(8,128)(2,1)S(1)}, u32[]{:S(2)}) copy-start(bf16[2,256,512]{2,1,0:T(8,128)(2,1)S(1)} %get-tuple-element.25.side_ref) | copy-start | bytes 1572868
  11.4 11.4 %collective-permute-start.2 = (bf16[2,256,512]{2,1,0:T(8,128)(2,1)S(1)}, bf16[2,256,512]{2,1,0:T(8,128)(2,1)S(1)}, u32[]{:S(2)}, u32[]{:S(2)}) collective-permute-start(bf16[2,256,512]{2,1,0:T(8,128)(2,1)S(1)} %get-tuple-element.25.side_ref), channel_id=1, source_target_pairs={{2,3},{3,2},{4,5},{5,4},{10,11},{11,10},{12,13},{13,12},{18,19},{1... | collective-permute-start | bytes 1572872 | tf_op jit(solution)/shard_map/ppermute | solution.py:98
  16.0 6.8 %collective-permute-start.9 = (bf16[2,256,512]{2,1,0:T(8,128)(2,1)}, bf16[2,256,512]{2,1,0:T(8,128)(2,1)S(1)}, u32[]{:S(2)}, u32[]{:S(2)}) collective-permute-start(bf16[2,256,512]{2,1,0:T(8,128)(2,1)} %get-tuple-element.26.own_ref.end_ref), channel_id=1, source_target_pairs={{0,2},{2,0},{4,6},{6,4},{8,10},{10,8},{12,14},{14,12},{16,18},{18,... | collective-permute-start | bytes 1572872 | tf_op jit(solution)/shard_map/ppermute | solution.py:84
  16.4 10.1 %collective-permute-start.14 = (bf16[2,128,1024]{2,1,0:T(8,128)(2,1)S(1)}, bf16[2,128,1024]{2,1,0:T(8,128)(2,1)S(1)}, u32[]{:S(2)}, u32[]{:S(2)}) collective-permute-start(bf16[2,128,1024]{2,1,0:T(8,128)(2,1)S(1)} %get-tuple-element.30), channel_id=1, source_target_pairs={{0,2},{2,0},{4,6},{6,4},{8,10},{10,8},{12,14},{14,12},{16,18},{18,... | collective-permute-start | bytes 1572872 | tf_op jit(solution)/shard_map/ppermute | solution.py:84
  16.6 12.4 %copy-start.1 = (bf16[2,256,512]{2,1,0:T(8,128)(2,1)}, bf16[2,256,512]{2,1,0:T(8,128)(2,1)S(1)}, u32[]{:S(2)}) copy-start(bf16[2,256,512]{2,1,0:T(8,128)(2,1)S(1)} %collective-permute-done.10.rest_0_) | copy-start | bytes 1572868
  16.6 12.3 %collective-permute-start.11 = (bf16[2,256,512]{2,1,0:T(8,128)(2,1)S(1)}, bf16[2,256,512]{2,1,0:T(8,128)(2,1)S(1)}, u32[]{:S(2)}, u32[]{:S(2)}) collective-permute-start(bf16[2,256,512]{2,1,0:T(8,128)(2,1)S(1)} %collective-permute-done.10.rest_0_), channel_id=1, source_target_pairs={{0,2},{2,0},{4,6},{6,4},{8,10},{10,8},{12,14},{14,12},{16,18},{18,... | collective-permute-start | bytes 1572872 | tf_op jit(solution)/shard_map/ppermute | solution.py:84
  22.9 6.2 %copy-start.5 = (bf16[2,256,512]{2,1,0:T(8,128)(2,1)}, bf16[2,256,512]{2,1,0:T(8,128)(2,1)S(1)}, u32[]{:S(2)}) copy-start(bf16[2,256,512]{2,1,0:T(8,128)(2,1)S(1)} %collective-permute-done.2.rest_4_.rest_2_) | copy-start | bytes 1572868
  22.9 6.1 %collective-permute-start.13 = (bf16[2,256,512]{2,1,0:T(8,128)(2,1)S(1)}, bf16[2,256,512]{2,1,0:T(8,128)(2,1)S(1)}, u32[]{:S(2)}, u32[]{:S(2)}) collective-permute-start(bf16[2,256,512]{2,1,0:T(8,128)(2,1)S(1)} %collective-permute-done.2.rest_4_.rest_2_), channel_id=1, source_target_pairs={{0,2},{2,0},{4,6},{6,4},{8,10},{10,8},{12,14},{14,12},{16,18},{18,... | collective-permute-start | bytes 1572872 | tf_op jit(solution)/shard_map/ppermute | solution.py:84
  22.9 6.1 %copy-start.7 = (bf16[2,256,512]{2,1,0:T(8,128)(2,1)}, bf16[2,256,512]{2,1,0:T(8,128)(2,1)S(1)}, u32[]{:S(2)}) copy-start(bf16[2,256,512]{2,1,0:T(8,128)(2,1)S(1)} %collective-permute-done.9.sib_ref.endsib_ref) | copy-start | bytes 1572868
  22.9 14.2 %collective-permute-start.3 = (bf16[2,256,512]{2,1,0:T(8,128)(2,1)}, bf16[2,256,512]{2,1,0:T(8,128)(2,1)}, u32[]{:S(2)}, u32[]{:S(2)}) collective-permute-start(bf16[2,256,512]{2,1,0:T(8,128)(2,1)} %get-tuple-element.26.own_ref.end_ref), channel_id=1, source_target_pairs={{2,3},{3,2},{4,5},{5,4},{10,11},{11,10},{12,13},{13,12},{18,19},{1... | collective-permute-start | bytes 1572872 | tf_op jit(solution)/shard_map/ppermute | solution.py:98
  29.0 1.8 %copy-start.9 = (bf16[2,256,512]{2,1,0:T(8,128)(2,1)}, bf16[2,256,512]{2,1,0:T(8,128)(2,1)S(1)}, u32[]{:S(2)}) copy-start(bf16[2,256,512]{2,1,0:T(8,128)(2,1)S(1)} %collective-permute-done.11.rest_1_) | copy-start | bytes 1572868
  29.0 1.7 %copy-start.11 = (bf16[2,256,512]{2,1,0:T(8,128)(2,1)}, bf16[2,256,512]{2,1,0:T(8,128)(2,1)S(1)}, u32[]{:S(2)}) copy-start(bf16[2,256,512]{2,1,0:T(8,128)(2,1)S(1)} %collective-permute-done.13.rest_5_.rest_3_) | copy-start | bytes 1572868
  30.7 9.8 %collective-permute-start.16 = (bf16[2,128,512]{2,1,0:T(8,128)(2,1)}, bf16[2,128,512]{2,1,0:T(8,128)(2,1)}, u32[]{:S(2)}, u32[]{:S(2)}) collective-permute-start(bf16[2,128,512]{2,1,0:T(8,128)(2,1)} %get-tuple-element.34.side_ref), channel_id=1, source_target_pairs={{0,4},{2,6},{4,0},{6,2},{8,12},{10,14},{12,8},{14,10},{16,20},{18,... | collective-permute-start | bytes 786440 | tf_op jit(solution)/shard_map/ppermute | solution.py:84
  36.2 0.9 %copy-start.13 = (bf16[2,128,1536]{2,1,0:T(8,128)(2,1)}, bf16[2,128,1536]{2,1,0:T(8,128)(2,1)S(1)}, u32[]{:S(2)}) copy-start(bf16[2,128,1536]{2,1,0:T(8,128)(2,1)S(1)} %get-tuple-element.28) | copy-start | bytes 2359300
  37.1 32.5 %collective-permute-start.4 = (bf16[2,128,1536]{2,1,0:T(8,128)(2,1)}, bf16[2,128,1536]{2,1,0:T(8,128)(2,1)}, u32[]{:S(2)}, u32[]{:S(2)}) collective-permute-start(bf16[2,128,1536]{2,1,0:T(8,128)(2,1)} %get-tuple-element.27), channel_id=1, source_target_pairs={{2,3},{3,2},{4,5},{5,4},{10,11},{11,10},{12,13},{13,12},{18,19},{1... | collective-permute-start | bytes 2359304 | tf_op jit(solution)/shard_map/ppermute | solution.py:98
  40.3 16.8 %collective-permute-start.17 = (bf16[2,128,512]{2,1,0:T(8,128)(2,1)}, bf16[2,128,512]{2,1,0:T(8,128)(2,1)S(1)}, u32[]{:S(2)}, u32[]{:S(2)}) collective-permute-start(bf16[2,128,512]{2,1,0:T(8,128)(2,1)} %get-tuple-element.33.end_ref), channel_id=1, source_target_pairs={{0,1},{1,0},{2,3},{3,2},{4,5},{5,4},{6,7},{7,6},{8,9},{9,8},{10,11... | collective-permute-start | bytes 786440 | tf_op jit(solution)/shard_map/ppermute | solution.py:98
  41.6 17.2 %collective-permute-start.19 = (bf16[2,128,256]{2,1,0:T(8,128)(2,1)S(1)}, bf16[2,128,256]{2,1,0:T(8,128)(2,1)S(1)}, u32[]{:S(2)}, u32[]{:S(2)}) collective-permute-start(bf16[2,128,256]{2,1,0:T(8,128)(2,1)S(1)} %dynamic-slice_add_fusion), channel_id=1, source_target_pairs={{0,1},{1,0},{2,3},{3,2},{4,5},{5,4},{6,7},{7,6},{8,9},{9,8},{10,11... | collective-permute-start | bytes 393224 | tf_op jit(solution)/shard_map/ppermute | solution.py:98
  42.9 18.5 %collective-permute-start.15 = (bf16[2,128,512]{2,1,0:T(8,128)(2,1)}, bf16[2,128,512]{2,1,0:T(8,128)(2,1)S(1)}, u32[]{:S(2)}, u32[]{:S(2)}) collective-permute-start(bf16[2,128,512]{2,1,0:T(8,128)(2,1)} %get-tuple-element.33.end_ref), channel_id=1, source_target_pairs={{0,4},{2,6},{4,0},{6,2},{8,12},{10,14},{12,8},{14,10},{16,20},{18,... | collective-permute-start | bytes 786440 | tf_op jit(solution)/shard_map/ppermute | solution.py:84
  57.1 8.4 %collective-permute-start.18 = (bf16[2,128,512]{2,1,0:T(8,128)(2,1)S(1)}, bf16[2,128,512]{2,1,0:T(8,128)(2,1)S(1)}, u32[]{:S(2)}, u32[]{:S(2)}) collective-permute-start(bf16[2,128,512]{2,1,0:T(8,128)(2,1)S(1)} %collective-permute-done.17.end_ref), channel_id=1, source_target_pairs={{0,4},{2,6},{4,0},{6,2},{8,12},{10,14},{12,8},{14,10},{16,20},{18,... | collective-permute-start | bytes 786440 | tf_op jit(solution)/shard_map/ppermute | solution.py:84
  58.8 9.5 %collective-permute-start.20 = (bf16[2,128,256]{2,1,0:T(8,128)(2,1)S(1)}, bf16[2,128,256]{2,1,0:T(8,128)(2,1)S(1)}, u32[]{:S(2)}, u32[]{:S(2)}) collective-permute-start(bf16[2,128,256]{2,1,0:T(8,128)(2,1)S(1)} %collective-permute-done.19.side_ref), channel_id=1, source_target_pairs={{0,4},{2,6},{4,0},{6,2},{8,12},{10,14},{12,8},{14,10},{16,20},{18,... | collective-permute-start | bytes 393224 | tf_op jit(solution)/shard_map/ppermute | solution.py:84
  59.8 9.1 %copy-start.15 = (bf16[2,1,128,512]{3,2,1,0:T(8,128)(2,1)S(1)}, bf16[2,1,128,512]{3,2,1,0:T(8,128)(2,1)}, u32[]{:S(2)}) copy-start(bf16[2,1,128,512]{3,2,1,0:T(8,128)(2,1)} %param.7) | copy-start | bytes 786436
  59.8 9.8 %copy-start.14 = (bf16[2,128,1536]{2,1,0:T(8,128)(2,1)S(1)}, bf16[2,128,1536]{2,1,0:T(8,128)(2,1)}, u32[]{:S(2)}) copy-start(bf16[2,128,1536]{2,1,0:T(8,128)(2,1)} %copy-done.13) | copy-start | bytes 2359300
  59.8 12.6 %collective-permute-start.7 = (bf16[2,128,512]{2,1,0:T(8,128)(2,1)S(1)}, bf16[2,128,512]{2,1,0:T(8,128)(2,1)S(1)}, u32[]{:S(2)}, u32[]{:S(2)}) collective-permute-start(bf16[2,128,512]{2,1,0:T(8,128)(2,1)S(1)} %fusion.1), channel_id=1, source_target_pairs={{0,4},{2,6},{4,0},{6,2},{8,12},{10,14},{12,8},{14,10},{16,20},{18,... | collective-permute-start | bytes 786440 | tf_op jit(solution)/shard_map/ppermute | solution.py:84
  63.1 9.5 %copy-start.2 = (bf16[2,256,512]{2,1,0:T(8,128)(2,1)S(1)}, bf16[2,256,512]{2,1,0:T(8,128)(2,1)}, u32[]{:S(2)}) copy-start(bf16[2,256,512]{2,1,0:T(8,128)(2,1)} %copy-done.1) | copy-start | bytes 1572868
  63.1 9.5 %copy-start.4 = (bf16[2,256,512]{2,1,0:T(8,128)(2,1)S(1)}, bf16[2,256,512]{2,1,0:T(8,128)(2,1)}, u32[]{:S(2)}) copy-start(bf16[2,256,512]{2,1,0:T(8,128)(2,1)} %copy-done.3) | copy-start | bytes 1572868
  63.1 9.5 %copy-start.6 = (bf16[2,256,512]{2,1,0:T(8,128)(2,1)S(1)}, bf16[2,256,512]{2,1,0:T(8,128)(2,1)}, u32[]{:S(2)}) copy-start(bf16[2,256,512]{2,1,0:T(8,128)(2,1)} %copy-done.5) | copy-start | bytes 1572868
  63.1 9.5 %copy-start.8 = (bf16[2,256,512]{2,1,0:T(8,128)(2,1)S(1)}, bf16[2,256,512]{2,1,0:T(8,128)(2,1)}, u32[]{:S(2)}) copy-start(bf16[2,256,512]{2,1,0:T(8,128)(2,1)} %copy-done.7) | copy-start | bytes 1572868
  63.1 9.5 %copy-start.10 = (bf16[2,256,512]{2,1,0:T(8,128)(2,1)S(1)}, bf16[2,256,512]{2,1,0:T(8,128)(2,1)}, u32[]{:S(2)}) copy-start(bf16[2,256,512]{2,1,0:T(8,128)(2,1)} %copy-done.9) | copy-start | bytes 1572868
  63.1 9.5 %copy-start.12 = (bf16[2,256,512]{2,1,0:T(8,128)(2,1)S(1)}, bf16[2,256,512]{2,1,0:T(8,128)(2,1)}, u32[]{:S(2)}) copy-start(bf16[2,256,512]{2,1,0:T(8,128)(2,1)} %copy-done.11) | copy-start | bytes 1572868
  63.2 11.5 %collective-permute-start.21 = (bf16[2,128,1536]{2,1,0:T(8,128)(2,1)S(1)}, bf16[2,128,1536]{2,1,0:T(8,128)(2,1)S(1)}, u32[]{:S(2)}, u32[]{:S(2)}) collective-permute-start(bf16[2,128,1536]{2,1,0:T(8,128)(2,1)S(1)} %shard_map.60.refs_8_), channel_id=1, source_target_pairs={{0,2},{2,0},{4,6},{6,4},{8,10},{10,8},{12,14},{14,12},{16,18},{18,... | collective-permute-start | bytes 2359304 | tf_op jit(solution)/shard_map/ppermute | solution.py:84
  68.9 5.8 %collective-permute-start.22 = (bf16[2,128,1536]{2,1,0:T(8,128)(2,1)S(1)}, bf16[2,128,1536]{2,1,0:T(8,128)(2,1)S(1)}, u32[]{:S(2)}, u32[]{:S(2)}) collective-permute-start(bf16[2,128,1536]{2,1,0:T(8,128)(2,1)S(1)} %shard_map.61.refs_9_), channel_id=1, source_target_pairs={{0,2},{2,0},{4,6},{6,4},{8,10},{10,8},{12,14},{14,12},{16,18},{18,... | collective-permute-start | bytes 2359304 | tf_op jit(solution)/shard_map/ppermute | solution.py:84
  69.1 3.5 %collective-permute-start.12 = (bf16[2,256,512]{2,1,0:T(8,128)(2,1)}, bf16[2,256,512]{2,1,0:T(8,128)(2,1)S(1)}, u32[]{:S(2)}, u32[]{:S(2)}) collective-permute-start(bf16[2,256,512]{2,1,0:T(8,128)(2,1)} %collective-permute-done.3.rest_2_), channel_id=1, source_target_pairs={{0,2},{2,0},{4,6},{6,4},{8,10},{10,8},{12,14},{14,12},{16,18},{18,... | collective-permute-start | bytes 1572872 | tf_op jit(solution)/shard_map/ppermute | solution.py:84
  69.6 12.7 %collective-permute-start.5 = (bf16[2,128,1536]{2,1,0:T(8,128)(2,1)S(1)}, bf16[2,128,1536]{2,1,0:T(8,128)(2,1)S(1)}, u32[]{:S(2)}, u32[]{:S(2)}) collective-permute-start(bf16[2,128,1536]{2,1,0:T(8,128)(2,1)S(1)} %copy-done.14), channel_id=1, source_target_pairs={{2,3},{3,2},{4,5},{5,4},{10,11},{11,10},{12,13},{13,12},{18,19},{1... | collective-permute-start | bytes 2359304 | tf_op jit(solution)/shard_map/ppermute | solution.py:98
  72.5 2.2 %collective-permute-start.8 = (bf16[2,2,128,512]{3,2,1,0:T(8,128)(2,1)S(1)}, bf16[2,2,128,512]{3,2,1,0:T(8,128)(2,1)S(1)}, u32[]{:S(2)}, u32[]{:S(2)}) collective-permute-start(bf16[2,2,128,512]{3,2,1,0:T(8,128)(2,1)S(1)} %pad_maximum_fusion.refs_5_), channel_id=1, source_target_pairs={{0,2},{2,0},{4,6},{6,4},{8,10},{10,8},{12,14},{14,12},{16,18},{18,... | collective-permute-start | bytes 1572872 | tf_op jit(solution)/shard_map/ppermute | solution.py:84

commit v3 on v2

--- a/solution.py
+++ b/solution.py
@@ -35,29 +35,19 @@
     return jnp.where(cols == index, 1.0, 0.0).astype(BF16)
 
 
-def call(kernel, scalars, inputs, out_shapes, specs=None, out_specs=None, scratch=(), flops=0, aliases=None):
-    specs = specs or [None] * len(inputs)
-    out_specs = out_specs or [None] * len(out_shapes)
-
-    def whole(array, spec):
-        if spec is not None:
-            return spec
-        rank = len(array.shape)
-        return pl.BlockSpec(array.shape, lambda i, sc: (0,) * rank)
-
-    moved = sum(s.size * s.dtype.itemsize for s in out_shapes)
+def call(kernel, scalars, inputs, out_shapes, specs=None, out_specs=None, scratch=(), aliases=None):
+    in_vmem = pl.BlockSpec(memory_space=pltpu.VMEM)
+    specs = specs or [in_vmem] * len(inputs)
+    out_specs = out_specs or [in_vmem] * len(out_shapes)
     return pl.pallas_call(
         kernel,
-        grid_spec=pltpu.PrefetchScalarGridSpec(
-            num_scalar_prefetch=1, grid=(1,),
-            in_specs=[whole(a, s) for a, s in zip(inputs, specs)],
-            out_specs=[whole(a, s) for a, s in zip(out_shapes, out_specs)],
-            scratch_shapes=list(scratch),
-        ),
+        in_specs=[pl.BlockSpec(memory_space=pltpu.SMEM)] + specs,
+        out_specs=out_specs,
         out_shape=out_shapes,
+        scratch_shapes=list(scratch),
         input_output_aliases=aliases or {},
         compiler_params=pltpu.CompilerParams(vmem_limit_bytes=VMEM_BYTES),
-        cost_estimate=pl.CostEstimate(flops=flops, bytes_accessed=2 * moved, transcendentals=0),
+        cost_estimate=pl.CostEstimate(flops=0, bytes_accessed=0, transcendentals=0),
     )(scalars, *inputs)
 
 
@@ -103,14 +93,37 @@
     skel_one = lax.dynamic_index_in_dim(skel_first[0], box // 2, 0, keepdims=True)
     skel_two = lax.dynamic_index_in_dim(skel_second[0], box // 4, 0, keepdims=True)
 
-    def iface_cols(start):
-        return lax.dynamic_slice(leaf, (0, 1 - par, 0, start), (2, 1, fr, k)).reshape(2, fr, k)
-
-    end_own = iface_cols(par * k)
+    in_hbm = pl.BlockSpec(memory_space=pl.ANY)
+
+    def copy_kernel(parts, sc, leaf_ref, *rest):
+        outs, sems = rest[:-1], rest[-1]
+        copies = [
+            pltpu.make_async_copy(part(sc, leaf_ref), out, sems.at[i])
+            for i, (part, out) in enumerate(zip(parts, outs))
+        ]
+        for copy in copies:
+            copy.start()
+        for copy in copies:
+            copy.wait()
+
+    def copy_parts(parts, width):
+        return call(
+            lambda *refs: copy_kernel(parts, *refs), scalars, [leaf],
+            [sds((2, fr, width), BF16)] * len(parts), specs=[in_hbm],
+            scratch=[pltpu.SemaphoreType.DMA((len(parts),))],
+        )
+
+    end_own, sides_raw = copy_parts([
+        lambda sc, ref: ref.at[:, 1 - sc[0], :, pl.ds(pl.multiple_of(sc[0] * k, k), k)],
+        lambda sc, ref: ref.at[:, 1 - sc[0], :, pl.ds(2 * k, k)],
+    ], k)
     end_far = over_face(end_own, giver)
-    sides_raw = iface_cols(2 * k)
     sides_sib = box_permute(sides_raw, 1)
     end_sib = box_permute(end_own, 1)
+    s_rows, end_rows = copy_parts([
+        lambda sc, ref: ref.at[:, 2], lambda sc, ref: ref.at[:, sc[0]],
+    ], 3 * k)
+    s_sib = box_permute(s_rows, 1)
 
     def slots_kernel(sc, own_ref, sib_ref, end_ref, skel_ref, skel2_ref,
                      comp_out, col_out, side_out, keep_out, send_out):
@@ -138,12 +151,9 @@
                 ref[t, :, k:] = dot(end_ref[t, take, 2 * k :], pick_own).astype(BF16)
 
     comp, skel_col, side, v_keep, v_send = call(
-        slots_kernel, scalars, [leaf, sides_sib, leaf, skel_one, skel_two],
+        slots_kernel, scalars, [sides_raw, sides_sib, end_rows, skel_one, skel_two],
         [sds((1, k), jnp.int32), sds((k, 1), jnp.int32), sds((2, fr, k), BF16),
          sds((2, hr, 2 * k), BF16), sds((2, hr, 2 * k), BF16)],
-        specs=[pl.BlockSpec((2, None, fr, k), lambda i, sc: (0, 1 - sc[0], 0, 2)), None,
-               pl.BlockSpec((2, None, fr, 3 * k), lambda i, sc: (0, sc[0], 0, 0)), None, None],
-        flops=12 * fr * k * k,
     )
     side_far = over_face(side, keeper)
     v_recv = box_permute(v_send, 1)
@@ -154,7 +164,6 @@
     w_two_pair = jnp.stack([w_two, box_permute(w_two, 2)])
     w_two_sib = box_permute(w_two_pair, 1)
 
-    s_sib = box_permute(leaf[:, 2], 1)
     cr = fr // ROW_CHUNKS
 
     def rows_kernel(sc, own_ref, sib_ref, end_ref, comp_ref, col_ref, *outs):
@@ -192,14 +201,9 @@
                             lo = s * fr + i * cr
                             outs[1 + (s - 1) * ROW_CHUNKS + i][t, :, cols] = picked[lo : lo + cr]
 
-    def face_block(which):
-        return pl.BlockSpec((2, None, fr, 3 * k), lambda i, sc: (0, which(sc), 0, 0))
-
     kept, *kept_out = call(
-        rows_kernel, scalars, [leaf, s_sib, leaf, comp, skel_col],
+        rows_kernel, scalars, [s_rows, s_sib, end_rows, comp, skel_col],
         [sds((2, fr, 3 * k), BF16)] + [sds((2, cr, 3 * k), BF16)] * (nf * ROW_CHUNKS),
-        specs=[face_block(lambda sc: 2), None, face_block(lambda sc: sc[0]), None, None],
-        flops=16 * fr * fr * n_face * 3 * k,
     )
 
     end_fwd = [box_permute(a, 1) for a in end_far]
@@ -240,9 +244,9 @@
         acc_out[:, :, k:] = rows[:, :, k:].astype(F32) - dot(left, flat(side_ref[...])).reshape(2, hr, k)
 
     v_acc, v_hid = call(
-        iface_kernel, scalars, [v_keep, v_recv, w_one, w_one_sib, end_own, end_sib, side],
+        iface_kernel, scalars, [after(v_keep, kept, w_two_sib), v_recv, w_one, w_one_sib, end_own, end_sib, side],
         [sds((2, hr, 2 * k), F32), sds((2, hr, k), BF16)],
-        scratch=[pltpu.VMEM((2, hr, 2 * k), BF16)], flops=8 * hr * k * 2 * k,
+        scratch=[pltpu.VMEM((2, hr, 2 * k), BF16)],
     )
 
     def iface_far_kernel(sc, acc_ref, hid_ref, *rest):
@@ -260,17 +264,19 @@
 
     two_end, two_side = call(
         iface_far_kernel, scalars, [v_acc, v_hid, *end_far, *end_fwd, *side_far, *side_fwd],
-        [sds((2, hr, k), BF16)] * 2, flops=8 * hr * k * k,
+        [sds((2, hr, k), BF16)] * 2,
     )
 
     side_x = box_permute(two_side, 2)
     end_y = over_face(two_end)
     end_x = box_permute(two_end, 2)
 
-    def half_slots(array):
-        return lax.dynamic_slice(array, (0, 0, par2 * half), (2, hr, half))
-
-    half_y = over_face(half_slots(two_side) + half_slots(side_x))
+    def half_kernel(sc, own_ref, x_ref, out_ref):
+        cols = pl.ds(pl.multiple_of(sc[1] * half, half), half)
+        out_ref[...] = own_ref[:, :, cols] + x_ref[:, :, cols]
+
+    (two_half,) = call(half_kernel, scalars, [two_side, side_x], [sds((2, hr, half), BF16)])
+    half_y = over_face(two_half)
     end_xy = [box_permute(a, 2) for a in end_y]
     half_xy = [box_permute(a, 2) for a in half_y]
 
@@ -320,12 +326,12 @@
         far, refs = refs[:nf], refs[nf:]
         col_ref, own_ref, sib_ref, w2_ref, w2sib_ref, iface_ref = refs[:6]
         mine, sibs = refs[6 : 6 + n_face], refs[6 + n_face : 6 + 2 * n_face]
-        out_ref, hid, w2 = refs[-3:]
+        out_ref, hid, w2, stage, sems = refs[-5:]
         p, q, f, r = sc[0], sc[1], sc[2], sc[3]
         is_end = p == q
 
         def rows(t, c):
-            total = kept_ref[t, :, c * k : (c + 1) * k]
+            total = kept_ref[t, chunk * cr : (chunk + 1) * cr, c * k : (c + 1) * k]
             for z in far:
                 total = total + z[t, :, c * k : (c + 1) * k]
             return total
@@ -368,6 +374,7 @@
             for h in range(2):
                 hid[s * 2 + h] = piece((second[:cr], second[cr:]), s * fr + h * hr, hr)
         none = jnp.zeros_like(merged[0])
+        copies = []
         first = [jnp.where(is_left, merged[0], none), jnp.where(is_left, none, merged[1]), merged[2]]
         for c in range(3):
             cols = slice(c * k, (c + 1) * k)
@@ -375,33 +382,35 @@
             for s in range(n_face):
                 total = total - dot(hid[s * 2 + p], flat(mine[s][:, :, cols]))
                 total = total - dot(hid[s * 2 + 1 - p], flat(sibs[s][:, :, cols]))
-            total = total.astype(BF16)
-            out_ref[0, 0, :, cols] = total[:cr]
-            out_ref[1, 0, :, cols] = total[cr:]
+            stage[:, :, cols] = total.astype(BF16).reshape(2, cr, k)
+            copies.append(pltpu.make_async_copy(
+                stage.at[:, :, pl.ds(c * k, k)],
+                out_ref.at[:, 0, pl.ds(chunk * cr, cr), pl.ds(c * k, k)],
+                sems.at[c],
+            ))
+            copies[-1].start()
+        for copy in copies:
+            copy.wait()
 
     out = None
-    sent = rest_far
     chunks = []
-    for i in range(ROW_CHUNKS):
-        outgoing = [kept_out[(s - 1) * ROW_CHUNKS + i] for s in range(1, n_face)]
-        outgoing = [after(a, *sent) for a in outgoing]
-        sent = [face_permute(a, s + 1, keeper) for s, a in enumerate(outgoing)]
-        chunks.append(sent)
+    for i, waits in enumerate((end_y, half_y)):
+        outgoing = [after(kept_out[(s - 1) * ROW_CHUNKS + i], *waits) for s in range(1, n_face)]
+        chunks.append([face_permute(a, s + 1, keeper) for s, a in enumerate(outgoing)])
     for i in range(ROW_CHUNKS):
         inputs = [kept, *chunks[i], skel_col, w_one, w_one_sib, w_two_pair, w_two_sib, iface, *two_rows, *two_sib]
-        specs = [pl.BlockSpec((2, cr, 3 * k), lambda g, sc, i=i: (0, i, 0))]
-        specs += [None] * (len(inputs) - 1)
+        specs = [pl.BlockSpec(memory_space=pltpu.VMEM)] * len(inputs)
         aliases = None
         if out is not None:
             inputs.append(out)
-            specs.append(pl.BlockSpec(memory_space=pl.ANY))
+            specs.append(in_hbm)
             aliases = {len(inputs): 0}
         (out,) = call(
             lambda sc, *refs, i=i: keep_kernel(i, sc, *refs), scalars, inputs,
-            [sds((2, 1, fr, 3 * k), BF16)], specs=specs,
-            out_specs=[pl.BlockSpec((2, 1, cr, 3 * k), lambda g, sc, i=i: (0, 0, i, 0))],
-            scratch=[pltpu.VMEM((2 * n_face, 2 * cr, 2 * hr), BF16), pltpu.VMEM((2, k, k), BF16)],
-            flops=8 * cr * k * 8 * k, aliases=aliases,
+            [sds((2, 1, fr, 3 * k), BF16)], specs=specs, out_specs=[in_hbm],
+            scratch=[pltpu.VMEM((2 * n_face, 2 * cr, 2 * hr), BF16), pltpu.VMEM((2, k, k), BF16),
+                     pltpu.VMEM((2, cr, 3 * k), BF16), pltpu.SemaphoreType.DMA((3,))],
+            aliases=aliases,
         )
     return out
 

time: 87.2 us -> 82.7 us (0.948)
  local copies, waits for them, and re-layouts: 8.86 us -> 3.1 us
  starting transfers between devices: 21.6 us -> 24.6 us
  Pallas kernels: 25.3 us -> 23 us
  waiting for transfers between devices: 28 us -> 29 us
    ppermute x16, waiting for transfers between devices: 5.09 us -> 9.03 us  [box_permute(): return lax.ppermute(array, 'box', [(b, b ^ mask) for b in range(n_box)])]
    ppermute x16, starting transfers between devices: 5.12 us -> 8.96 us  [box_permute(): return lax.ppermute(array, 'box', [(b, b ^ mask) for b in range(n_box)])]
    ppermute x7, waiting for transfers between devices: 22.9 us -> 20 us  [face_permute(): return lax.ppermute(array, ('box', 'face'), pairs)]
    squeeze x1 -> x0, local copies, waits for them, and re-layouts: 2.71 us -> none  [on_device(): s_sib = box_permute(leaf[:, 2], 1)]
    pallas_call x9 -> x12, Pallas kernels: 25.3 us -> 23 us  [call(): pl.pallas_call(kernel, in_specs=[pl.BlockSpec(memory_space=pltpu.SMEM)] +...]
    reshape x1 -> x0, local copies, waits for them, and re-layouts: 2.12 us -> none  [iface_cols(): lax.dynamic_slice(leaf, (0, 1 - par, 0, start), (2, 1, fr, k))]
    add x1 -> x0, other arithmetic: 1 us -> none  [on_device(): half_y = over_face(half_slots(two_side) + half_slots(side_x))]
    unnamed x38 -> x6, local copies, waits for them, and re-layouts: 3.3 us -> 2.35 us
  transfers between devices with their start and end apart: 23 -> 23, of which waited for: 6 -> 7; matrix products, arithmetic and copies ran while one was open for 7% -> 3% of each run, Pallas kernels for 24% -> 19%
where the time goes in v3:
time: 82.7 us; the launch traced here: 82.3 us
  waiting for transfers between devices  29 us (35%)
  starting transfers between devices  24.6 us (30%)
  Pallas kernels  23 us (28%)
  local copies, waits for them, and re-layouts  3.1 us (4%)
  other arithmetic  2.2 us (3%)
    pallas_call x12, Pallas kernels, call(): pl.pallas_call(kernel, in_specs=[pl.BlockSpec(memory_space=pltpu.SMEM)] +...  23 us
    ppermute x7, waiting for transfers between devices, face_permute(): return lax.ppermute(array, ('box', 'face'), pairs)  20 us
    ppermute x7, starting transfers between devices, face_permute(): return lax.ppermute(array, ('box', 'face'), pairs)  15.6 us
    ppermute x16, waiting for transfers between devices, box_permute(): return lax.ppermute(array, 'box', [(b, b ^ mask) for b in range(n_box)])  9.03 us
    ppermute x16, starting transfers between devices, box_permute(): return lax.ppermute(array, 'box', [(b, b ^ mask) for b in range(n_box)])  8.96 us
    unnamed x6, local copies, waits for them, and re-layouts  2.35 us
  transfers between devices with their start and end apart: 23, of which 7 were waited for; matrix products, arithmetic and copies ran while one was open for 3% of the time, Pallas kernels for 19%

profile of v3, /device:TPU:1, one launch (start us, length us, event | category | flops | bytes accessed | tf_op | source)
XLA Modules:
  0.0 82.3 jit_solution(6572436490021534920)
XLA Ops:
  0.0 0.1 pad_add_fusion.refs_0_.sc
  0.1 2.3 %copy-done = bf16[2,1,1,3,256,1536]{5,4,3,2,1,0:T(8,128)(2,1)S(1)} copy-done((bf16[2,1,1,3,256,1536]{5,4,3,2,1,0:T(8,128)(2,1)S(1)}, bf16[2,1,1,3,256,1536]{5,4,3,2,1,0:T(8,128)(2,1)}, u32[]{:S(2)}) %copy-start) | copy-done | bytes 4718616
  2.4 1.9 %shard_map.55 = (bf16[2,256,1536]{2,1,0:T(8,128)(2,1)}, bf16[2,256,1536]{2,1,0:T(8,128)(2,1)S(1)}) custom-call(s32[4]{0:T(128)S(1)} %pad_add_fusion.refs_0_.sc, bf16[2,3,256,1536]{3,2,1,0:T(8,128)(2,1)S(1)} %bitcast.14), custom_call_target="tpu_custom_call" | custom-call | tf_op jit(solution)/shard_map/pallas_call | solution.py:42
  4.3 0.0 copy-start.1
  4.4 0.1 collective-permute-start
  4.5 0.6 shard_map.56
  5.1 0.5 collective-permute-start.1
  5.6 0.8 fusion.1
  6.5 2.3 %collective-permute-start.2 = (bf16[2,128,512]{2,1,0:T(8,128)(2,1)}, bf16[2,128,512]{2,1,0:T(8,128)(2,1)}, u32[]{:S(2)}, u32[]{:S(2)}) collective-permute-start(bf16[2,128,512]{2,1,0:T(8,128)(2,1)} %fusion.1), channel_id=1, source_target_pairs={{0,4},{2,6},{4,0},{6,2},{8,12},{10,14},{12,8},{14,10},{16,20},{18,... | collective-permute-start | bytes 786440 | tf_op jit(solution)/shard_map/ppermute | solution.py:74
  8.7 0.7 collective-permute-start.7
  9.4 0.7 dynamic-slice_bitcast_fusion
  10.2 0.1 fusion.2
  10.3 5.0 %collective-permute-done.2 = bf16[2,128,512]{2,1,0:T(8,128)(2,1)} collective-permute-done((bf16[2,128,512]{2,1,0:T(8,128)(2,1)}, bf16[2,128,512]{2,1,0:T(8,128)(2,1)}, u32[]{:S(2)}, u32[]{:S(2)}) %collective-permute-start.2) | collective-permute-done | bytes 262176 | tf_op jit(solution)/shard_map/ppermute | solution.py:74
  15.3 1.0 %pad_maximum_fusion.refs_5_ = bf16[2,2,128,512]{3,2,1,0:T(8,128)(2,1)S(1)} fusion(bf16[1,2,128,512]{3,2,1,0:T(8,128)(2,1)} %bitcast.9, bf16[1,2,128,512]{3,2,1,0:T(8,128)(2,1)S(1)} %fusion.2), kind=kLoop, calls=%fused_computation.5 | loop fusion | flops 262144 | bytes 1048576 | tf_op jit(solution)/shard_map/stack | solution.py:164
  16.3 0.0 copy-start.2
  16.3 1.0 %collective-permute-start.3 = (bf16[2,2,128,512]{3,2,1,0:T(8,128)(2,1)S(1)}, bf16[2,2,128,512]{3,2,1,0:T(8,128)(2,1)S(1)}, u32[]{:S(2)}, u32[]{:S(2)}) collective-permute-start(bf16[2,2,128,512]{3,2,1,0:T(8,128)(2,1)S(1)} %pad_maximum_fusion.refs_5_), channel_id=1, source_target_pairs={{0,2},{2,0},{4,6},{6,4},{8,10},{10,8},{12,14},{14,12},{16,18},{18,... | collective-permute-start | bytes 1572872 | tf_op jit(solution)/shard_map/ppermute | solution.py:74
  17.4 2.3 %shard_map.57 = (s32[1,512]{1,0:T(1,128)S(1)}, s32[512,1]{1,0:T(8,128)S(1)}, bf16[2,256,512]{2,1,0:T(8,128)(2,1)S(1)}, bf16[2,128,1024]{2,1,0:T(8,128)(2,1)S(1)}, bf16[2,128,1024]{2,1,0:T(8,128)(2,1)S(1)}) custom-call(s32[4]{0:T(128)S(1)} %pad_add_fusion.refs_0_.sc, bf16[2,256,512]{2,1,0:T(8,128)(2,1)S(1)} %get-tuple-element.27.own_ref, ...), custom_call_target="tpu_custom_call" | custom-call | tf_op jit(solution)/shard_map/pallas_call | solution.py:42
  19.7 3.4 %collective-permute-start.9 = (bf16[2,256,512]{2,1,0:T(8,128)(2,1)S(1)}, bf16[2,256,512]{2,1,0:T(8,128)(2,1)S(1)}, u32[]{:S(2)}, u32[]{:S(2)}) collective-permute-start(bf16[2,256,512]{2,1,0:T(8,128)(2,1)S(1)} %get-tuple-element.36.side_ref), channel_id=1, source_target_pairs={{2,3},{3,2},{4,5},{5,4},{10,11},{11,10},{12,13},{13,12},{18,19},{1... | collective-permute-start | bytes 1572872 | tf_op jit(solution)/shard_map/ppermute | solution.py:88
  23.1 0.1 collective-permute-start.6
  23.2 0.2 fusion.own_ref.refs_3_
  23.4 0.5 collective-permute-start.5
  23.9 0.1 collective-permute-start.4
  24.0 5.6 %collective-permute-done.9.rest_2_.rest_4_ = bf16[2,256,512]{2,1,0:T(8,128)(2,1)S(1)} collective-permute-done((bf16[2,256,512]{2,1,0:T(8,128)(2,1)S(1)}, bf16[2,256,512]{2,1,0:T(8,128)(2,1)S(1)}, u32[]{:S(2)}, u32[]{:S(2)}) %collective-permute-start.9) | collective-permute-done | bytes 524320 | tf_op jit(solution)/shard_map/ppermute | solution.py:88
  29.7 0.5 collective-permute-start.10
  30.2 4.3 %shard_map.58 = (bf16[2,256,1536]{2,1,0:T(8,128)(2,1)S(1)}, bf16[2,128,1536]{2,1,0:T(8,128)(2,1)S(1)}, bf16[2,128,1536]{2,1,0:T(8,128)(2,1)S(1)}) custom-call(s32[4]{0:T(128)S(1)} %pad_add_fusion.refs_0_.sc, bf16[2,256,1536]{2,1,0:T(8,128)(2,1)} %get-tuple-element.25.own_ref, bf16[2,256,1536]{2,1,0:T(8,128)(2,1)} %collective-permute-done.sib_ref, ...), custom_call_target="tpu_custom_call" | custom-call | tf_op jit(solution)/shard_map/pallas_call | solution.py:42
  34.5 1.4 %shard_map.59 = (f32[2,128,1024]{2,1,0:T(8,128)S(1)}, bf16[2,128,512]{2,1,0:T(8,128)(2,1)S(1)}) custom-call(s32[4]{0:T(128)S(1)} %pad_add_fusion.refs_0_.sc, bf16[2,128,1024]{2,1,0:T(8,128)(2,1)S(1)} %get-tuple-element.33.keep_ref, bf16[2,128,1024]{2,1,0:T(8,128)(2,1)S(1)} %collective-permute-done.4.recv_ref, bf16[2,256,512]{2,1,0:T(8,128)(2,1)S(1)} %fusion.own_ref.refs_3_, ...), custom_call_target="tpu_custom_call" | custom-call | tf_op jit(solution)/shard_map/pallas_call | solution.py:42
  35.9 1.0 %shard_map.60 = (bf16[2,128,512]{2,1,0:T(8,128)(2,1)S(1)}, bf16[2,128,512]{2,1,0:T(8,128)(2,1)S(1)}) custom-call(s32[4]{0:T(128)S(1)} %pad_add_fusion.refs_0_.sc, f32[2,128,1024]{2,1,0:T(8,128)S(1)} %get-tuple-element.37.acc_ref, bf16[2,128,512]{2,1,0:T(8,128)(2,1)S(1)} %get-tuple-element.38.hid_ref, ...), custom_call_target="tpu_custom_call" | custom-call | tf_op jit(solution)/shard_map/pallas_call | solution.py:42
  36.9 0.3 collective-permute-start.11
  37.2 1.3 %collective-permute-start.17 = (bf16[2,128,512]{2,1,0:T(8,128)(2,1)S(1)}, bf16[2,128,512]{2,1,0:T(8,128)(2,1)S(1)}, u32[]{:S(2)}, u32[]{:S(2)}) collective-permute-start(bf16[2,128,512]{2,1,0:T(8,128)(2,1)S(1)} %get-tuple-element.42.end_ref), channel_id=1, source_target_pairs={{0,1},{1,0},{2,3},{3,2},{4,5},{5,4},{6,7},{7,6},{8,9},{9,8},{10,11... | collective-permute-start | bytes 786440 | tf_op jit(solution)/shard_map/ppermute | solution.py:88
  38.5 1.4 %collective-permute-start.16 = (bf16[2,128,512]{2,1,0:T(8,128)(2,1)S(1)}, bf16[2,128,512]{2,1,0:T(8,128)(2,1)S(1)}, u32[]{:S(2)}, u32[]{:S(2)}) collective-permute-start(bf16[2,128,512]{2,1,0:T(8,128)(2,1)S(1)} %get-tuple-element.42.end_ref), channel_id=1, source_target_pairs={{0,4},{2,6},{4,0},{6,2},{8,12},{10,14},{12,8},{14,10},{16,20},{18,... | collective-permute-start | bytes 786440 | tf_op jit(solution)/shard_map/ppermute | solution.py:74
  39.9 1.9 %collective-permute-start.14 = (bf16[2,256,512]{2,1,0:T(8,128)(2,1)S(1)}, bf16[2,256,512]{2,1,0:T(8,128)(2,1)S(1)}, u32[]{:S(2)}, u32[]{:S(2)}) collective-permute-start(bf16[2,256,512]{2,1,0:T(8,128)(2,1)S(1)} %get-tuple-element.41.end_ref.own_ref), channel_id=1, source_target_pairs={{2,3},{3,2},{4,5},{5,4},{10,11},{11,10},{12,13},{13,12},{18,19},{1... | collective-permute-start | bytes 1572872 | tf_op jit(solution)/shard_map/ppermute | solution.py:88
  41.8 2.1 %collective-permute-done.11.x_ref.sidex_ref = bf16[2,128,512]{2,1,0:T(8,128)(2,1)S(1)} collective-permute-done((bf16[2,128,512]{2,1,0:T(8,128)(2,1)S(1)}, bf16[2,128,512]{2,1,0:T(8,128)(2,1)S(1)}, u32[]{:S(2)}, u32[]{:S(2)}) %collective-permute-start.11) | collective-permute-done | bytes 262176 | tf_op jit(solution)/shard_map/ppermute | solution.py:74
  43.9 0.6 shard_map.61
  44.5 1.7 %collective-permute-start.12 = (bf16[2,128,256]{2,1,0:T(8,128)(2,1)S(1)}, bf16[2,128,256]{2,1,0:T(8,128)(2,1)S(1)}, u32[]{:S(2)}, u32[]{:S(2)}) collective-permute-start(bf16[2,128,256]{2,1,0:T(8,128)(2,1)S(1)} %shard_map.61), channel_id=1, source_target_pairs={{0,1},{1,0},{2,3},{3,2},{4,5},{5,4},{6,7},{7,6},{8,9},{9,8},{10,11... | collective-permute-start | bytes 393224 | tf_op jit(solution)/shard_map/ppermute | solution.py:88
  46.2 8.1 %collective-permute-done.12.side_ref = bf16[2,128,256]{2,1,0:T(8,128)(2,1)S(1)} collective-permute-done((bf16[2,128,256]{2,1,0:T(8,128)(2,1)S(1)}, bf16[2,128,256]{2,1,0:T(8,128)(2,1)S(1)}, u32[]{:S(2)}, u32[]{:S(2)}) %collective-permute-start.12) | collective-permute-done | bytes 131104 | tf_op jit(solution)/shard_map/ppermute | solution.py:88
  54.3 0.6 shard_map.63.refs_8_
  54.9 1.7 %collective-permute-start.20 = (bf16[2,128,1536]{2,1,0:T(8,128)(2,1)S(1)}, bf16[2,128,1536]{2,1,0:T(8,128)(2,1)S(1)}, u32[]{:S(2)}, u32[]{:S(2)}) collective-permute-start(bf16[2,128,1536]{2,1,0:T(8,128)(2,1)S(1)} %shard_map.63.refs_8_), channel_id=1, source_target_pairs={{0,2},{2,0},{4,6},{6,4},{8,10},{10,8},{12,14},{14,12},{16,18},{18,... | collective-permute-start | bytes 2359304 | tf_op jit(solution)/shard_map/ppermute | solution.py:74
  56.6 3.3 %collective-permute-start.22 = (bf16[2,128,1536]{2,1,0:T(8,128)(2,1)S(1)}, bf16[2,128,1536]{2,1,0:T(8,128)(2,1)S(1)}, u32[]{:S(2)}, u32[]{:S(2)}) collective-permute-start(bf16[2,128,1536]{2,1,0:T(8,128)(2,1)S(1)} %get-tuple-element.44), channel_id=1, source_target_pairs={{2,3},{3,2},{4,5},{5,4},{10,11},{11,10},{12,13},{13,12},{18,19},{1... | collective-permute-start | bytes 2359304 | tf_op jit(solution)/shard_map/ppermute | solution.py:88
  59.9 0.6 shard_map.64.refs_9_
  60.5 0.4 collective-permute-start.21
  60.9 3.3 %collective-permute-start.13 = (bf16[2,128,1536]{2,1,0:T(8,128)(2,1)S(1)}, bf16[2,128,1536]{2,1,0:T(8,128)(2,1)S(1)}, u32[]{:S(2)}, u32[]{:S(2)}) collective-permute-start(bf16[2,128,1536]{2,1,0:T(8,128)(2,1)S(1)} %get-tuple-element.40), channel_id=1, source_target_pairs={{2,3},{3,2},{4,5},{5,4},{10,11},{11,10},{12,13},{13,12},{18,19},{1... | collective-permute-start | bytes 2359304 | tf_op jit(solution)/shard_map/ppermute | solution.py:88
  64.2 0.1 collective-permute-start.15
  64.3 1.9 %collective-permute-done.15.rest_3_ = bf16[2,256,512]{2,1,0:T(8,128)(2,1)S(1)} collective-permute-done((bf16[2,256,512]{2,1,0:T(8,128)(2,1)S(1)}, bf16[2,256,512]{2,1,0:T(8,128)(2,1)S(1)}, u32[]{:S(2)}, u32[]{:S(2)}) %collective-permute-start.15) | collective-permute-done | bytes 524320 | tf_op jit(solution)/shard_map/ppermute | solution.py:74
  66.2 0.8 shard_map.62.refs_7_
  67.0 2.3 %collective-permute-done.22.refs_1_ = bf16[2,128,1536]{2,1,0:T(8,128)(2,1)S(1)} collective-permute-done((bf16[2,128,1536]{2,1,0:T(8,128)(2,1)S(1)}, bf16[2,128,1536]{2,1,0:T(8,128)(2,1)S(1)}, u32[]{:S(2)}, u32[]{:S(2)}) %collective-permute-start.22) | collective-permute-done | bytes 786464 | tf_op jit(solution)/shard_map/ppermute | solution.py:88
  69.3 4.4 %shard_map.65.refs_12_ = bf16[2,1,256,1536]{3,2,1,0:T(8,128)(2,1)} custom-call(s32[4]{0:T(128)S(1)} %pad_add_fusion.refs_0_.sc, bf16[2,256,1536]{2,1,0:T(8,128)(2,1)S(1)} %get-tuple-element.30.refs_0_, bf16[2,128,1536]{2,1,0:T(8,128)(2,1)S(1)} %collective-permute-done.22.refs_1_, s32[512,1]{1,0:T(8,128)S(1)} %get-tuple-element.29.col_ref.refs_2_, ...), custom_call_target="tpu_custom_call" | custom-call | tf_op jit(solution)/shard_map/pallas_call | solution.py:42
  73.8 4.0 %collective-permute-done.13.refs_1_ = bf16[2,128,1536]{2,1,0:T(8,128)(2,1)S(1)} collective-permute-done((bf16[2,128,1536]{2,1,0:T(8,128)(2,1)S(1)}, bf16[2,128,1536]{2,1,0:T(8,128)(2,1)S(1)}, u32[]{:S(2)}, u32[]{:S(2)}) %collective-permute-start.13) | collective-permute-done | bytes 786464 | tf_op jit(solution)/shard_map/ppermute | solution.py:88
  77.7 4.4 %shard_map.66 = bf16[2,1,256,1536]{3,2,1,0:T(8,128)(2,1)} custom-call(s32[4]{0:T(128)S(1)} %pad_add_fusion.refs_0_.sc, bf16[2,256,1536]{2,1,0:T(8,128)(2,1)S(1)} %get-tuple-element.30.refs_0_, bf16[2,128,1536]{2,1,0:T(8,128)(2,1)S(1)} %collective-permute-done.13.refs_1_, ...), custom_call_target="tpu_custom_call", output_to_operand_aliasing={{}: (13, {})} | custom-call | tf_op jit(solution)/shard_map/pallas_call | solution.py:42
  (22 shorter events, 0.1 us)
Async XLA Ops:
  0.1 2.3 %copy-start = (bf16[2,1,1,3,256,1536]{5,4,3,2,1,0:T(8,128)(2,1)S(1)}, bf16[2,1,1,3,256,1536]{5,4,3,2,1,0:T(8,128)(2,1)}, u32[]{:S(2)}) copy-start(bf16[2,1,1,3,256,1536]{5,4,3,2,1,0:T(8,128)(2,1)} %param.5) | copy-start | bytes 14155780
  4.3 1.3 %copy-start.1 = (bf16[2,1,128,512]{3,2,1,0:T(8,128)(2,1)S(1)}, bf16[2,1,128,512]{3,2,1,0:T(8,128)(2,1)}, u32[]{:S(2)}) copy-start(bf16[2,1,128,512]{3,2,1,0:T(8,128)(2,1)} %param.7) | copy-start | bytes 786436
  4.4 25.3 %collective-permute-start = (bf16[2,256,1536]{2,1,0:T(8,128)(2,1)}, bf16[2,256,1536]{2,1,0:T(8,128)(2,1)}, u32[]{:S(2)}, u32[]{:S(2)}) collective-permute-start(bf16[2,256,1536]{2,1,0:T(8,128)(2,1)} %get-tuple-element.25.own_ref), channel_id=1, source_target_pairs={{0,2},{2,0},{4,6},{6,4},{8,10},{10,8},{12,14},{14,12},{16,18},{18,... | collective-permute-start | bytes 4718600 | tf_op jit(solution)/shard_map/ppermute | solution.py:74
  5.1 12.3 %collective-permute-start.1 = (bf16[2,256,512]{2,1,0:T(8,128)(2,1)S(1)}, bf16[2,256,512]{2,1,0:T(8,128)(2,1)}, u32[]{:S(2)}, u32[]{:S(2)}) collective-permute-start(bf16[2,256,512]{2,1,0:T(8,128)(2,1)S(1)} %get-tuple-element.27.own_ref), channel_id=1, source_target_pairs={{0,2},{2,0},{4,6},{6,4},{8,10},{10,8},{12,14},{14,12},{16,18},{18,... | collective-permute-start | bytes 1572872 | tf_op jit(solution)/shard_map/ppermute | solution.py:74
  6.5 8.9 %collective-permute-start.2 = (bf16[2,128,512]{2,1,0:T(8,128)(2,1)}, bf16[2,128,512]{2,1,0:T(8,128)(2,1)}, u32[]{:S(2)}, u32[]{:S(2)}) collective-permute-start(bf16[2,128,512]{2,1,0:T(8,128)(2,1)} %fusion.1), channel_id=1, source_target_pairs={{0,4},{2,6},{4,0},{6,2},{8,12},{10,14},{12,8},{14,10},{16,20},{18,... | collective-permute-start | bytes 786440 | tf_op jit(solution)/shard_map/ppermute | solution.py:74
  8.7 14.7 %collective-permute-start.7 = (bf16[2,256,512]{2,1,0:T(8,128)(2,1)S(1)}, bf16[2,256,512]{2,1,0:T(8,128)(2,1)S(1)}, u32[]{:S(2)}, u32[]{:S(2)}) collective-permute-start(bf16[2,256,512]{2,1,0:T(8,128)(2,1)S(1)} %get-tuple-element.41.end_ref.own_ref), channel_id=1, source_target_pairs={{0,1},{1,0},{6,7},{7,6},{8,9},{9,8},{14,15},{15,14},{16,17},{17,16... | collective-permute-start | bytes 1572872 | tf_op jit(solution)/shard_map/ppermute | solution.py:88
  16.3 6.9 %copy-start.2 = (bf16[2,1,256,512]{3,2,1,0:T(8,128)(2,1)S(1)}, bf16[2,1,256,512]{3,2,1,0:T(8,128)(2,1)}, u32[]{:S(2)}) copy-start(bf16[2,1,256,512]{3,2,1,0:T(8,128)(2,1)} %param.6) | copy-start | bytes 1572868
  16.3 7.6 %collective-permute-start.3 = (bf16[2,2,128,512]{3,2,1,0:T(8,128)(2,1)S(1)}, bf16[2,2,128,512]{3,2,1,0:T(8,128)(2,1)S(1)}, u32[]{:S(2)}, u32[]{:S(2)}) collective-permute-start(bf16[2,2,128,512]{3,2,1,0:T(8,128)(2,1)S(1)} %pad_maximum_fusion.refs_5_), channel_id=1, source_target_pairs={{0,2},{2,0},{4,6},{6,4},{8,10},{10,8},{12,14},{14,12},{16,18},{18,... | collective-permute-start | bytes 1572872 | tf_op jit(solution)/shard_map/ppermute | solution.py:74
  19.7 10.0 %collective-permute-start.9 = (bf16[2,256,512]{2,1,0:T(8,128)(2,1)S(1)}, bf16[2,256,512]{2,1,0:T(8,128)(2,1)S(1)}, u32[]{:S(2)}, u32[]{:S(2)}) collective-permute-start(bf16[2,256,512]{2,1,0:T(8,128)(2,1)S(1)} %get-tuple-element.36.side_ref), channel_id=1, source_target_pairs={{2,3},{3,2},{4,5},{5,4},{10,11},{11,10},{12,13},{13,12},{18,19},{1... | collective-permute-start | bytes 1572872 | tf_op jit(solution)/shard_map/ppermute | solution.py:88
  23.1 11.4 %collective-permute-start.6 = (bf16[2,256,512]{2,1,0:T(8,128)(2,1)S(1)}, bf16[2,256,512]{2,1,0:T(8,128)(2,1)S(1)}, u32[]{:S(2)}, u32[]{:S(2)}) collective-permute-start(bf16[2,256,512]{2,1,0:T(8,128)(2,1)S(1)} %get-tuple-element.41.end_ref.own_ref), channel_id=1, source_target_pairs={{0,2},{2,0},{4,6},{6,4},{8,10},{10,8},{12,14},{14,12},{16,18},{18,... | collective-permute-start | bytes 1572872 | tf_op jit(solution)/shard_map/ppermute | solution.py:74
  23.4 11.1 %collective-permute-start.5 = (bf16[2,256,512]{2,1,0:T(8,128)(2,1)S(1)}, bf16[2,256,512]{2,1,0:T(8,128)(2,1)S(1)}, u32[]{:S(2)}, u32[]{:S(2)}) collective-permute-start(bf16[2,256,512]{2,1,0:T(8,128)(2,1)S(1)} %fusion.own_ref.refs_3_), channel_id=1, source_target_pairs={{0,2},{2,0},{4,6},{6,4},{8,10},{10,8},{12,14},{14,12},{16,18},{18,... | collective-permute-start | bytes 1572872 | tf_op jit(solution)/shard_map/ppermute | solution.py:74
  23.9 10.5 %collective-permute-start.4 = (bf16[2,128,1024]{2,1,0:T(8,128)(2,1)S(1)}, bf16[2,128,1024]{2,1,0:T(8,128)(2,1)S(1)}, u32[]{:S(2)}, u32[]{:S(2)}) collective-permute-start(bf16[2,128,1024]{2,1,0:T(8,128)(2,1)S(1)} %get-tuple-element.34), channel_id=1, source_target_pairs={{0,2},{2,0},{4,6},{6,4},{8,10},{10,8},{12,14},{14,12},{16,18},{18,... | collective-permute-start | bytes 1572872 | tf_op jit(solution)/shard_map/ppermute | solution.py:74
  29.6 6.2 %collective-permute-start.8 = (bf16[2,256,512]{2,1,0:T(8,128)(2,1)S(1)}, bf16[2,256,512]{2,1,0:T(8,128)(2,1)S(1)}, u32[]{:S(2)}, u32[]{:S(2)}) collective-permute-start(bf16[2,256,512]{2,1,0:T(8,128)(2,1)S(1)} %collective-permute-done.7.rest_0_), channel_id=1, source_target_pairs={{0,2},{2,0},{4,6},{6,4},{8,10},{10,8},{12,14},{14,12},{16,18},{18,... | collective-permute-start | bytes 1572872 | tf_op jit(solution)/shard_map/ppermute | solution.py:74
  29.7 6.2 %collective-permute-start.10 = (bf16[2,256,512]{2,1,0:T(8,128)(2,1)S(1)}, bf16[2,256,512]{2,1,0:T(8,128)(2,1)S(1)}, u32[]{:S(2)}, u32[]{:S(2)}) collective-permute-start(bf16[2,256,512]{2,1,0:T(8,128)(2,1)S(1)} %collective-permute-done.9.rest_2_.rest_4_), channel_id=1, source_target_pairs={{0,2},{2,0},{4,6},{6,4},{8,10},{10,8},{12,14},{14,12},{16,18},{18,... | collective-permute-start | bytes 1572872 | tf_op jit(solution)/shard_map/ppermute | solution.py:74
  36.9 7.0 %collective-permute-start.11 = (bf16[2,128,512]{2,1,0:T(8,128)(2,1)S(1)}, bf16[2,128,512]{2,1,0:T(8,128)(2,1)S(1)}, u32[]{:S(2)}, u32[]{:S(2)}) collective-permute-start(bf16[2,128,512]{2,1,0:T(8,128)(2,1)S(1)} %get-tuple-element.39.own_ref.side_ref), channel_id=1, source_target_pairs={{0,4},{2,6},{4,0},{6,2},{8,12},{10,14},{12,8},{14,10},{16,20},{18,... | collective-permute-start | bytes 786440 | tf_op jit(solution)/shard_map/ppermute | solution.py:74
  37.2 9.0 %collective-permute-start.17 = (bf16[2,128,512]{2,1,0:T(8,128)(2,1)S(1)}, bf16[2,128,512]{2,1,0:T(8,128)(2,1)S(1)}, u32[]{:S(2)}, u32[]{:S(2)}) collective-permute-start(bf16[2,128,512]{2,1,0:T(8,128)(2,1)S(1)} %get-tuple-element.42.end_ref), channel_id=1, source_target_pairs={{0,1},{1,0},{2,3},{3,2},{4,5},{5,4},{6,7},{7,6},{8,9},{9,8},{10,11... | collective-permute-start | bytes 786440 | tf_op jit(solution)/shard_map/ppermute | solution.py:88
  38.5 15.8 %collective-permute-start.16 = (bf16[2,128,512]{2,1,0:T(8,128)(2,1)S(1)}, bf16[2,128,512]{2,1,0:T(8,128)(2,1)S(1)}, u32[]{:S(2)}, u32[]{:S(2)}) collective-permute-start(bf16[2,128,512]{2,1,0:T(8,128)(2,1)S(1)} %get-tuple-element.42.end_ref), channel_id=1, source_target_pairs={{0,4},{2,6},{4,0},{6,2},{8,12},{10,14},{12,8},{14,10},{16,20},{18,... | collective-permute-start | bytes 786440 | tf_op jit(solution)/shard_map/ppermute | solution.py:74
  39.9 24.3 %collective-permute-start.14 = (bf16[2,256,512]{2,1,0:T(8,128)(2,1)S(1)}, bf16[2,256,512]{2,1,0:T(8,128)(2,1)S(1)}, u32[]{:S(2)}, u32[]{:S(2)}) collective-permute-start(bf16[2,256,512]{2,1,0:T(8,128)(2,1)S(1)} %get-tuple-element.41.end_ref.own_ref), channel_id=1, source_target_pairs={{2,3},{3,2},{4,5},{5,4},{10,11},{11,10},{12,13},{13,12},{18,19},{1... | collective-permute-start | bytes 1572872 | tf_op jit(solution)/shard_map/ppermute | solution.py:88
  44.5 9.8 %collective-permute-start.12 = (bf16[2,128,256]{2,1,0:T(8,128)(2,1)S(1)}, bf16[2,128,256]{2,1,0:T(8,128)(2,1)S(1)}, u32[]{:S(2)}, u32[]{:S(2)}) collective-permute-start(bf16[2,128,256]{2,1,0:T(8,128)(2,1)S(1)} %shard_map.61), channel_id=1, source_target_pairs={{0,1},{1,0},{2,3},{3,2},{4,5},{5,4},{6,7},{7,6},{8,9},{9,8},{10,11... | collective-permute-start | bytes 393224 | tf_op jit(solution)/shard_map/ppermute | solution.py:88
  46.2 13.7 %collective-permute-start.18 = (bf16[2,128,512]{2,1,0:T(8,128)(2,1)S(1)}, bf16[2,128,512]{2,1,0:T(8,128)(2,1)S(1)}, u32[]{:S(2)}, u32[]{:S(2)}) collective-permute-start(bf16[2,128,512]{2,1,0:T(8,128)(2,1)S(1)} %collective-permute-done.17.end_ref), channel_id=1, source_target_pairs={{0,4},{2,6},{4,0},{6,2},{8,12},{10,14},{12,8},{14,10},{16,20},{18,... | collective-permute-start | bytes 786440 | tf_op jit(solution)/shard_map/ppermute | solution.py:74
  54.3 5.6 %collective-permute-start.19 = (bf16[2,128,256]{2,1,0:T(8,128)(2,1)S(1)}, bf16[2,128,256]{2,1,0:T(8,128)(2,1)S(1)}, u32[]{:S(2)}, u32[]{:S(2)}) collective-permute-start(bf16[2,128,256]{2,1,0:T(8,128)(2,1)S(1)} %collective-permute-done.12.side_ref), channel_id=1, source_target_pairs={{0,4},{2,6},{4,0},{6,2},{8,12},{10,14},{12,8},{14,10},{16,20},{18,... | collective-permute-start | bytes 393224 | tf_op jit(solution)/shard_map/ppermute | solution.py:74
  54.9 12.1 %collective-permute-start.20 = (bf16[2,128,1536]{2,1,0:T(8,128)(2,1)S(1)}, bf16[2,128,1536]{2,1,0:T(8,128)(2,1)S(1)}, u32[]{:S(2)}, u32[]{:S(2)}) collective-permute-start(bf16[2,128,1536]{2,1,0:T(8,128)(2,1)S(1)} %shard_map.63.refs_8_), channel_id=1, source_target_pairs={{0,2},{2,0},{4,6},{6,4},{8,10},{10,8},{12,14},{14,12},{16,18},{18,... | collective-permute-start | bytes 2359304 | tf_op jit(solution)/shard_map/ppermute | solution.py:74
  56.6 12.7 %collective-permute-start.22 = (bf16[2,128,1536]{2,1,0:T(8,128)(2,1)S(1)}, bf16[2,128,1536]{2,1,0:T(8,128)(2,1)S(1)}, u32[]{:S(2)}, u32[]{:S(2)}) collective-permute-start(bf16[2,128,1536]{2,1,0:T(8,128)(2,1)S(1)} %get-tuple-element.44), channel_id=1, source_target_pairs={{2,3},{3,2},{4,5},{5,4},{10,11},{11,10},{12,13},{13,12},{18,19},{1... | collective-permute-start | bytes 2359304 | tf_op jit(solution)/shard_map/ppermute | solution.py:88
  60.5 8.8 %collective-permute-start.21 = (bf16[2,128,1536]{2,1,0:T(8,128)(2,1)S(1)}, bf16[2,128,1536]{2,1,0:T(8,128)(2,1)S(1)}, u32[]{:S(2)}, u32[]{:S(2)}) collective-permute-start(bf16[2,128,1536]{2,1,0:T(8,128)(2,1)S(1)} %shard_map.64.refs_9_), channel_id=1, source_target_pairs={{0,2},{2,0},{4,6},{6,4},{8,10},{10,8},{12,14},{14,12},{16,18},{18,... | collective-permute-start | bytes 2359304 | tf_op jit(solution)/shard_map/ppermute | solution.py:74
  60.9 16.9 %collective-permute-start.13 = (bf16[2,128,1536]{2,1,0:T(8,128)(2,1)S(1)}, bf16[2,128,1536]{2,1,0:T(8,128)(2,1)S(1)}, u32[]{:S(2)}, u32[]{:S(2)}) collective-permute-start(bf16[2,128,1536]{2,1,0:T(8,128)(2,1)S(1)} %get-tuple-element.40), channel_id=1, source_target_pairs={{2,3},{3,2},{4,5},{5,4},{10,11},{11,10},{12,13},{13,12},{18,19},{1... | collective-permute-start | bytes 2359304 | tf_op jit(solution)/shard_map/ppermute | solution.py:88
  64.2 2.0 %collective-permute-start.15 = (bf16[2,256,512]{2,1,0:T(8,128)(2,1)S(1)}, bf16[2,256,512]{2,1,0:T(8,128)(2,1)S(1)}, u32[]{:S(2)}, u32[]{:S(2)}) collective-permute-start(bf16[2,256,512]{2,1,0:T(8,128)(2,1)S(1)} %collective-permute-done.14.rest_2_), channel_id=1, source_target_pairs={{0,2},{2,0},{4,6},{6,4},{8,10},{10,8},{12,14},{14,12},{16,18},{18,... | collective-permute-start | bytes 1572872 | tf_op jit(solution)/shard_map/ppermute | solution.py:74

commit v4 on v3

--- a/solution.py
+++ b/solution.py
@@ -8,6 +8,7 @@
 BF16 = jnp.bfloat16
 F32 = jnp.float32
 VMEM_BYTES = 28 * 1024 * 1024
+LEAF_VMEM_BYTES = 60 * 1024 * 1024
 ROW_CHUNKS = 2
 
 
@@ -35,7 +36,7 @@
     return jnp.where(cols == index, 1.0, 0.0).astype(BF16)
 
 
-def call(kernel, scalars, inputs, out_shapes, specs=None, out_specs=None, scratch=(), aliases=None):
+def call(kernel, scalars, inputs, out_shapes, specs=None, out_specs=None, scratch=(), aliases=None, vmem=VMEM_BYTES):
     in_vmem = pl.BlockSpec(memory_space=pltpu.VMEM)
     specs = specs or [in_vmem] * len(inputs)
     out_specs = out_specs or [in_vmem] * len(out_shapes)
@@ -46,7 +47,7 @@
         out_shape=out_shapes,
         scratch_shapes=list(scratch),
         input_output_aliases=aliases or {},
-        compiler_params=pltpu.CompilerParams(vmem_limit_bytes=VMEM_BYTES),
+        compiler_params=pltpu.CompilerParams(vmem_limit_bytes=vmem),
         cost_estimate=pl.CostEstimate(flops=0, bytes_accessed=0, transcendentals=0),
     )(scalars, *inputs)
 
@@ -93,7 +94,7 @@
     skel_one = lax.dynamic_index_in_dim(skel_first[0], box // 2, 0, keepdims=True)
     skel_two = lax.dynamic_index_in_dim(skel_second[0], box // 4, 0, keepdims=True)
 
-    in_hbm = pl.BlockSpec(memory_space=pl.ANY)
+    in_hbm = pl.BlockSpec(memory_space=pltpu.HBM)
 
     def copy_kernel(parts, sc, leaf_ref, *rest):
         outs, sems = rest[:-1], rest[-1]
@@ -106,26 +107,26 @@
         for copy in copies:
             copy.wait()
 
-    def copy_parts(parts, width):
+    def copy_parts(where, parts, width):
         return call(
-            lambda *refs: copy_kernel(parts, *refs), scalars, [leaf],
+            lambda *refs: copy_kernel(parts, *refs), where, [leaf],
             [sds((2, fr, width), BF16)] * len(parts), specs=[in_hbm],
-            scratch=[pltpu.SemaphoreType.DMA((len(parts),))],
+            scratch=[pltpu.SemaphoreType.DMA((len(parts),))], vmem=LEAF_VMEM_BYTES,
         )
 
-    end_own, sides_raw = copy_parts([
+    end_own, sides_raw = copy_parts(scalars, [
         lambda sc, ref: ref.at[:, 1 - sc[0], :, pl.ds(pl.multiple_of(sc[0] * k, k), k)],
         lambda sc, ref: ref.at[:, 1 - sc[0], :, pl.ds(2 * k, k)],
     ], k)
     end_far = over_face(end_own, giver)
     sides_sib = box_permute(sides_raw, 1)
+    s_rows, end_rows = copy_parts(
+        after(scalars, sides_sib), [lambda sc, ref: ref.at[:, 2], lambda sc, ref: ref.at[:, sc[0]]], 3 * k
+    )
+    s_sib = box_permute(s_rows, 1)
     end_sib = box_permute(end_own, 1)
-    s_rows, end_rows = copy_parts([
-        lambda sc, ref: ref.at[:, 2], lambda sc, ref: ref.at[:, sc[0]],
-    ], 3 * k)
-    s_sib = box_permute(s_rows, 1)
-
-    def slots_kernel(sc, own_ref, sib_ref, end_ref, skel_ref, skel2_ref,
+
+    def slots_kernel(sc, end_ref, own_ref, sib_ref, skel_ref, skel2_ref,
                      comp_out, col_out, side_out, keep_out, send_out):
         p, q = sc[0], sc[1]
         rows = lax.broadcasted_iota(jnp.int32, (k, k), 0)
@@ -151,18 +152,31 @@
                 ref[t, :, k:] = dot(end_ref[t, take, 2 * k :], pick_own).astype(BF16)
 
     comp, skel_col, side, v_keep, v_send = call(
-        slots_kernel, scalars, [sides_raw, sides_sib, end_rows, skel_one, skel_two],
+        slots_kernel, scalars, [end_rows, sides_raw, sides_sib, skel_one, skel_two],
         [sds((1, k), jnp.int32), sds((k, 1), jnp.int32), sds((2, fr, k), BF16),
          sds((2, hr, 2 * k), BF16), sds((2, hr, 2 * k), BF16)],
     )
-    side_far = over_face(side, keeper)
+    side_far = over_face(after(side, *end_far), keeper)
     v_recv = box_permute(v_send, 1)
 
     w_one = jnp.roll(w_first[:, 0], -face * fr, axis=2)
     w_one_sib = box_permute(w_one, 1)
-    w_two = jnp.roll(w_second[:, 0], -face * fr, axis=2)
+    w_two = jnp.roll(after(w_second, comp)[:, 0], -face * fr, axis=2)
     w_two_pair = jnp.stack([w_two, box_permute(w_two, 2)])
     w_two_sib = box_permute(w_two_pair, 1)
+
+    def weights_kernel(sc, one_ref, onesib_ref, two_ref, twosib_ref, one_out, two_out):
+        p, r = sc[0], sc[3]
+        one_out[:, pl.ds(pl.multiple_of(p * half, half), half), :] = one_ref[...]
+        one_out[:, pl.ds(pl.multiple_of((1 - p) * half, half), half), :] = onesib_ref[...]
+        blk = k // 4
+        for i, (ref, part) in enumerate(((two_ref, 0), (two_ref, 1), (twosib_ref, 0), (twosib_ref, 1))):
+            place = r ^ (part * 2) ^ (i // 2)
+            two_out[:, pl.ds(pl.multiple_of(place * blk, blk), blk), :] = ref[part]
+
+    weight_one, weight_two = call(
+        weights_kernel, scalars, [w_one, w_one_sib, w_two_pair, w_two_sib], [sds((2, k, k), BF16)] * 2,
+    )
 
     cr = fr // ROW_CHUNKS
 
@@ -207,22 +221,12 @@
     )
 
     end_fwd = [box_permute(a, 1) for a in end_far]
-    side_fwd = [box_permute(a, 1) for a in side_far]
     rest_far = over_face(after(end_own, *side_far), keeper)
-    rest_fwd = [box_permute(a, 1) for a in rest_far]
-
-    def hidden_rows(couple, p, own_ref, sib_ref, m):
-        lo = pl.ds(pl.multiple_of(p * half, half), half)
-        hi = pl.ds(pl.multiple_of((1 - p) * half, half), half)
-        both = dot(stacked(couple(0, lo), couple(1, lo)), flat(own_ref[...]))
-        both = both + dot(stacked(couple(0, hi), couple(1, hi)), flat(sib_ref[...]))
-        both = both.astype(BF16)
-        return both[:m], both[m:]
 
     def piece(hidden, start, count):
         return stacked(hidden[0][:, start : start + count], hidden[1][:, start : start + count])
 
-    def iface_kernel(sc, keep_ref, recv_ref, own_ref, sib_ref, end_ref, endsib_ref, side_ref,
+    def iface_kernel(sc, keep_ref, recv_ref, w_ref, end_ref, endsib_ref, side_ref,
                      acc_out, hid_out, rows):
         p, q = sc[0], sc[1]
 
@@ -234,7 +238,8 @@
         def _():
             rows[...] = keep_ref[...]
 
-        hidden = hidden_rows(lambda t, c: rows[t, :, c], p, own_ref, sib_ref, hr)
+        both = dot(stacked(rows[0, :, :k], rows[1, :, :k]), flat(w_ref[...])).astype(BF16)
+        hidden = both[:hr], both[hr:]
         hid_out[0] = hidden[0]
         hid_out[1] = hidden[1]
         left = piece(hidden, 0, fr)
@@ -244,10 +249,12 @@
         acc_out[:, :, k:] = rows[:, :, k:].astype(F32) - dot(left, flat(side_ref[...])).reshape(2, hr, k)
 
     v_acc, v_hid = call(
-        iface_kernel, scalars, [after(v_keep, kept, w_two_sib), v_recv, w_one, w_one_sib, end_own, end_sib, side],
+        iface_kernel, scalars, [v_keep, v_recv, weight_one, end_own, end_sib, side],
         [sds((2, hr, 2 * k), F32), sds((2, hr, k), BF16)],
         scratch=[pltpu.VMEM((2, hr, 2 * k), BF16)],
     )
+    side_fwd = [box_permute(after(a, kept, v_acc), 1) for a in side_far]
+    rest_fwd = [box_permute(a, 1) for a in rest_far]
 
     def iface_far_kernel(sc, acc_ref, hid_ref, *rest):
         far, fwd, side_f, side_w = (rest[i * nf : (i + 1) * nf] for i in range(4))
@@ -268,7 +275,7 @@
     )
 
     side_x = box_permute(two_side, 2)
-    end_y = over_face(two_end)
+    end_y = over_face(after(two_end, *rest_far))
     end_x = box_permute(two_end, 2)
 
     def half_kernel(sc, own_ref, x_ref, out_ref):
@@ -298,6 +305,17 @@
     for s in range(nf):
         two_rows += call(join_far_kernel, scalars, [end_y[s], end_xy[s], half_y[s], half_xy[s]], two_shape)
     two_sib = [box_permute(a, 1) for a in two_rows]
+
+    def level_two_kernel(sc, *refs):
+        out_ref = refs[-1]
+        p = sc[0]
+        for s in range(n_face):
+            out_ref[s, :, pl.ds(pl.multiple_of(p * hr, hr), hr), :] = refs[s][...]
+            out_ref[s, :, pl.ds(pl.multiple_of((1 - p) * hr, hr), hr), :] = refs[n_face + s][...]
+
+    (iface_two,) = call(
+        level_two_kernel, scalars, [*two_rows, *two_sib], [sds((n_face, 2, fr, 3 * k), BF16)],
+    )
 
     def gather_kernel(sc, own_ref, sib_ref, side_ref, *rest):
         far, fwd, rfar, rfwd, sfar, sfwd = (rest[i * nf : (i + 1) * nf] for i in range(6))
@@ -324,11 +342,17 @@
     def keep_kernel(chunk, sc, *refs):
         kept_ref, refs = refs[0], refs[1:]
         far, refs = refs[:nf], refs[nf:]
-        col_ref, own_ref, sib_ref, w2_ref, w2sib_ref, iface_ref = refs[:6]
-        mine, sibs = refs[6 : 6 + n_face], refs[6 + n_face : 6 + 2 * n_face]
-        out_ref, hid, w2, stage, sems = refs[-5:]
-        p, q, f, r = sc[0], sc[1], sc[2], sc[3]
+        col_ref, w_ref, w2_ref, iface_ref, iface2_ref = refs[:5]
+        out_ref, stage, sems = refs[-3:]
+        p, q, f = sc[0], sc[1], sc[2]
         is_end = p == q
+
+        def wide(rows):
+            parts = [piece((rows[:cr], rows[cr:]), s * fr, fr) for s in range(n_face)]
+            return jnp.concatenate(parts, axis=1)
+
+        def gathered(ref, c):
+            return ref[:, :, :, c * k : (c + 1) * k].reshape(n_face * 2 * fr, k)
 
         def rows(t, c):
             total = kept_ref[t, chunk * cr : (chunk + 1) * cr, c * k : (c + 1) * k]
@@ -343,13 +367,8 @@
         rights = [rows(t, 1) for t in range(2)]
         couple = [jnp.where(right, a, b) for a, b in zip(lefts, rights)]
 
-        def columns(t, which):
-            return jnp.where(which == 0, couple[t][:, :half], couple[t][:, half:])
-
-        own = stacked(columns(0, p), columns(1, p))
-        sib = stacked(columns(0, 1 - p), columns(1, 1 - p))
-        both = (dot(own, flat(own_ref[...])) + dot(sib, flat(sib_ref[...]))).astype(BF16)
-        hidden = both[:cr], both[cr:]
+        both = dot(stacked(couple[0], couple[1]), flat(w_ref[...])).astype(BF16)
+        left = wide(both)
         nothing = jnp.zeros((cr, k), BF16)
         start = [
             jnp.concatenate([jnp.where(right, nothing, a) for a in lefts], axis=0),
@@ -358,30 +377,17 @@
         ]
         merged = []
         for c in range(3):
-            total = start[c].astype(F32)
-            for s in range(n_face):
-                total = total - dot(piece(hidden, s * fr, fr), flat(iface_ref[s, :, :, c * k : (c + 1) * k]))
-            merged.append(total.astype(BF16))
+            merged.append((start[c].astype(F32) - dot(left, gathered(iface_ref, c))).astype(BF16))
         is_left = q == 0
-        blk = k // 4
-        for i, (ref, part) in enumerate(((w2_ref, 0), (w2_ref, 1), (w2sib_ref, 0), (w2sib_ref, 1))):
-            place = r ^ (part * 2) ^ (i // 2)
-            for t in range(2):
-                w2[t, pl.ds(pl.multiple_of(place * blk, blk), blk), :] = ref[part, t]
         couple2 = jnp.where(is_left, merged[1], merged[0])
-        second = dot(stacked(couple2[:cr], couple2[cr:]), flat(w2[...])).astype(BF16)
-        for s in range(n_face):
-            for h in range(2):
-                hid[s * 2 + h] = piece((second[:cr], second[cr:]), s * fr + h * hr, hr)
+        second = dot(stacked(couple2[:cr], couple2[cr:]), flat(w2_ref[...])).astype(BF16)
+        left = wide(second)
         none = jnp.zeros_like(merged[0])
         copies = []
         first = [jnp.where(is_left, merged[0], none), jnp.where(is_left, none, merged[1]), merged[2]]
         for c in range(3):
             cols = slice(c * k, (c + 1) * k)
-            total = first[c].astype(F32)
-            for s in range(n_face):
-                total = total - dot(hid[s * 2 + p], flat(mine[s][:, :, cols]))
-                total = total - dot(hid[s * 2 + 1 - p], flat(sibs[s][:, :, cols]))
+            total = first[c].astype(F32) - dot(left, gathered(iface2_ref, c))
             stage[:, :, cols] = total.astype(BF16).reshape(2, cr, k)
             copies.append(pltpu.make_async_copy(
                 stage.at[:, :, pl.ds(c * k, k)],
@@ -394,11 +400,11 @@
 
     out = None
     chunks = []
-    for i, waits in enumerate((end_y, half_y)):
+    for i, waits in enumerate((rest_far, end_y)):
         outgoing = [after(kept_out[(s - 1) * ROW_CHUNKS + i], *waits) for s in range(1, n_face)]
         chunks.append([face_permute(a, s + 1, keeper) for s, a in enumerate(outgoing)])
     for i in range(ROW_CHUNKS):
-        inputs = [kept, *chunks[i], skel_col, w_one, w_one_sib, w_two_pair, w_two_sib, iface, *two_rows, *two_sib]
+        inputs = [kept, *chunks[i], skel_col, weight_one, weight_two, iface, iface_two]
         specs = [pl.BlockSpec(memory_space=pltpu.VMEM)] * len(inputs)
         aliases = None
         if out is not None:
@@ -408,8 +414,7 @@
         (out,) = call(
             lambda sc, *refs, i=i: keep_kernel(i, sc, *refs), scalars, inputs,
             [sds((2, 1, fr, 3 * k), BF16)], specs=specs, out_specs=[in_hbm],
-            scratch=[pltpu.VMEM((2 * n_face, 2 * cr, 2 * hr), BF16), pltpu.VMEM((2, k, k), BF16),
-                     pltpu.VMEM((2, cr, 3 * k), BF16), pltpu.SemaphoreType.DMA((3,))],
+            scratch=[pltpu.VMEM((2, cr, 3 * k), BF16), pltpu.SemaphoreType.DMA((3,))],
             aliases=aliases,
         )
     return out

time: 82.7 us -> 89.9 us (1.087); the launches traced: 82.3 us -> 88.2 us
  starting transfers between devices: 24.6 us -> 29.3 us
  waiting for transfers between devices: 29 us -> 24.5 us
  Pallas kernels: 23 us -> 27.4 us
  local copies, waits for them, and re-layouts: 3.1 us -> 5.5 us
  other arithmetic: 2.2 us -> 1.05 us
    ppermute x16, starting transfers between devices: 8.96 us -> 16.8 us  [box_permute(): return lax.ppermute(array, 'box', [(b, b ^ mask) for b in range(n_box)])]
    ppermute x7, waiting for transfers between devices: 20 us -> 14.8 us  [face_permute(): return lax.ppermute(array, ('box', 'face'), pairs)]
    pallas_call x12 -> x14, Pallas kernels: 23 us -> 27.4 us  [call(): pl.pallas_call(kernel, in_specs=[pl.BlockSpec(memory_space=pltpu.SMEM)] +...]
    ppermute x7, starting transfers between devices: 15.6 us -> 12.6 us  [face_permute(): return lax.ppermute(array, ('box', 'face'), pairs)]
    unnamed x6 -> x20, local copies, waits for them, and re-layouts: 2.35 us -> 4.76 us
    another operation x2, other arithmetic: 1.1 us -> 0.15 us  [on_device(): w_two_pair = jnp.stack([w_two, box_permute(w_two, 2)])]
  transfers between devices with their start and end apart: 23 -> 23, of which waited for: 7 -> 9; matrix products, arithmetic and copies ran while one was open for 3% -> 1% of each run, Pallas kernels for 19% -> 18%
where the time goes in v4:
time: 89.9 us; the launch traced here: 88.2 us
  starting transfers between devices  29.3 us (33%)
  Pallas kernels  27.4 us (30%)
  waiting for transfers between devices  24.5 us (27%)
  local copies, waits for them, and re-layouts  5.5 us (6%)
  other arithmetic  1.05 us (1%)
    pallas_call x14, Pallas kernels, call(): pl.pallas_call(kernel, in_specs=[pl.BlockSpec(memory_space=pltpu.SMEM)] +...  27.4 us
    ppermute x16, starting transfers between devices, box_permute(): return lax.ppermute(array, 'box', [(b, b ^ mask) for b in range(n_box)])  16.8 us
    ppermute x7, waiting for transfers between devices, face_permute(): return lax.ppermute(array, ('box', 'face'), pairs)  14.8 us
    ppermute x7, starting transfers between devices, face_permute(): return lax.ppermute(array, ('box', 'face'), pairs)  12.6 us
    ppermute x16, waiting for transfers between devices, box_permute(): return lax.ppermute(array, 'box', [(b, b ^ mask) for b in range(n_box)])  9.74 us
    unnamed x20, local copies, waits for them, and re-layouts  4.76 us
  transfers between devices with their start and end apart: 23, of which 9 were waited for; matrix products, arithmetic and copies ran while one was open for 1% of the time, Pallas kernels for 18%

profile of v4, /device:TPU:1, one launch (start us, length us, event | category | flops | bytes accessed | tf_op | source)
XLA Modules:
  0.0 88.2 jit_solution(4697575237158916793)
XLA Ops:
  0.0 0.6 pad_add_fusion.refs_0_.sc
  0.6 2.9 %shard_map.55 = (bf16[2,256,512]{2,1,0:T(8,128)(2,1)}, bf16[2,256,512]{2,1,0:T(8,128)(2,1)}) custom-call(s32[4]{0:T(128)} %pad_add_fusion.refs_0_.sc, bf16[2,3,256,1536]{3,2,1,0:T(8,128)(2,1)} %bitcast.14), custom_call_target="tpu_custom_call" | custom-call | tf_op jit(solution)/shard_map/pallas_call | solution.py:43
  3.5 0.1 collective-permute-start
  3.6 2.1 %collective-permute-done.sib_ref = bf16[2,256,512]{2,1,0:T(8,128)(2,1)S(1)} collective-permute-done((bf16[2,256,512]{2,1,0:T(8,128)(2,1)}, bf16[2,256,512]{2,1,0:T(8,128)(2,1)S(1)}, u32[]{:S(2)}, u32[]{:S(2)}) %collective-permute-start) | collective-permute-done | bytes 524320 | tf_op jit(solution)/shard_map/ppermute | solution.py:75
  5.7 0.8 copy-done.5
  6.5 4.3 %shard_map.56 = (bf16[2,256,1536]{2,1,0:T(8,128)(2,1)}, bf16[2,256,1536]{2,1,0:T(8,128)(2,1)}) custom-call(s32[4]{0:T(128)} %pad_add_fusion.refs_0_.sc, bf16[2,3,256,1536]{3,2,1,0:T(8,128)(2,1)} %bitcast.15), custom_call_target="tpu_custom_call" | custom-call | tf_op jit(solution)/shard_map/pallas_call | solution.py:43
  10.8 0.2 collective-permute-start.1
  11.0 0.2 fusion.one_ref
  11.2 0.4 collective-permute-start.3
  11.6 0.7 collective-permute-start.7
  12.3 0.7 dynamic-slice_bitcast_fusion
  13.1 1.4 %copy-done = bf16[2,256,1536]{2,1,0:T(8,128)(2,1)S(1)} copy-done((bf16[2,256,1536]{2,1,0:T(8,128)(2,1)S(1)}, bf16[2,256,1536]{2,1,0:T(8,128)(2,1)}, u32[]{:S(2)}) %copy-start) | copy-done | bytes 1572888
  14.5 1.0 %copy-done.4 = bf16[2,256,512]{2,1,0:T(8,128)(2,1)S(1)} copy-done((bf16[2,256,512]{2,1,0:T(8,128)(2,1)S(1)}, bf16[2,256,512]{2,1,0:T(8,128)(2,1)}, u32[]{:S(2)}) %copy-start.4) | copy-done | bytes 524312
  15.6 1.0 %copy-done.6 = bf16[2,256,512]{2,1,0:T(8,128)(2,1)S(1)} copy-done((bf16[2,256,512]{2,1,0:T(8,128)(2,1)S(1)}, bf16[2,256,512]{2,1,0:T(8,128)(2,1)}, u32[]{:S(2)}) %copy-start.6) | copy-done | bytes 524312
  16.6 1.8 %shard_map.57 = (s32[1,512]{1,0:T(1,128)S(1)}, s32[512,1]{1,0:T(8,128)S(1)}, bf16[2,256,512]{2,1,0:T(8,128)(2,1)S(1)}, bf16[2,128,1024]{2,1,0:T(8,128)(2,1)S(1)}, bf16[2,128,1024]{2,1,0:T(8,128)(2,1)S(1)}) custom-call(s32[4]{0:T(128)S(1)} %copy-done.7, bf16[2,256,1536]{2,1,0:T(8,128)(2,1)S(1)} %copy-done, bf16[2,256,512]{2,1,0:T(8,128)(2,1)S(1)} %copy-done.4, ...), custom_call_target="tpu_custom_call" | custom-call | tf_op jit(solution)/shard_map/pallas_call | solution.py:43
  18.4 0.1 fusion.1
  18.5 4.9 %collective-permute-start.4 = (bf16[2,128,512]{2,1,0:T(8,128)(2,1)S(1)}, bf16[2,128,512]{2,1,0:T(8,128)(2,1)S(1)}, u32[]{:S(2)}, u32[]{:S(2)}) collective-permute-start(bf16[2,128,512]{2,1,0:T(8,128)(2,1)S(1)} %fusion.1), channel_id=1, source_target_pairs={{0,4},{2,6},{4,0},{6,2},{8,12},{10,14},{12,8},{14,10},{16,20},{18,... | collective-permute-start | bytes 786440 | tf_op jit(solution)/shard_map/ppermute | solution.py:75
  23.4 0.1 fusion.2
  23.5 5.7 %collective-permute-done.4 = bf16[2,128,512]{2,1,0:T(8,128)(2,1)S(1)} collective-permute-done((bf16[2,128,512]{2,1,0:T(8,128)(2,1)S(1)}, bf16[2,128,512]{2,1,0:T(8,128)(2,1)S(1)}, u32[]{:S(2)}, u32[]{:S(2)}) %collective-permute-start.4) | collective-permute-done | bytes 262176 | tf_op jit(solution)/shard_map/ppermute | solution.py:75
  29.2 1.6 %collective-permute-start.5 = (bf16[2,2,128,512]{3,2,1,0:T(8,128)(2,1)S(1)}, bf16[2,2,128,512]{3,2,1,0:T(8,128)(2,1)S(1)}, u32[]{:S(2)}, u32[]{:S(2)}) collective-permute-start(bf16[2,2,128,512]{3,2,1,0:T(8,128)(2,1)S(1)} %pad_maximum_fusion.two_ref), channel_id=1, source_target_pairs={{0,2},{2,0},{4,6},{6,4},{8,10},{10,8},{12,14},{14,12},{16,18},{18,... | collective-permute-start | bytes 1572872 | tf_op jit(solution)/shard_map/ppermute | solution.py:75
  30.9 0.4 collective-permute-start.2
  31.3 2.1 %collective-permute-start.9 = (bf16[2,256,512]{2,1,0:T(8,128)(2,1)S(1)}, bf16[2,256,512]{2,1,0:T(8,128)(2,1)S(1)}, u32[]{:S(2)}, u32[]{:S(2)}) collective-permute-start(bf16[2,256,512]{2,1,0:T(8,128)(2,1)S(1)} %get-tuple-element.47.side_ref), channel_id=1, source_target_pairs={{2,3},{3,2},{4,5},{5,4},{10,11},{11,10},{12,13},{13,12},{18,19},{1... | collective-permute-start | bytes 1572872 | tf_op jit(solution)/shard_map/ppermute | solution.py:89
  33.5 1.2 %shard_map.59 = (bf16[2,512,512]{2,1,0:T(8,128)(2,1)S(1)}, bf16[2,512,512]{2,1,0:T(8,128)(2,1)S(1)}) custom-call(s32[4]{0:T(128)S(1)} %copy-done.7, bf16[2,256,512]{2,1,0:T(8,128)(2,1)S(1)} %fusion.one_ref, bf16[2,256,512]{2,1,0:T(8,128)(2,1)} %collective-permute-done.3.onesib_ref, bf16[2,2,128,512]{3,2,1,0:T(8,128)(2,1)S(1)} %pad_maximum_fusion.two_ref, ...), custom_call_target="tpu_custom_call" | custom-call | tf_op jit(solution)/shard_map/pallas_call | solution.py:43
  34.8 1.4 %shard_map.60 = (f32[2,128,1024]{2,1,0:T(8,128)S(1)}, bf16[2,128,512]{2,1,0:T(8,128)(2,1)S(1)}) custom-call(s32[4]{0:T(128)S(1)} %copy-done.7, bf16[2,128,1024]{2,1,0:T(8,128)(2,1)S(1)} %get-tuple-element.39.keep_ref, bf16[2,128,1024]{2,1,0:T(8,128)(2,1)S(1)} %collective-permute-done.2.recv_ref, bf16[2,512,512]{2,1,0:T(8,128)(2,1)S(1)} %get-tuple-element.42.w_ref.refs_3_, ...), custom_call_target="tpu_custom_call" | custom-call | tf_op jit(solution)/shard_map/pallas_call | solution.py:43
  36.2 0.4 copy-done.3
  36.6 2.9 %shard_map.58 = (bf16[2,256,1536]{2,1,0:T(8,128)(2,1)S(1)}, bf16[2,128,1536]{2,1,0:T(8,128)(2,1)S(1)}, bf16[2,128,1536]{2,1,0:T(8,128)(2,1)S(1)}) custom-call(s32[4]{0:T(128)S(1)} %copy-done.7, bf16[2,256,1536]{2,1,0:T(8,128)(2,1)S(1)} %copy-done.3, bf16[2,256,1536]{2,1,0:T(8,128)(2,1)S(1)} %collective-permute-done.1.sib_ref, ...), custom_call_target="tpu_custom_call" | custom-call | tf_op jit(solution)/shard_map/pallas_call | solution.py:43
  39.6 1.6 %collective-permute-done.9.rest_2_.rest_4_ = bf16[2,256,512]{2,1,0:T(8,128)(2,1)S(1)} collective-permute-done((bf16[2,256,512]{2,1,0:T(8,128)(2,1)S(1)}, bf16[2,256,512]{2,1,0:T(8,128)(2,1)S(1)}, u32[]{:S(2)}, u32[]{:S(2)}) %collective-permute-start.9) | collective-permute-done | bytes 524320 | tf_op jit(solution)/shard_map/ppermute | solution.py:89
  41.2 2.1 %collective-permute-start.11 = (bf16[2,256,512]{2,1,0:T(8,128)(2,1)S(1)}, bf16[2,256,512]{2,1,0:T(8,128)(2,1)S(1)}, u32[]{:S(2)}, u32[]{:S(2)}) collective-permute-start(bf16[2,256,512]{2,1,0:T(8,128)(2,1)S(1)} %copy-done.2), channel_id=1, source_target_pairs={{2,3},{3,2},{4,5},{5,4},{10,11},{11,10},{12,13},{13,12},{18,19},{1... | collective-permute-start | bytes 1572872 | tf_op jit(solution)/shard_map/ppermute | solution.py:89
  43.4 1.0 %shard_map.61 = (bf16[2,128,512]{2,1,0:T(8,128)(2,1)S(1)}, bf16[2,128,512]{2,1,0:T(8,128)(2,1)S(1)}) custom-call(s32[4]{0:T(128)S(1)} %copy-done.7, f32[2,128,1024]{2,1,0:T(8,128)S(1)} %get-tuple-element.45.acc_ref, bf16[2,128,512]{2,1,0:T(8,128)(2,1)S(1)} %get-tuple-element.46.hid_ref, bf16[2,256,512]{2,1,0:T(8,128)(2,1)S(1)} %collective-permute-done.7.rest_0_, ...), custom_call_target="tpu_custom_call" | custom-call | tf_op jit(solution)/shard_map/pallas_call | solution.py:43
  44.4 1.5 %collective-permute-start.16 = (bf16[2,128,512]{2,1,0:T(8,128)(2,1)S(1)}, bf16[2,128,512]{2,1,0:T(8,128)(2,1)S(1)}, u32[]{:S(2)}, u32[]{:S(2)}) collective-permute-start(bf16[2,128,512]{2,1,0:T(8,128)(2,1)S(1)} %get-tuple-element.54.side_ref.own_ref), channel_id=1, source_target_pairs={{0,4},{2,6},{4,0},{6,2},{8,12},{10,14},{12,8},{14,10},{16,20},{18,... | collective-permute-start | bytes 786440 | tf_op jit(solution)/shard_map/ppermute | solution.py:75
  45.9 6.8 %collective-permute-done.11.rest_2_ = bf16[2,256,512]{2,1,0:T(8,128)(2,1)S(1)} collective-permute-done((bf16[2,256,512]{2,1,0:T(8,128)(2,1)S(1)}, bf16[2,256,512]{2,1,0:T(8,128)(2,1)S(1)}, u32[]{:S(2)}, u32[]{:S(2)}) %collective-permute-start.11) | collective-permute-done | bytes 524320 | tf_op jit(solution)/shard_map/ppermute | solution.py:89
  52.8 0.6 shard_map.64
  53.3 1.5 %collective-permute-start.18 = (bf16[2,128,256]{2,1,0:T(8,128)(2,1)S(1)}, bf16[2,128,256]{2,1,0:T(8,128)(2,1)S(1)}, u32[]{:S(2)}, u32[]{:S(2)}) collective-permute-start(bf16[2,128,256]{2,1,0:T(8,128)(2,1)S(1)} %shard_map.64), channel_id=1, source_target_pairs={{0,1},{1,0},{2,3},{3,2},{4,5},{5,4},{6,7},{7,6},{8,9},{9,8},{10,11... | collective-permute-start | bytes 393224 | tf_op jit(solution)/shard_map/ppermute | solution.py:89
  54.9 3.1 %collective-permute-done.12.end_ref = bf16[2,128,512]{2,1,0:T(8,128)(2,1)S(1)} collective-permute-done((bf16[2,128,512]{2,1,0:T(8,128)(2,1)S(1)}, bf16[2,128,512]{2,1,0:T(8,128)(2,1)S(1)}, u32[]{:S(2)}, u32[]{:S(2)}) %collective-permute-start.12) | collective-permute-done | bytes 262176 | tf_op jit(solution)/shard_map/ppermute | solution.py:89
  58.0 1.7 %collective-permute-done.18.side_ref = bf16[2,128,256]{2,1,0:T(8,128)(2,1)S(1)} collective-permute-done((bf16[2,128,256]{2,1,0:T(8,128)(2,1)S(1)}, bf16[2,128,256]{2,1,0:T(8,128)(2,1)S(1)}, u32[]{:S(2)}, u32[]{:S(2)}) %collective-permute-start.18) | collective-permute-done | bytes 131104 | tf_op jit(solution)/shard_map/ppermute | solution.py:89
  59.7 2.7 %collective-permute-start.22 = (bf16[2,128,1536]{2,1,0:T(8,128)(2,1)S(1)}, bf16[2,128,1536]{2,1,0:T(8,128)(2,1)S(1)}, u32[]{:S(2)}, u32[]{:S(2)}) collective-permute-start(bf16[2,128,1536]{2,1,0:T(8,128)(2,1)S(1)} %get-tuple-element.56), channel_id=1, source_target_pairs={{2,3},{3,2},{4,5},{5,4},{10,11},{11,10},{12,13},{13,12},{18,19},{1... | collective-permute-start | bytes 2359304 | tf_op jit(solution)/shard_map/ppermute | solution.py:89
  62.4 0.6 shard_map.63.refs_0_
  63.0 3.6 %collective-permute-start.20 = (bf16[2,128,1536]{2,1,0:T(8,128)(2,1)S(1)}, bf16[2,128,1536]{2,1,0:T(8,128)(2,1)S(1)}, u32[]{:S(2)}, u32[]{:S(2)}) collective-permute-start(bf16[2,128,1536]{2,1,0:T(8,128)(2,1)S(1)} %shard_map.63.refs_0_), channel_id=1, source_target_pairs={{0,2},{2,0},{4,6},{6,4},{8,10},{10,8},{12,14},{14,12},{16,18},{18,... | collective-permute-start | bytes 2359304 | tf_op jit(solution)/shard_map/ppermute | solution.py:75
  66.6 0.1 collective-permute-done.19.sidex_ref
  66.7 0.6 shard_map.65.refs_1_
  67.3 3.8 %collective-permute-start.21 = (bf16[2,128,1536]{2,1,0:T(8,128)(2,1)S(1)}, bf16[2,128,1536]{2,1,0:T(8,128)(2,1)S(1)}, u32[]{:S(2)}, u32[]{:S(2)}) collective-permute-start(bf16[2,128,1536]{2,1,0:T(8,128)(2,1)S(1)} %shard_map.65.refs_1_), channel_id=1, source_target_pairs={{0,2},{2,0},{4,6},{6,4},{8,10},{10,8},{12,14},{14,12},{16,18},{18,... | collective-permute-start | bytes 2359304 | tf_op jit(solution)/shard_map/ppermute | solution.py:75
  71.1 3.4 %collective-permute-start.13 = (bf16[2,128,1536]{2,1,0:T(8,128)(2,1)S(1)}, bf16[2,128,1536]{2,1,0:T(8,128)(2,1)S(1)}, u32[]{:S(2)}, u32[]{:S(2)}) collective-permute-start(bf16[2,128,1536]{2,1,0:T(8,128)(2,1)S(1)} %get-tuple-element.52), channel_id=1, source_target_pairs={{2,3},{3,2},{4,5},{5,4},{10,11},{11,10},{12,13},{13,12},{18,19},{1... | collective-permute-start | bytes 2359304 | tf_op jit(solution)/shard_map/ppermute | solution.py:89
  74.6 1.9 %collective-permute-done.14.rest_3_ = bf16[2,256,512]{2,1,0:T(8,128)(2,1)S(1)} collective-permute-done((bf16[2,256,512]{2,1,0:T(8,128)(2,1)S(1)}, bf16[2,256,512]{2,1,0:T(8,128)(2,1)S(1)}, u32[]{:S(2)}, u32[]{:S(2)}) %collective-permute-start.14) | collective-permute-done | bytes 524320 | tf_op jit(solution)/shard_map/ppermute | solution.py:75
  76.5 0.8 shard_map.62.refs_5_
  77.4 0.8 shard_map.66.refs_6_
  78.1 4.3 %shard_map.67.refs_7_ = bf16[2,1,256,1536]{3,2,1,0:T(8,128)(2,1)} custom-call(s32[4]{0:T(128)S(1)} %copy-done.7, bf16[2,256,1536]{2,1,0:T(8,128)(2,1)S(1)} %get-tuple-element.37.refs_0_, bf16[2,128,1536]{2,1,0:T(8,128)(2,1)S(1)} %collective-permute-done.22.refs_1_, s32[512,1]{1,0:T(8,128)S(1)} %get-tuple-element.36.col_ref.refs_2_, ...), custom_call_target="tpu_custom_call" | custom-call | tf_op jit(solution)/shard_map/pallas_call | solution.py:43
  82.4 1.5 %collective-permute-done.13.refs_1_ = bf16[2,128,1536]{2,1,0:T(8,128)(2,1)S(1)} collective-permute-done((bf16[2,128,1536]{2,1,0:T(8,128)(2,1)S(1)}, bf16[2,128,1536]{2,1,0:T(8,128)(2,1)S(1)}, u32[]{:S(2)}, u32[]{:S(2)}) %collective-permute-start.13) | collective-permute-done | bytes 786464 | tf_op jit(solution)/shard_map/ppermute | solution.py:89
  83.9 4.3 %shard_map.68 = bf16[2,1,256,1536]{3,2,1,0:T(8,128)(2,1)} custom-call(s32[4]{0:T(128)S(1)} %copy-done.7, bf16[2,256,1536]{2,1,0:T(8,128)(2,1)S(1)} %get-tuple-element.37.refs_0_, bf16[2,128,1536]{2,1,0:T(8,128)(2,1)S(1)} %collective-permute-done.13.refs_1_, s32[512,1]{1,0:T(8,128)S(1)} %get-tuple-element.36.col_ref.refs_2_, ...), custom_call_target="tpu_custom_call", output_to_operand_aliasing={{}: (8, {})} | custom-call | tf_op jit(solution)/shard_map/pallas_call | solution.py:43
  (38 shorter events, 0.4 us)
Async XLA Ops:
  3.5 7.5 %copy-start.9 = (bf16[2,1,256,512]{3,2,1,0:T(8,128)(2,1)S(1)}, bf16[2,1,256,512]{3,2,1,0:T(8,128)(2,1)}, u32[]{:S(2)}) copy-start(bf16[2,1,256,512]{3,2,1,0:T(8,128)(2,1)} %param.6) | copy-start | bytes 1572868
  3.5 8.1 %copy-start.2 = (bf16[2,256,512]{2,1,0:T(8,128)(2,1)S(1)}, bf16[2,256,512]{2,1,0:T(8,128)(2,1)}, u32[]{:S(2)}) copy-start(bf16[2,256,512]{2,1,0:T(8,128)(2,1)} %get-tuple-element.50.end_ref.own_ref) | copy-start | bytes 1572868
  3.5 9.6 %copy-start.7 = (s32[4]{0:T(128)S(1)}, s32[4]{0:T(128)}, u32[]{:S(2)}) copy-start(s32[4]{0:T(128)} %pad_add_fusion.refs_0_.sc) | copy-start | bytes 52
  3.5 2.2 %collective-permute-start = (bf16[2,256,512]{2,1,0:T(8,128)(2,1)}, bf16[2,256,512]{2,1,0:T(8,128)(2,1)S(1)}, u32[]{:S(2)}, u32[]{:S(2)}) collective-permute-start(bf16[2,256,512]{2,1,0:T(8,128)(2,1)} %get-tuple-element.31.own_ref), channel_id=1, source_target_pairs={{0,2},{2,0},{4,6},{6,4},{8,10},{10,8},{12,14},{14,12},{16,18},{18,... | collective-permute-start | bytes 1572872 | tf_op jit(solution)/shard_map/ppermute | solution.py:75
  5.7 0.8 copy-start.5
  10.8 25.4 %collective-permute-start.1 = (bf16[2,256,1536]{2,1,0:T(8,128)(2,1)}, bf16[2,256,1536]{2,1,0:T(8,128)(2,1)S(1)}, u32[]{:S(2)}, u32[]{:S(2)}) collective-permute-start(bf16[2,256,1536]{2,1,0:T(8,128)(2,1)} %get-tuple-element.33.own_ref), channel_id=1, source_target_pairs={{0,2},{2,0},{4,6},{6,4},{8,10},{10,8},{12,14},{14,12},{16,18},{18,... | collective-permute-start | bytes 4718600 | tf_op jit(solution)/shard_map/ppermute | solution.py:75
  11.0 7.4 %copy-start.8 = (bf16[2,1,128,512]{3,2,1,0:T(8,128)(2,1)S(1)}, bf16[2,1,128,512]{3,2,1,0:T(8,128)(2,1)}, u32[]{:S(2)}) copy-start(bf16[2,1,128,512]{3,2,1,0:T(8,128)(2,1)} %param.7) | copy-start | bytes 786436
  11.2 20.1 %collective-permute-start.3 = (bf16[2,256,512]{2,1,0:T(8,128)(2,1)S(1)}, bf16[2,256,512]{2,1,0:T(8,128)(2,1)}, u32[]{:S(2)}, u32[]{:S(2)}) collective-permute-start(bf16[2,256,512]{2,1,0:T(8,128)(2,1)S(1)} %fusion.one_ref), channel_id=1, source_target_pairs={{0,2},{2,0},{4,6},{6,4},{8,10},{10,8},{12,14},{14,12},{16,18},{18,... | collective-permute-start | bytes 1572872 | tf_op jit(solution)/shard_map/ppermute | solution.py:75
  11.6 19.2 %collective-permute-start.7 = (bf16[2,256,512]{2,1,0:T(8,128)(2,1)S(1)}, bf16[2,256,512]{2,1,0:T(8,128)(2,1)S(1)}, u32[]{:S(2)}, u32[]{:S(2)}) collective-permute-start(bf16[2,256,512]{2,1,0:T(8,128)(2,1)S(1)} %copy-done.2), channel_id=1, source_target_pairs={{0,1},{1,0},{6,7},{7,6},{8,9},{9,8},{14,15},{15,14},{16,17},{17,16... | collective-permute-start | bytes 1572872 | tf_op jit(solution)/shard_map/ppermute | solution.py:89
  13.1 1.4 %copy-start = (bf16[2,256,1536]{2,1,0:T(8,128)(2,1)S(1)}, bf16[2,256,1536]{2,1,0:T(8,128)(2,1)}, u32[]{:S(2)}) copy-start(bf16[2,256,1536]{2,1,0:T(8,128)(2,1)} %get-tuple-element.34.end_ref) | copy-start | bytes 4718596
  14.5 1.0 %copy-start.4 = (bf16[2,256,512]{2,1,0:T(8,128)(2,1)S(1)}, bf16[2,256,512]{2,1,0:T(8,128)(2,1)}, u32[]{:S(2)}) copy-start(bf16[2,256,512]{2,1,0:T(8,128)(2,1)} %get-tuple-element.31.own_ref) | copy-start | bytes 1572868
  15.5 1.0 %copy-start.6 = (bf16[2,256,512]{2,1,0:T(8,128)(2,1)S(1)}, bf16[2,256,512]{2,1,0:T(8,128)(2,1)}, u32[]{:S(2)}) copy-start(bf16[2,256,512]{2,1,0:T(8,128)(2,1)} %copy-done.5) | copy-start | bytes 1572868
  18.5 10.6 %collective-permute-start.4 = (bf16[2,128,512]{2,1,0:T(8,128)(2,1)S(1)}, bf16[2,128,512]{2,1,0:T(8,128)(2,1)S(1)}, u32[]{:S(2)}, u32[]{:S(2)}) collective-permute-start(bf16[2,128,512]{2,1,0:T(8,128)(2,1)S(1)} %fusion.1), channel_id=1, source_target_pairs={{0,4},{2,6},{4,0},{6,2},{8,12},{10,14},{12,8},{14,10},{16,20},{18,... | collective-permute-start | bytes 786440 | tf_op jit(solution)/shard_map/ppermute | solution.py:75
  29.2 4.2 %collective-permute-start.5 = (bf16[2,2,128,512]{3,2,1,0:T(8,128)(2,1)S(1)}, bf16[2,2,128,512]{3,2,1,0:T(8,128)(2,1)S(1)}, u32[]{:S(2)}, u32[]{:S(2)}) collective-permute-start(bf16[2,2,128,512]{3,2,1,0:T(8,128)(2,1)S(1)} %pad_maximum_fusion.two_ref), channel_id=1, source_target_pairs={{0,2},{2,0},{4,6},{6,4},{8,10},{10,8},{12,14},{14,12},{16,18},{18,... | collective-permute-start | bytes 1572872 | tf_op jit(solution)/shard_map/ppermute | solution.py:75
  30.8 3.9 %collective-permute-start.6 = (bf16[2,256,512]{2,1,0:T(8,128)(2,1)S(1)}, bf16[2,256,512]{2,1,0:T(8,128)(2,1)S(1)}, u32[]{:S(2)}, u32[]{:S(2)}) collective-permute-start(bf16[2,256,512]{2,1,0:T(8,128)(2,1)S(1)} %copy-done.2), channel_id=1, source_target_pairs={{0,2},{2,0},{4,6},{6,4},{8,10},{10,8},{12,14},{14,12},{16,18},{18,... | collective-permute-start | bytes 1572872 | tf_op jit(solution)/shard_map/ppermute | solution.py:75
  30.9 3.9 %collective-permute-start.2 = (bf16[2,128,1024]{2,1,0:T(8,128)(2,1)S(1)}, bf16[2,128,1024]{2,1,0:T(8,128)(2,1)S(1)}, u32[]{:S(2)}, u32[]{:S(2)}) collective-permute-start(bf16[2,128,1024]{2,1,0:T(8,128)(2,1)S(1)} %get-tuple-element.40), channel_id=1, source_target_pairs={{0,2},{2,0},{4,6},{6,4},{8,10},{10,8},{12,14},{14,12},{16,18},{18,... | collective-permute-start | bytes 1572872 | tf_op jit(solution)/shard_map/ppermute | solution.py:75
  31.3 9.9 %collective-permute-start.9 = (bf16[2,256,512]{2,1,0:T(8,128)(2,1)S(1)}, bf16[2,256,512]{2,1,0:T(8,128)(2,1)S(1)}, u32[]{:S(2)}, u32[]{:S(2)}) collective-permute-start(bf16[2,256,512]{2,1,0:T(8,128)(2,1)S(1)} %get-tuple-element.47.side_ref), channel_id=1, source_target_pairs={{2,3},{3,2},{4,5},{5,4},{10,11},{11,10},{12,13},{13,12},{18,19},{1... | collective-permute-start | bytes 1572872 | tf_op jit(solution)/shard_map/ppermute | solution.py:89
  33.4 9.9 %collective-permute-start.8 = (bf16[2,256,512]{2,1,0:T(8,128)(2,1)S(1)}, bf16[2,256,512]{2,1,0:T(8,128)(2,1)S(1)}, u32[]{:S(2)}, u32[]{:S(2)}) collective-permute-start(bf16[2,256,512]{2,1,0:T(8,128)(2,1)S(1)} %collective-permute-done.7.rest_0_), channel_id=1, source_target_pairs={{0,2},{2,0},{4,6},{6,4},{8,10},{10,8},{12,14},{14,12},{16,18},{18,... | collective-permute-start | bytes 1572872 | tf_op jit(solution)/shard_map/ppermute | solution.py:75
  34.7 1.4 %copy-start.1 = (bf16[2,256,1536]{2,1,0:T(8,128)(2,1)S(1)}, bf16[2,256,1536]{2,1,0:T(8,128)(2,1)}, u32[]{:S(2)}) copy-start(bf16[2,256,1536]{2,1,0:T(8,128)(2,1)} %get-tuple-element.34.end_ref) | copy-start | bytes 4718596
  34.7 1.9 %copy-start.3 = (bf16[2,256,1536]{2,1,0:T(8,128)(2,1)S(1)}, bf16[2,256,1536]{2,1,0:T(8,128)(2,1)}, u32[]{:S(2)}) copy-start(bf16[2,256,1536]{2,1,0:T(8,128)(2,1)} %get-tuple-element.33.own_ref) | copy-start | bytes 4718596
  41.2 2.1 %collective-permute-start.10 = (bf16[2,256,512]{2,1,0:T(8,128)(2,1)S(1)}, bf16[2,256,512]{2,1,0:T(8,128)(2,1)S(1)}, u32[]{:S(2)}, u32[]{:S(2)}) collective-permute-start(bf16[2,256,512]{2,1,0:T(8,128)(2,1)S(1)} %collective-permute-done.9.rest_2_.rest_4_), channel_id=1, source_target_pairs={{0,2},{2,0},{4,6},{6,4},{8,10},{10,8},{12,14},{14,12},{16,18},{18,... | collective-permute-start | bytes 1572872 | tf_op jit(solution)/shard_map/ppermute | solution.py:75
  41.2 11.5 %collective-permute-start.11 = (bf16[2,256,512]{2,1,0:T(8,128)(2,1)S(1)}, bf16[2,256,512]{2,1,0:T(8,128)(2,1)S(1)}, u32[]{:S(2)}, u32[]{:S(2)}) collective-permute-start(bf16[2,256,512]{2,1,0:T(8,128)(2,1)S(1)} %copy-done.2), channel_id=1, source_target_pairs={{2,3},{3,2},{4,5},{5,4},{10,11},{11,10},{12,13},{13,12},{18,19},{1... | collective-permute-start | bytes 1572872 | tf_op jit(solution)/shard_map/ppermute | solution.py:89
  44.4 8.4 %collective-permute-start.16 = (bf16[2,128,512]{2,1,0:T(8,128)(2,1)S(1)}, bf16[2,128,512]{2,1,0:T(8,128)(2,1)S(1)}, u32[]{:S(2)}, u32[]{:S(2)}) collective-permute-start(bf16[2,128,512]{2,1,0:T(8,128)(2,1)S(1)} %get-tuple-element.54.side_ref.own_ref), channel_id=1, source_target_pairs={{0,4},{2,6},{4,0},{6,2},{8,12},{10,14},{12,8},{14,10},{16,20},{18,... | collective-permute-start | bytes 786440 | tf_op jit(solution)/shard_map/ppermute | solution.py:75
  52.7 5.2 %collective-permute-start.12 = (bf16[2,128,512]{2,1,0:T(8,128)(2,1)S(1)}, bf16[2,128,512]{2,1,0:T(8,128)(2,1)S(1)}, u32[]{:S(2)}, u32[]{:S(2)}) collective-permute-start(bf16[2,128,512]{2,1,0:T(8,128)(2,1)S(1)} %get-tuple-element.51.end_ref), channel_id=1, source_target_pairs={{0,1},{1,0},{2,3},{3,2},{4,5},{5,4},{6,7},{7,6},{8,9},{9,8},{10,11... | collective-permute-start | bytes 786440 | tf_op jit(solution)/shard_map/ppermute | solution.py:89
  52.8 9.7 %collective-permute-start.15 = (bf16[2,128,512]{2,1,0:T(8,128)(2,1)S(1)}, bf16[2,128,512]{2,1,0:T(8,128)(2,1)S(1)}, u32[]{:S(2)}, u32[]{:S(2)}) collective-permute-start(bf16[2,128,512]{2,1,0:T(8,128)(2,1)S(1)} %get-tuple-element.51.end_ref), channel_id=1, source_target_pairs={{0,4},{2,6},{4,0},{6,2},{8,12},{10,14},{12,8},{14,10},{16,20},{18,... | collective-permute-start | bytes 786440 | tf_op jit(solution)/shard_map/ppermute | solution.py:75
  53.3 6.3 %collective-permute-start.18 = (bf16[2,128,256]{2,1,0:T(8,128)(2,1)S(1)}, bf16[2,128,256]{2,1,0:T(8,128)(2,1)S(1)}, u32[]{:S(2)}, u32[]{:S(2)}) collective-permute-start(bf16[2,128,256]{2,1,0:T(8,128)(2,1)S(1)} %shard_map.64), channel_id=1, source_target_pairs={{0,1},{1,0},{2,3},{3,2},{4,5},{5,4},{6,7},{7,6},{8,9},{9,8},{10,11... | collective-permute-start | bytes 393224 | tf_op jit(solution)/shard_map/ppermute | solution.py:89
  58.0 8.6 %collective-permute-start.17 = (bf16[2,128,512]{2,1,0:T(8,128)(2,1)S(1)}, bf16[2,128,512]{2,1,0:T(8,128)(2,1)S(1)}, u32[]{:S(2)}, u32[]{:S(2)}) collective-permute-start(bf16[2,128,512]{2,1,0:T(8,128)(2,1)S(1)} %collective-permute-done.12.end_ref), channel_id=1, source_target_pairs={{0,4},{2,6},{4,0},{6,2},{8,12},{10,14},{12,8},{14,10},{16,20},{18,... | collective-permute-start | bytes 786440 | tf_op jit(solution)/shard_map/ppermute | solution.py:75
  59.7 7.0 %collective-permute-start.19 = (bf16[2,128,256]{2,1,0:T(8,128)(2,1)S(1)}, bf16[2,128,256]{2,1,0:T(8,128)(2,1)S(1)}, u32[]{:S(2)}, u32[]{:S(2)}) collective-permute-start(bf16[2,128,256]{2,1,0:T(8,128)(2,1)S(1)} %collective-permute-done.18.side_ref), channel_id=1, source_target_pairs={{0,4},{2,6},{4,0},{6,2},{8,12},{10,14},{12,8},{14,10},{16,20},{18,... | collective-permute-start | bytes 393224 | tf_op jit(solution)/shard_map/ppermute | solution.py:75
  59.7 18.4 %collective-permute-start.22 = (bf16[2,128,1536]{2,1,0:T(8,128)(2,1)S(1)}, bf16[2,128,1536]{2,1,0:T(8,128)(2,1)S(1)}, u32[]{:S(2)}, u32[]{:S(2)}) collective-permute-start(bf16[2,128,1536]{2,1,0:T(8,128)(2,1)S(1)} %get-tuple-element.56), channel_id=1, source_target_pairs={{2,3},{3,2},{4,5},{5,4},{10,11},{11,10},{12,13},{13,12},{18,19},{1... | collective-permute-start | bytes 2359304 | tf_op jit(solution)/shard_map/ppermute | solution.py:89
  63.0 14.3 %collective-permute-start.20 = (bf16[2,128,1536]{2,1,0:T(8,128)(2,1)S(1)}, bf16[2,128,1536]{2,1,0:T(8,128)(2,1)S(1)}, u32[]{:S(2)}, u32[]{:S(2)}) collective-permute-start(bf16[2,128,1536]{2,1,0:T(8,128)(2,1)S(1)} %shard_map.63.refs_0_), channel_id=1, source_target_pairs={{0,2},{2,0},{4,6},{6,4},{8,10},{10,8},{12,14},{14,12},{16,18},{18,... | collective-permute-start | bytes 2359304 | tf_op jit(solution)/shard_map/ppermute | solution.py:75
  67.3 10.0 %collective-permute-start.21 = (bf16[2,128,1536]{2,1,0:T(8,128)(2,1)S(1)}, bf16[2,128,1536]{2,1,0:T(8,128)(2,1)S(1)}, u32[]{:S(2)}, u32[]{:S(2)}) collective-permute-start(bf16[2,128,1536]{2,1,0:T(8,128)(2,1)S(1)} %shard_map.65.refs_1_), channel_id=1, source_target_pairs={{0,2},{2,0},{4,6},{6,4},{8,10},{10,8},{12,14},{14,12},{16,18},{18,... | collective-permute-start | bytes 2359304 | tf_op jit(solution)/shard_map/ppermute | solution.py:75
  71.1 12.8 %collective-permute-start.13 = (bf16[2,128,1536]{2,1,0:T(8,128)(2,1)S(1)}, bf16[2,128,1536]{2,1,0:T(8,128)(2,1)S(1)}, u32[]{:S(2)}, u32[]{:S(2)}) collective-permute-start(bf16[2,128,1536]{2,1,0:T(8,128)(2,1)S(1)} %get-tuple-element.52), channel_id=1, source_target_pairs={{2,3},{3,2},{4,5},{5,4},{10,11},{11,10},{12,13},{13,12},{18,19},{1... | collective-permute-start | bytes 2359304 | tf_op jit(solution)/shard_map/ppermute | solution.py:89
  74.5 2.0 %collective-permute-start.14 = (bf16[2,256,512]{2,1,0:T(8,128)(2,1)S(1)}, bf16[2,256,512]{2,1,0:T(8,128)(2,1)S(1)}, u32[]{:S(2)}, u32[]{:S(2)}) collective-permute-start(bf16[2,256,512]{2,1,0:T(8,128)(2,1)S(1)} %collective-permute-done.11.rest_2_), channel_id=1, source_target_pairs={{0,2},{2,0},{4,6},{6,4},{8,10},{10,8},{12,14},{14,12},{16,18},{18,... | collective-permute-start | bytes 1572872 | tf_op jit(solution)/shard_map/ppermute | solution.py:75

commit v5 on v4

v5 whole, which is shorter than its diff:
```python
import jax
import jax.numpy as jnp
from jax import lax
from jax.experimental import pallas as pl
from jax.experimental.pallas import tpu as pltpu
from jax.sharding import PartitionSpec as P

BF16 = jnp.bfloat16
F32 = jnp.float32
VMEM_BYTES = 28 * 1024 * 1024
SLOTS_COST = 20_000_000_000
LEAF_VMEM_BYTES = 60 * 1024 * 1024


def dot(first, second):
    return jnp.dot(first, second, preferred_element_type=F32)


def stacked(real, imag):
    return jnp.concatenate(
        [jnp.concatenate([real, -imag], axis=1), jnp.concatenate([imag, real], axis=1)], axis=0
    )


def flat(array):
    return array.reshape(array.shape[0] * array.shape[1], array.shape[2])


def column_picker(index, offset, count):
    rows = lax.broadcasted_iota(jnp.int32, (count, index.shape[1]), 0) + offset
    return jnp.where(rows == index, 1.0, 0.0).astype(BF16)


def row_picker(index, offset, count):
    cols = lax.broadcasted_iota(jnp.int32, (index.shape[0], count), 1) + offset
    return jnp.where(cols == index, 1.0, 0.0).astype(BF16)


def call(kernel, scalars, inputs, out_shapes, specs=None, out_specs=None, scratch=(), cost=0, vmem=VMEM_BYTES):
    in_vmem = pl.BlockSpec(memory_space=pltpu.VMEM)
    specs = specs or [in_vmem] * len(inputs)
    out_specs = out_specs or [in_vmem] * len(out_shapes)
    return pl.pallas_call(
        kernel,
        in_specs=[pl.BlockSpec(memory_space=pltpu.SMEM)] + specs,
        out_specs=out_specs,
        out_shape=out_shapes,
        scratch_shapes=list(scratch),
        compiler_params=pltpu.CompilerParams(vmem_limit_bytes=vmem),
        cost_estimate=pl.CostEstimate(flops=cost, bytes_accessed=0, transcendentals=0),
    )(scalars, *inputs)


def after(array, *others):
    return lax.optimization_barrier((array, *others))[0]


def on_device(leaf_maps, w_first, w_second, skel_first, skel_second):
    box = lax.axis_index("box")
    face = lax.axis_index("face")
    n_box, n_face = lax.axis_size("box"), lax.axis_size("face")
    nf = n_face - 1
    fr = leaf_maps.shape[4]
    hr = fr // 2
    k = leaf_maps.shape[5] // 3
    half = k // 2
    leaf = leaf_maps[:, 0, 0]
    par = box % 2
    par2 = box // 2 % 2
    scalars = jnp.stack([par, par2, face, box % 4]).astype(jnp.int32)
    sds = jax.ShapeDtypeStruct

    def box_permute(array, mask):
        return lax.ppermute(array, "box", [(b, b ^ mask) for b in range(n_box)])

    def keeper(b):
        return (b & 1) != (b >> 1 & 1)

    def giver(b):
        return not keeper(b)

    def face_permute(array, step, senders=None):
        pairs = [
            (b * n_face + f, b * n_face + (f + n_face - step) % n_face)
            for b in range(n_box) if senders is None or senders(b)
            for f in range(n_face)
        ]
        return lax.ppermute(array, ("box", "face"), pairs)

    def over_face(array, senders=None):
        return [face_permute(array, s, senders) for s in range(1, n_face)]

    skel_one = lax.dynamic_index_in_dim(skel_first[0], box // 2, 0, keepdims=True)
    skel_two = lax.dynamic_index_in_dim(skel_second[0], box // 4, 0, keepdims=True)

    in_hbm = pl.BlockSpec(memory_space=pltpu.HBM)
    in_vmem = pl.BlockSpec(memory_space=pltpu.VMEM)
    splits = 4
    qr = fr // splits

    def copy_kernel(sc, leaf_ref, end_out, side_out, sems):
        p = sc[0]
        copies = []
        for t in range(2):
            for i in range(splits):
                rows = pl.ds(i * qr, qr)
                for j, (out, start) in enumerate(((end_out, p * k), (side_out, 2 * k))):
                    copies.append(pltpu.make_async_copy(
                        leaf_ref.at[t, 1 - p, rows, pl.ds(pl.multiple_of(start, k), k)],
                        out.at[t, rows], sems.at[t, i, j],
                    ))
        for copy in copies:
            copy.start()
        for copy in copies:
            copy.wait()

    end_own, sides_raw = call(
        copy_kernel, scalars, [leaf], [sds((2, fr, k), BF16)] * 2, specs=[in_hbm], out_specs=[in_hbm] * 2,
        scratch=[pltpu.SemaphoreType.DMA((2, splits, 2))], vmem=LEAF_VMEM_BYTES,
    )
    end_sib = box_permute(end_own, 1)
    sides_sib = box_permute(sides_raw, 1)

    def split_kernel(sc, own_ref, sib_ref, first_out, rest_out):
        p, q = sc[0], sc[1]
        rows = pl.ds(pl.multiple_of(p * hr, hr), hr)
        own, sib = own_ref[:, rows, :], sib_ref[:, rows, :]
        first_out[...] = jnp.where(p == q, own, sib)
        rest_out[...] = jnp.where(p == q, sib, own)

    first_send, rest_send = call(
        split_kernel, scalars, [end_own, end_sib], [sds((2, hr, k), BF16)] * 2,
    )
    first_far = over_face(first_send)
    first_fwd = [box_permute(a, 1) for a in first_far]

    def slots_kernel(sc, leaf_ref, own_ref, sib_ref, skel_ref, skel2_ref,
                     comp_out, col_out, side_out, half_out, keep_out, send_out, rows_out, end_out):
        p, q = sc[0], sc[1]
        rows = lax.broadcasted_iota(jnp.int32, (k, k), 0)
        cols = lax.broadcasted_iota(jnp.int32, (k, k), 1)
        skel = jnp.broadcast_to(skel_ref[...].astype(F32), (k, k))
        column = jnp.sum(jnp.where(rows == cols, skel, 0.0), axis=1, keepdims=True)
        col_out[...] = column.astype(jnp.int32)
        place = skel2_ref[...] - q * k
        taken = jnp.where(rows == place, jnp.broadcast_to(column, (k, k)), 0.0)
        comp = jnp.sum(taken, axis=0, keepdims=True).astype(jnp.int32)
        mine = jnp.logical_and(place >= 0, place < k)
        comp = jnp.where(mine, comp, -1)
        comp_out[...] = comp
        pick_own = column_picker(comp, p * k, k)
        pick_sib = column_picker(comp, (1 - p) * k, k)
        side = dot(flat(own_ref[...]), pick_own) + dot(flat(sib_ref[...]), pick_sib)
        side_out[...] = side.astype(BF16).reshape(2, fr, k)
        half_out[...] = side_out[:, pl.ds(pl.multiple_of(p * hr, hr), hr), :]
        rows_out[...] = leaf_ref[:, 2]
        for t in range(2):
            end_out[t, :, : 2 * k] = leaf_ref[t, p, :, : 2 * k]
            end_out[t, :, 2 * k :] = dot(leaf_ref[t, p, :, 2 * k :], pick_own).astype(BF16)
        couple = pl.ds(pl.multiple_of((1 - p) * k, k), k)
        for ref, h in ((keep_out, p), (send_out, 1 - p)):
            take = pl.ds(pl.multiple_of(h * hr, hr), hr)
            for t in range(2):
                ref[t, :, :k] = leaf_ref[t, p, take, couple]
                ref[t, :, k:] = end_out[t, take, 2 * k :]

    comp, skel_col, side, side_half, v_keep, v_send, s_rows, end_kept = call(
        slots_kernel, after(scalars, first_send), [leaf, sides_raw, sides_sib, skel_one, skel_two],
        [sds((1, k), jnp.int32), sds((k, 1), jnp.int32), sds((2, fr, k), BF16),
         sds((2, hr, k), BF16), sds((2, hr, 2 * k), BF16), sds((2, hr, 2 * k), BF16),
         sds((2, fr, 3 * k), BF16), sds((2, fr, 3 * k), BF16)], cost=SLOTS_COST,
    )
    s_sib = box_permute(after(s_rows, *first_far), 1)
    side_far = over_face(after(side_half, *first_far))
    v_recv = box_permute(after(v_send, *first_far), 1)

    w_one = jnp.roll(w_first[:, 0], -face * fr, axis=2)
    w_one_sib = box_permute(w_one, 1)
    w_two = jnp.roll(w_second[:, 0], -face * fr, axis=2)
    w_two_x = box_permute(after(w_two, first_send), 2)

    def weight_one_kernel(sc, own_ref, sib_ref, out_ref):
        p = sc[0]
        out_ref[:, pl.ds(pl.multiple_of(p * half, half), half), :] = own_ref[...]
        out_ref[:, pl.ds(pl.multiple_of((1 - p) * half, half), half), :] = sib_ref[...]

    (weight_one,) = call(weight_one_kernel, scalars, [w_one, w_one_sib], [sds((2, k, k), BF16)])


    def rows_kernel(sc, own_ref, sib_ref, comp_ref, col_ref, kept_out, *outs):
        p, q, f = sc[0], sc[1], sc[2]
        pick_own = column_picker(comp_ref[...], p * k, k)
        pick_sib = column_picker(comp_ref[...], (1 - p) * k, k)

        def pick(slots, write):
            take_own = row_picker(slots, p * k + f * fr, fr)
            take_sib = row_picker(slots, (1 - p) * k + f * fr, fr)
            for t in range(2):
                for c in range(3):
                    cols = slice(c * k, (c + 1) * k)
                    own, sib = own_ref[t, :, cols], sib_ref[t, :, cols]
                    if c == 2:
                        own, sib = [dot(a, b).astype(BF16) for a, b in ((own, pick_own), (sib, pick_sib))]
                    write(t, cols, (dot(take_own, own) + dot(take_sib, sib)).astype(BF16))

        def col_half(s):
            start = (f + n_face - s - 1) % n_face * fr + p * hr
            return col_ref[pl.ds(pl.multiple_of(start, hr), hr), :]

        @pl.when(p == q)
        def _():
            far = jnp.concatenate([col_half(s) for s in range(nf)], axis=0)

            def write(t, cols, picked):
                for s in range(nf):
                    outs[s][t, :, cols] = picked[s * hr : (s + 1) * hr]

            pick(far, write)

        @pl.when(p != q)
        def _():
            far = jnp.concatenate([col_half(s) for s in range(nf)], axis=0)
            slots = jnp.concatenate([col_ref[pl.ds(pl.multiple_of(f * fr, fr), fr), :], far], axis=0)

            def write(t, cols, picked):
                kept_out[t, :, cols] = picked[:fr]
                for s in range(nf):
                    outs[s][t, :, cols] = picked[fr + s * hr : fr + (s + 1) * hr]

            pick(slots, write)

    kept, *kept_out = call(
        rows_kernel, scalars, [s_rows, s_sib, comp, skel_col],
        [sds((2, fr, 3 * k), BF16)] + [sds((2, hr, 3 * k), BF16)] * nf,
    )

    def piece(hidden, start, count):
        return stacked(hidden[0][:, start : start + count], hidden[1][:, start : start + count])

    def iface_kernel(sc, keep_ref, recv_ref, w_ref, end_ref, endsib_ref, side_ref,
                     acc_out, hid_out, rows):
        p, q = sc[0], sc[1]

        @pl.when(p == q)
        def _():
            rows[...] = recv_ref[...]

        @pl.when(p != q)
        def _():
            rows[...] = keep_ref[...]

        both = dot(stacked(rows[0, :, :k], rows[1, :, :k]), flat(w_ref[...])).astype(BF16)
        hidden = both[:hr], both[hr:]
        hid_out[0] = hidden[0]
        hid_out[1] = hidden[1]
        left = piece(hidden, 0, fr)
        is_end = p == q
        ends = jnp.where(is_end, end_ref[...], endsib_ref[...])
        acc_out[:, :, :k] = -dot(left, flat(ends)).reshape(2, hr, k)
        acc_out[:, :, k:] = rows[:, :, k:].astype(F32) - dot(left, flat(side_ref[...])).reshape(2, hr, k)

    v_acc, v_hid = call(
        iface_kernel, scalars, [v_keep, v_recv, weight_one, end_own, end_sib, side],
        [sds((2, hr, 2 * k), F32), sds((2, hr, k), BF16)],
        scratch=[pltpu.VMEM((2, hr, 2 * k), BF16)],
    )
    w_two_pair = jnp.stack([w_two, w_two_x])
    w_two_sib = box_permute(w_two_pair, 1)

    def weight_two_kernel(sc, own_ref, sib_ref, out_ref):
        r = sc[3]
        blk = k // 4
        for i, (ref, part) in enumerate(((own_ref, 0), (own_ref, 1), (sib_ref, 0), (sib_ref, 1))):
            place = r ^ (part * 2) ^ (i // 2)
            out_ref[:, pl.ds(pl.multiple_of(place * blk, blk), blk), :] = ref[part]

    (weight_two,) = call(weight_two_kernel, scalars, [w_two_pair, w_two_sib], [sds((2, k, k), BF16)])

    side_fwd = [box_permute(after(a, kept, v_acc, w_two_x), 1) for a in side_far]
    rest_far = over_face(after(rest_send, kept, v_acc))

    def iface_far_kernel(sc, acc_ref, hid_ref, *rest):
        refs = [rest[i * nf : (i + 1) * nf] for i in range(4)]
        out_ref, rows = rest[4 * nf :]
        p = sc[0]
        mine = pl.ds(pl.multiple_of(p * hr, hr), hr)
        other = pl.ds(pl.multiple_of((1 - p) * hr, hr), hr)
        hidden = [hid_ref[0], hid_ref[1]]
        total = acc_ref[...]
        for s in range(nf):
            rows[:, mine, :k] = refs[0][s][...]
            rows[:, other, :k] = refs[1][s][...]
            rows[:, mine, k:] = refs[2][s][...]
            rows[:, other, k:] = refs[3][s][...]
            left = piece(hidden, (s + 1) * fr, fr)
            total = total - dot(left, flat(rows[...])).reshape(2, hr, 2 * k)
        out_ref[...] = total.astype(BF16)

    (two_own,) = call(
        iface_far_kernel, scalars, [v_acc, v_hid, *first_far, *first_fwd, *side_far, *side_fwd],
        [sds((2, hr, 2 * k), BF16)], scratch=[pltpu.VMEM((2, fr, 2 * k), BF16)],
    )
    rest_fwd = [box_permute(after(a, two_own), 1) for a in rest_far]

    def gather_kernel(sc, own_ref, sib_ref, side_ref, *rest):
        refs = [rest[i * nf : (i + 1) * nf] for i in range(6)]
        out_ref = rest[6 * nf]
        p, q = sc[0], sc[1]

        def block(which):
            return pl.ds(pl.multiple_of(which * k, k), k)

        out_ref[0, :, :, block(p)] = own_ref[...]
        out_ref[0, :, :, block(1 - p)] = sib_ref[...]
        out_ref[0, :, :, 2 * k :] = side_ref[...]
        for i, which in enumerate((q, 1 - q, 2)):
            for h in range(2):
                rows = pl.ds(pl.multiple_of((p ^ h) * hr, hr), hr)
                for s in range(nf):
                    out_ref[s + 1, :, rows, block(which)] = refs[2 * i + h][s][...]

    (iface,) = call(
        gather_kernel, scalars,
        [end_own, end_sib, side, *first_far, *first_fwd, *rest_far, *rest_fwd, *side_far, *side_fwd],
        [sds((n_face, 2, fr, 3 * k), BF16)],
    )

    two_x = box_permute(two_own, 2)
    two_y = over_face(after(two_own, *rest_far))
    two_xy = [box_permute(after(a, two_x), 2) for a in two_y]

    def join_kernel(sc, own_ref, x_ref, out_ref):
        q = sc[1]
        out_ref[:, :, pl.ds(pl.multiple_of(q * k, k), k)] = own_ref[:, :, :k]
        out_ref[:, :, pl.ds(pl.multiple_of((1 - q) * k, k), k)] = x_ref[:, :, :k]
        out_ref[:, :, 2 * k :] = own_ref[:, :, k:] + x_ref[:, :, k:]

    two_rows = []
    ready = after(scalars, weight_two, iface)
    for own, other in zip([two_own, *two_y], [two_x, *two_xy]):
        two_rows += call(join_kernel, ready, [own, other], [sds((2, hr, 3 * k), BF16)])
    two_sib = [box_permute(a, 1) for a in two_rows]

    def level_two_kernel(sc, *refs):
        out_ref = refs[-1]
        p = sc[0]
        for s in range(n_face):
            out_ref[s, :, pl.ds(pl.multiple_of(p * hr, hr), hr), :] = refs[s][...]
            out_ref[s, :, pl.ds(pl.multiple_of((1 - p) * hr, hr), hr), :] = refs[n_face + s][...]

    (iface_two,) = call(
        level_two_kernel, scalars, [*two_rows, *two_sib], [sds((n_face, 2, fr, 3 * k), BF16)],
    )

    kept_far = [face_permute(after(a, two_own), i + 1) for i, a in enumerate(kept_out)]
    kept_fwd = [box_permute(a, 1) for a in kept_far]

    cr = fr

    def keep_kernel(sc, *refs):
        end_ref, kept_ref, *refs = refs
        far, fwd, refs = refs[:nf], refs[nf : 2 * nf], refs[2 * nf :]
        col_ref, w_ref, w2_ref, iface_ref, iface2_ref, out_ref, zs, stage, sems = refs
        p, q, f = sc[0], sc[1], sc[2]
        is_end = p == q

        @pl.when(is_end)
        def _():
            zs[...] = end_ref[...]

        @pl.when(p != q)
        def _():
            for h, parts in enumerate((far, fwd)):
                take = pl.ds(pl.multiple_of((p ^ h) * hr, hr), hr)
                total = kept_ref[:, take, :]
                for part in parts:
                    total = total + part[...]
                zs[:, take, :] = total

        def wide(rows):
            parts = [piece((rows[:cr], rows[cr:]), s * fr, fr) for s in range(n_face)]
            return jnp.concatenate(parts, axis=1)

        def gathered(ref, c):
            return ref[:, :, :, c * k : (c + 1) * k].reshape(n_face * 2 * fr, k)

        def rows(t, c):
            return zs[t, :, c * k : (c + 1) * k]

        slots = col_ref[pl.ds(pl.multiple_of(f * fr, fr), fr), :]
        right = jnp.where(slots >= k, 1, 0)
        right = jnp.where(is_end, p, right) > 0
        lefts = [rows(t, 0) for t in range(2)]
        rights = [rows(t, 1) for t in range(2)]
        couple = [jnp.where(right, a, b) for a, b in zip(lefts, rights)]

        both = dot(stacked(couple[0], couple[1]), flat(w_ref[...])).astype(BF16)
        left = wide(both)
        nothing = jnp.zeros((cr, k), BF16)
        start = [
            jnp.concatenate([jnp.where(right, nothing, a) for a in lefts], axis=0),
            jnp.concatenate([jnp.where(right, a, nothing) for a in rights], axis=0),
            jnp.concatenate([rows(t, 2) for t in range(2)], axis=0),
        ]
        merged = []
        for c in range(3):
            merged.append((start[c].astype(F32) - dot(left, gathered(iface_ref, c))).astype(BF16))
        is_left = q == 0
        couple2 = jnp.where(is_left, merged[1], merged[0])
        second = dot(stacked(couple2[:cr], couple2[cr:]), flat(w2_ref[...])).astype(BF16)
        left = wide(second)
        none = jnp.zeros_like(merged[0])
        copies = []
        first = [jnp.where(is_left, merged[0], none), jnp.where(is_left, none, merged[1]), merged[2]]
        for c in range(3):
            cols = slice(c * k, (c + 1) * k)
            total = first[c].astype(F32) - dot(left, gathered(iface2_ref, c))
            stage[:, :, cols] = total.astype(BF16).reshape(2, cr, k)
            copies.append(pltpu.make_async_copy(
                stage.at[:, :, pl.ds(c * k, k)],
                out_ref.at[:, 0, :, pl.ds(c * k, k)],
                sems.at[c],
            ))
            copies[-1].start()
        for copy in copies:
            copy.wait()

    (out,) = call(
        keep_kernel, scalars,
        [end_kept, kept, *kept_far, *kept_fwd, skel_col, weight_one, weight_two, iface, iface_two],
        [sds((2, 1, fr, 3 * k), BF16)], out_specs=[in_hbm],
        scratch=[pltpu.VMEM((2, fr, 3 * k), BF16), pltpu.VMEM((2, fr, 3 * k), BF16),
                 pltpu.SemaphoreType.DMA((3,))],
    )
    return out


def solution(mesh):
    return jax.shard_map(
        on_device,
        mesh=mesh,
        in_specs=(
            P(None, None, "box", None, "face", None),
            P(None, None, "box", None),
            P(None, None, "box", None),
            P(),
            P(),
        ),
        out_specs=P(None, None, ("box", "face"), None),
        check_vma=False,
    )
```

time: 89.9 us -> 113 us (1.26)
  Pallas kernels: 27.4 us -> 54.1 us
  starting transfers between devices: 29.3 us -> 20.7 us
  local copies, waits for them, and re-layouts: 5.5 us -> 9.32 us
  other arithmetic: 1.05 us -> 3.14 us
    pallas_call x14 -> x13, Pallas kernels: 27.4 us -> 54.1 us  [call(): pl.pallas_call(kernel, in_specs=[pl.BlockSpec(memory_space=pltpu.SMEM)] +...]
    ppermute x7 -> x5, starting transfers between devices: 12.6 us -> 4.47 us  [face_permute(): return lax.ppermute(array, ('box', 'face'), pairs)]
    unnamed x20 -> x26, local copies, waits for them, and re-layouts: 4.76 us -> 8.58 us
    ppermute x7 -> x5, waiting for transfers between devices: 14.8 us -> 17 us  [face_permute(): return lax.ppermute(array, ('box', 'face'), pairs)]
    ppermute x16 -> x15, waiting for transfers between devices: 9.74 us -> 7.61 us  [box_permute(): return lax.ppermute(array, 'box', [(b, b ^ mask) for b in range(n_box)])]
    ppermute x16 -> x15, starting transfers between devices: 16.8 us -> 16.2 us  [box_permute(): return lax.ppermute(array, 'box', [(b, b ^ mask) for b in range(n_box)])]
  transfers between devices with their start and end apart: 23 -> 20, of which waited for: 9 -> 10; matrix products, arithmetic and copies ran while one was open for 1% -> 3% of each run, Pallas kernels for 18% -> 13%
where the time goes in v5:
time: 113 us; the launch traced here: 112 us
  Pallas kernels  54.1 us (48%)
  waiting for transfers between devices  24.6 us (22%)
  starting transfers between devices  20.7 us (18%)
  local copies, waits for them, and re-layouts  9.32 us (8%)
  other arithmetic  3.14 us (3%)
    pallas_call x13, Pallas kernels, call(): pl.pallas_call(kernel, in_specs=[pl.BlockSpec(memory_space=pltpu.SMEM)] +...  54.1 us
    ppermute x5, waiting for transfers between devices, face_permute(): return lax.ppermute(array, ('box', 'face'), pairs)  17 us
    ppermute x15, starting transfers between devices, box_permute(): return lax.ppermute(array, 'box', [(b, b ^ mask) for b in range(n_box)])  16.2 us
    unnamed x26, local copies, waits for them, and re-layouts  8.58 us
    ppermute x15, waiting for transfers between devices, box_permute(): return lax.ppermute(array, 'box', [(b, b ^ mask) for b in range(n_box)])  7.61 us
    ppermute x5, starting transfers between devices, face_permute(): return lax.ppermute(array, ('box', 'face'), pairs)  4.47 us
  transfers between devices with their start and end apart: 20, of which 10 were waited for; matrix products, arithmetic and copies ran while one was open for 3% of the time, Pallas kernels for 13%

profile of v5, /device:TPU:1, one launch (start us, length us, event | category | flops | bytes accessed | tf_op | source)
XLA Modules:
  0.0 112.0 jit_solution(17034279086823748504)
XLA Ops:
  0.0 0.7 pad_add_fusion.sc
  0.7 33.8 %shard_map.55 = (bf16[2,256,512]{2,1,0:T(8,128)(2,1)}, bf16[2,256,512]{2,1,0:T(8,128)(2,1)}) custom-call(s32[4]{0:T(128)} %pad_add_fusion.sc, bf16[2,3,256,1536]{3,2,1,0:T(8,128)(2,1)} %bitcast.14), custom_call_target="tpu_custom_call" | custom-call | tf_op jit(solution)/shard_map/pallas_call | solution.py:43
  34.6 0.5 collective-permute-start.1
  35.1 0.7 dynamic-slice_bitcast_fusion
  35.8 0.9 collective-permute-done.sib_ref.endsib_ref
  36.7 1.0 copy-done.1
  37.7 0.6 shard_map.56
  38.3 2.4 %collective-permute-start.2 = (bf16[2,128,512]{2,1,0:T(8,128)(2,1)S(1)}, bf16[2,128,512]{2,1,0:T(8,128)(2,1)S(1)}, u32[]{:S(2)}, u32[]{:S(2)}) collective-permute-start(bf16[2,128,512]{2,1,0:T(8,128)(2,1)S(1)} %get-tuple-element.34), channel_id=1, source_target_pairs={{0,1},{1,0},{2,3},{3,2},{4,5},{5,4},{6,7},{7,6},{8,9},{9,8},{10,11... | collective-permute-start | bytes 786440 | tf_op jit(solution)/shard_map/ppermute | solution.py:88
  40.7 0.8 copy-done.8
  41.5 2.3 %copy-done = bf16[2,1,1,3,256,1536]{5,4,3,2,1,0:T(8,128)(2,1)S(1)} copy-done((bf16[2,1,1,3,256,1536]{5,4,3,2,1,0:T(8,128)(2,1)S(1)}, bf16[2,1,1,3,256,1536]{5,4,3,2,1,0:T(8,128)(2,1)}, u32[]{:S(2)}) %copy-start) | copy-done | bytes 4718616
  43.9 1.0 copy-done.7
  44.9 1.0 copy-done.9
  46.0 3.0 %shard_map.57 = (s32[1,512]{1,0:T(1,128)S(1)}, s32[512,1]{1,0:T(8,128)S(1)}, bf16[2,256,512]{2,1,0:T(8,128)(2,1)S(1)}, bf16[2,128,512]{2,1,0:T(8,128)(2,1)S(1)},...) custom-call(s32[4]{0:T(128)S(1)} %copy-done.5, ...), custom_call_target="tpu_custom_call" | custom-call | flops 20000000000 | tf_op jit(solution)/shard_map/pallas_call | solution.py:43
  49.0 0.8 copy-done.3
  49.8 0.8 copy-done.6
  50.6 0.7 copy-done.10
  51.3 0.7 collective-permute-start.3
  52.0 1.3 %fusion.own_ref = bf16[2,256,512]{2,1,0:T(8,128)(2,1)S(1)} fusion(s32[]{:T(128)S(6)} %select_n.57, bf16[2,256,512]{2,1,0:T(8,128)(2,1)} %bitcast.18), kind=kLoop, calls=%fused_computation.2 | loop fusion | flops 1048576 | bytes 1048580 | tf_op jit(solution)/shard_map/jit(_roll_dynamic)/concatenate | solution.py:177
  53.3 0.5 collective-permute-start.4
  53.8 1.0 fusion.1
  54.9 1.3 %collective-permute-start.8 = (bf16[2,128,512]{2,1,0:T(8,128)(2,1)S(1)}, bf16[2,128,512]{2,1,0:T(8,128)(2,1)S(1)}, u32[]{:S(2)}, u32[]{:S(2)}) collective-permute-start(bf16[2,128,512]{2,1,0:T(8,128)(2,1)S(1)} %fusion.1), channel_id=1, source_target_pairs={{0,4},{2,6},{4,0},{6,2},{8,12},{10,14},{12,8},{14,10},{16,20},{18,... | collective-permute-start | bytes 786440 | tf_op jit(solution)/shard_map/ppermute | solution.py:74
  56.5 0.6 shard_map.59.w_ref.refs_5_
  57.1 0.6 collective-permute-start.6
  57.7 1.4 %shard_map.60 = (f32[2,128,1024]{2,1,0:T(8,128)S(1)}, bf16[2,128,512]{2,1,0:T(8,128)(2,1)S(1)}) custom-call(s32[4]{0:T(128)S(1)} %copy-done.5, bf16[2,128,1024]{2,1,0:T(8,128)(2,1)S(1)} %copy-done.4, bf16[2,128,1024]{2,1,0:T(8,128)(2,1)S(1)} %collective-permute-done.4.recv_ref, bf16[2,512,512]{2,1,0:T(8,128)(2,1)S(1)} %shard_map.59.w_ref.refs_5_, ...), custom_call_target="tpu_custom_call" | custom-call | tf_op jit(solution)/shard_map/pallas_call | solution.py:43
  59.1 4.2 %shard_map.58 = (bf16[2,256,1536]{2,1,0:T(8,128)(2,1)S(1)}, bf16[2,128,1536]{2,1,0:T(8,128)(2,1)S(1)}) custom-call(s32[4]{0:T(128)S(1)} %copy-done.5, bf16[2,256,1536]{2,1,0:T(8,128)(2,1)} %get-tuple-element.39.own_ref, bf16[2,256,1536]{2,1,0:T(8,128)(2,1)} %collective-permute-done.3.sib_ref, s32[1,512]{1,0:T(1,128)S(1)} %get-tuple-element.40.comp_ref, ...), custom_call_target="tpu_custom_call" | custom-call | tf_op jit(solution)/shard_map/pallas_call | solution.py:43
  63.3 0.4 collective-permute-done.7.rest_2_.rest_4_
  63.7 1.2 %collective-permute-start.9 = (bf16[2,128,512]{2,1,0:T(8,128)(2,1)S(1)}, bf16[2,128,512]{2,1,0:T(8,128)(2,1)S(1)}, u32[]{:S(2)}, u32[]{:S(2)}) collective-permute-start(bf16[2,128,512]{2,1,0:T(8,128)(2,1)S(1)} %collective-permute-done.7.rest_2_.rest_4_), channel_id=1, source_target_pairs={{0,2},{2,0},{4,6},{6,4},{8,10},{10,8},{12,14},{14,12},{16,18},{18,... | collective-permute-start | bytes 786440 | tf_op jit(solution)/shard_map/ppermute | solution.py:74
  65.1 0.9 collective-permute-done.9.rest_3_.rest_5_
  66.1 1.1 shard_map.61.own_ref
  67.1 5.7 %collective-permute-done.13.rest_2_ = bf16[2,128,512]{2,1,0:T(8,128)(2,1)S(1)} collective-permute-done((bf16[2,128,512]{2,1,0:T(8,128)(2,1)S(1)}, bf16[2,128,512]{2,1,0:T(8,128)(2,1)S(1)}, u32[]{:S(2)}, u32[]{:S(2)}) %collective-permute-start.13) | collective-permute-done | bytes 262176 | tf_op jit(solution)/shard_map/ppermute | solution.py:88
  73.2 1.4 %collective-permute-start.10 = (bf16[2,128,1536]{2,1,0:T(8,128)(2,1)S(1)}, bf16[2,128,1536]{2,1,0:T(8,128)(2,1)S(1)}, u32[]{:S(2)}, u32[]{:S(2)}) collective-permute-start(bf16[2,128,1536]{2,1,0:T(8,128)(2,1)S(1)} %get-tuple-element.54), channel_id=1, source_target_pairs={{0,1},{1,0},{2,3},{3,2},{4,5},{5,4},{6,7},{7,6},{8,9},{9,8},{10,11... | collective-permute-start | bytes 2359304 | tf_op jit(solution)/shard_map/ppermute | solution.py:88
  74.7 1.7 %collective-permute-start.12 = (bf16[2,2,128,512]{3,2,1,0:T(8,128)(2,1)S(1)}, bf16[2,2,128,512]{3,2,1,0:T(8,128)(2,1)S(1)}, u32[]{:S(2)}, u32[]{:S(2)}) collective-permute-start(bf16[2,2,128,512]{3,2,1,0:T(8,128)(2,1)S(1)} %pad_maximum_fusion.own_ref), channel_id=1, source_target_pairs={{0,2},{2,0},{4,6},{6,4},{8,10},{10,8},{12,14},{14,12},{16,18},{18,... | collective-permute-start | bytes 1572872 | tf_op jit(solution)/shard_map/ppermute | solution.py:74
  76.4 9.1 %collective-permute-done.16.own_ref = bf16[2,128,1024]{2,1,0:T(8,128)(2,1)S(1)} collective-permute-done((bf16[2,128,1024]{2,1,0:T(8,128)(2,1)S(1)}, bf16[2,128,1024]{2,1,0:T(8,128)(2,1)S(1)}, u32[]{:S(2)}, u32[]{:S(2)}) %collective-permute-start.16) | collective-permute-done | bytes 524320 | tf_op jit(solution)/shard_map/ppermute | solution.py:88
  85.5 0.3 collective-permute-start.17
  85.8 3.2 %collective-permute-start.14 = (bf16[2,128,512]{2,1,0:T(8,128)(2,1)S(1)}, bf16[2,128,512]{2,1,0:T(8,128)(2,1)S(1)}, u32[]{:S(2)}, u32[]{:S(2)}) collective-permute-start(bf16[2,128,512]{2,1,0:T(8,128)(2,1)S(1)} %collective-permute-done.13.rest_2_), channel_id=1, source_target_pairs={{0,2},{2,0},{4,6},{6,4},{8,10},{10,8},{12,14},{14,12},{16,18},{18,... | collective-permute-start | bytes 786440 | tf_op jit(solution)/shard_map/ppermute | solution.py:74
  89.0 0.6 shard_map.62.refs_6_
  89.6 0.5 collective-permute-done.14.rest_3_
  90.1 0.7 shard_map.63.refs_7_
  90.9 0.6 shard_map.64.refs_0_
  91.5 0.4 collective-permute-start.18
  92.0 4.0 %collective-permute-done.17.x_ref = bf16[2,128,1024]{2,1,0:T(8,128)(2,1)S(1)} collective-permute-done((bf16[2,128,1024]{2,1,0:T(8,128)(2,1)S(1)}, bf16[2,128,1024]{2,1,0:T(8,128)(2,1)S(1)}, u32[]{:S(2)}, u32[]{:S(2)}) %collective-permute-start.17) | collective-permute-done | bytes 524320 | tf_op jit(solution)/shard_map/ppermute | solution.py:74
  96.0 0.6 shard_map.65.refs_1_
  96.6 3.9 %collective-permute-start.19 = (bf16[2,128,1536]{2,1,0:T(8,128)(2,1)S(1)}, bf16[2,128,1536]{2,1,0:T(8,128)(2,1)S(1)}, u32[]{:S(2)}, u32[]{:S(2)}) collective-permute-start(bf16[2,128,1536]{2,1,0:T(8,128)(2,1)S(1)} %shard_map.65.refs_1_), channel_id=1, source_target_pairs={{0,2},{2,0},{4,6},{6,4},{8,10},{10,8},{12,14},{14,12},{16,18},{18,... | collective-permute-start | bytes 2359304 | tf_op jit(solution)/shard_map/ppermute | solution.py:74
  100.5 1.8 %collective-permute-done.10.refs_2_ = bf16[2,128,1536]{2,1,0:T(8,128)(2,1)S(1)} collective-permute-done((bf16[2,128,1536]{2,1,0:T(8,128)(2,1)S(1)}, bf16[2,128,1536]{2,1,0:T(8,128)(2,1)S(1)}, u32[]{:S(2)}, u32[]{:S(2)}) %collective-permute-start.10) | collective-permute-done | bytes 786464 | tf_op jit(solution)/shard_map/ppermute | solution.py:88
  102.4 1.7 %collective-permute-start.11 = (bf16[2,128,1536]{2,1,0:T(8,128)(2,1)S(1)}, bf16[2,128,1536]{2,1,0:T(8,128)(2,1)S(1)}, u32[]{:S(2)}, u32[]{:S(2)}) collective-permute-start(bf16[2,128,1536]{2,1,0:T(8,128)(2,1)S(1)} %collective-permute-done.10.refs_2_), channel_id=1, source_target_pairs={{0,2},{2,0},{4,6},{6,4},{8,10},{10,8},{12,14},{14,12},{16,18},{18,... | collective-permute-start | bytes 2359304 | tf_op jit(solution)/shard_map/ppermute | solution.py:74
  104.0 0.7 shard_map.66.refs_8_
  104.8 1.1 %collective-permute-done.11.refs_3_ = bf16[2,128,1536]{2,1,0:T(8,128)(2,1)S(1)} collective-permute-done((bf16[2,128,1536]{2,1,0:T(8,128)(2,1)S(1)}, bf16[2,128,1536]{2,1,0:T(8,128)(2,1)S(1)}, u32[]{:S(2)}, u32[]{:S(2)}) %collective-permute-start.11) | collective-permute-done | bytes 786464 | tf_op jit(solution)/shard_map/ppermute | solution.py:74
  105.9 6.1 %shard_map.67 = bf16[2,1,256,1536]{3,2,1,0:T(8,128)(2,1)} custom-call(s32[4]{0:T(128)S(1)} %copy-done.5, bf16[2,256,1536]{2,1,0:T(8,128)(2,1)S(1)} %get-tuple-element.37.refs_0_, bf16[2,256,1536]{2,1,0:T(8,128)(2,1)S(1)} %get-tuple-element.42.refs_1_, bf16[2,128,1536]{2,1,0:T(8,128)(2,1)S(1)} %collective-permute-done.10.refs_2_, ...), custom_call_target="tpu_custom_call" | custom-call | tf_op jit(solution)/shard_map/pallas_call | solution.py:43
  (37 shorter events, 1.3 us)
Async XLA Ops:
  0.7 36.0 %copy-start.5 = (s32[4]{0:T(128)S(1)}, s32[4]{0:T(128)}, u32[]{:S(2)}) copy-start(s32[4]{0:T(128)} %pad_add_fusion.sc) | copy-start | bytes 52
  34.5 2.2 %collective-permute-start = (bf16[2,256,512]{2,1,0:T(8,128)(2,1)}, bf16[2,256,512]{2,1,0:T(8,128)(2,1)S(1)}, u32[]{:S(2)}, u32[]{:S(2)}) collective-permute-start(bf16[2,256,512]{2,1,0:T(8,128)(2,1)} %get-tuple-element.33.own_ref.end_ref), channel_id=1, source_target_pairs={{0,2},{2,0},{4,6},{6,4},{8,10},{10,8},{12,14},{14,12},{16,18},{18,... | collective-permute-start | bytes 1572872 | tf_op jit(solution)/shard_map/ppermute | solution.py:74
  34.6 6.1 %collective-permute-start.1 = (bf16[2,256,512]{2,1,0:T(8,128)(2,1)}, bf16[2,256,512]{2,1,0:T(8,128)(2,1)S(1)}, u32[]{:S(2)}, u32[]{:S(2)}) collective-permute-start(bf16[2,256,512]{2,1,0:T(8,128)(2,1)} %get-tuple-element.36.own_ref), channel_id=1, source_target_pairs={{0,2},{2,0},{4,6},{6,4},{8,10},{10,8},{12,14},{14,12},{16,18},{18,... | collective-permute-start | bytes 1572872 | tf_op jit(solution)/shard_map/ppermute | solution.py:74
  36.7 1.0 copy-start.1
  38.3 13.0 %collective-permute-start.2 = (bf16[2,128,512]{2,1,0:T(8,128)(2,1)S(1)}, bf16[2,128,512]{2,1,0:T(8,128)(2,1)S(1)}, u32[]{:S(2)}, u32[]{:S(2)}) collective-permute-start(bf16[2,128,512]{2,1,0:T(8,128)(2,1)S(1)} %get-tuple-element.34), channel_id=1, source_target_pairs={{0,1},{1,0},{2,3},{3,2},{4,5},{5,4},{6,7},{7,6},{8,9},{9,8},{10,11... | collective-permute-start | bytes 786440 | tf_op jit(solution)/shard_map/ppermute | solution.py:88
  40.7 0.8 copy-start.8
  41.5 2.3 %copy-start = (bf16[2,1,1,3,256,1536]{5,4,3,2,1,0:T(8,128)(2,1)S(1)}, bf16[2,1,1,3,256,1536]{5,4,3,2,1,0:T(8,128)(2,1)}, u32[]{:S(2)}) copy-start(bf16[2,1,1,3,256,1536]{5,4,3,2,1,0:T(8,128)(2,1)} %param.5) | copy-start | bytes 14155780
  43.9 1.0 copy-start.7
  44.9 1.0 copy-start.9
  49.0 0.8 copy-start.3
  49.8 0.8 copy-start.6
  50.6 0.7 copy-start.10
  51.3 7.8 %collective-permute-start.3 = (bf16[2,256,1536]{2,1,0:T(8,128)(2,1)}, bf16[2,256,1536]{2,1,0:T(8,128)(2,1)}, u32[]{:S(2)}, u32[]{:S(2)}) collective-permute-start(bf16[2,256,1536]{2,1,0:T(8,128)(2,1)} %get-tuple-element.39.own_ref), channel_id=1, source_target_pairs={{0,2},{2,0},{4,6},{6,4},{8,10},{10,8},{12,14},{14,12},{16,18},{18,... | collective-permute-start | bytes 4718600 | tf_op jit(solution)/shard_map/ppermute | solution.py:74
  52.0 4.2 %copy-start.11 = (bf16[2,128,512]{2,1,0:T(8,128)(2,1)S(1)}, bf16[2,128,512]{2,1,0:T(8,128)(2,1)}, u32[]{:S(2)}) copy-start(bf16[2,128,512]{2,1,0:T(8,128)(2,1)} %copy-done.10) | copy-start | bytes 786436
  53.2 4.5 %copy-start.2 = (bf16[2,256,512]{2,1,0:T(8,128)(2,1)S(1)}, bf16[2,256,512]{2,1,0:T(8,128)(2,1)}, u32[]{:S(2)}) copy-start(bf16[2,256,512]{2,1,0:T(8,128)(2,1)} %get-tuple-element.33.own_ref.end_ref) | copy-start | bytes 1572868
  53.2 4.5 %copy-start.4 = (bf16[2,128,1024]{2,1,0:T(8,128)(2,1)S(1)}, bf16[2,128,1024]{2,1,0:T(8,128)(2,1)}, u32[]{:S(2)}) copy-start(bf16[2,128,1024]{2,1,0:T(8,128)(2,1)} %copy-done.3) | copy-start | bytes 1572868
  53.3 3.2 %collective-permute-start.5 = (bf16[2,256,512]{2,1,0:T(8,128)(2,1)S(1)}, bf16[2,256,512]{2,1,0:T(8,128)(2,1)S(1)}, u32[]{:S(2)}, u32[]{:S(2)}) collective-permute-start(bf16[2,256,512]{2,1,0:T(8,128)(2,1)S(1)} %fusion.own_ref), channel_id=1, source_target_pairs={{0,2},{2,0},{4,6},{6,4},{8,10},{10,8},{12,14},{14,12},{16,18},{18,... | collective-permute-start | bytes 1572872 | tf_op jit(solution)/shard_map/ppermute | solution.py:74
  53.3 4.4 %collective-permute-start.4 = (bf16[2,128,1024]{2,1,0:T(8,128)(2,1)}, bf16[2,128,1024]{2,1,0:T(8,128)(2,1)S(1)}, u32[]{:S(2)}, u32[]{:S(2)}) collective-permute-start(bf16[2,128,1024]{2,1,0:T(8,128)(2,1)} %copy-done.6), channel_id=1, source_target_pairs={{0,2},{2,0},{4,6},{6,4},{8,10},{10,8},{12,14},{14,12},{16,18},{18,... | collective-permute-start | bytes 1572872 | tf_op jit(solution)/shard_map/ppermute | solution.py:74
  54.9 8.4 %collective-permute-start.8 = (bf16[2,128,512]{2,1,0:T(8,128)(2,1)S(1)}, bf16[2,128,512]{2,1,0:T(8,128)(2,1)S(1)}, u32[]{:S(2)}, u32[]{:S(2)}) collective-permute-start(bf16[2,128,512]{2,1,0:T(8,128)(2,1)S(1)} %fusion.1), channel_id=1, source_target_pairs={{0,4},{2,6},{4,0},{6,2},{8,12},{10,14},{12,8},{14,10},{16,20},{18,... | collective-permute-start | bytes 786440 | tf_op jit(solution)/shard_map/ppermute | solution.py:74
  56.2 7.5 %collective-permute-start.7 = (bf16[2,128,512]{2,1,0:T(8,128)(2,1)S(1)}, bf16[2,128,512]{2,1,0:T(8,128)(2,1)S(1)}, u32[]{:S(2)}, u32[]{:S(2)}) collective-permute-start(bf16[2,128,512]{2,1,0:T(8,128)(2,1)S(1)} %copy-done.11), channel_id=1, source_target_pairs={{0,1},{1,0},{2,3},{3,2},{4,5},{5,4},{6,7},{7,6},{8,9},{9,8},{10,11... | collective-permute-start | bytes 786440 | tf_op jit(solution)/shard_map/ppermute | solution.py:88
  57.1 8.0 %collective-permute-start.6 = (bf16[2,128,512]{2,1,0:T(8,128)(2,1)S(1)}, bf16[2,128,512]{2,1,0:T(8,128)(2,1)S(1)}, u32[]{:S(2)}, u32[]{:S(2)}) collective-permute-start(bf16[2,128,512]{2,1,0:T(8,128)(2,1)S(1)} %collective-permute-done.2.rest_0_), channel_id=1, source_target_pairs={{0,2},{2,0},{4,6},{6,4},{8,10},{10,8},{12,14},{14,12},{16,18},{18,... | collective-permute-start | bytes 786440 | tf_op jit(solution)/shard_map/ppermute | solution.py:74
  63.3 11.2 %copy-start.12 = (bf16[2,1,128,512]{3,2,1,0:T(8,128)(2,1)S(1)}, bf16[2,1,128,512]{3,2,1,0:T(8,128)(2,1)}, u32[]{:S(2)}) copy-start(bf16[2,1,128,512]{3,2,1,0:T(8,128)(2,1)} %param.7) | copy-start | bytes 786436
  63.7 2.3 %collective-permute-start.9 = (bf16[2,128,512]{2,1,0:T(8,128)(2,1)S(1)}, bf16[2,128,512]{2,1,0:T(8,128)(2,1)S(1)}, u32[]{:S(2)}, u32[]{:S(2)}) collective-permute-start(bf16[2,128,512]{2,1,0:T(8,128)(2,1)S(1)} %collective-permute-done.7.rest_2_.rest_4_), channel_id=1, source_target_pairs={{0,2},{2,0},{4,6},{6,4},{8,10},{10,8},{12,14},{14,12},{16,18},{18,... | collective-permute-start | bytes 786440 | tf_op jit(solution)/shard_map/ppermute | solution.py:74
  64.9 7.9 %collective-permute-start.13 = (bf16[2,128,512]{2,1,0:T(8,128)(2,1)S(1)}, bf16[2,128,512]{2,1,0:T(8,128)(2,1)S(1)}, u32[]{:S(2)}, u32[]{:S(2)}) collective-permute-start(bf16[2,128,512]{2,1,0:T(8,128)(2,1)S(1)} %get-tuple-element.56), channel_id=1, source_target_pairs={{0,1},{1,0},{2,3},{3,2},{4,5},{5,4},{6,7},{7,6},{8,9},{9,8},{10,11... | collective-permute-start | bytes 786440 | tf_op jit(solution)/shard_map/ppermute | solution.py:88
  72.8 12.7 %collective-permute-start.16 = (bf16[2,128,1024]{2,1,0:T(8,128)(2,1)S(1)}, bf16[2,128,1024]{2,1,0:T(8,128)(2,1)S(1)}, u32[]{:S(2)}, u32[]{:S(2)}) collective-permute-start(bf16[2,128,1024]{2,1,0:T(8,128)(2,1)S(1)} %shard_map.61.own_ref), channel_id=1, source_target_pairs={{0,1},{1,0},{2,3},{3,2},{4,5},{5,4},{6,7},{7,6},{8,9},{9,8},{10,11... | collective-permute-start | bytes 1572872 | tf_op jit(solution)/shard_map/ppermute | solution.py:88
  73.0 12.5 %collective-permute-start.15 = (bf16[2,128,1024]{2,1,0:T(8,128)(2,1)S(1)}, bf16[2,128,1024]{2,1,0:T(8,128)(2,1)S(1)}, u32[]{:S(2)}, u32[]{:S(2)}) collective-permute-start(bf16[2,128,1024]{2,1,0:T(8,128)(2,1)S(1)} %shard_map.61.own_ref), channel_id=1, source_target_pairs={{0,4},{2,6},{4,0},{6,2},{8,12},{10,14},{12,8},{14,10},{16,20},{18,... | collective-permute-start | bytes 1572872 | tf_op jit(solution)/shard_map/ppermute | solution.py:74
  73.2 29.2 %collective-permute-start.10 = (bf16[2,128,1536]{2,1,0:T(8,128)(2,1)S(1)}, bf16[2,128,1536]{2,1,0:T(8,128)(2,1)S(1)}, u32[]{:S(2)}, u32[]{:S(2)}) collective-permute-start(bf16[2,128,1536]{2,1,0:T(8,128)(2,1)S(1)} %get-tuple-element.54), channel_id=1, source_target_pairs={{0,1},{1,0},{2,3},{3,2},{4,5},{5,4},{6,7},{7,6},{8,9},{9,8},{10,11... | collective-permute-start | bytes 2359304 | tf_op jit(solution)/shard_map/ppermute | solution.py:88
  74.7 14.3 %collective-permute-start.12 = (bf16[2,2,128,512]{3,2,1,0:T(8,128)(2,1)S(1)}, bf16[2,2,128,512]{3,2,1,0:T(8,128)(2,1)S(1)}, u32[]{:S(2)}, u32[]{:S(2)}) collective-permute-start(bf16[2,2,128,512]{3,2,1,0:T(8,128)(2,1)S(1)} %pad_maximum_fusion.own_ref), channel_id=1, source_target_pairs={{0,2},{2,0},{4,6},{6,4},{8,10},{10,8},{12,14},{14,12},{16,18},{18,... | collective-permute-start | bytes 1572872 | tf_op jit(solution)/shard_map/ppermute | solution.py:74
  85.5 10.5 %collective-permute-start.17 = (bf16[2,128,1024]{2,1,0:T(8,128)(2,1)S(1)}, bf16[2,128,1024]{2,1,0:T(8,128)(2,1)S(1)}, u32[]{:S(2)}, u32[]{:S(2)}) collective-permute-start(bf16[2,128,1024]{2,1,0:T(8,128)(2,1)S(1)} %collective-permute-done.16.own_ref), channel_id=1, source_target_pairs={{0,4},{2,6},{4,0},{6,2},{8,12},{10,14},{12,8},{14,10},{16,20},{18,... | collective-permute-start | bytes 1572872 | tf_op jit(solution)/shard_map/ppermute | solution.py:74
  85.8 4.4 %collective-permute-start.14 = (bf16[2,128,512]{2,1,0:T(8,128)(2,1)S(1)}, bf16[2,128,512]{2,1,0:T(8,128)(2,1)S(1)}, u32[]{:S(2)}, u32[]{:S(2)}) collective-permute-start(bf16[2,128,512]{2,1,0:T(8,128)(2,1)S(1)} %collective-permute-done.13.rest_2_), channel_id=1, source_target_pairs={{0,2},{2,0},{4,6},{6,4},{8,10},{10,8},{12,14},{14,12},{16,18},{18,... | collective-permute-start | bytes 786440 | tf_op jit(solution)/shard_map/ppermute | solution.py:74
  91.5 12.5 %collective-permute-start.18 = (bf16[2,128,1536]{2,1,0:T(8,128)(2,1)S(1)}, bf16[2,128,1536]{2,1,0:T(8,128)(2,1)S(1)}, u32[]{:S(2)}, u32[]{:S(2)}) collective-permute-start(bf16[2,128,1536]{2,1,0:T(8,128)(2,1)S(1)} %shard_map.64.refs_0_), channel_id=1, source_target_pairs={{0,2},{2,0},{4,6},{6,4},{8,10},{10,8},{12,14},{14,12},{16,18},{18,... | collective-permute-start | bytes 2359304 | tf_op jit(solution)/shard_map/ppermute | solution.py:74
  96.6 7.4 %collective-permute-start.19 = (bf16[2,128,1536]{2,1,0:T(8,128)(2,1)S(1)}, bf16[2,128,1536]{2,1,0:T(8,128)(2,1)S(1)}, u32[]{:S(2)}, u32[]{:S(2)}) collective-permute-start(bf16[2,128,1536]{2,1,0:T(8,128)(2,1)S(1)} %shard_map.65.refs_1_), channel_id=1, source_target_pairs={{0,2},{2,0},{4,6},{6,4},{8,10},{10,8},{12,14},{14,12},{16,18},{18,... | collective-permute-start | bytes 2359304 | tf_op jit(solution)/shard_map/ppermute | solution.py:74
  102.4 3.6 %collective-permute-start.11 = (bf16[2,128,1536]{2,1,0:T(8,128)(2,1)S(1)}, bf16[2,128,1536]{2,1,0:T(8,128)(2,1)S(1)}, u32[]{:S(2)}, u32[]{:S(2)}) collective-permute-start(bf16[2,128,1536]{2,1,0:T(8,128)(2,1)S(1)} %collective-permute-done.10.refs_2_), channel_id=1, source_target_pairs={{0,2},{2,0},{4,6},{6,4},{8,10},{10,8},{12,14},{14,12},{16,18},{18,... | collective-permute-start | bytes 2359304 | tf_op jit(solution)/shard_map/ppermute | solution.py:74

commit v6 on v5

--- a/solution.py
+++ b/solution.py
@@ -9,7 +9,6 @@
 F32 = jnp.float32
 VMEM_BYTES = 28 * 1024 * 1024
 SLOTS_COST = 20_000_000_000
-LEAF_VMEM_BYTES = 60 * 1024 * 1024
 
 
 def dot(first, second):
@@ -94,48 +93,23 @@
     skel_two = lax.dynamic_index_in_dim(skel_second[0], box // 4, 0, keepdims=True)
 
     in_hbm = pl.BlockSpec(memory_space=pltpu.HBM)
-    in_vmem = pl.BlockSpec(memory_space=pltpu.VMEM)
-    splits = 4
-    qr = fr // splits
-
-    def copy_kernel(sc, leaf_ref, end_out, side_out, sems):
+
+    def parts_kernel(sc, leaf_ref, end_out, side_out, rows_out):
         p = sc[0]
-        copies = []
-        for t in range(2):
-            for i in range(splits):
-                rows = pl.ds(i * qr, qr)
-                for j, (out, start) in enumerate(((end_out, p * k), (side_out, 2 * k))):
-                    copies.append(pltpu.make_async_copy(
-                        leaf_ref.at[t, 1 - p, rows, pl.ds(pl.multiple_of(start, k), k)],
-                        out.at[t, rows], sems.at[t, i, j],
-                    ))
-        for copy in copies:
-            copy.start()
-        for copy in copies:
-            copy.wait()
-
-    end_own, sides_raw = call(
-        copy_kernel, scalars, [leaf], [sds((2, fr, k), BF16)] * 2, specs=[in_hbm], out_specs=[in_hbm] * 2,
-        scratch=[pltpu.SemaphoreType.DMA((2, splits, 2))], vmem=LEAF_VMEM_BYTES,
-    )
+        end_out[...] = leaf_ref[:, 1 - p, :, pl.ds(pl.multiple_of(p * k, k), k)]
+        side_out[...] = leaf_ref[:, 1 - p, :, 2 * k :]
+        rows_out[...] = leaf_ref[:, 2]
+
+    end_own, sides_raw, s_rows = call(
+        parts_kernel, scalars, [leaf], [sds((2, fr, k), BF16)] * 2 + [sds((2, fr, 3 * k), BF16)]
+    )
+    end_far = over_face(end_own)
+    sides_sib = box_permute(sides_raw, 1)
     end_sib = box_permute(end_own, 1)
-    sides_sib = box_permute(sides_raw, 1)
-
-    def split_kernel(sc, own_ref, sib_ref, first_out, rest_out):
-        p, q = sc[0], sc[1]
-        rows = pl.ds(pl.multiple_of(p * hr, hr), hr)
-        own, sib = own_ref[:, rows, :], sib_ref[:, rows, :]
-        first_out[...] = jnp.where(p == q, own, sib)
-        rest_out[...] = jnp.where(p == q, sib, own)
-
-    first_send, rest_send = call(
-        split_kernel, scalars, [end_own, end_sib], [sds((2, hr, k), BF16)] * 2,
-    )
-    first_far = over_face(first_send)
-    first_fwd = [box_permute(a, 1) for a in first_far]
+    s_sib = box_permute(s_rows, 1)
 
     def slots_kernel(sc, leaf_ref, own_ref, sib_ref, skel_ref, skel2_ref,
-                     comp_out, col_out, side_out, half_out, keep_out, send_out, rows_out, end_out):
+                     comp_out, col_out, side_out, half_out, keep_out, send_out, end_out):
         p, q = sc[0], sc[1]
         rows = lax.broadcasted_iota(jnp.int32, (k, k), 0)
         cols = lax.broadcasted_iota(jnp.int32, (k, k), 1)
@@ -153,7 +127,6 @@
         side = dot(flat(own_ref[...]), pick_own) + dot(flat(sib_ref[...]), pick_sib)
         side_out[...] = side.astype(BF16).reshape(2, fr, k)
         half_out[...] = side_out[:, pl.ds(pl.multiple_of(p * hr, hr), hr), :]
-        rows_out[...] = leaf_ref[:, 2]
         for t in range(2):
             end_out[t, :, : 2 * k] = leaf_ref[t, p, :, : 2 * k]
             end_out[t, :, 2 * k :] = dot(leaf_ref[t, p, :, 2 * k :], pick_own).astype(BF16)
@@ -164,20 +137,19 @@
                 ref[t, :, :k] = leaf_ref[t, p, take, couple]
                 ref[t, :, k:] = end_out[t, take, 2 * k :]
 
-    comp, skel_col, side, side_half, v_keep, v_send, s_rows, end_kept = call(
-        slots_kernel, after(scalars, first_send), [leaf, sides_raw, sides_sib, skel_one, skel_two],
+    comp, skel_col, side, side_half, v_keep, v_send, end_kept = call(
+        slots_kernel, scalars, [leaf, sides_raw, sides_sib, skel_one, skel_two],
         [sds((1, k), jnp.int32), sds((k, 1), jnp.int32), sds((2, fr, k), BF16),
          sds((2, hr, k), BF16), sds((2, hr, 2 * k), BF16), sds((2, hr, 2 * k), BF16),
-         sds((2, fr, 3 * k), BF16), sds((2, fr, 3 * k), BF16)], cost=SLOTS_COST,
-    )
-    s_sib = box_permute(after(s_rows, *first_far), 1)
-    side_far = over_face(after(side_half, *first_far))
-    v_recv = box_permute(after(v_send, *first_far), 1)
+         sds((2, fr, 3 * k), BF16)], cost=SLOTS_COST,
+    )
+    side_far = over_face(side_half)
+    v_recv = box_permute(v_send, 1)
 
     w_one = jnp.roll(w_first[:, 0], -face * fr, axis=2)
     w_one_sib = box_permute(w_one, 1)
     w_two = jnp.roll(w_second[:, 0], -face * fr, axis=2)
-    w_two_x = box_permute(after(w_two, first_send), 2)
+    w_two_x = box_permute(after(w_two, side_half), 2)
 
     def weight_one_kernel(sc, own_ref, sib_ref, out_ref):
         p = sc[0]
@@ -230,7 +202,7 @@
             pick(slots, write)
 
     kept, *kept_out = call(
-        rows_kernel, scalars, [s_rows, s_sib, comp, skel_col],
+        rows_kernel, after(scalars, *end_far), [s_rows, s_sib, comp, skel_col],
         [sds((2, fr, 3 * k), BF16)] + [sds((2, hr, 3 * k), BF16)] * nf,
     )
 
@@ -260,7 +232,7 @@
         acc_out[:, :, k:] = rows[:, :, k:].astype(F32) - dot(left, flat(side_ref[...])).reshape(2, hr, k)
 
     v_acc, v_hid = call(
-        iface_kernel, scalars, [v_keep, v_recv, weight_one, end_own, end_sib, side],
+        iface_kernel, after(scalars, *end_far), [v_keep, v_recv, weight_one, end_own, end_sib, side],
         [sds((2, hr, 2 * k), F32), sds((2, hr, k), BF16)],
         scratch=[pltpu.VMEM((2, hr, 2 * k), BF16)],
     )
@@ -277,19 +249,18 @@
     (weight_two,) = call(weight_two_kernel, scalars, [w_two_pair, w_two_sib], [sds((2, k, k), BF16)])
 
     side_fwd = [box_permute(after(a, kept, v_acc, w_two_x), 1) for a in side_far]
-    rest_far = over_face(after(rest_send, kept, v_acc))
+    end_fwd = [box_permute(a, 1) for a in end_far]
 
     def iface_far_kernel(sc, acc_ref, hid_ref, *rest):
         refs = [rest[i * nf : (i + 1) * nf] for i in range(4)]
         out_ref, rows = rest[4 * nf :]
-        p = sc[0]
+        p, q = sc[0], sc[1]
         mine = pl.ds(pl.multiple_of(p * hr, hr), hr)
         other = pl.ds(pl.multiple_of((1 - p) * hr, hr), hr)
         hidden = [hid_ref[0], hid_ref[1]]
         total = acc_ref[...]
         for s in range(nf):
-            rows[:, mine, :k] = refs[0][s][...]
-            rows[:, other, :k] = refs[1][s][...]
+            rows[:, :, :k] = jnp.where(p == q, refs[0][s][...], refs[1][s][...])
             rows[:, mine, k:] = refs[2][s][...]
             rows[:, other, k:] = refs[3][s][...]
             left = piece(hidden, (s + 1) * fr, fr)
@@ -297,36 +268,42 @@
         out_ref[...] = total.astype(BF16)
 
     (two_own,) = call(
-        iface_far_kernel, scalars, [v_acc, v_hid, *first_far, *first_fwd, *side_far, *side_fwd],
+        iface_far_kernel, scalars, [v_acc, v_hid, *end_far, *end_fwd, *side_far, *side_fwd],
         [sds((2, hr, 2 * k), BF16)], scratch=[pltpu.VMEM((2, fr, 2 * k), BF16)],
     )
-    rest_fwd = [box_permute(after(a, two_own), 1) for a in rest_far]
-
-    def gather_kernel(sc, own_ref, sib_ref, side_ref, *rest):
-        refs = [rest[i * nf : (i + 1) * nf] for i in range(6)]
-        out_ref = rest[6 * nf]
-        p, q = sc[0], sc[1]
-
-        def block(which):
-            return pl.ds(pl.multiple_of(which * k, k), k)
-
-        out_ref[0, :, :, block(p)] = own_ref[...]
-        out_ref[0, :, :, block(1 - p)] = sib_ref[...]
-        out_ref[0, :, :, 2 * k :] = side_ref[...]
-        for i, which in enumerate((q, 1 - q, 2)):
-            for h in range(2):
-                rows = pl.ds(pl.multiple_of((p ^ h) * hr, hr), hr)
-                for s in range(nf):
-                    out_ref[s + 1, :, rows, block(which)] = refs[2 * i + h][s][...]
-
-    (iface,) = call(
-        gather_kernel, scalars,
-        [end_own, end_sib, side, *first_far, *first_fwd, *rest_far, *rest_fwd, *side_far, *side_fwd],
-        [sds((n_face, 2, fr, 3 * k), BF16)],
+    def weighted(w_ref, rows, out_ref):
+        left = jnp.concatenate([piece((w_ref[0], w_ref[1]), s * fr, fr) for s in range(n_face)], axis=1)
+        for c in range(3):
+            cols = slice(c * k, (c + 1) * k)
+            right = rows[:, :, :, cols].reshape(n_face * 2 * fr, k)
+            out_ref[:, :, cols] = dot(left, right).astype(BF16).reshape(2, k, k)
+
+    def weighted_one_kernel(sc, w_ref, own_ref, sib_ref, side_ref, *rest):
+        far, fwd, sfar, sfwd = (rest[i * nf : (i + 1) * nf] for i in range(4))
+        out_ref, rows = rest[4 * nf :]
+        p = sc[0]
+        own_cols = pl.ds(pl.multiple_of(p * k, k), k)
+        sib_cols = pl.ds(pl.multiple_of((1 - p) * k, k), k)
+        mine = pl.ds(pl.multiple_of(p * hr, hr), hr)
+        other = pl.ds(pl.multiple_of((1 - p) * hr, hr), hr)
+        rows[0, :, :, own_cols] = own_ref[...]
+        rows[0, :, :, sib_cols] = sib_ref[...]
+        rows[0, :, :, 2 * k :] = side_ref[...]
+        for s in range(nf):
+            rows[s + 1, :, :, own_cols] = far[s][...]
+            rows[s + 1, :, :, sib_cols] = fwd[s][...]
+            rows[s + 1, :, mine, 2 * k :] = sfar[s][...]
+            rows[s + 1, :, other, 2 * k :] = sfwd[s][...]
+        weighted(w_ref, rows, out_ref)
+
+    (solved_one,) = call(
+        weighted_one_kernel, after(scalars, two_own),
+        [weight_one, end_own, end_sib, side, *end_far, *end_fwd, *side_far, *side_fwd],
+        [sds((2, k, 3 * k), BF16)], scratch=[pltpu.VMEM((n_face, 2, fr, 3 * k), BF16)],
     )
 
     two_x = box_permute(two_own, 2)
-    two_y = over_face(after(two_own, *rest_far))
+    two_y = over_face(two_own)
     two_xy = [box_permute(after(a, two_x), 2) for a in two_y]
 
     def join_kernel(sc, own_ref, x_ref, out_ref):
@@ -336,20 +313,22 @@
         out_ref[:, :, 2 * k :] = own_ref[:, :, k:] + x_ref[:, :, k:]
 
     two_rows = []
-    ready = after(scalars, weight_two, iface)
+    ready = after(scalars, weight_two, solved_one)
     for own, other in zip([two_own, *two_y], [two_x, *two_xy]):
         two_rows += call(join_kernel, ready, [own, other], [sds((2, hr, 3 * k), BF16)])
     two_sib = [box_permute(a, 1) for a in two_rows]
 
-    def level_two_kernel(sc, *refs):
-        out_ref = refs[-1]
+    def weighted_two_kernel(sc, w_ref, *refs):
+        out_ref, rows = refs[2 * n_face :]
         p = sc[0]
         for s in range(n_face):
-            out_ref[s, :, pl.ds(pl.multiple_of(p * hr, hr), hr), :] = refs[s][...]
-            out_ref[s, :, pl.ds(pl.multiple_of((1 - p) * hr, hr), hr), :] = refs[n_face + s][...]
-
-    (iface_two,) = call(
-        level_two_kernel, scalars, [*two_rows, *two_sib], [sds((n_face, 2, fr, 3 * k), BF16)],
+            rows[s, :, pl.ds(pl.multiple_of(p * hr, hr), hr), :] = refs[s][...]
+            rows[s, :, pl.ds(pl.multiple_of((1 - p) * hr, hr), hr), :] = refs[n_face + s][...]
+        weighted(w_ref, rows, out_ref)
+
+    (solved_two,) = call(
+        weighted_two_kernel, scalars, [weight_two, *two_rows, *two_sib],
+        [sds((2, k, 3 * k), BF16)], scratch=[pltpu.VMEM((n_face, 2, fr, 3 * k), BF16)],
     )
 
     kept_far = [face_permute(after(a, two_own), i + 1) for i, a in enumerate(kept_out)]
@@ -360,7 +339,7 @@
     def keep_kernel(sc, *refs):
         end_ref, kept_ref, *refs = refs
         far, fwd, refs = refs[:nf], refs[nf : 2 * nf], refs[2 * nf :]
-        col_ref, w_ref, w2_ref, iface_ref, iface2_ref, out_ref, zs, stage, sems = refs
+        col_ref, one_ref, two_ref, out_ref, zs, stage, sems = refs
         p, q, f = sc[0], sc[1], sc[2]
         is_end = p == q
 
@@ -377,12 +356,8 @@
                     total = total + part[...]
                 zs[:, take, :] = total
 
-        def wide(rows):
-            parts = [piece((rows[:cr], rows[cr:]), s * fr, fr) for s in range(n_face)]
-            return jnp.concatenate(parts, axis=1)
-
-        def gathered(ref, c):
-            return ref[:, :, :, c * k : (c + 1) * k].reshape(n_face * 2 * fr, k)
+        def solved(ref, c):
+            return flat(ref[:, :, c * k : (c + 1) * k])
 
         def rows(t, c):
             return zs[t, :, c * k : (c + 1) * k]
@@ -394,8 +369,7 @@
         rights = [rows(t, 1) for t in range(2)]
         couple = [jnp.where(right, a, b) for a, b in zip(lefts, rights)]
 
-        both = dot(stacked(couple[0], couple[1]), flat(w_ref[...])).astype(BF16)
-        left = wide(both)
+        left = stacked(couple[0], couple[1])
         nothing = jnp.zeros((cr, k), BF16)
         start = [
             jnp.concatenate([jnp.where(right, nothing, a) for a in lefts], axis=0),
@@ -404,17 +378,16 @@
         ]
         merged = []
         for c in range(3):
-            merged.append((start[c].astype(F32) - dot(left, gathered(iface_ref, c))).astype(BF16))
+            merged.append((start[c].astype(F32) - dot(left, solved(one_ref, c))).astype(BF16))
         is_left = q == 0
         couple2 = jnp.where(is_left, merged[1], merged[0])
-        second = dot(stacked(couple2[:cr], couple2[cr:]), flat(w2_ref[...])).astype(BF16)
-        left = wide(second)
+        left = stacked(couple2[:cr], couple2[cr:])
         none = jnp.zeros_like(merged[0])
         copies = []
         first = [jnp.where(is_left, merged[0], none), jnp.where(is_left, none, merged[1]), merged[2]]
         for c in range(3):
             cols = slice(c * k, (c + 1) * k)
-            total = first[c].astype(F32) - dot(left, gathered(iface2_ref, c))
+            total = first[c].astype(F32) - dot(left, solved(two_ref, c))
             stage[:, :, cols] = total.astype(BF16).reshape(2, cr, k)
             copies.append(pltpu.make_async_copy(
                 stage.at[:, :, pl.ds(c * k, k)],
@@ -427,7 +400,7 @@
 
     (out,) = call(
         keep_kernel, scalars,
-        [end_kept, kept, *kept_far, *kept_fwd, skel_col, weight_one, weight_two, iface, iface_two],
+        [end_kept, kept, *kept_far, *kept_fwd, skel_col, solved_one, solved_two],
         [sds((2, 1, fr, 3 * k), BF16)], out_specs=[in_hbm],
         scratch=[pltpu.VMEM((2, fr, 3 * k), BF16), pltpu.VMEM((2, fr, 3 * k), BF16),
                  pltpu.SemaphoreType.DMA((3,))],

time: 113 us -> 70.6 us (0.62)
  Pallas kernels: 54.1 us -> 25 us
  waiting for transfers between devices: 24.6 us -> 20.5 us
  starting transfers between devices: 20.7 us -> 17.3 us
  local copies, waits for them, and re-layouts: 9.32 us -> 6.57 us
  other arithmetic: 3.14 us -> 0.52 us
    pallas_call x13 -> x12, Pallas kernels: 54.1 us -> 25 us  [call(): pl.pallas_call(kernel, in_specs=[pl.BlockSpec(memory_space=pltpu.SMEM)] +...]
    ppermute x15 -> x14, starting transfers between devices: 16.2 us -> 12.5 us  [box_permute(): return lax.ppermute(array, 'box', [(b, b ^ mask) for b in range(n_box)])]
    ppermute x5 -> x4, waiting for transfers between devices: 17 us -> 13.5 us  [face_permute(): return lax.ppermute(array, ('box', 'face'), pairs)]
    unnamed x26 -> x12, local copies, waits for them, and re-layouts: 8.58 us -> 5.83 us
    ppermute x15 -> x14, waiting for transfers between devices: 7.61 us -> 6.98 us  [box_permute(): return lax.ppermute(array, 'box', [(b, b ^ mask) for b in range(n_box)])]
    ppermute x5 -> x4, starting transfers between devices: 4.47 us -> 4.74 us  [face_permute(): return lax.ppermute(array, ('box', 'face'), pairs)]
  transfers between devices with their start and end apart: 20 -> 18, of which waited for: 10 -> 7; matrix products, arithmetic and copies ran while one was open for 3% -> 2% of each run, Pallas kernels for 13% -> 26%
where the time goes in v6:
time: 70.6 us; the launch traced here: 70.1 us
  Pallas kernels  25 us (35%)
  waiting for transfers between devices  20.5 us (29%)
  starting transfers between devices  17.3 us (25%)
  local copies, waits for them, and re-layouts  6.57 us (9%)
    pallas_call x12, Pallas kernels, call(): pl.pallas_call(kernel, in_specs=[pl.BlockSpec(memory_space=pltpu.SMEM)] +...  25 us
    ppermute x4, waiting for transfers between devices, face_permute(): return lax.ppermute(array, ('box', 'face'), pairs)  13.5 us
    ppermute x14, starting transfers between devices, box_permute(): return lax.ppermute(array, 'box', [(b, b ^ mask) for b in range(n_box)])  12.5 us
    ppermute x14, waiting for transfers between devices, box_permute(): return lax.ppermute(array, 'box', [(b, b ^ mask) for b in range(n_box)])  6.98 us
    unnamed x12, local copies, waits for them, and re-layouts  5.83 us
    ppermute x4, starting transfers between devices, face_permute(): return lax.ppermute(array, ('box', 'face'), pairs)  4.74 us
  transfers between devices with their start and end apart: 18, of which 7 were waited for; matrix products, arithmetic and copies ran while one was open for 2% of the time, Pallas kernels for 26%

profile of v6, /device:TPU:1, one launch (start us, length us, event | category | flops | bytes accessed | tf_op | source)
XLA Modules:
  0.0 70.1 jit_solution(2252256392096148586)
XLA Ops:
  0.0 0.1 pad_add_fusion.sc
  0.1 2.3 %copy-done = bf16[2,1,1,3,256,1536]{5,4,3,2,1,0:T(8,128)(2,1)S(1)} copy-done((bf16[2,1,1,3,256,1536]{5,4,3,2,1,0:T(8,128)(2,1)S(1)}, bf16[2,1,1,3,256,1536]{5,4,3,2,1,0:T(8,128)(2,1)}, u32[]{:S(2)}) %copy-start) | copy-done | bytes 4718616
  2.4 0.7 %shard_map.55 = (bf16[2,256,512]{2,1,0:T(8,128)(2,1)S(1)}, bf16[2,256,512]{2,1,0:T(8,128)(2,1)S(1)}, bf16[2,256,1536]{2,1,0:T(8,128)(2,1)S(1)}) custom-call(s32[4]{0:T(128)S(1)} %pad_add_fusion.sc, bf16[2,3,256,1536]{3,2,1,0:T(8,128)(2,1)S(1)} %bitcast.14), custom_call_target="tpu_custom_call" | custom-call | tf_op jit(solution)/shard_map/pallas_call | solution.py:42
  3.1 0.0 copy-start.2
  3.1 1.1 %copy-done.2 = bf16[2,256,1536]{2,1,0:T(8,128)(2,1)} copy-done((bf16[2,256,1536]{2,1,0:T(8,128)(2,1)}, bf16[2,256,1536]{2,1,0:T(8,128)(2,1)S(1)}, u32[]{:S(2)}) %copy-start.2) | copy-done | bytes 1572888
  4.3 0.1 collective-permute-start
  4.3 0.5 collective-permute-start.5
  4.8 2.2 %collective-permute-start.1 = (bf16[2,256,512]{2,1,0:T(8,128)(2,1)S(1)}, bf16[2,256,512]{2,1,0:T(8,128)(2,1)S(1)}, u32[]{:S(2)}, u32[]{:S(2)}) collective-permute-start(bf16[2,256,512]{2,1,0:T(8,128)(2,1)S(1)} %get-tuple-element.28.end_ref.own_ref), channel_id=1, source_target_pairs={{0,1},{1,0},{2,3},{3,2},{4,5},{5,4},{6,7},{7,6},{8,9},{9,8},{10,11... | collective-permute-start | bytes 1572872 | tf_op jit(solution)/shard_map/ppermute | solution.py:87
  7.0 0.2 fusion.own_ref
  7.2 0.9 %collective-permute-start.4 = (bf16[2,256,512]{2,1,0:T(8,128)(2,1)S(1)}, bf16[2,256,512]{2,1,0:T(8,128)(2,1)S(1)}, u32[]{:S(2)}, u32[]{:S(2)}) collective-permute-start(bf16[2,256,512]{2,1,0:T(8,128)(2,1)S(1)} %fusion.own_ref), channel_id=1, source_target_pairs={{0,2},{2,0},{4,6},{6,4},{8,10},{10,8},{12,14},{14,12},{16,18},{18,... | collective-permute-start | bytes 1572872 | tf_op jit(solution)/shard_map/ppermute | solution.py:73
  8.1 0.1 collective-permute-start.2
  8.2 0.7 %dynamic-slice_bitcast_fusion = (s32[1,512]{1,0:T(1,128)S(1)}, s32[1,512]{1,0:T(1,128)S(1)}) fusion(s32[1,4,512]{2,1,0:T(4,128)} %param.9, s32[]{:T(128)S(6)} %select_n.55, s32[1,8,512]{2,1,0:T(8,128)} %param.8, s32[]{:T(128)S(6)} %select_n.53), kind=kLoop, calls=%fused_computation.7 | loop fusion | bytes 8200 | tf_op jit(solution)/shard_map/jit(dynamic_index_in_dim)/dynamic_slice | solution.py:93
  8.9 2.3 %copy-done.1 = bf16[2,1,1,3,256,1536]{5,4,3,2,1,0:T(8,128)(2,1)S(1)} copy-done((bf16[2,1,1,3,256,1536]{5,4,3,2,1,0:T(8,128)(2,1)S(1)}, bf16[2,1,1,3,256,1536]{5,4,3,2,1,0:T(8,128)(2,1)}, u32[]{:S(2)}) %copy-start.1) | copy-done | bytes 4718616
  11.2 2.4 %shard_map.56 = (s32[1,512]{1,0:T(1,128)S(1)}, s32[512,1]{1,0:T(8,128)S(1)}, bf16[2,256,512]{2,1,0:T(8,128)(2,1)S(1)}, bf16[2,128,512]{2,1,0:T(8,128)(2,1)S(1)},...) custom-call(s32[4]{0:T(128)S(1)} %pad_add_fusion.sc, ...), custom_call_target="tpu_custom_call" | custom-call | flops 20000000000 | tf_op jit(solution)/shard_map/pallas_call | solution.py:42
  13.6 0.5 collective-permute-start.3
  14.1 0.1 fusion.1
  14.2 1.3 %collective-permute-start.8 = (bf16[2,128,512]{2,1,0:T(8,128)(2,1)S(1)}, bf16[2,128,512]{2,1,0:T(8,128)(2,1)S(1)}, u32[]{:S(2)}, u32[]{:S(2)}) collective-permute-start(bf16[2,128,512]{2,1,0:T(8,128)(2,1)S(1)} %fusion.1), channel_id=1, source_target_pairs={{0,4},{2,6},{4,0},{6,2},{8,12},{10,14},{12,8},{14,10},{16,20},{18,... | collective-permute-start | bytes 786440 | tf_op jit(solution)/shard_map/ppermute | solution.py:73
  15.5 0.4 collective-permute-start.7
  16.0 2.9 %collective-permute-done.1.rest_0_ = bf16[2,256,512]{2,1,0:T(8,128)(2,1)S(1)} collective-permute-done((bf16[2,256,512]{2,1,0:T(8,128)(2,1)S(1)}, bf16[2,256,512]{2,1,0:T(8,128)(2,1)S(1)}, u32[]{:S(2)}, u32[]{:S(2)}) %collective-permute-start.1) | collective-permute-done | bytes 524320 | tf_op jit(solution)/shard_map/ppermute | solution.py:87
  18.9 1.7 %collective-permute-start.6 = (bf16[2,256,512]{2,1,0:T(8,128)(2,1)S(1)}, bf16[2,256,512]{2,1,0:T(8,128)(2,1)S(1)}, u32[]{:S(2)}, u32[]{:S(2)}) collective-permute-start(bf16[2,256,512]{2,1,0:T(8,128)(2,1)S(1)} %collective-permute-done.1.rest_0_), channel_id=1, source_target_pairs={{0,2},{2,0},{4,6},{6,4},{8,10},{10,8},{12,14},{14,12},{16,18},{18,... | collective-permute-start | bytes 1572872 | tf_op jit(solution)/shard_map/ppermute | solution.py:73
  20.5 0.6 shard_map.58.w_ref
  21.2 1.4 %shard_map.59 = (f32[2,128,1024]{2,1,0:T(8,128)S(1)}, bf16[2,128,512]{2,1,0:T(8,128)(2,1)S(1)}) custom-call(s32[4]{0:T(128)S(1)} %pad_add_fusion.sc, bf16[2,128,1024]{2,1,0:T(8,128)(2,1)S(1)} %get-tuple-element.35.keep_ref, bf16[2,128,1024]{2,1,0:T(8,128)(2,1)S(1)} %collective-permute-done.3.recv_ref, bf16[2,512,512]{2,1,0:T(8,128)(2,1)S(1)} %shard_map.58.w_ref, ...), custom_call_target="tpu_custom_call" | custom-call | tf_op jit(solution)/shard_map/pallas_call | solution.py:42
  22.6 0.0 copy-done.3
  22.6 3.7 %shard_map.57 = (bf16[2,256,1536]{2,1,0:T(8,128)(2,1)S(1)}, bf16[2,128,1536]{2,1,0:T(8,128)(2,1)S(1)}) custom-call(s32[4]{0:T(128)S(1)} %pad_add_fusion.sc, bf16[2,256,1536]{2,1,0:T(8,128)(2,1)S(1)} %copy-done.3, bf16[2,256,1536]{2,1,0:T(8,128)(2,1)} %collective-permute-done.2.sib_ref, s32[1,512]{1,0:T(1,128)S(1)} %get-tuple-element.31.comp_ref, ...), custom_call_target="tpu_custom_call" | custom-call | tf_op jit(solution)/shard_map/pallas_call | solution.py:42
  26.3 0.1 collective-permute-start.9
  26.4 1.5 %collective-permute-done.9.rest_3_ = bf16[2,128,512]{2,1,0:T(8,128)(2,1)S(1)} collective-permute-done((bf16[2,128,512]{2,1,0:T(8,128)(2,1)S(1)}, bf16[2,128,512]{2,1,0:T(8,128)(2,1)S(1)}, u32[]{:S(2)}, u32[]{:S(2)}) %collective-permute-start.9) | collective-permute-done | bytes 262176 | tf_op jit(solution)/shard_map/ppermute | solution.py:73
  27.9 1.1 %shard_map.60.own_ref = bf16[2,128,1024]{2,1,0:T(8,128)(2,1)S(1)} custom-call(s32[4]{0:T(128)S(1)} %pad_add_fusion.sc, f32[2,128,1024]{2,1,0:T(8,128)S(1)} %get-tuple-element.38.acc_ref, bf16[2,128,512]{2,1,0:T(8,128)(2,1)S(1)} %get-tuple-element.39.hid_ref, bf16[2,256,512]{2,1,0:T(8,128)(2,1)S(1)} %collective-permute-done.1.rest_0_, ...), custom_call_target="tpu_custom_call" | custom-call | tf_op jit(solution)/shard_map/pallas_call | solution.py:42
  29.0 1.8 %collective-permute-start.14 = (bf16[2,128,1024]{2,1,0:T(8,128)(2,1)S(1)}, bf16[2,128,1024]{2,1,0:T(8,128)(2,1)S(1)}, u32[]{:S(2)}, u32[]{:S(2)}) collective-permute-start(bf16[2,128,1024]{2,1,0:T(8,128)(2,1)S(1)} %shard_map.60.own_ref), channel_id=1, source_target_pairs={{0,1},{1,0},{2,3},{3,2},{4,5},{5,4},{6,7},{7,6},{8,9},{9,8},{10,11... | collective-permute-start | bytes 1572872 | tf_op jit(solution)/shard_map/ppermute | solution.py:87
  30.9 0.8 %collective-permute-start.13 = (bf16[2,128,1024]{2,1,0:T(8,128)(2,1)S(1)}, bf16[2,128,1024]{2,1,0:T(8,128)(2,1)S(1)}, u32[]{:S(2)}, u32[]{:S(2)}) collective-permute-start(bf16[2,128,1024]{2,1,0:T(8,128)(2,1)S(1)} %shard_map.60.own_ref), channel_id=1, source_target_pairs={{0,4},{2,6},{4,0},{6,2},{8,12},{10,14},{12,8},{14,10},{16,20},{18,... | collective-permute-start | bytes 1572872 | tf_op jit(solution)/shard_map/ppermute | solution.py:73
  31.7 0.2 collective-permute-start.10
  31.9 0.1 fusion.2
  32.0 0.1 pad_maximum_fusion.own_ref
  32.1 1.3 %collective-permute-start.12 = (bf16[2,2,128,512]{3,2,1,0:T(8,128)(2,1)S(1)}, bf16[2,2,128,512]{3,2,1,0:T(8,128)(2,1)S(1)}, u32[]{:S(2)}, u32[]{:S(2)}) collective-permute-start(bf16[2,2,128,512]{3,2,1,0:T(8,128)(2,1)S(1)} %pad_maximum_fusion.own_ref), channel_id=1, source_target_pairs={{0,2},{2,0},{4,6},{6,4},{8,10},{10,8},{12,14},{14,12},{16,18},{18,... | collective-permute-start | bytes 1572872 | tf_op jit(solution)/shard_map/ppermute | solution.py:73
  33.4 9.7 %collective-permute-done.14.own_ref = bf16[2,128,1024]{2,1,0:T(8,128)(2,1)S(1)} collective-permute-done((bf16[2,128,1024]{2,1,0:T(8,128)(2,1)S(1)}, bf16[2,128,1024]{2,1,0:T(8,128)(2,1)S(1)}, u32[]{:S(2)}, u32[]{:S(2)}) %collective-permute-start.14) | collective-permute-done | bytes 524320 | tf_op jit(solution)/shard_map/ppermute | solution.py:87
  43.0 0.9 %collective-permute-done.13.x_ref = bf16[2,128,1024]{2,1,0:T(8,128)(2,1)S(1)} collective-permute-done((bf16[2,128,1024]{2,1,0:T(8,128)(2,1)S(1)}, bf16[2,128,1024]{2,1,0:T(8,128)(2,1)S(1)}, u32[]{:S(2)}, u32[]{:S(2)}) %collective-permute-start.13) | collective-permute-done | bytes 524320 | tf_op jit(solution)/shard_map/ppermute | solution.py:73
  43.9 0.6 collective-permute-start.15
  44.5 0.6 shard_map.62.w_ref
  45.1 4.2 %shard_map.61.refs_5_ = bf16[2,512,1536]{2,1,0:T(8,128)(2,1)S(1)} custom-call(s32[4]{0:T(128)S(1)} %pad_add_fusion.sc, bf16[2,512,512]{2,1,0:T(8,128)(2,1)S(1)} %shard_map.58.w_ref, bf16[2,256,512]{2,1,0:T(8,128)(2,1)S(1)} %get-tuple-element.28.end_ref.own_ref, bf16[2,256,512]{2,1,0:T(8,128)(2,1)S(1)} %collective-permute-done.5.endsib_ref.sib_ref, ...), custom_call_target="tpu_custom_call" | custom-call | tf_op jit(solution)/shard_map/pallas_call | solution.py:42
  49.3 0.6 shard_map.63.refs_0_
  49.9 1.9 %collective-permute-start.16 = (bf16[2,128,1536]{2,1,0:T(8,128)(2,1)S(1)}, bf16[2,128,1536]{2,1,0:T(8,128)(2,1)S(1)}, u32[]{:S(2)}, u32[]{:S(2)}) collective-permute-start(bf16[2,128,1536]{2,1,0:T(8,128)(2,1)S(1)} %shard_map.63.refs_0_), channel_id=1, source_target_pairs={{0,2},{2,0},{4,6},{6,4},{8,10},{10,8},{12,14},{14,12},{16,18},{18,... | collective-permute-start | bytes 2359304 | tf_op jit(solution)/shard_map/ppermute | solution.py:73
  51.8 4.3 %collective-permute-done.15.x_ref = bf16[2,128,1024]{2,1,0:T(8,128)(2,1)S(1)} collective-permute-done((bf16[2,128,1024]{2,1,0:T(8,128)(2,1)S(1)}, bf16[2,128,1024]{2,1,0:T(8,128)(2,1)S(1)}, u32[]{:S(2)}, u32[]{:S(2)}) %collective-permute-start.15) | collective-permute-done | bytes 524320 | tf_op jit(solution)/shard_map/ppermute | solution.py:73
  56.1 0.6 shard_map.64.refs_1_
  56.7 2.3 %collective-permute-start.17 = (bf16[2,128,1536]{2,1,0:T(8,128)(2,1)S(1)}, bf16[2,128,1536]{2,1,0:T(8,128)(2,1)S(1)}, u32[]{:S(2)}, u32[]{:S(2)}) collective-permute-start(bf16[2,128,1536]{2,1,0:T(8,128)(2,1)S(1)} %shard_map.64.refs_1_), channel_id=1, source_target_pairs={{0,2},{2,0},{4,6},{6,4},{8,10},{10,8},{12,14},{14,12},{16,18},{18,... | collective-permute-start | bytes 2359304 | tf_op jit(solution)/shard_map/ppermute | solution.py:73
  58.9 0.9 %collective-permute-done.10.refs_2_ = bf16[2,128,1536]{2,1,0:T(8,128)(2,1)S(1)} collective-permute-done((bf16[2,128,1536]{2,1,0:T(8,128)(2,1)S(1)}, bf16[2,128,1536]{2,1,0:T(8,128)(2,1)S(1)}, u32[]{:S(2)}, u32[]{:S(2)}) %collective-permute-start.10) | collective-permute-done | bytes 786464 | tf_op jit(solution)/shard_map/ppermute | solution.py:87
  59.9 0.7 %collective-permute-start.11 = (bf16[2,128,1536]{2,1,0:T(8,128)(2,1)S(1)}, bf16[2,128,1536]{2,1,0:T(8,128)(2,1)S(1)}, u32[]{:S(2)}, u32[]{:S(2)}) collective-permute-start(bf16[2,128,1536]{2,1,0:T(8,128)(2,1)S(1)} %collective-permute-done.10.refs_2_), channel_id=1, source_target_pairs={{0,2},{2,0},{4,6},{6,4},{8,10},{10,8},{12,14},{14,12},{16,18},{18,... | collective-permute-start | bytes 2359304 | tf_op jit(solution)/shard_map/ppermute | solution.py:73
  60.6 0.3 collective-permute-done.17.refs_3_
  60.9 4.2 %shard_map.65.refs_6_ = bf16[2,512,1536]{2,1,0:T(8,128)(2,1)S(1)} custom-call(s32[4]{0:T(128)S(1)} %pad_add_fusion.sc, bf16[2,512,512]{2,1,0:T(8,128)(2,1)S(1)} %shard_map.62.w_ref, bf16[2,128,1536]{2,1,0:T(8,128)(2,1)S(1)} %shard_map.63.refs_0_, bf16[2,128,1536]{2,1,0:T(8,128)(2,1)S(1)} %shard_map.64.refs_1_, ...), custom_call_target="tpu_custom_call" | custom-call | tf_op jit(solution)/shard_map/pallas_call | solution.py:42
  65.0 5.0 %shard_map.66 = bf16[2,1,256,1536]{3,2,1,0:T(8,128)(2,1)} custom-call(s32[4]{0:T(128)S(1)} %pad_add_fusion.sc, bf16[2,256,1536]{2,1,0:T(8,128)(2,1)S(1)} %get-tuple-element.27.refs_0_, bf16[2,256,1536]{2,1,0:T(8,128)(2,1)S(1)} %get-tuple-element.33.refs_1_, bf16[2,128,1536]{2,1,0:T(8,128)(2,1)S(1)} %collective-permute-done.10.refs_2_, ...), custom_call_target="tpu_custom_call" | custom-call | tf_op jit(solution)/shard_map/pallas_call | solution.py:42
  (18 shorter events, 0.0 us)
Async XLA Ops:
  0.1 2.3 %copy-start = (bf16[2,1,1,3,256,1536]{5,4,3,2,1,0:T(8,128)(2,1)S(1)}, bf16[2,1,1,3,256,1536]{5,4,3,2,1,0:T(8,128)(2,1)}, u32[]{:S(2)}) copy-start(bf16[2,1,1,3,256,1536]{5,4,3,2,1,0:T(8,128)(2,1)} %param.5) | copy-start | bytes 14155780
  2.4 4.6 %copy-start.5 = (bf16[2,1,256,512]{3,2,1,0:T(8,128)(2,1)S(1)}, bf16[2,1,256,512]{3,2,1,0:T(8,128)(2,1)}, u32[]{:S(2)}) copy-start(bf16[2,1,256,512]{3,2,1,0:T(8,128)(2,1)} %param.6) | copy-start | bytes 1572868
  3.1 1.1 %copy-start.2 = (bf16[2,256,1536]{2,1,0:T(8,128)(2,1)}, bf16[2,256,1536]{2,1,0:T(8,128)(2,1)S(1)}, u32[]{:S(2)}) copy-start(bf16[2,256,1536]{2,1,0:T(8,128)(2,1)S(1)} %get-tuple-element.30.own_ref) | copy-start | bytes 4718596
  4.3 4.6 %collective-permute-start = (bf16[2,256,512]{2,1,0:T(8,128)(2,1)S(1)}, bf16[2,256,512]{2,1,0:T(8,128)(2,1)}, u32[]{:S(2)}, u32[]{:S(2)}) collective-permute-start(bf16[2,256,512]{2,1,0:T(8,128)(2,1)S(1)} %get-tuple-element.26.own_ref), channel_id=1, source_target_pairs={{0,2},{2,0},{4,6},{6,4},{8,10},{10,8},{12,14},{14,12},{16,18},{18,... | collective-permute-start | bytes 1572872 | tf_op jit(solution)/shard_map/ppermute | solution.py:73
  4.3 11.2 %collective-permute-start.5 = (bf16[2,256,512]{2,1,0:T(8,128)(2,1)S(1)}, bf16[2,256,512]{2,1,0:T(8,128)(2,1)S(1)}, u32[]{:S(2)}, u32[]{:S(2)}) collective-permute-start(bf16[2,256,512]{2,1,0:T(8,128)(2,1)S(1)} %get-tuple-element.28.end_ref.own_ref), channel_id=1, source_target_pairs={{0,2},{2,0},{4,6},{6,4},{8,10},{10,8},{12,14},{14,12},{16,18},{18,... | collective-permute-start | bytes 1572872 | tf_op jit(solution)/shard_map/ppermute | solution.py:73
  4.8 14.1 %collective-permute-start.1 = (bf16[2,256,512]{2,1,0:T(8,128)(2,1)S(1)}, bf16[2,256,512]{2,1,0:T(8,128)(2,1)S(1)}, u32[]{:S(2)}, u32[]{:S(2)}) collective-permute-start(bf16[2,256,512]{2,1,0:T(8,128)(2,1)S(1)} %get-tuple-element.28.end_ref.own_ref), channel_id=1, source_target_pairs={{0,1},{1,0},{2,3},{3,2},{4,5},{5,4},{6,7},{7,6},{8,9},{9,8},{10,11... | collective-permute-start | bytes 1572872 | tf_op jit(solution)/shard_map/ppermute | solution.py:87
  7.2 7.0 %collective-permute-start.4 = (bf16[2,256,512]{2,1,0:T(8,128)(2,1)S(1)}, bf16[2,256,512]{2,1,0:T(8,128)(2,1)S(1)}, u32[]{:S(2)}, u32[]{:S(2)}) collective-permute-start(bf16[2,256,512]{2,1,0:T(8,128)(2,1)S(1)} %fusion.own_ref), channel_id=1, source_target_pairs={{0,2},{2,0},{4,6},{6,4},{8,10},{10,8},{12,14},{14,12},{16,18},{18,... | collective-permute-start | bytes 1572872 | tf_op jit(solution)/shard_map/ppermute | solution.py:73
  8.1 14.5 %collective-permute-start.2 = (bf16[2,256,1536]{2,1,0:T(8,128)(2,1)}, bf16[2,256,1536]{2,1,0:T(8,128)(2,1)}, u32[]{:S(2)}, u32[]{:S(2)}) collective-permute-start(bf16[2,256,1536]{2,1,0:T(8,128)(2,1)} %copy-done.2), channel_id=1, source_target_pairs={{0,2},{2,0},{4,6},{6,4},{8,10},{10,8},{12,14},{14,12},{16,18},{18,... | collective-permute-start | bytes 4718600 | tf_op jit(solution)/shard_map/ppermute | solution.py:73
  8.9 2.3 %copy-start.1 = (bf16[2,1,1,3,256,1536]{5,4,3,2,1,0:T(8,128)(2,1)S(1)}, bf16[2,1,1,3,256,1536]{5,4,3,2,1,0:T(8,128)(2,1)}, u32[]{:S(2)}) copy-start(bf16[2,1,1,3,256,1536]{5,4,3,2,1,0:T(8,128)(2,1)} %param.5) | copy-start | bytes 14155780
  11.2 2.9 %copy-start.4 = (bf16[2,1,128,512]{3,2,1,0:T(8,128)(2,1)S(1)}, bf16[2,1,128,512]{3,2,1,0:T(8,128)(2,1)}, u32[]{:S(2)}) copy-start(bf16[2,1,128,512]{3,2,1,0:T(8,128)(2,1)} %param.7) | copy-start | bytes 786436
  13.6 7.5 %collective-permute-start.3 = (bf16[2,128,1024]{2,1,0:T(8,128)(2,1)S(1)}, bf16[2,128,1024]{2,1,0:T(8,128)(2,1)S(1)}, u32[]{:S(2)}, u32[]{:S(2)}) collective-permute-start(bf16[2,128,1024]{2,1,0:T(8,128)(2,1)S(1)} %get-tuple-element.36), channel_id=1, source_target_pairs={{0,2},{2,0},{4,6},{6,4},{8,10},{10,8},{12,14},{14,12},{16,18},{18,... | collective-permute-start | bytes 1572872 | tf_op jit(solution)/shard_map/ppermute | solution.py:73
  14.2 12.1 %collective-permute-start.8 = (bf16[2,128,512]{2,1,0:T(8,128)(2,1)S(1)}, bf16[2,128,512]{2,1,0:T(8,128)(2,1)S(1)}, u32[]{:S(2)}, u32[]{:S(2)}) collective-permute-start(bf16[2,128,512]{2,1,0:T(8,128)(2,1)S(1)} %fusion.1), channel_id=1, source_target_pairs={{0,4},{2,6},{4,0},{6,2},{8,12},{10,14},{12,8},{14,10},{16,20},{18,... | collective-permute-start | bytes 786440 | tf_op jit(solution)/shard_map/ppermute | solution.py:73
  15.5 10.8 %collective-permute-start.7 = (bf16[2,128,512]{2,1,0:T(8,128)(2,1)S(1)}, bf16[2,128,512]{2,1,0:T(8,128)(2,1)S(1)}, u32[]{:S(2)}, u32[]{:S(2)}) collective-permute-start(bf16[2,128,512]{2,1,0:T(8,128)(2,1)S(1)} %get-tuple-element.40), channel_id=1, source_target_pairs={{0,1},{1,0},{2,3},{3,2},{4,5},{5,4},{6,7},{7,6},{8,9},{9,8},{10,11... | collective-permute-start | bytes 786440 | tf_op jit(solution)/shard_map/ppermute | solution.py:87
  18.9 7.6 %collective-permute-start.6 = (bf16[2,256,512]{2,1,0:T(8,128)(2,1)S(1)}, bf16[2,256,512]{2,1,0:T(8,128)(2,1)S(1)}, u32[]{:S(2)}, u32[]{:S(2)}) collective-permute-start(bf16[2,256,512]{2,1,0:T(8,128)(2,1)S(1)} %collective-permute-done.1.rest_0_), channel_id=1, source_target_pairs={{0,2},{2,0},{4,6},{6,4},{8,10},{10,8},{12,14},{14,12},{16,18},{18,... | collective-permute-start | bytes 1572872 | tf_op jit(solution)/shard_map/ppermute | solution.py:73
  21.2 1.4 %copy-start.3 = (bf16[2,256,1536]{2,1,0:T(8,128)(2,1)S(1)}, bf16[2,256,1536]{2,1,0:T(8,128)(2,1)}, u32[]{:S(2)}) copy-start(bf16[2,256,1536]{2,1,0:T(8,128)(2,1)} %copy-done.2) | copy-start | bytes 4718596
  26.3 1.6 %collective-permute-start.9 = (bf16[2,128,512]{2,1,0:T(8,128)(2,1)S(1)}, bf16[2,128,512]{2,1,0:T(8,128)(2,1)S(1)}, u32[]{:S(2)}, u32[]{:S(2)}) collective-permute-start(bf16[2,128,512]{2,1,0:T(8,128)(2,1)S(1)} %collective-permute-done.7.rest_2_), channel_id=1, source_target_pairs={{0,2},{2,0},{4,6},{6,4},{8,10},{10,8},{12,14},{14,12},{16,18},{18,... | collective-permute-start | bytes 786440 | tf_op jit(solution)/shard_map/ppermute | solution.py:73
  29.0 14.0 %collective-permute-start.14 = (bf16[2,128,1024]{2,1,0:T(8,128)(2,1)S(1)}, bf16[2,128,1024]{2,1,0:T(8,128)(2,1)S(1)}, u32[]{:S(2)}, u32[]{:S(2)}) collective-permute-start(bf16[2,128,1024]{2,1,0:T(8,128)(2,1)S(1)} %shard_map.60.own_ref), channel_id=1, source_target_pairs={{0,1},{1,0},{2,3},{3,2},{4,5},{5,4},{6,7},{7,6},{8,9},{9,8},{10,11... | collective-permute-start | bytes 1572872 | tf_op jit(solution)/shard_map/ppermute | solution.py:87
  30.9 13.1 %collective-permute-start.13 = (bf16[2,128,1024]{2,1,0:T(8,128)(2,1)S(1)}, bf16[2,128,1024]{2,1,0:T(8,128)(2,1)S(1)}, u32[]{:S(2)}, u32[]{:S(2)}) collective-permute-start(bf16[2,128,1024]{2,1,0:T(8,128)(2,1)S(1)} %shard_map.60.own_ref), channel_id=1, source_target_pairs={{0,4},{2,6},{4,0},{6,2},{8,12},{10,14},{12,8},{14,10},{16,20},{18,... | collective-permute-start | bytes 1572872 | tf_op jit(solution)/shard_map/ppermute | solution.py:73
  31.7 28.2 %collective-permute-start.10 = (bf16[2,128,1536]{2,1,0:T(8,128)(2,1)S(1)}, bf16[2,128,1536]{2,1,0:T(8,128)(2,1)S(1)}, u32[]{:S(2)}, u32[]{:S(2)}) collective-permute-start(bf16[2,128,1536]{2,1,0:T(8,128)(2,1)S(1)} %get-tuple-element.43), channel_id=1, source_target_pairs={{0,1},{1,0},{2,3},{3,2},{4,5},{5,4},{6,7},{7,6},{8,9},{9,8},{10,11... | collective-permute-start | bytes 2359304 | tf_op jit(solution)/shard_map/ppermute | solution.py:87
  32.1 12.4 %collective-permute-start.12 = (bf16[2,2,128,512]{3,2,1,0:T(8,128)(2,1)S(1)}, bf16[2,2,128,512]{3,2,1,0:T(8,128)(2,1)S(1)}, u32[]{:S(2)}, u32[]{:S(2)}) collective-permute-start(bf16[2,2,128,512]{3,2,1,0:T(8,128)(2,1)S(1)} %pad_maximum_fusion.own_ref), channel_id=1, source_target_pairs={{0,2},{2,0},{4,6},{6,4},{8,10},{10,8},{12,14},{14,12},{16,18},{18,... | collective-permute-start | bytes 1572872 | tf_op jit(solution)/shard_map/ppermute | solution.py:73
  43.9 12.1 %collective-permute-start.15 = (bf16[2,128,1024]{2,1,0:T(8,128)(2,1)S(1)}, bf16[2,128,1024]{2,1,0:T(8,128)(2,1)S(1)}, u32[]{:S(2)}, u32[]{:S(2)}) collective-permute-start(bf16[2,128,1024]{2,1,0:T(8,128)(2,1)S(1)} %collective-permute-done.14.own_ref), channel_id=1, source_target_pairs={{0,4},{2,6},{4,0},{6,2},{8,12},{10,14},{12,8},{14,10},{16,20},{18,... | collective-permute-start | bytes 1572872 | tf_op jit(solution)/shard_map/ppermute | solution.py:73
  49.9 10.7 %collective-permute-start.16 = (bf16[2,128,1536]{2,1,0:T(8,128)(2,1)S(1)}, bf16[2,128,1536]{2,1,0:T(8,128)(2,1)S(1)}, u32[]{:S(2)}, u32[]{:S(2)}) collective-permute-start(bf16[2,128,1536]{2,1,0:T(8,128)(2,1)S(1)} %shard_map.63.refs_0_), channel_id=1, source_target_pairs={{0,2},{2,0},{4,6},{6,4},{8,10},{10,8},{12,14},{14,12},{16,18},{18,... | collective-permute-start | bytes 2359304 | tf_op jit(solution)/shard_map/ppermute | solution.py:73
  56.7 4.2 %collective-permute-start.17 = (bf16[2,128,1536]{2,1,0:T(8,128)(2,1)S(1)}, bf16[2,128,1536]{2,1,0:T(8,128)(2,1)S(1)}, u32[]{:S(2)}, u32[]{:S(2)}) collective-permute-start(bf16[2,128,1536]{2,1,0:T(8,128)(2,1)S(1)} %shard_map.64.refs_1_), channel_id=1, source_target_pairs={{0,2},{2,0},{4,6},{6,4},{8,10},{10,8},{12,14},{14,12},{16,18},{18,... | collective-permute-start | bytes 2359304 | tf_op jit(solution)/shard_map/ppermute | solution.py:73
  59.9 5.1 %collective-permute-start.11 = (bf16[2,128,1536]{2,1,0:T(8,128)(2,1)S(1)}, bf16[2,128,1536]{2,1,0:T(8,128)(2,1)S(1)}, u32[]{:S(2)}, u32[]{:S(2)}) collective-permute-start(bf16[2,128,1536]{2,1,0:T(8,128)(2,1)S(1)} %collective-permute-done.10.refs_2_), channel_id=1, source_target_pairs={{0,2},{2,0},{4,6},{6,4},{8,10},{10,8},{12,14},{14,12},{16,18},{18,... | collective-permute-start | bytes 2359304 | tf_op jit(solution)/shard_map/ppermute | solution.py:73

commit v7 on v6

--- a/solution.py
+++ b/solution.py
@@ -7,8 +7,9 @@
 
 BF16 = jnp.bfloat16
 F32 = jnp.float32
-VMEM_BYTES = 28 * 1024 * 1024
+VMEM_BYTES = 16 * 1024 * 1024
 SLOTS_COST = 20_000_000_000
+JOIN_COST = 300_000_000
 
 
 def dot(first, second):
@@ -94,21 +95,32 @@
 
     in_hbm = pl.BlockSpec(memory_space=pltpu.HBM)
 
-    def parts_kernel(sc, leaf_ref, end_out, side_out, rows_out):
+    def parts_kernel(sc, leaf_ref, end_out, side_out, rows_out, ends_out):
         p = sc[0]
         end_out[...] = leaf_ref[:, 1 - p, :, pl.ds(pl.multiple_of(p * k, k), k)]
         side_out[...] = leaf_ref[:, 1 - p, :, 2 * k :]
         rows_out[...] = leaf_ref[:, 2]
-
-    end_own, sides_raw, s_rows = call(
-        parts_kernel, scalars, [leaf], [sds((2, fr, k), BF16)] * 2 + [sds((2, fr, 3 * k), BF16)]
-    )
-    end_far = over_face(end_own)
+        ends_out[...] = leaf_ref[:, p]
+
+    end_own, sides_raw, s_rows, end_rows = call(
+        parts_kernel, scalars, [leaf], [sds((2, fr, k), BF16)] * 2 + [sds((2, fr, 3 * k), BF16)] * 2
+    )
+    end_sib = box_permute(end_own, 1)
     sides_sib = box_permute(sides_raw, 1)
-    end_sib = box_permute(end_own, 1)
     s_sib = box_permute(s_rows, 1)
 
-    def slots_kernel(sc, leaf_ref, own_ref, sib_ref, skel_ref, skel2_ref,
+    def split_kernel(sc, own_ref, sib_ref, first_out, rest_out):
+        p, q = sc[0], sc[1]
+        rows = pl.ds(pl.multiple_of(p * hr, hr), hr)
+        own, sib = own_ref[:, rows, :], sib_ref[:, rows, :]
+        first_out[...] = jnp.where(p == q, own, sib)
+        rest_out[...] = jnp.where(p == q, sib, own)
+
+    first_send, rest_send = call(split_kernel, scalars, [end_own, end_sib], [sds((2, hr, k), BF16)] * 2)
+    first_far = over_face(first_send)
+    first_fwd = [box_permute(a, 1) for a in first_far]
+
+    def slots_kernel(sc, end_ref, own_ref, sib_ref, skel_ref, skel2_ref,
                      comp_out, col_out, side_out, half_out, keep_out, send_out, end_out):
         p, q = sc[0], sc[1]
         rows = lax.broadcasted_iota(jnp.int32, (k, k), 0)
@@ -128,17 +140,17 @@
         side_out[...] = side.astype(BF16).reshape(2, fr, k)
         half_out[...] = side_out[:, pl.ds(pl.multiple_of(p * hr, hr), hr), :]
         for t in range(2):
-            end_out[t, :, : 2 * k] = leaf_ref[t, p, :, : 2 * k]
-            end_out[t, :, 2 * k :] = dot(leaf_ref[t, p, :, 2 * k :], pick_own).astype(BF16)
+            end_out[t, :, : 2 * k] = end_ref[t, :, : 2 * k]
+            end_out[t, :, 2 * k :] = dot(end_ref[t, :, 2 * k :], pick_own).astype(BF16)
         couple = pl.ds(pl.multiple_of((1 - p) * k, k), k)
         for ref, h in ((keep_out, p), (send_out, 1 - p)):
             take = pl.ds(pl.multiple_of(h * hr, hr), hr)
             for t in range(2):
-                ref[t, :, :k] = leaf_ref[t, p, take, couple]
+                ref[t, :, :k] = end_ref[t, take, couple]
                 ref[t, :, k:] = end_out[t, take, 2 * k :]
 
     comp, skel_col, side, side_half, v_keep, v_send, end_kept = call(
-        slots_kernel, scalars, [leaf, sides_raw, sides_sib, skel_one, skel_two],
+        slots_kernel, after(scalars, first_send), [end_rows, sides_raw, sides_sib, skel_one, skel_two],
         [sds((1, k), jnp.int32), sds((k, 1), jnp.int32), sds((2, fr, k), BF16),
          sds((2, hr, k), BF16), sds((2, hr, 2 * k), BF16), sds((2, hr, 2 * k), BF16),
          sds((2, fr, 3 * k), BF16)], cost=SLOTS_COST,
@@ -159,7 +171,7 @@
     (weight_one,) = call(weight_one_kernel, scalars, [w_one, w_one_sib], [sds((2, k, k), BF16)])
 
 
-    def rows_kernel(sc, own_ref, sib_ref, comp_ref, col_ref, kept_out, *outs):
+    def rows_kernel(sc, own_ref, sib_ref, comp_ref, col_ref, rest_ref, kept_out, *outs):
         p, q, f = sc[0], sc[1], sc[2]
         pick_own = column_picker(comp_ref[...], p * k, k)
         pick_sib = column_picker(comp_ref[...], (1 - p) * k, k)
@@ -173,7 +185,16 @@
                     own, sib = own_ref[t, :, cols], sib_ref[t, :, cols]
                     if c == 2:
                         own, sib = [dot(a, b).astype(BF16) for a, b in ((own, pick_own), (sib, pick_sib))]
-                    write(t, cols, (dot(take_own, own) + dot(take_sib, sib)).astype(BF16))
+                    write(t, c, (dot(take_own, own) + dot(take_sib, sib)).astype(BF16))
+
+        for s in range(nf):
+            outs[s][:, :, :k] = rest_ref[...]
+
+        def write_far(s, t, c, picked):
+            if c == 0:
+                outs[s][t, :, k:] = picked
+            else:
+                outs[nf + s][t, :, (c - 1) * k : c * k] = picked
 
         def col_half(s):
             start = (f + n_face - s - 1) % n_face * fr + p * hr
@@ -183,9 +204,9 @@
         def _():
             far = jnp.concatenate([col_half(s) for s in range(nf)], axis=0)
 
-            def write(t, cols, picked):
+            def write(t, c, picked):
                 for s in range(nf):
-                    outs[s][t, :, cols] = picked[s * hr : (s + 1) * hr]
+                    write_far(s, t, c, picked[s * hr : (s + 1) * hr])
 
             pick(far, write)
 
@@ -194,16 +215,16 @@
             far = jnp.concatenate([col_half(s) for s in range(nf)], axis=0)
             slots = jnp.concatenate([col_ref[pl.ds(pl.multiple_of(f * fr, fr), fr), :], far], axis=0)
 
-            def write(t, cols, picked):
-                kept_out[t, :, cols] = picked[:fr]
+            def write(t, c, picked):
+                kept_out[t, :, c * k : (c + 1) * k] = picked[:fr]
                 for s in range(nf):
-                    outs[s][t, :, cols] = picked[fr + s * hr : fr + (s + 1) * hr]
+                    write_far(s, t, c, picked[fr + s * hr : fr + (s + 1) * hr])
 
             pick(slots, write)
 
     kept, *kept_out = call(
-        rows_kernel, after(scalars, *end_far), [s_rows, s_sib, comp, skel_col],
-        [sds((2, fr, 3 * k), BF16)] + [sds((2, hr, 3 * k), BF16)] * nf,
+        rows_kernel, after(scalars, *first_far), [s_rows, s_sib, comp, skel_col, rest_send],
+        [sds((2, fr, 3 * k), BF16)] + [sds((2, hr, 2 * k), BF16)] * (2 * nf),
     )
 
     def piece(hidden, start, count):
@@ -232,7 +253,7 @@
         acc_out[:, :, k:] = rows[:, :, k:].astype(F32) - dot(left, flat(side_ref[...])).reshape(2, hr, k)
 
     v_acc, v_hid = call(
-        iface_kernel, after(scalars, *end_far), [v_keep, v_recv, weight_one, end_own, end_sib, side],
+        iface_kernel, after(scalars, *first_far), [v_keep, v_recv, weight_one, end_own, end_sib, side],
         [sds((2, hr, 2 * k), F32), sds((2, hr, k), BF16)],
         scratch=[pltpu.VMEM((2, hr, 2 * k), BF16)],
     )
@@ -249,28 +270,47 @@
     (weight_two,) = call(weight_two_kernel, scalars, [w_two_pair, w_two_sib], [sds((2, k, k), BF16)])
 
     side_fwd = [box_permute(after(a, kept, v_acc, w_two_x), 1) for a in side_far]
-    end_fwd = [box_permute(a, 1) for a in end_far]
+    mixed_far = [face_permute(after(a, v_acc), i + 1) for i, a in enumerate(kept_out[:nf])]
 
     def iface_far_kernel(sc, acc_ref, hid_ref, *rest):
         refs = [rest[i * nf : (i + 1) * nf] for i in range(4)]
-        out_ref, rows = rest[4 * nf :]
+        end_out, keep_out, send_out, rows = rest[4 * nf :]
         p, q = sc[0], sc[1]
         mine = pl.ds(pl.multiple_of(p * hr, hr), hr)
         other = pl.ds(pl.multiple_of((1 - p) * hr, hr), hr)
         hidden = [hid_ref[0], hid_ref[1]]
         total = acc_ref[...]
         for s in range(nf):
-            rows[:, :, :k] = jnp.where(p == q, refs[0][s][...], refs[1][s][...])
+            rows[:, mine, :k] = refs[0][s][...]
+            rows[:, other, :k] = refs[1][s][...]
             rows[:, mine, k:] = refs[2][s][...]
             rows[:, other, k:] = refs[3][s][...]
             left = piece(hidden, (s + 1) * fr, fr)
             total = total - dot(left, flat(rows[...])).reshape(2, hr, 2 * k)
-        out_ref[...] = total.astype(BF16)
+        total = total.astype(BF16)
+        end_out[...] = total[:, :, :k]
+        low, high = total[:, :, k : k + half], total[:, :, k + half :]
+        keep_out[...] = jnp.where(q == 0, low, high)
+        send_out[...] = jnp.where(q == 0, high, low)
+
+    two_end, side_keep, side_send = call(
+        iface_far_kernel, scalars, [v_acc, v_hid, *first_far, *first_fwd, *side_far, *side_fwd],
+        [sds((2, hr, k), BF16)] + [sds((2, hr, half), BF16)] * 2, scratch=[pltpu.VMEM((2, fr, 2 * k), BF16)],
+    )
+
+    side_x = box_permute(side_send, 2)
+
+    def pack_kernel(sc, end_ref, keep_ref, x_ref, out_ref):
+        out_ref[:, :, :k] = end_ref[...]
+        out_ref[:, :, k:] = keep_ref[...] + x_ref[...]
 
     (two_own,) = call(
-        iface_far_kernel, scalars, [v_acc, v_hid, *end_far, *end_fwd, *side_far, *side_fwd],
-        [sds((2, hr, 2 * k), BF16)], scratch=[pltpu.VMEM((2, fr, 2 * k), BF16)],
-    )
+        pack_kernel, scalars, [two_end, side_keep, side_x], [sds((2, hr, k + half), BF16)]
+    )
+    two_x = box_permute(two_own, 2)
+    two_y = over_face(after(two_own, *mixed_far))
+    mixed_fwd = [box_permute(after(a, two_own), 1) for a in mixed_far]
+
     def weighted(w_ref, rows, out_ref):
         left = jnp.concatenate([piece((w_ref[0], w_ref[1]), s * fr, fr) for s in range(n_face)], axis=1)
         for c in range(3):
@@ -279,9 +319,11 @@
             out_ref[:, :, cols] = dot(left, right).astype(BF16).reshape(2, k, k)
 
     def weighted_one_kernel(sc, w_ref, own_ref, sib_ref, side_ref, *rest):
-        far, fwd, sfar, sfwd = (rest[i * nf : (i + 1) * nf] for i in range(4))
-        out_ref, rows = rest[4 * nf :]
-        p = sc[0]
+        refs = [rest[i * nf : (i + 1) * nf] for i in range(6)]
+        out_ref, rows = rest[6 * nf :]
+        p, q = sc[0], sc[1]
+        first_cols = pl.ds(pl.multiple_of(q * k, k), k)
+        rest_cols = pl.ds(pl.multiple_of((1 - q) * k, k), k)
         own_cols = pl.ds(pl.multiple_of(p * k, k), k)
         sib_cols = pl.ds(pl.multiple_of((1 - p) * k, k), k)
         mine = pl.ds(pl.multiple_of(p * hr, hr), hr)
@@ -290,56 +332,51 @@
         rows[0, :, :, sib_cols] = sib_ref[...]
         rows[0, :, :, 2 * k :] = side_ref[...]
         for s in range(nf):
-            rows[s + 1, :, :, own_cols] = far[s][...]
-            rows[s + 1, :, :, sib_cols] = fwd[s][...]
-            rows[s + 1, :, mine, 2 * k :] = sfar[s][...]
-            rows[s + 1, :, other, 2 * k :] = sfwd[s][...]
+            for h, take in enumerate((mine, other)):
+                rows[s + 1, :, take, first_cols] = refs[h][s][...]
+                rows[s + 1, :, take, rest_cols] = refs[2 + h][s][:, :, :k]
+                rows[s + 1, :, take, 2 * k :] = refs[4 + h][s][...]
         weighted(w_ref, rows, out_ref)
 
     (solved_one,) = call(
-        weighted_one_kernel, after(scalars, two_own),
-        [weight_one, end_own, end_sib, side, *end_far, *end_fwd, *side_far, *side_fwd],
+        weighted_one_kernel, scalars,
+        [weight_one, end_own, end_sib, side, *first_far, *first_fwd, *mixed_far, *mixed_fwd, *side_far, *side_fwd],
         [sds((2, k, 3 * k), BF16)], scratch=[pltpu.VMEM((n_face, 2, fr, 3 * k), BF16)],
     )
-
-    two_x = box_permute(two_own, 2)
-    two_y = over_face(two_own)
-    two_xy = [box_permute(after(a, two_x), 2) for a in two_y]
 
     def join_kernel(sc, own_ref, x_ref, out_ref):
         q = sc[1]
-        out_ref[:, :, pl.ds(pl.multiple_of(q * k, k), k)] = own_ref[:, :, :k]
-        out_ref[:, :, pl.ds(pl.multiple_of((1 - q) * k, k), k)] = x_ref[:, :, :k]
-        out_ref[:, :, 2 * k :] = own_ref[:, :, k:] + x_ref[:, :, k:]
-
-    two_rows = []
-    ready = after(scalars, weight_two, solved_one)
-    for own, other in zip([two_own, *two_y], [two_x, *two_xy]):
-        two_rows += call(join_kernel, ready, [own, other], [sds((2, hr, 3 * k), BF16)])
+        for ref, which in ((own_ref, q), (x_ref, 1 - q)):
+            out_ref[:, :, pl.ds(pl.multiple_of(which * k, k), k)] = ref[:, :, :k]
+            out_ref[:, :, pl.ds(pl.multiple_of(2 * k + which * half, half), half)] = ref[:, :, k:]
+
+    two_shape = [sds((2, hr, 3 * k), BF16)]
+    two_rows = call(join_kernel, scalars, [two_own, two_x], two_shape, cost=JOIN_COST)
+    two_xy = [box_permute(after(a, *two_rows), 2) for a in two_y]
+    for own, other in zip(two_y, two_xy):
+        two_rows += call(join_kernel, after(scalars, weight_two, solved_one), [own, other], two_shape)
     two_sib = [box_permute(a, 1) for a in two_rows]
 
-    def weighted_two_kernel(sc, w_ref, *refs):
-        out_ref, rows = refs[2 * n_face :]
+    def level_two_kernel(sc, *refs):
+        out_ref = refs[-1]
         p = sc[0]
         for s in range(n_face):
-            rows[s, :, pl.ds(pl.multiple_of(p * hr, hr), hr), :] = refs[s][...]
-            rows[s, :, pl.ds(pl.multiple_of((1 - p) * hr, hr), hr), :] = refs[n_face + s][...]
-        weighted(w_ref, rows, out_ref)
-
-    (solved_two,) = call(
-        weighted_two_kernel, scalars, [weight_two, *two_rows, *two_sib],
-        [sds((2, k, 3 * k), BF16)], scratch=[pltpu.VMEM((n_face, 2, fr, 3 * k), BF16)],
-    )
-
-    kept_far = [face_permute(after(a, two_own), i + 1) for i, a in enumerate(kept_out)]
+            out_ref[s, :, pl.ds(pl.multiple_of(p * hr, hr), hr), :] = refs[s][...]
+            out_ref[s, :, pl.ds(pl.multiple_of((1 - p) * hr, hr), hr), :] = refs[n_face + s][...]
+
+    (iface_two,) = call(
+        level_two_kernel, scalars, [*two_rows, *two_sib], [sds((n_face, 2, fr, 3 * k), BF16)]
+    )
+
+    kept_far = [face_permute(after(a, two_own), i + 1) for i, a in enumerate(kept_out[nf:])]
     kept_fwd = [box_permute(a, 1) for a in kept_far]
 
     cr = fr
 
     def keep_kernel(sc, *refs):
         end_ref, kept_ref, *refs = refs
-        far, fwd, refs = refs[:nf], refs[nf : 2 * nf], refs[2 * nf :]
-        col_ref, one_ref, two_ref, out_ref, zs, stage, sems = refs
+        parts = [refs[i * nf : (i + 1) * nf] for i in range(4)]
+        col_ref, one_ref, w_ref, two_ref, out_ref, zs, stage, sems = refs[4 * nf :]
         p, q, f = sc[0], sc[1], sc[2]
         is_end = p == q
 
@@ -349,15 +386,25 @@
 
         @pl.when(p != q)
         def _():
-            for h, parts in enumerate((far, fwd)):
+            for h in range(2):
                 take = pl.ds(pl.multiple_of((p ^ h) * hr, hr), hr)
-                total = kept_ref[:, take, :]
-                for part in parts:
-                    total = total + part[...]
-                zs[:, take, :] = total
+                for refs, cols, source in (
+                    (parts[h], slice(0, k), slice(k, 2 * k)), (parts[2 + h], slice(k, 3 * k), slice(0, 2 * k)),
+                ):
+                    total = kept_ref[:, take, cols]
+                    for ref in refs:
+                        total = total + ref[:, :, source]
+                    zs[:, take, cols] = total
+
+        def wide(rows):
+            parts = [piece((rows[:cr], rows[cr:]), s * fr, fr) for s in range(n_face)]
+            return jnp.concatenate(parts, axis=1)
 
         def solved(ref, c):
             return flat(ref[:, :, c * k : (c + 1) * k])
+
+        def gathered(ref, c):
+            return ref[:, :, :, c * k : (c + 1) * k].reshape(n_face * 2 * fr, k)
 
         def rows(t, c):
             return zs[t, :, c * k : (c + 1) * k]
@@ -381,13 +428,14 @@
             merged.append((start[c].astype(F32) - dot(left, solved(one_ref, c))).astype(BF16))
         is_left = q == 0
         couple2 = jnp.where(is_left, merged[1], merged[0])
-        left = stacked(couple2[:cr], couple2[cr:])
+        second = dot(stacked(couple2[:cr], couple2[cr:]), flat(w_ref[...])).astype(BF16)
+        left = wide(second)
         none = jnp.zeros_like(merged[0])
         copies = []
         first = [jnp.where(is_left, merged[0], none), jnp.where(is_left, none, merged[1]), merged[2]]
         for c in range(3):
             cols = slice(c * k, (c + 1) * k)
-            total = first[c].astype(F32) - dot(left, solved(two_ref, c))
+            total = first[c].astype(F32) - dot(left, gathered(two_ref, c))
             stage[:, :, cols] = total.astype(BF16).reshape(2, cr, k)
             copies.append(pltpu.make_async_copy(
                 stage.at[:, :, pl.ds(c * k, k)],
@@ -400,7 +448,7 @@
 
     (out,) = call(
         keep_kernel, scalars,
-        [end_kept, kept, *kept_far, *kept_fwd, skel_col, solved_one, solved_two],
+        [end_kept, kept, *mixed_far, *mixed_fwd, *kept_far, *kept_fwd, skel_col, solved_one, weight_two, iface_two],
         [sds((2, 1, fr, 3 * k), BF16)], out_specs=[in_hbm],
         scratch=[pltpu.VMEM((2, fr, 3 * k), BF16), pltpu.VMEM((2, fr, 3 * k), BF16),
                  pltpu.SemaphoreType.DMA((3,))],

time: 70.6 us -> 73 us (1.034)
  starting transfers between devices: 17.3 us -> 21.6 us
  waiting for transfers between devices: 20.5 us -> 18 us
  other arithmetic: 0.52 us -> 1.56 us
  local copies, waits for them, and re-layouts: 6.57 us -> 5.63 us
    ppermute x4 -> x5, waiting for transfers between devices: 13.5 us -> 6.81 us  [face_permute(): return lax.ppermute(array, ('box', 'face'), pairs)]
    ppermute x14 -> x16, waiting for transfers between devices: 6.98 us -> 11.2 us  [box_permute(): return lax.ppermute(array, 'box', [(b, b ^ mask) for b in range(n_box)])]
    ppermute x14 -> x16, starting transfers between devices: 12.5 us -> 16.1 us  [box_permute(): return lax.ppermute(array, 'box', [(b, b ^ mask) for b in range(n_box)])]
    concatenate x1, other arithmetic: 0.19 us -> 1.23 us  [on_device(): w_one = jnp.roll(w_first[:, 0], -face * fr, axis=2)]
    unnamed x12 -> x8, local copies, waits for them, and re-layouts: 5.83 us -> 4.89 us
    ppermute x4 -> x5, starting transfers between devices: 4.74 us -> 5.55 us  [face_permute(): return lax.ppermute(array, ('box', 'face'), pairs)]
    pallas_call x12 -> x14, Pallas kernels: 25 us -> 25.2 us  [call(): pl.pallas_call(kernel, in_specs=[pl.BlockSpec(memory_space=pltpu.SMEM)] +...]
  transfers between devices with their start and end apart: 18 -> 21, of which waited for: 7 -> 9; matrix products, arithmetic and copies ran while one was open for 2% -> 3% of each run, Pallas kernels for 26% -> 25%
where the time goes in v7:
time: 73 us; the launch traced here: 72.4 us
  Pallas kernels  25.2 us (35%)
  starting transfers between devices  21.6 us (30%)
  waiting for transfers between devices  18 us (25%)
  local copies, waits for them, and re-layouts  5.63 us (8%)
  other arithmetic  1.56 us (2%)
    pallas_call x14, Pallas kernels, call(): pl.pallas_call(kernel, in_specs=[pl.BlockSpec(memory_space=pltpu.SMEM)] +...  25.2 us
    ppermute x16, starting transfers between devices, box_permute(): return lax.ppermute(array, 'box', [(b, b ^ mask) for b in range(n_box)])  16.1 us
    ppermute x16, waiting for transfers between devices, box_permute(): return lax.ppermute(array, 'box', [(b, b ^ mask) for b in range(n_box)])  11.2 us
    ppermute x5, waiting for transfers between devices, face_permute(): return lax.ppermute(array, ('box', 'face'), pairs)  6.81 us
    ppermute x5, starting transfers between devices, face_permute(): return lax.ppermute(array, ('box', 'face'), pairs)  5.55 us
    unnamed x8, local copies, waits for them, and re-layouts  4.89 us
  transfers between devices with their start and end apart: 21, of which 9 were waited for; matrix products, arithmetic and copies ran while one was open for 3% of the time, Pallas kernels for 25%

profile of v7, /device:TPU:1, one launch (start us, length us, event | category | flops | bytes accessed | tf_op | source)
XLA Modules:
  0.0 72.4 jit_solution(15712848339124673497)
XLA Ops:
  0.1 2.3 %copy-done = bf16[2,1,1,3,256,1536]{5,4,3,2,1,0:T(8,128)(2,1)S(1)} copy-done((bf16[2,1,1,3,256,1536]{5,4,3,2,1,0:T(8,128)(2,1)S(1)}, bf16[2,1,1,3,256,1536]{5,4,3,2,1,0:T(8,128)(2,1)}, u32[]{:S(2)}) %copy-start) | copy-done | bytes 4718616
  2.4 1.6 %shard_map.55 = (bf16[2,256,512]{2,1,0:T(8,128)(2,1)S(1)}, bf16[2,256,512]{2,1,0:T(8,128)(2,1)}, bf16[2,256,1536]{2,1,0:T(8,128)(2,1)S(1)}, bf16[2,256,1536]{2,1,0:T(8,128)(2,1)S(1)}) custom-call(s32[4]{0:T(128)S(1)} %pad_add_fusion.sc, bf16[2,3,256,1536]{3,2,1,0:T(8,128)(2,1)S(1)} %bitcast.14), custom_call_target="tpu_custom_call" | custom-call | tf_op jit(solution)/shard_map/pallas_call | solution.py:43
  4.0 1.1 %copy-done.1 = bf16[2,256,1536]{2,1,0:T(8,128)(2,1)} copy-done((bf16[2,256,1536]{2,1,0:T(8,128)(2,1)}, bf16[2,256,1536]{2,1,0:T(8,128)(2,1)S(1)}, u32[]{:S(2)}) %copy-start.1) | copy-done | bytes 1572888
  5.2 0.5 collective-permute-start.1
  5.7 1.2 %fusion.own_ref = bf16[2,256,512]{2,1,0:T(8,128)(2,1)S(1)} fusion(s32[]{:T(128)S(6)} %select_n.57, bf16[2,256,512]{2,1,0:T(8,128)(2,1)} %bitcast.17), kind=kLoop, calls=%fused_computation.2 | loop fusion | flops 1048576 | bytes 1048580 | tf_op jit(solution)/shard_map/jit(_roll_dynamic)/concatenate | solution.py:161
  6.9 0.1 collective-permute-start.5
  7.0 0.5 collective-permute-start.3
  7.5 0.7 %dynamic-slice_bitcast_fusion = (s32[1,512]{1,0:T(1,128)S(1)}, s32[1,512]{1,0:T(1,128)S(1)}) fusion(s32[1,4,512]{2,1,0:T(4,128)} %param.9, s32[]{:T(128)S(6)} %select_n.55, s32[1,8,512]{2,1,0:T(8,128)} %param.8, s32[]{:T(128)S(6)} %select_n.53), kind=kLoop, calls=%fused_computation.7 | loop fusion | bytes 8200 | tf_op jit(solution)/shard_map/jit(dynamic_index_in_dim)/dynamic_slice | solution.py:94
  8.2 0.6 shard_map.56
  8.9 1.4 %copy-done.2 = bf16[2,256,1536]{2,1,0:T(8,128)(2,1)S(1)} copy-done((bf16[2,256,1536]{2,1,0:T(8,128)(2,1)S(1)}, bf16[2,256,1536]{2,1,0:T(8,128)(2,1)}, u32[]{:S(2)}) %copy-start.2) | copy-done | bytes 1572888
  10.3 2.5 %shard_map.57 = (s32[1,512]{1,0:T(1,128)S(1)}, s32[512,1]{1,0:T(8,128)S(1)}, bf16[2,256,512]{2,1,0:T(8,128)(2,1)S(1)}, bf16[2,128,512]{2,1,0:T(8,128)(2,1)S(1)},...) custom-call(s32[4]{0:T(128)S(1)} %pad_add_fusion.sc, ...), custom_call_target="tpu_custom_call" | custom-call | flops 20000000000 | tf_op jit(solution)/shard_map/pallas_call | solution.py:43
  12.8 0.1 collective-permute-start.4
  13.0 2.7 %collective-permute-start.2 = (bf16[2,128,512]{2,1,0:T(8,128)(2,1)S(1)}, bf16[2,128,512]{2,1,0:T(8,128)(2,1)S(1)}, u32[]{:S(2)}, u32[]{:S(2)}) collective-permute-start(bf16[2,128,512]{2,1,0:T(8,128)(2,1)S(1)} %get-tuple-element.37), channel_id=1, source_target_pairs={{0,1},{1,0},{2,3},{3,2},{4,5},{5,4},{6,7},{7,6},{8,9},{9,8},{10,11... | collective-permute-start | bytes 786440 | tf_op jit(solution)/shard_map/ppermute | solution.py:88
  15.6 0.1 fusion.1
  15.7 1.3 %collective-permute-start.9 = (bf16[2,128,512]{2,1,0:T(8,128)(2,1)S(1)}, bf16[2,128,512]{2,1,0:T(8,128)(2,1)S(1)}, u32[]{:S(2)}, u32[]{:S(2)}) collective-permute-start(bf16[2,128,512]{2,1,0:T(8,128)(2,1)S(1)} %fusion.1), channel_id=1, source_target_pairs={{0,4},{2,6},{4,0},{6,2},{8,12},{10,14},{12,8},{14,10},{16,20},{18,... | collective-permute-start | bytes 786440 | tf_op jit(solution)/shard_map/ppermute | solution.py:74
  17.0 0.2 collective-permute-start.8
  17.2 1.1 %shard_map.59.w_ref = bf16[2,512,512]{2,1,0:T(8,128)(2,1)S(1)} custom-call(s32[4]{0:T(128)S(1)} %pad_add_fusion.sc, bf16[2,256,512]{2,1,0:T(8,128)(2,1)S(1)} %fusion.own_ref, bf16[2,256,512]{2,1,0:T(8,128)(2,1)} %collective-permute-done.5.sib_ref), custom_call_target="tpu_custom_call" | custom-call | tf_op jit(solution)/shard_map/pallas_call | solution.py:43
  18.4 3.8 %collective-permute-done.2.rest_0_ = bf16[2,128,512]{2,1,0:T(8,128)(2,1)S(1)} collective-permute-done((bf16[2,128,512]{2,1,0:T(8,128)(2,1)S(1)}, bf16[2,128,512]{2,1,0:T(8,128)(2,1)S(1)}, u32[]{:S(2)}, u32[]{:S(2)}) %collective-permute-start.2) | collective-permute-done | bytes 262176 | tf_op jit(solution)/shard_map/ppermute | solution.py:88
  22.2 1.4 %shard_map.60 = (f32[2,128,1024]{2,1,0:T(8,128)S(1)}, bf16[2,128,512]{2,1,0:T(8,128)(2,1)S(1)}) custom-call(s32[4]{0:T(128)S(1)} %pad_add_fusion.sc, bf16[2,128,1024]{2,1,0:T(8,128)(2,1)S(1)} %get-tuple-element.49.keep_ref, bf16[2,128,1024]{2,1,0:T(8,128)(2,1)S(1)} %collective-permute-done.4.recv_ref, bf16[2,512,512]{2,1,0:T(8,128)(2,1)S(1)} %shard_map.59.w_ref, ...), custom_call_target="tpu_custom_call" | custom-call | tf_op jit(solution)/shard_map/pallas_call | solution.py:43
  23.6 3.8 %shard_map.58 = (bf16[2,256,1536]{2,1,0:T(8,128)(2,1)S(1)}, bf16[2,128,1024]{2,1,0:T(8,128)(2,1)S(1)}, bf16[2,128,1024]{2,1,0:T(8,128)(2,1)S(1)}) custom-call(s32[4]{0:T(128)S(1)} %pad_add_fusion.sc, bf16[2,256,1536]{2,1,0:T(8,128)(2,1)S(1)} %get-tuple-element.43.own_ref, bf16[2,256,1536]{2,1,0:T(8,128)(2,1)} %collective-permute-done.3.sib_ref, ...), custom_call_target="tpu_custom_call" | custom-call | tf_op jit(solution)/shard_map/pallas_call | solution.py:43
  27.4 1.4 %collective-permute-start.6 = (bf16[2,128,1024]{2,1,0:T(8,128)(2,1)S(1)}, bf16[2,128,1024]{2,1,0:T(8,128)(2,1)S(1)}, u32[]{:S(2)}, u32[]{:S(2)}) collective-permute-start(bf16[2,128,1024]{2,1,0:T(8,128)(2,1)S(1)} %get-tuple-element.53), channel_id=1, source_target_pairs={{0,1},{1,0},{2,3},{3,2},{4,5},{5,4},{6,7},{7,6},{8,9},{9,8},{10,11... | collective-permute-start | bytes 1572872 | tf_op jit(solution)/shard_map/ppermute | solution.py:88
  28.7 0.8 %collective-permute-start.7 = (bf16[2,128,512]{2,1,0:T(8,128)(2,1)S(1)}, bf16[2,128,512]{2,1,0:T(8,128)(2,1)S(1)}, u32[]{:S(2)}, u32[]{:S(2)}) collective-permute-start(bf16[2,128,512]{2,1,0:T(8,128)(2,1)S(1)} %collective-permute-done.2.rest_0_), channel_id=1, source_target_pairs={{0,2},{2,0},{4,6},{6,4},{8,10},{10,8},{12,14},{14,12},{16,18},{18,... | collective-permute-start | bytes 786440 | tf_op jit(solution)/shard_map/ppermute | solution.py:74
  29.6 1.1 %collective-permute-done.7.rest_1_ = bf16[2,128,512]{2,1,0:T(8,128)(2,1)S(1)} collective-permute-done((bf16[2,128,512]{2,1,0:T(8,128)(2,1)S(1)}, bf16[2,128,512]{2,1,0:T(8,128)(2,1)S(1)}, u32[]{:S(2)}, u32[]{:S(2)}) %collective-permute-start.7) | collective-permute-done | bytes 262176 | tf_op jit(solution)/shard_map/ppermute | solution.py:74
  30.7 0.4 collective-permute-done.10.rest_3_.rest_5_
  31.1 1.1 %shard_map.61 = (bf16[2,128,512]{2,1,0:T(8,128)(2,1)S(1)}, bf16[2,128,256]{2,1,0:T(8,128)(2,1)S(1)}, bf16[2,128,256]{2,1,0:T(8,128)(2,1)S(1)}) custom-call(s32[4]{0:T(128)S(1)} %pad_add_fusion.sc, f32[2,128,1024]{2,1,0:T(8,128)S(1)} %get-tuple-element.52.acc_ref, bf16[2,128,512]{2,1,0:T(8,128)(2,1)S(1)} %get-tuple-element.54.hid_ref, ...), custom_call_target="tpu_custom_call" | custom-call | tf_op jit(solution)/shard_map/pallas_call | solution.py:43
  32.1 2.0 %collective-permute-start.11 = (bf16[2,128,256]{2,1,0:T(8,128)(2,1)S(1)}, bf16[2,128,256]{2,1,0:T(8,128)(2,1)S(1)}, u32[]{:S(2)}, u32[]{:S(2)}) collective-permute-start(bf16[2,128,256]{2,1,0:T(8,128)(2,1)S(1)} %get-tuple-element.60), channel_id=1, source_target_pairs={{0,4},{2,6},{4,0},{6,2},{8,12},{10,14},{12,8},{14,10},{16,20},{18,... | collective-permute-start | bytes 393224 | tf_op jit(solution)/shard_map/ppermute | solution.py:74
  34.2 3.6 %collective-permute-done.11.x_ref = bf16[2,128,256]{2,1,0:T(8,128)(2,1)S(1)} collective-permute-done((bf16[2,128,256]{2,1,0:T(8,128)(2,1)S(1)}, bf16[2,128,256]{2,1,0:T(8,128)(2,1)S(1)}, u32[]{:S(2)}, u32[]{:S(2)}) %collective-permute-start.11) | collective-permute-done | bytes 131104 | tf_op jit(solution)/shard_map/ppermute | solution.py:74
  37.8 0.6 shard_map.62.own_ref
  38.3 1.2 %collective-permute-start.16 = (bf16[2,128,768]{2,1,0:T(8,128)(2,1)S(1)}, bf16[2,128,768]{2,1,0:T(8,128)(2,1)S(1)}, u32[]{:S(2)}, u32[]{:S(2)}) collective-permute-start(bf16[2,128,768]{2,1,0:T(8,128)(2,1)S(1)} %shard_map.62.own_ref), channel_id=1, source_target_pairs={{0,4},{2,6},{4,0},{6,2},{8,12},{10,14},{12,8},{14,10},{16,20},{18,... | collective-permute-start | bytes 1179656 | tf_op jit(solution)/shard_map/ppermute | solution.py:74
  39.6 1.3 %collective-permute-done.6.rest_2_.refs_2_ = bf16[2,128,1024]{2,1,0:T(8,128)(2,1)S(1)} collective-permute-done((bf16[2,128,1024]{2,1,0:T(8,128)(2,1)S(1)}, bf16[2,128,1024]{2,1,0:T(8,128)(2,1)S(1)}, u32[]{:S(2)}, u32[]{:S(2)}) %collective-permute-start.6) | collective-permute-done | bytes 524320 | tf_op jit(solution)/shard_map/ppermute | solution.py:88
  40.8 0.9 %collective-permute-start.17 = (bf16[2,128,768]{2,1,0:T(8,128)(2,1)S(1)}, bf16[2,128,768]{2,1,0:T(8,128)(2,1)S(1)}, u32[]{:S(2)}, u32[]{:S(2)}) collective-permute-start(bf16[2,128,768]{2,1,0:T(8,128)(2,1)S(1)} %shard_map.62.own_ref), channel_id=1, source_target_pairs={{0,1},{1,0},{2,3},{3,2},{4,5},{5,4},{6,7},{7,6},{8,9},{9,8},{10,11... | collective-permute-start | bytes 1179656 | tf_op jit(solution)/shard_map/ppermute | solution.py:88
  41.7 0.1 fusion.2
  41.8 1.7 %collective-permute-start.15 = (bf16[2,2,128,512]{3,2,1,0:T(8,128)(2,1)S(1)}, bf16[2,2,128,512]{3,2,1,0:T(8,128)(2,1)S(1)}, u32[]{:S(2)}, u32[]{:S(2)}) collective-permute-start(bf16[2,2,128,512]{3,2,1,0:T(8,128)(2,1)S(1)} %pad_maximum_fusion.own_ref), channel_id=1, source_target_pairs={{0,2},{2,0},{4,6},{6,4},{8,10},{10,8},{12,14},{14,12},{16,18},{18,... | collective-permute-start | bytes 1572872 | tf_op jit(solution)/shard_map/ppermute | solution.py:74
  43.6 0.1 collective-permute-start.12
  43.6 4.5 %collective-permute-done.16.x_ref = bf16[2,128,768]{2,1,0:T(8,128)(2,1)S(1)} collective-permute-done((bf16[2,128,768]{2,1,0:T(8,128)(2,1)S(1)}, bf16[2,128,768]{2,1,0:T(8,128)(2,1)S(1)}, u32[]{:S(2)}, u32[]{:S(2)}) %collective-permute-start.16) | collective-permute-done | bytes 393248 | tf_op jit(solution)/shard_map/ppermute | solution.py:74
  48.2 0.6 shard_map.65.refs_0_
  48.8 1.7 %collective-permute-done.17.own_ref = bf16[2,128,768]{2,1,0:T(8,128)(2,1)S(1)} collective-permute-done((bf16[2,128,768]{2,1,0:T(8,128)(2,1)S(1)}, bf16[2,128,768]{2,1,0:T(8,128)(2,1)S(1)}, u32[]{:S(2)}, u32[]{:S(2)}) %collective-permute-start.17) | collective-permute-done | bytes 393248 | tf_op jit(solution)/shard_map/ppermute | solution.py:88
  50.5 0.4 collective-permute-start.13
  50.9 0.6 shard_map.64.refs_8_
  51.5 2.6 %collective-permute-start.19 = (bf16[2,128,1536]{2,1,0:T(8,128)(2,1)S(1)}, bf16[2,128,1536]{2,1,0:T(8,128)(2,1)S(1)}, u32[]{:S(2)}, u32[]{:S(2)}) collective-permute-start(bf16[2,128,1536]{2,1,0:T(8,128)(2,1)S(1)} %shard_map.65.refs_0_), channel_id=1, source_target_pairs={{0,2},{2,0},{4,6},{6,4},{8,10},{10,8},{12,14},{14,12},{16,18},{18,... | collective-permute-start | bytes 2359304 | tf_op jit(solution)/shard_map/ppermute | solution.py:74
  54.2 4.2 %shard_map.63.refs_7_ = bf16[2,512,1536]{2,1,0:T(8,128)(2,1)S(1)} custom-call(s32[4]{0:T(128)S(1)} %pad_add_fusion.sc, bf16[2,512,512]{2,1,0:T(8,128)(2,1)S(1)} %shard_map.59.w_ref, bf16[2,256,512]{2,1,0:T(8,128)(2,1)S(1)} %get-tuple-element.36.own_ref.end_ref, bf16[2,256,512]{2,1,0:T(8,128)(2,1)S(1)} %collective-permute-done.sib_ref.endsib_ref, ...), custom_call_target="tpu_custom_call" | custom-call | tf_op jit(solution)/shard_map/pallas_call | solution.py:43
  58.4 0.9 %collective-permute-done.18.x_ref = bf16[2,128,768]{2,1,0:T(8,128)(2,1)S(1)} collective-permute-done((bf16[2,128,768]{2,1,0:T(8,128)(2,1)S(1)}, bf16[2,128,768]{2,1,0:T(8,128)(2,1)S(1)}, u32[]{:S(2)}, u32[]{:S(2)}) %collective-permute-start.18) | collective-permute-done | bytes 393248 | tf_op jit(solution)/shard_map/ppermute | solution.py:74
  59.2 0.6 shard_map.66.refs_1_
  59.8 2.9 %collective-permute-start.20 = (bf16[2,128,1536]{2,1,0:T(8,128)(2,1)S(1)}, bf16[2,128,1536]{2,1,0:T(8,128)(2,1)S(1)}, u32[]{:S(2)}, u32[]{:S(2)}) collective-permute-start(bf16[2,128,1536]{2,1,0:T(8,128)(2,1)S(1)} %shard_map.66.refs_1_), channel_id=1, source_target_pairs={{0,2},{2,0},{4,6},{6,4},{8,10},{10,8},{12,14},{14,12},{16,18},{18,... | collective-permute-start | bytes 2359304 | tf_op jit(solution)/shard_map/ppermute | solution.py:74
  62.7 2.1 %collective-permute-start.14 = (bf16[2,128,1024]{2,1,0:T(8,128)(2,1)S(1)}, bf16[2,128,1024]{2,1,0:T(8,128)(2,1)S(1)}, u32[]{:S(2)}, u32[]{:S(2)}) collective-permute-start(bf16[2,128,1024]{2,1,0:T(8,128)(2,1)S(1)} %collective-permute-done.13.refs_4_), channel_id=1, source_target_pairs={{0,2},{2,0},{4,6},{6,4},{8,10},{10,8},{12,14},{14,12},{16,18},{18,... | collective-permute-start | bytes 1572872 | tf_op jit(solution)/shard_map/ppermute | solution.py:74
  64.8 0.7 %shard_map.67.refs_9_ = bf16[2,2,256,1536]{3,2,1,0:T(8,128)(2,1)S(1)} custom-call(s32[4]{0:T(128)S(1)} %pad_add_fusion.sc, bf16[2,128,1536]{2,1,0:T(8,128)(2,1)S(1)} %shard_map.65.refs_0_, bf16[2,128,1536]{2,1,0:T(8,128)(2,1)S(1)} %shard_map.66.refs_1_, bf16[2,128,1536]{2,1,0:T(8,128)(2,1)S(1)} %collective-permute-done.19.refs_2_, ...), custom_call_target="tpu_custom_call" | custom-call | tf_op jit(solution)/shard_map/pallas_call | solution.py:43
  65.6 0.8 %collective-permute-done.14.refs_5_ = bf16[2,128,1024]{2,1,0:T(8,128)(2,1)S(1)} collective-permute-done((bf16[2,128,1024]{2,1,0:T(8,128)(2,1)S(1)}, bf16[2,128,1024]{2,1,0:T(8,128)(2,1)S(1)}, u32[]{:S(2)}, u32[]{:S(2)}) %collective-permute-start.14) | collective-permute-done | bytes 524320 | tf_op jit(solution)/shard_map/ppermute | solution.py:74
  66.4 5.8 %shard_map.68 = bf16[2,1,256,1536]{3,2,1,0:T(8,128)(2,1)} custom-call(s32[4]{0:T(128)S(1)} %pad_add_fusion.sc, bf16[2,256,1536]{2,1,0:T(8,128)(2,1)S(1)} %get-tuple-element.41.refs_0_, bf16[2,256,1536]{2,1,0:T(8,128)(2,1)S(1)} %get-tuple-element.47.refs_1_, bf16[2,128,1024]{2,1,0:T(8,128)(2,1)S(1)} %collective-permute-done.6.rest_2_.refs_2_, ...), custom_call_target="tpu_custom_call" | custom-call | tf_op jit(solution)/shard_map/pallas_call | solution.py:43
  (22 shorter events, 0.3 us)
Async XLA Ops:
  0.1 2.3 %copy-start = (bf16[2,1,1,3,256,1536]{5,4,3,2,1,0:T(8,128)(2,1)S(1)}, bf16[2,1,1,3,256,1536]{5,4,3,2,1,0:T(8,128)(2,1)}, u32[]{:S(2)}) copy-start(bf16[2,1,1,3,256,1536]{5,4,3,2,1,0:T(8,128)(2,1)} %param.5) | copy-start | bytes 14155780
  4.0 1.1 %copy-start.1 = (bf16[2,256,1536]{2,1,0:T(8,128)(2,1)}, bf16[2,256,1536]{2,1,0:T(8,128)(2,1)S(1)}, u32[]{:S(2)}) copy-start(bf16[2,256,1536]{2,1,0:T(8,128)(2,1)S(1)} %get-tuple-element.39.end_ref) | copy-start | bytes 4718596
  5.2 3.1 %collective-permute-start = (bf16[2,256,512]{2,1,0:T(8,128)(2,1)S(1)}, bf16[2,256,512]{2,1,0:T(8,128)(2,1)S(1)}, u32[]{:S(2)}, u32[]{:S(2)}) collective-permute-start(bf16[2,256,512]{2,1,0:T(8,128)(2,1)S(1)} %get-tuple-element.36.own_ref.end_ref), channel_id=1, source_target_pairs={{0,2},{2,0},{4,6},{6,4},{8,10},{10,8},{12,14},{14,12},{16,18},{18,... | collective-permute-start | bytes 1572872 | tf_op jit(solution)/shard_map/ppermute | solution.py:74
  5.2 3.6 %collective-permute-start.1 = (bf16[2,256,512]{2,1,0:T(8,128)(2,1)}, bf16[2,256,512]{2,1,0:T(8,128)(2,1)}, u32[]{:S(2)}, u32[]{:S(2)}) collective-permute-start(bf16[2,256,512]{2,1,0:T(8,128)(2,1)} %get-tuple-element.40.own_ref), channel_id=1, source_target_pairs={{0,2},{2,0},{4,6},{6,4},{8,10},{10,8},{12,14},{14,12},{16,18},{18,... | collective-permute-start | bytes 1572872 | tf_op jit(solution)/shard_map/ppermute | solution.py:74
  6.9 10.1 %collective-permute-start.5 = (bf16[2,256,512]{2,1,0:T(8,128)(2,1)S(1)}, bf16[2,256,512]{2,1,0:T(8,128)(2,1)}, u32[]{:S(2)}, u32[]{:S(2)}) collective-permute-start(bf16[2,256,512]{2,1,0:T(8,128)(2,1)S(1)} %fusion.own_ref), channel_id=1, source_target_pairs={{0,2},{2,0},{4,6},{6,4},{8,10},{10,8},{12,14},{14,12},{16,18},{18,... | collective-permute-start | bytes 1572872 | tf_op jit(solution)/shard_map/ppermute | solution.py:74
  7.0 16.6 %collective-permute-start.3 = (bf16[2,256,1536]{2,1,0:T(8,128)(2,1)S(1)}, bf16[2,256,1536]{2,1,0:T(8,128)(2,1)}, u32[]{:S(2)}, u32[]{:S(2)}) collective-permute-start(bf16[2,256,1536]{2,1,0:T(8,128)(2,1)S(1)} %get-tuple-element.43.own_ref), channel_id=1, source_target_pairs={{0,2},{2,0},{4,6},{6,4},{8,10},{10,8},{12,14},{14,12},{16,18},{18,... | collective-permute-start | bytes 4718600 | tf_op jit(solution)/shard_map/ppermute | solution.py:74
  8.8 1.4 %copy-start.2 = (bf16[2,256,1536]{2,1,0:T(8,128)(2,1)S(1)}, bf16[2,256,1536]{2,1,0:T(8,128)(2,1)}, u32[]{:S(2)}) copy-start(bf16[2,256,1536]{2,1,0:T(8,128)(2,1)} %copy-done.1) | copy-start | bytes 4718596
  10.3 5.4 %copy-start.3 = (bf16[2,1,128,512]{3,2,1,0:T(8,128)(2,1)S(1)}, bf16[2,1,128,512]{3,2,1,0:T(8,128)(2,1)}, u32[]{:S(2)}) copy-start(bf16[2,1,128,512]{3,2,1,0:T(8,128)(2,1)} %param.7) | copy-start | bytes 786436
  12.8 9.4 %collective-permute-start.4 = (bf16[2,128,1024]{2,1,0:T(8,128)(2,1)S(1)}, bf16[2,128,1024]{2,1,0:T(8,128)(2,1)S(1)}, u32[]{:S(2)}, u32[]{:S(2)}) collective-permute-start(bf16[2,128,1024]{2,1,0:T(8,128)(2,1)S(1)} %get-tuple-element.50), channel_id=1, source_target_pairs={{0,2},{2,0},{4,6},{6,4},{8,10},{10,8},{12,14},{14,12},{16,18},{18,... | collective-permute-start | bytes 1572872 | tf_op jit(solution)/shard_map/ppermute | solution.py:74
  13.0 9.3 %collective-permute-start.2 = (bf16[2,128,512]{2,1,0:T(8,128)(2,1)S(1)}, bf16[2,128,512]{2,1,0:T(8,128)(2,1)S(1)}, u32[]{:S(2)}, u32[]{:S(2)}) collective-permute-start(bf16[2,128,512]{2,1,0:T(8,128)(2,1)S(1)} %get-tuple-element.37), channel_id=1, source_target_pairs={{0,1},{1,0},{2,3},{3,2},{4,5},{5,4},{6,7},{7,6},{8,9},{9,8},{10,11... | collective-permute-start | bytes 786440 | tf_op jit(solution)/shard_map/ppermute | solution.py:88
  15.7 13.8 %collective-permute-start.9 = (bf16[2,128,512]{2,1,0:T(8,128)(2,1)S(1)}, bf16[2,128,512]{2,1,0:T(8,128)(2,1)S(1)}, u32[]{:S(2)}, u32[]{:S(2)}) collective-permute-start(bf16[2,128,512]{2,1,0:T(8,128)(2,1)S(1)} %fusion.1), channel_id=1, source_target_pairs={{0,4},{2,6},{4,0},{6,2},{8,12},{10,14},{12,8},{14,10},{16,20},{18,... | collective-permute-start | bytes 786440 | tf_op jit(solution)/shard_map/ppermute | solution.py:74
  17.0 12.5 %collective-permute-start.8 = (bf16[2,128,512]{2,1,0:T(8,128)(2,1)S(1)}, bf16[2,128,512]{2,1,0:T(8,128)(2,1)S(1)}, u32[]{:S(2)}, u32[]{:S(2)}) collective-permute-start(bf16[2,128,512]{2,1,0:T(8,128)(2,1)S(1)} %get-tuple-element.55), channel_id=1, source_target_pairs={{0,1},{1,0},{2,3},{3,2},{4,5},{5,4},{6,7},{7,6},{8,9},{9,8},{10,11... | collective-permute-start | bytes 786440 | tf_op jit(solution)/shard_map/ppermute | solution.py:88
  27.4 13.4 %collective-permute-start.6 = (bf16[2,128,1024]{2,1,0:T(8,128)(2,1)S(1)}, bf16[2,128,1024]{2,1,0:T(8,128)(2,1)S(1)}, u32[]{:S(2)}, u32[]{:S(2)}) collective-permute-start(bf16[2,128,1024]{2,1,0:T(8,128)(2,1)S(1)} %get-tuple-element.53), channel_id=1, source_target_pairs={{0,1},{1,0},{2,3},{3,2},{4,5},{5,4},{6,7},{7,6},{8,9},{9,8},{10,11... | collective-permute-start | bytes 1572872 | tf_op jit(solution)/shard_map/ppermute | solution.py:88
  28.7 2.0 %collective-permute-start.7 = (bf16[2,128,512]{2,1,0:T(8,128)(2,1)S(1)}, bf16[2,128,512]{2,1,0:T(8,128)(2,1)S(1)}, u32[]{:S(2)}, u32[]{:S(2)}) collective-permute-start(bf16[2,128,512]{2,1,0:T(8,128)(2,1)S(1)} %collective-permute-done.2.rest_0_), channel_id=1, source_target_pairs={{0,2},{2,0},{4,6},{6,4},{8,10},{10,8},{12,14},{14,12},{16,18},{18,... | collective-permute-start | bytes 786440 | tf_op jit(solution)/shard_map/ppermute | solution.py:74
  29.5 1.5 %collective-permute-start.10 = (bf16[2,128,512]{2,1,0:T(8,128)(2,1)S(1)}, bf16[2,128,512]{2,1,0:T(8,128)(2,1)S(1)}, u32[]{:S(2)}, u32[]{:S(2)}) collective-permute-start(bf16[2,128,512]{2,1,0:T(8,128)(2,1)S(1)} %collective-permute-done.8.rest_2_.rest_4_), channel_id=1, source_target_pairs={{0,2},{2,0},{4,6},{6,4},{8,10},{10,8},{12,14},{14,12},{16,18},{18,... | collective-permute-start | bytes 786440 | tf_op jit(solution)/shard_map/ppermute | solution.py:74
  32.1 5.6 %collective-permute-start.11 = (bf16[2,128,256]{2,1,0:T(8,128)(2,1)S(1)}, bf16[2,128,256]{2,1,0:T(8,128)(2,1)S(1)}, u32[]{:S(2)}, u32[]{:S(2)}) collective-permute-start(bf16[2,128,256]{2,1,0:T(8,128)(2,1)S(1)} %get-tuple-element.60), channel_id=1, source_target_pairs={{0,4},{2,6},{4,0},{6,2},{8,12},{10,14},{12,8},{14,10},{16,20},{18,... | collective-permute-start | bytes 393224 | tf_op jit(solution)/shard_map/ppermute | solution.py:74
  38.3 9.8 %collective-permute-start.16 = (bf16[2,128,768]{2,1,0:T(8,128)(2,1)S(1)}, bf16[2,128,768]{2,1,0:T(8,128)(2,1)S(1)}, u32[]{:S(2)}, u32[]{:S(2)}) collective-permute-start(bf16[2,128,768]{2,1,0:T(8,128)(2,1)S(1)} %shard_map.62.own_ref), channel_id=1, source_target_pairs={{0,4},{2,6},{4,0},{6,2},{8,12},{10,14},{12,8},{14,10},{16,20},{18,... | collective-permute-start | bytes 1179656 | tf_op jit(solution)/shard_map/ppermute | solution.py:74
  40.8 9.7 %collective-permute-start.17 = (bf16[2,128,768]{2,1,0:T(8,128)(2,1)S(1)}, bf16[2,128,768]{2,1,0:T(8,128)(2,1)S(1)}, u32[]{:S(2)}, u32[]{:S(2)}) collective-permute-start(bf16[2,128,768]{2,1,0:T(8,128)(2,1)S(1)} %shard_map.62.own_ref), channel_id=1, source_target_pairs={{0,1},{1,0},{2,3},{3,2},{4,5},{5,4},{6,7},{7,6},{8,9},{9,8},{10,11... | collective-permute-start | bytes 1179656 | tf_op jit(solution)/shard_map/ppermute | solution.py:88
  41.8 9.1 %collective-permute-start.15 = (bf16[2,2,128,512]{3,2,1,0:T(8,128)(2,1)S(1)}, bf16[2,2,128,512]{3,2,1,0:T(8,128)(2,1)S(1)}, u32[]{:S(2)}, u32[]{:S(2)}) collective-permute-start(bf16[2,2,128,512]{3,2,1,0:T(8,128)(2,1)S(1)} %pad_maximum_fusion.own_ref), channel_id=1, source_target_pairs={{0,2},{2,0},{4,6},{6,4},{8,10},{10,8},{12,14},{14,12},{16,18},{18,... | collective-permute-start | bytes 1572872 | tf_op jit(solution)/shard_map/ppermute | solution.py:74
  43.6 10.6 %collective-permute-start.12 = (bf16[2,128,1024]{2,1,0:T(8,128)(2,1)S(1)}, bf16[2,128,1024]{2,1,0:T(8,128)(2,1)S(1)}, u32[]{:S(2)}, u32[]{:S(2)}) collective-permute-start(bf16[2,128,1024]{2,1,0:T(8,128)(2,1)S(1)} %collective-permute-done.6.rest_2_.refs_2_), channel_id=1, source_target_pairs={{0,2},{2,0},{4,6},{6,4},{8,10},{10,8},{12,14},{14,12},{16,18},{18,... | collective-permute-start | bytes 1572872 | tf_op jit(solution)/shard_map/ppermute | solution.py:74
  50.5 8.7 %collective-permute-start.18 = (bf16[2,128,768]{2,1,0:T(8,128)(2,1)S(1)}, bf16[2,128,768]{2,1,0:T(8,128)(2,1)S(1)}, u32[]{:S(2)}, u32[]{:S(2)}) collective-permute-start(bf16[2,128,768]{2,1,0:T(8,128)(2,1)S(1)} %collective-permute-done.17.own_ref), channel_id=1, source_target_pairs={{0,4},{2,6},{4,0},{6,2},{8,12},{10,14},{12,8},{14,10},{16,20},{18,... | collective-permute-start | bytes 1179656 | tf_op jit(solution)/shard_map/ppermute | solution.py:74
  50.5 12.2 %collective-permute-start.13 = (bf16[2,128,1024]{2,1,0:T(8,128)(2,1)S(1)}, bf16[2,128,1024]{2,1,0:T(8,128)(2,1)S(1)}, u32[]{:S(2)}, u32[]{:S(2)}) collective-permute-start(bf16[2,128,1024]{2,1,0:T(8,128)(2,1)S(1)} %get-tuple-element.63), channel_id=1, source_target_pairs={{0,1},{1,0},{2,3},{3,2},{4,5},{5,4},{6,7},{7,6},{8,9},{9,8},{10,11... | collective-permute-start | bytes 1572872 | tf_op jit(solution)/shard_map/ppermute | solution.py:88
  51.5 13.3 %collective-permute-start.19 = (bf16[2,128,1536]{2,1,0:T(8,128)(2,1)S(1)}, bf16[2,128,1536]{2,1,0:T(8,128)(2,1)S(1)}, u32[]{:S(2)}, u32[]{:S(2)}) collective-permute-start(bf16[2,128,1536]{2,1,0:T(8,128)(2,1)S(1)} %shard_map.65.refs_0_), channel_id=1, source_target_pairs={{0,2},{2,0},{4,6},{6,4},{8,10},{10,8},{12,14},{14,12},{16,18},{18,... | collective-permute-start | bytes 2359304 | tf_op jit(solution)/shard_map/ppermute | solution.py:74
  59.8 5.0 %collective-permute-start.20 = (bf16[2,128,1536]{2,1,0:T(8,128)(2,1)S(1)}, bf16[2,128,1536]{2,1,0:T(8,128)(2,1)S(1)}, u32[]{:S(2)}, u32[]{:S(2)}) collective-permute-start(bf16[2,128,1536]{2,1,0:T(8,128)(2,1)S(1)} %shard_map.66.refs_1_), channel_id=1, source_target_pairs={{0,2},{2,0},{4,6},{6,4},{8,10},{10,8},{12,14},{14,12},{16,18},{18,... | collective-permute-start | bytes 2359304 | tf_op jit(solution)/shard_map/ppermute | solution.py:74
  62.7 3.7 %collective-permute-start.14 = (bf16[2,128,1024]{2,1,0:T(8,128)(2,1)S(1)}, bf16[2,128,1024]{2,1,0:T(8,128)(2,1)S(1)}, u32[]{:S(2)}, u32[]{:S(2)}) collective-permute-start(bf16[2,128,1024]{2,1,0:T(8,128)(2,1)S(1)} %collective-permute-done.13.refs_4_), channel_id=1, source_target_pairs={{0,2},{2,0},{4,6},{6,4},{8,10},{10,8},{12,14},{14,12},{16,18},{18,... | collective-permute-start | bytes 1572872 | tf_op jit(solution)/shard_map/ppermute | solution.py:74

commit v8 on v7

v8 whole, which is shorter than its diff:
```python
import jax
import jax.numpy as jnp
from jax import lax
from jax.experimental import pallas as pl
from jax.experimental.pallas import tpu as pltpu
from jax.sharding import PartitionSpec as P

BF16 = jnp.bfloat16
F32 = jnp.float32
VMEM_BYTES = 16 * 1024 * 1024
SLOTS_COST = 20_000_000_000
JOIN_COST = 300_000_000
MERGE_COST = 2_000_000_000
KEEP_COST = 6_000_000_000
SLOT_ROWS_COST = 2_000_000_000


def dot(first, second):
    return jnp.dot(first, second, preferred_element_type=F32)


def stacked(real, imag):
    return jnp.concatenate(
        [jnp.concatenate([real, -imag], axis=1), jnp.concatenate([imag, real], axis=1)], axis=0
    )


def flat(array):
    return array.reshape(array.shape[0] * array.shape[1], array.shape[2])


def column_picker(index, offset, count):
    rows = lax.broadcasted_iota(jnp.int32, (count, index.shape[1]), 0) + offset
    return jnp.where(rows == index, 1.0, 0.0).astype(BF16)


def row_picker(index, offset, count):
    cols = lax.broadcasted_iota(jnp.int32, (index.shape[0], count), 1) + offset
    return jnp.where(cols == index, 1.0, 0.0).astype(BF16)


def call(kernel, scalars, inputs, out_shapes, specs=None, out_specs=None, scratch=(), cost=0, aliases=None):
    in_vmem = pl.BlockSpec(memory_space=pltpu.VMEM)
    specs = specs or [in_vmem] * len(inputs)
    out_specs = out_specs or [in_vmem] * len(out_shapes)
    return pl.pallas_call(
        kernel,
        in_specs=[pl.BlockSpec(memory_space=pltpu.SMEM)] + specs,
        out_specs=out_specs,
        out_shape=out_shapes,
        scratch_shapes=list(scratch),
        input_output_aliases=aliases or {},
        compiler_params=pltpu.CompilerParams(vmem_limit_bytes=VMEM_BYTES),
        cost_estimate=pl.CostEstimate(flops=cost, bytes_accessed=0, transcendentals=0),
    )(scalars, *inputs)


def after(array, *others):
    return lax.optimization_barrier((array, *others))[0]


def on_device(leaf_maps, w_first, w_second, skel_first, skel_second):
    box = lax.axis_index("box")
    face = lax.axis_index("face")
    n_box, n_face = lax.axis_size("box"), lax.axis_size("face")
    nf = n_face - 1
    fr = leaf_maps.shape[4]
    hr = fr // 2
    k = leaf_maps.shape[5] // 3
    half = k // 2
    leaf = leaf_maps[:, 0, 0]
    par = box % 2
    par2 = box // 2 % 2
    scalars = jnp.stack([par, par2, face, box % 4]).astype(jnp.int32)
    sds = jax.ShapeDtypeStruct

    def box_permute(array, mask):
        return lax.ppermute(array, "box", [(b, b ^ mask) for b in range(n_box)])

    def keeper(b):
        return (b & 1) != (b >> 1 & 1)

    def giver(b):
        return not keeper(b)

    def face_permute(array, step, senders=None):
        pairs = [
            (b * n_face + f, b * n_face + (f + n_face - step) % n_face)
            for b in range(n_box) if senders is None or senders(b)
            for f in range(n_face)
        ]
        return lax.ppermute(array, ("box", "face"), pairs)

    def over_face(array, senders=None):
        return [face_permute(array, s, senders) for s in range(1, n_face)]

    skel_one = lax.dynamic_index_in_dim(skel_first[0], box // 2, 0, keepdims=True)
    skel_two = lax.dynamic_index_in_dim(skel_second[0], box // 4, 0, keepdims=True)

    in_hbm = pl.BlockSpec(memory_space=pltpu.HBM)

    def parts_kernel(sc, leaf_ref, end_out, side_out):
        p = sc[0]
        end_out[...] = leaf_ref[:, 1 - p, :, pl.ds(pl.multiple_of(p * k, k), k)]
        side_out[...] = leaf_ref[:, 1 - p, :, 2 * k :]

    end_own, sides_raw = call(parts_kernel, scalars, [leaf], [sds((2, fr, k), BF16)] * 2)
    end_sib = box_permute(end_own, 1)
    sides_sib = box_permute(sides_raw, 1)

    def slots_kernel(sc, leaf_ref, skel_ref, skel2_ref, comp_out, col_out, keep_out, send_out, end_out, rows_out):
        p, q = sc[0], sc[1]
        rows = lax.broadcasted_iota(jnp.int32, (k, k), 0)
        cols = lax.broadcasted_iota(jnp.int32, (k, k), 1)
        skel = jnp.broadcast_to(skel_ref[...].astype(F32), (k, k))
        column = jnp.sum(jnp.where(rows == cols, skel, 0.0), axis=1, keepdims=True)
        col_out[...] = column.astype(jnp.int32)
        place = skel2_ref[...] - q * k
        taken = jnp.where(rows == place, jnp.broadcast_to(column, (k, k)), 0.0)
        comp = jnp.sum(taken, axis=0, keepdims=True).astype(jnp.int32)
        mine = jnp.logical_and(place >= 0, place < k)
        comp = jnp.where(mine, comp, -1)
        comp_out[...] = comp
        rows_out[...] = leaf_ref[:, 2]
        pick_own = column_picker(comp, p * k, k)
        for t in range(2):
            end_out[t, :, : 2 * k] = leaf_ref[t, p, :, : 2 * k]
            end_out[t, :, 2 * k :] = dot(leaf_ref[t, p, :, 2 * k :], pick_own).astype(BF16)
        couple = pl.ds(pl.multiple_of((1 - p) * k, k), k)
        for ref, h in ((keep_out, p), (send_out, 1 - p)):
            take = pl.ds(pl.multiple_of(h * hr, hr), hr)
            ref[:, :, :k] = end_out[:, take, couple]
            ref[:, :, k:] = end_out[:, take, 2 * k :]

    comp, skel_col, v_keep, v_send, end_kept, s_rows = call(
        slots_kernel, scalars, [leaf, skel_one, skel_two],
        [sds((1, k), jnp.int32), sds((k, 1), jnp.int32), sds((2, hr, 2 * k), BF16), sds((2, hr, 2 * k), BF16),
         sds((2, fr, 3 * k), BF16), sds((2, fr, 3 * k), BF16)],
    )
    s_sib = box_permute(s_rows, 1)
    v_recv = box_permute(v_send, 1)

    def split_kernel(sc, own_ref, sib_ref, first_out, rest_out):
        p, q = sc[0], sc[1]
        rows = pl.ds(pl.multiple_of(p * hr, hr), hr)
        own, sib = own_ref[:, rows, :], sib_ref[:, rows, :]
        first_out[...] = jnp.where(p == q, own, sib)
        rest_out[...] = jnp.where(p == q, sib, own)

    first_send, rest_send = call(split_kernel, after(scalars, comp), [end_own, end_sib], [sds((2, hr, k), BF16)] * 2)
    first_far = over_face(first_send)
    first_fwd = [box_permute(a, 1) for a in first_far]

    def merge_kernel(sc, *refs):
        p = sc[0]
        mine = pl.ds(pl.multiple_of(p * hr, hr), hr)
        other = pl.ds(pl.multiple_of((1 - p) * hr, hr), hr)
        for s in range(nf):
            refs[2 * nf + s][:, mine, :] = refs[s][...]
            refs[2 * nf + s][:, other, :] = refs[nf + s][...]

    first_rows = call(
        merge_kernel, scalars, [*first_far, *first_fwd], [sds((2, fr, k), BF16)] * nf, cost=MERGE_COST
    )

    def side_kernel(sc, own_ref, sib_ref, comp_ref, side_out, half_out):
        p = sc[0]
        pick_own = column_picker(comp_ref[...], p * k, k)
        pick_sib = column_picker(comp_ref[...], (1 - p) * k, k)
        side = dot(flat(own_ref[...]), pick_own) + dot(flat(sib_ref[...]), pick_sib)
        side_out[...] = side.astype(BF16).reshape(2, fr, k)
        half_out[...] = side_out[:, pl.ds(pl.multiple_of(p * hr, hr), hr), :]

    side, side_half = call(
        side_kernel, after(scalars, first_send), [sides_raw, sides_sib, comp],
        [sds((2, fr, k), BF16), sds((2, hr, k), BF16)], cost=SLOTS_COST,
    )
    side_far = over_face(side_half)

    w_one = jnp.roll(w_first[:, 0], -face * fr, axis=2)
    w_one_sib = box_permute(w_one, 1)
    w_two = jnp.roll(w_second[:, 0], -face * fr, axis=2)
    w_two_x = box_permute(after(w_two, first_send), 2)

    def weight_one_kernel(sc, own_ref, sib_ref, out_ref):
        p = sc[0]
        out_ref[:, pl.ds(pl.multiple_of(p * half, half), half), :] = own_ref[...]
        out_ref[:, pl.ds(pl.multiple_of((1 - p) * half, half), half), :] = sib_ref[...]

    (weight_one,) = call(weight_one_kernel, scalars, [w_one, w_one_sib], [sds((2, k, k), BF16)])


    def rows_kernel(sc, own_ref, sib_ref, comp_ref, col_ref, rest_ref, kept_out, *outs):
        p, q, f = sc[0], sc[1], sc[2]
        pick_own = column_picker(comp_ref[...], p * k, k)
        pick_sib = column_picker(comp_ref[...], (1 - p) * k, k)

        def pick(slots, write):
            take_own = row_picker(slots, p * k + f * fr, fr)
            take_sib = row_picker(slots, (1 - p) * k + f * fr, fr)
            for t in range(2):
                for c in range(3):
                    cols = slice(c * k, (c + 1) * k)
                    own, sib = own_ref[t, :, cols], sib_ref[t, :, cols]
                    if c == 2:
                        own, sib = [dot(a, b).astype(BF16) for a, b in ((own, pick_own), (sib, pick_sib))]
                    write(t, c, (dot(take_own, own) + dot(take_sib, sib)).astype(BF16))

        for s in range(nf):
            outs[s][:, :, :k] = rest_ref[...]

        def write_far(s, t, c, picked):
            if c == 0:
                outs[s][t, :, k:] = picked
            else:
                outs[c * nf + s][t] = picked

        def col_half(s):
            start = (f + n_face - s - 1) % n_face * fr + p * hr
            return col_ref[pl.ds(pl.multiple_of(start, hr), hr), :]

        @pl.when(p == q)
        def _():
            far = jnp.concatenate([col_half(s) for s in range(nf)], axis=0)

            def write(t, c, picked):
                for s in range(nf):
                    write_far(s, t, c, picked[s * hr : (s + 1) * hr])

            pick(far, write)

        @pl.when(p != q)
        def _():
            far = jnp.concatenate([col_half(s) for s in range(nf)], axis=0)
            slots = jnp.concatenate([col_ref[pl.ds(pl.multiple_of(f * fr, fr), fr), :], far], axis=0)

            def write(t, c, picked):
                kept_out[t, :, c * k : (c + 1) * k] = picked[:fr]
                for s in range(nf):
                    write_far(s, t, c, picked[fr + s * hr : fr + (s + 1) * hr])

            pick(slots, write)

    kept, *kept_out = call(
        rows_kernel, scalars, [s_rows, s_sib, comp, skel_col, rest_send],
        [sds((2, fr, 3 * k), BF16)] + [sds((2, hr, 2 * k), BF16)] * nf + [sds((2, hr, k), BF16)] * (2 * nf),
    )

    def piece(hidden, start, count):
        return stacked(hidden[0][:, start : start + count], hidden[1][:, start : start + count])

    def iface_kernel(sc, keep_ref, recv_ref, w_ref, end_ref, endsib_ref, side_ref,
                     acc_out, hid_out, rows):
        p, q = sc[0], sc[1]

        @pl.when(p == q)
        def _():
            rows[...] = recv_ref[...]

        @pl.when(p != q)
        def _():
            rows[...] = keep_ref[...]

        both = dot(stacked(rows[0, :, :k], rows[1, :, :k]), flat(w_ref[...])).astype(BF16)
        hidden = both[:hr], both[hr:]
        hid_out[0] = hidden[0]
        hid_out[1] = hidden[1]
        left = piece(hidden, 0, fr)
        is_end = p == q
        ends = jnp.where(is_end, end_ref[...], endsib_ref[...])
        acc_out[:, :, :k] = -dot(left, flat(ends)).reshape(2, hr, k)
        acc_out[:, :, k:] = rows[:, :, k:].astype(F32) - dot(left, flat(side_ref[...])).reshape(2, hr, k)

    v_acc, v_hid = call(
        iface_kernel, scalars, [v_keep, v_recv, weight_one, end_own, end_sib, side],
        [sds((2, hr, 2 * k), F32), sds((2, hr, k), BF16)],
        scratch=[pltpu.VMEM((2, hr, 2 * k), BF16)],
    )
    w_two_pair = jnp.stack([w_two, w_two_x])
    w_two_sib = box_permute(w_two_pair, 1)

    def weight_two_kernel(sc, own_ref, sib_ref, out_ref):
        r = sc[3]
        blk = k // 4
        for i, (ref, part) in enumerate(((own_ref, 0), (own_ref, 1), (sib_ref, 0), (sib_ref, 1))):
            place = r ^ (part * 2) ^ (i // 2)
            out_ref[:, pl.ds(pl.multiple_of(place * blk, blk), blk), :] = ref[part]

    (weight_two,) = call(weight_two_kernel, scalars, [w_two_pair, w_two_sib], [sds((2, k, k), BF16)])

    side_fwd = [box_permute(after(a, kept, w_two_x, weight_one), 1) for a in side_far]
    mixed_far = [face_permute(a, i + 1) for i, a in enumerate(kept_out[:nf])]

    def iface_far_kernel(sc, acc_ref, hid_ref, *rest):
        refs = [rest[i * nf : (i + 1) * nf] for i in range(3)]
        end_out, keep_out, send_out, rows = rest[3 * nf :]
        p, q = sc[0], sc[1]
        mine = pl.ds(pl.multiple_of(p * hr, hr), hr)
        other = pl.ds(pl.multiple_of((1 - p) * hr, hr), hr)
        hidden = [hid_ref[0], hid_ref[1]]
        total = acc_ref[...]
        for s in range(nf):
            rows[:, mine, :] = refs[1][s][...]
            rows[:, other, :] = refs[2][s][...]
            left = piece(hidden, (s + 1) * fr, fr)
            far = jnp.concatenate([dot(left, flat(refs[0][s][...])), dot(left, flat(rows[...]))], axis=1)
            total = total - far.reshape(2, hr, 2 * k)
        total = total.astype(BF16)
        end_out[...] = total[:, :, :k]
        low, high = total[:, :, k : k + half], total[:, :, k + half :]
        keep_out[...] = jnp.where(q == 0, low, high)
        send_out[...] = jnp.where(q == 0, high, low)

    two_end, side_keep, side_send = call(
        iface_far_kernel, scalars, [v_acc, v_hid, *first_rows, *side_far, *side_fwd],
        [sds((2, hr, k), BF16)] + [sds((2, hr, half), BF16)] * 2, scratch=[pltpu.VMEM((2, fr, k), BF16)],
    )

    side_x = box_permute(side_send, 2)

    def pack_kernel(sc, end_ref, keep_ref, x_ref, out_ref):
        out_ref[:, :, :k] = end_ref[...]
        out_ref[:, :, k:] = keep_ref[...] + x_ref[...]

    (two_own,) = call(
        pack_kernel, scalars, [two_end, side_keep, side_x], [sds((2, hr, k + half), BF16)]
    )
    two_x = box_permute(two_own, 2)
    two_y = over_face(after(two_own, *mixed_far))
    mixed_fwd = [box_permute(after(a, two_own), 1) for a in mixed_far]

    def weighted(w_ref, rows, out_ref):
        left = jnp.concatenate([piece((w_ref[0], w_ref[1]), s * fr, fr) for s in range(n_face)], axis=1)
        for c in range(3):
            cols = slice(c * k, (c + 1) * k)
            right = rows[:, :, :, cols].reshape(n_face * 2 * fr, k)
            out_ref[:, :, cols] = dot(left, right).astype(BF16).reshape(2, k, k)

    def weighted_one_kernel(sc, w_ref, own_ref, sib_ref, side_ref, *rest):
        refs = [rest[i * nf : (i + 1) * nf] for i in range(5)]
        out_ref, rows = rest[5 * nf :]
        p, q = sc[0], sc[1]
        first_cols = pl.ds(pl.multiple_of(q * k, k), k)
        rest_cols = pl.ds(pl.multiple_of((1 - q) * k, k), k)
        own_cols = pl.ds(pl.multiple_of(p * k, k), k)
        sib_cols = pl.ds(pl.multiple_of((1 - p) * k, k), k)
        mine = pl.ds(pl.multiple_of(p * hr, hr), hr)
        other = pl.ds(pl.multiple_of((1 - p) * hr, hr), hr)
        rows[0, :, :, own_cols] = own_ref[...]
        rows[0, :, :, sib_cols] = sib_ref[...]
        rows[0, :, :, 2 * k :] = side_ref[...]
        for s in range(nf):
            rows[s + 1, :, :, first_cols] = refs[0][s][...]
            for h, take in enumerate((mine, other)):
                rows[s + 1, :, take, rest_cols] = refs[1 + h][s][:, :, :k]
                rows[s + 1, :, take, 2 * k :] = refs[3 + h][s][...]
        weighted(w_ref, rows, out_ref)

    (solved_one,) = call(
        weighted_one_kernel, scalars,
        [weight_one, end_own, end_sib, side, *first_rows, *mixed_far, *mixed_fwd, *side_far, *side_fwd],
        [sds((2, k, 3 * k), BF16)], scratch=[pltpu.VMEM((n_face, 2, fr, 3 * k), BF16)],
    )

    def join_kernel(sc, own_ref, x_ref, out_ref):
        q = sc[1]
        for ref, which in ((own_ref, q), (x_ref, 1 - q)):
            out_ref[:, :, pl.ds(pl.multiple_of(which * k, k), k)] = ref[:, :, :k]
            out_ref[:, :, pl.ds(pl.multiple_of(2 * k + which * half, half), half)] = ref[:, :, k:]

    two_shape = [sds((2, hr, 3 * k), BF16)]
    two_rows = call(join_kernel, after(scalars, solved_one), [two_own, two_x], two_shape, cost=JOIN_COST)
    two_xy = [box_permute(after(a, *two_rows), 2) for a in two_y]
    for own, other in zip(two_y, two_xy):
        two_rows += call(join_kernel, after(scalars, weight_two), [own, other], two_shape)
    two_sib = [box_permute(a, 1) for a in two_rows]

    ends_far = [face_permute(after(a, two_own), i + 1) for i, a in enumerate(kept_out[nf : 2 * nf])]
    ends_fwd = [box_permute(a, 1) for a in ends_far]
    slots_far = [face_permute(after(a, two_own), i + 1) for i, a in enumerate(kept_out[2 * nf :])]

    def whole_rows(sc, out_ref, cols, end_ref, kept_ref, far, fwd, source, place=slice(None)):
        p, q = sc[0], sc[1]

        @pl.when(p == q)
        def _():
            out_ref[:, :, place] = end_ref[:, :, cols]

        @pl.when(p != q)
        def _():
            for h, parts in enumerate((far, fwd)):
                take = pl.ds(pl.multiple_of((p ^ h) * hr, hr), hr)
                total = kept_ref[:, take, cols]
                for part in parts:
                    total = total + part[:, :, source]
                out_ref[:, take, place] = total

    def level_one_kernel(sc, end_ref, kept_ref, *refs):
        parts = [refs[i * nf : (i + 1) * nf] for i in range(4)]
        col_ref, one_ref, w_ref, hid_out, first_out, sub_out, zs = refs[4 * nf :]
        p, q, f = sc[0], sc[1], sc[2]
        whole_rows(sc, zs, slice(0, k), end_ref, kept_ref, parts[0], parts[1], slice(k, 2 * k), slice(0, k))
        whole_rows(sc, zs, slice(k, 2 * k), end_ref, kept_ref, parts[2], parts[3], slice(0, k), slice(k, 2 * k))
        slots = col_ref[pl.ds(pl.multiple_of(f * fr, fr), fr), :]
        right = jnp.where(slots >= k, 1, 0)
        right = jnp.where(p == q, p, right) > 0
        lefts = [zs[t, :, :k] for t in range(2)]
        rights = [zs[t, :, k:] for t in range(2)]
        left = stacked(*[jnp.where(right, a, b) for a, b in zip(lefts, rights)])
        nothing = jnp.zeros((fr, k), BF16)
        start = [
            jnp.concatenate([jnp.where(right, nothing, a) for a in lefts], axis=0),
            jnp.concatenate([jnp.where(right, a, nothing) for a in rights], axis=0),
        ]
        merged = [
            (start[c].astype(F32) - dot(left, flat(one_ref[:, :, c * k : (c + 1) * k]))).astype(BF16)
            for c in range(2)
        ]
        sub_out[...] = dot(left, flat(one_ref[:, :, 2 * k :]))
        is_left = q == 0
        first_out[...] = jnp.where(is_left, merged[0], merged[1])
        couple = jnp.where(is_left, merged[1], merged[0])
        second = dot(stacked(couple[:fr], couple[fr:]), flat(w_ref[...])).astype(BF16)
        for s in range(n_face):
            hid_out[s] = piece((second[:fr], second[fr:]), s * fr, fr)

    hid_two, first_two, sub_one = call(
        level_one_kernel, scalars,
        [end_kept, kept, *mixed_far, *mixed_fwd, *ends_far, *ends_fwd, skel_col, solved_one, weight_two],
        [sds((n_face, 2 * fr, 2 * fr), BF16), sds((2 * fr, k), BF16), sds((2 * fr, k), F32)],
        scratch=[pltpu.VMEM((2, fr, 2 * k), BF16)], cost=KEEP_COST,
    )

    slots_fwd = [box_permute(after(a, hid_two), 1) for a in slots_far]

    def level_two_kernel(sc, hid_ref, first_ref, *refs):
        out_ref, sub_out, rows, stage, sems = refs[2 * n_face :]
        p, q = sc[0], sc[1]
        left = jnp.concatenate([hid_ref[s] for s in range(n_face)], axis=1)
        for s in range(n_face):
            rows[s, :, pl.ds(pl.multiple_of(p * hr, hr), hr), :] = refs[s][...]
            rows[s, :, pl.ds(pl.multiple_of((1 - p) * hr, hr), hr), :] = refs[n_face + s][...]
        copies = []
        for c in range(2):
            first = jnp.where(q == c, first_ref[...], jnp.zeros((2 * fr, k), BF16)).astype(F32)
            right = rows[:, :, :, c * k : (c + 1) * k].reshape(n_face * 2 * fr, k)
            stage[c] = (first - dot(left, right)).astype(BF16).reshape(2, fr, k)
            copies.append(pltpu.make_async_copy(
                stage.at[c], out_ref.at[:, 0, :, pl.ds(c * k, k)], sems.at[c]
            ))
            copies[-1].start()
        sub_out[...] = dot(left, rows[:, :, :, 2 * k :].reshape(n_face * 2 * fr, k))
        for copy in copies:
            copy.wait()

    out, sub_two = call(
        level_two_kernel, scalars, [hid_two, first_two, *two_rows, *two_sib],
        [sds((2, 1, fr, 3 * k), BF16), sds((2 * fr, k), F32)],
        out_specs=[in_hbm, pl.BlockSpec(memory_space=pltpu.VMEM)],
        scratch=[pltpu.VMEM((n_face, 2, fr, 3 * k), BF16), pltpu.VMEM((2, 2, fr, k), BF16),
                 pltpu.SemaphoreType.DMA((2,))],
    )

    def slot_rows_kernel(sc, end_ref, kept_ref, *refs):
        whole_rows(sc, refs[2 * nf], slice(2 * k, 3 * k), end_ref, kept_ref, refs[:nf], refs[nf : 2 * nf], slice(0, k))

    (slot_rows,) = call(
        slot_rows_kernel, scalars, [end_kept, kept, *slots_far, *slots_fwd], [sds((2, fr, k), BF16)], cost=SLOT_ROWS_COST
    )

    def finish_kernel(sc, rows_ref, one_ref, two_ref, _, out_ref, stage, sem):
        merged = (flat(rows_ref[...]).astype(F32) - one_ref[...]).astype(BF16)
        stage[...] = (merged.astype(F32) - two_ref[...]).astype(BF16).reshape(2, fr, k)
        copy = pltpu.make_async_copy(stage, out_ref.at[:, 0, :, pl.ds(2 * k, k)], sem.at[0])
        copy.start()
        copy.wait()

    (out,) = call(
        finish_kernel, scalars, [slot_rows, sub_one, sub_two, out], [sds((2, 1, fr, 3 * k), BF16)],
        specs=[pl.BlockSpec(memory_space=pltpu.VMEM)] * 3 + [in_hbm], out_specs=[in_hbm],
        scratch=[pltpu.VMEM((2, fr, k), BF16), pltpu.SemaphoreType.DMA((1,))], aliases={4: 0},
    )
    return out


def solution(mesh):
    return jax.shard_map(
        on_device,
        mesh=mesh,
        in_specs=(
            P(None, None, "box", None, "face", None),
            P(None, None, "box", None),
            P(None, None, "box", None),
            P(),
            P(),
        ),
        out_specs=P(None, None, ("box", "face"), None),
        check_vma=False,
    )
```

time: 73 us -> 77.6 us (1.063)
  starting transfers between devices: 21.6 us -> 17.2 us
  waiting for transfers between devices: 18 us -> 22.1 us
  Pallas kernels: 25.2 us -> 28.5 us
  other arithmetic: 1.56 us -> 2.51 us
  local copies, waits for them, and re-layouts: 5.63 us -> 6.57 us
    ppermute x16 -> x17, starting transfers between devices: 16.1 us -> 10.2 us  [box_permute(): return lax.ppermute(array, 'box', [(b, b ^ mask) for b in range(n_box)])]
    ppermute x5 -> x6, waiting for transfers between devices: 6.81 us -> 11.3 us  [face_permute(): return lax.ppermute(array, ('box', 'face'), pairs)]
    pallas_call x14 -> x18, Pallas kernels: 25.2 us -> 28.5 us  [call(): pl.pallas_call(kernel, in_specs=[pl.BlockSpec(memory_space=pltpu.SMEM)] +...]
    ppermute x5 -> x6, starting transfers between devices: 5.55 us -> 6.96 us  [face_permute(): return lax.ppermute(array, ('box', 'face'), pairs)]
    concatenate x1, other arithmetic: 0.1 us -> 1.05 us  [on_device(): w_two = jnp.roll(w_second[:, 0], -face * fr, axis=2)]
    unnamed x8 -> x10, local copies, waits for them, and re-layouts: 4.89 us -> 5.83 us
    ppermute x16 -> x17, waiting for transfers between devices: 11.2 us -> 10.8 us  [box_permute(): return lax.ppermute(array, 'box', [(b, b ^ mask) for b in range(n_box)])]
  transfers between devices with their start and end apart: 21 -> 23, of which waited for: 9 -> 7; matrix products, arithmetic and copies ran while one was open for 3% -> 4% of each run, Pallas kernels for 25% -> 30%
where the time goes in v8:
time: 77.6 us; the launch traced here: 77.1 us
  Pallas kernels  28.5 us (37%)
  waiting for transfers between devices  22.1 us (28%)
  starting transfers between devices  17.2 us (22%)
  local copies, waits for them, and re-layouts  6.57 us (8%)
  other arithmetic  2.51 us (3%)
    pallas_call x18, Pallas kernels, call(): pl.pallas_call(kernel, in_specs=[pl.BlockSpec(memory_space=pltpu.SMEM)] +...  28.5 us
    ppermute x6, waiting for transfers between devices, face_permute(): return lax.ppermute(array, ('box', 'face'), pairs)  11.3 us
    ppermute x17, waiting for transfers between devices, box_permute(): return lax.ppermute(array, 'box', [(b, b ^ mask) for b in range(n_box)])  10.8 us
    ppermute x17, starting transfers between devices, box_permute(): return lax.ppermute(array, 'box', [(b, b ^ mask) for b in range(n_box)])  10.2 us
    ppermute x6, starting transfers between devices, face_permute(): return lax.ppermute(array, ('box', 'face'), pairs)  6.96 us
    unnamed x10, local copies, waits for them, and re-layouts  5.83 us
  transfers between devices with their start and end apart: 23, of which 7 were waited for; matrix products, arithmetic and copies ran while one was open for 4% of the time, Pallas kernels for 30%

profile of v8, /device:TPU:1, one launch (start us, length us, event | category | flops | bytes accessed | tf_op | source)
XLA Modules:
  0.0 77.1 jit_solution(8958330587765968000)
XLA Ops:
  0.1 2.3 %copy-done = bf16[2,1,1,3,256,1536]{5,4,3,2,1,0:T(8,128)(2,1)S(1)} copy-done((bf16[2,1,1,3,256,1536]{5,4,3,2,1,0:T(8,128)(2,1)S(1)}, bf16[2,1,1,3,256,1536]{5,4,3,2,1,0:T(8,128)(2,1)}, u32[]{:S(2)}) %copy-start) | copy-done | bytes 4718616
  2.4 1.4 %shard_map.56 = (bf16[2,256,512]{2,1,0:T(8,128)(2,1)S(1)}, bf16[2,256,512]{2,1,0:T(8,128)(2,1)}) custom-call(s32[4]{0:T(128)S(1)} %pad_add_fusion.sc, bf16[2,3,256,1536]{3,2,1,0:T(8,128)(2,1)S(1)} %bitcast.14), custom_call_target="tpu_custom_call" | custom-call | tf_op jit(solution)/shard_map/pallas_call | solution.py:46
  3.9 0.5 collective-permute-start.4
  4.3 0.7 dynamic-slice_bitcast_fusion
  5.1 2.3 %copy-done.1 = bf16[2,1,1,3,256,1536]{5,4,3,2,1,0:T(8,128)(2,1)S(1)} copy-done((bf16[2,1,1,3,256,1536]{5,4,3,2,1,0:T(8,128)(2,1)S(1)}, bf16[2,1,1,3,256,1536]{5,4,3,2,1,0:T(8,128)(2,1)}, u32[]{:S(2)}) %copy-start.1) | copy-done | bytes 4718616
  7.4 2.1 %shard_map.55 = (s32[1,512]{1,0:T(1,128)S(1)}, s32[512,1]{1,0:T(8,128)S(1)}, bf16[2,128,1024]{2,1,0:T(8,128)(2,1)S(1)}, bf16[2,128,1024]{2,1,0:T(8,128)(2,1)}, b...) custom-call(s32[4]{0:T(128)S(1)} %pad_add_fusion.sc, bf16[2,3,256,1536]{3,2,1,0:T(8,128)(2,1)S(1)} %bitcast.15, ...), custom_call_target="tpu_custom_call" | custom-call | tf_op jit(solution)/shard_map/pallas_call | solution.py:46
  9.6 1.1 %copy-done.2 = bf16[2,256,1536]{2,1,0:T(8,128)(2,1)} copy-done((bf16[2,256,1536]{2,1,0:T(8,128)(2,1)}, bf16[2,256,1536]{2,1,0:T(8,128)(2,1)S(1)}, u32[]{:S(2)}) %copy-start.2) | copy-done | bytes 1572888
  10.8 0.5 collective-permute-start.2
  11.2 1.2 %fusion.own_ref = bf16[2,256,512]{2,1,0:T(8,128)(2,1)S(1)} fusion(s32[]{:T(128)S(6)} %select_n.57, bf16[2,256,512]{2,1,0:T(8,128)(2,1)} %bitcast.18), kind=kLoop, calls=%fused_computation.2 | loop fusion | flops 1048576 | bytes 1048580 | tf_op jit(solution)/shard_map/jit(_roll_dynamic)/concatenate | solution.py:180
  12.4 0.1 collective-permute-start.3
  12.6 1.0 %fusion.1 = bf16[2,128,512]{2,1,0:T(8,128)(2,1)S(1)} fusion(s32[]{:T(128)S(6)} %select_n.57, bf16[2,128,512]{2,1,0:T(8,128)(2,1)} %bitcast.16), kind=kLoop, calls=%fused_computation.6 | loop fusion | flops 524288 | bytes 524292 | tf_op jit(solution)/shard_map/jit(_roll_dynamic)/concatenate | solution.py:182
  13.6 0.6 shard_map.57
  14.2 2.8 %collective-permute-start.5 = (bf16[2,128,512]{2,1,0:T(8,128)(2,1)S(1)}, bf16[2,128,512]{2,1,0:T(8,128)(2,1)S(1)}, u32[]{:S(2)}, u32[]{:S(2)}) collective-permute-start(bf16[2,128,512]{2,1,0:T(8,128)(2,1)S(1)} %get-tuple-element.54), channel_id=1, source_target_pairs={{0,1},{1,0},{2,3},{3,2},{4,5},{5,4},{6,7},{7,6},{8,9},{9,8},{10,11... | collective-permute-start | bytes 786440 | tf_op jit(solution)/shard_map/ppermute | solution.py:92
  17.0 1.9 %shard_map.60 = (bf16[2,256,512]{2,1,0:T(8,128)(2,1)S(1)}, bf16[2,128,512]{2,1,0:T(8,128)(2,1)S(1)}) custom-call(s32[4]{0:T(128)S(1)} %pad_add_fusion.sc, bf16[2,256,512]{2,1,0:T(8,128)(2,1)} %get-tuple-element.56.own_ref, bf16[2,256,512]{2,1,0:T(8,128)(2,1)} %collective-permute-done.4.sib_ref, s32[1,512]{1,0:T(1,128)S(1)} %get-tuple-element.45.comp_ref), custom_call_target="tpu_custom_call" | custom-call | flops 20000000000 | tf_op jit(solution)/shard_map/pallas_call | solution.py:46
  19.0 4.6 %collective-permute-done.5.refs_0_ = bf16[2,128,512]{2,1,0:T(8,128)(2,1)S(1)} collective-permute-done((bf16[2,128,512]{2,1,0:T(8,128)(2,1)S(1)}, bf16[2,128,512]{2,1,0:T(8,128)(2,1)S(1)}, u32[]{:S(2)}, u32[]{:S(2)}) %collective-permute-start.5) | collective-permute-done | bytes 262176 | tf_op jit(solution)/shard_map/ppermute | solution.py:92
  23.6 1.2 %collective-permute-start.8 = (bf16[2,128,512]{2,1,0:T(8,128)(2,1)S(1)}, bf16[2,128,512]{2,1,0:T(8,128)(2,1)S(1)}, u32[]{:S(2)}, u32[]{:S(2)}) collective-permute-start(bf16[2,128,512]{2,1,0:T(8,128)(2,1)S(1)} %fusion.1), channel_id=1, source_target_pairs={{0,4},{2,6},{4,0},{6,2},{8,12},{10,14},{12,8},{14,10},{16,20},{18,... | collective-permute-start | bytes 786440 | tf_op jit(solution)/shard_map/ppermute | solution.py:78
  24.9 1.5 %collective-permute-start.6 = (bf16[2,128,512]{2,1,0:T(8,128)(2,1)S(1)}, bf16[2,128,512]{2,1,0:T(8,128)(2,1)S(1)}, u32[]{:S(2)}, u32[]{:S(2)}) collective-permute-start(bf16[2,128,512]{2,1,0:T(8,128)(2,1)S(1)} %collective-permute-done.5.refs_0_), channel_id=1, source_target_pairs={{0,2},{2,0},{4,6},{6,4},{8,10},{10,8},{12,14},{14,12},{16,18},{18,... | collective-permute-start | bytes 786440 | tf_op jit(solution)/shard_map/ppermute | solution.py:78
  26.4 3.7 %shard_map.58 = (bf16[2,256,1536]{2,1,0:T(8,128)(2,1)S(1)}, bf16[2,128,1024]{2,1,0:T(8,128)(2,1)S(1)}, bf16[2,128,512]{2,1,0:T(8,128)(2,1)S(1)}, bf16[2,128,512]{2,1,0:T(8,128)(2,1)S(1)}) custom-call(s32[4]{0:T(128)S(1)} %pad_add_fusion.sc, bf16[2,256,1536]{2,1,0:T(8,128)(2,1)S(1)} %get-tuple-element.44.own_ref, ...), custom_call_target="tpu_custom_call" | custom-call | tf_op jit(solution)/shard_map/pallas_call | solution.py:46
  30.1 1.3 %collective-permute-start.12 = (bf16[2,128,1024]{2,1,0:T(8,128)(2,1)S(1)}, bf16[2,128,1024]{2,1,0:T(8,128)(2,1)S(1)}, u32[]{:S(2)}, u32[]{:S(2)}) collective-permute-start(bf16[2,128,1024]{2,1,0:T(8,128)(2,1)S(1)} %get-tuple-element.67), channel_id=1, source_target_pairs={{0,1},{1,0},{2,3},{3,2},{4,5},{5,4},{6,7},{7,6},{8,9},{9,8},{10,11... | collective-permute-start | bytes 1572872 | tf_op jit(solution)/shard_map/ppermute | solution.py:92
  31.4 0.6 shard_map.59.w_ref
  32.1 0.3 collective-permute-start.9
  32.4 1.9 %shard_map.61 = (f32[2,128,1024]{2,1,0:T(8,128)S(1)}, bf16[2,128,512]{2,1,0:T(8,128)(2,1)S(1)}) custom-call(s32[4]{0:T(128)S(1)} %pad_add_fusion.sc, bf16[2,128,1024]{2,1,0:T(8,128)(2,1)S(1)} %get-tuple-element.52.keep_ref, bf16[2,128,1024]{2,1,0:T(8,128)(2,1)} %collective-permute-done.2.recv_ref, bf16[2,512,512]{2,1,0:T(8,128)(2,1)S(1)} %shard_map.59.w_ref, ...), custom_call_target="tpu_custom_call" | custom-call | tf_op jit(solution)/shard_map/pallas_call | solution.py:46
  34.3 0.6 shard_map.62.rest_0_
  34.9 1.0 %shard_map.63 = (bf16[2,128,512]{2,1,0:T(8,128)(2,1)S(1)}, bf16[2,128,256]{2,1,0:T(8,128)(2,1)S(1)}, bf16[2,128,256]{2,1,0:T(8,128)(2,1)S(1)}) custom-call(s32[4]{0:T(128)S(1)} %pad_add_fusion.sc, f32[2,128,1024]{2,1,0:T(8,128)S(1)} %get-tuple-element.58.acc_ref, bf16[2,128,512]{2,1,0:T(8,128)(2,1)S(1)} %get-tuple-element.59.hid_ref, ...), custom_call_target="tpu_custom_call" | custom-call | tf_op jit(solution)/shard_map/pallas_call | solution.py:46
  35.9 1.3 %collective-permute-start.10 = (bf16[2,128,256]{2,1,0:T(8,128)(2,1)S(1)}, bf16[2,128,256]{2,1,0:T(8,128)(2,1)S(1)}, u32[]{:S(2)}, u32[]{:S(2)}) collective-permute-start(bf16[2,128,256]{2,1,0:T(8,128)(2,1)S(1)} %get-tuple-element.65), channel_id=1, source_target_pairs={{0,4},{2,6},{4,0},{6,2},{8,12},{10,14},{12,8},{14,10},{16,20},{18,... | collective-permute-start | bytes 393224 | tf_op jit(solution)/shard_map/ppermute | solution.py:78
  37.2 3.6 %collective-permute-done.10.x_ref = bf16[2,128,256]{2,1,0:T(8,128)(2,1)S(1)} collective-permute-done((bf16[2,128,256]{2,1,0:T(8,128)(2,1)S(1)}, bf16[2,128,256]{2,1,0:T(8,128)(2,1)S(1)}, u32[]{:S(2)}, u32[]{:S(2)}) %collective-permute-start.10) | collective-permute-done | bytes 131104 | tf_op jit(solution)/shard_map/ppermute | solution.py:78
  40.7 0.6 shard_map.64.own_ref
  41.3 2.2 %collective-permute-done.12.rest_1_.refs_0_ = bf16[2,128,1024]{2,1,0:T(8,128)(2,1)S(1)} collective-permute-done((bf16[2,128,1024]{2,1,0:T(8,128)(2,1)S(1)}, bf16[2,128,1024]{2,1,0:T(8,128)(2,1)S(1)}, u32[]{:S(2)}, u32[]{:S(2)}) %collective-permute-start.12) | collective-permute-done | bytes 524320 | tf_op jit(solution)/shard_map/ppermute | solution.py:92
  43.5 0.4 collective-permute-start.13
  43.9 1.4 %collective-permute-start.19 = (bf16[2,128,768]{2,1,0:T(8,128)(2,1)S(1)}, bf16[2,128,768]{2,1,0:T(8,128)(2,1)S(1)}, u32[]{:S(2)}, u32[]{:S(2)}) collective-permute-start(bf16[2,128,768]{2,1,0:T(8,128)(2,1)S(1)} %shard_map.64.own_ref), channel_id=1, source_target_pairs={{0,1},{1,0},{2,3},{3,2},{4,5},{5,4},{6,7},{7,6},{8,9},{9,8},{10,11... | collective-permute-start | bytes 1179656 | tf_op jit(solution)/shard_map/ppermute | solution.py:92
  45.4 0.6 collective-permute-start.16
  46.1 4.2 %shard_map.65.refs_5_ = bf16[2,512,1536]{2,1,0:T(8,128)(2,1)S(1)} custom-call(s32[4]{0:T(128)S(1)} %pad_add_fusion.sc, bf16[2,512,512]{2,1,0:T(8,128)(2,1)S(1)} %shard_map.59.w_ref, bf16[2,256,512]{2,1,0:T(8,128)(2,1)S(1)} %get-tuple-element.48.own_ref.end_ref, bf16[2,256,512]{2,1,0:T(8,128)(2,1)S(1)} %collective-permute-done.1.sib_ref.endsib_ref, ...), custom_call_target="tpu_custom_call" | custom-call | tf_op jit(solution)/shard_map/pallas_call | solution.py:46
  50.3 4.2 %collective-permute-done.18.x_ref = bf16[2,128,768]{2,1,0:T(8,128)(2,1)S(1)} collective-permute-done((bf16[2,128,768]{2,1,0:T(8,128)(2,1)S(1)}, bf16[2,128,768]{2,1,0:T(8,128)(2,1)S(1)}, u32[]{:S(2)}, u32[]{:S(2)}) %collective-permute-start.18) | collective-permute-done | bytes 393248 | tf_op jit(solution)/shard_map/ppermute | solution.py:78
  54.5 0.6 shard_map.69.refs_0_
  55.1 0.5 collective-permute-start.20
  55.6 4.4 %collective-permute-done.14.refs_2_ = bf16[2,128,512]{2,1,0:T(8,128)(2,1)S(1)} collective-permute-done((bf16[2,128,512]{2,1,0:T(8,128)(2,1)S(1)}, bf16[2,128,512]{2,1,0:T(8,128)(2,1)S(1)}, u32[]{:S(2)}, u32[]{:S(2)}) %collective-permute-start.14) | collective-permute-done | bytes 262176 | tf_op jit(solution)/shard_map/ppermute | solution.py:92
  60.1 1.0 %collective-permute-start.15 = (bf16[2,128,512]{2,1,0:T(8,128)(2,1)S(1)}, bf16[2,128,512]{2,1,0:T(8,128)(2,1)S(1)}, u32[]{:S(2)}, u32[]{:S(2)}) collective-permute-start(bf16[2,128,512]{2,1,0:T(8,128)(2,1)S(1)} %collective-permute-done.14.refs_2_), channel_id=1, source_target_pairs={{0,2},{2,0},{4,6},{6,4},{8,10},{10,8},{12,14},{14,12},{16,18},{18,... | collective-permute-start | bytes 786440 | tf_op jit(solution)/shard_map/ppermute | solution.py:78
  61.1 0.6 shard_map.66.refs_6_
  61.7 1.4 %collective-permute-start.11 = (bf16[2,128,512]{2,1,0:T(8,128)(2,1)S(1)}, bf16[2,128,512]{2,1,0:T(8,128)(2,1)S(1)}, u32[]{:S(2)}, u32[]{:S(2)}) collective-permute-start(bf16[2,128,512]{2,1,0:T(8,128)(2,1)S(1)} %get-tuple-element.66), channel_id=1, source_target_pairs={{0,1},{1,0},{2,3},{3,2},{4,5},{5,4},{6,7},{7,6},{8,9},{9,8},{10,11... | collective-permute-start | bytes 786440 | tf_op jit(solution)/shard_map/ppermute | solution.py:92
  63.1 0.3 collective-permute-start.21
  63.4 1.4 %collective-permute-done.20.x_ref = bf16[2,128,768]{2,1,0:T(8,128)(2,1)S(1)} collective-permute-done((bf16[2,128,768]{2,1,0:T(8,128)(2,1)S(1)}, bf16[2,128,768]{2,1,0:T(8,128)(2,1)S(1)}, u32[]{:S(2)}, u32[]{:S(2)}) %collective-permute-start.20) | collective-permute-done | bytes 393248 | tf_op jit(solution)/shard_map/ppermute | solution.py:78
  64.8 0.6 shard_map.70.refs_1_
  65.4 1.9 %collective-permute-start.22 = (bf16[2,128,1536]{2,1,0:T(8,128)(2,1)S(1)}, bf16[2,128,1536]{2,1,0:T(8,128)(2,1)S(1)}, u32[]{:S(2)}, u32[]{:S(2)}) collective-permute-start(bf16[2,128,1536]{2,1,0:T(8,128)(2,1)S(1)} %shard_map.70.refs_1_), channel_id=1, source_target_pairs={{0,2},{2,0},{4,6},{6,4},{8,10},{10,8},{12,14},{14,12},{16,18},{18,... | collective-permute-start | bytes 2359304 | tf_op jit(solution)/shard_map/ppermute | solution.py:78
  67.4 3.1 %shard_map.67 = (bf16[2,512,512]{2,1,0:T(8,128)(2,1)S(1)}, bf16[512,512]{1,0:T(8,128)(2,1)S(1)}, f32[512,512]{1,0:T(8,128)S(1)}) custom-call(s32[4]{0:T(128)S(1)} %pad_add_fusion.sc, bf16[2,256,1536]{2,1,0:T(8,128)(2,1)S(1)} %copy-done.3, bf16[2,256,1536]{2,1,0:T(8,128)(2,1)S(1)} %get-tuple-element.50.kept_ref, ...), custom_call_target="tpu_custom_call" | custom-call | flops 6000000000 | tf_op jit(solution)/shard_map/pallas_call | solution.py:46
  70.6 1.5 %collective-permute-done.17.refs_1_ = bf16[2,128,512]{2,1,0:T(8,128)(2,1)S(1)} collective-permute-done((bf16[2,128,512]{2,1,0:T(8,128)(2,1)S(1)}, bf16[2,128,512]{2,1,0:T(8,128)(2,1)S(1)}, u32[]{:S(2)}, u32[]{:S(2)}) %collective-permute-start.17) | collective-permute-done | bytes 262176 | tf_op jit(solution)/shard_map/ppermute | solution.py:78
  72.1 0.6 shard_map.68.rows_ref
  72.8 2.8 %shard_map.71 = (bf16[2,1,256,1536]{3,2,1,0:T(8,128)(2,1)}, f32[512,512]{1,0:T(8,128)S(1)}) custom-call(s32[4]{0:T(128)S(1)} %pad_add_fusion.sc, bf16[2,512,512]{2,1,0:T(8,128)(2,1)S(1)} %get-tuple-element.71.hid_ref, bf16[512,512]{1,0:T(8,128)(2,1)S(1)} %get-tuple-element.74.first_ref, bf16[2,128,1536]{2,1,0:T(8,128)(2,1)S(1)} %shard_map.69.refs_0_, ...), custom_call_target="tpu_custom_call" | custom-call | tf_op jit(solution)/shard_map/pallas_call | solution.py:46
  75.6 1.5 %shard_map.72 = bf16[2,1,256,1536]{3,2,1,0:T(8,128)(2,1)} custom-call(s32[4]{0:T(128)S(1)} %pad_add_fusion.sc, bf16[2,256,512]{2,1,0:T(8,128)(2,1)S(1)} %shard_map.68.rows_ref, f32[512,512]{1,0:T(8,128)S(1)} %get-tuple-element.73.one_ref, f32[512,512]{1,0:T(8,128)S(1)} %get-tuple-element.79.two_ref, ...), custom_call_target="tpu_custom_call", output_to_operand_aliasing={{}: (4, {})} | custom-call | tf_op jit(solution)/shard_map/pallas_call | solution.py:46
  (32 shorter events, 0.6 us)
Async XLA Ops:
  0.1 2.3 %copy-start = (bf16[2,1,1,3,256,1536]{5,4,3,2,1,0:T(8,128)(2,1)S(1)}, bf16[2,1,1,3,256,1536]{5,4,3,2,1,0:T(8,128)(2,1)}, u32[]{:S(2)}) copy-start(bf16[2,1,1,3,256,1536]{5,4,3,2,1,0:T(8,128)(2,1)} %param.5) | copy-start | bytes 14155780
  3.8 9.8 %collective-permute-start.1 = (bf16[2,256,512]{2,1,0:T(8,128)(2,1)S(1)}, bf16[2,256,512]{2,1,0:T(8,128)(2,1)S(1)}, u32[]{:S(2)}, u32[]{:S(2)}) collective-permute-start(bf16[2,256,512]{2,1,0:T(8,128)(2,1)S(1)} %get-tuple-element.48.own_ref.end_ref), channel_id=1, source_target_pairs={{0,2},{2,0},{4,6},{6,4},{8,10},{10,8},{12,14},{14,12},{16,18},{18,... | collective-permute-start | bytes 1572872 | tf_op jit(solution)/shard_map/ppermute | solution.py:78
  3.9 13.1 %collective-permute-start.4 = (bf16[2,256,512]{2,1,0:T(8,128)(2,1)}, bf16[2,256,512]{2,1,0:T(8,128)(2,1)}, u32[]{:S(2)}, u32[]{:S(2)}) collective-permute-start(bf16[2,256,512]{2,1,0:T(8,128)(2,1)} %get-tuple-element.56.own_ref), channel_id=1, source_target_pairs={{0,2},{2,0},{4,6},{6,4},{8,10},{10,8},{12,14},{14,12},{16,18},{18,... | collective-permute-start | bytes 1572872 | tf_op jit(solution)/shard_map/ppermute | solution.py:78
  5.1 2.3 %copy-start.1 = (bf16[2,1,1,3,256,1536]{5,4,3,2,1,0:T(8,128)(2,1)S(1)}, bf16[2,1,1,3,256,1536]{5,4,3,2,1,0:T(8,128)(2,1)}, u32[]{:S(2)}) copy-start(bf16[2,1,1,3,256,1536]{5,4,3,2,1,0:T(8,128)(2,1)} %param.5) | copy-start | bytes 14155780
  9.6 1.1 %copy-start.2 = (bf16[2,256,1536]{2,1,0:T(8,128)(2,1)}, bf16[2,256,1536]{2,1,0:T(8,128)(2,1)S(1)}, u32[]{:S(2)}) copy-start(bf16[2,256,1536]{2,1,0:T(8,128)(2,1)S(1)} %get-tuple-element.43.end_ref) | copy-start | bytes 4718596
  10.7 14.2 %collective-permute-start = (bf16[2,256,1536]{2,1,0:T(8,128)(2,1)S(1)}, bf16[2,256,1536]{2,1,0:T(8,128)(2,1)}, u32[]{:S(2)}, u32[]{:S(2)}) collective-permute-start(bf16[2,256,1536]{2,1,0:T(8,128)(2,1)S(1)} %get-tuple-element.44.own_ref), channel_id=1, source_target_pairs={{0,2},{2,0},{4,6},{6,4},{8,10},{10,8},{12,14},{14,12},{16,18},{18,... | collective-permute-start | bytes 4718600 | tf_op jit(solution)/shard_map/ppermute | solution.py:78
  10.8 21.6 %collective-permute-start.2 = (bf16[2,128,1024]{2,1,0:T(8,128)(2,1)}, bf16[2,128,1024]{2,1,0:T(8,128)(2,1)}, u32[]{:S(2)}, u32[]{:S(2)}) collective-permute-start(bf16[2,128,1024]{2,1,0:T(8,128)(2,1)} %get-tuple-element.53), channel_id=1, source_target_pairs={{0,2},{2,0},{4,6},{6,4},{8,10},{10,8},{12,14},{14,12},{16,18},{18,... | collective-permute-start | bytes 1572872 | tf_op jit(solution)/shard_map/ppermute | solution.py:78
  12.4 17.7 %collective-permute-start.3 = (bf16[2,256,512]{2,1,0:T(8,128)(2,1)S(1)}, bf16[2,256,512]{2,1,0:T(8,128)(2,1)S(1)}, u32[]{:S(2)}, u32[]{:S(2)}) collective-permute-start(bf16[2,256,512]{2,1,0:T(8,128)(2,1)S(1)} %fusion.own_ref), channel_id=1, source_target_pairs={{0,2},{2,0},{4,6},{6,4},{8,10},{10,8},{12,14},{14,12},{16,18},{18,... | collective-permute-start | bytes 1572872 | tf_op jit(solution)/shard_map/ppermute | solution.py:78
  14.2 9.4 %collective-permute-start.5 = (bf16[2,128,512]{2,1,0:T(8,128)(2,1)S(1)}, bf16[2,128,512]{2,1,0:T(8,128)(2,1)S(1)}, u32[]{:S(2)}, u32[]{:S(2)}) collective-permute-start(bf16[2,128,512]{2,1,0:T(8,128)(2,1)S(1)} %get-tuple-element.54), channel_id=1, source_target_pairs={{0,1},{1,0},{2,3},{3,2},{4,5},{5,4},{6,7},{7,6},{8,9},{9,8},{10,11... | collective-permute-start | bytes 786440 | tf_op jit(solution)/shard_map/ppermute | solution.py:92
  18.9 13.1 %collective-permute-start.7 = (bf16[2,128,512]{2,1,0:T(8,128)(2,1)S(1)}, bf16[2,128,512]{2,1,0:T(8,128)(2,1)S(1)}, u32[]{:S(2)}, u32[]{:S(2)}) collective-permute-start(bf16[2,128,512]{2,1,0:T(8,128)(2,1)S(1)} %get-tuple-element.60), channel_id=1, source_target_pairs={{0,1},{1,0},{2,3},{3,2},{4,5},{5,4},{6,7},{7,6},{8,9},{9,8},{10,11... | collective-permute-start | bytes 786440 | tf_op jit(solution)/shard_map/ppermute | solution.py:92
  23.6 8.4 %collective-permute-start.8 = (bf16[2,128,512]{2,1,0:T(8,128)(2,1)S(1)}, bf16[2,128,512]{2,1,0:T(8,128)(2,1)S(1)}, u32[]{:S(2)}, u32[]{:S(2)}) collective-permute-start(bf16[2,128,512]{2,1,0:T(8,128)(2,1)S(1)} %fusion.1), channel_id=1, source_target_pairs={{0,4},{2,6},{4,0},{6,2},{8,12},{10,14},{12,8},{14,10},{16,20},{18,... | collective-permute-start | bytes 786440 | tf_op jit(solution)/shard_map/ppermute | solution.py:78
  24.9 9.4 %collective-permute-start.6 = (bf16[2,128,512]{2,1,0:T(8,128)(2,1)S(1)}, bf16[2,128,512]{2,1,0:T(8,128)(2,1)S(1)}, u32[]{:S(2)}, u32[]{:S(2)}) collective-permute-start(bf16[2,128,512]{2,1,0:T(8,128)(2,1)S(1)} %collective-permute-done.5.refs_0_), channel_id=1, source_target_pairs={{0,2},{2,0},{4,6},{6,4},{8,10},{10,8},{12,14},{14,12},{16,18},{18,... | collective-permute-start | bytes 786440 | tf_op jit(solution)/shard_map/ppermute | solution.py:78
  30.1 13.4 %collective-permute-start.12 = (bf16[2,128,1024]{2,1,0:T(8,128)(2,1)S(1)}, bf16[2,128,1024]{2,1,0:T(8,128)(2,1)S(1)}, u32[]{:S(2)}, u32[]{:S(2)}) collective-permute-start(bf16[2,128,1024]{2,1,0:T(8,128)(2,1)S(1)} %get-tuple-element.67), channel_id=1, source_target_pairs={{0,1},{1,0},{2,3},{3,2},{4,5},{5,4},{6,7},{7,6},{8,9},{9,8},{10,11... | collective-permute-start | bytes 1572872 | tf_op jit(solution)/shard_map/ppermute | solution.py:92
  32.1 2.8 %collective-permute-start.9 = (bf16[2,128,512]{2,1,0:T(8,128)(2,1)S(1)}, bf16[2,128,512]{2,1,0:T(8,128)(2,1)S(1)}, u32[]{:S(2)}, u32[]{:S(2)}) collective-permute-start(bf16[2,128,512]{2,1,0:T(8,128)(2,1)S(1)} %collective-permute-done.7.rest_1_.rest_3_), channel_id=1, source_target_pairs={{0,2},{2,0},{4,6},{6,4},{8,10},{10,8},{12,14},{14,12},{16,18},{18,... | collective-permute-start | bytes 786440 | tf_op jit(solution)/shard_map/ppermute | solution.py:78
  34.9 10.4 %copy-start.4 = (bf16[2,1,128,512]{3,2,1,0:T(8,128)(2,1)S(1)}, bf16[2,1,128,512]{3,2,1,0:T(8,128)(2,1)}, u32[]{:S(2)}) copy-start(bf16[2,1,128,512]{3,2,1,0:T(8,128)(2,1)} %param.7) | copy-start | bytes 786436
  35.9 4.9 %collective-permute-start.10 = (bf16[2,128,256]{2,1,0:T(8,128)(2,1)S(1)}, bf16[2,128,256]{2,1,0:T(8,128)(2,1)S(1)}, u32[]{:S(2)}, u32[]{:S(2)}) collective-permute-start(bf16[2,128,256]{2,1,0:T(8,128)(2,1)S(1)} %get-tuple-element.65), channel_id=1, source_target_pairs={{0,4},{2,6},{4,0},{6,2},{8,12},{10,14},{12,8},{14,10},{16,20},{18,... | collective-permute-start | bytes 393224 | tf_op jit(solution)/shard_map/ppermute | solution.py:78
  43.5 2.6 %collective-permute-start.13 = (bf16[2,128,1024]{2,1,0:T(8,128)(2,1)S(1)}, bf16[2,128,1024]{2,1,0:T(8,128)(2,1)S(1)}, u32[]{:S(2)}, u32[]{:S(2)}) collective-permute-start(bf16[2,128,1024]{2,1,0:T(8,128)(2,1)S(1)} %collective-permute-done.12.rest_1_.refs_0_), channel_id=1, source_target_pairs={{0,2},{2,0},{4,6},{6,4},{8,10},{10,8},{12,14},{14,12},{16,18},{18,... | collective-permute-start | bytes 1572872 | tf_op jit(solution)/shard_map/ppermute | solution.py:78
  43.9 10.6 %collective-permute-start.18 = (bf16[2,128,768]{2,1,0:T(8,128)(2,1)S(1)}, bf16[2,128,768]{2,1,0:T(8,128)(2,1)S(1)}, u32[]{:S(2)}, u32[]{:S(2)}) collective-permute-start(bf16[2,128,768]{2,1,0:T(8,128)(2,1)S(1)} %shard_map.64.own_ref), channel_id=1, source_target_pairs={{0,4},{2,6},{4,0},{6,2},{8,12},{10,14},{12,8},{14,10},{16,20},{18,... | collective-permute-start | bytes 1179656 | tf_op jit(solution)/shard_map/ppermute | solution.py:78
  43.9 11.2 %collective-permute-start.19 = (bf16[2,128,768]{2,1,0:T(8,128)(2,1)S(1)}, bf16[2,128,768]{2,1,0:T(8,128)(2,1)S(1)}, u32[]{:S(2)}, u32[]{:S(2)}) collective-permute-start(bf16[2,128,768]{2,1,0:T(8,128)(2,1)S(1)} %shard_map.64.own_ref), channel_id=1, source_target_pairs={{0,1},{1,0},{2,3},{3,2},{4,5},{5,4},{6,7},{7,6},{8,9},{9,8},{10,11... | collective-permute-start | bytes 1179656 | tf_op jit(solution)/shard_map/ppermute | solution.py:92
  45.4 15.6 %collective-permute-start.16 = (bf16[2,2,128,512]{3,2,1,0:T(8,128)(2,1)S(1)}, bf16[2,2,128,512]{3,2,1,0:T(8,128)(2,1)S(1)}, u32[]{:S(2)}, u32[]{:S(2)}) collective-permute-start(bf16[2,2,128,512]{3,2,1,0:T(8,128)(2,1)S(1)} %pad_maximum_fusion.own_ref), channel_id=1, source_target_pairs={{0,2},{2,0},{4,6},{6,4},{8,10},{10,8},{12,14},{14,12},{16,18},{18,... | collective-permute-start | bytes 1572872 | tf_op jit(solution)/shard_map/ppermute | solution.py:78
  46.1 14.0 %collective-permute-start.14 = (bf16[2,128,512]{2,1,0:T(8,128)(2,1)S(1)}, bf16[2,128,512]{2,1,0:T(8,128)(2,1)S(1)}, u32[]{:S(2)}, u32[]{:S(2)}) collective-permute-start(bf16[2,128,512]{2,1,0:T(8,128)(2,1)S(1)} %get-tuple-element.70), channel_id=1, source_target_pairs={{0,1},{1,0},{2,3},{3,2},{4,5},{5,4},{6,7},{7,6},{8,9},{9,8},{10,11... | collective-permute-start | bytes 786440 | tf_op jit(solution)/shard_map/ppermute | solution.py:92
  55.1 12.3 %copy-start.3 = (bf16[2,256,1536]{2,1,0:T(8,128)(2,1)S(1)}, bf16[2,256,1536]{2,1,0:T(8,128)(2,1)}, u32[]{:S(2)}) copy-start(bf16[2,256,1536]{2,1,0:T(8,128)(2,1)} %copy-done.2) | copy-start | bytes 4718596
  55.1 9.7 %collective-permute-start.20 = (bf16[2,128,768]{2,1,0:T(8,128)(2,1)S(1)}, bf16[2,128,768]{2,1,0:T(8,128)(2,1)S(1)}, u32[]{:S(2)}, u32[]{:S(2)}) collective-permute-start(bf16[2,128,768]{2,1,0:T(8,128)(2,1)S(1)} %collective-permute-done.19.own_ref), channel_id=1, source_target_pairs={{0,4},{2,6},{4,0},{6,2},{8,12},{10,14},{12,8},{14,10},{16,20},{18,... | collective-permute-start | bytes 1179656 | tf_op jit(solution)/shard_map/ppermute | solution.py:78
  60.1 7.3 %collective-permute-start.15 = (bf16[2,128,512]{2,1,0:T(8,128)(2,1)S(1)}, bf16[2,128,512]{2,1,0:T(8,128)(2,1)S(1)}, u32[]{:S(2)}, u32[]{:S(2)}) collective-permute-start(bf16[2,128,512]{2,1,0:T(8,128)(2,1)S(1)} %collective-permute-done.14.refs_2_), channel_id=1, source_target_pairs={{0,2},{2,0},{4,6},{6,4},{8,10},{10,8},{12,14},{14,12},{16,18},{18,... | collective-permute-start | bytes 786440 | tf_op jit(solution)/shard_map/ppermute | solution.py:78
  61.7 8.8 %collective-permute-start.11 = (bf16[2,128,512]{2,1,0:T(8,128)(2,1)S(1)}, bf16[2,128,512]{2,1,0:T(8,128)(2,1)S(1)}, u32[]{:S(2)}, u32[]{:S(2)}) collective-permute-start(bf16[2,128,512]{2,1,0:T(8,128)(2,1)S(1)} %get-tuple-element.66), channel_id=1, source_target_pairs={{0,1},{1,0},{2,3},{3,2},{4,5},{5,4},{6,7},{7,6},{8,9},{9,8},{10,11... | collective-permute-start | bytes 786440 | tf_op jit(solution)/shard_map/ppermute | solution.py:92
  63.1 9.6 %collective-permute-start.21 = (bf16[2,128,1536]{2,1,0:T(8,128)(2,1)S(1)}, bf16[2,128,1536]{2,1,0:T(8,128)(2,1)S(1)}, u32[]{:S(2)}, u32[]{:S(2)}) collective-permute-start(bf16[2,128,1536]{2,1,0:T(8,128)(2,1)S(1)} %shard_map.69.refs_0_), channel_id=1, source_target_pairs={{0,2},{2,0},{4,6},{6,4},{8,10},{10,8},{12,14},{14,12},{16,18},{18,... | collective-permute-start | bytes 2359304 | tf_op jit(solution)/shard_map/ppermute | solution.py:78
  65.4 7.3 %collective-permute-start.22 = (bf16[2,128,1536]{2,1,0:T(8,128)(2,1)S(1)}, bf16[2,128,1536]{2,1,0:T(8,128)(2,1)S(1)}, u32[]{:S(2)}, u32[]{:S(2)}) collective-permute-start(bf16[2,128,1536]{2,1,0:T(8,128)(2,1)S(1)} %shard_map.70.refs_1_), channel_id=1, source_target_pairs={{0,2},{2,0},{4,6},{6,4},{8,10},{10,8},{12,14},{14,12},{16,18},{18,... | collective-permute-start | bytes 2359304 | tf_op jit(solution)/shard_map/ppermute | solution.py:78
  70.5 1.6 %collective-permute-start.17 = (bf16[2,128,512]{2,1,0:T(8,128)(2,1)S(1)}, bf16[2,128,512]{2,1,0:T(8,128)(2,1)S(1)}, u32[]{:S(2)}, u32[]{:S(2)}) collective-permute-start(bf16[2,128,512]{2,1,0:T(8,128)(2,1)S(1)} %collective-permute-done.11.refs_0_), channel_id=1, source_target_pairs={{0,2},{2,0},{4,6},{6,4},{8,10},{10,8},{12,14},{14,12},{16,18},{18,... | collective-permute-start | bytes 786440 | tf_op jit(solution)/shard_map/ppermute | solution.py:78

commit v9 on v8

v9 whole, which is shorter than its diff:
```python
import functools

import jax
import jax.numpy as jnp
from jax import lax
from jax.experimental import pallas as pl
from jax.experimental.pallas import tpu as pltpu
from jax.sharding import PartitionSpec as P

BF16 = jnp.bfloat16
F32 = jnp.float32
VMEM_BYTES = 16 * 1024 * 1024
JOIN_COST = 300_000_000
ROWS_COST = 0
OWN_COST = 1_000_000_000
KEEP_COST = 6_000_000_000
SLOT_ROWS_COST = 2_000_000_000


def dot(first, second):
    return jnp.dot(first, second, preferred_element_type=F32)


def stacked(real, imag):
    return jnp.concatenate(
        [jnp.concatenate([real, -imag], axis=1), jnp.concatenate([imag, real], axis=1)], axis=0
    )


def flat(array):
    return array.reshape(array.shape[0] * array.shape[1], array.shape[2])


def column_picker(index, offset, count):
    rows = lax.broadcasted_iota(jnp.int32, (count, index.shape[1]), 0) + offset
    return jnp.where(rows == index, 1.0, 0.0).astype(BF16)


def row_picker(index, offset, count):
    cols = lax.broadcasted_iota(jnp.int32, (index.shape[0], count), 1) + offset
    return jnp.where(cols == index, 1.0, 0.0).astype(BF16)


def call(kernel, scalars, inputs, out_shapes, specs=None, out_specs=None, scratch=(), cost=0, aliases=None):
    in_vmem = pl.BlockSpec(memory_space=pltpu.VMEM)
    specs = specs or [in_vmem] * len(inputs)
    out_specs = out_specs or [in_vmem] * len(out_shapes)
    return pl.pallas_call(
        kernel,
        in_specs=[pl.BlockSpec(memory_space=pltpu.SMEM)] + specs,
        out_specs=out_specs,
        out_shape=out_shapes,
        scratch_shapes=list(scratch),
        input_output_aliases=aliases or {},
        compiler_params=pltpu.CompilerParams(vmem_limit_bytes=VMEM_BYTES),
        cost_estimate=pl.CostEstimate(flops=cost, bytes_accessed=0, transcendentals=0),
    )(scalars, *inputs)


def after(array, *others):
    return lax.optimization_barrier((array, *others))[0]


def on_device(leaf_maps, w_first, w_second, skel_first, skel_second):
    box = lax.axis_index("box")
    face = lax.axis_index("face")
    n_box, n_face = lax.axis_size("box"), lax.axis_size("face")
    nf = n_face - 1
    fr = leaf_maps.shape[4]
    hr = fr // 2
    k = leaf_maps.shape[5] // 3
    half = k // 2
    leaf = leaf_maps[:, 0, 0]
    scalars = jnp.stack([box % 2, box // 2 % 2, face, box % 4, box // 2, box // 4]).astype(jnp.int32)
    sds = jax.ShapeDtypeStruct
    in_hbm = pl.BlockSpec(memory_space=pltpu.HBM)

    def box_permute(array, mask):
        return lax.ppermute(array, "box", [(b, b ^ mask) for b in range(n_box)])

    def face_permute(array, step):
        pairs = [
            (b * n_face + f, b * n_face + (f + n_face - step) % n_face)
            for b in range(n_box) for f in range(n_face)
        ]
        return lax.ppermute(array, ("box", "face"), pairs)

    def over_face(array):
        return [face_permute(array, s) for s in range(1, n_face)]

    def halves(p):
        mine = pl.ds(pl.multiple_of(p * hr, hr), hr)
        other = pl.ds(pl.multiple_of((1 - p) * hr, hr), hr)
        return mine, other

    def slots_kernel(sc, skel_ref, skel2_ref, comp_out, col_out):
        q = sc[1]
        rows = lax.broadcasted_iota(jnp.int32, (k, k), 0)
        cols = lax.broadcasted_iota(jnp.int32, (k, k), 1)
        skel = jnp.broadcast_to(skel_ref[pl.ds(sc[4], 1), :].astype(F32), (k, k))
        column = jnp.sum(jnp.where(rows == cols, skel, 0.0), axis=1, keepdims=True)
        col_out[...] = column.astype(jnp.int32)
        place = skel2_ref[pl.ds(sc[5], 1), :] - q * k
        taken = jnp.where(rows == place, jnp.broadcast_to(column, (k, k)), 0.0)
        found = jnp.sum(taken, axis=0, keepdims=True).astype(jnp.int32)
        comp_out[...] = jnp.where(jnp.logical_and(place >= 0, place < k), found, -1)

    comp, skel_col = call(
        slots_kernel, scalars, [skel_first[0], skel_second[0]], [sds((1, k), jnp.int32), sds((k, 1), jnp.int32)]
    )

    def parts_kernel(sc, leaf_ref, end_out, side_out, *rows_outs):
        p = sc[0]
        end_out[...] = leaf_ref[:, 1 - p, :, pl.ds(pl.multiple_of(p * k, k), k)]
        side_out[...] = leaf_ref[:, 1 - p, :, 2 * k :]
        for i, rows_out in enumerate(rows_outs):
            rows_out[...] = leaf_ref[:, 2, i % 2 * hr : (i % 2 + 1) * hr, i // 2 * k : (i // 2 + 1) * k]

    end_own, sides_raw, *s_rows = call(
        parts_kernel, scalars, [leaf], [sds((2, fr, k), BF16)] * 2 + [sds((2, hr, k), BF16)] * 6
    )
    sides_sib = box_permute(sides_raw, 1)
    end_sib = box_permute(end_own, 1)
    s_sib = [box_permute(a, 1) for a in s_rows]

    def side_kernel(sc, own_ref, sib_ref, comp_ref, end_ref, side_out, send_out):
        p, q = sc[0], sc[1]
        pick_own = column_picker(comp_ref[...], p * k, k)
        pick_sib = column_picker(comp_ref[...], (1 - p) * k, k)
        side = dot(flat(own_ref[...]), pick_own) + dot(flat(sib_ref[...]), pick_sib)
        side_out[...] = side.astype(BF16).reshape(2, fr, k)
        send_out[...] = jnp.where(p == q, end_ref[...], side_out[...])

    side, first_send = call(
        side_kernel, scalars, [sides_raw, sides_sib, comp, end_own], [sds((2, fr, k), BF16)] * 2
    )
    first_far = over_face(first_send)

    def ends_kernel(sc, leaf_ref, comp_ref, keep_out, send_out, end_out):
        p = sc[0]
        pick_own = column_picker(comp_ref[...], p * k, k)
        for t in range(2):
            end_out[t, :, : 2 * k] = leaf_ref[t, p, :, : 2 * k]
            end_out[t, :, 2 * k :] = dot(leaf_ref[t, p, :, 2 * k :], pick_own).astype(BF16)
        couple = pl.ds(pl.multiple_of((1 - p) * k, k), k)
        for ref, take in zip((keep_out, send_out), halves(p)):
            ref[:, :, :k] = end_out[:, take, couple]
            ref[:, :, k:] = end_out[:, take, 2 * k :]

    v_keep, v_send, end_kept = call(
        ends_kernel, after(scalars, side), [leaf, comp],
        [sds((2, hr, 2 * k), BF16)] * 2 + [sds((2, fr, 3 * k), BF16)],
    )
    v_recv = box_permute(v_send, 1)

    w_one, w_two = w_first[:, 0], w_second[:, 0]
    w_one_sib = box_permute(after(w_one, side), 1)
    w_two_x = box_permute(after(w_two, side), 2)
    w_two_sib = box_permute(after(w_two, side), 1)
    w_two_x_sib = box_permute(w_two_x, 1)

    def weight_kernel(place, sc, *refs):
        out_ref = refs[-1]
        count = refs[0].shape[1]
        for i, ref in enumerate(refs[:-1]):
            take = pl.ds(pl.multiple_of(place(sc, i) * count, count), count)
            for f in range(n_face):
                @pl.when(sc[2] == f)
                def _(ref=ref, take=take, f=f):
                    out_ref[:, take, : k - f * fr] = ref[:, :, f * fr :]
                    if f > 0:
                        out_ref[:, take, k - f * fr :] = ref[:, :, : f * fr]

    (weight_one,) = call(
        functools.partial(weight_kernel, lambda sc, i: sc[0] ^ i), scalars, [w_one, w_one_sib],
        [sds((2, k, k), BF16)],
    )
    (weight_two,) = call(
        functools.partial(weight_kernel, lambda sc, i: sc[3] ^ (0, 2, 1, 3)[i]), scalars,
        [w_two, w_two_x, w_two_sib, w_two_x_sib], [sds((2, k, k), BF16)],
    )

    def rows_kernel(sc, *refs):
        owns, sibs, refs = refs[:6], refs[6:12], refs[12:]
        comp_ref, col_ref, end_ref, endsib_ref, rest_out, kept_out, *outs = refs
        p, q, f = sc[0], sc[1], sc[2]
        mine, _ = halves(p)
        rest_out[...] = jnp.where(p == q, endsib_ref[:, mine, :], end_ref[:, mine, :])
        pick_own = column_picker(comp_ref[...], p * k, k)
        pick_sib = column_picker(comp_ref[...], (1 - p) * k, k)

        def pick(slots, write):
            take_own = row_picker(slots, p * k + f * fr, fr)
            take_sib = row_picker(slots, (1 - p) * k + f * fr, fr)
            for t in range(2):
                for c in range(3):
                    own, sib = [
                        jnp.concatenate([a[2 * c][t], a[2 * c + 1][t]], axis=0) for a in (owns, sibs)
                    ]
                    if c == 2:
                        own, sib = [dot(a, b).astype(BF16) for a, b in ((own, pick_own), (sib, pick_sib))]
                    write(t, c, (dot(take_own, own) + dot(take_sib, sib)).astype(BF16))

        def write_far(s, t, c, picked):
            if c < 2:
                outs[s][t, :, c * k : (c + 1) * k] = picked
            else:
                outs[nf + s][t] = picked

        def col_half(s):
            start = (f + n_face - s - 1) % n_face * fr + p * hr
            return col_ref[pl.ds(pl.multiple_of(start, hr), hr), :]

        far = jnp.concatenate([col_half(s) for s in range(nf)], axis=0)

        @pl.when(p == q)
        def _():
            def write(t, c, picked):
                for s in range(nf):
                    write_far(s, t, c, picked[s * hr : (s + 1) * hr])

            pick(far, write)

        @pl.when(p != q)
        def _():
            def write(t, c, picked):
                kept_out[t, :, c * k : (c + 1) * k] = picked[:fr]
                for s in range(nf):
                    write_far(s, t, c, picked[fr + s * hr : fr + (s + 1) * hr])

            pick(jnp.concatenate([col_ref[pl.ds(pl.multiple_of(f * fr, fr), fr), :], far], axis=0), write)

    rest_send, kept, *kept_out = call(
        rows_kernel, scalars, [*s_rows, *s_sib, comp, skel_col, end_own, end_sib],
        [sds((2, hr, k), BF16), sds((2, fr, 3 * k), BF16)] + [sds((2, hr, 2 * k), BF16)] * nf
        + [sds((2, hr, k), BF16)] * nf, cost=ROWS_COST,
    )
    rest_far = over_face(rest_send)

    def piece(hidden, start, count):
        return stacked(hidden[0][:, start : start + count], hidden[1][:, start : start + count])

    def iface_kernel(sc, keep_ref, recv_ref, w_ref, end_ref, endsib_ref, side_ref,
                     acc_out, hid_out, rows):
        p, q = sc[0], sc[1]

        @pl.when(p == q)
        def _():
            rows[...] = recv_ref[...]

        @pl.when(p != q)
        def _():
            rows[...] = keep_ref[...]

        both = dot(stacked(rows[0, :, :k], rows[1, :, :k]), flat(w_ref[...])).astype(BF16)
        hidden = both[:hr], both[hr:]
        hid_out[0] = hidden[0]
        hid_out[1] = hidden[1]
        left = piece(hidden, 0, fr)
        is_end = p == q
        ends = jnp.where(is_end, end_ref[...], endsib_ref[...])
        acc_out[:, :, :k] = -dot(left, flat(ends)).reshape(2, hr, k)
        acc_out[:, :, k:] = rows[:, :, k:].astype(F32) - dot(left, flat(side_ref[...])).reshape(2, hr, k)

    v_acc, v_hid = call(
        iface_kernel, scalars, [v_keep, v_recv, weight_one, end_own, end_sib, side],
        [sds((2, hr, 2 * k), F32), sds((2, hr, k), BF16)],
        scratch=[pltpu.VMEM((2, hr, 2 * k), BF16)], cost=OWN_COST,
    )
    first_fwd = [box_permute(after(a, kept, w_two_x), 1) for a in first_far]

    def iface_far_kernel(sc, acc_ref, hid_ref, *rest):
        far, fwd, out_ref = rest[:nf], rest[nf : 2 * nf], rest[2 * nf]
        is_end = sc[0] == sc[1]
        hidden = [hid_ref[0], hid_ref[1]]
        total = acc_ref[...]
        for s in range(nf):
            left = piece(hidden, (s + 1) * fr, fr)
            mine, other = dot(left, flat(far[s][...])), dot(left, flat(fwd[s][...]))
            both = [jnp.where(is_end, mine, other), jnp.where(is_end, other, mine)]
            total = total - jnp.concatenate(both, axis=1).reshape(2, hr, 2 * k)
        out_ref[...] = total.astype(BF16)

    (two_own,) = call(
        iface_far_kernel, scalars, [v_acc, v_hid, *first_far, *first_fwd], [sds((2, hr, 2 * k), BF16)],
    )

    two_x = box_permute(two_own, 2)
    two_y = over_face(after(two_own, *rest_far))
    rest_fwd = [box_permute(after(a, two_own), 1) for a in rest_far]

    def weighted(w_ref, rows, out_ref):
        left = jnp.concatenate([piece((w_ref[0], w_ref[1]), s * fr, fr) for s in range(n_face)], axis=1)
        for c in range(3):
            cols = slice(c * k, (c + 1) * k)
            right = rows[:, :, :, cols].reshape(n_face * 2 * fr, k)
            out_ref[:, :, cols] = dot(left, right).astype(BF16).reshape(2, k, k)

    def weighted_one_kernel(sc, w_ref, own_ref, sib_ref, side_ref, *rest):
        refs = [rest[i * nf : (i + 1) * nf] for i in range(4)]
        out_ref, rows = rest[4 * nf :]
        p, q = sc[0], sc[1]
        is_end = p == q
        first_cols = pl.ds(pl.multiple_of(q * k, k), k)
        rest_cols = pl.ds(pl.multiple_of((1 - q) * k, k), k)
        rows[0, :, :, pl.ds(pl.multiple_of(p * k, k), k)] = own_ref[...]
        rows[0, :, :, pl.ds(pl.multiple_of((1 - p) * k, k), k)] = sib_ref[...]
        rows[0, :, :, 2 * k :] = side_ref[...]
        for s in range(nf):
            mine, other = refs[0][s][...], refs[1][s][...]
            rows[s + 1, :, :, first_cols] = jnp.where(is_end, mine, other)
            rows[s + 1, :, :, 2 * k :] = jnp.where(is_end, other, mine)
            for take, parts in zip(halves(p), refs[2:]):
                rows[s + 1, :, take, rest_cols] = parts[s][...]
        weighted(w_ref, rows, out_ref)

    (solved_one,) = call(
        weighted_one_kernel, scalars,
        [weight_one, end_own, end_sib, side, *first_far, *first_fwd, *rest_far, *rest_fwd],
        [sds((2, k, 3 * k), BF16)], scratch=[pltpu.VMEM((n_face, 2, fr, 3 * k), BF16)],
    )

    def join_kernel(sc, own_ref, x_ref, out_ref):
        q = sc[1]
        out_ref[:, :, pl.ds(pl.multiple_of(q * k, k), k)] = own_ref[:, :, :k]
        out_ref[:, :, pl.ds(pl.multiple_of((1 - q) * k, k), k)] = x_ref[:, :, :k]
        out_ref[:, :, 2 * k :] = own_ref[:, :, k:] + x_ref[:, :, k:]

    two_shape = [sds((2, hr, 3 * k), BF16)]
    two_rows = call(join_kernel, after(scalars, solved_one), [two_own, two_x], two_shape, cost=JOIN_COST)
    two_xy = [box_permute(after(a, *two_rows), 2) for a in two_y]
    for own, other in zip(two_y, two_xy):
        two_rows += call(join_kernel, after(scalars, weight_two), [own, other], two_shape)
    two_sib = [box_permute(a, 1) for a in two_rows]

    ends_far = [face_permute(after(a, two_own), i + 1) for i, a in enumerate(kept_out[:nf])]
    ends_fwd = [box_permute(a, 1) for a in ends_far]
    slots_far = [face_permute(after(a, two_own), i + 1) for i, a in enumerate(kept_out[nf:])]

    def whole_rows(sc, out_ref, cols, end_ref, kept_ref, far, fwd):
        p, q = sc[0], sc[1]

        @pl.when(p == q)
        def _():
            out_ref[...] = end_ref[:, :, cols]

        @pl.when(p != q)
        def _():
            for h, parts in enumerate((far, fwd)):
                take = pl.ds(pl.multiple_of((p ^ h) * hr, hr), hr)
                total = kept_ref[:, take, cols]
                for part in parts:
                    total = total + part[...]
                out_ref[:, take, :] = total

    def level_one_kernel(sc, end_ref, kept_ref, *refs):
        far, fwd = refs[:nf], refs[nf : 2 * nf]
        col_ref, one_ref, w_ref, hid_out, first_out, sub_out, zs = refs[2 * nf :]
        p, q, f = sc[0], sc[1], sc[2]
        whole_rows(sc, zs, slice(0, 2 * k), end_ref, kept_ref, far, fwd)
        slots = col_ref[pl.ds(pl.multiple_of(f * fr, fr), fr), :]
        right = jnp.where(slots >= k, 1, 0)
        right = jnp.where(p == q, p, right) > 0
        lefts = [zs[t, :, :k] for t in range(2)]
        rights = [zs[t, :, k:] for t in range(2)]
        left = stacked(*[jnp.where(right, a, b) for a, b in zip(lefts, rights)])
        nothing = jnp.zeros((fr, k), BF16)
        start = [
            jnp.concatenate([jnp.where(right, nothing, a) for a in lefts], axis=0),
            jnp.concatenate([jnp.where(right, a, nothing) for a in rights], axis=0),
        ]
        merged = [
            (start[c].astype(F32) - dot(left, flat(one_ref[:, :, c * k : (c + 1) * k]))).astype(BF16)
            for c in range(2)
        ]
        sub_out[...] = dot(left, flat(one_ref[:, :, 2 * k :]))
        is_left = q == 0
        first_out[...] = jnp.where(is_left, merged[0], merged[1])
        couple = jnp.where(is_left, merged[1], merged[0])
        second = dot(stacked(couple[:fr], couple[fr:]), flat(w_ref[...])).astype(BF16)
        for s in range(n_face):
            hid_out[s] = piece((second[:fr], second[fr:]), s * fr, fr)

    hid_two, first_two, sub_one = call(
        level_one_kernel, scalars,
        [end_kept, kept, *ends_far, *ends_fwd, skel_col, solved_one, weight_two],
        [sds((n_face, 2 * fr, 2 * fr), BF16), sds((2 * fr, k), BF16), sds((2 * fr, k), F32)],
        scratch=[pltpu.VMEM((2, fr, 2 * k), BF16)], cost=KEEP_COST,
    )

    slots_fwd = [box_permute(after(a, hid_two), 1) for a in slots_far]

    def level_two_kernel(sc, hid_ref, first_ref, *refs):
        out_ref, sub_out, rows, stage, sems = refs[2 * n_face :]
        p, q = sc[0], sc[1]
        left = jnp.concatenate([hid_ref[s] for s in range(n_face)], axis=1)
        for s in range(n_face):
            rows[s, :, pl.ds(pl.multiple_of(p * hr, hr), hr), :] = refs[s][...]
            rows[s, :, pl.ds(pl.multiple_of((1 - p) * hr, hr), hr), :] = refs[n_face + s][...]
        copies = []
        for c in range(2):
            first = jnp.where(q == c, first_ref[...], jnp.zeros((2 * fr, k), BF16)).astype(F32)
            right = rows[:, :, :, c * k : (c + 1) * k].reshape(n_face * 2 * fr, k)
            stage[c] = (first - dot(left, right)).astype(BF16).reshape(2, fr, k)
            copies.append(pltpu.make_async_copy(
                stage.at[c], out_ref.at[:, 0, :, pl.ds(c * k, k)], sems.at[c]
            ))
            copies[-1].start()
        sub_out[...] = dot(left, rows[:, :, :, 2 * k :].reshape(n_face * 2 * fr, k))
        for copy in copies:
            copy.wait()

    out, sub_two = call(
        level_two_kernel, scalars, [hid_two, first_two, *two_rows, *two_sib],
        [sds((2, 1, fr, 3 * k), BF16), sds((2 * fr, k), F32)],
        out_specs=[in_hbm, pl.BlockSpec(memory_space=pltpu.VMEM)],
        scratch=[pltpu.VMEM((n_face, 2, fr, 3 * k), BF16), pltpu.VMEM((2, 2, fr, k), BF16),
                 pltpu.SemaphoreType.DMA((2,))],
    )

    def slot_rows_kernel(sc, end_ref, kept_ref, *refs):
        whole_rows(sc, refs[2 * nf], slice(2 * k, 3 * k), end_ref, kept_ref, refs[:nf], refs[nf : 2 * nf])

    (slot_rows,) = call(
        slot_rows_kernel, scalars, [end_kept, kept, *slots_far, *slots_fwd], [sds((2, fr, k), BF16)], cost=SLOT_ROWS_COST
    )

    def finish_kernel(sc, rows_ref, one_ref, two_ref, _, out_ref, stage, sem):
        merged = (flat(rows_ref[...]).astype(F32) - one_ref[...]).astype(BF16)
        stage[...] = (merged.astype(F32) - two_ref[...]).astype(BF16).reshape(2, fr, k)
        copy = pltpu.make_async_copy(stage, out_ref.at[:, 0, :, pl.ds(2 * k, k)], sem.at[0])
        copy.start()
        copy.wait()

    (out,) = call(
        finish_kernel, scalars, [slot_rows, sub_one, sub_two, out], [sds((2, 1, fr, 3 * k), BF16)],
        specs=[pl.BlockSpec(memory_space=pltpu.VMEM)] * 3 + [in_hbm], out_specs=[in_hbm],
        scratch=[pltpu.VMEM((2, fr, k), BF16), pltpu.SemaphoreType.DMA((1,))], aliases={4: 0},
    )
    return out


def solution(mesh):
    return jax.shard_map(
        on_device,
        mesh=mesh,
        in_specs=(
            P(None, None, "box", None, "face", None),
            P(None, None, "box", None),
            P(None, None, "box", None),
            P(),
            P(),
        ),
        out_specs=P(None, None, ("box", "face"), None),
        check_vma=False,
    )
```

time: 77.6 us -> 74 us (0.954)
  Pallas kernels: 28.5 us -> 24 us
  waiting for transfers between devices: 22.1 us -> 26.3 us
  local copies, waits for them, and re-layouts: 6.57 us -> 2.44 us
  starting transfers between devices: 17.2 us -> 20.5 us
  other arithmetic: 2.51 us -> 0 us
    ppermute x6 -> x5, waiting for transfers between devices: 11.3 us -> 19.2 us  [face_permute(): return lax.ppermute(array, ('box', 'face'), pairs)]
    pallas_call x18 -> x16, Pallas kernels: 28.5 us -> 24 us  [call(): pl.pallas_call(kernel, in_specs=[pl.BlockSpec(memory_space=pltpu.SMEM)] +...]
    ppermute x17 -> x21, waiting for transfers between devices: 10.8 us -> 7.13 us  [box_permute(): return lax.ppermute(array, 'box', [(b, b ^ mask) for b in range(n_box)])]
    unnamed x10 -> x12, local copies, waits for them, and re-layouts: 5.83 us -> 2.36 us
    ppermute x17 -> x21, starting transfers between devices: 10.2 us -> 13.7 us  [box_permute(): return lax.ppermute(array, 'box', [(b, b ^ mask) for b in range(n_box)])]
    concatenate x2 -> x0, other arithmetic: 2.28 us -> none  [the longest x1 1.23 us: on_device(): w_one = jnp.roll(w_first[:, 0], -face * fr, axis=2)]
    ppermute x6 -> x5, starting transfers between devices: 6.96 us -> 6.85 us  [face_permute(): return lax.ppermute(array, ('box', 'face'), pairs)]
  transfers between devices with their start and end apart: 23 -> 26, of which waited for: 7 -> 11; matrix products, arithmetic and copies ran while one was open for 4% -> 0% of each run, Pallas kernels for 30% -> 26%
where the time goes in v9:
time: 74 us; the launch traced here: 73.6 us
  waiting for transfers between devices  26.3 us (36%)
  Pallas kernels  24 us (32%)
  starting transfers between devices  20.5 us (28%)
  local copies, waits for them, and re-layouts  2.44 us (3%)
    pallas_call x16, Pallas kernels, call(): pl.pallas_call(kernel, in_specs=[pl.BlockSpec(memory_space=pltpu.SMEM)] +...  24 us
    ppermute x5, waiting for transfers between devices, face_permute(): return lax.ppermute(array, ('box', 'face'), pairs)  19.2 us
    ppermute x21, starting transfers between devices, box_permute(): return lax.ppermute(array, 'box', [(b, b ^ mask) for b in range(n_box)])  13.7 us
    ppermute x21, waiting for transfers between devices, box_permute(): return lax.ppermute(array, 'box', [(b, b ^ mask) for b in range(n_box)])  7.13 us
    ppermute x5, starting transfers between devices, face_permute(): return lax.ppermute(array, ('box', 'face'), pairs)  6.85 us
    unnamed x12, local copies, waits for them, and re-layouts  2.36 us
  transfers between devices with their start and end apart: 26, of which 11 were waited for; matrix products, arithmetic and copies ran while one was open for 0% of the time, Pallas kernels for 26%

profile of v9, /device:TPU:1, one launch (start us, length us, event | category | flops | bytes accessed | tf_op | source)
XLA Modules:
  0.0 73.6 jit_solution(3078972289467575516)
XLA Ops:
  0.1 2.3 %copy-done = bf16[2,1,1,3,256,1536]{5,4,3,2,1,0:T(8,128)(2,1)S(1)} copy-done((bf16[2,1,1,3,256,1536]{5,4,3,2,1,0:T(8,128)(2,1)S(1)}, bf16[2,1,1,3,256,1536]{5,4,3,2,1,0:T(8,128)(2,1)}, u32[]{:S(2)}) %copy-start) | copy-done | bytes 4718616
  2.4 0.7 shard_map.55
  3.2 0.1 collective-permute-start
  3.3 0.5 collective-permute-start.1
  3.8 0.4 collective-permute-start.3
  4.3 0.8 %shard_map.56 = (s32[1,512]{1,0:T(1,128)S(1)}, s32[512,1]{1,0:T(8,128)S(1)}) custom-call(s32[6]{0:T(128)S(1)} %stack.27.sc, s32[8,512]{1,0:T(8,128)S(1)} %bitcast.18, s32[4,512]{1,0:T(4,128)S(1)} %bitcast.19), custom_call_target="tpu_custom_call" | custom-call | tf_op jit(solution)/shard_map/pallas_call | solution.py:48
  5.1 0.5 collective-permute-start.7
  5.6 1.3 %shard_map.57 = (bf16[2,256,512]{2,1,0:T(8,128)(2,1)S(1)}, bf16[2,256,512]{2,1,0:T(8,128)(2,1)S(1)}) custom-call(s32[6]{0:T(128)S(1)} %stack.27.sc, bf16[2,256,512]{2,1,0:T(8,128)(2,1)S(1)} %get-tuple-element.43.own_ref, bf16[2,256,512]{2,1,0:T(8,128)(2,1)S(1)} %collective-permute-done.sib_ref, s32[1,512]{1,0:T(1,128)S(1)} %get-tuple-element.44.comp_ref.refs_12_, ...), custom_call_target="tpu_custom_call" | custom-call | tf_op jit(solution)/shard_map/pallas_call | solution.py:48
  6.9 2.4 %collective-permute-start.10 = (bf16[2,256,512]{2,1,0:T(8,128)(2,1)S(1)}, bf16[2,256,512]{2,1,0:T(8,128)(2,1)S(1)}, u32[]{:S(2)}, u32[]{:S(2)}) collective-permute-start(bf16[2,256,512]{2,1,0:T(8,128)(2,1)S(1)} %get-tuple-element.63), channel_id=1, source_target_pairs={{0,1},{1,0},{2,3},{3,2},{4,5},{5,4},{6,7},{7,6},{8,9},{9,8},{10,11... | collective-permute-start | bytes 1572872 | tf_op jit(solution)/shard_map/ppermute | solution.py:86
  9.3 0.7 collective-permute-start.5
  10.1 1.3 %collective-permute-start.11 = (bf16[2,128,512]{2,1,0:T(8,128)(2,1)S(1)}, bf16[2,128,512]{2,1,0:T(8,128)(2,1)S(1)}, u32[]{:S(2)}, u32[]{:S(2)}) collective-permute-start(bf16[2,128,512]{2,1,0:T(8,128)(2,1)S(1)} %bitcast.15), channel_id=1, source_target_pairs={{0,4},{2,6},{4,0},{6,2},{8,12},{10,14},{12,8},{14,10},{16,20},{18,... | collective-permute-start | bytes 786440 | tf_op jit(solution)/shard_map/ppermute | solution.py:79
  11.4 1.1 %shard_map.58 = (bf16[2,128,1024]{2,1,0:T(8,128)(2,1)S(1)}, bf16[2,128,1024]{2,1,0:T(8,128)(2,1)S(1)}, bf16[2,256,1536]{2,1,0:T(8,128)(2,1)S(1)}) custom-call(s32[6]{0:T(128)S(1)} %stack.27.sc, bf16[2,3,256,1536]{3,2,1,0:T(8,128)(2,1)S(1)} %bitcast.12, s32[1,512]{1,0:T(1,128)S(1)} %get-tuple-element.44.comp_ref.refs_12_), custom_call_target="tpu_custom_call" | custom-call | tf_op jit(solution)/shard_map/pallas_call | solution.py:48
  12.5 0.8 %collective-permute-start.9 = (bf16[2,256,512]{2,1,0:T(8,128)(2,1)S(1)}, bf16[2,256,512]{2,1,0:T(8,128)(2,1)S(1)}, u32[]{:S(2)}, u32[]{:S(2)}) collective-permute-start(bf16[2,256,512]{2,1,0:T(8,128)(2,1)S(1)} %bitcast.13), channel_id=1, source_target_pairs={{0,2},{2,0},{4,6},{6,4},{8,10},{10,8},{12,14},{14,12},{16,18},{18,... | collective-permute-start | bytes 1572872 | tf_op jit(solution)/shard_map/ppermute | solution.py:79
  13.3 0.1 collective-permute-start.8
  13.4 2.9 %shard_map.59 = (bf16[2,128,512]{2,1,0:T(8,128)(2,1)S(1)}, bf16[2,256,1536]{2,1,0:T(8,128)(2,1)S(1)}, bf16[2,128,1024]{2,1,0:T(8,128)(2,1)S(1)}, bf16[2,128,512]{2,1,0:T(8,128)(2,1)S(1)}) custom-call(s32[6]{0:T(128)S(1)} %stack.27.sc, bf16[2,128,512]{2,1,0:T(8,128)(2,1)S(1)} %get-tuple-element.49.refs_0_, ...), custom_call_target="tpu_custom_call" | custom-call | tf_op jit(solution)/shard_map/pallas_call | solution.py:48
  16.3 1.3 %collective-permute-done.11.refs_1_ = bf16[2,128,512]{2,1,0:T(8,128)(2,1)S(1)} collective-permute-done((bf16[2,128,512]{2,1,0:T(8,128)(2,1)S(1)}, bf16[2,128,512]{2,1,0:T(8,128)(2,1)S(1)}, u32[]{:S(2)}, u32[]{:S(2)}) %collective-permute-start.11) | collective-permute-done | bytes 262176 | tf_op jit(solution)/shard_map/ppermute | solution.py:79
  17.6 3.6 %collective-permute-done.10.rest_0_ = bf16[2,256,512]{2,1,0:T(8,128)(2,1)S(1)} collective-permute-done((bf16[2,256,512]{2,1,0:T(8,128)(2,1)S(1)}, bf16[2,256,512]{2,1,0:T(8,128)(2,1)S(1)}, u32[]{:S(2)}, u32[]{:S(2)}) %collective-permute-start.10) | collective-permute-done | bytes 524320 | tf_op jit(solution)/shard_map/ppermute | solution.py:86
  21.2 1.0 %collective-permute-start.12 = (bf16[2,256,512]{2,1,0:T(8,128)(2,1)S(1)}, bf16[2,256,512]{2,1,0:T(8,128)(2,1)S(1)}, u32[]{:S(2)}, u32[]{:S(2)}) collective-permute-start(bf16[2,256,512]{2,1,0:T(8,128)(2,1)S(1)} %collective-permute-done.10.rest_0_), channel_id=1, source_target_pairs={{0,2},{2,0},{4,6},{6,4},{8,10},{10,8},{12,14},{14,12},{16,18},{18,... | collective-permute-start | bytes 1572872 | tf_op jit(solution)/shard_map/ppermute | solution.py:79
  22.2 1.5 %collective-permute-start.16 = (bf16[2,128,512]{2,1,0:T(8,128)(2,1)S(1)}, bf16[2,128,512]{2,1,0:T(8,128)(2,1)S(1)}, u32[]{:S(2)}, u32[]{:S(2)}) collective-permute-start(bf16[2,128,512]{2,1,0:T(8,128)(2,1)S(1)} %get-tuple-element.69), channel_id=1, source_target_pairs={{0,1},{1,0},{2,3},{3,2},{4,5},{5,4},{6,7},{7,6},{8,9},{9,8},{10,11... | collective-permute-start | bytes 786440 | tf_op jit(solution)/shard_map/ppermute | solution.py:86
  23.6 0.6 shard_map.60.w_ref
  24.3 1.4 %shard_map.61 = (f32[2,128,1024]{2,1,0:T(8,128)S(1)}, bf16[2,128,512]{2,1,0:T(8,128)(2,1)S(1)}) custom-call(s32[6]{0:T(128)S(1)} %stack.27.sc, bf16[2,128,1024]{2,1,0:T(8,128)(2,1)S(1)} %get-tuple-element.58.keep_ref, bf16[2,128,1024]{2,1,0:T(8,128)(2,1)S(1)} %collective-permute-done.8.recv_ref, bf16[2,512,512]{2,1,0:T(8,128)(2,1)S(1)} %shard_map.60.w_ref, ...), custom_call_target="tpu_custom_call" | custom-call | flops 1000000000 | tf_op jit(solution)/shard_map/pallas_call | solution.py:48
  25.7 1.0 %shard_map.62.own_ref = bf16[2,128,1024]{2,1,0:T(8,128)(2,1)S(1)} custom-call(s32[6]{0:T(128)S(1)} %stack.27.sc, f32[2,128,1024]{2,1,0:T(8,128)S(1)} %get-tuple-element.61.acc_ref, bf16[2,128,512]{2,1,0:T(8,128)(2,1)S(1)} %get-tuple-element.62.hid_ref, bf16[2,256,512]{2,1,0:T(8,128)(2,1)S(1)} %collective-permute-done.10.rest_0_, ...), custom_call_target="tpu_custom_call" | custom-call | tf_op jit(solution)/shard_map/pallas_call | solution.py:48
  26.7 1.3 %collective-permute-start.21 = (bf16[2,128,1024]{2,1,0:T(8,128)(2,1)S(1)}, bf16[2,128,1024]{2,1,0:T(8,128)(2,1)S(1)}, u32[]{:S(2)}, u32[]{:S(2)}) collective-permute-start(bf16[2,128,1024]{2,1,0:T(8,128)(2,1)S(1)} %shard_map.62.own_ref), channel_id=1, source_target_pairs={{0,4},{2,6},{4,0},{6,2},{8,12},{10,14},{12,8},{14,10},{16,20},{18,... | collective-permute-start | bytes 1572872 | tf_op jit(solution)/shard_map/ppermute | solution.py:79
  28.0 2.1 %collective-permute-done.16.rest_2_ = bf16[2,128,512]{2,1,0:T(8,128)(2,1)S(1)} collective-permute-done((bf16[2,128,512]{2,1,0:T(8,128)(2,1)S(1)}, bf16[2,128,512]{2,1,0:T(8,128)(2,1)S(1)}, u32[]{:S(2)}, u32[]{:S(2)}) %collective-permute-start.16) | collective-permute-done | bytes 262176 | tf_op jit(solution)/shard_map/ppermute | solution.py:86
  30.1 1.5 %collective-permute-start.22 = (bf16[2,128,1024]{2,1,0:T(8,128)(2,1)S(1)}, bf16[2,128,1024]{2,1,0:T(8,128)(2,1)S(1)}, u32[]{:S(2)}, u32[]{:S(2)}) collective-permute-start(bf16[2,128,1024]{2,1,0:T(8,128)(2,1)S(1)} %shard_map.62.own_ref), channel_id=1, source_target_pairs={{0,1},{1,0},{2,3},{3,2},{4,5},{5,4},{6,7},{7,6},{8,9},{9,8},{10,11... | collective-permute-start | bytes 1572872 | tf_op jit(solution)/shard_map/ppermute | solution.py:86
  31.6 1.3 %collective-permute-start.17 = (bf16[2,128,512]{2,1,0:T(8,128)(2,1)S(1)}, bf16[2,128,512]{2,1,0:T(8,128)(2,1)S(1)}, u32[]{:S(2)}, u32[]{:S(2)}) collective-permute-start(bf16[2,128,512]{2,1,0:T(8,128)(2,1)S(1)} %collective-permute-done.16.rest_2_), channel_id=1, source_target_pairs={{0,2},{2,0},{4,6},{6,4},{8,10},{10,8},{12,14},{14,12},{16,18},{18,... | collective-permute-start | bytes 786440 | tf_op jit(solution)/shard_map/ppermute | solution.py:79
  32.9 1.2 %collective-permute-done.17.rest_3_ = bf16[2,128,512]{2,1,0:T(8,128)(2,1)S(1)} collective-permute-done((bf16[2,128,512]{2,1,0:T(8,128)(2,1)S(1)}, bf16[2,128,512]{2,1,0:T(8,128)(2,1)S(1)}, u32[]{:S(2)}, u32[]{:S(2)}) %collective-permute-start.17) | collective-permute-done | bytes 262176 | tf_op jit(solution)/shard_map/ppermute | solution.py:79
  34.1 4.2 %shard_map.63.refs_3_ = bf16[2,512,1536]{2,1,0:T(8,128)(2,1)S(1)} custom-call(s32[6]{0:T(128)S(1)} %stack.27.sc, bf16[2,512,512]{2,1,0:T(8,128)(2,1)S(1)} %shard_map.60.w_ref, bf16[2,256,512]{2,1,0:T(8,128)(2,1)S(1)} %get-tuple-element.45.end_ref.refs_14_.own_ref, bf16[2,256,512]{2,1,0:T(8,128)(2,1)S(1)} %collective-permute-done.7.refs_15_.endsib_ref.sib_ref, ...), custom_call_target="tpu_custom_call" | custom-call | tf_op jit(solution)/shard_map/pallas_call | solution.py:48
  38.3 1.7 %collective-permute-done.21.x_ref = bf16[2,128,1024]{2,1,0:T(8,128)(2,1)S(1)} collective-permute-done((bf16[2,128,1024]{2,1,0:T(8,128)(2,1)S(1)}, bf16[2,128,1024]{2,1,0:T(8,128)(2,1)S(1)}, u32[]{:S(2)}, u32[]{:S(2)}) %collective-permute-start.21) | collective-permute-done | bytes 524320 | tf_op jit(solution)/shard_map/ppermute | solution.py:79
  40.0 0.6 shard_map.67.refs_0_
  40.6 2.1 %collective-permute-done.22.own_ref = bf16[2,128,1024]{2,1,0:T(8,128)(2,1)S(1)} collective-permute-done((bf16[2,128,1024]{2,1,0:T(8,128)(2,1)S(1)}, bf16[2,128,1024]{2,1,0:T(8,128)(2,1)S(1)}, u32[]{:S(2)}, u32[]{:S(2)}) %collective-permute-start.22) | collective-permute-done | bytes 524320 | tf_op jit(solution)/shard_map/ppermute | solution.py:86
  42.8 1.4 %collective-permute-start.23 = (bf16[2,128,1024]{2,1,0:T(8,128)(2,1)S(1)}, bf16[2,128,1024]{2,1,0:T(8,128)(2,1)S(1)}, u32[]{:S(2)}, u32[]{:S(2)}) collective-permute-start(bf16[2,128,1024]{2,1,0:T(8,128)(2,1)S(1)} %collective-permute-done.22.own_ref), channel_id=1, source_target_pairs={{0,4},{2,6},{4,0},{6,2},{8,12},{10,14},{12,8},{14,10},{16,20},{18,... | collective-permute-start | bytes 1572872 | tf_op jit(solution)/shard_map/ppermute | solution.py:79
  44.2 9.8 %collective-permute-done.14.refs_0_ = bf16[2,128,1024]{2,1,0:T(8,128)(2,1)S(1)} collective-permute-done((bf16[2,128,1024]{2,1,0:T(8,128)(2,1)S(1)}, bf16[2,128,1024]{2,1,0:T(8,128)(2,1)S(1)}, u32[]{:S(2)}, u32[]{:S(2)}) %collective-permute-start.14) | collective-permute-done | bytes 524320 | tf_op jit(solution)/shard_map/ppermute | solution.py:86
  54.0 1.7 %collective-permute-start.15 = (bf16[2,128,1024]{2,1,0:T(8,128)(2,1)S(1)}, bf16[2,128,1024]{2,1,0:T(8,128)(2,1)S(1)}, u32[]{:S(2)}, u32[]{:S(2)}) collective-permute-start(bf16[2,128,1024]{2,1,0:T(8,128)(2,1)S(1)} %collective-permute-done.14.refs_0_), channel_id=1, source_target_pairs={{0,2},{2,0},{4,6},{6,4},{8,10},{10,8},{12,14},{14,12},{16,18},{18,... | collective-permute-start | bytes 1572872 | tf_op jit(solution)/shard_map/ppermute | solution.py:79
  55.7 0.5 collective-permute-start.19
  56.2 1.4 %collective-permute-done.18.refs_2_ = bf16[2,128,512]{2,1,0:T(8,128)(2,1)S(1)} collective-permute-done((bf16[2,128,512]{2,1,0:T(8,128)(2,1)S(1)}, bf16[2,128,512]{2,1,0:T(8,128)(2,1)S(1)}, u32[]{:S(2)}, u32[]{:S(2)}) %collective-permute-start.18) | collective-permute-done | bytes 262176 | tf_op jit(solution)/shard_map/ppermute | solution.py:79
  57.6 0.4 collective-permute-done.19.refs_3_
  58.0 0.7 shard_map.64.refs_4_
  58.7 1.5 %collective-permute-start.13 = (bf16[2,128,512]{2,1,0:T(8,128)(2,1)S(1)}, bf16[2,128,512]{2,1,0:T(8,128)(2,1)S(1)}, u32[]{:S(2)}, u32[]{:S(2)}) collective-permute-start(bf16[2,128,512]{2,1,0:T(8,128)(2,1)S(1)} %get-tuple-element.66), channel_id=1, source_target_pairs={{0,1},{1,0},{2,3},{3,2},{4,5},{5,4},{6,7},{7,6},{8,9},{9,8},{10,11... | collective-permute-start | bytes 786440 | tf_op jit(solution)/shard_map/ppermute | solution.py:86
  60.2 0.7 collective-permute-start.24
  60.8 0.6 shard_map.68.refs_1_
  61.5 3.2 %shard_map.65 = (bf16[2,512,512]{2,1,0:T(8,128)(2,1)S(1)}, bf16[512,512]{1,0:T(8,128)(2,1)S(1)}, f32[512,512]{1,0:T(8,128)S(1)}) custom-call(s32[6]{0:T(128)S(1)} %stack.27.sc, bf16[2,256,1536]{2,1,0:T(8,128)(2,1)S(1)} %get-tuple-element.48.end_ref, bf16[2,256,1536]{2,1,0:T(8,128)(2,1)S(1)} %get-tuple-element.56.kept_ref, ...), custom_call_target="tpu_custom_call" | custom-call | flops 6000000000 | tf_op jit(solution)/shard_map/pallas_call | solution.py:48
  64.7 1.5 %collective-permute-done.13.refs_0_ = bf16[2,128,512]{2,1,0:T(8,128)(2,1)S(1)} collective-permute-done((bf16[2,128,512]{2,1,0:T(8,128)(2,1)S(1)}, bf16[2,128,512]{2,1,0:T(8,128)(2,1)S(1)}, u32[]{:S(2)}, u32[]{:S(2)}) %collective-permute-start.13) | collective-permute-done | bytes 262176 | tf_op jit(solution)/shard_map/ppermute | solution.py:86
  66.2 1.2 %collective-permute-start.20 = (bf16[2,128,512]{2,1,0:T(8,128)(2,1)S(1)}, bf16[2,128,512]{2,1,0:T(8,128)(2,1)S(1)}, u32[]{:S(2)}, u32[]{:S(2)}) collective-permute-start(bf16[2,128,512]{2,1,0:T(8,128)(2,1)S(1)} %collective-permute-done.13.refs_0_), channel_id=1, source_target_pairs={{0,2},{2,0},{4,6},{6,4},{8,10},{10,8},{12,14},{14,12},{16,18},{18,... | collective-permute-start | bytes 786440 | tf_op jit(solution)/shard_map/ppermute | solution.py:79
  67.4 1.2 %collective-permute-done.20.refs_1_ = bf16[2,128,512]{2,1,0:T(8,128)(2,1)S(1)} collective-permute-done((bf16[2,128,512]{2,1,0:T(8,128)(2,1)S(1)}, bf16[2,128,512]{2,1,0:T(8,128)(2,1)S(1)}, u32[]{:S(2)}, u32[]{:S(2)}) %collective-permute-start.20) | collective-permute-done | bytes 262176 | tf_op jit(solution)/shard_map/ppermute | solution.py:79
  68.6 0.6 shard_map.66.rows_ref
  69.2 2.8 %shard_map.69 = (bf16[2,1,256,1536]{3,2,1,0:T(8,128)(2,1)}, f32[512,512]{1,0:T(8,128)S(1)}) custom-call(s32[6]{0:T(128)S(1)} %stack.27.sc, bf16[2,512,512]{2,1,0:T(8,128)(2,1)S(1)} %get-tuple-element.71.hid_ref, bf16[512,512]{1,0:T(8,128)(2,1)S(1)} %get-tuple-element.74.first_ref, bf16[2,128,1536]{2,1,0:T(8,128)(2,1)S(1)} %shard_map.67.refs_0_, ...), custom_call_target="tpu_custom_call" | custom-call | tf_op jit(solution)/shard_map/pallas_call | solution.py:48
  72.1 1.5 %shard_map.70 = bf16[2,1,256,1536]{3,2,1,0:T(8,128)(2,1)} custom-call(s32[6]{0:T(128)S(1)} %stack.27.sc, bf16[2,256,512]{2,1,0:T(8,128)(2,1)S(1)} %shard_map.66.rows_ref, f32[512,512]{1,0:T(8,128)S(1)} %get-tuple-element.73.one_ref, f32[512,512]{1,0:T(8,128)S(1)} %get-tuple-element.79.two_ref, ...), custom_call_target="tpu_custom_call", output_to_operand_aliasing={{}: (4, {})} | custom-call | tf_op jit(solution)/shard_map/pallas_call | solution.py:48
  (33 shorter events, 0.5 us)
Async XLA Ops:
  0.0 4.3 %copy-start.4 = (s32[1,8,512]{2,1,0:T(8,128)S(1)}, s32[1,8,512]{2,1,0:T(8,128)}, u32[]{:S(2)}) copy-start(s32[1,8,512]{2,1,0:T(8,128)} %param.8) | copy-start | bytes 49156
  0.1 2.3 %copy-start = (bf16[2,1,1,3,256,1536]{5,4,3,2,1,0:T(8,128)(2,1)S(1)}, bf16[2,1,1,3,256,1536]{5,4,3,2,1,0:T(8,128)(2,1)}, u32[]{:S(2)}) copy-start(bf16[2,1,1,3,256,1536]{5,4,3,2,1,0:T(8,128)(2,1)} %param.5) | copy-start | bytes 14155780
  2.4 1.9 %copy-start.5 = (s32[1,4,512]{2,1,0:T(4,128)S(1)}, s32[1,4,512]{2,1,0:T(4,128)}, u32[]{:S(2)}) copy-start(s32[1,4,512]{2,1,0:T(4,128)} %param.9) | copy-start | bytes 24580
  2.4 8.9 %copy-start.1 = (bf16[2,1,1,3,256,1536]{5,4,3,2,1,0:T(8,128)(2,1)S(1)}, bf16[2,1,1,3,256,1536]{5,4,3,2,1,0:T(8,128)(2,1)}, u32[]{:S(2)}) copy-start(bf16[2,1,1,3,256,1536]{5,4,3,2,1,0:T(8,128)(2,1)} %param.5) | copy-start | bytes 14155780
  3.1 6.9 %copy-start.3 = (bf16[2,1,128,512]{3,2,1,0:T(8,128)(2,1)S(1)}, bf16[2,1,128,512]{3,2,1,0:T(8,128)(2,1)}, u32[]{:S(2)}) copy-start(bf16[2,1,128,512]{3,2,1,0:T(8,128)(2,1)} %param.7) | copy-start | bytes 786436
  3.2 2.0 %collective-permute-start = (bf16[2,256,512]{2,1,0:T(8,128)(2,1)S(1)}, bf16[2,256,512]{2,1,0:T(8,128)(2,1)S(1)}, u32[]{:S(2)}, u32[]{:S(2)}) collective-permute-start(bf16[2,256,512]{2,1,0:T(8,128)(2,1)S(1)} %get-tuple-element.43.own_ref), channel_id=1, source_target_pairs={{0,2},{2,0},{4,6},{6,4},{8,10},{10,8},{12,14},{14,12},{16,18},{18,... | collective-permute-start | bytes 1572872 | tf_op jit(solution)/shard_map/ppermute | solution.py:79
  3.3 3.6 %collective-permute-start.1 = (bf16[2,128,512]{2,1,0:T(8,128)(2,1)S(1)}, bf16[2,128,512]{2,1,0:T(8,128)(2,1)S(1)}, u32[]{:S(2)}, u32[]{:S(2)}) collective-permute-start(bf16[2,128,512]{2,1,0:T(8,128)(2,1)S(1)} %get-tuple-element.49.refs_0_), channel_id=1, source_target_pairs={{0,2},{2,0},{4,6},{6,4},{8,10},{10,8},{12,14},{14,12},{16,18},{18,... | collective-permute-start | bytes 786440 | tf_op jit(solution)/shard_map/ppermute | solution.py:79
  3.7 5.6 %collective-permute-start.2 = (bf16[2,128,512]{2,1,0:T(8,128)(2,1)S(1)}, bf16[2,128,512]{2,1,0:T(8,128)(2,1)S(1)}, u32[]{:S(2)}, u32[]{:S(2)}) collective-permute-start(bf16[2,128,512]{2,1,0:T(8,128)(2,1)S(1)} %get-tuple-element.50.refs_1_), channel_id=1, source_target_pairs={{0,2},{2,0},{4,6},{6,4},{8,10},{10,8},{12,14},{14,12},{16,18},{18,... | collective-permute-start | bytes 786440 | tf_op jit(solution)/shard_map/ppermute | solution.py:79
  3.8 6.2 %collective-permute-start.3 = (bf16[2,128,512]{2,1,0:T(8,128)(2,1)S(1)}, bf16[2,128,512]{2,1,0:T(8,128)(2,1)S(1)}, u32[]{:S(2)}, u32[]{:S(2)}) collective-permute-start(bf16[2,128,512]{2,1,0:T(8,128)(2,1)S(1)} %get-tuple-element.51.refs_2_), channel_id=1, source_target_pairs={{0,2},{2,0},{4,6},{6,4},{8,10},{10,8},{12,14},{14,12},{16,18},{18,... | collective-permute-start | bytes 786440 | tf_op jit(solution)/shard_map/ppermute | solution.py:79
  4.2 5.8 %collective-permute-start.4 = (bf16[2,128,512]{2,1,0:T(8,128)(2,1)S(1)}, bf16[2,128,512]{2,1,0:T(8,128)(2,1)S(1)}, u32[]{:S(2)}, u32[]{:S(2)}) collective-permute-start(bf16[2,128,512]{2,1,0:T(8,128)(2,1)S(1)} %get-tuple-element.52.refs_3_), channel_id=1, source_target_pairs={{0,2},{2,0},{4,6},{6,4},{8,10},{10,8},{12,14},{14,12},{16,18},{18,... | collective-permute-start | bytes 786440 | tf_op jit(solution)/shard_map/ppermute | solution.py:79
  5.1 8.2 %collective-permute-start.7 = (bf16[2,256,512]{2,1,0:T(8,128)(2,1)S(1)}, bf16[2,256,512]{2,1,0:T(8,128)(2,1)S(1)}, u32[]{:S(2)}, u32[]{:S(2)}) collective-permute-start(bf16[2,256,512]{2,1,0:T(8,128)(2,1)S(1)} %get-tuple-element.45.end_ref.refs_14_.own_ref), channel_id=1, source_target_pairs={{0,2},{2,0},{4,6},{6,4},{8,10},{10,8},{12,14},{14,12},{16,18},{18,... | collective-permute-start | bytes 1572872 | tf_op jit(solution)/shard_map/ppermute | solution.py:79
  6.9 14.3 %collective-permute-start.10 = (bf16[2,256,512]{2,1,0:T(8,128)(2,1)S(1)}, bf16[2,256,512]{2,1,0:T(8,128)(2,1)S(1)}, u32[]{:S(2)}, u32[]{:S(2)}) collective-permute-start(bf16[2,256,512]{2,1,0:T(8,128)(2,1)S(1)} %get-tuple-element.63), channel_id=1, source_target_pairs={{0,1},{1,0},{2,3},{3,2},{4,5},{5,4},{6,7},{7,6},{8,9},{9,8},{10,11... | collective-permute-start | bytes 1572872 | tf_op jit(solution)/shard_map/ppermute | solution.py:86
  9.3 3.2 %collective-permute-start.5 = (bf16[2,128,512]{2,1,0:T(8,128)(2,1)S(1)}, bf16[2,128,512]{2,1,0:T(8,128)(2,1)S(1)}, u32[]{:S(2)}, u32[]{:S(2)}) collective-permute-start(bf16[2,128,512]{2,1,0:T(8,128)(2,1)S(1)} %get-tuple-element.53.refs_4_), channel_id=1, source_target_pairs={{0,2},{2,0},{4,6},{6,4},{8,10},{10,8},{12,14},{14,12},{16,18},{18,... | collective-permute-start | bytes 786440 | tf_op jit(solution)/shard_map/ppermute | solution.py:79
  10.0 3.3 %collective-permute-start.6 = (bf16[2,128,512]{2,1,0:T(8,128)(2,1)S(1)}, bf16[2,128,512]{2,1,0:T(8,128)(2,1)S(1)}, u32[]{:S(2)}, u32[]{:S(2)}) collective-permute-start(bf16[2,128,512]{2,1,0:T(8,128)(2,1)S(1)} %get-tuple-element.54.refs_5_), channel_id=1, source_target_pairs={{0,2},{2,0},{4,6},{6,4},{8,10},{10,8},{12,14},{14,12},{16,18},{18,... | collective-permute-start | bytes 786440 | tf_op jit(solution)/shard_map/ppermute | solution.py:79
  10.1 2.4 %copy-start.2 = (bf16[2,1,256,512]{3,2,1,0:T(8,128)(2,1)S(1)}, bf16[2,1,256,512]{3,2,1,0:T(8,128)(2,1)}, u32[]{:S(2)}) copy-start(bf16[2,1,256,512]{3,2,1,0:T(8,128)(2,1)} %param.6) | copy-start | bytes 1572868
  10.1 7.5 %collective-permute-start.11 = (bf16[2,128,512]{2,1,0:T(8,128)(2,1)S(1)}, bf16[2,128,512]{2,1,0:T(8,128)(2,1)S(1)}, u32[]{:S(2)}, u32[]{:S(2)}) collective-permute-start(bf16[2,128,512]{2,1,0:T(8,128)(2,1)S(1)} %bitcast.15), channel_id=1, source_target_pairs={{0,4},{2,6},{4,0},{6,2},{8,12},{10,14},{12,8},{14,10},{16,20},{18,... | collective-permute-start | bytes 786440 | tf_op jit(solution)/shard_map/ppermute | solution.py:79
  12.5 11.1 %collective-permute-start.9 = (bf16[2,256,512]{2,1,0:T(8,128)(2,1)S(1)}, bf16[2,256,512]{2,1,0:T(8,128)(2,1)S(1)}, u32[]{:S(2)}, u32[]{:S(2)}) collective-permute-start(bf16[2,256,512]{2,1,0:T(8,128)(2,1)S(1)} %bitcast.13), channel_id=1, source_target_pairs={{0,2},{2,0},{4,6},{6,4},{8,10},{10,8},{12,14},{14,12},{16,18},{18,... | collective-permute-start | bytes 1572872 | tf_op jit(solution)/shard_map/ppermute | solution.py:79
  13.3 11.0 %collective-permute-start.8 = (bf16[2,128,1024]{2,1,0:T(8,128)(2,1)S(1)}, bf16[2,128,1024]{2,1,0:T(8,128)(2,1)S(1)}, u32[]{:S(2)}, u32[]{:S(2)}) collective-permute-start(bf16[2,128,1024]{2,1,0:T(8,128)(2,1)S(1)} %get-tuple-element.59), channel_id=1, source_target_pairs={{0,2},{2,0},{4,6},{6,4},{8,10},{10,8},{12,14},{14,12},{16,18},{18,... | collective-permute-start | bytes 1572872 | tf_op jit(solution)/shard_map/ppermute | solution.py:79
  21.2 4.5 %collective-permute-start.12 = (bf16[2,256,512]{2,1,0:T(8,128)(2,1)S(1)}, bf16[2,256,512]{2,1,0:T(8,128)(2,1)S(1)}, u32[]{:S(2)}, u32[]{:S(2)}) collective-permute-start(bf16[2,256,512]{2,1,0:T(8,128)(2,1)S(1)} %collective-permute-done.10.rest_0_), channel_id=1, source_target_pairs={{0,2},{2,0},{4,6},{6,4},{8,10},{10,8},{12,14},{14,12},{16,18},{18,... | collective-permute-start | bytes 1572872 | tf_op jit(solution)/shard_map/ppermute | solution.py:79
  22.2 7.9 %collective-permute-start.16 = (bf16[2,128,512]{2,1,0:T(8,128)(2,1)S(1)}, bf16[2,128,512]{2,1,0:T(8,128)(2,1)S(1)}, u32[]{:S(2)}, u32[]{:S(2)}) collective-permute-start(bf16[2,128,512]{2,1,0:T(8,128)(2,1)S(1)} %get-tuple-element.69), channel_id=1, source_target_pairs={{0,1},{1,0},{2,3},{3,2},{4,5},{5,4},{6,7},{7,6},{8,9},{9,8},{10,11... | collective-permute-start | bytes 786440 | tf_op jit(solution)/shard_map/ppermute | solution.py:86
  26.7 13.3 %collective-permute-start.21 = (bf16[2,128,1024]{2,1,0:T(8,128)(2,1)S(1)}, bf16[2,128,1024]{2,1,0:T(8,128)(2,1)S(1)}, u32[]{:S(2)}, u32[]{:S(2)}) collective-permute-start(bf16[2,128,1024]{2,1,0:T(8,128)(2,1)S(1)} %shard_map.62.own_ref), channel_id=1, source_target_pairs={{0,4},{2,6},{4,0},{6,2},{8,12},{10,14},{12,8},{14,10},{16,20},{18,... | collective-permute-start | bytes 1572872 | tf_op jit(solution)/shard_map/ppermute | solution.py:79
  30.1 12.7 %collective-permute-start.22 = (bf16[2,128,1024]{2,1,0:T(8,128)(2,1)S(1)}, bf16[2,128,1024]{2,1,0:T(8,128)(2,1)S(1)}, u32[]{:S(2)}, u32[]{:S(2)}) collective-permute-start(bf16[2,128,1024]{2,1,0:T(8,128)(2,1)S(1)} %shard_map.62.own_ref), channel_id=1, source_target_pairs={{0,1},{1,0},{2,3},{3,2},{4,5},{5,4},{6,7},{7,6},{8,9},{9,8},{10,11... | collective-permute-start | bytes 1572872 | tf_op jit(solution)/shard_map/ppermute | solution.py:86
  31.6 22.4 %collective-permute-start.14 = (bf16[2,128,1024]{2,1,0:T(8,128)(2,1)S(1)}, bf16[2,128,1024]{2,1,0:T(8,128)(2,1)S(1)}, u32[]{:S(2)}, u32[]{:S(2)}) collective-permute-start(bf16[2,128,1024]{2,1,0:T(8,128)(2,1)S(1)} %get-tuple-element.68), channel_id=1, source_target_pairs={{0,1},{1,0},{2,3},{3,2},{4,5},{5,4},{6,7},{7,6},{8,9},{9,8},{10,11... | collective-permute-start | bytes 1572872 | tf_op jit(solution)/shard_map/ppermute | solution.py:86
  31.6 2.5 %collective-permute-start.17 = (bf16[2,128,512]{2,1,0:T(8,128)(2,1)S(1)}, bf16[2,128,512]{2,1,0:T(8,128)(2,1)S(1)}, u32[]{:S(2)}, u32[]{:S(2)}) collective-permute-start(bf16[2,128,512]{2,1,0:T(8,128)(2,1)S(1)} %collective-permute-done.16.rest_2_), channel_id=1, source_target_pairs={{0,2},{2,0},{4,6},{6,4},{8,10},{10,8},{12,14},{14,12},{16,18},{18,... | collective-permute-start | bytes 786440 | tf_op jit(solution)/shard_map/ppermute | solution.py:79
  42.8 18.0 %collective-permute-start.23 = (bf16[2,128,1024]{2,1,0:T(8,128)(2,1)S(1)}, bf16[2,128,1024]{2,1,0:T(8,128)(2,1)S(1)}, u32[]{:S(2)}, u32[]{:S(2)}) collective-permute-start(bf16[2,128,1024]{2,1,0:T(8,128)(2,1)S(1)} %collective-permute-done.22.own_ref), channel_id=1, source_target_pairs={{0,4},{2,6},{4,0},{6,2},{8,12},{10,14},{12,8},{14,10},{16,20},{18,... | collective-permute-start | bytes 1572872 | tf_op jit(solution)/shard_map/ppermute | solution.py:79
  54.0 7.5 %collective-permute-start.15 = (bf16[2,128,1024]{2,1,0:T(8,128)(2,1)S(1)}, bf16[2,128,1024]{2,1,0:T(8,128)(2,1)S(1)}, u32[]{:S(2)}, u32[]{:S(2)}) collective-permute-start(bf16[2,128,1024]{2,1,0:T(8,128)(2,1)S(1)} %collective-permute-done.14.refs_0_), channel_id=1, source_target_pairs={{0,2},{2,0},{4,6},{6,4},{8,10},{10,8},{12,14},{14,12},{16,18},{18,... | collective-permute-start | bytes 1572872 | tf_op jit(solution)/shard_map/ppermute | solution.py:79
  55.7 1.9 %collective-permute-start.18 = (bf16[2,128,512]{2,1,0:T(8,128)(2,1)S(1)}, bf16[2,128,512]{2,1,0:T(8,128)(2,1)S(1)}, u32[]{:S(2)}, u32[]{:S(2)}) collective-permute-start(bf16[2,128,512]{2,1,0:T(8,128)(2,1)S(1)} %bitcast.16), channel_id=1, source_target_pairs={{0,2},{2,0},{4,6},{6,4},{8,10},{10,8},{12,14},{14,12},{16,18},{18,... | collective-permute-start | bytes 786440 | tf_op jit(solution)/shard_map/ppermute | solution.py:79
  55.7 2.3 %collective-permute-start.19 = (bf16[2,128,512]{2,1,0:T(8,128)(2,1)S(1)}, bf16[2,128,512]{2,1,0:T(8,128)(2,1)S(1)}, u32[]{:S(2)}, u32[]{:S(2)}) collective-permute-start(bf16[2,128,512]{2,1,0:T(8,128)(2,1)S(1)} %collective-permute-done.11.refs_1_), channel_id=1, source_target_pairs={{0,2},{2,0},{4,6},{6,4},{8,10},{10,8},{12,14},{14,12},{16,18},{18,... | collective-permute-start | bytes 786440 | tf_op jit(solution)/shard_map/ppermute | solution.py:79
  58.7 7.6 %collective-permute-start.13 = (bf16[2,128,512]{2,1,0:T(8,128)(2,1)S(1)}, bf16[2,128,512]{2,1,0:T(8,128)(2,1)S(1)}, u32[]{:S(2)}, u32[]{:S(2)}) collective-permute-start(bf16[2,128,512]{2,1,0:T(8,128)(2,1)S(1)} %get-tuple-element.66), channel_id=1, source_target_pairs={{0,1},{1,0},{2,3},{3,2},{4,5},{5,4},{6,7},{7,6},{8,9},{9,8},{10,11... | collective-permute-start | bytes 786440 | tf_op jit(solution)/shard_map/ppermute | solution.py:86
  60.2 9.0 %collective-permute-start.24 = (bf16[2,128,1536]{2,1,0:T(8,128)(2,1)S(1)}, bf16[2,128,1536]{2,1,0:T(8,128)(2,1)S(1)}, u32[]{:S(2)}, u32[]{:S(2)}) collective-permute-start(bf16[2,128,1536]{2,1,0:T(8,128)(2,1)S(1)} %shard_map.67.refs_0_), channel_id=1, source_target_pairs={{0,2},{2,0},{4,6},{6,4},{8,10},{10,8},{12,14},{14,12},{16,18},{18,... | collective-permute-start | bytes 2359304 | tf_op jit(solution)/shard_map/ppermute | solution.py:79
  61.4 7.8 %collective-permute-start.25 = (bf16[2,128,1536]{2,1,0:T(8,128)(2,1)S(1)}, bf16[2,128,1536]{2,1,0:T(8,128)(2,1)S(1)}, u32[]{:S(2)}, u32[]{:S(2)}) collective-permute-start(bf16[2,128,1536]{2,1,0:T(8,128)(2,1)S(1)} %shard_map.68.refs_1_), channel_id=1, source_target_pairs={{0,2},{2,0},{4,6},{6,4},{8,10},{10,8},{12,14},{14,12},{16,18},{18,... | collective-permute-start | bytes 2359304 | tf_op jit(solution)/shard_map/ppermute | solution.py:79
  66.2 2.4 %collective-permute-start.20 = (bf16[2,128,512]{2,1,0:T(8,128)(2,1)S(1)}, bf16[2,128,512]{2,1,0:T(8,128)(2,1)S(1)}, u32[]{:S(2)}, u32[]{:S(2)}) collective-permute-start(bf16[2,128,512]{2,1,0:T(8,128)(2,1)S(1)} %collective-permute-done.13.refs_0_), channel_id=1, source_target_pairs={{0,2},{2,0},{4,6},{6,4},{8,10},{10,8},{12,14},{14,12},{16,18},{18,... | collective-permute-start | bytes 786440 | tf_op jit(solution)/shard_map/ppermute | solution.py:79

commit v10 on v9

--- a/solution.py
+++ b/solution.py
@@ -10,11 +10,9 @@
 BF16 = jnp.bfloat16
 F32 = jnp.float32
 VMEM_BYTES = 16 * 1024 * 1024
-JOIN_COST = 300_000_000
-ROWS_COST = 0
+JOIN_COST = 300000000
 OWN_COST = 1_000_000_000
-KEEP_COST = 6_000_000_000
-SLOT_ROWS_COST = 2_000_000_000
+KEEP_COST = 2000000000
 
 
 def dot(first, second):
@@ -233,7 +231,7 @@
     rest_send, kept, *kept_out = call(
         rows_kernel, scalars, [*s_rows, *s_sib, comp, skel_col, end_own, end_sib],
         [sds((2, hr, k), BF16), sds((2, fr, 3 * k), BF16)] + [sds((2, hr, 2 * k), BF16)] * nf
-        + [sds((2, hr, k), BF16)] * nf, cost=ROWS_COST,
+        + [sds((2, hr, k), BF16)] * nf,
     )
     rest_far = over_face(rest_send)
 
@@ -286,7 +284,7 @@
     )
 
     two_x = box_permute(two_own, 2)
-    two_y = over_face(after(two_own, *rest_far))
+    two_y = over_face(two_own)
     rest_fwd = [box_permute(after(a, two_own), 1) for a in rest_far]
 
     def weighted(w_ref, rows, out_ref):
@@ -320,6 +318,10 @@
         [sds((2, k, 3 * k), BF16)], scratch=[pltpu.VMEM((n_face, 2, fr, 3 * k), BF16)],
     )
 
+    ends_far = [face_permute(after(a, two_own), i + 1) for i, a in enumerate(kept_out[:nf])]
+    ends_fwd = [box_permute(a, 1) for a in ends_far]
+    slots_far = [face_permute(after(a, two_own), i + 1) for i, a in enumerate(kept_out[nf:])]
+
     def join_kernel(sc, own_ref, x_ref, out_ref):
         q = sc[1]
         out_ref[:, :, pl.ds(pl.multiple_of(q * k, k), k)] = own_ref[:, :, :k]
@@ -327,15 +329,12 @@
         out_ref[:, :, 2 * k :] = own_ref[:, :, k:] + x_ref[:, :, k:]
 
     two_shape = [sds((2, hr, 3 * k), BF16)]
-    two_rows = call(join_kernel, after(scalars, solved_one), [two_own, two_x], two_shape, cost=JOIN_COST)
+    two_rows = call(join_kernel, after(scalars, solved_one, weight_two), [two_own, two_x], two_shape, cost=JOIN_COST)
     two_xy = [box_permute(after(a, *two_rows), 2) for a in two_y]
+
     for own, other in zip(two_y, two_xy):
-        two_rows += call(join_kernel, after(scalars, weight_two), [own, other], two_shape)
+        two_rows += call(join_kernel, after(scalars, *slots_far), [own, other], two_shape)
     two_sib = [box_permute(a, 1) for a in two_rows]
-
-    ends_far = [face_permute(after(a, two_own), i + 1) for i, a in enumerate(kept_out[:nf])]
-    ends_fwd = [box_permute(a, 1) for a in ends_far]
-    slots_far = [face_permute(after(a, two_own), i + 1) for i, a in enumerate(kept_out[nf:])]
 
     def whole_rows(sc, out_ref, cols, end_ref, kept_ref, far, fwd):
         p, q = sc[0], sc[1]
@@ -418,24 +417,20 @@
                  pltpu.SemaphoreType.DMA((2,))],
     )
 
-    def slot_rows_kernel(sc, end_ref, kept_ref, *refs):
-        whole_rows(sc, refs[2 * nf], slice(2 * k, 3 * k), end_ref, kept_ref, refs[:nf], refs[nf : 2 * nf])
-
-    (slot_rows,) = call(
-        slot_rows_kernel, scalars, [end_kept, kept, *slots_far, *slots_fwd], [sds((2, fr, k), BF16)], cost=SLOT_ROWS_COST
-    )
-
-    def finish_kernel(sc, rows_ref, one_ref, two_ref, _, out_ref, stage, sem):
-        merged = (flat(rows_ref[...]).astype(F32) - one_ref[...]).astype(BF16)
+    def finish_kernel(sc, end_ref, kept_ref, *refs):
+        one_ref, two_ref, _, out_ref, rows, stage, sem = refs[2 * nf :]
+        whole_rows(sc, rows, slice(2 * k, 3 * k), end_ref, kept_ref, refs[:nf], refs[nf : 2 * nf])
+        merged = (flat(rows[...]).astype(F32) - one_ref[...]).astype(BF16)
         stage[...] = (merged.astype(F32) - two_ref[...]).astype(BF16).reshape(2, fr, k)
         copy = pltpu.make_async_copy(stage, out_ref.at[:, 0, :, pl.ds(2 * k, k)], sem.at[0])
         copy.start()
         copy.wait()
 
+    inputs = [end_kept, kept, *slots_far, *slots_fwd, sub_one, sub_two, out]
     (out,) = call(
-        finish_kernel, scalars, [slot_rows, sub_one, sub_two, out], [sds((2, 1, fr, 3 * k), BF16)],
-        specs=[pl.BlockSpec(memory_space=pltpu.VMEM)] * 3 + [in_hbm], out_specs=[in_hbm],
-        scratch=[pltpu.VMEM((2, fr, k), BF16), pltpu.SemaphoreType.DMA((1,))], aliases={4: 0},
+        finish_kernel, scalars, inputs, [sds((2, 1, fr, 3 * k), BF16)],
+        specs=[pl.BlockSpec(memory_space=pltpu.VMEM)] * (len(inputs) - 1) + [in_hbm], out_specs=[in_hbm],
+        scratch=[pltpu.VMEM((2, fr, k), BF16)] * 2 + [pltpu.SemaphoreType.DMA((1,))], aliases={len(inputs): 0},
     )
     return out
 

time: 74 us -> 68.5 us (0.926)
  waiting for transfers between devices: 26.3 us -> 20 us
  starting transfers between devices: 20.5 us -> 21.9 us
    ppermute x21, waiting for transfers between devices: 7.13 us -> 3.71 us  [box_permute(): return lax.ppermute(array, 'box', [(b, b ^ mask) for b in range(n_box)])]
    ppermute x5, waiting for transfers between devices: 19.2 us -> 16.2 us  [face_permute(): return lax.ppermute(array, ('box', 'face'), pairs)]
    ppermute x21, starting transfers between devices: 13.7 us -> 14.8 us  [box_permute(): return lax.ppermute(array, 'box', [(b, b ^ mask) for b in range(n_box)])]
    pallas_call x16 -> x15, Pallas kernels: 24 us -> 23.7 us  [call(): pl.pallas_call(kernel, in_specs=[pl.BlockSpec(memory_space=pltpu.SMEM)] +...]
  transfers between devices with their start and end apart: 26 -> 26, of which waited for: 11 -> 7; matrix products, arithmetic and copies ran while one was open for 0% -> 0% of each run, Pallas kernels for 26% -> 31%
where the time goes in v10:
time: 68.5 us; the launch traced here: 68.4 us
  Pallas kernels  23.7 us (35%)
  starting transfers between devices  21.9 us (32%)
  waiting for transfers between devices  20 us (29%)
  local copies, waits for them, and re-layouts  2.44 us (4%)
    pallas_call x15, Pallas kernels, call(): pl.pallas_call(kernel, in_specs=[pl.BlockSpec(memory_space=pltpu.SMEM)] +...  23.7 us
    ppermute x5, waiting for transfers between devices, face_permute(): return lax.ppermute(array, ('box', 'face'), pairs)  16.2 us
    ppermute x21, starting transfers between devices, box_permute(): return lax.ppermute(array, 'box', [(b, b ^ mask) for b in range(n_box)])  14.8 us
    ppermute x5, starting transfers between devices, face_permute(): return lax.ppermute(array, ('box', 'face'), pairs)  7.15 us
    ppermute x21, waiting for transfers between devices, box_permute(): return lax.ppermute(array, 'box', [(b, b ^ mask) for b in range(n_box)])  3.71 us
    unnamed x12, local copies, waits for them, and re-layouts  2.36 us
  transfers between devices with their start and end apart: 26, of which 7 were waited for; matrix products, arithmetic and copies ran while one was open for 0% of the time, Pallas kernels for 31%

profile of v10, /device:TPU:1, one launch (start us, length us, event | category | flops | bytes accessed | tf_op | source)
XLA Modules:
  0.0 68.4 jit_solution(8029686583327641859)
XLA Ops:
  0.0 0.1 stack.27.sc
  0.1 2.3 %copy-done = bf16[2,1,1,3,256,1536]{5,4,3,2,1,0:T(8,128)(2,1)S(1)} copy-done((bf16[2,1,1,3,256,1536]{5,4,3,2,1,0:T(8,128)(2,1)S(1)}, bf16[2,1,1,3,256,1536]{5,4,3,2,1,0:T(8,128)(2,1)}, u32[]{:S(2)}) %copy-start) | copy-done | bytes 4718616
  2.4 0.7 %shard_map.55 = (bf16[2,256,512]{2,1,0:T(8,128)(2,1)S(1)}, bf16[2,256,512]{2,1,0:T(8,128)(2,1)S(1)}, bf16[2,128,512]{2,1,0:T(8,128)(2,1)S(1)}, bf16[2,128,512]{2...) custom-call(s32[6]{0:T(128)S(1)} %stack.27.sc, ...), custom_call_target="tpu_custom_call" | custom-call | tf_op jit(solution)/shard_map/pallas_call | solution.py:46
  3.2 0.1 collective-permute-start
  3.3 0.5 collective-permute-start.1
  3.7 0.1 collective-permute-start.2
  3.8 0.4 collective-permute-start.3
  4.2 0.1 collective-permute-start.4
  4.3 0.8 %shard_map.56 = (s32[1,512]{1,0:T(1,128)S(1)}, s32[512,1]{1,0:T(8,128)S(1)}) custom-call(s32[6]{0:T(128)S(1)} %stack.27.sc, s32[8,512]{1,0:T(8,128)S(1)} %bitcast.18, s32[4,512]{1,0:T(4,128)S(1)} %bitcast.19), custom_call_target="tpu_custom_call" | custom-call | tf_op jit(solution)/shard_map/pallas_call | solution.py:46
  5.1 0.5 collective-permute-start.7
  5.6 1.3 %shard_map.57 = (bf16[2,256,512]{2,1,0:T(8,128)(2,1)S(1)}, bf16[2,256,512]{2,1,0:T(8,128)(2,1)S(1)}) custom-call(s32[6]{0:T(128)S(1)} %stack.27.sc, bf16[2,256,512]{2,1,0:T(8,128)(2,1)S(1)} %get-tuple-element.42.own_ref, bf16[2,256,512]{2,1,0:T(8,128)(2,1)S(1)} %collective-permute-done.sib_ref, s32[1,512]{1,0:T(1,128)S(1)} %get-tuple-element.43.comp_ref.refs_12_, ...), custom_call_target="tpu_custom_call" | custom-call | tf_op jit(solution)/shard_map/pallas_call | solution.py:46
  6.9 2.4 %collective-permute-start.10 = (bf16[2,256,512]{2,1,0:T(8,128)(2,1)S(1)}, bf16[2,256,512]{2,1,0:T(8,128)(2,1)S(1)}, u32[]{:S(2)}, u32[]{:S(2)}) collective-permute-start(bf16[2,256,512]{2,1,0:T(8,128)(2,1)S(1)} %get-tuple-element.62), channel_id=1, source_target_pairs={{0,1},{1,0},{2,3},{3,2},{4,5},{5,4},{6,7},{7,6},{8,9},{9,8},{10,11... | collective-permute-start | bytes 1572872 | tf_op jit(solution)/shard_map/ppermute | solution.py:84
  9.3 0.7 %collective-permute-start.5 = (bf16[2,128,512]{2,1,0:T(8,128)(2,1)S(1)}, bf16[2,128,512]{2,1,0:T(8,128)(2,1)S(1)}, u32[]{:S(2)}, u32[]{:S(2)}) collective-permute-start(bf16[2,128,512]{2,1,0:T(8,128)(2,1)S(1)} %get-tuple-element.52.refs_4_), channel_id=1, source_target_pairs={{0,2},{2,0},{4,6},{6,4},{8,10},{10,8},{12,14},{14,12},{16,18},{18,... | collective-permute-start | bytes 786440 | tf_op jit(solution)/shard_map/ppermute | solution.py:77
  10.1 1.3 %collective-permute-start.11 = (bf16[2,128,512]{2,1,0:T(8,128)(2,1)S(1)}, bf16[2,128,512]{2,1,0:T(8,128)(2,1)S(1)}, u32[]{:S(2)}, u32[]{:S(2)}) collective-permute-start(bf16[2,128,512]{2,1,0:T(8,128)(2,1)S(1)} %bitcast.15), channel_id=1, source_target_pairs={{0,4},{2,6},{4,0},{6,2},{8,12},{10,14},{12,8},{14,10},{16,20},{18,... | collective-permute-start | bytes 786440 | tf_op jit(solution)/shard_map/ppermute | solution.py:77
  11.4 1.1 %shard_map.58 = (bf16[2,128,1024]{2,1,0:T(8,128)(2,1)S(1)}, bf16[2,128,1024]{2,1,0:T(8,128)(2,1)S(1)}, bf16[2,256,1536]{2,1,0:T(8,128)(2,1)S(1)}) custom-call(s32[6]{0:T(128)S(1)} %stack.27.sc, bf16[2,3,256,1536]{3,2,1,0:T(8,128)(2,1)S(1)} %bitcast.12, s32[1,512]{1,0:T(1,128)S(1)} %get-tuple-element.43.comp_ref.refs_12_), custom_call_target="tpu_custom_call" | custom-call | tf_op jit(solution)/shard_map/pallas_call | solution.py:46
  12.5 0.8 %collective-permute-start.9 = (bf16[2,256,512]{2,1,0:T(8,128)(2,1)S(1)}, bf16[2,256,512]{2,1,0:T(8,128)(2,1)S(1)}, u32[]{:S(2)}, u32[]{:S(2)}) collective-permute-start(bf16[2,256,512]{2,1,0:T(8,128)(2,1)S(1)} %bitcast.13), channel_id=1, source_target_pairs={{0,2},{2,0},{4,6},{6,4},{8,10},{10,8},{12,14},{14,12},{16,18},{18,... | collective-permute-start | bytes 1572872 | tf_op jit(solution)/shard_map/ppermute | solution.py:77
  13.3 0.1 collective-permute-start.8
  13.4 2.9 %shard_map.59 = (bf16[2,128,512]{2,1,0:T(8,128)(2,1)S(1)}, bf16[2,256,1536]{2,1,0:T(8,128)(2,1)S(1)}, bf16[2,128,1024]{2,1,0:T(8,128)(2,1)S(1)}, bf16[2,128,512]{2,1,0:T(8,128)(2,1)S(1)}) custom-call(s32[6]{0:T(128)S(1)} %stack.27.sc, bf16[2,128,512]{2,1,0:T(8,128)(2,1)S(1)} %get-tuple-element.48.refs_0_, ...), custom_call_target="tpu_custom_call" | custom-call | tf_op jit(solution)/shard_map/pallas_call | solution.py:46
  16.3 1.3 %collective-permute-done.11.refs_1_ = bf16[2,128,512]{2,1,0:T(8,128)(2,1)S(1)} collective-permute-done((bf16[2,128,512]{2,1,0:T(8,128)(2,1)S(1)}, bf16[2,128,512]{2,1,0:T(8,128)(2,1)S(1)}, u32[]{:S(2)}, u32[]{:S(2)}) %collective-permute-start.11) | collective-permute-done | bytes 262176 | tf_op jit(solution)/shard_map/ppermute | solution.py:77
  17.6 3.6 %collective-permute-done.10.rest_0_ = bf16[2,256,512]{2,1,0:T(8,128)(2,1)S(1)} collective-permute-done((bf16[2,256,512]{2,1,0:T(8,128)(2,1)S(1)}, bf16[2,256,512]{2,1,0:T(8,128)(2,1)S(1)}, u32[]{:S(2)}, u32[]{:S(2)}) %collective-permute-start.10) | collective-permute-done | bytes 524320 | tf_op jit(solution)/shard_map/ppermute | solution.py:84
  21.2 1.0 %collective-permute-start.12 = (bf16[2,256,512]{2,1,0:T(8,128)(2,1)S(1)}, bf16[2,256,512]{2,1,0:T(8,128)(2,1)S(1)}, u32[]{:S(2)}, u32[]{:S(2)}) collective-permute-start(bf16[2,256,512]{2,1,0:T(8,128)(2,1)S(1)} %collective-permute-done.10.rest_0_), channel_id=1, source_target_pairs={{0,2},{2,0},{4,6},{6,4},{8,10},{10,8},{12,14},{14,12},{16,18},{18,... | collective-permute-start | bytes 1572872 | tf_op jit(solution)/shard_map/ppermute | solution.py:77
  22.2 1.5 %collective-permute-start.16 = (bf16[2,128,512]{2,1,0:T(8,128)(2,1)S(1)}, bf16[2,128,512]{2,1,0:T(8,128)(2,1)S(1)}, u32[]{:S(2)}, u32[]{:S(2)}) collective-permute-start(bf16[2,128,512]{2,1,0:T(8,128)(2,1)S(1)} %get-tuple-element.68), channel_id=1, source_target_pairs={{0,1},{1,0},{2,3},{3,2},{4,5},{5,4},{6,7},{7,6},{8,9},{9,8},{10,11... | collective-permute-start | bytes 786440 | tf_op jit(solution)/shard_map/ppermute | solution.py:84
  23.6 0.6 shard_map.60.w_ref
  24.3 1.4 %shard_map.61 = (f32[2,128,1024]{2,1,0:T(8,128)S(1)}, bf16[2,128,512]{2,1,0:T(8,128)(2,1)S(1)}) custom-call(s32[6]{0:T(128)S(1)} %stack.27.sc, bf16[2,128,1024]{2,1,0:T(8,128)(2,1)S(1)} %get-tuple-element.57.keep_ref, bf16[2,128,1024]{2,1,0:T(8,128)(2,1)S(1)} %collective-permute-done.8.recv_ref, bf16[2,512,512]{2,1,0:T(8,128)(2,1)S(1)} %shard_map.60.w_ref, ...), custom_call_target="tpu_custom_call" | custom-call | flops 1000000000 | tf_op jit(solution)/shard_map/pallas_call | solution.py:46
  25.7 1.0 %shard_map.62.own_ref = bf16[2,128,1024]{2,1,0:T(8,128)(2,1)S(1)} custom-call(s32[6]{0:T(128)S(1)} %stack.27.sc, f32[2,128,1024]{2,1,0:T(8,128)S(1)} %get-tuple-element.60.acc_ref, bf16[2,128,512]{2,1,0:T(8,128)(2,1)S(1)} %get-tuple-element.61.hid_ref, bf16[2,256,512]{2,1,0:T(8,128)(2,1)S(1)} %collective-permute-done.10.rest_0_, ...), custom_call_target="tpu_custom_call" | custom-call | tf_op jit(solution)/shard_map/pallas_call | solution.py:46
  26.7 1.3 %collective-permute-start.21 = (bf16[2,128,1024]{2,1,0:T(8,128)(2,1)S(1)}, bf16[2,128,1024]{2,1,0:T(8,128)(2,1)S(1)}, u32[]{:S(2)}, u32[]{:S(2)}) collective-permute-start(bf16[2,128,1024]{2,1,0:T(8,128)(2,1)S(1)} %shard_map.62.own_ref), channel_id=1, source_target_pairs={{0,4},{2,6},{4,0},{6,2},{8,12},{10,14},{12,8},{14,10},{16,20},{18,... | collective-permute-start | bytes 1572872 | tf_op jit(solution)/shard_map/ppermute | solution.py:77
  28.0 0.2 collective-permute-start.22
  28.2 0.8 %collective-permute-start.18 = (bf16[2,128,512]{2,1,0:T(8,128)(2,1)S(1)}, bf16[2,128,512]{2,1,0:T(8,128)(2,1)S(1)}, u32[]{:S(2)}, u32[]{:S(2)}) collective-permute-start(bf16[2,128,512]{2,1,0:T(8,128)(2,1)S(1)} %bitcast.16), channel_id=1, source_target_pairs={{0,2},{2,0},{4,6},{6,4},{8,10},{10,8},{12,14},{14,12},{16,18},{18,... | collective-permute-start | bytes 786440 | tf_op jit(solution)/shard_map/ppermute | solution.py:77
  29.1 1.0 %collective-permute-done.16.rest_2_ = bf16[2,128,512]{2,1,0:T(8,128)(2,1)S(1)} collective-permute-done((bf16[2,128,512]{2,1,0:T(8,128)(2,1)S(1)}, bf16[2,128,512]{2,1,0:T(8,128)(2,1)S(1)}, u32[]{:S(2)}, u32[]{:S(2)}) %collective-permute-start.16) | collective-permute-done | bytes 262176 | tf_op jit(solution)/shard_map/ppermute | solution.py:84
  30.1 0.8 %collective-permute-start.17 = (bf16[2,128,512]{2,1,0:T(8,128)(2,1)S(1)}, bf16[2,128,512]{2,1,0:T(8,128)(2,1)S(1)}, u32[]{:S(2)}, u32[]{:S(2)}) collective-permute-start(bf16[2,128,512]{2,1,0:T(8,128)(2,1)S(1)} %collective-permute-done.16.rest_2_), channel_id=1, source_target_pairs={{0,2},{2,0},{4,6},{6,4},{8,10},{10,8},{12,14},{14,12},{16,18},{18,... | collective-permute-start | bytes 786440 | tf_op jit(solution)/shard_map/ppermute | solution.py:77
  30.9 1.8 %collective-permute-start.14 = (bf16[2,128,1024]{2,1,0:T(8,128)(2,1)S(1)}, bf16[2,128,1024]{2,1,0:T(8,128)(2,1)S(1)}, u32[]{:S(2)}, u32[]{:S(2)}) collective-permute-start(bf16[2,128,1024]{2,1,0:T(8,128)(2,1)S(1)} %get-tuple-element.67), channel_id=1, source_target_pairs={{0,1},{1,0},{2,3},{3,2},{4,5},{5,4},{6,7},{7,6},{8,9},{9,8},{10,11... | collective-permute-start | bytes 1572872 | tf_op jit(solution)/shard_map/ppermute | solution.py:84
  32.8 0.7 shard_map.64.refs_4_
  33.4 4.2 %shard_map.63.refs_3_ = bf16[2,512,1536]{2,1,0:T(8,128)(2,1)S(1)} custom-call(s32[6]{0:T(128)S(1)} %stack.27.sc, bf16[2,512,512]{2,1,0:T(8,128)(2,1)S(1)} %shard_map.60.w_ref, bf16[2,256,512]{2,1,0:T(8,128)(2,1)S(1)} %get-tuple-element.44.end_ref.refs_14_.own_ref, bf16[2,256,512]{2,1,0:T(8,128)(2,1)S(1)} %collective-permute-done.7.refs_15_.endsib_ref.sib_ref, ...), custom_call_target="tpu_custom_call" | custom-call | tf_op jit(solution)/shard_map/pallas_call | solution.py:46
  37.7 2.3 %collective-permute-done.21.x_ref = bf16[2,128,1024]{2,1,0:T(8,128)(2,1)S(1)} collective-permute-done((bf16[2,128,1024]{2,1,0:T(8,128)(2,1)S(1)}, bf16[2,128,1024]{2,1,0:T(8,128)(2,1)S(1)}, u32[]{:S(2)}, u32[]{:S(2)}) %collective-permute-start.21) | collective-permute-done | bytes 524320 | tf_op jit(solution)/shard_map/ppermute | solution.py:77
  40.0 0.6 shard_map.66.refs_0_
  40.6 0.3 collective-permute-done.22.own_ref
  40.9 1.9 %collective-permute-start.23 = (bf16[2,128,1024]{2,1,0:T(8,128)(2,1)S(1)}, bf16[2,128,1024]{2,1,0:T(8,128)(2,1)S(1)}, u32[]{:S(2)}, u32[]{:S(2)}) collective-permute-start(bf16[2,128,1024]{2,1,0:T(8,128)(2,1)S(1)} %collective-permute-done.22.own_ref), channel_id=1, source_target_pairs={{0,4},{2,6},{4,0},{6,2},{8,12},{10,14},{12,8},{14,10},{16,20},{18,... | collective-permute-start | bytes 1572872 | tf_op jit(solution)/shard_map/ppermute | solution.py:77
  42.8 1.2 %collective-permute-start.13 = (bf16[2,128,512]{2,1,0:T(8,128)(2,1)S(1)}, bf16[2,128,512]{2,1,0:T(8,128)(2,1)S(1)}, u32[]{:S(2)}, u32[]{:S(2)}) collective-permute-start(bf16[2,128,512]{2,1,0:T(8,128)(2,1)S(1)} %get-tuple-element.65), channel_id=1, source_target_pairs={{0,1},{1,0},{2,3},{3,2},{4,5},{5,4},{6,7},{7,6},{8,9},{9,8},{10,11... | collective-permute-start | bytes 786440 | tf_op jit(solution)/shard_map/ppermute | solution.py:84
  44.0 8.1 %collective-permute-done.14.refs_0_ = bf16[2,128,1024]{2,1,0:T(8,128)(2,1)S(1)} collective-permute-done((bf16[2,128,1024]{2,1,0:T(8,128)(2,1)S(1)}, bf16[2,128,1024]{2,1,0:T(8,128)(2,1)S(1)}, u32[]{:S(2)}, u32[]{:S(2)}) %collective-permute-start.14) | collective-permute-done | bytes 524320 | tf_op jit(solution)/shard_map/ppermute | solution.py:84
  52.2 2.4 %collective-permute-start.15 = (bf16[2,128,1024]{2,1,0:T(8,128)(2,1)S(1)}, bf16[2,128,1024]{2,1,0:T(8,128)(2,1)S(1)}, u32[]{:S(2)}, u32[]{:S(2)}) collective-permute-start(bf16[2,128,1024]{2,1,0:T(8,128)(2,1)S(1)} %collective-permute-done.14.refs_0_), channel_id=1, source_target_pairs={{0,2},{2,0},{4,6},{6,4},{8,10},{10,8},{12,14},{14,12},{16,18},{18,... | collective-permute-start | bytes 1572872 | tf_op jit(solution)/shard_map/ppermute | solution.py:77
  54.6 3.2 %collective-permute-done.13.refs_0_ = bf16[2,128,512]{2,1,0:T(8,128)(2,1)S(1)} collective-permute-done((bf16[2,128,512]{2,1,0:T(8,128)(2,1)S(1)}, bf16[2,128,512]{2,1,0:T(8,128)(2,1)S(1)}, u32[]{:S(2)}, u32[]{:S(2)}) %collective-permute-start.13) | collective-permute-done | bytes 262176 | tf_op jit(solution)/shard_map/ppermute | solution.py:84
  57.8 1.4 %collective-permute-start.24 = (bf16[2,128,1536]{2,1,0:T(8,128)(2,1)S(1)}, bf16[2,128,1536]{2,1,0:T(8,128)(2,1)S(1)}, u32[]{:S(2)}, u32[]{:S(2)}) collective-permute-start(bf16[2,128,1536]{2,1,0:T(8,128)(2,1)S(1)} %shard_map.66.refs_0_), channel_id=1, source_target_pairs={{0,2},{2,0},{4,6},{6,4},{8,10},{10,8},{12,14},{14,12},{16,18},{18,... | collective-permute-start | bytes 2359304 | tf_op jit(solution)/shard_map/ppermute | solution.py:77
  59.2 0.6 shard_map.67.refs_1_
  59.8 0.1 collective-permute-start.25
  59.9 3.3 %shard_map.65 = (bf16[2,512,512]{2,1,0:T(8,128)(2,1)S(1)}, bf16[512,512]{1,0:T(8,128)(2,1)S(1)}, f32[512,512]{1,0:T(8,128)S(1)}) custom-call(s32[6]{0:T(128)S(1)} %stack.27.sc, bf16[2,256,1536]{2,1,0:T(8,128)(2,1)S(1)} %get-tuple-element.47.end_ref, bf16[2,256,1536]{2,1,0:T(8,128)(2,1)S(1)} %get-tuple-element.55.kept_ref, ...), custom_call_target="tpu_custom_call" | custom-call | flops 2000000000 | tf_op jit(solution)/shard_map/pallas_call | solution.py:46
  63.2 0.5 collective-permute-start.20
  63.8 2.8 %shard_map.68 = (bf16[2,1,256,1536]{3,2,1,0:T(8,128)(2,1)}, f32[512,512]{1,0:T(8,128)S(1)}) custom-call(s32[6]{0:T(128)S(1)} %stack.27.sc, bf16[2,512,512]{2,1,0:T(8,128)(2,1)S(1)} %get-tuple-element.70.hid_ref, bf16[512,512]{1,0:T(8,128)(2,1)S(1)} %get-tuple-element.73.first_ref, bf16[2,128,1536]{2,1,0:T(8,128)(2,1)S(1)} %shard_map.66.refs_0_, ...), custom_call_target="tpu_custom_call" | custom-call | tf_op jit(solution)/shard_map/pallas_call | solution.py:46
  66.6 1.6 %shard_map.69 = bf16[2,1,256,1536]{3,2,1,0:T(8,128)(2,1)} custom-call(s32[6]{0:T(128)S(1)} %stack.27.sc, bf16[2,256,1536]{2,1,0:T(8,128)(2,1)S(1)} %get-tuple-element.47.end_ref, bf16[2,256,1536]{2,1,0:T(8,128)(2,1)S(1)} %get-tuple-element.55.kept_ref, bf16[2,128,512]{2,1,0:T(8,128)(2,1)S(1)} %collective-permute-done.13.refs_0_, ...), custom_call_target="tpu_custom_call", output_to_operand_aliasing={{}: (7, {})} | custom-call | tf_op jit(solution)/shard_map/pallas_call | solution.py:46
  (32 shorter events, 0.1 us)
Async XLA Ops:
  0.0 4.3 %copy-start.4 = (s32[1,8,512]{2,1,0:T(8,128)S(1)}, s32[1,8,512]{2,1,0:T(8,128)}, u32[]{:S(2)}) copy-start(s32[1,8,512]{2,1,0:T(8,128)} %param.8) | copy-start | bytes 49156
  0.1 2.3 %copy-start = (bf16[2,1,1,3,256,1536]{5,4,3,2,1,0:T(8,128)(2,1)S(1)}, bf16[2,1,1,3,256,1536]{5,4,3,2,1,0:T(8,128)(2,1)}, u32[]{:S(2)}) copy-start(bf16[2,1,1,3,256,1536]{5,4,3,2,1,0:T(8,128)(2,1)} %param.5) | copy-start | bytes 14155780
  2.4 1.9 %copy-start.5 = (s32[1,4,512]{2,1,0:T(4,128)S(1)}, s32[1,4,512]{2,1,0:T(4,128)}, u32[]{:S(2)}) copy-start(s32[1,4,512]{2,1,0:T(4,128)} %param.9) | copy-start | bytes 24580
  2.4 8.9 %copy-start.1 = (bf16[2,1,1,3,256,1536]{5,4,3,2,1,0:T(8,128)(2,1)S(1)}, bf16[2,1,1,3,256,1536]{5,4,3,2,1,0:T(8,128)(2,1)}, u32[]{:S(2)}) copy-start(bf16[2,1,1,3,256,1536]{5,4,3,2,1,0:T(8,128)(2,1)} %param.5) | copy-start | bytes 14155780
  3.1 7.0 %copy-start.3 = (bf16[2,1,128,512]{3,2,1,0:T(8,128)(2,1)S(1)}, bf16[2,1,128,512]{3,2,1,0:T(8,128)(2,1)}, u32[]{:S(2)}) copy-start(bf16[2,1,128,512]{3,2,1,0:T(8,128)(2,1)} %param.7) | copy-start | bytes 786436
  3.2 2.0 %collective-permute-start = (bf16[2,256,512]{2,1,0:T(8,128)(2,1)S(1)}, bf16[2,256,512]{2,1,0:T(8,128)(2,1)S(1)}, u32[]{:S(2)}, u32[]{:S(2)}) collective-permute-start(bf16[2,256,512]{2,1,0:T(8,128)(2,1)S(1)} %get-tuple-element.42.own_ref), channel_id=1, source_target_pairs={{0,2},{2,0},{4,6},{6,4},{8,10},{10,8},{12,14},{14,12},{16,18},{18,... | collective-permute-start | bytes 1572872 | tf_op jit(solution)/shard_map/ppermute | solution.py:77
  3.3 3.6 %collective-permute-start.1 = (bf16[2,128,512]{2,1,0:T(8,128)(2,1)S(1)}, bf16[2,128,512]{2,1,0:T(8,128)(2,1)S(1)}, u32[]{:S(2)}, u32[]{:S(2)}) collective-permute-start(bf16[2,128,512]{2,1,0:T(8,128)(2,1)S(1)} %get-tuple-element.48.refs_0_), channel_id=1, source_target_pairs={{0,2},{2,0},{4,6},{6,4},{8,10},{10,8},{12,14},{14,12},{16,18},{18,... | collective-permute-start | bytes 786440 | tf_op jit(solution)/shard_map/ppermute | solution.py:77
  3.7 5.6 %collective-permute-start.2 = (bf16[2,128,512]{2,1,0:T(8,128)(2,1)S(1)}, bf16[2,128,512]{2,1,0:T(8,128)(2,1)S(1)}, u32[]{:S(2)}, u32[]{:S(2)}) collective-permute-start(bf16[2,128,512]{2,1,0:T(8,128)(2,1)S(1)} %get-tuple-element.49.refs_1_), channel_id=1, source_target_pairs={{0,2},{2,0},{4,6},{6,4},{8,10},{10,8},{12,14},{14,12},{16,18},{18,... | collective-permute-start | bytes 786440 | tf_op jit(solution)/shard_map/ppermute | solution.py:77
  3.8 6.2 %collective-permute-start.3 = (bf16[2,128,512]{2,1,0:T(8,128)(2,1)S(1)}, bf16[2,128,512]{2,1,0:T(8,128)(2,1)S(1)}, u32[]{:S(2)}, u32[]{:S(2)}) collective-permute-start(bf16[2,128,512]{2,1,0:T(8,128)(2,1)S(1)} %get-tuple-element.50.refs_2_), channel_id=1, source_target_pairs={{0,2},{2,0},{4,6},{6,4},{8,10},{10,8},{12,14},{14,12},{16,18},{18,... | collective-permute-start | bytes 786440 | tf_op jit(solution)/shard_map/ppermute | solution.py:77
  4.2 5.8 %collective-permute-start.4 = (bf16[2,128,512]{2,1,0:T(8,128)(2,1)S(1)}, bf16[2,128,512]{2,1,0:T(8,128)(2,1)S(1)}, u32[]{:S(2)}, u32[]{:S(2)}) collective-permute-start(bf16[2,128,512]{2,1,0:T(8,128)(2,1)S(1)} %get-tuple-element.51.refs_3_), channel_id=1, source_target_pairs={{0,2},{2,0},{4,6},{6,4},{8,10},{10,8},{12,14},{14,12},{16,18},{18,... | collective-permute-start | bytes 786440 | tf_op jit(solution)/shard_map/ppermute | solution.py:77
  5.1 8.2 %collective-permute-start.7 = (bf16[2,256,512]{2,1,0:T(8,128)(2,1)S(1)}, bf16[2,256,512]{2,1,0:T(8,128)(2,1)S(1)}, u32[]{:S(2)}, u32[]{:S(2)}) collective-permute-start(bf16[2,256,512]{2,1,0:T(8,128)(2,1)S(1)} %get-tuple-element.44.end_ref.refs_14_.own_ref), channel_id=1, source_target_pairs={{0,2},{2,0},{4,6},{6,4},{8,10},{10,8},{12,14},{14,12},{16,18},{18,... | collective-permute-start | bytes 1572872 | tf_op jit(solution)/shard_map/ppermute | solution.py:77
  6.9 14.3 %collective-permute-start.10 = (bf16[2,256,512]{2,1,0:T(8,128)(2,1)S(1)}, bf16[2,256,512]{2,1,0:T(8,128)(2,1)S(1)}, u32[]{:S(2)}, u32[]{:S(2)}) collective-permute-start(bf16[2,256,512]{2,1,0:T(8,128)(2,1)S(1)} %get-tuple-element.62), channel_id=1, source_target_pairs={{0,1},{1,0},{2,3},{3,2},{4,5},{5,4},{6,7},{7,6},{8,9},{9,8},{10,11... | collective-permute-start | bytes 1572872 | tf_op jit(solution)/shard_map/ppermute | solution.py:84
  9.3 3.2 %collective-permute-start.5 = (bf16[2,128,512]{2,1,0:T(8,128)(2,1)S(1)}, bf16[2,128,512]{2,1,0:T(8,128)(2,1)S(1)}, u32[]{:S(2)}, u32[]{:S(2)}) collective-permute-start(bf16[2,128,512]{2,1,0:T(8,128)(2,1)S(1)} %get-tuple-element.52.refs_4_), channel_id=1, source_target_pairs={{0,2},{2,0},{4,6},{6,4},{8,10},{10,8},{12,14},{14,12},{16,18},{18,... | collective-permute-start | bytes 786440 | tf_op jit(solution)/shard_map/ppermute | solution.py:77
  10.0 3.3 %collective-permute-start.6 = (bf16[2,128,512]{2,1,0:T(8,128)(2,1)S(1)}, bf16[2,128,512]{2,1,0:T(8,128)(2,1)S(1)}, u32[]{:S(2)}, u32[]{:S(2)}) collective-permute-start(bf16[2,128,512]{2,1,0:T(8,128)(2,1)S(1)} %get-tuple-element.53.refs_5_), channel_id=1, source_target_pairs={{0,2},{2,0},{4,6},{6,4},{8,10},{10,8},{12,14},{14,12},{16,18},{18,... | collective-permute-start | bytes 786440 | tf_op jit(solution)/shard_map/ppermute | solution.py:77
  10.1 2.4 %copy-start.2 = (bf16[2,1,256,512]{3,2,1,0:T(8,128)(2,1)S(1)}, bf16[2,1,256,512]{3,2,1,0:T(8,128)(2,1)}, u32[]{:S(2)}) copy-start(bf16[2,1,256,512]{3,2,1,0:T(8,128)(2,1)} %param.6) | copy-start | bytes 1572868
  10.1 7.5 %collective-permute-start.11 = (bf16[2,128,512]{2,1,0:T(8,128)(2,1)S(1)}, bf16[2,128,512]{2,1,0:T(8,128)(2,1)S(1)}, u32[]{:S(2)}, u32[]{:S(2)}) collective-permute-start(bf16[2,128,512]{2,1,0:T(8,128)(2,1)S(1)} %bitcast.15), channel_id=1, source_target_pairs={{0,4},{2,6},{4,0},{6,2},{8,12},{10,14},{12,8},{14,10},{16,20},{18,... | collective-permute-start | bytes 786440 | tf_op jit(solution)/shard_map/ppermute | solution.py:77
  12.5 11.1 %collective-permute-start.9 = (bf16[2,256,512]{2,1,0:T(8,128)(2,1)S(1)}, bf16[2,256,512]{2,1,0:T(8,128)(2,1)S(1)}, u32[]{:S(2)}, u32[]{:S(2)}) collective-permute-start(bf16[2,256,512]{2,1,0:T(8,128)(2,1)S(1)} %bitcast.13), channel_id=1, source_target_pairs={{0,2},{2,0},{4,6},{6,4},{8,10},{10,8},{12,14},{14,12},{16,18},{18,... | collective-permute-start | bytes 1572872 | tf_op jit(solution)/shard_map/ppermute | solution.py:77
  13.3 11.0 %collective-permute-start.8 = (bf16[2,128,1024]{2,1,0:T(8,128)(2,1)S(1)}, bf16[2,128,1024]{2,1,0:T(8,128)(2,1)S(1)}, u32[]{:S(2)}, u32[]{:S(2)}) collective-permute-start(bf16[2,128,1024]{2,1,0:T(8,128)(2,1)S(1)} %get-tuple-element.58), channel_id=1, source_target_pairs={{0,2},{2,0},{4,6},{6,4},{8,10},{10,8},{12,14},{14,12},{16,18},{18,... | collective-permute-start | bytes 1572872 | tf_op jit(solution)/shard_map/ppermute | solution.py:77
  21.2 4.5 %collective-permute-start.12 = (bf16[2,256,512]{2,1,0:T(8,128)(2,1)S(1)}, bf16[2,256,512]{2,1,0:T(8,128)(2,1)S(1)}, u32[]{:S(2)}, u32[]{:S(2)}) collective-permute-start(bf16[2,256,512]{2,1,0:T(8,128)(2,1)S(1)} %collective-permute-done.10.rest_0_), channel_id=1, source_target_pairs={{0,2},{2,0},{4,6},{6,4},{8,10},{10,8},{12,14},{14,12},{16,18},{18,... | collective-permute-start | bytes 1572872 | tf_op jit(solution)/shard_map/ppermute | solution.py:77
  22.2 7.9 %collective-permute-start.16 = (bf16[2,128,512]{2,1,0:T(8,128)(2,1)S(1)}, bf16[2,128,512]{2,1,0:T(8,128)(2,1)S(1)}, u32[]{:S(2)}, u32[]{:S(2)}) collective-permute-start(bf16[2,128,512]{2,1,0:T(8,128)(2,1)S(1)} %get-tuple-element.68), channel_id=1, source_target_pairs={{0,1},{1,0},{2,3},{3,2},{4,5},{5,4},{6,7},{7,6},{8,9},{9,8},{10,11... | collective-permute-start | bytes 786440 | tf_op jit(solution)/shard_map/ppermute | solution.py:84
  26.7 13.3 %collective-permute-start.21 = (bf16[2,128,1024]{2,1,0:T(8,128)(2,1)S(1)}, bf16[2,128,1024]{2,1,0:T(8,128)(2,1)S(1)}, u32[]{:S(2)}, u32[]{:S(2)}) collective-permute-start(bf16[2,128,1024]{2,1,0:T(8,128)(2,1)S(1)} %shard_map.62.own_ref), channel_id=1, source_target_pairs={{0,4},{2,6},{4,0},{6,2},{8,12},{10,14},{12,8},{14,10},{16,20},{18,... | collective-permute-start | bytes 1572872 | tf_op jit(solution)/shard_map/ppermute | solution.py:77
  28.0 12.9 %collective-permute-start.22 = (bf16[2,128,1024]{2,1,0:T(8,128)(2,1)S(1)}, bf16[2,128,1024]{2,1,0:T(8,128)(2,1)S(1)}, u32[]{:S(2)}, u32[]{:S(2)}) collective-permute-start(bf16[2,128,1024]{2,1,0:T(8,128)(2,1)S(1)} %shard_map.62.own_ref), channel_id=1, source_target_pairs={{0,1},{1,0},{2,3},{3,2},{4,5},{5,4},{6,7},{7,6},{8,9},{9,8},{10,11... | collective-permute-start | bytes 1572872 | tf_op jit(solution)/shard_map/ppermute | solution.py:84
  28.2 2.7 %collective-permute-start.18 = (bf16[2,128,512]{2,1,0:T(8,128)(2,1)S(1)}, bf16[2,128,512]{2,1,0:T(8,128)(2,1)S(1)}, u32[]{:S(2)}, u32[]{:S(2)}) collective-permute-start(bf16[2,128,512]{2,1,0:T(8,128)(2,1)S(1)} %bitcast.16), channel_id=1, source_target_pairs={{0,2},{2,0},{4,6},{6,4},{8,10},{10,8},{12,14},{14,12},{16,18},{18,... | collective-permute-start | bytes 786440 | tf_op jit(solution)/shard_map/ppermute | solution.py:77
  29.1 3.7 %collective-permute-start.19 = (bf16[2,128,512]{2,1,0:T(8,128)(2,1)S(1)}, bf16[2,128,512]{2,1,0:T(8,128)(2,1)S(1)}, u32[]{:S(2)}, u32[]{:S(2)}) collective-permute-start(bf16[2,128,512]{2,1,0:T(8,128)(2,1)S(1)} %collective-permute-done.11.refs_1_), channel_id=1, source_target_pairs={{0,2},{2,0},{4,6},{6,4},{8,10},{10,8},{12,14},{14,12},{16,18},{18,... | collective-permute-start | bytes 786440 | tf_op jit(solution)/shard_map/ppermute | solution.py:77
  30.1 3.3 %collective-permute-start.17 = (bf16[2,128,512]{2,1,0:T(8,128)(2,1)S(1)}, bf16[2,128,512]{2,1,0:T(8,128)(2,1)S(1)}, u32[]{:S(2)}, u32[]{:S(2)}) collective-permute-start(bf16[2,128,512]{2,1,0:T(8,128)(2,1)S(1)} %collective-permute-done.16.rest_2_), channel_id=1, source_target_pairs={{0,2},{2,0},{4,6},{6,4},{8,10},{10,8},{12,14},{14,12},{16,18},{18,... | collective-permute-start | bytes 786440 | tf_op jit(solution)/shard_map/ppermute | solution.py:77
  30.9 21.2 %collective-permute-start.14 = (bf16[2,128,1024]{2,1,0:T(8,128)(2,1)S(1)}, bf16[2,128,1024]{2,1,0:T(8,128)(2,1)S(1)}, u32[]{:S(2)}, u32[]{:S(2)}) collective-permute-start(bf16[2,128,1024]{2,1,0:T(8,128)(2,1)S(1)} %get-tuple-element.67), channel_id=1, source_target_pairs={{0,1},{1,0},{2,3},{3,2},{4,5},{5,4},{6,7},{7,6},{8,9},{9,8},{10,11... | collective-permute-start | bytes 1572872 | tf_op jit(solution)/shard_map/ppermute | solution.py:84
  40.9 18.3 %collective-permute-start.23 = (bf16[2,128,1024]{2,1,0:T(8,128)(2,1)S(1)}, bf16[2,128,1024]{2,1,0:T(8,128)(2,1)S(1)}, u32[]{:S(2)}, u32[]{:S(2)}) collective-permute-start(bf16[2,128,1024]{2,1,0:T(8,128)(2,1)S(1)} %collective-permute-done.22.own_ref), channel_id=1, source_target_pairs={{0,4},{2,6},{4,0},{6,2},{8,12},{10,14},{12,8},{14,10},{16,20},{18,... | collective-permute-start | bytes 1572872 | tf_op jit(solution)/shard_map/ppermute | solution.py:77
  42.8 15.0 %collective-permute-start.13 = (bf16[2,128,512]{2,1,0:T(8,128)(2,1)S(1)}, bf16[2,128,512]{2,1,0:T(8,128)(2,1)S(1)}, u32[]{:S(2)}, u32[]{:S(2)}) collective-permute-start(bf16[2,128,512]{2,1,0:T(8,128)(2,1)S(1)} %get-tuple-element.65), channel_id=1, source_target_pairs={{0,1},{1,0},{2,3},{3,2},{4,5},{5,4},{6,7},{7,6},{8,9},{9,8},{10,11... | collective-permute-start | bytes 786440 | tf_op jit(solution)/shard_map/ppermute | solution.py:84
  52.2 7.7 %collective-permute-start.15 = (bf16[2,128,1024]{2,1,0:T(8,128)(2,1)S(1)}, bf16[2,128,1024]{2,1,0:T(8,128)(2,1)S(1)}, u32[]{:S(2)}, u32[]{:S(2)}) collective-permute-start(bf16[2,128,1024]{2,1,0:T(8,128)(2,1)S(1)} %collective-permute-done.14.refs_0_), channel_id=1, source_target_pairs={{0,2},{2,0},{4,6},{6,4},{8,10},{10,8},{12,14},{14,12},{16,18},{18,... | collective-permute-start | bytes 1572872 | tf_op jit(solution)/shard_map/ppermute | solution.py:77
  57.8 6.0 %collective-permute-start.24 = (bf16[2,128,1536]{2,1,0:T(8,128)(2,1)S(1)}, bf16[2,128,1536]{2,1,0:T(8,128)(2,1)S(1)}, u32[]{:S(2)}, u32[]{:S(2)}) collective-permute-start(bf16[2,128,1536]{2,1,0:T(8,128)(2,1)S(1)} %shard_map.66.refs_0_), channel_id=1, source_target_pairs={{0,2},{2,0},{4,6},{6,4},{8,10},{10,8},{12,14},{14,12},{16,18},{18,... | collective-permute-start | bytes 2359304 | tf_op jit(solution)/shard_map/ppermute | solution.py:77
  59.8 4.0 %collective-permute-start.25 = (bf16[2,128,1536]{2,1,0:T(8,128)(2,1)S(1)}, bf16[2,128,1536]{2,1,0:T(8,128)(2,1)S(1)}, u32[]{:S(2)}, u32[]{:S(2)}) collective-permute-start(bf16[2,128,1536]{2,1,0:T(8,128)(2,1)S(1)} %shard_map.67.refs_1_), channel_id=1, source_target_pairs={{0,2},{2,0},{4,6},{6,4},{8,10},{10,8},{12,14},{14,12},{16,18},{18,... | collective-permute-start | bytes 2359304 | tf_op jit(solution)/shard_map/ppermute | solution.py:77
  63.2 3.4 %collective-permute-start.20 = (bf16[2,128,512]{2,1,0:T(8,128)(2,1)S(1)}, bf16[2,128,512]{2,1,0:T(8,128)(2,1)S(1)}, u32[]{:S(2)}, u32[]{:S(2)}) collective-permute-start(bf16[2,128,512]{2,1,0:T(8,128)(2,1)S(1)} %collective-permute-done.13.refs_0_), channel_id=1, source_target_pairs={{0,2},{2,0},{4,6},{6,4},{8,10},{10,8},{12,14},{14,12},{16,18},{18,... | collective-permute-start | bytes 786440 | tf_op jit(solution)/shard_map/ppermute | solution.py:77

commit v11 on v9

--- a/solution.py
+++ b/solution.py
@@ -10,11 +10,9 @@
 BF16 = jnp.bfloat16
 F32 = jnp.float32
 VMEM_BYTES = 16 * 1024 * 1024
-JOIN_COST = 300_000_000
-ROWS_COST = 0
+JOIN_COST = 300000000
 OWN_COST = 1_000_000_000
-KEEP_COST = 6_000_000_000
-SLOT_ROWS_COST = 2_000_000_000
+KEEP_COST = 2_000_000_000
 
 
 def dot(first, second):
@@ -41,7 +39,7 @@
     return jnp.where(cols == index, 1.0, 0.0).astype(BF16)
 
 
-def call(kernel, scalars, inputs, out_shapes, specs=None, out_specs=None, scratch=(), cost=0, aliases=None):
+def call(kernel, scalars, inputs, out_shapes, specs=None, out_specs=None, scratch=(), cost=0):
     in_vmem = pl.BlockSpec(memory_space=pltpu.VMEM)
     specs = specs or [in_vmem] * len(inputs)
     out_specs = out_specs or [in_vmem] * len(out_shapes)
@@ -51,7 +49,6 @@
         out_specs=out_specs,
         out_shape=out_shapes,
         scratch_shapes=list(scratch),
-        input_output_aliases=aliases or {},
         compiler_params=pltpu.CompilerParams(vmem_limit_bytes=VMEM_BYTES),
         cost_estimate=pl.CostEstimate(flops=cost, bytes_accessed=0, transcendentals=0),
     )(scalars, *inputs)
@@ -182,10 +179,12 @@
 
     def rows_kernel(sc, *refs):
         owns, sibs, refs = refs[:6], refs[6:12], refs[12:]
-        comp_ref, col_ref, end_ref, endsib_ref, rest_out, kept_out, *outs = refs
+        comp_ref, col_ref, end_ref, endsib_ref, kept_out, *outs = refs
         p, q, f = sc[0], sc[1], sc[2]
         mine, _ = halves(p)
-        rest_out[...] = jnp.where(p == q, endsib_ref[:, mine, :], end_ref[:, mine, :])
+        rest = jnp.where(p == q, endsib_ref[:, mine, :], end_ref[:, mine, :])
+        for s in range(nf):
+            outs[nf + s][:, :, :k] = rest
         pick_own = column_picker(comp_ref[...], p * k, k)
         pick_sib = column_picker(comp_ref[...], (1 - p) * k, k)
 
@@ -205,7 +204,7 @@
             if c < 2:
                 outs[s][t, :, c * k : (c + 1) * k] = picked
             else:
-                outs[nf + s][t] = picked
+                outs[nf + s][t, :, k:] = picked
 
         def col_half(s):
             start = (f + n_face - s - 1) % n_face * fr + p * hr
@@ -230,12 +229,11 @@
 
             pick(jnp.concatenate([col_ref[pl.ds(pl.multiple_of(f * fr, fr), fr), :], far], axis=0), write)
 
-    rest_send, kept, *kept_out = call(
+    kept, *kept_out = call(
         rows_kernel, scalars, [*s_rows, *s_sib, comp, skel_col, end_own, end_sib],
-        [sds((2, hr, k), BF16), sds((2, fr, 3 * k), BF16)] + [sds((2, hr, 2 * k), BF16)] * nf
-        + [sds((2, hr, k), BF16)] * nf, cost=ROWS_COST,
-    )
-    rest_far = over_face(rest_send)
+        [sds((2, fr, 3 * k), BF16)] + [sds((2, hr, 2 * k), BF16)] * (2 * nf),
+    )
+    mixed_far = [face_permute(a, i + 1) for i, a in enumerate(kept_out[nf:])]
 
     def piece(hidden, start, count):
         return stacked(hidden[0][:, start : start + count], hidden[1][:, start : start + count])
@@ -270,8 +268,10 @@
     first_fwd = [box_permute(after(a, kept, w_two_x), 1) for a in first_far]
 
     def iface_far_kernel(sc, acc_ref, hid_ref, *rest):
-        far, fwd, out_ref = rest[:nf], rest[nf : 2 * nf], rest[2 * nf]
-        is_end = sc[0] == sc[1]
+        far, fwd = rest[:nf], rest[nf : 2 * nf]
+        end_out, keep_out, send_out = rest[2 * nf :]
+        q = sc[1]
+        is_end = sc[0] == q
         hidden = [hid_ref[0], hid_ref[1]]
         total = acc_ref[...]
         for s in range(nf):
@@ -279,15 +279,29 @@
             mine, other = dot(left, flat(far[s][...])), dot(left, flat(fwd[s][...]))
             both = [jnp.where(is_end, mine, other), jnp.where(is_end, other, mine)]
             total = total - jnp.concatenate(both, axis=1).reshape(2, hr, 2 * k)
-        out_ref[...] = total.astype(BF16)
+        total = total.astype(BF16)
+        end_out[...] = total[:, :, :k]
+        low, high = total[:, :, k : k + half], total[:, :, k + half :]
+        keep_out[...] = jnp.where(q == 0, low, high)
+        send_out[...] = jnp.where(q == 0, high, low)
+
+    two_end, side_keep, side_send = call(
+        iface_far_kernel, scalars, [v_acc, v_hid, *first_far, *first_fwd],
+        [sds((2, hr, k), BF16)] + [sds((2, hr, half), BF16)] * 2,
+    )
+
+    side_x = box_permute(side_send, 2)
+
+    def pack_kernel(sc, end_ref, keep_ref, x_ref, out_ref):
+        out_ref[:, :, :k] = end_ref[...]
+        out_ref[:, :, k:] = keep_ref[...] + x_ref[...]
 
     (two_own,) = call(
-        iface_far_kernel, scalars, [v_acc, v_hid, *first_far, *first_fwd], [sds((2, hr, 2 * k), BF16)],
-    )
-
+        pack_kernel, scalars, [two_end, side_keep, side_x], [sds((2, hr, k + half), BF16)]
+    )
     two_x = box_permute(two_own, 2)
-    two_y = over_face(after(two_own, *rest_far))
-    rest_fwd = [box_permute(after(a, two_own), 1) for a in rest_far]
+    two_y = over_face(two_own)
+    mixed_fwd = [box_permute(after(a, two_own), 1) for a in mixed_far]
 
     def weighted(w_ref, rows, out_ref):
         left = jnp.concatenate([piece((w_ref[0], w_ref[1]), s * fr, fr) for s in range(n_face)], axis=1)
@@ -311,131 +325,108 @@
             rows[s + 1, :, :, first_cols] = jnp.where(is_end, mine, other)
             rows[s + 1, :, :, 2 * k :] = jnp.where(is_end, other, mine)
             for take, parts in zip(halves(p), refs[2:]):
-                rows[s + 1, :, take, rest_cols] = parts[s][...]
+                rows[s + 1, :, take, rest_cols] = parts[s][:, :, :k]
         weighted(w_ref, rows, out_ref)
 
     (solved_one,) = call(
         weighted_one_kernel, scalars,
-        [weight_one, end_own, end_sib, side, *first_far, *first_fwd, *rest_far, *rest_fwd],
+        [weight_one, end_own, end_sib, side, *first_far, *first_fwd, *mixed_far, *mixed_fwd],
         [sds((2, k, 3 * k), BF16)], scratch=[pltpu.VMEM((n_face, 2, fr, 3 * k), BF16)],
     )
 
     def join_kernel(sc, own_ref, x_ref, out_ref):
         q = sc[1]
-        out_ref[:, :, pl.ds(pl.multiple_of(q * k, k), k)] = own_ref[:, :, :k]
-        out_ref[:, :, pl.ds(pl.multiple_of((1 - q) * k, k), k)] = x_ref[:, :, :k]
-        out_ref[:, :, 2 * k :] = own_ref[:, :, k:] + x_ref[:, :, k:]
+        for ref, which in ((own_ref, q), (x_ref, 1 - q)):
+            out_ref[:, :, pl.ds(pl.multiple_of(which * k, k), k)] = ref[:, :, :k]
+            out_ref[:, :, pl.ds(pl.multiple_of(2 * k + which * half, half), half)] = ref[:, :, k:]
 
     two_shape = [sds((2, hr, 3 * k), BF16)]
-    two_rows = call(join_kernel, after(scalars, solved_one), [two_own, two_x], two_shape, cost=JOIN_COST)
+    two_rows = call(join_kernel, after(scalars, weight_two), [two_own, two_x], two_shape, cost=JOIN_COST)
     two_xy = [box_permute(after(a, *two_rows), 2) for a in two_y]
     for own, other in zip(two_y, two_xy):
-        two_rows += call(join_kernel, after(scalars, weight_two), [own, other], two_shape)
+        two_rows += call(join_kernel, after(scalars, solved_one), [own, other], two_shape)
     two_sib = [box_permute(a, 1) for a in two_rows]
 
     ends_far = [face_permute(after(a, two_own), i + 1) for i, a in enumerate(kept_out[:nf])]
     ends_fwd = [box_permute(a, 1) for a in ends_far]
-    slots_far = [face_permute(after(a, two_own), i + 1) for i, a in enumerate(kept_out[nf:])]
-
-    def whole_rows(sc, out_ref, cols, end_ref, kept_ref, far, fwd):
-        p, q = sc[0], sc[1]
+
+    def level_one_kernel(sc, end_ref, kept_ref, *refs):
+        parts = [refs[i * nf : (i + 1) * nf] for i in range(4)]
+        col_ref, one_ref, w_ref, hid_out, first_out, slots_out, zs = refs[4 * nf :]
+        p, q, f = sc[0], sc[1], sc[2]
 
         @pl.when(p == q)
         def _():
-            out_ref[...] = end_ref[:, :, cols]
+            zs[...] = end_ref[...]
 
         @pl.when(p != q)
         def _():
-            for h, parts in enumerate((far, fwd)):
-                take = pl.ds(pl.multiple_of((p ^ h) * hr, hr), hr)
-                total = kept_ref[:, take, cols]
-                for part in parts:
-                    total = total + part[...]
-                out_ref[:, take, :] = total
-
-    def level_one_kernel(sc, end_ref, kept_ref, *refs):
-        far, fwd = refs[:nf], refs[nf : 2 * nf]
-        col_ref, one_ref, w_ref, hid_out, first_out, sub_out, zs = refs[2 * nf :]
-        p, q, f = sc[0], sc[1], sc[2]
-        whole_rows(sc, zs, slice(0, 2 * k), end_ref, kept_ref, far, fwd)
+            for h, take in enumerate(halves(p)):
+                for part, cols, source in (
+                    (parts[h], slice(2 * k, 3 * k), slice(k, 2 * k)), (parts[2 + h], slice(0, 2 * k), slice(0, 2 * k)),
+                ):
+                    total = kept_ref[:, take, cols]
+                    for ref in part:
+                        total = total + ref[:, :, source]
+                    zs[:, take, cols] = total
+
         slots = col_ref[pl.ds(pl.multiple_of(f * fr, fr), fr), :]
         right = jnp.where(slots >= k, 1, 0)
         right = jnp.where(p == q, p, right) > 0
         lefts = [zs[t, :, :k] for t in range(2)]
-        rights = [zs[t, :, k:] for t in range(2)]
+        rights = [zs[t, :, k : 2 * k] for t in range(2)]
         left = stacked(*[jnp.where(right, a, b) for a, b in zip(lefts, rights)])
         nothing = jnp.zeros((fr, k), BF16)
         start = [
             jnp.concatenate([jnp.where(right, nothing, a) for a in lefts], axis=0),
             jnp.concatenate([jnp.where(right, a, nothing) for a in rights], axis=0),
+            flat(zs[:, :, 2 * k :]),
         ]
         merged = [
             (start[c].astype(F32) - dot(left, flat(one_ref[:, :, c * k : (c + 1) * k]))).astype(BF16)
-            for c in range(2)
+            for c in range(3)
         ]
-        sub_out[...] = dot(left, flat(one_ref[:, :, 2 * k :]))
         is_left = q == 0
         first_out[...] = jnp.where(is_left, merged[0], merged[1])
+        slots_out[...] = merged[2]
         couple = jnp.where(is_left, merged[1], merged[0])
         second = dot(stacked(couple[:fr], couple[fr:]), flat(w_ref[...])).astype(BF16)
         for s in range(n_face):
             hid_out[s] = piece((second[:fr], second[fr:]), s * fr, fr)
 
-    hid_two, first_two, sub_one = call(
+    hid_two, first_two, slots_two = call(
         level_one_kernel, scalars,
-        [end_kept, kept, *ends_far, *ends_fwd, skel_col, solved_one, weight_two],
-        [sds((n_face, 2 * fr, 2 * fr), BF16), sds((2 * fr, k), BF16), sds((2 * fr, k), F32)],
-        scratch=[pltpu.VMEM((2, fr, 2 * k), BF16)], cost=KEEP_COST,
-    )
-
-    slots_fwd = [box_permute(after(a, hid_two), 1) for a in slots_far]
-
-    def level_two_kernel(sc, hid_ref, first_ref, *refs):
-        out_ref, sub_out, rows, stage, sems = refs[2 * n_face :]
-        p, q = sc[0], sc[1]
+        [end_kept, kept, *mixed_far, *mixed_fwd, *ends_far, *ends_fwd, skel_col, solved_one, weight_two],
+        [sds((n_face, 2 * fr, 2 * fr), BF16), sds((2 * fr, k), BF16), sds((2 * fr, k), BF16)],
+        scratch=[pltpu.VMEM((2, fr, 3 * k), BF16)], cost=KEEP_COST,
+    )
+
+    def level_two_kernel(sc, hid_ref, first_ref, slots_ref, *refs):
+        out_ref, rows, stage, sems = refs[2 * n_face :]
+        q = sc[1]
         left = jnp.concatenate([hid_ref[s] for s in range(n_face)], axis=1)
-        for s in range(n_face):
-            rows[s, :, pl.ds(pl.multiple_of(p * hr, hr), hr), :] = refs[s][...]
-            rows[s, :, pl.ds(pl.multiple_of((1 - p) * hr, hr), hr), :] = refs[n_face + s][...]
+        for h, take in enumerate(halves(sc[0])):
+            for s in range(n_face):
+                rows[s, :, take, :] = refs[h * n_face + s][...]
         copies = []
-        for c in range(2):
-            first = jnp.where(q == c, first_ref[...], jnp.zeros((2 * fr, k), BF16)).astype(F32)
+        for c in range(3):
+            first = slots_ref[...]
+            if c < 2:
+                first = jnp.where(q == c, first_ref[...], jnp.zeros((2 * fr, k), BF16))
             right = rows[:, :, :, c * k : (c + 1) * k].reshape(n_face * 2 * fr, k)
-            stage[c] = (first - dot(left, right)).astype(BF16).reshape(2, fr, k)
+            stage[c] = (first.astype(F32) - dot(left, right)).astype(BF16).reshape(2, fr, k)
             copies.append(pltpu.make_async_copy(
                 stage.at[c], out_ref.at[:, 0, :, pl.ds(c * k, k)], sems.at[c]
             ))
             copies[-1].start()
-        sub_out[...] = dot(left, rows[:, :, :, 2 * k :].reshape(n_face * 2 * fr, k))
         for copy in copies:
             copy.wait()
 
-    out, sub_two = call(
-        level_two_kernel, scalars, [hid_two, first_two, *two_rows, *two_sib],
-        [sds((2, 1, fr, 3 * k), BF16), sds((2 * fr, k), F32)],
-        out_specs=[in_hbm, pl.BlockSpec(memory_space=pltpu.VMEM)],
-        scratch=[pltpu.VMEM((n_face, 2, fr, 3 * k), BF16), pltpu.VMEM((2, 2, fr, k), BF16),
-                 pltpu.SemaphoreType.DMA((2,))],
-    )
-
-    def slot_rows_kernel(sc, end_ref, kept_ref, *refs):
-        whole_rows(sc, refs[2 * nf], slice(2 * k, 3 * k), end_ref, kept_ref, refs[:nf], refs[nf : 2 * nf])
-
-    (slot_rows,) = call(
-        slot_rows_kernel, scalars, [end_kept, kept, *slots_far, *slots_fwd], [sds((2, fr, k), BF16)], cost=SLOT_ROWS_COST
-    )
-
-    def finish_kernel(sc, rows_ref, one_ref, two_ref, _, out_ref, stage, sem):
-        merged = (flat(rows_ref[...]).astype(F32) - one_ref[...]).astype(BF16)
-        stage[...] = (merged.astype(F32) - two_ref[...]).astype(BF16).reshape(2, fr, k)
-        copy = pltpu.make_async_copy(stage, out_ref.at[:, 0, :, pl.ds(2 * k, k)], sem.at[0])
-        copy.start()
-        copy.wait()
-
     (out,) = call(
-        finish_kernel, scalars, [slot_rows, sub_one, sub_two, out], [sds((2, 1, fr, 3 * k), BF16)],
-        specs=[pl.BlockSpec(memory_space=pltpu.VMEM)] * 3 + [in_hbm], out_specs=[in_hbm],
-        scratch=[pltpu.VMEM((2, fr, k), BF16), pltpu.SemaphoreType.DMA((1,))], aliases={4: 0},
+        level_two_kernel, scalars, [hid_two, first_two, slots_two, *two_rows, *two_sib],
+        [sds((2, 1, fr, 3 * k), BF16)], out_specs=[in_hbm],
+        scratch=[pltpu.VMEM((n_face, 2, fr, 3 * k), BF16), pltpu.VMEM((3, 2, fr, k), BF16),
+                 pltpu.SemaphoreType.DMA((3,))],
     )
     return out
 

time: 74 us -> 65.9 us (0.89)
  waiting for transfers between devices: 26.3 us -> 14.8 us
  starting transfers between devices: 20.5 us -> 24.7 us
  Pallas kernels: 24 us -> 23.2 us
    ppermute x5 -> x4, waiting for transfers between devices: 19.2 us -> 4.73 us  [face_permute(): return lax.ppermute(array, ('box', 'face'), pairs)]
    ppermute x21, starting transfers between devices: 13.7 us -> 18.8 us  [box_permute(): return lax.ppermute(array, 'box', [(b, b ^ mask) for b in range(n_box)])]
    ppermute x21, waiting for transfers between devices: 7.13 us -> 10.1 us  [box_permute(): return lax.ppermute(array, 'box', [(b, b ^ mask) for b in range(n_box)])]
    ppermute x5 -> x4, starting transfers between devices: 6.85 us -> 5.91 us  [face_permute(): return lax.ppermute(array, ('box', 'face'), pairs)]
    pallas_call x16 -> x15, Pallas kernels: 24 us -> 23.2 us  [call(): pl.pallas_call(kernel, in_specs=[pl.BlockSpec(memory_space=pltpu.SMEM)] +...]
  transfers between devices with their start and end apart: 26 -> 25, of which waited for: 11 -> 7; matrix products, arithmetic and copies ran while one was open for 0% -> 0% of each run, Pallas kernels for 26% -> 29%
where the time goes in v11:
time: 65.9 us; the launch traced here: 65.5 us
  starting transfers between devices  24.7 us (37%)
  Pallas kernels  23.2 us (35%)
  waiting for transfers between devices  14.8 us (22%)
  local copies, waits for them, and re-layouts  2.44 us (4%)
    pallas_call x15, Pallas kernels, call(): pl.pallas_call(kernel, in_specs=[pl.BlockSpec(memory_space=pltpu.SMEM)] +...  23.2 us
    ppermute x21, starting transfers between devices, box_permute(): return lax.ppermute(array, 'box', [(b, b ^ mask) for b in range(n_box)])  18.8 us
    ppermute x21, waiting for transfers between devices, box_permute(): return lax.ppermute(array, 'box', [(b, b ^ mask) for b in range(n_box)])  10.1 us
    ppermute x4, starting transfers between devices, face_permute(): return lax.ppermute(array, ('box', 'face'), pairs)  5.91 us
    ppermute x4, waiting for transfers between devices, face_permute(): return lax.ppermute(array, ('box', 'face'), pairs)  4.73 us
    unnamed x12, local copies, waits for them, and re-layouts  2.36 us
  transfers between devices with their start and end apart: 25, of which 7 were waited for; matrix products, arithmetic and copies ran while one was open for 0% of the time, Pallas kernels for 29%

profile of v11, /device:TPU:1, one launch (start us, length us, event | category | flops | bytes accessed | tf_op | source)
XLA Modules:
  0.0 65.5 jit_solution(7800046989291553441)
XLA Ops:
  0.0 0.1 stack.27.sc
  0.1 2.3 %copy-done = bf16[2,1,1,3,256,1536]{5,4,3,2,1,0:T(8,128)(2,1)S(1)} copy-done((bf16[2,1,1,3,256,1536]{5,4,3,2,1,0:T(8,128)(2,1)S(1)}, bf16[2,1,1,3,256,1536]{5,4,3,2,1,0:T(8,128)(2,1)}, u32[]{:S(2)}) %copy-start) | copy-done | bytes 4718616
  2.4 0.7 %shard_map.55 = (bf16[2,256,512]{2,1,0:T(8,128)(2,1)S(1)}, bf16[2,256,512]{2,1,0:T(8,128)(2,1)S(1)}, bf16[2,128,512]{2,1,0:T(8,128)(2,1)S(1)}, bf16[2,128,512]{2...) custom-call(s32[6]{0:T(128)S(1)} %stack.27.sc, ...), custom_call_target="tpu_custom_call" | custom-call | tf_op jit(solution)/shard_map/pallas_call | solution.py:46
  3.2 0.1 collective-permute-start
  3.3 0.5 collective-permute-start.1
  3.7 0.1 collective-permute-start.2
  3.8 0.4 collective-permute-start.3
  4.2 0.1 collective-permute-start.4
  4.3 0.8 %shard_map.56 = (s32[1,512]{1,0:T(1,128)S(1)}, s32[512,1]{1,0:T(8,128)S(1)}) custom-call(s32[6]{0:T(128)S(1)} %stack.27.sc, s32[8,512]{1,0:T(8,128)S(1)} %bitcast.18, s32[4,512]{1,0:T(4,128)S(1)} %bitcast.19), custom_call_target="tpu_custom_call" | custom-call | tf_op jit(solution)/shard_map/pallas_call | solution.py:46
  5.1 0.5 collective-permute-start.7
  5.6 1.3 %shard_map.57 = (bf16[2,256,512]{2,1,0:T(8,128)(2,1)S(1)}, bf16[2,256,512]{2,1,0:T(8,128)(2,1)S(1)}) custom-call(s32[6]{0:T(128)S(1)} %stack.27.sc, bf16[2,256,512]{2,1,0:T(8,128)(2,1)S(1)} %get-tuple-element.40.own_ref, bf16[2,256,512]{2,1,0:T(8,128)(2,1)S(1)} %collective-permute-done.sib_ref, s32[1,512]{1,0:T(1,128)S(1)} %get-tuple-element.41.comp_ref.refs_12_, ...), custom_call_target="tpu_custom_call" | custom-call | tf_op jit(solution)/shard_map/pallas_call | solution.py:46
  6.9 2.4 %collective-permute-start.11 = (bf16[2,256,512]{2,1,0:T(8,128)(2,1)S(1)}, bf16[2,256,512]{2,1,0:T(8,128)(2,1)S(1)}, u32[]{:S(2)}, u32[]{:S(2)}) collective-permute-start(bf16[2,256,512]{2,1,0:T(8,128)(2,1)S(1)} %get-tuple-element.60), channel_id=1, source_target_pairs={{0,1},{1,0},{2,3},{3,2},{4,5},{5,4},{6,7},{7,6},{8,9},{9,8},{10,11... | collective-permute-start | bytes 1572872 | tf_op jit(solution)/shard_map/ppermute | solution.py:83
  9.3 0.7 %collective-permute-start.5 = (bf16[2,128,512]{2,1,0:T(8,128)(2,1)S(1)}, bf16[2,128,512]{2,1,0:T(8,128)(2,1)S(1)}, u32[]{:S(2)}, u32[]{:S(2)}) collective-permute-start(bf16[2,128,512]{2,1,0:T(8,128)(2,1)S(1)} %get-tuple-element.50.refs_4_), channel_id=1, source_target_pairs={{0,2},{2,0},{4,6},{6,4},{8,10},{10,8},{12,14},{14,12},{16,18},{18,... | collective-permute-start | bytes 786440 | tf_op jit(solution)/shard_map/ppermute | solution.py:76
  10.0 0.1 collective-permute-start.6
  10.1 1.3 %collective-permute-start.12 = (bf16[2,128,512]{2,1,0:T(8,128)(2,1)S(1)}, bf16[2,128,512]{2,1,0:T(8,128)(2,1)S(1)}, u32[]{:S(2)}, u32[]{:S(2)}) collective-permute-start(bf16[2,128,512]{2,1,0:T(8,128)(2,1)S(1)} %bitcast.15), channel_id=1, source_target_pairs={{0,4},{2,6},{4,0},{6,2},{8,12},{10,14},{12,8},{14,10},{16,20},{18,... | collective-permute-start | bytes 786440 | tf_op jit(solution)/shard_map/ppermute | solution.py:76
  11.4 1.1 %shard_map.58 = (bf16[2,128,1024]{2,1,0:T(8,128)(2,1)S(1)}, bf16[2,128,1024]{2,1,0:T(8,128)(2,1)S(1)}, bf16[2,256,1536]{2,1,0:T(8,128)(2,1)S(1)}) custom-call(s32[6]{0:T(128)S(1)} %stack.27.sc, bf16[2,3,256,1536]{3,2,1,0:T(8,128)(2,1)S(1)} %bitcast.12, s32[1,512]{1,0:T(1,128)S(1)} %get-tuple-element.41.comp_ref.refs_12_), custom_call_target="tpu_custom_call" | custom-call | tf_op jit(solution)/shard_map/pallas_call | solution.py:46
  12.5 0.8 %collective-permute-start.10 = (bf16[2,256,512]{2,1,0:T(8,128)(2,1)S(1)}, bf16[2,256,512]{2,1,0:T(8,128)(2,1)S(1)}, u32[]{:S(2)}, u32[]{:S(2)}) collective-permute-start(bf16[2,256,512]{2,1,0:T(8,128)(2,1)S(1)} %bitcast.13), channel_id=1, source_target_pairs={{0,2},{2,0},{4,6},{6,4},{8,10},{10,8},{12,14},{14,12},{16,18},{18,... | collective-permute-start | bytes 1572872 | tf_op jit(solution)/shard_map/ppermute | solution.py:76
  13.3 0.1 collective-permute-start.9
  13.4 2.9 %shard_map.59 = (bf16[2,256,1536]{2,1,0:T(8,128)(2,1)S(1)}, bf16[2,128,1024]{2,1,0:T(8,128)(2,1)S(1)}, bf16[2,128,1024]{2,1,0:T(8,128)(2,1)S(1)}) custom-call(s32[6]{0:T(128)S(1)} %stack.27.sc, bf16[2,128,512]{2,1,0:T(8,128)(2,1)S(1)} %get-tuple-element.46.refs_0_, bf16[2,128,512]{2,1,0:T(8,128)(2,1)S(1)} %get-tuple-element.47.refs_1_, ...), custom_call_target="tpu_custom_call" | custom-call | tf_op jit(solution)/shard_map/pallas_call | solution.py:46
  16.3 1.3 %collective-permute-done.12.refs_1_ = bf16[2,128,512]{2,1,0:T(8,128)(2,1)S(1)} collective-permute-done((bf16[2,128,512]{2,1,0:T(8,128)(2,1)S(1)}, bf16[2,128,512]{2,1,0:T(8,128)(2,1)S(1)}, u32[]{:S(2)}, u32[]{:S(2)}) %collective-permute-start.12) | collective-permute-done | bytes 262176 | tf_op jit(solution)/shard_map/ppermute | solution.py:76
  17.6 3.6 %collective-permute-done.11.rest_0_ = bf16[2,256,512]{2,1,0:T(8,128)(2,1)S(1)} collective-permute-done((bf16[2,256,512]{2,1,0:T(8,128)(2,1)S(1)}, bf16[2,256,512]{2,1,0:T(8,128)(2,1)S(1)}, u32[]{:S(2)}, u32[]{:S(2)}) %collective-permute-start.11) | collective-permute-done | bytes 524320 | tf_op jit(solution)/shard_map/ppermute | solution.py:83
  21.2 1.0 %collective-permute-start.13 = (bf16[2,256,512]{2,1,0:T(8,128)(2,1)S(1)}, bf16[2,256,512]{2,1,0:T(8,128)(2,1)S(1)}, u32[]{:S(2)}, u32[]{:S(2)}) collective-permute-start(bf16[2,256,512]{2,1,0:T(8,128)(2,1)S(1)} %collective-permute-done.11.rest_0_), channel_id=1, source_target_pairs={{0,2},{2,0},{4,6},{6,4},{8,10},{10,8},{12,14},{14,12},{16,18},{18,... | collective-permute-start | bytes 1572872 | tf_op jit(solution)/shard_map/ppermute | solution.py:76
  22.2 1.5 %collective-permute-start.8 = (bf16[2,128,1024]{2,1,0:T(8,128)(2,1)S(1)}, bf16[2,128,1024]{2,1,0:T(8,128)(2,1)S(1)}, u32[]{:S(2)}, u32[]{:S(2)}) collective-permute-start(bf16[2,128,1024]{2,1,0:T(8,128)(2,1)S(1)} %get-tuple-element.54), channel_id=1, source_target_pairs={{0,1},{1,0},{2,3},{3,2},{4,5},{5,4},{6,7},{7,6},{8,9},{9,8},{10,11... | collective-permute-start | bytes 1572872 | tf_op jit(solution)/shard_map/ppermute | solution.py:83
  23.6 0.6 shard_map.60.w_ref
  24.3 1.4 %shard_map.61 = (f32[2,128,1024]{2,1,0:T(8,128)S(1)}, bf16[2,128,512]{2,1,0:T(8,128)(2,1)S(1)}) custom-call(s32[6]{0:T(128)S(1)} %stack.27.sc, bf16[2,128,1024]{2,1,0:T(8,128)(2,1)S(1)} %get-tuple-element.55.keep_ref, bf16[2,128,1024]{2,1,0:T(8,128)(2,1)S(1)} %collective-permute-done.9.recv_ref, bf16[2,512,512]{2,1,0:T(8,128)(2,1)S(1)} %shard_map.60.w_ref, ...), custom_call_target="tpu_custom_call" | custom-call | flops 1000000000 | tf_op jit(solution)/shard_map/pallas_call | solution.py:46
  25.7 1.0 %shard_map.62 = (bf16[2,128,512]{2,1,0:T(8,128)(2,1)S(1)}, bf16[2,128,256]{2,1,0:T(8,128)(2,1)S(1)}, bf16[2,128,256]{2,1,0:T(8,128)(2,1)S(1)}) custom-call(s32[6]{0:T(128)S(1)} %stack.27.sc, f32[2,128,1024]{2,1,0:T(8,128)S(1)} %get-tuple-element.58.acc_ref, bf16[2,128,512]{2,1,0:T(8,128)(2,1)S(1)} %get-tuple-element.59.hid_ref, ...), custom_call_target="tpu_custom_call" | custom-call | tf_op jit(solution)/shard_map/pallas_call | solution.py:46
  26.7 1.3 %collective-permute-start.14 = (bf16[2,128,256]{2,1,0:T(8,128)(2,1)S(1)}, bf16[2,128,256]{2,1,0:T(8,128)(2,1)S(1)}, u32[]{:S(2)}, u32[]{:S(2)}) collective-permute-start(bf16[2,128,256]{2,1,0:T(8,128)(2,1)S(1)} %get-tuple-element.65), channel_id=1, source_target_pairs={{0,4},{2,6},{4,0},{6,2},{8,12},{10,14},{12,8},{14,10},{16,20},{18,... | collective-permute-start | bytes 393224 | tf_op jit(solution)/shard_map/ppermute | solution.py:76
  28.0 3.6 %collective-permute-done.14.x_ref = bf16[2,128,256]{2,1,0:T(8,128)(2,1)S(1)} collective-permute-done((bf16[2,128,256]{2,1,0:T(8,128)(2,1)S(1)}, bf16[2,128,256]{2,1,0:T(8,128)(2,1)S(1)}, u32[]{:S(2)}, u32[]{:S(2)}) %collective-permute-start.14) | collective-permute-done | bytes 131104 | tf_op jit(solution)/shard_map/ppermute | solution.py:76
  31.6 0.6 shard_map.63.own_ref
  32.2 1.3 %collective-permute-start.20 = (bf16[2,128,768]{2,1,0:T(8,128)(2,1)S(1)}, bf16[2,128,768]{2,1,0:T(8,128)(2,1)S(1)}, u32[]{:S(2)}, u32[]{:S(2)}) collective-permute-start(bf16[2,128,768]{2,1,0:T(8,128)(2,1)S(1)} %shard_map.63.own_ref), channel_id=1, source_target_pairs={{0,4},{2,6},{4,0},{6,2},{8,12},{10,14},{12,8},{14,10},{16,20},{18,... | collective-permute-start | bytes 1179656 | tf_op jit(solution)/shard_map/ppermute | solution.py:76
  33.5 0.2 collective-permute-start.21
  33.7 1.7 %collective-permute-start.18 = (bf16[2,128,512]{2,1,0:T(8,128)(2,1)S(1)}, bf16[2,128,512]{2,1,0:T(8,128)(2,1)S(1)}, u32[]{:S(2)}, u32[]{:S(2)}) collective-permute-start(bf16[2,128,512]{2,1,0:T(8,128)(2,1)S(1)} %bitcast.16), channel_id=1, source_target_pairs={{0,2},{2,0},{4,6},{6,4},{8,10},{10,8},{12,14},{14,12},{16,18},{18,... | collective-permute-start | bytes 786440 | tf_op jit(solution)/shard_map/ppermute | solution.py:76
  35.4 0.4 collective-permute-done.8.rest_2_.refs_0_
  35.7 0.8 %collective-permute-start.15 = (bf16[2,128,1024]{2,1,0:T(8,128)(2,1)S(1)}, bf16[2,128,1024]{2,1,0:T(8,128)(2,1)S(1)}, u32[]{:S(2)}, u32[]{:S(2)}) collective-permute-start(bf16[2,128,1024]{2,1,0:T(8,128)(2,1)S(1)} %collective-permute-done.8.rest_2_.refs_0_), channel_id=1, source_target_pairs={{0,2},{2,0},{4,6},{6,4},{8,10},{10,8},{12,14},{14,12},{16,18},{18,... | collective-permute-start | bytes 1572872 | tf_op jit(solution)/shard_map/ppermute | solution.py:76
  36.5 1.8 %collective-permute-start.16 = (bf16[2,128,1024]{2,1,0:T(8,128)(2,1)S(1)}, bf16[2,128,1024]{2,1,0:T(8,128)(2,1)S(1)}, u32[]{:S(2)}, u32[]{:S(2)}) collective-permute-start(bf16[2,128,1024]{2,1,0:T(8,128)(2,1)S(1)} %get-tuple-element.68), channel_id=1, source_target_pairs={{0,1},{1,0},{2,3},{3,2},{4,5},{5,4},{6,7},{7,6},{8,9},{9,8},{10,11... | collective-permute-start | bytes 1572872 | tf_op jit(solution)/shard_map/ppermute | solution.py:83
  38.4 0.7 %shard_map.65.refs_6_ = bf16[2,512,512]{2,1,0:T(8,128)(2,1)S(1)} custom-call(s32[6]{0:T(128)S(1)} %stack.27.sc, bf16[2,128,512]{2,1,0:T(8,128)(2,1)S(1)} %bitcast.17, bf16[2,128,512]{2,1,0:T(8,128)(2,1)S(1)} %collective-permute-done.12.refs_1_, bf16[2,128,512]{2,1,0:T(8,128)(2,1)S(1)} %collective-permute-done.18.refs_2_, ...), custom_call_target="tpu_custom_call" | custom-call | tf_op jit(solution)/shard_map/pallas_call | solution.py:46
  39.0 2.7 %collective-permute-done.20.x_ref = bf16[2,128,768]{2,1,0:T(8,128)(2,1)S(1)} collective-permute-done((bf16[2,128,768]{2,1,0:T(8,128)(2,1)S(1)}, bf16[2,128,768]{2,1,0:T(8,128)(2,1)S(1)}, u32[]{:S(2)}, u32[]{:S(2)}) %collective-permute-start.20) | collective-permute-done | bytes 393248 | tf_op jit(solution)/shard_map/ppermute | solution.py:76
  41.8 0.6 shard_map.67.refs_0_
  42.4 0.7 %collective-permute-done.21.own_ref = bf16[2,128,768]{2,1,0:T(8,128)(2,1)S(1)} collective-permute-done((bf16[2,128,768]{2,1,0:T(8,128)(2,1)S(1)}, bf16[2,128,768]{2,1,0:T(8,128)(2,1)S(1)}, u32[]{:S(2)}, u32[]{:S(2)}) %collective-permute-start.21) | collective-permute-done | bytes 393248 | tf_op jit(solution)/shard_map/ppermute | solution.py:83
  43.1 2.1 %collective-permute-start.22 = (bf16[2,128,768]{2,1,0:T(8,128)(2,1)S(1)}, bf16[2,128,768]{2,1,0:T(8,128)(2,1)S(1)}, u32[]{:S(2)}, u32[]{:S(2)}) collective-permute-start(bf16[2,128,768]{2,1,0:T(8,128)(2,1)S(1)} %collective-permute-done.21.own_ref), channel_id=1, source_target_pairs={{0,4},{2,6},{4,0},{6,2},{8,12},{10,14},{12,8},{14,10},{16,20},{18,... | collective-permute-start | bytes 1179656 | tf_op jit(solution)/shard_map/ppermute | solution.py:76
  45.2 2.2 %collective-permute-start.23 = (bf16[2,128,1536]{2,1,0:T(8,128)(2,1)S(1)}, bf16[2,128,1536]{2,1,0:T(8,128)(2,1)S(1)}, u32[]{:S(2)}, u32[]{:S(2)}) collective-permute-start(bf16[2,128,1536]{2,1,0:T(8,128)(2,1)S(1)} %shard_map.67.refs_0_), channel_id=1, source_target_pairs={{0,2},{2,0},{4,6},{6,4},{8,10},{10,8},{12,14},{14,12},{16,18},{18,... | collective-permute-start | bytes 2359304 | tf_op jit(solution)/shard_map/ppermute | solution.py:76
  47.4 4.2 %shard_map.64.refs_5_ = bf16[2,512,1536]{2,1,0:T(8,128)(2,1)S(1)} custom-call(s32[6]{0:T(128)S(1)} %stack.27.sc, bf16[2,512,512]{2,1,0:T(8,128)(2,1)S(1)} %shard_map.60.w_ref, bf16[2,256,512]{2,1,0:T(8,128)(2,1)S(1)} %get-tuple-element.42.end_ref.refs_14_.own_ref, bf16[2,256,512]{2,1,0:T(8,128)(2,1)S(1)} %collective-permute-done.7.refs_15_.endsib_ref.sib_ref, ...), custom_call_target="tpu_custom_call" | custom-call | tf_op jit(solution)/shard_map/pallas_call | solution.py:46
  51.7 0.6 shard_map.68.refs_1_
  52.3 3.6 %collective-permute-start.24 = (bf16[2,128,1536]{2,1,0:T(8,128)(2,1)S(1)}, bf16[2,128,1536]{2,1,0:T(8,128)(2,1)S(1)}, u32[]{:S(2)}, u32[]{:S(2)}) collective-permute-start(bf16[2,128,1536]{2,1,0:T(8,128)(2,1)S(1)} %shard_map.68.refs_1_), channel_id=1, source_target_pairs={{0,2},{2,0},{4,6},{6,4},{8,10},{10,8},{12,14},{14,12},{16,18},{18,... | collective-permute-start | bytes 2359304 | tf_op jit(solution)/shard_map/ppermute | solution.py:76
  55.9 0.3 collective-permute-start.17
  56.2 2.4 %collective-permute-done.17.refs_3_ = bf16[2,128,1024]{2,1,0:T(8,128)(2,1)S(1)} collective-permute-done((bf16[2,128,1024]{2,1,0:T(8,128)(2,1)S(1)}, bf16[2,128,1024]{2,1,0:T(8,128)(2,1)S(1)}, u32[]{:S(2)}, u32[]{:S(2)}) %collective-permute-start.17) | collective-permute-done | bytes 524320 | tf_op jit(solution)/shard_map/ppermute | solution.py:76
  58.6 3.4 %shard_map.66 = (bf16[2,512,512]{2,1,0:T(8,128)(2,1)S(1)}, bf16[512,512]{1,0:T(8,128)(2,1)S(1)}, bf16[512,512]{1,0:T(8,128)(2,1)S(1)}) custom-call(s32[6]{0:T(128)S(1)} %stack.27.sc, bf16[2,256,1536]{2,1,0:T(8,128)(2,1)S(1)} %get-tuple-element.45.end_ref, bf16[2,256,1536]{2,1,0:T(8,128)(2,1)S(1)} %get-tuple-element.53.kept_ref, ...), custom_call_target="tpu_custom_call" | custom-call | flops 2000000000 | tf_op jit(solution)/shard_map/pallas_call | solution.py:46
  62.0 3.4 %shard_map.69 = bf16[2,1,256,1536]{3,2,1,0:T(8,128)(2,1)} custom-call(s32[6]{0:T(128)S(1)} %stack.27.sc, bf16[2,512,512]{2,1,0:T(8,128)(2,1)S(1)} %get-tuple-element.69.hid_ref, bf16[512,512]{1,0:T(8,128)(2,1)S(1)} %get-tuple-element.70.first_ref, bf16[512,512]{1,0:T(8,128)(2,1)S(1)} %get-tuple-element.71.slots_ref, ...), custom_call_target="tpu_custom_call" | custom-call | tf_op jit(solution)/shard_map/pallas_call | solution.py:46
  (30 shorter events, 0.1 us)
Async XLA Ops:
  0.0 4.3 %copy-start.4 = (s32[1,8,512]{2,1,0:T(8,128)S(1)}, s32[1,8,512]{2,1,0:T(8,128)}, u32[]{:S(2)}) copy-start(s32[1,8,512]{2,1,0:T(8,128)} %param.8) | copy-start | bytes 49156
  0.1 2.3 %copy-start = (bf16[2,1,1,3,256,1536]{5,4,3,2,1,0:T(8,128)(2,1)S(1)}, bf16[2,1,1,3,256,1536]{5,4,3,2,1,0:T(8,128)(2,1)}, u32[]{:S(2)}) copy-start(bf16[2,1,1,3,256,1536]{5,4,3,2,1,0:T(8,128)(2,1)} %param.5) | copy-start | bytes 14155780
  2.4 1.9 %copy-start.5 = (s32[1,4,512]{2,1,0:T(4,128)S(1)}, s32[1,4,512]{2,1,0:T(4,128)}, u32[]{:S(2)}) copy-start(s32[1,4,512]{2,1,0:T(4,128)} %param.9) | copy-start | bytes 24580
  2.4 8.9 %copy-start.1 = (bf16[2,1,1,3,256,1536]{5,4,3,2,1,0:T(8,128)(2,1)S(1)}, bf16[2,1,1,3,256,1536]{5,4,3,2,1,0:T(8,128)(2,1)}, u32[]{:S(2)}) copy-start(bf16[2,1,1,3,256,1536]{5,4,3,2,1,0:T(8,128)(2,1)} %param.5) | copy-start | bytes 14155780
  3.1 7.0 %copy-start.3 = (bf16[2,1,128,512]{3,2,1,0:T(8,128)(2,1)S(1)}, bf16[2,1,128,512]{3,2,1,0:T(8,128)(2,1)}, u32[]{:S(2)}) copy-start(bf16[2,1,128,512]{3,2,1,0:T(8,128)(2,1)} %param.7) | copy-start | bytes 786436
  3.2 2.0 %collective-permute-start = (bf16[2,256,512]{2,1,0:T(8,128)(2,1)S(1)}, bf16[2,256,512]{2,1,0:T(8,128)(2,1)S(1)}, u32[]{:S(2)}, u32[]{:S(2)}) collective-permute-start(bf16[2,256,512]{2,1,0:T(8,128)(2,1)S(1)} %get-tuple-element.40.own_ref), channel_id=1, source_target_pairs={{0,2},{2,0},{4,6},{6,4},{8,10},{10,8},{12,14},{14,12},{16,18},{18,... | collective-permute-start | bytes 1572872 | tf_op jit(solution)/shard_map/ppermute | solution.py:76
  3.3 3.6 %collective-permute-start.1 = (bf16[2,128,512]{2,1,0:T(8,128)(2,1)S(1)}, bf16[2,128,512]{2,1,0:T(8,128)(2,1)S(1)}, u32[]{:S(2)}, u32[]{:S(2)}) collective-permute-start(bf16[2,128,512]{2,1,0:T(8,128)(2,1)S(1)} %get-tuple-element.46.refs_0_), channel_id=1, source_target_pairs={{0,2},{2,0},{4,6},{6,4},{8,10},{10,8},{12,14},{14,12},{16,18},{18,... | collective-permute-start | bytes 786440 | tf_op jit(solution)/shard_map/ppermute | solution.py:76
  3.7 5.6 %collective-permute-start.2 = (bf16[2,128,512]{2,1,0:T(8,128)(2,1)S(1)}, bf16[2,128,512]{2,1,0:T(8,128)(2,1)S(1)}, u32[]{:S(2)}, u32[]{:S(2)}) collective-permute-start(bf16[2,128,512]{2,1,0:T(8,128)(2,1)S(1)} %get-tuple-element.47.refs_1_), channel_id=1, source_target_pairs={{0,2},{2,0},{4,6},{6,4},{8,10},{10,8},{12,14},{14,12},{16,18},{18,... | collective-permute-start | bytes 786440 | tf_op jit(solution)/shard_map/ppermute | solution.py:76
  3.8 6.2 %collective-permute-start.3 = (bf16[2,128,512]{2,1,0:T(8,128)(2,1)S(1)}, bf16[2,128,512]{2,1,0:T(8,128)(2,1)S(1)}, u32[]{:S(2)}, u32[]{:S(2)}) collective-permute-start(bf16[2,128,512]{2,1,0:T(8,128)(2,1)S(1)} %get-tuple-element.48.refs_2_), channel_id=1, source_target_pairs={{0,2},{2,0},{4,6},{6,4},{8,10},{10,8},{12,14},{14,12},{16,18},{18,... | collective-permute-start | bytes 786440 | tf_op jit(solution)/shard_map/ppermute | solution.py:76
  4.2 5.8 %collective-permute-start.4 = (bf16[2,128,512]{2,1,0:T(8,128)(2,1)S(1)}, bf16[2,128,512]{2,1,0:T(8,128)(2,1)S(1)}, u32[]{:S(2)}, u32[]{:S(2)}) collective-permute-start(bf16[2,128,512]{2,1,0:T(8,128)(2,1)S(1)} %get-tuple-element.49.refs_3_), channel_id=1, source_target_pairs={{0,2},{2,0},{4,6},{6,4},{8,10},{10,8},{12,14},{14,12},{16,18},{18,... | collective-permute-start | bytes 786440 | tf_op jit(solution)/shard_map/ppermute | solution.py:76
  5.1 8.2 %collective-permute-start.7 = (bf16[2,256,512]{2,1,0:T(8,128)(2,1)S(1)}, bf16[2,256,512]{2,1,0:T(8,128)(2,1)S(1)}, u32[]{:S(2)}, u32[]{:S(2)}) collective-permute-start(bf16[2,256,512]{2,1,0:T(8,128)(2,1)S(1)} %get-tuple-element.42.end_ref.refs_14_.own_ref), channel_id=1, source_target_pairs={{0,2},{2,0},{4,6},{6,4},{8,10},{10,8},{12,14},{14,12},{16,18},{18,... | collective-permute-start | bytes 1572872 | tf_op jit(solution)/shard_map/ppermute | solution.py:76
  6.9 14.3 %collective-permute-start.11 = (bf16[2,256,512]{2,1,0:T(8,128)(2,1)S(1)}, bf16[2,256,512]{2,1,0:T(8,128)(2,1)S(1)}, u32[]{:S(2)}, u32[]{:S(2)}) collective-permute-start(bf16[2,256,512]{2,1,0:T(8,128)(2,1)S(1)} %get-tuple-element.60), channel_id=1, source_target_pairs={{0,1},{1,0},{2,3},{3,2},{4,5},{5,4},{6,7},{7,6},{8,9},{9,8},{10,11... | collective-permute-start | bytes 1572872 | tf_op jit(solution)/shard_map/ppermute | solution.py:83
  9.3 3.2 %collective-permute-start.5 = (bf16[2,128,512]{2,1,0:T(8,128)(2,1)S(1)}, bf16[2,128,512]{2,1,0:T(8,128)(2,1)S(1)}, u32[]{:S(2)}, u32[]{:S(2)}) collective-permute-start(bf16[2,128,512]{2,1,0:T(8,128)(2,1)S(1)} %get-tuple-element.50.refs_4_), channel_id=1, source_target_pairs={{0,2},{2,0},{4,6},{6,4},{8,10},{10,8},{12,14},{14,12},{16,18},{18,... | collective-permute-start | bytes 786440 | tf_op jit(solution)/shard_map/ppermute | solution.py:76
  10.0 3.3 %collective-permute-start.6 = (bf16[2,128,512]{2,1,0:T(8,128)(2,1)S(1)}, bf16[2,128,512]{2,1,0:T(8,128)(2,1)S(1)}, u32[]{:S(2)}, u32[]{:S(2)}) collective-permute-start(bf16[2,128,512]{2,1,0:T(8,128)(2,1)S(1)} %get-tuple-element.51.refs_5_), channel_id=1, source_target_pairs={{0,2},{2,0},{4,6},{6,4},{8,10},{10,8},{12,14},{14,12},{16,18},{18,... | collective-permute-start | bytes 786440 | tf_op jit(solution)/shard_map/ppermute | solution.py:76
  10.1 2.4 %copy-start.2 = (bf16[2,1,256,512]{3,2,1,0:T(8,128)(2,1)S(1)}, bf16[2,1,256,512]{3,2,1,0:T(8,128)(2,1)}, u32[]{:S(2)}) copy-start(bf16[2,1,256,512]{3,2,1,0:T(8,128)(2,1)} %param.6) | copy-start | bytes 1572868
  10.1 7.5 %collective-permute-start.12 = (bf16[2,128,512]{2,1,0:T(8,128)(2,1)S(1)}, bf16[2,128,512]{2,1,0:T(8,128)(2,1)S(1)}, u32[]{:S(2)}, u32[]{:S(2)}) collective-permute-start(bf16[2,128,512]{2,1,0:T(8,128)(2,1)S(1)} %bitcast.15), channel_id=1, source_target_pairs={{0,4},{2,6},{4,0},{6,2},{8,12},{10,14},{12,8},{14,10},{16,20},{18,... | collective-permute-start | bytes 786440 | tf_op jit(solution)/shard_map/ppermute | solution.py:76
  12.5 11.1 %collective-permute-start.10 = (bf16[2,256,512]{2,1,0:T(8,128)(2,1)S(1)}, bf16[2,256,512]{2,1,0:T(8,128)(2,1)S(1)}, u32[]{:S(2)}, u32[]{:S(2)}) collective-permute-start(bf16[2,256,512]{2,1,0:T(8,128)(2,1)S(1)} %bitcast.13), channel_id=1, source_target_pairs={{0,2},{2,0},{4,6},{6,4},{8,10},{10,8},{12,14},{14,12},{16,18},{18,... | collective-permute-start | bytes 1572872 | tf_op jit(solution)/shard_map/ppermute | solution.py:76
  13.3 11.0 %collective-permute-start.9 = (bf16[2,128,1024]{2,1,0:T(8,128)(2,1)S(1)}, bf16[2,128,1024]{2,1,0:T(8,128)(2,1)S(1)}, u32[]{:S(2)}, u32[]{:S(2)}) collective-permute-start(bf16[2,128,1024]{2,1,0:T(8,128)(2,1)S(1)} %get-tuple-element.56), channel_id=1, source_target_pairs={{0,2},{2,0},{4,6},{6,4},{8,10},{10,8},{12,14},{14,12},{16,18},{18,... | collective-permute-start | bytes 1572872 | tf_op jit(solution)/shard_map/ppermute | solution.py:76
  21.2 4.5 %collective-permute-start.13 = (bf16[2,256,512]{2,1,0:T(8,128)(2,1)S(1)}, bf16[2,256,512]{2,1,0:T(8,128)(2,1)S(1)}, u32[]{:S(2)}, u32[]{:S(2)}) collective-permute-start(bf16[2,256,512]{2,1,0:T(8,128)(2,1)S(1)} %collective-permute-done.11.rest_0_), channel_id=1, source_target_pairs={{0,2},{2,0},{4,6},{6,4},{8,10},{10,8},{12,14},{14,12},{16,18},{18,... | collective-permute-start | bytes 1572872 | tf_op jit(solution)/shard_map/ppermute | solution.py:76
  22.2 13.6 %collective-permute-start.8 = (bf16[2,128,1024]{2,1,0:T(8,128)(2,1)S(1)}, bf16[2,128,1024]{2,1,0:T(8,128)(2,1)S(1)}, u32[]{:S(2)}, u32[]{:S(2)}) collective-permute-start(bf16[2,128,1024]{2,1,0:T(8,128)(2,1)S(1)} %get-tuple-element.54), channel_id=1, source_target_pairs={{0,1},{1,0},{2,3},{3,2},{4,5},{5,4},{6,7},{7,6},{8,9},{9,8},{10,11... | collective-permute-start | bytes 1572872 | tf_op jit(solution)/shard_map/ppermute | solution.py:83
  26.7 4.9 %collective-permute-start.14 = (bf16[2,128,256]{2,1,0:T(8,128)(2,1)S(1)}, bf16[2,128,256]{2,1,0:T(8,128)(2,1)S(1)}, u32[]{:S(2)}, u32[]{:S(2)}) collective-permute-start(bf16[2,128,256]{2,1,0:T(8,128)(2,1)S(1)} %get-tuple-element.65), channel_id=1, source_target_pairs={{0,4},{2,6},{4,0},{6,2},{8,12},{10,14},{12,8},{14,10},{16,20},{18,... | collective-permute-start | bytes 393224 | tf_op jit(solution)/shard_map/ppermute | solution.py:76
  32.2 9.6 %collective-permute-start.20 = (bf16[2,128,768]{2,1,0:T(8,128)(2,1)S(1)}, bf16[2,128,768]{2,1,0:T(8,128)(2,1)S(1)}, u32[]{:S(2)}, u32[]{:S(2)}) collective-permute-start(bf16[2,128,768]{2,1,0:T(8,128)(2,1)S(1)} %shard_map.63.own_ref), channel_id=1, source_target_pairs={{0,4},{2,6},{4,0},{6,2},{8,12},{10,14},{12,8},{14,10},{16,20},{18,... | collective-permute-start | bytes 1179656 | tf_op jit(solution)/shard_map/ppermute | solution.py:76
  33.5 9.6 %collective-permute-start.21 = (bf16[2,128,768]{2,1,0:T(8,128)(2,1)S(1)}, bf16[2,128,768]{2,1,0:T(8,128)(2,1)S(1)}, u32[]{:S(2)}, u32[]{:S(2)}) collective-permute-start(bf16[2,128,768]{2,1,0:T(8,128)(2,1)S(1)} %shard_map.63.own_ref), channel_id=1, source_target_pairs={{0,1},{1,0},{2,3},{3,2},{4,5},{5,4},{6,7},{7,6},{8,9},{9,8},{10,11... | collective-permute-start | bytes 1179656 | tf_op jit(solution)/shard_map/ppermute | solution.py:83
  33.7 2.8 %collective-permute-start.18 = (bf16[2,128,512]{2,1,0:T(8,128)(2,1)S(1)}, bf16[2,128,512]{2,1,0:T(8,128)(2,1)S(1)}, u32[]{:S(2)}, u32[]{:S(2)}) collective-permute-start(bf16[2,128,512]{2,1,0:T(8,128)(2,1)S(1)} %bitcast.16), channel_id=1, source_target_pairs={{0,2},{2,0},{4,6},{6,4},{8,10},{10,8},{12,14},{14,12},{16,18},{18,... | collective-permute-start | bytes 786440 | tf_op jit(solution)/shard_map/ppermute | solution.py:76
  35.3 3.0 %collective-permute-start.19 = (bf16[2,128,512]{2,1,0:T(8,128)(2,1)S(1)}, bf16[2,128,512]{2,1,0:T(8,128)(2,1)S(1)}, u32[]{:S(2)}, u32[]{:S(2)}) collective-permute-start(bf16[2,128,512]{2,1,0:T(8,128)(2,1)S(1)} %collective-permute-done.12.refs_1_), channel_id=1, source_target_pairs={{0,2},{2,0},{4,6},{6,4},{8,10},{10,8},{12,14},{14,12},{16,18},{18,... | collective-permute-start | bytes 786440 | tf_op jit(solution)/shard_map/ppermute | solution.py:76
  35.7 11.7 %collective-permute-start.15 = (bf16[2,128,1024]{2,1,0:T(8,128)(2,1)S(1)}, bf16[2,128,1024]{2,1,0:T(8,128)(2,1)S(1)}, u32[]{:S(2)}, u32[]{:S(2)}) collective-permute-start(bf16[2,128,1024]{2,1,0:T(8,128)(2,1)S(1)} %collective-permute-done.8.rest_2_.refs_0_), channel_id=1, source_target_pairs={{0,2},{2,0},{4,6},{6,4},{8,10},{10,8},{12,14},{14,12},{16,18},{18,... | collective-permute-start | bytes 1572872 | tf_op jit(solution)/shard_map/ppermute | solution.py:76
  36.5 19.4 %collective-permute-start.16 = (bf16[2,128,1024]{2,1,0:T(8,128)(2,1)S(1)}, bf16[2,128,1024]{2,1,0:T(8,128)(2,1)S(1)}, u32[]{:S(2)}, u32[]{:S(2)}) collective-permute-start(bf16[2,128,1024]{2,1,0:T(8,128)(2,1)S(1)} %get-tuple-element.68), channel_id=1, source_target_pairs={{0,1},{1,0},{2,3},{3,2},{4,5},{5,4},{6,7},{7,6},{8,9},{9,8},{10,11... | collective-permute-start | bytes 1572872 | tf_op jit(solution)/shard_map/ppermute | solution.py:83
  43.1 8.6 %collective-permute-start.22 = (bf16[2,128,768]{2,1,0:T(8,128)(2,1)S(1)}, bf16[2,128,768]{2,1,0:T(8,128)(2,1)S(1)}, u32[]{:S(2)}, u32[]{:S(2)}) collective-permute-start(bf16[2,128,768]{2,1,0:T(8,128)(2,1)S(1)} %collective-permute-done.21.own_ref), channel_id=1, source_target_pairs={{0,4},{2,6},{4,0},{6,2},{8,12},{10,14},{12,8},{14,10},{16,20},{18,... | collective-permute-start | bytes 1179656 | tf_op jit(solution)/shard_map/ppermute | solution.py:76
  45.2 16.8 %collective-permute-start.23 = (bf16[2,128,1536]{2,1,0:T(8,128)(2,1)S(1)}, bf16[2,128,1536]{2,1,0:T(8,128)(2,1)S(1)}, u32[]{:S(2)}, u32[]{:S(2)}) collective-permute-start(bf16[2,128,1536]{2,1,0:T(8,128)(2,1)S(1)} %shard_map.67.refs_0_), channel_id=1, source_target_pairs={{0,2},{2,0},{4,6},{6,4},{8,10},{10,8},{12,14},{14,12},{16,18},{18,... | collective-permute-start | bytes 2359304 | tf_op jit(solution)/shard_map/ppermute | solution.py:76
  52.3 9.7 %collective-permute-start.24 = (bf16[2,128,1536]{2,1,0:T(8,128)(2,1)S(1)}, bf16[2,128,1536]{2,1,0:T(8,128)(2,1)S(1)}, u32[]{:S(2)}, u32[]{:S(2)}) collective-permute-start(bf16[2,128,1536]{2,1,0:T(8,128)(2,1)S(1)} %shard_map.68.refs_1_), channel_id=1, source_target_pairs={{0,2},{2,0},{4,6},{6,4},{8,10},{10,8},{12,14},{14,12},{16,18},{18,... | collective-permute-start | bytes 2359304 | tf_op jit(solution)/shard_map/ppermute | solution.py:76
  55.9 2.7 %collective-permute-start.17 = (bf16[2,128,1024]{2,1,0:T(8,128)(2,1)S(1)}, bf16[2,128,1024]{2,1,0:T(8,128)(2,1)S(1)}, u32[]{:S(2)}, u32[]{:S(2)}) collective-permute-start(bf16[2,128,1024]{2,1,0:T(8,128)(2,1)S(1)} %collective-permute-done.16.refs_2_), channel_id=1, source_target_pairs={{0,2},{2,0},{4,6},{6,4},{8,10},{10,8},{12,14},{14,12},{16,18},{18,... | collective-permute-start | bytes 1572872 | tf_op jit(solution)/shard_map/ppermute | solution.py:76

commit v12 on v11

--- a/solution.py
+++ b/solution.py
@@ -11,7 +11,9 @@
 F32 = jnp.float32
 VMEM_BYTES = 16 * 1024 * 1024
 JOIN_COST = 300000000
-OWN_COST = 1_000_000_000
+SLOTS_COST = 0
+OWN_COST = 700000000
+SOLVED_COST = 2200000000
 KEEP_COST = 2_000_000_000
 
 
@@ -103,7 +105,8 @@
         comp_out[...] = jnp.where(jnp.logical_and(place >= 0, place < k), found, -1)
 
     comp, skel_col = call(
-        slots_kernel, scalars, [skel_first[0], skel_second[0]], [sds((1, k), jnp.int32), sds((k, 1), jnp.int32)]
+        slots_kernel, scalars, [skel_first[0], skel_second[0]], [sds((1, k), jnp.int32), sds((k, 1), jnp.int32)],
+        cost=SLOTS_COST,
     )
 
     def parts_kernel(sc, leaf_ref, end_out, side_out, *rows_outs):
@@ -118,37 +121,42 @@
     )
     sides_sib = box_permute(sides_raw, 1)
     end_sib = box_permute(end_own, 1)
-    s_sib = [box_permute(a, 1) for a in s_rows]
-
-    def side_kernel(sc, own_ref, sib_ref, comp_ref, end_ref, side_out, send_out):
+    s_sib = [box_permute(after(a, comp), 1) for a in s_rows]
+
+    def side_kernel(sc, own_ref, sib_ref, comp_ref, end_ref, side_out, *send_outs):
         p, q = sc[0], sc[1]
         pick_own = column_picker(comp_ref[...], p * k, k)
         pick_sib = column_picker(comp_ref[...], (1 - p) * k, k)
         side = dot(flat(own_ref[...]), pick_own) + dot(flat(sib_ref[...]), pick_sib)
         side_out[...] = side.astype(BF16).reshape(2, fr, k)
-        send_out[...] = jnp.where(p == q, end_ref[...], side_out[...])
-
-    side, first_send = call(
-        side_kernel, scalars, [sides_raw, sides_sib, comp, end_own], [sds((2, fr, k), BF16)] * 2
-    )
-    first_far = over_face(first_send)
-
-    def ends_kernel(sc, leaf_ref, comp_ref, keep_out, send_out, end_out):
+        for h, send_out in enumerate(send_outs):
+            take = slice(h * hr, (h + 1) * hr)
+            send_out[...] = jnp.where(p == q, end_ref[:, take, :], side_out[:, take, :])
+
+    side, *first_send = call(
+        side_kernel, scalars, [sides_raw, sides_sib, comp, end_own],
+        [sds((2, fr, k), BF16)] + [sds((2, hr, k), BF16)] * 2,
+    )
+    first_far = [face_permute(a, s) for s in range(1, n_face) for a in first_send]
+
+    def ends_kernel(sc, leaf_ref, comp_ref, keep_out, couple_out, slots_out, end_out):
         p = sc[0]
         pick_own = column_picker(comp_ref[...], p * k, k)
         for t in range(2):
             end_out[t, :, : 2 * k] = leaf_ref[t, p, :, : 2 * k]
             end_out[t, :, 2 * k :] = dot(leaf_ref[t, p, :, 2 * k :], pick_own).astype(BF16)
         couple = pl.ds(pl.multiple_of((1 - p) * k, k), k)
-        for ref, take in zip((keep_out, send_out), halves(p)):
-            ref[:, :, :k] = end_out[:, take, couple]
-            ref[:, :, k:] = end_out[:, take, 2 * k :]
-
-    v_keep, v_send, end_kept = call(
+        mine, other = halves(p)
+        keep_out[:, :, :k] = end_out[:, mine, couple]
+        keep_out[:, :, k:] = end_out[:, mine, 2 * k :]
+        couple_out[...] = end_out[:, other, couple]
+        slots_out[...] = end_out[:, other, 2 * k :]
+
+    v_keep, *v_send, end_kept = call(
         ends_kernel, after(scalars, side), [leaf, comp],
-        [sds((2, hr, 2 * k), BF16)] * 2 + [sds((2, fr, 3 * k), BF16)],
-    )
-    v_recv = box_permute(v_send, 1)
+        [sds((2, hr, 2 * k), BF16)] + [sds((2, hr, k), BF16)] * 2 + [sds((2, fr, 3 * k), BF16)],
+    )
+    v_recv = [box_permute(a, 1) for a in v_send]
 
     w_one, w_two = w_first[:, 0], w_second[:, 0]
     w_one_sib = box_permute(after(w_one, side), 1)
@@ -238,13 +246,14 @@
     def piece(hidden, start, count):
         return stacked(hidden[0][:, start : start + count], hidden[1][:, start : start + count])
 
-    def iface_kernel(sc, keep_ref, recv_ref, w_ref, end_ref, endsib_ref, side_ref,
+    def iface_kernel(sc, keep_ref, couple_ref, slots_ref, w_ref, end_ref, endsib_ref, side_ref,
                      acc_out, hid_out, rows):
         p, q = sc[0], sc[1]
 
         @pl.when(p == q)
         def _():
-            rows[...] = recv_ref[...]
+            rows[:, :, :k] = couple_ref[...]
+            rows[:, :, k:] = slots_ref[...]
 
         @pl.when(p != q)
         def _():
@@ -261,22 +270,22 @@
         acc_out[:, :, k:] = rows[:, :, k:].astype(F32) - dot(left, flat(side_ref[...])).reshape(2, hr, k)
 
     v_acc, v_hid = call(
-        iface_kernel, scalars, [v_keep, v_recv, weight_one, end_own, end_sib, side],
+        iface_kernel, scalars, [v_keep, *v_recv, weight_one, end_own, end_sib, side],
         [sds((2, hr, 2 * k), F32), sds((2, hr, k), BF16)],
         scratch=[pltpu.VMEM((2, hr, 2 * k), BF16)], cost=OWN_COST,
     )
     first_fwd = [box_permute(after(a, kept, w_two_x), 1) for a in first_far]
 
     def iface_far_kernel(sc, acc_ref, hid_ref, *rest):
-        far, fwd = rest[:nf], rest[nf : 2 * nf]
-        end_out, keep_out, send_out = rest[2 * nf :]
+        far, fwd = rest[: 2 * nf], rest[2 * nf : 4 * nf]
+        end_out, keep_out, send_out = rest[4 * nf :]
         q = sc[1]
         is_end = sc[0] == q
         hidden = [hid_ref[0], hid_ref[1]]
         total = acc_ref[...]
-        for s in range(nf):
-            left = piece(hidden, (s + 1) * fr, fr)
-            mine, other = dot(left, flat(far[s][...])), dot(left, flat(fwd[s][...]))
+        for i in range(2 * nf):
+            left = piece(hidden, fr + i * hr, hr)
+            mine, other = dot(left, flat(far[i][...])), dot(left, flat(fwd[i][...]))
             both = [jnp.where(is_end, mine, other), jnp.where(is_end, other, mine)]
             total = total - jnp.concatenate(both, axis=1).reshape(2, hr, 2 * k)
         total = total.astype(BF16)
@@ -311,8 +320,9 @@
             out_ref[:, :, cols] = dot(left, right).astype(BF16).reshape(2, k, k)
 
     def weighted_one_kernel(sc, w_ref, own_ref, sib_ref, side_ref, *rest):
-        refs = [rest[i * nf : (i + 1) * nf] for i in range(4)]
-        out_ref, rows = rest[4 * nf :]
+        refs = [rest[i * nf : (i + 1) * nf] for i in range(6)]
+        far, fwd = rest[: 2 * nf], rest[2 * nf : 4 * nf]
+        out_ref, rows = rest[6 * nf :]
         p, q = sc[0], sc[1]
         is_end = p == q
         first_cols = pl.ds(pl.multiple_of(q * k, k), k)
@@ -321,17 +331,19 @@
         rows[0, :, :, pl.ds(pl.multiple_of((1 - p) * k, k), k)] = sib_ref[...]
         rows[0, :, :, 2 * k :] = side_ref[...]
         for s in range(nf):
-            mine, other = refs[0][s][...], refs[1][s][...]
-            rows[s + 1, :, :, first_cols] = jnp.where(is_end, mine, other)
-            rows[s + 1, :, :, 2 * k :] = jnp.where(is_end, other, mine)
-            for take, parts in zip(halves(p), refs[2:]):
+            for h in range(2):
+                take = slice(h * hr, (h + 1) * hr)
+                mine, other = far[2 * s + h][...], fwd[2 * s + h][...]
+                rows[s + 1, :, take, first_cols] = jnp.where(is_end, mine, other)
+                rows[s + 1, :, take, 2 * k :] = jnp.where(is_end, other, mine)
+            for take, parts in zip(halves(p), refs[4:]):
                 rows[s + 1, :, take, rest_cols] = parts[s][:, :, :k]
         weighted(w_ref, rows, out_ref)
 
     (solved_one,) = call(
         weighted_one_kernel, scalars,
         [weight_one, end_own, end_sib, side, *first_far, *first_fwd, *mixed_far, *mixed_fwd],
-        [sds((2, k, 3 * k), BF16)], scratch=[pltpu.VMEM((n_face, 2, fr, 3 * k), BF16)],
+        [sds((2, k, 3 * k), BF16)], scratch=[pltpu.VMEM((n_face, 2, fr, 3 * k), BF16)], cost=SOLVED_COST,
     )
 
     def join_kernel(sc, own_ref, x_ref, out_ref):

time: 65.9 us -> 65.7 us (level)
  waiting for transfers between devices: 14.8 us -> 12.5 us
  starting transfers between devices: 24.7 us -> 26.7 us
    ppermute x21 -> x23, starting transfers between devices: 18.8 us -> 20.7 us  [box_permute(): return lax.ppermute(array, 'box', [(b, b ^ mask) for b in range(n_box)])]
    ppermute x4 -> x5, waiting for transfers between devices: 4.73 us -> 3.46 us  [face_permute(): return lax.ppermute(array, ('box', 'face'), pairs)]
    ppermute x21 -> x23, waiting for transfers between devices: 10.1 us -> 9 us  [box_permute(): return lax.ppermute(array, 'box', [(b, b ^ mask) for b in range(n_box)])]
    ppermute x4 -> x5, starting transfers between devices: 5.91 us -> 6.06 us  [face_permute(): return lax.ppermute(array, ('box', 'face'), pairs)]
  transfers between devices with their start and end apart: 25 -> 28, of which waited for: 7 -> 8; matrix products, arithmetic and copies ran while one was open for 0% -> 0% of each run, Pallas kernels for 29% -> 29%
where the time goes in v12:
time: 65.7 us; the launch traced here: 65.4 us
  starting transfers between devices  26.7 us (41%)
  Pallas kernels  23.3 us (35%)
  waiting for transfers between devices  12.5 us (19%)
  local copies, waits for them, and re-layouts  2.45 us (4%)
    pallas_call x15, Pallas kernels, call(): pl.pallas_call(kernel, in_specs=[pl.BlockSpec(memory_space=pltpu.SMEM)] +...  23.3 us
    ppermute x23, starting transfers between devices, box_permute(): return lax.ppermute(array, 'box', [(b, b ^ mask) for b in range(n_box)])  20.7 us
    ppermute x23, waiting for transfers between devices, box_permute(): return lax.ppermute(array, 'box', [(b, b ^ mask) for b in range(n_box)])  9 us
    ppermute x5, starting transfers between devices, face_permute(): return lax.ppermute(array, ('box', 'face'), pairs)  6.06 us
    ppermute x5, waiting for transfers between devices, face_permute(): return lax.ppermute(array, ('box', 'face'), pairs)  3.46 us
    unnamed x12, local copies, waits for them, and re-layouts  2.36 us
  transfers between devices with their start and end apart: 28, of which 8 were waited for; matrix products, arithmetic and copies ran while one was open for 0% of the time, Pallas kernels for 29%

profile of v12, /device:TPU:1, one launch (start us, length us, event | category | flops | bytes accessed | tf_op | source)
XLA Modules:
  0.0 65.4 jit_solution(13741105470893782710)
XLA Ops:
  0.1 2.3 %copy-done = bf16[2,1,1,3,256,1536]{5,4,3,2,1,0:T(8,128)(2,1)S(1)} copy-done((bf16[2,1,1,3,256,1536]{5,4,3,2,1,0:T(8,128)(2,1)S(1)}, bf16[2,1,1,3,256,1536]{5,4,3,2,1,0:T(8,128)(2,1)}, u32[]{:S(2)}) %copy-start) | copy-done | bytes 4718616
  2.4 0.7 %shard_map.55 = (bf16[2,256,512]{2,1,0:T(8,128)(2,1)S(1)}, bf16[2,256,512]{2,1,0:T(8,128)(2,1)S(1)}, bf16[2,128,512]{2,1,0:T(8,128)(2,1)S(1)}, bf16[2,128,512]{2...) custom-call(s32[6]{0:T(128)S(1)} %stack.27.sc, ...), custom_call_target="tpu_custom_call" | custom-call | tf_op jit(solution)/shard_map/pallas_call | solution.py:48
  3.2 0.1 collective-permute-start
  3.3 0.8 %shard_map.56 = (s32[1,512]{1,0:T(1,128)S(1)}, s32[512,1]{1,0:T(8,128)S(1)}) custom-call(s32[6]{0:T(128)S(1)} %stack.27.sc, s32[8,512]{1,0:T(8,128)S(1)} %bitcast.18, s32[4,512]{1,0:T(4,128)S(1)} %bitcast.19), custom_call_target="tpu_custom_call" | custom-call | tf_op jit(solution)/shard_map/pallas_call | solution.py:48
  4.1 0.5 collective-permute-start.1
  4.7 0.4 collective-permute-start.3
  5.2 0.6 collective-permute-done.1.refs_6_
  5.8 0.4 collective-permute-start.4
  6.2 0.1 collective-permute-start.5
  6.3 1.3 %shard_map.57 = (bf16[2,256,512]{2,1,0:T(8,128)(2,1)S(1)}, bf16[2,128,512]{2,1,0:T(8,128)(2,1)S(1)}, bf16[2,128,512]{2,1,0:T(8,128)(2,1)S(1)}) custom-call(s32[6]{0:T(128)S(1)} %stack.27.sc, bf16[2,256,512]{2,1,0:T(8,128)(2,1)S(1)} %get-tuple-element.49.own_ref, bf16[2,256,512]{2,1,0:T(8,128)(2,1)S(1)} %collective-permute-done.sib_ref, ...), custom_call_target="tpu_custom_call" | custom-call | tf_op jit(solution)/shard_map/pallas_call | solution.py:48
  7.6 0.4 collective-permute-start.6
  8.0 0.1 collective-permute-start.11
  8.2 2.6 %collective-permute-start.12 = (bf16[2,128,512]{2,1,0:T(8,128)(2,1)S(1)}, bf16[2,128,512]{2,1,0:T(8,128)(2,1)S(1)}, u32[]{:S(2)}, u32[]{:S(2)}) collective-permute-start(bf16[2,128,512]{2,1,0:T(8,128)(2,1)S(1)} %get-tuple-element.76), channel_id=1, source_target_pairs={{0,1},{1,0},{2,3},{3,2},{4,5},{5,4},{6,7},{7,6},{8,9},{9,8},{10,11... | collective-permute-start | bytes 786440 | tf_op jit(solution)/shard_map/ppermute | solution.py:85
  10.8 1.2 %collective-permute-start.14 = (bf16[2,128,512]{2,1,0:T(8,128)(2,1)S(1)}, bf16[2,128,512]{2,1,0:T(8,128)(2,1)S(1)}, u32[]{:S(2)}, u32[]{:S(2)}) collective-permute-start(bf16[2,128,512]{2,1,0:T(8,128)(2,1)S(1)} %bitcast.15), channel_id=1, source_target_pairs={{0,4},{2,6},{4,0},{6,2},{8,12},{10,14},{12,8},{14,10},{16,20},{18,... | collective-permute-start | bytes 786440 | tf_op jit(solution)/shard_map/ppermute | solution.py:78
  12.0 0.2 collective-permute-start.13
  12.2 1.1 %shard_map.58 = (bf16[2,128,1024]{2,1,0:T(8,128)(2,1)S(1)}, bf16[2,128,512]{2,1,0:T(8,128)(2,1)S(1)}, bf16[2,128,512]{2,1,0:T(8,128)(2,1)S(1)}, bf16[2,256,1536]{2,1,0:T(8,128)(2,1)S(1)}) custom-call(s32[6]{0:T(128)S(1)} %stack.27.sc, bf16[2,3,256,1536]{3,2,1,0:T(8,128)(2,1)S(1)} %bitcast.12, s32[1,512]{1,0:T(1,128)S(1)} %get-tuple-element.50.comp_ref.refs_12_), custom_call_target="tpu_custom_call" | custom-call | tf_op jit(solution)/shard_map/pallas_call | solution.py:48
  13.4 1.1 %collective-permute-start.9 = (bf16[2,128,512]{2,1,0:T(8,128)(2,1)S(1)}, bf16[2,128,512]{2,1,0:T(8,128)(2,1)S(1)}, u32[]{:S(2)}, u32[]{:S(2)}) collective-permute-start(bf16[2,128,512]{2,1,0:T(8,128)(2,1)S(1)} %get-tuple-element.71), channel_id=1, source_target_pairs={{0,2},{2,0},{4,6},{6,4},{8,10},{10,8},{12,14},{14,12},{16,18},{18,... | collective-permute-start | bytes 786440 | tf_op jit(solution)/shard_map/ppermute | solution.py:78
  14.4 2.9 %collective-permute-done.12.rest_0_ = bf16[2,128,512]{2,1,0:T(8,128)(2,1)S(1)} collective-permute-done((bf16[2,128,512]{2,1,0:T(8,128)(2,1)S(1)}, bf16[2,128,512]{2,1,0:T(8,128)(2,1)S(1)}, u32[]{:S(2)}, u32[]{:S(2)}) %collective-permute-start.12) | collective-permute-done | bytes 262176 | tf_op jit(solution)/shard_map/ppermute | solution.py:85
  17.3 1.0 %collective-permute-start.10 = (bf16[2,128,512]{2,1,0:T(8,128)(2,1)S(1)}, bf16[2,128,512]{2,1,0:T(8,128)(2,1)S(1)}, u32[]{:S(2)}, u32[]{:S(2)}) collective-permute-start(bf16[2,128,512]{2,1,0:T(8,128)(2,1)S(1)} %get-tuple-element.72), channel_id=1, source_target_pairs={{0,2},{2,0},{4,6},{6,4},{8,10},{10,8},{12,14},{14,12},{16,18},{18,... | collective-permute-start | bytes 786440 | tf_op jit(solution)/shard_map/ppermute | solution.py:78
  18.4 2.9 %shard_map.59 = (bf16[2,256,1536]{2,1,0:T(8,128)(2,1)S(1)}, bf16[2,128,1024]{2,1,0:T(8,128)(2,1)S(1)}, bf16[2,128,1024]{2,1,0:T(8,128)(2,1)S(1)}) custom-call(s32[6]{0:T(128)S(1)} %stack.27.sc, bf16[2,128,512]{2,1,0:T(8,128)(2,1)S(1)} %get-tuple-element.61.refs_0_, bf16[2,128,512]{2,1,0:T(8,128)(2,1)S(1)} %get-tuple-element.62.refs_1_, ...), custom_call_target="tpu_custom_call" | custom-call | tf_op jit(solution)/shard_map/pallas_call | solution.py:48
  21.2 1.8 %collective-permute-start.8 = (bf16[2,128,1024]{2,1,0:T(8,128)(2,1)S(1)}, bf16[2,128,1024]{2,1,0:T(8,128)(2,1)S(1)}, u32[]{:S(2)}, u32[]{:S(2)}) collective-permute-start(bf16[2,128,1024]{2,1,0:T(8,128)(2,1)S(1)} %get-tuple-element.69), channel_id=1, source_target_pairs={{0,1},{1,0},{2,3},{3,2},{4,5},{5,4},{6,7},{7,6},{8,9},{9,8},{10,11... | collective-permute-start | bytes 1572872 | tf_op jit(solution)/shard_map/ppermute | solution.py:85
  23.0 0.6 collective-permute-start.15
  23.7 0.6 shard_map.60.w_ref
  24.3 1.4 %shard_map.61 = (f32[2,128,1024]{2,1,0:T(8,128)S(1)}, bf16[2,128,512]{2,1,0:T(8,128)(2,1)S(1)}) custom-call(s32[6]{0:T(128)S(1)} %stack.27.sc, bf16[2,128,1024]{2,1,0:T(8,128)(2,1)S(1)} %get-tuple-element.70.keep_ref, bf16[2,128,512]{2,1,0:T(8,128)(2,1)S(1)} %collective-permute-done.9.couple_ref, bf16[2,128,512]{2,1,0:T(8,128)(2,1)S(1)} %collective-permute-done.10.slots_ref, ...), custom_call_target="tpu_custom_call" | custom-call | flops 700000000 | tf_op jit(solution)/shard_map/pallas_call | solution.py:48
  25.7 1.1 %shard_map.62 = (bf16[2,128,512]{2,1,0:T(8,128)(2,1)S(1)}, bf16[2,128,256]{2,1,0:T(8,128)(2,1)S(1)}, bf16[2,128,256]{2,1,0:T(8,128)(2,1)S(1)}) custom-call(s32[6]{0:T(128)S(1)} %stack.27.sc, f32[2,128,1024]{2,1,0:T(8,128)S(1)} %get-tuple-element.74.acc_ref, bf16[2,128,512]{2,1,0:T(8,128)(2,1)S(1)} %get-tuple-element.75.hid_ref, ...), custom_call_target="tpu_custom_call" | custom-call | tf_op jit(solution)/shard_map/pallas_call | solution.py:48
  26.9 1.5 %collective-permute-start.17 = (bf16[2,128,256]{2,1,0:T(8,128)(2,1)S(1)}, bf16[2,128,256]{2,1,0:T(8,128)(2,1)S(1)}, u32[]{:S(2)}, u32[]{:S(2)}) collective-permute-start(bf16[2,128,256]{2,1,0:T(8,128)(2,1)S(1)} %get-tuple-element.83), channel_id=1, source_target_pairs={{0,4},{2,6},{4,0},{6,2},{8,12},{10,14},{12,8},{14,10},{16,20},{18,... | collective-permute-start | bytes 393224 | tf_op jit(solution)/shard_map/ppermute | solution.py:78
  28.4 3.1 %collective-permute-done.17.x_ref = bf16[2,128,256]{2,1,0:T(8,128)(2,1)S(1)} collective-permute-done((bf16[2,128,256]{2,1,0:T(8,128)(2,1)S(1)}, bf16[2,128,256]{2,1,0:T(8,128)(2,1)S(1)}, u32[]{:S(2)}, u32[]{:S(2)}) %collective-permute-start.17) | collective-permute-done | bytes 131104 | tf_op jit(solution)/shard_map/ppermute | solution.py:78
  31.5 0.6 shard_map.63.own_ref
  32.1 1.5 %collective-permute-start.23 = (bf16[2,128,768]{2,1,0:T(8,128)(2,1)S(1)}, bf16[2,128,768]{2,1,0:T(8,128)(2,1)S(1)}, u32[]{:S(2)}, u32[]{:S(2)}) collective-permute-start(bf16[2,128,768]{2,1,0:T(8,128)(2,1)S(1)} %shard_map.63.own_ref), channel_id=1, source_target_pairs={{0,4},{2,6},{4,0},{6,2},{8,12},{10,14},{12,8},{14,10},{16,20},{18,... | collective-permute-start | bytes 1179656 | tf_op jit(solution)/shard_map/ppermute | solution.py:78
  33.6 1.2 %collective-permute-start.24 = (bf16[2,128,768]{2,1,0:T(8,128)(2,1)S(1)}, bf16[2,128,768]{2,1,0:T(8,128)(2,1)S(1)}, u32[]{:S(2)}, u32[]{:S(2)}) collective-permute-start(bf16[2,128,768]{2,1,0:T(8,128)(2,1)S(1)} %shard_map.63.own_ref), channel_id=1, source_target_pairs={{0,1},{1,0},{2,3},{3,2},{4,5},{5,4},{6,7},{7,6},{8,9},{9,8},{10,11... | collective-permute-start | bytes 1179656 | tf_op jit(solution)/shard_map/ppermute | solution.py:85
  34.8 1.9 %collective-permute-start.18 = (bf16[2,128,1024]{2,1,0:T(8,128)(2,1)S(1)}, bf16[2,128,1024]{2,1,0:T(8,128)(2,1)S(1)}, u32[]{:S(2)}, u32[]{:S(2)}) collective-permute-start(bf16[2,128,1024]{2,1,0:T(8,128)(2,1)S(1)} %collective-permute-done.8.rest_4_.refs_0_), channel_id=1, source_target_pairs={{0,2},{2,0},{4,6},{6,4},{8,10},{10,8},{12,14},{14,12},{16,18},{18,... | collective-permute-start | bytes 1572872 | tf_op jit(solution)/shard_map/ppermute | solution.py:78
  36.7 0.5 collective-permute-start.22
  37.3 1.4 %collective-permute-done.21.refs_2_ = bf16[2,128,512]{2,1,0:T(8,128)(2,1)S(1)} collective-permute-done((bf16[2,128,512]{2,1,0:T(8,128)(2,1)S(1)}, bf16[2,128,512]{2,1,0:T(8,128)(2,1)S(1)}, u32[]{:S(2)}, u32[]{:S(2)}) %collective-permute-start.21) | collective-permute-done | bytes 262176 | tf_op jit(solution)/shard_map/ppermute | solution.py:78
  38.7 0.2 collective-permute-start.19
  38.9 0.1 collective-permute-done.22.refs_3_
  39.0 0.7 %shard_map.65.refs_6_ = bf16[2,512,512]{2,1,0:T(8,128)(2,1)S(1)} custom-call(s32[6]{0:T(128)S(1)} %stack.27.sc, bf16[2,128,512]{2,1,0:T(8,128)(2,1)S(1)} %bitcast.17, bf16[2,128,512]{2,1,0:T(8,128)(2,1)S(1)} %collective-permute-done.14.refs_1_, bf16[2,128,512]{2,1,0:T(8,128)(2,1)S(1)} %collective-permute-done.21.refs_2_, ...), custom_call_target="tpu_custom_call" | custom-call | tf_op jit(solution)/shard_map/pallas_call | solution.py:48
  39.7 1.7 %collective-permute-done.23.x_ref = bf16[2,128,768]{2,1,0:T(8,128)(2,1)S(1)} collective-permute-done((bf16[2,128,768]{2,1,0:T(8,128)(2,1)S(1)}, bf16[2,128,768]{2,1,0:T(8,128)(2,1)S(1)}, u32[]{:S(2)}, u32[]{:S(2)}) %collective-permute-start.23) | collective-permute-done | bytes 393248 | tf_op jit(solution)/shard_map/ppermute | solution.py:78
  41.4 0.6 shard_map.67.refs_0_
  42.0 0.6 collective-permute-done.24.own_ref
  42.5 1.0 %collective-permute-start.25 = (bf16[2,128,768]{2,1,0:T(8,128)(2,1)S(1)}, bf16[2,128,768]{2,1,0:T(8,128)(2,1)S(1)}, u32[]{:S(2)}, u32[]{:S(2)}) collective-permute-start(bf16[2,128,768]{2,1,0:T(8,128)(2,1)S(1)} %collective-permute-done.24.own_ref), channel_id=1, source_target_pairs={{0,4},{2,6},{4,0},{6,2},{8,12},{10,14},{12,8},{14,10},{16,20},{18,... | collective-permute-start | bytes 1179656 | tf_op jit(solution)/shard_map/ppermute | solution.py:78
  43.5 4.1 %collective-permute-start.26 = (bf16[2,128,1536]{2,1,0:T(8,128)(2,1)S(1)}, bf16[2,128,1536]{2,1,0:T(8,128)(2,1)S(1)}, u32[]{:S(2)}, u32[]{:S(2)}) collective-permute-start(bf16[2,128,1536]{2,1,0:T(8,128)(2,1)S(1)} %shard_map.67.refs_0_), channel_id=1, source_target_pairs={{0,2},{2,0},{4,6},{6,4},{8,10},{10,8},{12,14},{14,12},{16,18},{18,... | collective-permute-start | bytes 2359304 | tf_op jit(solution)/shard_map/ppermute | solution.py:78
  47.6 4.2 %shard_map.64.refs_5_ = bf16[2,512,1536]{2,1,0:T(8,128)(2,1)S(1)} custom-call(s32[6]{0:T(128)S(1)} %stack.27.sc, bf16[2,512,512]{2,1,0:T(8,128)(2,1)S(1)} %shard_map.60.w_ref, bf16[2,256,512]{2,1,0:T(8,128)(2,1)S(1)} %get-tuple-element.51.end_ref.refs_14_.own_ref, bf16[2,256,512]{2,1,0:T(8,128)(2,1)S(1)} %collective-permute-done.7.refs_15_.endsib_ref.sib_ref, ...), custom_call_target="tpu_custom_call" | custom-call | flops 2200000000 | tf_op jit(solution)/shard_map/pallas_call | solution.py:48
  51.8 0.6 shard_map.68.refs_1_
  52.4 3.3 %collective-permute-start.27 = (bf16[2,128,1536]{2,1,0:T(8,128)(2,1)S(1)}, bf16[2,128,1536]{2,1,0:T(8,128)(2,1)S(1)}, u32[]{:S(2)}, u32[]{:S(2)}) collective-permute-start(bf16[2,128,1536]{2,1,0:T(8,128)(2,1)S(1)} %shard_map.68.refs_1_), channel_id=1, source_target_pairs={{0,2},{2,0},{4,6},{6,4},{8,10},{10,8},{12,14},{14,12},{16,18},{18,... | collective-permute-start | bytes 2359304 | tf_op jit(solution)/shard_map/ppermute | solution.py:78
  55.7 0.6 collective-permute-start.20
  56.3 2.0 %collective-permute-done.20.refs_3_ = bf16[2,128,1024]{2,1,0:T(8,128)(2,1)S(1)} collective-permute-done((bf16[2,128,1024]{2,1,0:T(8,128)(2,1)S(1)}, bf16[2,128,1024]{2,1,0:T(8,128)(2,1)S(1)}, u32[]{:S(2)}, u32[]{:S(2)}) %collective-permute-start.20) | collective-permute-done | bytes 524320 | tf_op jit(solution)/shard_map/ppermute | solution.py:78
  58.4 3.4 %shard_map.66 = (bf16[2,512,512]{2,1,0:T(8,128)(2,1)S(1)}, bf16[512,512]{1,0:T(8,128)(2,1)S(1)}, bf16[512,512]{1,0:T(8,128)(2,1)S(1)}) custom-call(s32[6]{0:T(128)S(1)} %stack.27.sc, bf16[2,256,1536]{2,1,0:T(8,128)(2,1)S(1)} %get-tuple-element.54.end_ref, bf16[2,256,1536]{2,1,0:T(8,128)(2,1)S(1)} %get-tuple-element.68.kept_ref, ...), custom_call_target="tpu_custom_call" | custom-call | flops 2000000000 | tf_op jit(solution)/shard_map/pallas_call | solution.py:48
  61.8 3.4 %shard_map.69 = bf16[2,1,256,1536]{3,2,1,0:T(8,128)(2,1)} custom-call(s32[6]{0:T(128)S(1)} %stack.27.sc, bf16[2,512,512]{2,1,0:T(8,128)(2,1)S(1)} %get-tuple-element.87.hid_ref, bf16[512,512]{1,0:T(8,128)(2,1)S(1)} %get-tuple-element.88.first_ref, bf16[512,512]{1,0:T(8,128)(2,1)S(1)} %get-tuple-element.89.slots_ref, ...), custom_call_target="tpu_custom_call" | custom-call | tf_op jit(solution)/shard_map/pallas_call | solution.py:48
  (36 shorter events, 0.3 us)
Async XLA Ops:
  0.0 3.3 %copy-start.4 = (s32[1,8,512]{2,1,0:T(8,128)S(1)}, s32[1,8,512]{2,1,0:T(8,128)}, u32[]{:S(2)}) copy-start(s32[1,8,512]{2,1,0:T(8,128)} %param.8) | copy-start | bytes 49156
  0.0 3.3 %copy-start.5 = (s32[1,4,512]{2,1,0:T(4,128)S(1)}, s32[1,4,512]{2,1,0:T(4,128)}, u32[]{:S(2)}) copy-start(s32[1,4,512]{2,1,0:T(4,128)} %param.9) | copy-start | bytes 24580
  0.1 2.3 %copy-start = (bf16[2,1,1,3,256,1536]{5,4,3,2,1,0:T(8,128)(2,1)S(1)}, bf16[2,1,1,3,256,1536]{5,4,3,2,1,0:T(8,128)(2,1)}, u32[]{:S(2)}) copy-start(bf16[2,1,1,3,256,1536]{5,4,3,2,1,0:T(8,128)(2,1)} %param.5) | copy-start | bytes 14155780
  2.4 9.8 %copy-start.1 = (bf16[2,1,1,3,256,1536]{5,4,3,2,1,0:T(8,128)(2,1)S(1)}, bf16[2,1,1,3,256,1536]{5,4,3,2,1,0:T(8,128)(2,1)}, u32[]{:S(2)}) copy-start(bf16[2,1,1,3,256,1536]{5,4,3,2,1,0:T(8,128)(2,1)} %param.5) | copy-start | bytes 14155780
  3.1 4.9 %copy-start.2 = (bf16[2,1,256,512]{3,2,1,0:T(8,128)(2,1)S(1)}, bf16[2,1,256,512]{3,2,1,0:T(8,128)(2,1)}, u32[]{:S(2)}) copy-start(bf16[2,1,256,512]{3,2,1,0:T(8,128)(2,1)} %param.6) | copy-start | bytes 1572868
  3.2 7.6 %copy-start.3 = (bf16[2,1,128,512]{3,2,1,0:T(8,128)(2,1)S(1)}, bf16[2,1,128,512]{3,2,1,0:T(8,128)(2,1)}, u32[]{:S(2)}) copy-start(bf16[2,1,128,512]{3,2,1,0:T(8,128)(2,1)} %param.7) | copy-start | bytes 786436
  3.2 3.0 %collective-permute-start = (bf16[2,256,512]{2,1,0:T(8,128)(2,1)S(1)}, bf16[2,256,512]{2,1,0:T(8,128)(2,1)S(1)}, u32[]{:S(2)}, u32[]{:S(2)}) collective-permute-start(bf16[2,256,512]{2,1,0:T(8,128)(2,1)S(1)} %get-tuple-element.49.own_ref), channel_id=1, source_target_pairs={{0,2},{2,0},{4,6},{6,4},{8,10},{10,8},{12,14},{14,12},{16,18},{18,... | collective-permute-start | bytes 1572872 | tf_op jit(solution)/shard_map/ppermute | solution.py:78
  4.1 1.7 %collective-permute-start.1 = (bf16[2,128,512]{2,1,0:T(8,128)(2,1)S(1)}, bf16[2,128,512]{2,1,0:T(8,128)(2,1)S(1)}, u32[]{:S(2)}, u32[]{:S(2)}) collective-permute-start(bf16[2,128,512]{2,1,0:T(8,128)(2,1)S(1)} %get-tuple-element.61.refs_0_), channel_id=1, source_target_pairs={{0,2},{2,0},{4,6},{6,4},{8,10},{10,8},{12,14},{14,12},{16,18},{18,... | collective-permute-start | bytes 786440 | tf_op jit(solution)/shard_map/ppermute | solution.py:78
  4.6 2.9 %collective-permute-start.2 = (bf16[2,128,512]{2,1,0:T(8,128)(2,1)S(1)}, bf16[2,128,512]{2,1,0:T(8,128)(2,1)S(1)}, u32[]{:S(2)}, u32[]{:S(2)}) collective-permute-start(bf16[2,128,512]{2,1,0:T(8,128)(2,1)S(1)} %get-tuple-element.62.refs_1_), channel_id=1, source_target_pairs={{0,2},{2,0},{4,6},{6,4},{8,10},{10,8},{12,14},{14,12},{16,18},{18,... | collective-permute-start | bytes 786440 | tf_op jit(solution)/shard_map/ppermute | solution.py:78
  4.7 3.3 %collective-permute-start.3 = (bf16[2,128,512]{2,1,0:T(8,128)(2,1)S(1)}, bf16[2,128,512]{2,1,0:T(8,128)(2,1)S(1)}, u32[]{:S(2)}, u32[]{:S(2)}) collective-permute-start(bf16[2,128,512]{2,1,0:T(8,128)(2,1)S(1)} %get-tuple-element.63.refs_2_), channel_id=1, source_target_pairs={{0,2},{2,0},{4,6},{6,4},{8,10},{10,8},{12,14},{14,12},{16,18},{18,... | collective-permute-start | bytes 786440 | tf_op jit(solution)/shard_map/ppermute | solution.py:78
  5.1 8.2 %collective-permute-start.7 = (bf16[2,256,512]{2,1,0:T(8,128)(2,1)S(1)}, bf16[2,256,512]{2,1,0:T(8,128)(2,1)S(1)}, u32[]{:S(2)}, u32[]{:S(2)}) collective-permute-start(bf16[2,256,512]{2,1,0:T(8,128)(2,1)S(1)} %get-tuple-element.51.end_ref.refs_14_.own_ref), channel_id=1, source_target_pairs={{0,2},{2,0},{4,6},{6,4},{8,10},{10,8},{12,14},{14,12},{16,18},{18,... | collective-permute-start | bytes 1572872 | tf_op jit(solution)/shard_map/ppermute | solution.py:78
  5.8 2.4 %collective-permute-start.4 = (bf16[2,128,512]{2,1,0:T(8,128)(2,1)S(1)}, bf16[2,128,512]{2,1,0:T(8,128)(2,1)S(1)}, u32[]{:S(2)}, u32[]{:S(2)}) collective-permute-start(bf16[2,128,512]{2,1,0:T(8,128)(2,1)S(1)} %get-tuple-element.64.refs_3_), channel_id=1, source_target_pairs={{0,2},{2,0},{4,6},{6,4},{8,10},{10,8},{12,14},{14,12},{16,18},{18,... | collective-permute-start | bytes 786440 | tf_op jit(solution)/shard_map/ppermute | solution.py:78
  6.2 4.6 %collective-permute-start.5 = (bf16[2,128,512]{2,1,0:T(8,128)(2,1)S(1)}, bf16[2,128,512]{2,1,0:T(8,128)(2,1)S(1)}, u32[]{:S(2)}, u32[]{:S(2)}) collective-permute-start(bf16[2,128,512]{2,1,0:T(8,128)(2,1)S(1)} %get-tuple-element.65.refs_4_), channel_id=1, source_target_pairs={{0,2},{2,0},{4,6},{6,4},{8,10},{10,8},{12,14},{14,12},{16,18},{18,... | collective-permute-start | bytes 786440 | tf_op jit(solution)/shard_map/ppermute | solution.py:78
  7.6 4.4 %collective-permute-start.6 = (bf16[2,128,512]{2,1,0:T(8,128)(2,1)S(1)}, bf16[2,128,512]{2,1,0:T(8,128)(2,1)S(1)}, u32[]{:S(2)}, u32[]{:S(2)}) collective-permute-start(bf16[2,128,512]{2,1,0:T(8,128)(2,1)S(1)} %get-tuple-element.66.refs_5_), channel_id=1, source_target_pairs={{0,2},{2,0},{4,6},{6,4},{8,10},{10,8},{12,14},{14,12},{16,18},{18,... | collective-permute-start | bytes 786440 | tf_op jit(solution)/shard_map/ppermute | solution.py:78
  8.0 15.6 %collective-permute-start.11 = (bf16[2,256,512]{2,1,0:T(8,128)(2,1)S(1)}, bf16[2,256,512]{2,1,0:T(8,128)(2,1)S(1)}, u32[]{:S(2)}, u32[]{:S(2)}) collective-permute-start(bf16[2,256,512]{2,1,0:T(8,128)(2,1)S(1)} %bitcast.13), channel_id=1, source_target_pairs={{0,2},{2,0},{4,6},{6,4},{8,10},{10,8},{12,14},{14,12},{16,18},{18,... | collective-permute-start | bytes 1572872 | tf_op jit(solution)/shard_map/ppermute | solution.py:78
  8.2 9.1 %collective-permute-start.12 = (bf16[2,128,512]{2,1,0:T(8,128)(2,1)S(1)}, bf16[2,128,512]{2,1,0:T(8,128)(2,1)S(1)}, u32[]{:S(2)}, u32[]{:S(2)}) collective-permute-start(bf16[2,128,512]{2,1,0:T(8,128)(2,1)S(1)} %get-tuple-element.76), channel_id=1, source_target_pairs={{0,1},{1,0},{2,3},{3,2},{4,5},{5,4},{6,7},{7,6},{8,9},{9,8},{10,11... | collective-permute-start | bytes 786440 | tf_op jit(solution)/shard_map/ppermute | solution.py:85
  10.8 10.4 %collective-permute-start.14 = (bf16[2,128,512]{2,1,0:T(8,128)(2,1)S(1)}, bf16[2,128,512]{2,1,0:T(8,128)(2,1)S(1)}, u32[]{:S(2)}, u32[]{:S(2)}) collective-permute-start(bf16[2,128,512]{2,1,0:T(8,128)(2,1)S(1)} %bitcast.15), channel_id=1, source_target_pairs={{0,4},{2,6},{4,0},{6,2},{8,12},{10,14},{12,8},{14,10},{16,20},{18,... | collective-permute-start | bytes 786440 | tf_op jit(solution)/shard_map/ppermute | solution.py:78
  12.0 11.0 %collective-permute-start.13 = (bf16[2,128,512]{2,1,0:T(8,128)(2,1)S(1)}, bf16[2,128,512]{2,1,0:T(8,128)(2,1)S(1)}, u32[]{:S(2)}, u32[]{:S(2)}) collective-permute-start(bf16[2,128,512]{2,1,0:T(8,128)(2,1)S(1)} %get-tuple-element.77), channel_id=1, source_target_pairs={{0,1},{1,0},{2,3},{3,2},{4,5},{5,4},{6,7},{7,6},{8,9},{9,8},{10,11... | collective-permute-start | bytes 786440 | tf_op jit(solution)/shard_map/ppermute | solution.py:85
  13.4 10.9 %collective-permute-start.9 = (bf16[2,128,512]{2,1,0:T(8,128)(2,1)S(1)}, bf16[2,128,512]{2,1,0:T(8,128)(2,1)S(1)}, u32[]{:S(2)}, u32[]{:S(2)}) collective-permute-start(bf16[2,128,512]{2,1,0:T(8,128)(2,1)S(1)} %get-tuple-element.71), channel_id=1, source_target_pairs={{0,2},{2,0},{4,6},{6,4},{8,10},{10,8},{12,14},{14,12},{16,18},{18,... | collective-permute-start | bytes 786440 | tf_op jit(solution)/shard_map/ppermute | solution.py:78
  17.3 7.0 %collective-permute-start.10 = (bf16[2,128,512]{2,1,0:T(8,128)(2,1)S(1)}, bf16[2,128,512]{2,1,0:T(8,128)(2,1)S(1)}, u32[]{:S(2)}, u32[]{:S(2)}) collective-permute-start(bf16[2,128,512]{2,1,0:T(8,128)(2,1)S(1)} %get-tuple-element.72), channel_id=1, source_target_pairs={{0,2},{2,0},{4,6},{6,4},{8,10},{10,8},{12,14},{14,12},{16,18},{18,... | collective-permute-start | bytes 786440 | tf_op jit(solution)/shard_map/ppermute | solution.py:78
  21.2 13.6 %collective-permute-start.8 = (bf16[2,128,1024]{2,1,0:T(8,128)(2,1)S(1)}, bf16[2,128,1024]{2,1,0:T(8,128)(2,1)S(1)}, u32[]{:S(2)}, u32[]{:S(2)}) collective-permute-start(bf16[2,128,1024]{2,1,0:T(8,128)(2,1)S(1)} %get-tuple-element.69), channel_id=1, source_target_pairs={{0,1},{1,0},{2,3},{3,2},{4,5},{5,4},{6,7},{7,6},{8,9},{9,8},{10,11... | collective-permute-start | bytes 1572872 | tf_op jit(solution)/shard_map/ppermute | solution.py:85
  23.0 2.7 %collective-permute-start.15 = (bf16[2,128,512]{2,1,0:T(8,128)(2,1)S(1)}, bf16[2,128,512]{2,1,0:T(8,128)(2,1)S(1)}, u32[]{:S(2)}, u32[]{:S(2)}) collective-permute-start(bf16[2,128,512]{2,1,0:T(8,128)(2,1)S(1)} %collective-permute-done.12.rest_0_), channel_id=1, source_target_pairs={{0,2},{2,0},{4,6},{6,4},{8,10},{10,8},{12,14},{14,12},{16,18},{18,... | collective-permute-start | bytes 786440 | tf_op jit(solution)/shard_map/ppermute | solution.py:78
  23.7 2.1 %collective-permute-start.16 = (bf16[2,128,512]{2,1,0:T(8,128)(2,1)S(1)}, bf16[2,128,512]{2,1,0:T(8,128)(2,1)S(1)}, u32[]{:S(2)}, u32[]{:S(2)}) collective-permute-start(bf16[2,128,512]{2,1,0:T(8,128)(2,1)S(1)} %collective-permute-done.13.rest_1_), channel_id=1, source_target_pairs={{0,2},{2,0},{4,6},{6,4},{8,10},{10,8},{12,14},{14,12},{16,18},{18,... | collective-permute-start | bytes 786440 | tf_op jit(solution)/shard_map/ppermute | solution.py:78
  26.9 4.6 %collective-permute-start.17 = (bf16[2,128,256]{2,1,0:T(8,128)(2,1)S(1)}, bf16[2,128,256]{2,1,0:T(8,128)(2,1)S(1)}, u32[]{:S(2)}, u32[]{:S(2)}) collective-permute-start(bf16[2,128,256]{2,1,0:T(8,128)(2,1)S(1)} %get-tuple-element.83), channel_id=1, source_target_pairs={{0,4},{2,6},{4,0},{6,2},{8,12},{10,14},{12,8},{14,10},{16,20},{18,... | collective-permute-start | bytes 393224 | tf_op jit(solution)/shard_map/ppermute | solution.py:78
  32.1 9.3 %collective-permute-start.23 = (bf16[2,128,768]{2,1,0:T(8,128)(2,1)S(1)}, bf16[2,128,768]{2,1,0:T(8,128)(2,1)S(1)}, u32[]{:S(2)}, u32[]{:S(2)}) collective-permute-start(bf16[2,128,768]{2,1,0:T(8,128)(2,1)S(1)} %shard_map.63.own_ref), channel_id=1, source_target_pairs={{0,4},{2,6},{4,0},{6,2},{8,12},{10,14},{12,8},{14,10},{16,20},{18,... | collective-permute-start | bytes 1179656 | tf_op jit(solution)/shard_map/ppermute | solution.py:78
  33.6 9.0 %collective-permute-start.24 = (bf16[2,128,768]{2,1,0:T(8,128)(2,1)S(1)}, bf16[2,128,768]{2,1,0:T(8,128)(2,1)S(1)}, u32[]{:S(2)}, u32[]{:S(2)}) collective-permute-start(bf16[2,128,768]{2,1,0:T(8,128)(2,1)S(1)} %shard_map.63.own_ref), channel_id=1, source_target_pairs={{0,1},{1,0},{2,3},{3,2},{4,5},{5,4},{6,7},{7,6},{8,9},{9,8},{10,11... | collective-permute-start | bytes 1179656 | tf_op jit(solution)/shard_map/ppermute | solution.py:85
  34.8 12.8 %collective-permute-start.18 = (bf16[2,128,1024]{2,1,0:T(8,128)(2,1)S(1)}, bf16[2,128,1024]{2,1,0:T(8,128)(2,1)S(1)}, u32[]{:S(2)}, u32[]{:S(2)}) collective-permute-start(bf16[2,128,1024]{2,1,0:T(8,128)(2,1)S(1)} %collective-permute-done.8.rest_4_.refs_0_), channel_id=1, source_target_pairs={{0,2},{2,0},{4,6},{6,4},{8,10},{10,8},{12,14},{14,12},{16,18},{18,... | collective-permute-start | bytes 1572872 | tf_op jit(solution)/shard_map/ppermute | solution.py:78
  36.7 1.9 %collective-permute-start.21 = (bf16[2,128,512]{2,1,0:T(8,128)(2,1)S(1)}, bf16[2,128,512]{2,1,0:T(8,128)(2,1)S(1)}, u32[]{:S(2)}, u32[]{:S(2)}) collective-permute-start(bf16[2,128,512]{2,1,0:T(8,128)(2,1)S(1)} %bitcast.16), channel_id=1, source_target_pairs={{0,2},{2,0},{4,6},{6,4},{8,10},{10,8},{12,14},{14,12},{16,18},{18,... | collective-permute-start | bytes 786440 | tf_op jit(solution)/shard_map/ppermute | solution.py:78
  36.7 2.3 %collective-permute-start.22 = (bf16[2,128,512]{2,1,0:T(8,128)(2,1)S(1)}, bf16[2,128,512]{2,1,0:T(8,128)(2,1)S(1)}, u32[]{:S(2)}, u32[]{:S(2)}) collective-permute-start(bf16[2,128,512]{2,1,0:T(8,128)(2,1)S(1)} %collective-permute-done.14.refs_1_), channel_id=1, source_target_pairs={{0,2},{2,0},{4,6},{6,4},{8,10},{10,8},{12,14},{14,12},{16,18},{18,... | collective-permute-start | bytes 786440 | tf_op jit(solution)/shard_map/ppermute | solution.py:78
  38.7 17.1 %collective-permute-start.19 = (bf16[2,128,1024]{2,1,0:T(8,128)(2,1)S(1)}, bf16[2,128,1024]{2,1,0:T(8,128)(2,1)S(1)}, u32[]{:S(2)}, u32[]{:S(2)}) collective-permute-start(bf16[2,128,1024]{2,1,0:T(8,128)(2,1)S(1)} %get-tuple-element.86), channel_id=1, source_target_pairs={{0,1},{1,0},{2,3},{3,2},{4,5},{5,4},{6,7},{7,6},{8,9},{9,8},{10,11... | collective-permute-start | bytes 1572872 | tf_op jit(solution)/shard_map/ppermute | solution.py:85
  42.5 9.3 %collective-permute-start.25 = (bf16[2,128,768]{2,1,0:T(8,128)(2,1)S(1)}, bf16[2,128,768]{2,1,0:T(8,128)(2,1)S(1)}, u32[]{:S(2)}, u32[]{:S(2)}) collective-permute-start(bf16[2,128,768]{2,1,0:T(8,128)(2,1)S(1)} %collective-permute-done.24.own_ref), channel_id=1, source_target_pairs={{0,4},{2,6},{4,0},{6,2},{8,12},{10,14},{12,8},{14,10},{16,20},{18,... | collective-permute-start | bytes 1179656 | tf_op jit(solution)/shard_map/ppermute | solution.py:78
  43.5 18.3 %collective-permute-start.26 = (bf16[2,128,1536]{2,1,0:T(8,128)(2,1)S(1)}, bf16[2,128,1536]{2,1,0:T(8,128)(2,1)S(1)}, u32[]{:S(2)}, u32[]{:S(2)}) collective-permute-start(bf16[2,128,1536]{2,1,0:T(8,128)(2,1)S(1)} %shard_map.67.refs_0_), channel_id=1, source_target_pairs={{0,2},{2,0},{4,6},{6,4},{8,10},{10,8},{12,14},{14,12},{16,18},{18,... | collective-permute-start | bytes 2359304 | tf_op jit(solution)/shard_map/ppermute | solution.py:78
  52.4 9.4 %collective-permute-start.27 = (bf16[2,128,1536]{2,1,0:T(8,128)(2,1)S(1)}, bf16[2,128,1536]{2,1,0:T(8,128)(2,1)S(1)}, u32[]{:S(2)}, u32[]{:S(2)}) collective-permute-start(bf16[2,128,1536]{2,1,0:T(8,128)(2,1)S(1)} %shard_map.68.refs_1_), channel_id=1, source_target_pairs={{0,2},{2,0},{4,6},{6,4},{8,10},{10,8},{12,14},{14,12},{16,18},{18,... | collective-permute-start | bytes 2359304 | tf_op jit(solution)/shard_map/ppermute | solution.py:78
  55.7 2.7 %collective-permute-start.20 = (bf16[2,128,1024]{2,1,0:T(8,128)(2,1)S(1)}, bf16[2,128,1024]{2,1,0:T(8,128)(2,1)S(1)}, u32[]{:S(2)}, u32[]{:S(2)}) collective-permute-start(bf16[2,128,1024]{2,1,0:T(8,128)(2,1)S(1)} %collective-permute-done.19.refs_2_), channel_id=1, source_target_pairs={{0,2},{2,0},{4,6},{6,4},{8,10},{10,8},{12,14},{14,12},{16,18},{18,... | collective-permute-start | bytes 1572872 | tf_op jit(solution)/shard_map/ppermute | solution.py:78

commit v13 on v12

--- a/solution.py
+++ b/solution.py
@@ -114,14 +114,14 @@
         end_out[...] = leaf_ref[:, 1 - p, :, pl.ds(pl.multiple_of(p * k, k), k)]
         side_out[...] = leaf_ref[:, 1 - p, :, 2 * k :]
         for i, rows_out in enumerate(rows_outs):
-            rows_out[...] = leaf_ref[:, 2, i % 2 * hr : (i % 2 + 1) * hr, i // 2 * k : (i // 2 + 1) * k]
+            rows_out[...] = leaf_ref[:, 2, :, i * k : (i + 1) * k]
 
     end_own, sides_raw, *s_rows = call(
-        parts_kernel, scalars, [leaf], [sds((2, fr, k), BF16)] * 2 + [sds((2, hr, k), BF16)] * 6
+        parts_kernel, scalars, [leaf], [sds((2, fr, k), BF16)] * 5
     )
     sides_sib = box_permute(sides_raw, 1)
     end_sib = box_permute(end_own, 1)
-    s_sib = [box_permute(after(a, comp), 1) for a in s_rows]
+    s_sib = [box_permute(a, 1) for a in s_rows]
 
     def side_kernel(sc, own_ref, sib_ref, comp_ref, end_ref, side_out, *send_outs):
         p, q = sc[0], sc[1]
@@ -186,7 +186,7 @@
     )
 
     def rows_kernel(sc, *refs):
-        owns, sibs, refs = refs[:6], refs[6:12], refs[12:]
+        owns, sibs, refs = refs[:3], refs[3:6], refs[6:]
         comp_ref, col_ref, end_ref, endsib_ref, kept_out, *outs = refs
         p, q, f = sc[0], sc[1], sc[2]
         mine, _ = halves(p)
@@ -201,9 +201,7 @@
             take_sib = row_picker(slots, (1 - p) * k + f * fr, fr)
             for t in range(2):
                 for c in range(3):
-                    own, sib = [
-                        jnp.concatenate([a[2 * c][t], a[2 * c + 1][t]], axis=0) for a in (owns, sibs)
-                    ]
+                    own, sib = owns[c][t], sibs[c][t]
                     if c == 2:
                         own, sib = [dot(a, b).astype(BF16) for a, b in ((own, pick_own), (sib, pick_sib))]
                     write(t, c, (dot(take_own, own) + dot(take_sib, sib)).astype(BF16))

time: 65.7 us -> 64.2 us (0.977)
  starting transfers between devices: 26.7 us -> 25.9 us
  waiting for transfers between devices: 12.5 us -> 11.8 us
    ppermute x5, waiting for transfers between devices: 3.46 us -> 2.5 us  [face_permute(): return lax.ppermute(array, ('box', 'face'), pairs)]
    ppermute x23 -> x20, starting transfers between devices: 20.7 us -> 19.9 us  [box_permute(): return lax.ppermute(array, 'box', [(b, b ^ mask) for b in range(n_box)])]
    ppermute x23 -> x20, waiting for transfers between devices: 9 us -> 9.32 us  [box_permute(): return lax.ppermute(array, 'box', [(b, b ^ mask) for b in range(n_box)])]
  transfers between devices with their start and end apart: 28 -> 25, of which waited for: 8 -> 7; matrix products, arithmetic and copies ran while one was open for 0% -> 0% of each run, Pallas kernels for 29% -> 30%
where the time goes in v13:
time: 64.2 us; the launch traced here: 63.9 us
  starting transfers between devices  25.9 us (40%)
  Pallas kernels  23.4 us (36%)
  waiting for transfers between devices  11.8 us (18%)
  local copies, waits for them, and re-layouts  2.45 us (4%)
    pallas_call x15, Pallas kernels, call(): pl.pallas_call(kernel, in_specs=[pl.BlockSpec(memory_space=pltpu.SMEM)] +...  23.4 us
    ppermute x20, starting transfers between devices, box_permute(): return lax.ppermute(array, 'box', [(b, b ^ mask) for b in range(n_box)])  19.9 us
    ppermute x20, waiting for transfers between devices, box_permute(): return lax.ppermute(array, 'box', [(b, b ^ mask) for b in range(n_box)])  9.32 us
    ppermute x5, starting transfers between devices, face_permute(): return lax.ppermute(array, ('box', 'face'), pairs)  5.92 us
    ppermute x5, waiting for transfers between devices, face_permute(): return lax.ppermute(array, ('box', 'face'), pairs)  2.5 us
    unnamed x12, local copies, waits for them, and re-layouts  2.36 us
  transfers between devices with their start and end apart: 25, of which 7 were waited for; matrix products, arithmetic and copies ran while one was open for 0% of the time, Pallas kernels for 30%

profile of v13, /device:TPU:1, one launch (start us, length us, event | category | flops | bytes accessed | tf_op | source)
XLA Modules:
  0.0 63.9 jit_solution(4035239082640389633)
XLA Ops:
  0.0 0.1 stack.27.sc
  0.1 2.3 %copy-done = bf16[2,1,1,3,256,1536]{5,4,3,2,1,0:T(8,128)(2,1)S(1)} copy-done((bf16[2,1,1,3,256,1536]{5,4,3,2,1,0:T(8,128)(2,1)S(1)}, bf16[2,1,1,3,256,1536]{5,4,3,2,1,0:T(8,128)(2,1)}, u32[]{:S(2)}) %copy-start) | copy-done | bytes 4718616
  2.4 0.7 %shard_map.55 = (bf16[2,256,512]{2,1,0:T(8,128)(2,1)S(1)}, bf16[2,256,512]{2,1,0:T(8,128)(2,1)S(1)}, bf16[2,256,512]{2,1,0:T(8,128)(2,1)S(1)}, bf16[2,256,512]{2,1,0:T(8,128)(2,1)S(1)}, bf16[2,256,512]{2,1,0:T(8,128)(2,1)S(1)}) custom-call(s32[6]{0:T(128)S(1)} %stack.27.sc, bf16[2,3,256,1536]{3,2,1,0:T(8,128)(2,1)S(1)} %bitcast.11), custom_call_target="tpu_custom_call" | custom-call | tf_op jit(solution)/shard_map/pallas_call | solution.py:48
  3.2 0.1 collective-permute-start
  3.3 0.5 collective-permute-start.1
  3.7 0.1 collective-permute-start.2
  3.8 0.4 collective-permute-start.3
  4.3 0.1 collective-permute-start.4
  4.3 0.8 %shard_map.56 = (s32[1,512]{1,0:T(1,128)S(1)}, s32[512,1]{1,0:T(8,128)S(1)}) custom-call(s32[6]{0:T(128)S(1)} %stack.27.sc, s32[8,512]{1,0:T(8,128)S(1)} %bitcast.18, s32[4,512]{1,0:T(4,128)S(1)} %bitcast.19), custom_call_target="tpu_custom_call" | custom-call | tf_op jit(solution)/shard_map/pallas_call | solution.py:48
  5.2 1.3 %shard_map.57 = (bf16[2,256,512]{2,1,0:T(8,128)(2,1)S(1)}, bf16[2,128,512]{2,1,0:T(8,128)(2,1)S(1)}, bf16[2,128,512]{2,1,0:T(8,128)(2,1)S(1)}) custom-call(s32[6]{0:T(128)S(1)} %stack.27.sc, bf16[2,256,512]{2,1,0:T(8,128)(2,1)S(1)} %get-tuple-element.40.own_ref, bf16[2,256,512]{2,1,0:T(8,128)(2,1)S(1)} %collective-permute-done.sib_ref, ...), custom_call_target="tpu_custom_call" | custom-call | tf_op jit(solution)/shard_map/pallas_call | solution.py:48
  6.4 0.5 collective-permute-start.8
  6.9 2.3 %collective-permute-start.9 = (bf16[2,128,512]{2,1,0:T(8,128)(2,1)S(1)}, bf16[2,128,512]{2,1,0:T(8,128)(2,1)S(1)}, u32[]{:S(2)}, u32[]{:S(2)}) collective-permute-start(bf16[2,128,512]{2,1,0:T(8,128)(2,1)S(1)} %get-tuple-element.58), channel_id=1, source_target_pairs={{0,1},{1,0},{2,3},{3,2},{4,5},{5,4},{6,7},{7,6},{8,9},{9,8},{10,11... | collective-permute-start | bytes 786440 | tf_op jit(solution)/shard_map/ppermute | solution.py:85
  9.3 1.2 %collective-permute-start.11 = (bf16[2,128,512]{2,1,0:T(8,128)(2,1)S(1)}, bf16[2,128,512]{2,1,0:T(8,128)(2,1)S(1)}, u32[]{:S(2)}, u32[]{:S(2)}) collective-permute-start(bf16[2,128,512]{2,1,0:T(8,128)(2,1)S(1)} %bitcast.15), channel_id=1, source_target_pairs={{0,4},{2,6},{4,0},{6,2},{8,12},{10,14},{12,8},{14,10},{16,20},{18,... | collective-permute-start | bytes 786440 | tf_op jit(solution)/shard_map/ppermute | solution.py:78
  10.5 0.2 collective-permute-start.10
  10.7 1.1 %shard_map.58 = (bf16[2,128,1024]{2,1,0:T(8,128)(2,1)S(1)}, bf16[2,128,512]{2,1,0:T(8,128)(2,1)S(1)}, bf16[2,128,512]{2,1,0:T(8,128)(2,1)S(1)}, bf16[2,256,1536]{2,1,0:T(8,128)(2,1)S(1)}) custom-call(s32[6]{0:T(128)S(1)} %stack.27.sc, bf16[2,3,256,1536]{3,2,1,0:T(8,128)(2,1)S(1)} %bitcast.12, s32[1,512]{1,0:T(1,128)S(1)} %get-tuple-element.41.comp_ref.refs_6_), custom_call_target="tpu_custom_call" | custom-call | tf_op jit(solution)/shard_map/pallas_call | solution.py:48
  11.8 1.3 %collective-permute-start.6 = (bf16[2,128,512]{2,1,0:T(8,128)(2,1)S(1)}, bf16[2,128,512]{2,1,0:T(8,128)(2,1)S(1)}, u32[]{:S(2)}, u32[]{:S(2)}) collective-permute-start(bf16[2,128,512]{2,1,0:T(8,128)(2,1)S(1)} %get-tuple-element.53), channel_id=1, source_target_pairs={{0,2},{2,0},{4,6},{6,4},{8,10},{10,8},{12,14},{14,12},{16,18},{18,... | collective-permute-start | bytes 786440 | tf_op jit(solution)/shard_map/ppermute | solution.py:78
  13.2 2.4 %collective-permute-done.9.rest_0_ = bf16[2,128,512]{2,1,0:T(8,128)(2,1)S(1)} collective-permute-done((bf16[2,128,512]{2,1,0:T(8,128)(2,1)S(1)}, bf16[2,128,512]{2,1,0:T(8,128)(2,1)S(1)}, u32[]{:S(2)}, u32[]{:S(2)}) %collective-permute-start.9) | collective-permute-done | bytes 262176 | tf_op jit(solution)/shard_map/ppermute | solution.py:85
  15.6 1.5 %collective-permute-start.7 = (bf16[2,128,512]{2,1,0:T(8,128)(2,1)S(1)}, bf16[2,128,512]{2,1,0:T(8,128)(2,1)S(1)}, u32[]{:S(2)}, u32[]{:S(2)}) collective-permute-start(bf16[2,128,512]{2,1,0:T(8,128)(2,1)S(1)} %get-tuple-element.54), channel_id=1, source_target_pairs={{0,2},{2,0},{4,6},{6,4},{8,10},{10,8},{12,14},{14,12},{16,18},{18,... | collective-permute-start | bytes 786440 | tf_op jit(solution)/shard_map/ppermute | solution.py:78
  17.1 2.9 %shard_map.59 = (bf16[2,256,1536]{2,1,0:T(8,128)(2,1)S(1)}, bf16[2,128,1024]{2,1,0:T(8,128)(2,1)S(1)}, bf16[2,128,1024]{2,1,0:T(8,128)(2,1)S(1)}) custom-call(s32[6]{0:T(128)S(1)} %stack.27.sc, bf16[2,256,512]{2,1,0:T(8,128)(2,1)S(1)} %get-tuple-element.46.refs_0_, bf16[2,256,512]{2,1,0:T(8,128)(2,1)S(1)} %get-tuple-element.47.refs_1_, ...), custom_call_target="tpu_custom_call" | custom-call | tf_op jit(solution)/shard_map/pallas_call | solution.py:48
  19.9 1.9 %collective-permute-start.5 = (bf16[2,128,1024]{2,1,0:T(8,128)(2,1)S(1)}, bf16[2,128,1024]{2,1,0:T(8,128)(2,1)S(1)}, u32[]{:S(2)}, u32[]{:S(2)}) collective-permute-start(bf16[2,128,1024]{2,1,0:T(8,128)(2,1)S(1)} %get-tuple-element.51), channel_id=1, source_target_pairs={{0,1},{1,0},{2,3},{3,2},{4,5},{5,4},{6,7},{7,6},{8,9},{9,8},{10,11... | collective-permute-start | bytes 1572872 | tf_op jit(solution)/shard_map/ppermute | solution.py:85
  21.8 0.3 collective-permute-start.12
  22.1 0.2 collective-permute-start.13
  22.3 0.6 shard_map.60.w_ref
  23.0 1.4 %shard_map.61 = (f32[2,128,1024]{2,1,0:T(8,128)S(1)}, bf16[2,128,512]{2,1,0:T(8,128)(2,1)S(1)}) custom-call(s32[6]{0:T(128)S(1)} %stack.27.sc, bf16[2,128,1024]{2,1,0:T(8,128)(2,1)S(1)} %get-tuple-element.52.keep_ref, bf16[2,128,512]{2,1,0:T(8,128)(2,1)S(1)} %collective-permute-done.6.couple_ref, bf16[2,128,512]{2,1,0:T(8,128)(2,1)S(1)} %collective-permute-done.7.slots_ref, ...), custom_call_target="tpu_custom_call" | custom-call | flops 700000000 | tf_op jit(solution)/shard_map/pallas_call | solution.py:48
  24.4 1.2 %shard_map.62 = (bf16[2,128,512]{2,1,0:T(8,128)(2,1)S(1)}, bf16[2,128,256]{2,1,0:T(8,128)(2,1)S(1)}, bf16[2,128,256]{2,1,0:T(8,128)(2,1)S(1)}) custom-call(s32[6]{0:T(128)S(1)} %stack.27.sc, f32[2,128,1024]{2,1,0:T(8,128)S(1)} %get-tuple-element.56.acc_ref, bf16[2,128,512]{2,1,0:T(8,128)(2,1)S(1)} %get-tuple-element.57.hid_ref, ...), custom_call_target="tpu_custom_call" | custom-call | tf_op jit(solution)/shard_map/pallas_call | solution.py:48
  25.5 1.3 %collective-permute-start.14 = (bf16[2,128,256]{2,1,0:T(8,128)(2,1)S(1)}, bf16[2,128,256]{2,1,0:T(8,128)(2,1)S(1)}, u32[]{:S(2)}, u32[]{:S(2)}) collective-permute-start(bf16[2,128,256]{2,1,0:T(8,128)(2,1)S(1)} %get-tuple-element.65), channel_id=1, source_target_pairs={{0,4},{2,6},{4,0},{6,2},{8,12},{10,14},{12,8},{14,10},{16,20},{18,... | collective-permute-start | bytes 393224 | tf_op jit(solution)/shard_map/ppermute | solution.py:78
  26.9 3.5 %collective-permute-done.14.x_ref = bf16[2,128,256]{2,1,0:T(8,128)(2,1)S(1)} collective-permute-done((bf16[2,128,256]{2,1,0:T(8,128)(2,1)S(1)}, bf16[2,128,256]{2,1,0:T(8,128)(2,1)S(1)}, u32[]{:S(2)}, u32[]{:S(2)}) %collective-permute-start.14) | collective-permute-done | bytes 131104 | tf_op jit(solution)/shard_map/ppermute | solution.py:78
  30.4 0.6 shard_map.63.own_ref
  30.9 1.1 %collective-permute-start.20 = (bf16[2,128,768]{2,1,0:T(8,128)(2,1)S(1)}, bf16[2,128,768]{2,1,0:T(8,128)(2,1)S(1)}, u32[]{:S(2)}, u32[]{:S(2)}) collective-permute-start(bf16[2,128,768]{2,1,0:T(8,128)(2,1)S(1)} %shard_map.63.own_ref), channel_id=1, source_target_pairs={{0,4},{2,6},{4,0},{6,2},{8,12},{10,14},{12,8},{14,10},{16,20},{18,... | collective-permute-start | bytes 1179656 | tf_op jit(solution)/shard_map/ppermute | solution.py:78
  32.1 1.2 %collective-permute-start.21 = (bf16[2,128,768]{2,1,0:T(8,128)(2,1)S(1)}, bf16[2,128,768]{2,1,0:T(8,128)(2,1)S(1)}, u32[]{:S(2)}, u32[]{:S(2)}) collective-permute-start(bf16[2,128,768]{2,1,0:T(8,128)(2,1)S(1)} %shard_map.63.own_ref), channel_id=1, source_target_pairs={{0,1},{1,0},{2,3},{3,2},{4,5},{5,4},{6,7},{7,6},{8,9},{9,8},{10,11... | collective-permute-start | bytes 1179656 | tf_op jit(solution)/shard_map/ppermute | solution.py:85
  33.3 0.1 collective-permute-done.5.rest_4_.refs_0_
  33.4 1.8 %collective-permute-start.15 = (bf16[2,128,1024]{2,1,0:T(8,128)(2,1)S(1)}, bf16[2,128,1024]{2,1,0:T(8,128)(2,1)S(1)}, u32[]{:S(2)}, u32[]{:S(2)}) collective-permute-start(bf16[2,128,1024]{2,1,0:T(8,128)(2,1)S(1)} %collective-permute-done.5.rest_4_.refs_0_), channel_id=1, source_target_pairs={{0,2},{2,0},{4,6},{6,4},{8,10},{10,8},{12,14},{14,12},{16,18},{18,... | collective-permute-start | bytes 1572872 | tf_op jit(solution)/shard_map/ppermute | solution.py:78
  35.2 0.5 collective-permute-start.19
  35.7 1.4 %collective-permute-done.18.refs_2_ = bf16[2,128,512]{2,1,0:T(8,128)(2,1)S(1)} collective-permute-done((bf16[2,128,512]{2,1,0:T(8,128)(2,1)S(1)}, bf16[2,128,512]{2,1,0:T(8,128)(2,1)S(1)}, u32[]{:S(2)}, u32[]{:S(2)}) %collective-permute-start.18) | collective-permute-done | bytes 262176 | tf_op jit(solution)/shard_map/ppermute | solution.py:78
  37.1 0.3 collective-permute-start.16
  37.4 0.1 collective-permute-done.19.refs_3_
  37.5 0.7 %shard_map.65.refs_6_ = bf16[2,512,512]{2,1,0:T(8,128)(2,1)S(1)} custom-call(s32[6]{0:T(128)S(1)} %stack.27.sc, bf16[2,128,512]{2,1,0:T(8,128)(2,1)S(1)} %bitcast.17, bf16[2,128,512]{2,1,0:T(8,128)(2,1)S(1)} %collective-permute-done.11.refs_1_, bf16[2,128,512]{2,1,0:T(8,128)(2,1)S(1)} %collective-permute-done.18.refs_2_, ...), custom_call_target="tpu_custom_call" | custom-call | tf_op jit(solution)/shard_map/pallas_call | solution.py:48
  38.2 2.3 %collective-permute-done.20.x_ref = bf16[2,128,768]{2,1,0:T(8,128)(2,1)S(1)} collective-permute-done((bf16[2,128,768]{2,1,0:T(8,128)(2,1)S(1)}, bf16[2,128,768]{2,1,0:T(8,128)(2,1)S(1)}, u32[]{:S(2)}, u32[]{:S(2)}) %collective-permute-start.20) | collective-permute-done | bytes 393248 | tf_op jit(solution)/shard_map/ppermute | solution.py:78
  40.5 0.6 shard_map.67.refs_0_
  41.1 0.9 %collective-permute-start.22 = (bf16[2,128,768]{2,1,0:T(8,128)(2,1)S(1)}, bf16[2,128,768]{2,1,0:T(8,128)(2,1)S(1)}, u32[]{:S(2)}, u32[]{:S(2)}) collective-permute-start(bf16[2,128,768]{2,1,0:T(8,128)(2,1)S(1)} %collective-permute-done.21.own_ref), channel_id=1, source_target_pairs={{0,4},{2,6},{4,0},{6,2},{8,12},{10,14},{12,8},{14,10},{16,20},{18,... | collective-permute-start | bytes 1179656 | tf_op jit(solution)/shard_map/ppermute | solution.py:78
  42.0 4.2 %collective-permute-start.23 = (bf16[2,128,1536]{2,1,0:T(8,128)(2,1)S(1)}, bf16[2,128,1536]{2,1,0:T(8,128)(2,1)S(1)}, u32[]{:S(2)}, u32[]{:S(2)}) collective-permute-start(bf16[2,128,1536]{2,1,0:T(8,128)(2,1)S(1)} %shard_map.67.refs_0_), channel_id=1, source_target_pairs={{0,2},{2,0},{4,6},{6,4},{8,10},{10,8},{12,14},{14,12},{16,18},{18,... | collective-permute-start | bytes 2359304 | tf_op jit(solution)/shard_map/ppermute | solution.py:78
  46.2 4.2 %shard_map.64.refs_5_ = bf16[2,512,1536]{2,1,0:T(8,128)(2,1)S(1)} custom-call(s32[6]{0:T(128)S(1)} %stack.27.sc, bf16[2,512,512]{2,1,0:T(8,128)(2,1)S(1)} %shard_map.60.w_ref, bf16[2,256,512]{2,1,0:T(8,128)(2,1)S(1)} %get-tuple-element.42.end_ref.refs_8_.own_ref, bf16[2,256,512]{2,1,0:T(8,128)(2,1)S(1)} %collective-permute-done.4.refs_9_.endsib_ref.sib_ref, ...), custom_call_target="tpu_custom_call" | custom-call | flops 2200000000 | tf_op jit(solution)/shard_map/pallas_call | solution.py:48
  50.5 0.6 shard_map.68.refs_1_
  51.1 3.1 %collective-permute-start.24 = (bf16[2,128,1536]{2,1,0:T(8,128)(2,1)S(1)}, bf16[2,128,1536]{2,1,0:T(8,128)(2,1)S(1)}, u32[]{:S(2)}, u32[]{:S(2)}) collective-permute-start(bf16[2,128,1536]{2,1,0:T(8,128)(2,1)S(1)} %shard_map.68.refs_1_), channel_id=1, source_target_pairs={{0,2},{2,0},{4,6},{6,4},{8,10},{10,8},{12,14},{14,12},{16,18},{18,... | collective-permute-start | bytes 2359304 | tf_op jit(solution)/shard_map/ppermute | solution.py:78
  54.2 0.6 collective-permute-start.17
  54.8 2.0 %collective-permute-done.17.refs_3_ = bf16[2,128,1024]{2,1,0:T(8,128)(2,1)S(1)} collective-permute-done((bf16[2,128,1024]{2,1,0:T(8,128)(2,1)S(1)}, bf16[2,128,1024]{2,1,0:T(8,128)(2,1)S(1)}, u32[]{:S(2)}, u32[]{:S(2)}) %collective-permute-start.17) | collective-permute-done | bytes 524320 | tf_op jit(solution)/shard_map/ppermute | solution.py:78
  56.9 3.4 %shard_map.66 = (bf16[2,512,512]{2,1,0:T(8,128)(2,1)S(1)}, bf16[512,512]{1,0:T(8,128)(2,1)S(1)}, bf16[512,512]{1,0:T(8,128)(2,1)S(1)}) custom-call(s32[6]{0:T(128)S(1)} %stack.27.sc, bf16[2,256,1536]{2,1,0:T(8,128)(2,1)S(1)} %get-tuple-element.45.end_ref, bf16[2,256,1536]{2,1,0:T(8,128)(2,1)S(1)} %get-tuple-element.50.kept_ref, ...), custom_call_target="tpu_custom_call" | custom-call | flops 2000000000 | tf_op jit(solution)/shard_map/pallas_call | solution.py:48
  60.3 3.4 %shard_map.69 = bf16[2,1,256,1536]{3,2,1,0:T(8,128)(2,1)} custom-call(s32[6]{0:T(128)S(1)} %stack.27.sc, bf16[2,512,512]{2,1,0:T(8,128)(2,1)S(1)} %get-tuple-element.69.hid_ref, bf16[512,512]{1,0:T(8,128)(2,1)S(1)} %get-tuple-element.70.first_ref, bf16[512,512]{1,0:T(8,128)(2,1)S(1)} %get-tuple-element.71.slots_ref, ...), custom_call_target="tpu_custom_call" | custom-call | tf_op jit(solution)/shard_map/pallas_call | solution.py:48
  (30 shorter events, 0.1 us)
Async XLA Ops:
  0.0 4.3 %copy-start.4 = (s32[1,8,512]{2,1,0:T(8,128)S(1)}, s32[1,8,512]{2,1,0:T(8,128)}, u32[]{:S(2)}) copy-start(s32[1,8,512]{2,1,0:T(8,128)} %param.8) | copy-start | bytes 49156
  0.1 2.3 %copy-start = (bf16[2,1,1,3,256,1536]{5,4,3,2,1,0:T(8,128)(2,1)S(1)}, bf16[2,1,1,3,256,1536]{5,4,3,2,1,0:T(8,128)(2,1)}, u32[]{:S(2)}) copy-start(bf16[2,1,1,3,256,1536]{5,4,3,2,1,0:T(8,128)(2,1)} %param.5) | copy-start | bytes 14155780
  2.4 1.9 %copy-start.5 = (s32[1,4,512]{2,1,0:T(4,128)S(1)}, s32[1,4,512]{2,1,0:T(4,128)}, u32[]{:S(2)}) copy-start(s32[1,4,512]{2,1,0:T(4,128)} %param.9) | copy-start | bytes 24580
  2.4 8.3 %copy-start.1 = (bf16[2,1,1,3,256,1536]{5,4,3,2,1,0:T(8,128)(2,1)S(1)}, bf16[2,1,1,3,256,1536]{5,4,3,2,1,0:T(8,128)(2,1)}, u32[]{:S(2)}) copy-start(bf16[2,1,1,3,256,1536]{5,4,3,2,1,0:T(8,128)(2,1)} %param.5) | copy-start | bytes 14155780
  3.1 3.3 %copy-start.2 = (bf16[2,1,256,512]{3,2,1,0:T(8,128)(2,1)S(1)}, bf16[2,1,256,512]{3,2,1,0:T(8,128)(2,1)}, u32[]{:S(2)}) copy-start(bf16[2,1,256,512]{3,2,1,0:T(8,128)(2,1)} %param.6) | copy-start | bytes 1572868
  3.2 6.1 %copy-start.3 = (bf16[2,1,128,512]{3,2,1,0:T(8,128)(2,1)S(1)}, bf16[2,1,128,512]{3,2,1,0:T(8,128)(2,1)}, u32[]{:S(2)}) copy-start(bf16[2,1,128,512]{3,2,1,0:T(8,128)(2,1)} %param.7) | copy-start | bytes 786436
  3.2 2.0 %collective-permute-start = (bf16[2,256,512]{2,1,0:T(8,128)(2,1)S(1)}, bf16[2,256,512]{2,1,0:T(8,128)(2,1)S(1)}, u32[]{:S(2)}, u32[]{:S(2)}) collective-permute-start(bf16[2,256,512]{2,1,0:T(8,128)(2,1)S(1)} %get-tuple-element.40.own_ref), channel_id=1, source_target_pairs={{0,2},{2,0},{4,6},{6,4},{8,10},{10,8},{12,14},{14,12},{16,18},{18,... | collective-permute-start | bytes 1572872 | tf_op jit(solution)/shard_map/ppermute | solution.py:78
  3.3 3.6 %collective-permute-start.1 = (bf16[2,256,512]{2,1,0:T(8,128)(2,1)S(1)}, bf16[2,256,512]{2,1,0:T(8,128)(2,1)S(1)}, u32[]{:S(2)}, u32[]{:S(2)}) collective-permute-start(bf16[2,256,512]{2,1,0:T(8,128)(2,1)S(1)} %get-tuple-element.46.refs_0_), channel_id=1, source_target_pairs={{0,2},{2,0},{4,6},{6,4},{8,10},{10,8},{12,14},{14,12},{16,18},{18,... | collective-permute-start | bytes 1572872 | tf_op jit(solution)/shard_map/ppermute | solution.py:78
  3.7 5.5 %collective-permute-start.2 = (bf16[2,256,512]{2,1,0:T(8,128)(2,1)S(1)}, bf16[2,256,512]{2,1,0:T(8,128)(2,1)S(1)}, u32[]{:S(2)}, u32[]{:S(2)}) collective-permute-start(bf16[2,256,512]{2,1,0:T(8,128)(2,1)S(1)} %get-tuple-element.47.refs_1_), channel_id=1, source_target_pairs={{0,2},{2,0},{4,6},{6,4},{8,10},{10,8},{12,14},{14,12},{16,18},{18,... | collective-permute-start | bytes 1572872 | tf_op jit(solution)/shard_map/ppermute | solution.py:78
  3.8 6.7 %collective-permute-start.3 = (bf16[2,256,512]{2,1,0:T(8,128)(2,1)S(1)}, bf16[2,256,512]{2,1,0:T(8,128)(2,1)S(1)}, u32[]{:S(2)}, u32[]{:S(2)}) collective-permute-start(bf16[2,256,512]{2,1,0:T(8,128)(2,1)S(1)} %get-tuple-element.48.refs_2_), channel_id=1, source_target_pairs={{0,2},{2,0},{4,6},{6,4},{8,10},{10,8},{12,14},{14,12},{16,18},{18,... | collective-permute-start | bytes 1572872 | tf_op jit(solution)/shard_map/ppermute | solution.py:78
  4.3 7.6 %collective-permute-start.4 = (bf16[2,256,512]{2,1,0:T(8,128)(2,1)S(1)}, bf16[2,256,512]{2,1,0:T(8,128)(2,1)S(1)}, u32[]{:S(2)}, u32[]{:S(2)}) collective-permute-start(bf16[2,256,512]{2,1,0:T(8,128)(2,1)S(1)} %get-tuple-element.42.end_ref.refs_8_.own_ref), channel_id=1, source_target_pairs={{0,2},{2,0},{4,6},{6,4},{8,10},{10,8},{12,14},{14,12},{16,18},{18,... | collective-permute-start | bytes 1572872 | tf_op jit(solution)/shard_map/ppermute | solution.py:78
  6.4 15.7 %collective-permute-start.8 = (bf16[2,256,512]{2,1,0:T(8,128)(2,1)S(1)}, bf16[2,256,512]{2,1,0:T(8,128)(2,1)S(1)}, u32[]{:S(2)}, u32[]{:S(2)}) collective-permute-start(bf16[2,256,512]{2,1,0:T(8,128)(2,1)S(1)} %bitcast.13), channel_id=1, source_target_pairs={{0,2},{2,0},{4,6},{6,4},{8,10},{10,8},{12,14},{14,12},{16,18},{18,... | collective-permute-start | bytes 1572872 | tf_op jit(solution)/shard_map/ppermute | solution.py:78
  6.9 8.6 %collective-permute-start.9 = (bf16[2,128,512]{2,1,0:T(8,128)(2,1)S(1)}, bf16[2,128,512]{2,1,0:T(8,128)(2,1)S(1)}, u32[]{:S(2)}, u32[]{:S(2)}) collective-permute-start(bf16[2,128,512]{2,1,0:T(8,128)(2,1)S(1)} %get-tuple-element.58), channel_id=1, source_target_pairs={{0,1},{1,0},{2,3},{3,2},{4,5},{5,4},{6,7},{7,6},{8,9},{9,8},{10,11... | collective-permute-start | bytes 786440 | tf_op jit(solution)/shard_map/ppermute | solution.py:85
  9.3 10.7 %collective-permute-start.11 = (bf16[2,128,512]{2,1,0:T(8,128)(2,1)S(1)}, bf16[2,128,512]{2,1,0:T(8,128)(2,1)S(1)}, u32[]{:S(2)}, u32[]{:S(2)}) collective-permute-start(bf16[2,128,512]{2,1,0:T(8,128)(2,1)S(1)} %bitcast.15), channel_id=1, source_target_pairs={{0,4},{2,6},{4,0},{6,2},{8,12},{10,14},{12,8},{14,10},{16,20},{18,... | collective-permute-start | bytes 786440 | tf_op jit(solution)/shard_map/ppermute | solution.py:78
  10.5 11.3 %collective-permute-start.10 = (bf16[2,128,512]{2,1,0:T(8,128)(2,1)S(1)}, bf16[2,128,512]{2,1,0:T(8,128)(2,1)S(1)}, u32[]{:S(2)}, u32[]{:S(2)}) collective-permute-start(bf16[2,128,512]{2,1,0:T(8,128)(2,1)S(1)} %get-tuple-element.59), channel_id=1, source_target_pairs={{0,1},{1,0},{2,3},{3,2},{4,5},{5,4},{6,7},{7,6},{8,9},{9,8},{10,11... | collective-permute-start | bytes 786440 | tf_op jit(solution)/shard_map/ppermute | solution.py:85
  11.8 11.1 %collective-permute-start.6 = (bf16[2,128,512]{2,1,0:T(8,128)(2,1)S(1)}, bf16[2,128,512]{2,1,0:T(8,128)(2,1)S(1)}, u32[]{:S(2)}, u32[]{:S(2)}) collective-permute-start(bf16[2,128,512]{2,1,0:T(8,128)(2,1)S(1)} %get-tuple-element.53), channel_id=1, source_target_pairs={{0,2},{2,0},{4,6},{6,4},{8,10},{10,8},{12,14},{14,12},{16,18},{18,... | collective-permute-start | bytes 786440 | tf_op jit(solution)/shard_map/ppermute | solution.py:78
  15.6 7.4 %collective-permute-start.7 = (bf16[2,128,512]{2,1,0:T(8,128)(2,1)S(1)}, bf16[2,128,512]{2,1,0:T(8,128)(2,1)S(1)}, u32[]{:S(2)}, u32[]{:S(2)}) collective-permute-start(bf16[2,128,512]{2,1,0:T(8,128)(2,1)S(1)} %get-tuple-element.54), channel_id=1, source_target_pairs={{0,2},{2,0},{4,6},{6,4},{8,10},{10,8},{12,14},{14,12},{16,18},{18,... | collective-permute-start | bytes 786440 | tf_op jit(solution)/shard_map/ppermute | solution.py:78
  19.9 13.5 %collective-permute-start.5 = (bf16[2,128,1024]{2,1,0:T(8,128)(2,1)S(1)}, bf16[2,128,1024]{2,1,0:T(8,128)(2,1)S(1)}, u32[]{:S(2)}, u32[]{:S(2)}) collective-permute-start(bf16[2,128,1024]{2,1,0:T(8,128)(2,1)S(1)} %get-tuple-element.51), channel_id=1, source_target_pairs={{0,1},{1,0},{2,3},{3,2},{4,5},{5,4},{6,7},{7,6},{8,9},{9,8},{10,11... | collective-permute-start | bytes 1572872 | tf_op jit(solution)/shard_map/ppermute | solution.py:85
  21.8 2.6 %collective-permute-start.12 = (bf16[2,128,512]{2,1,0:T(8,128)(2,1)S(1)}, bf16[2,128,512]{2,1,0:T(8,128)(2,1)S(1)}, u32[]{:S(2)}, u32[]{:S(2)}) collective-permute-start(bf16[2,128,512]{2,1,0:T(8,128)(2,1)S(1)} %collective-permute-done.9.rest_0_), channel_id=1, source_target_pairs={{0,2},{2,0},{4,6},{6,4},{8,10},{10,8},{12,14},{14,12},{16,18},{18,... | collective-permute-start | bytes 786440 | tf_op jit(solution)/shard_map/ppermute | solution.py:78
  22.1 2.2 %collective-permute-start.13 = (bf16[2,128,512]{2,1,0:T(8,128)(2,1)S(1)}, bf16[2,128,512]{2,1,0:T(8,128)(2,1)S(1)}, u32[]{:S(2)}, u32[]{:S(2)}) collective-permute-start(bf16[2,128,512]{2,1,0:T(8,128)(2,1)S(1)} %collective-permute-done.10.rest_1_), channel_id=1, source_target_pairs={{0,2},{2,0},{4,6},{6,4},{8,10},{10,8},{12,14},{14,12},{16,18},{18,... | collective-permute-start | bytes 786440 | tf_op jit(solution)/shard_map/ppermute | solution.py:78
  25.5 4.8 %collective-permute-start.14 = (bf16[2,128,256]{2,1,0:T(8,128)(2,1)S(1)}, bf16[2,128,256]{2,1,0:T(8,128)(2,1)S(1)}, u32[]{:S(2)}, u32[]{:S(2)}) collective-permute-start(bf16[2,128,256]{2,1,0:T(8,128)(2,1)S(1)} %get-tuple-element.65), channel_id=1, source_target_pairs={{0,4},{2,6},{4,0},{6,2},{8,12},{10,14},{12,8},{14,10},{16,20},{18,... | collective-permute-start | bytes 393224 | tf_op jit(solution)/shard_map/ppermute | solution.py:78
  30.9 9.5 %collective-permute-start.20 = (bf16[2,128,768]{2,1,0:T(8,128)(2,1)S(1)}, bf16[2,128,768]{2,1,0:T(8,128)(2,1)S(1)}, u32[]{:S(2)}, u32[]{:S(2)}) collective-permute-start(bf16[2,128,768]{2,1,0:T(8,128)(2,1)S(1)} %shard_map.63.own_ref), channel_id=1, source_target_pairs={{0,4},{2,6},{4,0},{6,2},{8,12},{10,14},{12,8},{14,10},{16,20},{18,... | collective-permute-start | bytes 1179656 | tf_op jit(solution)/shard_map/ppermute | solution.py:78
  32.1 9.0 %collective-permute-start.21 = (bf16[2,128,768]{2,1,0:T(8,128)(2,1)S(1)}, bf16[2,128,768]{2,1,0:T(8,128)(2,1)S(1)}, u32[]{:S(2)}, u32[]{:S(2)}) collective-permute-start(bf16[2,128,768]{2,1,0:T(8,128)(2,1)S(1)} %shard_map.63.own_ref), channel_id=1, source_target_pairs={{0,1},{1,0},{2,3},{3,2},{4,5},{5,4},{6,7},{7,6},{8,9},{9,8},{10,11... | collective-permute-start | bytes 1179656 | tf_op jit(solution)/shard_map/ppermute | solution.py:85
  33.4 12.9 %collective-permute-start.15 = (bf16[2,128,1024]{2,1,0:T(8,128)(2,1)S(1)}, bf16[2,128,1024]{2,1,0:T(8,128)(2,1)S(1)}, u32[]{:S(2)}, u32[]{:S(2)}) collective-permute-start(bf16[2,128,1024]{2,1,0:T(8,128)(2,1)S(1)} %collective-permute-done.5.rest_4_.refs_0_), channel_id=1, source_target_pairs={{0,2},{2,0},{4,6},{6,4},{8,10},{10,8},{12,14},{14,12},{16,18},{18,... | collective-permute-start | bytes 1572872 | tf_op jit(solution)/shard_map/ppermute | solution.py:78
  35.2 1.9 %collective-permute-start.18 = (bf16[2,128,512]{2,1,0:T(8,128)(2,1)S(1)}, bf16[2,128,512]{2,1,0:T(8,128)(2,1)S(1)}, u32[]{:S(2)}, u32[]{:S(2)}) collective-permute-start(bf16[2,128,512]{2,1,0:T(8,128)(2,1)S(1)} %bitcast.16), channel_id=1, source_target_pairs={{0,2},{2,0},{4,6},{6,4},{8,10},{10,8},{12,14},{14,12},{16,18},{18,... | collective-permute-start | bytes 786440 | tf_op jit(solution)/shard_map/ppermute | solution.py:78
  35.2 2.3 %collective-permute-start.19 = (bf16[2,128,512]{2,1,0:T(8,128)(2,1)S(1)}, bf16[2,128,512]{2,1,0:T(8,128)(2,1)S(1)}, u32[]{:S(2)}, u32[]{:S(2)}) collective-permute-start(bf16[2,128,512]{2,1,0:T(8,128)(2,1)S(1)} %collective-permute-done.11.refs_1_), channel_id=1, source_target_pairs={{0,2},{2,0},{4,6},{6,4},{8,10},{10,8},{12,14},{14,12},{16,18},{18,... | collective-permute-start | bytes 786440 | tf_op jit(solution)/shard_map/ppermute | solution.py:78
  37.1 17.1 %collective-permute-start.16 = (bf16[2,128,1024]{2,1,0:T(8,128)(2,1)S(1)}, bf16[2,128,1024]{2,1,0:T(8,128)(2,1)S(1)}, u32[]{:S(2)}, u32[]{:S(2)}) collective-permute-start(bf16[2,128,1024]{2,1,0:T(8,128)(2,1)S(1)} %get-tuple-element.68), channel_id=1, source_target_pairs={{0,1},{1,0},{2,3},{3,2},{4,5},{5,4},{6,7},{7,6},{8,9},{9,8},{10,11... | collective-permute-start | bytes 1572872 | tf_op jit(solution)/shard_map/ppermute | solution.py:85
  41.1 9.4 %collective-permute-start.22 = (bf16[2,128,768]{2,1,0:T(8,128)(2,1)S(1)}, bf16[2,128,768]{2,1,0:T(8,128)(2,1)S(1)}, u32[]{:S(2)}, u32[]{:S(2)}) collective-permute-start(bf16[2,128,768]{2,1,0:T(8,128)(2,1)S(1)} %collective-permute-done.21.own_ref), channel_id=1, source_target_pairs={{0,4},{2,6},{4,0},{6,2},{8,12},{10,14},{12,8},{14,10},{16,20},{18,... | collective-permute-start | bytes 1179656 | tf_op jit(solution)/shard_map/ppermute | solution.py:78
  42.0 18.3 %collective-permute-start.23 = (bf16[2,128,1536]{2,1,0:T(8,128)(2,1)S(1)}, bf16[2,128,1536]{2,1,0:T(8,128)(2,1)S(1)}, u32[]{:S(2)}, u32[]{:S(2)}) collective-permute-start(bf16[2,128,1536]{2,1,0:T(8,128)(2,1)S(1)} %shard_map.67.refs_0_), channel_id=1, source_target_pairs={{0,2},{2,0},{4,6},{6,4},{8,10},{10,8},{12,14},{14,12},{16,18},{18,... | collective-permute-start | bytes 2359304 | tf_op jit(solution)/shard_map/ppermute | solution.py:78
  51.1 9.2 %collective-permute-start.24 = (bf16[2,128,1536]{2,1,0:T(8,128)(2,1)S(1)}, bf16[2,128,1536]{2,1,0:T(8,128)(2,1)S(1)}, u32[]{:S(2)}, u32[]{:S(2)}) collective-permute-start(bf16[2,128,1536]{2,1,0:T(8,128)(2,1)S(1)} %shard_map.68.refs_1_), channel_id=1, source_target_pairs={{0,2},{2,0},{4,6},{6,4},{8,10},{10,8},{12,14},{14,12},{16,18},{18,... | collective-permute-start | bytes 2359304 | tf_op jit(solution)/shard_map/ppermute | solution.py:78
  54.2 2.7 %collective-permute-start.17 = (bf16[2,128,1024]{2,1,0:T(8,128)(2,1)S(1)}, bf16[2,128,1024]{2,1,0:T(8,128)(2,1)S(1)}, u32[]{:S(2)}, u32[]{:S(2)}) collective-permute-start(bf16[2,128,1024]{2,1,0:T(8,128)(2,1)S(1)} %collective-permute-done.16.refs_2_), channel_id=1, source_target_pairs={{0,2},{2,0},{4,6},{6,4},{8,10},{10,8},{12,14},{14,12},{16,18},{18,... | collective-permute-start | bytes 1572872 | tf_op jit(solution)/shard_map/ppermute | solution.py:78

commit v14 on v13

--- a/solution.py
+++ b/solution.py
@@ -12,9 +12,9 @@
 VMEM_BYTES = 16 * 1024 * 1024
 JOIN_COST = 300000000
 SLOTS_COST = 0
-OWN_COST = 700000000
-SOLVED_COST = 2200000000
-KEEP_COST = 2_000_000_000
+OWN_COST = 700_000_000
+SOLVED_COST = 800_000_000
+KEEP_COST = 300_000_000
 
 
 def dot(first, second):
@@ -353,12 +353,30 @@
     two_shape = [sds((2, hr, 3 * k), BF16)]
     two_rows = call(join_kernel, after(scalars, weight_two), [two_own, two_x], two_shape, cost=JOIN_COST)
     two_xy = [box_permute(after(a, *two_rows), 2) for a in two_y]
+
+    def join_far_kernel(sc, own_ref, x_ref, *refs):
+        join_kernel(sc, own_ref, x_ref, refs[-1])
+        for h in range(2):
+            refs[h][...] = refs[-1][:, :, h * 3 * half : (h + 1) * 3 * half]
+
     for own, other in zip(two_y, two_xy):
-        two_rows += call(join_kernel, after(scalars, solved_one), [own, other], two_shape)
-    two_sib = [box_permute(a, 1) for a in two_rows]
+        two_rows += call(
+            join_far_kernel, after(scalars, solved_one), [own, other], [sds((2, hr, 3 * half), BF16)] * 2,
+            scratch=[pltpu.VMEM((2, hr, 3 * k), BF16)],
+        )
+    two_sib = [box_permute(a, 1) for a in two_rows[:1]]
+
+    def layout_kernel(sc, own_ref, sib_ref, out_ref):
+        for ref, take in zip((own_ref, sib_ref), halves(sc[0])):
+            out_ref[:, take, :] = ref[...]
+
+    (two_first,) = call(
+        layout_kernel, scalars, [two_rows[0], two_sib[0]], [sds((2, fr, 3 * k), BF16)]
+    )
 
     ends_far = [face_permute(after(a, two_own), i + 1) for i, a in enumerate(kept_out[:nf])]
-    ends_fwd = [box_permute(a, 1) for a in ends_far]
+    ends_fwd = [box_permute(after(a, solved_one), 1) for a in ends_far]
+    two_sib += [box_permute(a, 1) for a in two_rows[1:]]
 
     def level_one_kernel(sc, end_ref, kept_ref, *refs):
         parts = [refs[i * nf : (i + 1) * nf] for i in range(4)]
@@ -405,38 +423,41 @@
             hid_out[s] = piece((second[:fr], second[fr:]), s * fr, fr)
 
     hid_two, first_two, slots_two = call(
-        level_one_kernel, scalars,
+        level_one_kernel, after(scalars, two_first),
         [end_kept, kept, *mixed_far, *mixed_fwd, *ends_far, *ends_fwd, skel_col, solved_one, weight_two],
         [sds((n_face, 2 * fr, 2 * fr), BF16), sds((2 * fr, k), BF16), sds((2 * fr, k), BF16)],
         scratch=[pltpu.VMEM((2, fr, 3 * k), BF16)], cost=KEEP_COST,
     )
 
-    def level_two_kernel(sc, hid_ref, first_ref, slots_ref, *refs):
-        out_ref, rows, stage, sems = refs[2 * n_face :]
+    def level_two_kernel(sc, hid_ref, first_ref, slots_ref, near_ref, *refs):
+        out_ref, rows, stage, sems = refs[4 * nf :]
         q = sc[1]
-        left = jnp.concatenate([hid_ref[s] for s in range(n_face)], axis=1)
+        far = jnp.concatenate([hid_ref[s] for s in range(1, n_face)], axis=1)
         for h, take in enumerate(halves(sc[0])):
-            for s in range(n_face):
-                rows[s, :, take, :] = refs[h * n_face + s][...]
+            for i, ref in enumerate(refs[h * 2 * nf : (h + 1) * 2 * nf]):
+                rows[i // 2, :, take, i % 2 * 3 * half : (i % 2 + 1) * 3 * half] = ref[...]
         copies = []
         for c in range(3):
+            cols = slice(c * k, (c + 1) * k)
             first = slots_ref[...]
             if c < 2:
                 first = jnp.where(q == c, first_ref[...], jnp.zeros((2 * fr, k), BF16))
-            right = rows[:, :, :, c * k : (c + 1) * k].reshape(n_face * 2 * fr, k)
-            stage[c] = (first.astype(F32) - dot(left, right)).astype(BF16).reshape(2, fr, k)
-            copies.append(pltpu.make_async_copy(
-                stage.at[c], out_ref.at[:, 0, :, pl.ds(c * k, k)], sems.at[c]
-            ))
-            copies[-1].start()
+            total = first.astype(F32) - dot(hid_ref[0], flat(near_ref[:, :, cols]))
+            total = total - dot(far, rows[:, :, :, cols].reshape(nf * 2 * fr, k))
+            stage[c] = total.astype(BF16).reshape(2, fr, k)
+            for t in range(2):
+                copies.append(pltpu.make_async_copy(
+                    stage.at[c, t], out_ref.at[t, 0, :, pl.ds(c * k, k)], sems.at[c, t]
+                ))
+                copies[-1].start()
         for copy in copies:
             copy.wait()
 
     (out,) = call(
-        level_two_kernel, scalars, [hid_two, first_two, slots_two, *two_rows, *two_sib],
+        level_two_kernel, scalars, [hid_two, first_two, slots_two, two_first, *two_rows[1:], *two_sib[1:]],
         [sds((2, 1, fr, 3 * k), BF16)], out_specs=[in_hbm],
-        scratch=[pltpu.VMEM((n_face, 2, fr, 3 * k), BF16), pltpu.VMEM((3, 2, fr, k), BF16),
-                 pltpu.SemaphoreType.DMA((3,))],
+        scratch=[pltpu.VMEM((nf, 2, fr, 3 * k), BF16), pltpu.VMEM((3, 2, fr, k), BF16),
+                 pltpu.SemaphoreType.DMA((3, 2))],
     )
     return out
 

time: 64.2 us -> 65.5 us (1.020)
  waiting for transfers between devices: 11.8 us -> 16.8 us
  starting transfers between devices: 25.9 us -> 21.6 us
    ppermute x5, waiting for transfers between devices: 2.5 us -> 5.17 us  [face_permute(): return lax.ppermute(array, ('box', 'face'), pairs)]
    ppermute x20 -> x21, starting transfers between devices: 19.9 us -> 17.4 us  [box_permute(): return lax.ppermute(array, 'box', [(b, b ^ mask) for b in range(n_box)])]
    ppermute x20 -> x21, waiting for transfers between devices: 9.32 us -> 11.6 us  [box_permute(): return lax.ppermute(array, 'box', [(b, b ^ mask) for b in range(n_box)])]
    ppermute x5, starting transfers between devices: 5.92 us -> 4.17 us  [face_permute(): return lax.ppermute(array, ('box', 'face'), pairs)]
    pallas_call x15 -> x16, Pallas kernels: 23.4 us -> 23.9 us  [call(): pl.pallas_call(kernel, in_specs=[pl.BlockSpec(memory_space=pltpu.SMEM)] +...]
  transfers between devices with their start and end apart: 25 -> 26, of which waited for: 7 -> 6; matrix products, arithmetic and copies ran while one was open for 0% -> 0% of each run, Pallas kernels for 30% -> 31%
where the time goes in v14:
time: 65.5 us; the launch traced here: 65 us
  Pallas kernels  23.9 us (36%)
  starting transfers between devices  21.6 us (33%)
  waiting for transfers between devices  16.8 us (26%)
  local copies, waits for them, and re-layouts  2.45 us (4%)
    pallas_call x16, Pallas kernels, call(): pl.pallas_call(kernel, in_specs=[pl.BlockSpec(memory_space=pltpu.SMEM)] +...  23.9 us
    ppermute x21, starting transfers between devices, box_permute(): return lax.ppermute(array, 'box', [(b, b ^ mask) for b in range(n_box)])  17.4 us
    ppermute x21, waiting for transfers between devices, box_permute(): return lax.ppermute(array, 'box', [(b, b ^ mask) for b in range(n_box)])  11.6 us
    ppermute x5, waiting for transfers between devices, face_permute(): return lax.ppermute(array, ('box', 'face'), pairs)  5.17 us
    ppermute x5, starting transfers between devices, face_permute(): return lax.ppermute(array, ('box', 'face'), pairs)  4.17 us
    unnamed x12, local copies, waits for them, and re-layouts  2.36 us
  transfers between devices with their start and end apart: 26, of which 6 were waited for; matrix products, arithmetic and copies ran while one was open for 0% of the time, Pallas kernels for 31%

profile of v14, /device:TPU:1, one launch (start us, length us, event | category | flops | bytes accessed | tf_op | source)
XLA Modules:
  0.0 65.0 jit_solution(567393741447363424)
XLA Ops:
  0.0 0.1 stack.27.sc
  0.1 2.3 %copy-done = bf16[2,1,1,3,256,1536]{5,4,3,2,1,0:T(8,128)(2,1)S(1)} copy-done((bf16[2,1,1,3,256,1536]{5,4,3,2,1,0:T(8,128)(2,1)S(1)}, bf16[2,1,1,3,256,1536]{5,4,3,2,1,0:T(8,128)(2,1)}, u32[]{:S(2)}) %copy-start) | copy-done | bytes 4718616
  2.4 0.7 %shard_map.55 = (bf16[2,256,512]{2,1,0:T(8,128)(2,1)S(1)}, bf16[2,256,512]{2,1,0:T(8,128)(2,1)S(1)}, bf16[2,256,512]{2,1,0:T(8,128)(2,1)S(1)}, bf16[2,256,512]{2,1,0:T(8,128)(2,1)S(1)}, bf16[2,256,512]{2,1,0:T(8,128)(2,1)S(1)}) custom-call(s32[6]{0:T(128)S(1)} %stack.27.sc, bf16[2,3,256,1536]{3,2,1,0:T(8,128)(2,1)S(1)} %bitcast.11), custom_call_target="tpu_custom_call" | custom-call | tf_op jit(solution)/shard_map/pallas_call | solution.py:48
  3.2 0.1 collective-permute-start
  3.3 0.5 collective-permute-start.10
  3.7 0.1 collective-permute-start.11
  3.8 0.4 collective-permute-start.12
  4.3 0.1 collective-permute-start.7
  4.3 0.8 %shard_map.56 = (s32[1,512]{1,0:T(1,128)S(1)}, s32[512,1]{1,0:T(8,128)S(1)}) custom-call(s32[6]{0:T(128)S(1)} %stack.27.sc, s32[8,512]{1,0:T(8,128)S(1)} %bitcast.18, s32[4,512]{1,0:T(4,128)S(1)} %bitcast.19), custom_call_target="tpu_custom_call" | custom-call | tf_op jit(solution)/shard_map/pallas_call | solution.py:48
  5.2 1.3 %shard_map.57 = (bf16[2,256,512]{2,1,0:T(8,128)(2,1)S(1)}, bf16[2,128,512]{2,1,0:T(8,128)(2,1)S(1)}, bf16[2,128,512]{2,1,0:T(8,128)(2,1)S(1)}) custom-call(s32[6]{0:T(128)S(1)} %stack.27.sc, bf16[2,256,512]{2,1,0:T(8,128)(2,1)S(1)} %get-tuple-element.44.own_ref, bf16[2,256,512]{2,1,0:T(8,128)(2,1)S(1)} %collective-permute-done.sib_ref, ...), custom_call_target="tpu_custom_call" | custom-call | tf_op jit(solution)/shard_map/pallas_call | solution.py:48
  6.4 0.5 collective-permute-start.6
  6.9 2.3 %collective-permute-start.1 = (bf16[2,128,512]{2,1,0:T(8,128)(2,1)S(1)}, bf16[2,128,512]{2,1,0:T(8,128)(2,1)S(1)}, u32[]{:S(2)}, u32[]{:S(2)}) collective-permute-start(bf16[2,128,512]{2,1,0:T(8,128)(2,1)S(1)} %bitcast.15), channel_id=1, source_target_pairs={{0,4},{2,6},{4,0},{6,2},{8,12},{10,14},{12,8},{14,10},{16,20},{18,... | collective-permute-start | bytes 786440 | tf_op jit(solution)/shard_map/ppermute | solution.py:78
  9.2 1.2 %collective-permute-start.9 = (bf16[2,128,512]{2,1,0:T(8,128)(2,1)S(1)}, bf16[2,128,512]{2,1,0:T(8,128)(2,1)S(1)}, u32[]{:S(2)}, u32[]{:S(2)}) collective-permute-start(bf16[2,128,512]{2,1,0:T(8,128)(2,1)S(1)} %get-tuple-element.58), channel_id=1, source_target_pairs={{0,1},{1,0},{2,3},{3,2},{4,5},{5,4},{6,7},{7,6},{8,9},{9,8},{10,11... | collective-permute-start | bytes 786440 | tf_op jit(solution)/shard_map/ppermute | solution.py:85
  10.5 0.2 collective-permute-start.8
  10.7 1.1 %shard_map.59 = (bf16[2,128,1024]{2,1,0:T(8,128)(2,1)S(1)}, bf16[2,128,512]{2,1,0:T(8,128)(2,1)S(1)}, bf16[2,128,512]{2,1,0:T(8,128)(2,1)S(1)}, bf16[2,256,1536]{2,1,0:T(8,128)(2,1)S(1)}) custom-call(s32[6]{0:T(128)S(1)} %stack.27.sc, bf16[2,3,256,1536]{3,2,1,0:T(8,128)(2,1)S(1)} %bitcast.12, s32[1,512]{1,0:T(1,128)S(1)} %get-tuple-element.45.comp_ref.refs_6_), custom_call_target="tpu_custom_call" | custom-call | tf_op jit(solution)/shard_map/pallas_call | solution.py:48
  11.8 1.3 %collective-permute-start.4 = (bf16[2,128,512]{2,1,0:T(8,128)(2,1)S(1)}, bf16[2,128,512]{2,1,0:T(8,128)(2,1)S(1)}, u32[]{:S(2)}, u32[]{:S(2)}) collective-permute-start(bf16[2,128,512]{2,1,0:T(8,128)(2,1)S(1)} %get-tuple-element.52), channel_id=1, source_target_pairs={{0,2},{2,0},{4,6},{6,4},{8,10},{10,8},{12,14},{14,12},{16,18},{18,... | collective-permute-start | bytes 786440 | tf_op jit(solution)/shard_map/ppermute | solution.py:78
  13.2 2.4 %collective-permute-done.1.refs_1_ = bf16[2,128,512]{2,1,0:T(8,128)(2,1)S(1)} collective-permute-done((bf16[2,128,512]{2,1,0:T(8,128)(2,1)S(1)}, bf16[2,128,512]{2,1,0:T(8,128)(2,1)S(1)}, u32[]{:S(2)}, u32[]{:S(2)}) %collective-permute-start.1) | collective-permute-done | bytes 262176 | tf_op jit(solution)/shard_map/ppermute | solution.py:78
  15.6 0.9 %collective-permute-start.5 = (bf16[2,128,512]{2,1,0:T(8,128)(2,1)S(1)}, bf16[2,128,512]{2,1,0:T(8,128)(2,1)S(1)}, u32[]{:S(2)}, u32[]{:S(2)}) collective-permute-start(bf16[2,128,512]{2,1,0:T(8,128)(2,1)S(1)} %get-tuple-element.53), channel_id=1, source_target_pairs={{0,2},{2,0},{4,6},{6,4},{8,10},{10,8},{12,14},{14,12},{16,18},{18,... | collective-permute-start | bytes 786440 | tf_op jit(solution)/shard_map/ppermute | solution.py:78
  16.5 2.9 %shard_map.62 = (bf16[2,256,1536]{2,1,0:T(8,128)(2,1)S(1)}, bf16[2,128,1024]{2,1,0:T(8,128)(2,1)S(1)}, bf16[2,128,1024]{2,1,0:T(8,128)(2,1)S(1)}) custom-call(s32[6]{0:T(128)S(1)} %stack.27.sc, bf16[2,256,512]{2,1,0:T(8,128)(2,1)S(1)} %get-tuple-element.59.refs_0_, bf16[2,256,512]{2,1,0:T(8,128)(2,1)S(1)} %get-tuple-element.60.refs_1_, ...), custom_call_target="tpu_custom_call" | custom-call | tf_op jit(solution)/shard_map/pallas_call | solution.py:48
  19.4 1.6 %collective-permute-start.18 = (bf16[2,128,1024]{2,1,0:T(8,128)(2,1)S(1)}, bf16[2,128,1024]{2,1,0:T(8,128)(2,1)S(1)}, u32[]{:S(2)}, u32[]{:S(2)}) collective-permute-start(bf16[2,128,1024]{2,1,0:T(8,128)(2,1)S(1)} %get-tuple-element.71), channel_id=1, source_target_pairs={{0,1},{1,0},{2,3},{3,2},{4,5},{5,4},{6,7},{7,6},{8,9},{9,8},{10,11... | collective-permute-start | bytes 1572872 | tf_op jit(solution)/shard_map/ppermute | solution.py:85
  20.9 1.1 %collective-permute-done.8.rest_0_ = bf16[2,128,512]{2,1,0:T(8,128)(2,1)S(1)} collective-permute-done((bf16[2,128,512]{2,1,0:T(8,128)(2,1)S(1)}, bf16[2,128,512]{2,1,0:T(8,128)(2,1)S(1)}, u32[]{:S(2)}, u32[]{:S(2)}) %collective-permute-start.8) | collective-permute-done | bytes 262176 | tf_op jit(solution)/shard_map/ppermute | solution.py:85
  22.0 2.5 %collective-permute-start.13 = (bf16[2,128,512]{2,1,0:T(8,128)(2,1)S(1)}, bf16[2,128,512]{2,1,0:T(8,128)(2,1)S(1)}, u32[]{:S(2)}, u32[]{:S(2)}) collective-permute-start(bf16[2,128,512]{2,1,0:T(8,128)(2,1)S(1)} %collective-permute-done.8.rest_0_), channel_id=1, source_target_pairs={{0,2},{2,0},{4,6},{6,4},{8,10},{10,8},{12,14},{14,12},{16,18},{18,... | collective-permute-start | bytes 786440 | tf_op jit(solution)/shard_map/ppermute | solution.py:78
  24.5 0.6 shard_map.60.w_ref
  25.2 1.4 %shard_map.61 = (f32[2,128,1024]{2,1,0:T(8,128)S(1)}, bf16[2,128,512]{2,1,0:T(8,128)(2,1)S(1)}) custom-call(s32[6]{0:T(128)S(1)} %stack.27.sc, bf16[2,128,1024]{2,1,0:T(8,128)(2,1)S(1)} %get-tuple-element.51.keep_ref, bf16[2,128,512]{2,1,0:T(8,128)(2,1)S(1)} %collective-permute-done.4.couple_ref, bf16[2,128,512]{2,1,0:T(8,128)(2,1)S(1)} %collective-permute-done.5.slots_ref, ...), custom_call_target="tpu_custom_call" | custom-call | flops 700000000 | tf_op jit(solution)/shard_map/pallas_call | solution.py:48
  26.6 1.1 %shard_map.63 = (bf16[2,128,512]{2,1,0:T(8,128)(2,1)S(1)}, bf16[2,128,256]{2,1,0:T(8,128)(2,1)S(1)}, bf16[2,128,256]{2,1,0:T(8,128)(2,1)S(1)}) custom-call(s32[6]{0:T(128)S(1)} %stack.27.sc, f32[2,128,1024]{2,1,0:T(8,128)S(1)} %get-tuple-element.55.acc_ref, bf16[2,128,512]{2,1,0:T(8,128)(2,1)S(1)} %get-tuple-element.56.hid_ref, ...), custom_call_target="tpu_custom_call" | custom-call | tf_op jit(solution)/shard_map/pallas_call | solution.py:48
  27.7 0.1 collective-permute-start.15
  27.8 0.6 collective-permute-start.2
  28.4 4.0 %collective-permute-done.15.x_ref = bf16[2,128,256]{2,1,0:T(8,128)(2,1)S(1)} collective-permute-done((bf16[2,128,256]{2,1,0:T(8,128)(2,1)S(1)}, bf16[2,128,256]{2,1,0:T(8,128)(2,1)S(1)}, u32[]{:S(2)}, u32[]{:S(2)}) %collective-permute-start.15) | collective-permute-done | bytes 131104 | tf_op jit(solution)/shard_map/ppermute | solution.py:78
  32.4 0.6 shard_map.64.own_ref
  32.9 0.4 collective-permute-start.16
  33.3 0.8 %collective-permute-start.22 = (bf16[2,128,768]{2,1,0:T(8,128)(2,1)S(1)}, bf16[2,128,768]{2,1,0:T(8,128)(2,1)S(1)}, u32[]{:S(2)}, u32[]{:S(2)}) collective-permute-start(bf16[2,128,768]{2,1,0:T(8,128)(2,1)S(1)} %shard_map.64.own_ref), channel_id=1, source_target_pairs={{0,1},{1,0},{2,3},{3,2},{4,5},{5,4},{6,7},{7,6},{8,9},{9,8},{10,11... | collective-permute-start | bytes 1179656 | tf_op jit(solution)/shard_map/ppermute | solution.py:85
  34.1 1.9 %collective-permute-start.19 = (bf16[2,128,1024]{2,1,0:T(8,128)(2,1)S(1)}, bf16[2,128,1024]{2,1,0:T(8,128)(2,1)S(1)}, u32[]{:S(2)}, u32[]{:S(2)}) collective-permute-start(bf16[2,128,1024]{2,1,0:T(8,128)(2,1)S(1)} %collective-permute-done.18.rest_4_.refs_0_), channel_id=1, source_target_pairs={{0,2},{2,0},{4,6},{6,4},{8,10},{10,8},{12,14},{14,12},{16,18},{18,... | collective-permute-start | bytes 1572872 | tf_op jit(solution)/shard_map/ppermute | solution.py:78
  36.0 0.4 collective-permute-start.20
  36.4 1.5 %collective-permute-done.3.refs_3_ = bf16[2,128,512]{2,1,0:T(8,128)(2,1)S(1)} collective-permute-done((bf16[2,128,512]{2,1,0:T(8,128)(2,1)S(1)}, bf16[2,128,512]{2,1,0:T(8,128)(2,1)S(1)}, u32[]{:S(2)}, u32[]{:S(2)}) %collective-permute-start.3) | collective-permute-done | bytes 262176 | tf_op jit(solution)/shard_map/ppermute | solution.py:78
  37.9 0.7 %shard_map.58.refs_6_ = bf16[2,512,512]{2,1,0:T(8,128)(2,1)S(1)} custom-call(s32[6]{0:T(128)S(1)} %stack.27.sc, bf16[2,128,512]{2,1,0:T(8,128)(2,1)S(1)} %bitcast.17, bf16[2,128,512]{2,1,0:T(8,128)(2,1)S(1)} %collective-permute-done.1.refs_1_, bf16[2,128,512]{2,1,0:T(8,128)(2,1)S(1)} %collective-permute-done.2.refs_2_, ...), custom_call_target="tpu_custom_call" | custom-call | tf_op jit(solution)/shard_map/pallas_call | solution.py:48
  38.6 3.7 %collective-permute-done.16.x_ref = bf16[2,128,768]{2,1,0:T(8,128)(2,1)S(1)} collective-permute-done((bf16[2,128,768]{2,1,0:T(8,128)(2,1)S(1)}, bf16[2,128,768]{2,1,0:T(8,128)(2,1)S(1)}, u32[]{:S(2)}, u32[]{:S(2)}) %collective-permute-start.16) | collective-permute-done | bytes 393248 | tf_op jit(solution)/shard_map/ppermute | solution.py:78
  42.3 0.6 shard_map.65.own_ref
  42.9 2.3 %collective-permute-start.17 = (bf16[2,128,1536]{2,1,0:T(8,128)(2,1)S(1)}, bf16[2,128,1536]{2,1,0:T(8,128)(2,1)S(1)}, u32[]{:S(2)}, u32[]{:S(2)}) collective-permute-start(bf16[2,128,1536]{2,1,0:T(8,128)(2,1)S(1)} %shard_map.65.own_ref), channel_id=1, source_target_pairs={{0,2},{2,0},{4,6},{6,4},{8,10},{10,8},{12,14},{14,12},{16,18},{18,... | collective-permute-start | bytes 2359304 | tf_op jit(solution)/shard_map/ppermute | solution.py:78
  45.2 0.3 collective-permute-start.23
  45.5 4.2 %shard_map.67.refs_5_ = bf16[2,512,1536]{2,1,0:T(8,128)(2,1)S(1)} custom-call(s32[6]{0:T(128)S(1)} %stack.27.sc, bf16[2,512,512]{2,1,0:T(8,128)(2,1)S(1)} %shard_map.60.w_ref, bf16[2,256,512]{2,1,0:T(8,128)(2,1)S(1)} %get-tuple-element.46.end_ref.refs_8_.own_ref, bf16[2,256,512]{2,1,0:T(8,128)(2,1)S(1)} %collective-permute-done.7.endsib_ref.refs_9_.sib_ref, ...), custom_call_target="tpu_custom_call" | custom-call | flops 800000000 | tf_op jit(solution)/shard_map/pallas_call | solution.py:48
  49.8 4.1 %collective-permute-done.20.refs_2_ = bf16[2,128,1024]{2,1,0:T(8,128)(2,1)S(1)} collective-permute-done((bf16[2,128,1024]{2,1,0:T(8,128)(2,1)S(1)}, bf16[2,128,1024]{2,1,0:T(8,128)(2,1)S(1)}, u32[]{:S(2)}, u32[]{:S(2)}) %collective-permute-start.20) | collective-permute-done | bytes 524320 | tf_op jit(solution)/shard_map/ppermute | solution.py:85
  53.9 2.2 %collective-permute-start.21 = (bf16[2,128,1024]{2,1,0:T(8,128)(2,1)S(1)}, bf16[2,128,1024]{2,1,0:T(8,128)(2,1)S(1)}, u32[]{:S(2)}, u32[]{:S(2)}) collective-permute-start(bf16[2,128,1024]{2,1,0:T(8,128)(2,1)S(1)} %collective-permute-done.20.refs_2_), channel_id=1, source_target_pairs={{0,2},{2,0},{4,6},{6,4},{8,10},{10,8},{12,14},{14,12},{16,18},{18,... | collective-permute-start | bytes 1572872 | tf_op jit(solution)/shard_map/ppermute | solution.py:78
  56.1 0.6 shard_map.69
  56.8 0.7 %collective-permute-start.24 = (bf16[2,128,768]{2,1,0:T(8,128)(2,1)S(1)}, bf16[2,128,768]{2,1,0:T(8,128)(2,1)S(1)}, u32[]{:S(2)}, u32[]{:S(2)}) collective-permute-start(bf16[2,128,768]{2,1,0:T(8,128)(2,1)S(1)} %get-tuple-element.81.refs_0_), channel_id=1, source_target_pairs={{0,2},{2,0},{4,6},{6,4},{8,10},{10,8},{12,14},{14,12},{16,18},{18,... | collective-permute-start | bytes 1179656 | tf_op jit(solution)/shard_map/ppermute | solution.py:78
  57.5 0.1 collective-permute-start.25
  57.5 0.6 shard_map.66.near_ref
  58.2 3.4 %shard_map.68 = (bf16[2,512,512]{2,1,0:T(8,128)(2,1)S(1)}, bf16[512,512]{1,0:T(8,128)(2,1)S(1)}, bf16[512,512]{1,0:T(8,128)(2,1)S(1)}) custom-call(s32[6]{0:T(128)S(1)} %stack.27.sc, bf16[2,256,1536]{2,1,0:T(8,128)(2,1)S(1)} %get-tuple-element.70.end_ref, bf16[2,256,1536]{2,1,0:T(8,128)(2,1)S(1)} %get-tuple-element.63.kept_ref, ...), custom_call_target="tpu_custom_call" | custom-call | flops 300000000 | tf_op jit(solution)/shard_map/pallas_call | solution.py:48
  61.6 3.3 %shard_map.70 = bf16[2,1,256,1536]{3,2,1,0:T(8,128)(2,1)} custom-call(s32[6]{0:T(128)S(1)} %stack.27.sc, bf16[2,512,512]{2,1,0:T(8,128)(2,1)S(1)} %get-tuple-element.76.hid_ref, bf16[512,512]{1,0:T(8,128)(2,1)S(1)} %get-tuple-element.77.first_ref, bf16[512,512]{1,0:T(8,128)(2,1)S(1)} %get-tuple-element.78.slots_ref, ...), custom_call_target="tpu_custom_call" | custom-call | tf_op jit(solution)/shard_map/pallas_call | solution.py:48
  (33 shorter events, 0.1 us)
Async XLA Ops:
  0.0 4.3 %copy-start.4 = (s32[1,8,512]{2,1,0:T(8,128)S(1)}, s32[1,8,512]{2,1,0:T(8,128)}, u32[]{:S(2)}) copy-start(s32[1,8,512]{2,1,0:T(8,128)} %param.8) | copy-start | bytes 49156
  0.1 2.3 %copy-start = (bf16[2,1,1,3,256,1536]{5,4,3,2,1,0:T(8,128)(2,1)S(1)}, bf16[2,1,1,3,256,1536]{5,4,3,2,1,0:T(8,128)(2,1)}, u32[]{:S(2)}) copy-start(bf16[2,1,1,3,256,1536]{5,4,3,2,1,0:T(8,128)(2,1)} %param.5) | copy-start | bytes 14155780
  2.4 1.9 %copy-start.5 = (s32[1,4,512]{2,1,0:T(4,128)S(1)}, s32[1,4,512]{2,1,0:T(4,128)}, u32[]{:S(2)}) copy-start(s32[1,4,512]{2,1,0:T(4,128)} %param.9) | copy-start | bytes 24580
  2.4 8.3 %copy-start.1 = (bf16[2,1,1,3,256,1536]{5,4,3,2,1,0:T(8,128)(2,1)S(1)}, bf16[2,1,1,3,256,1536]{5,4,3,2,1,0:T(8,128)(2,1)}, u32[]{:S(2)}) copy-start(bf16[2,1,1,3,256,1536]{5,4,3,2,1,0:T(8,128)(2,1)} %param.5) | copy-start | bytes 14155780
  3.1 3.3 %copy-start.2 = (bf16[2,1,256,512]{3,2,1,0:T(8,128)(2,1)S(1)}, bf16[2,1,256,512]{3,2,1,0:T(8,128)(2,1)}, u32[]{:S(2)}) copy-start(bf16[2,1,256,512]{3,2,1,0:T(8,128)(2,1)} %param.6) | copy-start | bytes 1572868
  3.2 3.8 %copy-start.3 = (bf16[2,1,128,512]{3,2,1,0:T(8,128)(2,1)S(1)}, bf16[2,1,128,512]{3,2,1,0:T(8,128)(2,1)}, u32[]{:S(2)}) copy-start(bf16[2,1,128,512]{3,2,1,0:T(8,128)(2,1)} %param.7) | copy-start | bytes 786436
  3.2 2.0 %collective-permute-start = (bf16[2,256,512]{2,1,0:T(8,128)(2,1)S(1)}, bf16[2,256,512]{2,1,0:T(8,128)(2,1)S(1)}, u32[]{:S(2)}, u32[]{:S(2)}) collective-permute-start(bf16[2,256,512]{2,1,0:T(8,128)(2,1)S(1)} %get-tuple-element.44.own_ref), channel_id=1, source_target_pairs={{0,2},{2,0},{4,6},{6,4},{8,10},{10,8},{12,14},{14,12},{16,18},{18,... | collective-permute-start | bytes 1572872 | tf_op jit(solution)/shard_map/ppermute | solution.py:78
  3.3 3.6 %collective-permute-start.10 = (bf16[2,256,512]{2,1,0:T(8,128)(2,1)S(1)}, bf16[2,256,512]{2,1,0:T(8,128)(2,1)S(1)}, u32[]{:S(2)}, u32[]{:S(2)}) collective-permute-start(bf16[2,256,512]{2,1,0:T(8,128)(2,1)S(1)} %get-tuple-element.59.refs_0_), channel_id=1, source_target_pairs={{0,2},{2,0},{4,6},{6,4},{8,10},{10,8},{12,14},{14,12},{16,18},{18,... | collective-permute-start | bytes 1572872 | tf_op jit(solution)/shard_map/ppermute | solution.py:78
  3.7 5.5 %collective-permute-start.11 = (bf16[2,256,512]{2,1,0:T(8,128)(2,1)S(1)}, bf16[2,256,512]{2,1,0:T(8,128)(2,1)S(1)}, u32[]{:S(2)}, u32[]{:S(2)}) collective-permute-start(bf16[2,256,512]{2,1,0:T(8,128)(2,1)S(1)} %get-tuple-element.60.refs_1_), channel_id=1, source_target_pairs={{0,2},{2,0},{4,6},{6,4},{8,10},{10,8},{12,14},{14,12},{16,18},{18,... | collective-permute-start | bytes 1572872 | tf_op jit(solution)/shard_map/ppermute | solution.py:78
  3.8 6.7 %collective-permute-start.12 = (bf16[2,256,512]{2,1,0:T(8,128)(2,1)S(1)}, bf16[2,256,512]{2,1,0:T(8,128)(2,1)S(1)}, u32[]{:S(2)}, u32[]{:S(2)}) collective-permute-start(bf16[2,256,512]{2,1,0:T(8,128)(2,1)S(1)} %get-tuple-element.61.refs_2_), channel_id=1, source_target_pairs={{0,2},{2,0},{4,6},{6,4},{8,10},{10,8},{12,14},{14,12},{16,18},{18,... | collective-permute-start | bytes 1572872 | tf_op jit(solution)/shard_map/ppermute | solution.py:78
  4.3 7.6 %collective-permute-start.7 = (bf16[2,256,512]{2,1,0:T(8,128)(2,1)S(1)}, bf16[2,256,512]{2,1,0:T(8,128)(2,1)S(1)}, u32[]{:S(2)}, u32[]{:S(2)}) collective-permute-start(bf16[2,256,512]{2,1,0:T(8,128)(2,1)S(1)} %get-tuple-element.46.end_ref.refs_8_.own_ref), channel_id=1, source_target_pairs={{0,2},{2,0},{4,6},{6,4},{8,10},{10,8},{12,14},{14,12},{16,18},{18,... | collective-permute-start | bytes 1572872 | tf_op jit(solution)/shard_map/ppermute | solution.py:78
  6.4 18.1 %collective-permute-start.6 = (bf16[2,256,512]{2,1,0:T(8,128)(2,1)S(1)}, bf16[2,256,512]{2,1,0:T(8,128)(2,1)S(1)}, u32[]{:S(2)}, u32[]{:S(2)}) collective-permute-start(bf16[2,256,512]{2,1,0:T(8,128)(2,1)S(1)} %bitcast.13), channel_id=1, source_target_pairs={{0,2},{2,0},{4,6},{6,4},{8,10},{10,8},{12,14},{14,12},{16,18},{18,... | collective-permute-start | bytes 1572872 | tf_op jit(solution)/shard_map/ppermute | solution.py:78
  6.9 8.6 %collective-permute-start.1 = (bf16[2,128,512]{2,1,0:T(8,128)(2,1)S(1)}, bf16[2,128,512]{2,1,0:T(8,128)(2,1)S(1)}, u32[]{:S(2)}, u32[]{:S(2)}) collective-permute-start(bf16[2,128,512]{2,1,0:T(8,128)(2,1)S(1)} %bitcast.15), channel_id=1, source_target_pairs={{0,4},{2,6},{4,0},{6,2},{8,12},{10,14},{12,8},{14,10},{16,20},{18,... | collective-permute-start | bytes 786440 | tf_op jit(solution)/shard_map/ppermute | solution.py:78
  9.2 10.1 %collective-permute-start.9 = (bf16[2,128,512]{2,1,0:T(8,128)(2,1)S(1)}, bf16[2,128,512]{2,1,0:T(8,128)(2,1)S(1)}, u32[]{:S(2)}, u32[]{:S(2)}) collective-permute-start(bf16[2,128,512]{2,1,0:T(8,128)(2,1)S(1)} %get-tuple-element.58), channel_id=1, source_target_pairs={{0,1},{1,0},{2,3},{3,2},{4,5},{5,4},{6,7},{7,6},{8,9},{9,8},{10,11... | collective-permute-start | bytes 786440 | tf_op jit(solution)/shard_map/ppermute | solution.py:85
  10.5 11.5 %collective-permute-start.8 = (bf16[2,128,512]{2,1,0:T(8,128)(2,1)S(1)}, bf16[2,128,512]{2,1,0:T(8,128)(2,1)S(1)}, u32[]{:S(2)}, u32[]{:S(2)}) collective-permute-start(bf16[2,128,512]{2,1,0:T(8,128)(2,1)S(1)} %get-tuple-element.57), channel_id=1, source_target_pairs={{0,1},{1,0},{2,3},{3,2},{4,5},{5,4},{6,7},{7,6},{8,9},{9,8},{10,11... | collective-permute-start | bytes 786440 | tf_op jit(solution)/shard_map/ppermute | solution.py:85
  11.8 13.3 %collective-permute-start.4 = (bf16[2,128,512]{2,1,0:T(8,128)(2,1)S(1)}, bf16[2,128,512]{2,1,0:T(8,128)(2,1)S(1)}, u32[]{:S(2)}, u32[]{:S(2)}) collective-permute-start(bf16[2,128,512]{2,1,0:T(8,128)(2,1)S(1)} %get-tuple-element.52), channel_id=1, source_target_pairs={{0,2},{2,0},{4,6},{6,4},{8,10},{10,8},{12,14},{14,12},{16,18},{18,... | collective-permute-start | bytes 786440 | tf_op jit(solution)/shard_map/ppermute | solution.py:78
  15.6 9.6 %collective-permute-start.5 = (bf16[2,128,512]{2,1,0:T(8,128)(2,1)S(1)}, bf16[2,128,512]{2,1,0:T(8,128)(2,1)S(1)}, u32[]{:S(2)}, u32[]{:S(2)}) collective-permute-start(bf16[2,128,512]{2,1,0:T(8,128)(2,1)S(1)} %get-tuple-element.53), channel_id=1, source_target_pairs={{0,2},{2,0},{4,6},{6,4},{8,10},{10,8},{12,14},{14,12},{16,18},{18,... | collective-permute-start | bytes 786440 | tf_op jit(solution)/shard_map/ppermute | solution.py:78
  19.4 14.7 %collective-permute-start.18 = (bf16[2,128,1024]{2,1,0:T(8,128)(2,1)S(1)}, bf16[2,128,1024]{2,1,0:T(8,128)(2,1)S(1)}, u32[]{:S(2)}, u32[]{:S(2)}) collective-permute-start(bf16[2,128,1024]{2,1,0:T(8,128)(2,1)S(1)} %get-tuple-element.71), channel_id=1, source_target_pairs={{0,1},{1,0},{2,3},{3,2},{4,5},{5,4},{6,7},{7,6},{8,9},{9,8},{10,11... | collective-permute-start | bytes 1572872 | tf_op jit(solution)/shard_map/ppermute | solution.py:85
  22.0 4.6 %collective-permute-start.13 = (bf16[2,128,512]{2,1,0:T(8,128)(2,1)S(1)}, bf16[2,128,512]{2,1,0:T(8,128)(2,1)S(1)}, u32[]{:S(2)}, u32[]{:S(2)}) collective-permute-start(bf16[2,128,512]{2,1,0:T(8,128)(2,1)S(1)} %collective-permute-done.8.rest_0_), channel_id=1, source_target_pairs={{0,2},{2,0},{4,6},{6,4},{8,10},{10,8},{12,14},{14,12},{16,18},{18,... | collective-permute-start | bytes 786440 | tf_op jit(solution)/shard_map/ppermute | solution.py:78
  24.5 2.1 %collective-permute-start.14 = (bf16[2,128,512]{2,1,0:T(8,128)(2,1)S(1)}, bf16[2,128,512]{2,1,0:T(8,128)(2,1)S(1)}, u32[]{:S(2)}, u32[]{:S(2)}) collective-permute-start(bf16[2,128,512]{2,1,0:T(8,128)(2,1)S(1)} %collective-permute-done.9.rest_1_), channel_id=1, source_target_pairs={{0,2},{2,0},{4,6},{6,4},{8,10},{10,8},{12,14},{14,12},{16,18},{18,... | collective-permute-start | bytes 786440 | tf_op jit(solution)/shard_map/ppermute | solution.py:78
  27.7 4.6 %collective-permute-start.15 = (bf16[2,128,256]{2,1,0:T(8,128)(2,1)S(1)}, bf16[2,128,256]{2,1,0:T(8,128)(2,1)S(1)}, u32[]{:S(2)}, u32[]{:S(2)}) collective-permute-start(bf16[2,128,256]{2,1,0:T(8,128)(2,1)S(1)} %get-tuple-element.68), channel_id=1, source_target_pairs={{0,4},{2,6},{4,0},{6,2},{8,12},{10,14},{12,8},{14,10},{16,20},{18,... | collective-permute-start | bytes 393224 | tf_op jit(solution)/shard_map/ppermute | solution.py:78
  27.8 8.2 %collective-permute-start.2 = (bf16[2,128,512]{2,1,0:T(8,128)(2,1)S(1)}, bf16[2,128,512]{2,1,0:T(8,128)(2,1)S(1)}, u32[]{:S(2)}, u32[]{:S(2)}) collective-permute-start(bf16[2,128,512]{2,1,0:T(8,128)(2,1)S(1)} %bitcast.16), channel_id=1, source_target_pairs={{0,2},{2,0},{4,6},{6,4},{8,10},{10,8},{12,14},{14,12},{16,18},{18,... | collective-permute-start | bytes 786440 | tf_op jit(solution)/shard_map/ppermute | solution.py:78
  32.9 9.3 %collective-permute-start.16 = (bf16[2,128,768]{2,1,0:T(8,128)(2,1)S(1)}, bf16[2,128,768]{2,1,0:T(8,128)(2,1)S(1)}, u32[]{:S(2)}, u32[]{:S(2)}) collective-permute-start(bf16[2,128,768]{2,1,0:T(8,128)(2,1)S(1)} %shard_map.64.own_ref), channel_id=1, source_target_pairs={{0,4},{2,6},{4,0},{6,2},{8,12},{10,14},{12,8},{14,10},{16,20},{18,... | collective-permute-start | bytes 1179656 | tf_op jit(solution)/shard_map/ppermute | solution.py:78
  33.3 11.9 %collective-permute-start.22 = (bf16[2,128,768]{2,1,0:T(8,128)(2,1)S(1)}, bf16[2,128,768]{2,1,0:T(8,128)(2,1)S(1)}, u32[]{:S(2)}, u32[]{:S(2)}) collective-permute-start(bf16[2,128,768]{2,1,0:T(8,128)(2,1)S(1)} %shard_map.64.own_ref), channel_id=1, source_target_pairs={{0,1},{1,0},{2,3},{3,2},{4,5},{5,4},{6,7},{7,6},{8,9},{9,8},{10,11... | collective-permute-start | bytes 1179656 | tf_op jit(solution)/shard_map/ppermute | solution.py:85
  34.1 11.4 %collective-permute-start.19 = (bf16[2,128,1024]{2,1,0:T(8,128)(2,1)S(1)}, bf16[2,128,1024]{2,1,0:T(8,128)(2,1)S(1)}, u32[]{:S(2)}, u32[]{:S(2)}) collective-permute-start(bf16[2,128,1024]{2,1,0:T(8,128)(2,1)S(1)} %collective-permute-done.18.rest_4_.refs_0_), channel_id=1, source_target_pairs={{0,2},{2,0},{4,6},{6,4},{8,10},{10,8},{12,14},{14,12},{16,18},{18,... | collective-permute-start | bytes 1572872 | tf_op jit(solution)/shard_map/ppermute | solution.py:78
  36.0 1.9 %collective-permute-start.3 = (bf16[2,128,512]{2,1,0:T(8,128)(2,1)S(1)}, bf16[2,128,512]{2,1,0:T(8,128)(2,1)S(1)}, u32[]{:S(2)}, u32[]{:S(2)}) collective-permute-start(bf16[2,128,512]{2,1,0:T(8,128)(2,1)S(1)} %collective-permute-done.1.refs_1_), channel_id=1, source_target_pairs={{0,2},{2,0},{4,6},{6,4},{8,10},{10,8},{12,14},{14,12},{16,18},{18,... | collective-permute-start | bytes 786440 | tf_op jit(solution)/shard_map/ppermute | solution.py:78
  36.0 17.8 %collective-permute-start.20 = (bf16[2,128,1024]{2,1,0:T(8,128)(2,1)S(1)}, bf16[2,128,1024]{2,1,0:T(8,128)(2,1)S(1)}, u32[]{:S(2)}, u32[]{:S(2)}) collective-permute-start(bf16[2,128,1024]{2,1,0:T(8,128)(2,1)S(1)} %get-tuple-element.74), channel_id=1, source_target_pairs={{0,1},{1,0},{2,3},{3,2},{4,5},{5,4},{6,7},{7,6},{8,9},{9,8},{10,11... | collective-permute-start | bytes 1572872 | tf_op jit(solution)/shard_map/ppermute | solution.py:85
  42.9 14.7 %collective-permute-start.17 = (bf16[2,128,1536]{2,1,0:T(8,128)(2,1)S(1)}, bf16[2,128,1536]{2,1,0:T(8,128)(2,1)S(1)}, u32[]{:S(2)}, u32[]{:S(2)}) collective-permute-start(bf16[2,128,1536]{2,1,0:T(8,128)(2,1)S(1)} %shard_map.65.own_ref), channel_id=1, source_target_pairs={{0,2},{2,0},{4,6},{6,4},{8,10},{10,8},{12,14},{14,12},{16,18},{18,... | collective-permute-start | bytes 2359304 | tf_op jit(solution)/shard_map/ppermute | solution.py:78
  45.2 10.9 %collective-permute-start.23 = (bf16[2,128,768]{2,1,0:T(8,128)(2,1)S(1)}, bf16[2,128,768]{2,1,0:T(8,128)(2,1)S(1)}, u32[]{:S(2)}, u32[]{:S(2)}) collective-permute-start(bf16[2,128,768]{2,1,0:T(8,128)(2,1)S(1)} %collective-permute-done.22.own_ref), channel_id=1, source_target_pairs={{0,4},{2,6},{4,0},{6,2},{8,12},{10,14},{12,8},{14,10},{16,20},{18,... | collective-permute-start | bytes 1179656 | tf_op jit(solution)/shard_map/ppermute | solution.py:78
  53.9 4.3 %collective-permute-start.21 = (bf16[2,128,1024]{2,1,0:T(8,128)(2,1)S(1)}, bf16[2,128,1024]{2,1,0:T(8,128)(2,1)S(1)}, u32[]{:S(2)}, u32[]{:S(2)}) collective-permute-start(bf16[2,128,1024]{2,1,0:T(8,128)(2,1)S(1)} %collective-permute-done.20.refs_2_), channel_id=1, source_target_pairs={{0,2},{2,0},{4,6},{6,4},{8,10},{10,8},{12,14},{14,12},{16,18},{18,... | collective-permute-start | bytes 1572872 | tf_op jit(solution)/shard_map/ppermute | solution.py:78
  56.8 4.9 %collective-permute-start.24 = (bf16[2,128,768]{2,1,0:T(8,128)(2,1)S(1)}, bf16[2,128,768]{2,1,0:T(8,128)(2,1)S(1)}, u32[]{:S(2)}, u32[]{:S(2)}) collective-permute-start(bf16[2,128,768]{2,1,0:T(8,128)(2,1)S(1)} %get-tuple-element.81.refs_0_), channel_id=1, source_target_pairs={{0,2},{2,0},{4,6},{6,4},{8,10},{10,8},{12,14},{14,12},{16,18},{18,... | collective-permute-start | bytes 1179656 | tf_op jit(solution)/shard_map/ppermute | solution.py:78
  57.5 4.2 %collective-permute-start.25 = (bf16[2,128,768]{2,1,0:T(8,128)(2,1)S(1)}, bf16[2,128,768]{2,1,0:T(8,128)(2,1)S(1)}, u32[]{:S(2)}, u32[]{:S(2)}) collective-permute-start(bf16[2,128,768]{2,1,0:T(8,128)(2,1)S(1)} %get-tuple-element.82.refs_1_), channel_id=1, source_target_pairs={{0,2},{2,0},{4,6},{6,4},{8,10},{10,8},{12,14},{14,12},{16,18},{18,... | collective-permute-start | bytes 1179656 | tf_op jit(solution)/shard_map/ppermute | solution.py:78

commit v15 on v14

--- a/solution.py
+++ b/solution.py
@@ -365,14 +365,6 @@
             scratch=[pltpu.VMEM((2, hr, 3 * k), BF16)],
         )
     two_sib = [box_permute(a, 1) for a in two_rows[:1]]
-
-    def layout_kernel(sc, own_ref, sib_ref, out_ref):
-        for ref, take in zip((own_ref, sib_ref), halves(sc[0])):
-            out_ref[:, take, :] = ref[...]
-
-    (two_first,) = call(
-        layout_kernel, scalars, [two_rows[0], two_sib[0]], [sds((2, fr, 3 * k), BF16)]
-    )
 
     ends_far = [face_permute(after(a, two_own), i + 1) for i, a in enumerate(kept_out[:nf])]
     ends_fwd = [box_permute(after(a, solved_one), 1) for a in ends_far]
@@ -423,28 +415,28 @@
             hid_out[s] = piece((second[:fr], second[fr:]), s * fr, fr)
 
     hid_two, first_two, slots_two = call(
-        level_one_kernel, after(scalars, two_first),
+        level_one_kernel, scalars,
         [end_kept, kept, *mixed_far, *mixed_fwd, *ends_far, *ends_fwd, skel_col, solved_one, weight_two],
         [sds((n_face, 2 * fr, 2 * fr), BF16), sds((2 * fr, k), BF16), sds((2 * fr, k), BF16)],
         scratch=[pltpu.VMEM((2, fr, 3 * k), BF16)], cost=KEEP_COST,
     )
 
-    def level_two_kernel(sc, hid_ref, first_ref, slots_ref, near_ref, *refs):
-        out_ref, rows, stage, sems = refs[4 * nf :]
+    def level_two_kernel(sc, hid_ref, first_ref, slots_ref, *refs):
+        mine, other = refs[: 1 + 2 * nf], refs[1 + 2 * nf : 2 + 4 * nf]
+        out_ref, rows, stage, sems = refs[2 + 4 * nf :]
         q = sc[1]
-        far = jnp.concatenate([hid_ref[s] for s in range(1, n_face)], axis=1)
-        for h, take in enumerate(halves(sc[0])):
-            for i, ref in enumerate(refs[h * 2 * nf : (h + 1) * 2 * nf]):
-                rows[i // 2, :, take, i % 2 * 3 * half : (i % 2 + 1) * 3 * half] = ref[...]
+        left = jnp.concatenate([hid_ref[s] for s in range(n_face)], axis=1)
+        for take, parts in zip(halves(sc[0]), (mine, other)):
+            rows[0, :, take, :] = parts[0][...]
+            for i, ref in enumerate(parts[1:]):
+                rows[1 + i // 2, :, take, i % 2 * 3 * half : (i % 2 + 1) * 3 * half] = ref[...]
         copies = []
         for c in range(3):
-            cols = slice(c * k, (c + 1) * k)
             first = slots_ref[...]
             if c < 2:
                 first = jnp.where(q == c, first_ref[...], jnp.zeros((2 * fr, k), BF16))
-            total = first.astype(F32) - dot(hid_ref[0], flat(near_ref[:, :, cols]))
-            total = total - dot(far, rows[:, :, :, cols].reshape(nf * 2 * fr, k))
-            stage[c] = total.astype(BF16).reshape(2, fr, k)
+            right = rows[:, :, :, c * k : (c + 1) * k].reshape(n_face * 2 * fr, k)
+            stage[c] = (first.astype(F32) - dot(left, right)).astype(BF16).reshape(2, fr, k)
             for t in range(2):
                 copies.append(pltpu.make_async_copy(
                     stage.at[c, t], out_ref.at[t, 0, :, pl.ds(c * k, k)], sems.at[c, t]
@@ -454,9 +446,9 @@
             copy.wait()
 
     (out,) = call(
-        level_two_kernel, scalars, [hid_two, first_two, slots_two, two_first, *two_rows[1:], *two_sib[1:]],
+        level_two_kernel, scalars, [hid_two, first_two, slots_two, *two_rows, *two_sib],
         [sds((2, 1, fr, 3 * k), BF16)], out_specs=[in_hbm],
-        scratch=[pltpu.VMEM((nf, 2, fr, 3 * k), BF16), pltpu.VMEM((3, 2, fr, k), BF16),
+        scratch=[pltpu.VMEM((n_face, 2, fr, 3 * k), BF16), pltpu.VMEM((3, 2, fr, k), BF16),
                  pltpu.SemaphoreType.DMA((3, 2))],
     )
     return out

time: 65.5 us -> 64.6 us (0.986)
  waiting for transfers between devices: 16.8 us -> 12.5 us
  starting transfers between devices: 21.6 us -> 25.4 us
    ppermute x21, waiting for transfers between devices: 11.6 us -> 7.32 us  [box_permute(): return lax.ppermute(array, 'box', [(b, b ^ mask) for b in range(n_box)])]
    ppermute x21, starting transfers between devices: 17.4 us -> 20.1 us  [box_permute(): return lax.ppermute(array, 'box', [(b, b ^ mask) for b in range(n_box)])]
    ppermute x5, starting transfers between devices: 4.17 us -> 5.31 us  [face_permute(): return lax.ppermute(array, ('box', 'face'), pairs)]
    pallas_call x16 -> x15, Pallas kernels: 23.9 us -> 23.4 us  [call(): pl.pallas_call(kernel, in_specs=[pl.BlockSpec(memory_space=pltpu.SMEM)] +...]
  transfers between devices with their start and end apart: 26 -> 26, of which waited for: 6 -> 6; matrix products, arithmetic and copies ran while one was open for 0% -> 0% of each run, Pallas kernels for 31% -> 30%
where the time goes in v15:
time: 64.6 us; the launch traced here: 64.2 us
  starting transfers between devices  25.4 us (39%)
  Pallas kernels  23.4 us (36%)
  waiting for transfers between devices  12.5 us (19%)
  local copies, waits for them, and re-layouts  2.45 us (4%)
    pallas_call x15, Pallas kernels, call(): pl.pallas_call(kernel, in_specs=[pl.BlockSpec(memory_space=pltpu.SMEM)] +...  23.4 us
    ppermute x21, starting transfers between devices, box_permute(): return lax.ppermute(array, 'box', [(b, b ^ mask) for b in range(n_box)])  20.1 us
    ppermute x21, waiting for transfers between devices, box_permute(): return lax.ppermute(array, 'box', [(b, b ^ mask) for b in range(n_box)])  7.32 us
    ppermute x5, starting transfers between devices, face_permute(): return lax.ppermute(array, ('box', 'face'), pairs)  5.31 us
    ppermute x5, waiting for transfers between devices, face_permute(): return lax.ppermute(array, ('box', 'face'), pairs)  5.23 us
    unnamed x12, local copies, waits for them, and re-layouts  2.36 us
  transfers between devices with their start and end apart: 26, of which 6 were waited for; matrix products, arithmetic and copies ran while one was open for 0% of the time, Pallas kernels for 30%

profile of v15, /device:TPU:1, one launch (start us, length us, event | category | flops | bytes accessed | tf_op | source)
XLA Modules:
  0.0 64.2 jit_solution(1630717722437995070)
XLA Ops:
  0.0 0.1 stack.27.sc
  0.1 2.3 %copy-done = bf16[2,1,1,3,256,1536]{5,4,3,2,1,0:T(8,128)(2,1)S(1)} copy-done((bf16[2,1,1,3,256,1536]{5,4,3,2,1,0:T(8,128)(2,1)S(1)}, bf16[2,1,1,3,256,1536]{5,4,3,2,1,0:T(8,128)(2,1)}, u32[]{:S(2)}) %copy-start) | copy-done | bytes 4718616
  2.4 0.7 %shard_map.55 = (bf16[2,256,512]{2,1,0:T(8,128)(2,1)S(1)}, bf16[2,256,512]{2,1,0:T(8,128)(2,1)S(1)}, bf16[2,256,512]{2,1,0:T(8,128)(2,1)S(1)}, bf16[2,256,512]{2,1,0:T(8,128)(2,1)S(1)}, bf16[2,256,512]{2,1,0:T(8,128)(2,1)S(1)}) custom-call(s32[6]{0:T(128)S(1)} %stack.27.sc, bf16[2,3,256,1536]{3,2,1,0:T(8,128)(2,1)S(1)} %bitcast.11), custom_call_target="tpu_custom_call" | custom-call | tf_op jit(solution)/shard_map/pallas_call | solution.py:48
  3.2 0.1 collective-permute-start
  3.3 0.5 collective-permute-start.1
  3.7 0.1 collective-permute-start.2
  3.8 0.4 collective-permute-start.3
  4.3 0.1 collective-permute-start.4
  4.3 0.8 %shard_map.56 = (s32[1,512]{1,0:T(1,128)S(1)}, s32[512,1]{1,0:T(8,128)S(1)}) custom-call(s32[6]{0:T(128)S(1)} %stack.27.sc, s32[8,512]{1,0:T(8,128)S(1)} %bitcast.18, s32[4,512]{1,0:T(4,128)S(1)} %bitcast.19), custom_call_target="tpu_custom_call" | custom-call | tf_op jit(solution)/shard_map/pallas_call | solution.py:48
  5.2 0.0 copy-start.1
  5.2 1.3 %shard_map.57 = (bf16[2,256,512]{2,1,0:T(8,128)(2,1)S(1)}, bf16[2,128,512]{2,1,0:T(8,128)(2,1)S(1)}, bf16[2,128,512]{2,1,0:T(8,128)(2,1)S(1)}) custom-call(s32[6]{0:T(128)S(1)} %stack.27.sc, bf16[2,256,512]{2,1,0:T(8,128)(2,1)S(1)} %get-tuple-element.43.own_ref, bf16[2,256,512]{2,1,0:T(8,128)(2,1)S(1)} %collective-permute-done.sib_ref, ...), custom_call_target="tpu_custom_call" | custom-call | tf_op jit(solution)/shard_map/pallas_call | solution.py:48
  6.4 0.5 collective-permute-start.8
  6.9 2.3 %collective-permute-start.9 = (bf16[2,128,512]{2,1,0:T(8,128)(2,1)S(1)}, bf16[2,128,512]{2,1,0:T(8,128)(2,1)S(1)}, u32[]{:S(2)}, u32[]{:S(2)}) collective-permute-start(bf16[2,128,512]{2,1,0:T(8,128)(2,1)S(1)} %get-tuple-element.61), channel_id=1, source_target_pairs={{0,1},{1,0},{2,3},{3,2},{4,5},{5,4},{6,7},{7,6},{8,9},{9,8},{10,11... | collective-permute-start | bytes 786440 | tf_op jit(solution)/shard_map/ppermute | solution.py:85
  9.3 1.2 %collective-permute-start.11 = (bf16[2,128,512]{2,1,0:T(8,128)(2,1)S(1)}, bf16[2,128,512]{2,1,0:T(8,128)(2,1)S(1)}, u32[]{:S(2)}, u32[]{:S(2)}) collective-permute-start(bf16[2,128,512]{2,1,0:T(8,128)(2,1)S(1)} %bitcast.15), channel_id=1, source_target_pairs={{0,4},{2,6},{4,0},{6,2},{8,12},{10,14},{12,8},{14,10},{16,20},{18,... | collective-permute-start | bytes 786440 | tf_op jit(solution)/shard_map/ppermute | solution.py:78
  10.5 0.2 collective-permute-start.10
  10.7 2.9 %shard_map.59 = (bf16[2,256,1536]{2,1,0:T(8,128)(2,1)S(1)}, bf16[2,128,1024]{2,1,0:T(8,128)(2,1)S(1)}, bf16[2,128,1024]{2,1,0:T(8,128)(2,1)S(1)}) custom-call(s32[6]{0:T(128)S(1)} %stack.27.sc, bf16[2,256,512]{2,1,0:T(8,128)(2,1)S(1)} %get-tuple-element.49.refs_0_, bf16[2,256,512]{2,1,0:T(8,128)(2,1)S(1)} %get-tuple-element.50.refs_1_, ...), custom_call_target="tpu_custom_call" | custom-call | tf_op jit(solution)/shard_map/pallas_call | solution.py:48
  13.6 1.3 %collective-permute-start.5 = (bf16[2,128,1024]{2,1,0:T(8,128)(2,1)S(1)}, bf16[2,128,1024]{2,1,0:T(8,128)(2,1)S(1)}, u32[]{:S(2)}, u32[]{:S(2)}) collective-permute-start(bf16[2,128,1024]{2,1,0:T(8,128)(2,1)S(1)} %get-tuple-element.54), channel_id=1, source_target_pairs={{0,1},{1,0},{2,3},{3,2},{4,5},{5,4},{6,7},{7,6},{8,9},{9,8},{10,11... | collective-permute-start | bytes 1572872 | tf_op jit(solution)/shard_map/ppermute | solution.py:85
  14.9 1.1 %shard_map.58 = (bf16[2,128,1024]{2,1,0:T(8,128)(2,1)S(1)}, bf16[2,128,512]{2,1,0:T(8,128)(2,1)S(1)}, bf16[2,128,512]{2,1,0:T(8,128)(2,1)S(1)}, bf16[2,256,1536]{2,1,0:T(8,128)(2,1)S(1)}) custom-call(s32[6]{0:T(128)S(1)} %stack.27.sc, bf16[2,3,256,1536]{3,2,1,0:T(8,128)(2,1)S(1)} %bitcast.12, s32[1,512]{1,0:T(1,128)S(1)} %get-tuple-element.44.comp_ref.refs_6_), custom_call_target="tpu_custom_call" | custom-call | tf_op jit(solution)/shard_map/pallas_call | solution.py:48
  16.0 1.0 %collective-permute-start.6 = (bf16[2,128,512]{2,1,0:T(8,128)(2,1)S(1)}, bf16[2,128,512]{2,1,0:T(8,128)(2,1)S(1)}, u32[]{:S(2)}, u32[]{:S(2)}) collective-permute-start(bf16[2,128,512]{2,1,0:T(8,128)(2,1)S(1)} %get-tuple-element.56), channel_id=1, source_target_pairs={{0,2},{2,0},{4,6},{6,4},{8,10},{10,8},{12,14},{14,12},{16,18},{18,... | collective-permute-start | bytes 786440 | tf_op jit(solution)/shard_map/ppermute | solution.py:78
  17.1 0.9 %collective-permute-start.7 = (bf16[2,128,512]{2,1,0:T(8,128)(2,1)S(1)}, bf16[2,128,512]{2,1,0:T(8,128)(2,1)S(1)}, u32[]{:S(2)}, u32[]{:S(2)}) collective-permute-start(bf16[2,128,512]{2,1,0:T(8,128)(2,1)S(1)} %get-tuple-element.57), channel_id=1, source_target_pairs={{0,2},{2,0},{4,6},{6,4},{8,10},{10,8},{12,14},{14,12},{16,18},{18,... | collective-permute-start | bytes 786440 | tf_op jit(solution)/shard_map/ppermute | solution.py:78
  18.0 3.2 %collective-permute-done.10.rest_1_ = bf16[2,128,512]{2,1,0:T(8,128)(2,1)S(1)} collective-permute-done((bf16[2,128,512]{2,1,0:T(8,128)(2,1)S(1)}, bf16[2,128,512]{2,1,0:T(8,128)(2,1)S(1)}, u32[]{:S(2)}, u32[]{:S(2)}) %collective-permute-start.10) | collective-permute-done | bytes 262176 | tf_op jit(solution)/shard_map/ppermute | solution.py:85
  21.2 1.5 %collective-permute-start.12 = (bf16[2,128,512]{2,1,0:T(8,128)(2,1)S(1)}, bf16[2,128,512]{2,1,0:T(8,128)(2,1)S(1)}, u32[]{:S(2)}, u32[]{:S(2)}) collective-permute-start(bf16[2,128,512]{2,1,0:T(8,128)(2,1)S(1)} %collective-permute-done.9.rest_0_), channel_id=1, source_target_pairs={{0,2},{2,0},{4,6},{6,4},{8,10},{10,8},{12,14},{14,12},{16,18},{18,... | collective-permute-start | bytes 786440 | tf_op jit(solution)/shard_map/ppermute | solution.py:78
  22.7 0.6 shard_map.60.w_ref
  23.4 1.4 %shard_map.61 = (f32[2,128,1024]{2,1,0:T(8,128)S(1)}, bf16[2,128,512]{2,1,0:T(8,128)(2,1)S(1)}) custom-call(s32[6]{0:T(128)S(1)} %stack.27.sc, bf16[2,128,1024]{2,1,0:T(8,128)(2,1)S(1)} %get-tuple-element.55.keep_ref, bf16[2,128,512]{2,1,0:T(8,128)(2,1)S(1)} %collective-permute-done.6.couple_ref, bf16[2,128,512]{2,1,0:T(8,128)(2,1)S(1)} %collective-permute-done.7.slots_ref, ...), custom_call_target="tpu_custom_call" | custom-call | flops 700000000 | tf_op jit(solution)/shard_map/pallas_call | solution.py:48
  24.8 1.1 %shard_map.62 = (bf16[2,128,512]{2,1,0:T(8,128)(2,1)S(1)}, bf16[2,128,256]{2,1,0:T(8,128)(2,1)S(1)}, bf16[2,128,256]{2,1,0:T(8,128)(2,1)S(1)}) custom-call(s32[6]{0:T(128)S(1)} %stack.27.sc, f32[2,128,1024]{2,1,0:T(8,128)S(1)} %get-tuple-element.59.acc_ref, bf16[2,128,512]{2,1,0:T(8,128)(2,1)S(1)} %get-tuple-element.60.hid_ref, ...), custom_call_target="tpu_custom_call" | custom-call | tf_op jit(solution)/shard_map/pallas_call | solution.py:48
  25.9 1.8 %collective-permute-start.14 = (bf16[2,128,256]{2,1,0:T(8,128)(2,1)S(1)}, bf16[2,128,256]{2,1,0:T(8,128)(2,1)S(1)}, u32[]{:S(2)}, u32[]{:S(2)}) collective-permute-start(bf16[2,128,256]{2,1,0:T(8,128)(2,1)S(1)} %get-tuple-element.68), channel_id=1, source_target_pairs={{0,4},{2,6},{4,0},{6,2},{8,12},{10,14},{12,8},{14,10},{16,20},{18,... | collective-permute-start | bytes 393224 | tf_op jit(solution)/shard_map/ppermute | solution.py:78
  27.7 0.8 %collective-permute-start.18 = (bf16[2,128,512]{2,1,0:T(8,128)(2,1)S(1)}, bf16[2,128,512]{2,1,0:T(8,128)(2,1)S(1)}, u32[]{:S(2)}, u32[]{:S(2)}) collective-permute-start(bf16[2,128,512]{2,1,0:T(8,128)(2,1)S(1)} %bitcast.16), channel_id=1, source_target_pairs={{0,2},{2,0},{4,6},{6,4},{8,10},{10,8},{12,14},{14,12},{16,18},{18,... | collective-permute-start | bytes 786440 | tf_op jit(solution)/shard_map/ppermute | solution.py:78
  28.5 2.6 %collective-permute-done.14.x_ref = bf16[2,128,256]{2,1,0:T(8,128)(2,1)S(1)} collective-permute-done((bf16[2,128,256]{2,1,0:T(8,128)(2,1)S(1)}, bf16[2,128,256]{2,1,0:T(8,128)(2,1)S(1)}, u32[]{:S(2)}, u32[]{:S(2)}) %collective-permute-start.14) | collective-permute-done | bytes 131104 | tf_op jit(solution)/shard_map/ppermute | solution.py:78
  31.2 0.6 shard_map.63.own_ref
  31.7 1.2 %collective-permute-start.20 = (bf16[2,128,768]{2,1,0:T(8,128)(2,1)S(1)}, bf16[2,128,768]{2,1,0:T(8,128)(2,1)S(1)}, u32[]{:S(2)}, u32[]{:S(2)}) collective-permute-start(bf16[2,128,768]{2,1,0:T(8,128)(2,1)S(1)} %shard_map.63.own_ref), channel_id=1, source_target_pairs={{0,4},{2,6},{4,0},{6,2},{8,12},{10,14},{12,8},{14,10},{16,20},{18,... | collective-permute-start | bytes 1179656 | tf_op jit(solution)/shard_map/ppermute | solution.py:78
  32.9 1.2 %collective-permute-start.21 = (bf16[2,128,768]{2,1,0:T(8,128)(2,1)S(1)}, bf16[2,128,768]{2,1,0:T(8,128)(2,1)S(1)}, u32[]{:S(2)}, u32[]{:S(2)}) collective-permute-start(bf16[2,128,768]{2,1,0:T(8,128)(2,1)S(1)} %shard_map.63.own_ref), channel_id=1, source_target_pairs={{0,1},{1,0},{2,3},{3,2},{4,5},{5,4},{6,7},{7,6},{8,9},{9,8},{10,11... | collective-permute-start | bytes 1179656 | tf_op jit(solution)/shard_map/ppermute | solution.py:85
  34.2 1.9 %collective-permute-start.15 = (bf16[2,128,1024]{2,1,0:T(8,128)(2,1)S(1)}, bf16[2,128,1024]{2,1,0:T(8,128)(2,1)S(1)}, u32[]{:S(2)}, u32[]{:S(2)}) collective-permute-start(bf16[2,128,1024]{2,1,0:T(8,128)(2,1)S(1)} %collective-permute-done.5.rest_4_.refs_0_), channel_id=1, source_target_pairs={{0,2},{2,0},{4,6},{6,4},{8,10},{10,8},{12,14},{14,12},{16,18},{18,... | collective-permute-start | bytes 1572872 | tf_op jit(solution)/shard_map/ppermute | solution.py:78
  36.1 0.2 collective-permute-start.16
  36.3 1.7 %collective-permute-done.19.refs_3_ = bf16[2,128,512]{2,1,0:T(8,128)(2,1)S(1)} collective-permute-done((bf16[2,128,512]{2,1,0:T(8,128)(2,1)S(1)}, bf16[2,128,512]{2,1,0:T(8,128)(2,1)S(1)}, u32[]{:S(2)}, u32[]{:S(2)}) %collective-permute-start.19) | collective-permute-done | bytes 262176 | tf_op jit(solution)/shard_map/ppermute | solution.py:78
  38.0 0.7 %shard_map.65.refs_6_ = bf16[2,512,512]{2,1,0:T(8,128)(2,1)S(1)} custom-call(s32[6]{0:T(128)S(1)} %stack.27.sc, bf16[2,128,512]{2,1,0:T(8,128)(2,1)S(1)} %bitcast.17, bf16[2,128,512]{2,1,0:T(8,128)(2,1)S(1)} %collective-permute-done.11.refs_1_, bf16[2,128,512]{2,1,0:T(8,128)(2,1)S(1)} %collective-permute-done.18.refs_2_, ...), custom_call_target="tpu_custom_call" | custom-call | tf_op jit(solution)/shard_map/pallas_call | solution.py:48
  38.7 2.7 %collective-permute-done.20.x_ref = bf16[2,128,768]{2,1,0:T(8,128)(2,1)S(1)} collective-permute-done((bf16[2,128,768]{2,1,0:T(8,128)(2,1)S(1)}, bf16[2,128,768]{2,1,0:T(8,128)(2,1)S(1)}, u32[]{:S(2)}, u32[]{:S(2)}) %collective-permute-start.20) | collective-permute-done | bytes 393248 | tf_op jit(solution)/shard_map/ppermute | solution.py:78
  41.4 0.6 shard_map.67.refs_0_
  42.0 0.9 %collective-permute-start.22 = (bf16[2,128,768]{2,1,0:T(8,128)(2,1)S(1)}, bf16[2,128,768]{2,1,0:T(8,128)(2,1)S(1)}, u32[]{:S(2)}, u32[]{:S(2)}) collective-permute-start(bf16[2,128,768]{2,1,0:T(8,128)(2,1)S(1)} %collective-permute-done.21.own_ref), channel_id=1, source_target_pairs={{0,4},{2,6},{4,0},{6,2},{8,12},{10,14},{12,8},{14,10},{16,20},{18,... | collective-permute-start | bytes 1179656 | tf_op jit(solution)/shard_map/ppermute | solution.py:78
  42.9 4.0 %collective-permute-start.23 = (bf16[2,128,1536]{2,1,0:T(8,128)(2,1)S(1)}, bf16[2,128,1536]{2,1,0:T(8,128)(2,1)S(1)}, u32[]{:S(2)}, u32[]{:S(2)}) collective-permute-start(bf16[2,128,1536]{2,1,0:T(8,128)(2,1)S(1)} %shard_map.67.refs_0_), channel_id=1, source_target_pairs={{0,2},{2,0},{4,6},{6,4},{8,10},{10,8},{12,14},{14,12},{16,18},{18,... | collective-permute-start | bytes 2359304 | tf_op jit(solution)/shard_map/ppermute | solution.py:78
  46.9 4.2 %shard_map.64.refs_5_ = bf16[2,512,1536]{2,1,0:T(8,128)(2,1)S(1)} custom-call(s32[6]{0:T(128)S(1)} %stack.27.sc, bf16[2,512,512]{2,1,0:T(8,128)(2,1)S(1)} %shard_map.60.w_ref, bf16[2,256,512]{2,1,0:T(8,128)(2,1)S(1)} %get-tuple-element.45.end_ref.refs_8_.own_ref, bf16[2,256,512]{2,1,0:T(8,128)(2,1)S(1)} %collective-permute-done.4.refs_9_.endsib_ref.sib_ref, ...), custom_call_target="tpu_custom_call" | custom-call | flops 800000000 | tf_op jit(solution)/shard_map/pallas_call | solution.py:48
  51.1 2.0 %collective-permute-done.16.refs_2_ = bf16[2,128,1024]{2,1,0:T(8,128)(2,1)S(1)} collective-permute-done((bf16[2,128,1024]{2,1,0:T(8,128)(2,1)S(1)}, bf16[2,128,1024]{2,1,0:T(8,128)(2,1)S(1)}, u32[]{:S(2)}, u32[]{:S(2)}) %collective-permute-start.16) | collective-permute-done | bytes 524320 | tf_op jit(solution)/shard_map/ppermute | solution.py:85
  53.1 2.6 %collective-permute-start.17 = (bf16[2,128,1024]{2,1,0:T(8,128)(2,1)S(1)}, bf16[2,128,1024]{2,1,0:T(8,128)(2,1)S(1)}, u32[]{:S(2)}, u32[]{:S(2)}) collective-permute-start(bf16[2,128,1024]{2,1,0:T(8,128)(2,1)S(1)} %collective-permute-done.16.refs_2_), channel_id=1, source_target_pairs={{0,2},{2,0},{4,6},{6,4},{8,10},{10,8},{12,14},{14,12},{16,18},{18,... | collective-permute-start | bytes 1572872 | tf_op jit(solution)/shard_map/ppermute | solution.py:78
  55.7 0.6 %shard_map.68 = (bf16[2,128,768]{2,1,0:T(8,128)(2,1)S(1)}, bf16[2,128,768]{2,1,0:T(8,128)(2,1)S(1)}) custom-call(s32[6]{0:T(128)S(1)} %stack.27.sc, bf16[2,128,768]{2,1,0:T(8,128)(2,1)S(1)} %collective-permute-done.21.own_ref, bf16[2,128,768]{2,1,0:T(8,128)(2,1)S(1)} %collective-permute-done.22.x_ref), custom_call_target="tpu_custom_call" | custom-call | tf_op jit(solution)/shard_map/pallas_call | solution.py:48
  56.4 0.1 collective-permute-start.24
  56.4 0.5 collective-permute-start.25
  56.9 0.3 collective-permute-done.17.refs_3_
  57.2 3.4 %shard_map.66 = (bf16[2,512,512]{2,1,0:T(8,128)(2,1)S(1)}, bf16[512,512]{1,0:T(8,128)(2,1)S(1)}, bf16[512,512]{1,0:T(8,128)(2,1)S(1)}) custom-call(s32[6]{0:T(128)S(1)} %stack.27.sc, bf16[2,256,1536]{2,1,0:T(8,128)(2,1)S(1)} %get-tuple-element.48.end_ref, bf16[2,256,1536]{2,1,0:T(8,128)(2,1)S(1)} %get-tuple-element.53.kept_ref, ...), custom_call_target="tpu_custom_call" | custom-call | flops 300000000 | tf_op jit(solution)/shard_map/pallas_call | solution.py:48
  60.7 3.4 %shard_map.69 = bf16[2,1,256,1536]{3,2,1,0:T(8,128)(2,1)} custom-call(s32[6]{0:T(128)S(1)} %stack.27.sc, bf16[2,512,512]{2,1,0:T(8,128)(2,1)S(1)} %get-tuple-element.73.hid_ref, bf16[512,512]{1,0:T(8,128)(2,1)S(1)} %get-tuple-element.74.first_ref, bf16[512,512]{1,0:T(8,128)(2,1)S(1)} %get-tuple-element.75.slots_ref, ...), custom_call_target="tpu_custom_call" | custom-call | tf_op jit(solution)/shard_map/pallas_call | solution.py:48
  (32 shorter events, 0.1 us)
Async XLA Ops:
  0.1 2.3 %copy-start = (bf16[2,1,1,3,256,1536]{5,4,3,2,1,0:T(8,128)(2,1)S(1)}, bf16[2,1,1,3,256,1536]{5,4,3,2,1,0:T(8,128)(2,1)}, u32[]{:S(2)}) copy-start(bf16[2,1,1,3,256,1536]{5,4,3,2,1,0:T(8,128)(2,1)} %param.5) | copy-start | bytes 14155780
  2.4 1.9 %copy-start.4 = (s32[1,8,512]{2,1,0:T(8,128)S(1)}, s32[1,8,512]{2,1,0:T(8,128)}, u32[]{:S(2)}) copy-start(s32[1,8,512]{2,1,0:T(8,128)} %param.8) | copy-start | bytes 49156
  2.4 1.9 %copy-start.5 = (s32[1,4,512]{2,1,0:T(4,128)S(1)}, s32[1,4,512]{2,1,0:T(4,128)}, u32[]{:S(2)}) copy-start(s32[1,4,512]{2,1,0:T(4,128)} %param.9) | copy-start | bytes 24580
  3.1 3.3 %copy-start.2 = (bf16[2,1,256,512]{3,2,1,0:T(8,128)(2,1)S(1)}, bf16[2,1,256,512]{3,2,1,0:T(8,128)(2,1)}, u32[]{:S(2)}) copy-start(bf16[2,1,256,512]{3,2,1,0:T(8,128)(2,1)} %param.6) | copy-start | bytes 1572868
  3.2 6.1 %copy-start.3 = (bf16[2,1,128,512]{3,2,1,0:T(8,128)(2,1)S(1)}, bf16[2,1,128,512]{3,2,1,0:T(8,128)(2,1)}, u32[]{:S(2)}) copy-start(bf16[2,1,128,512]{3,2,1,0:T(8,128)(2,1)} %param.7) | copy-start | bytes 786436
  3.2 2.0 %collective-permute-start = (bf16[2,256,512]{2,1,0:T(8,128)(2,1)S(1)}, bf16[2,256,512]{2,1,0:T(8,128)(2,1)S(1)}, u32[]{:S(2)}, u32[]{:S(2)}) collective-permute-start(bf16[2,256,512]{2,1,0:T(8,128)(2,1)S(1)} %get-tuple-element.43.own_ref), channel_id=1, source_target_pairs={{0,2},{2,0},{4,6},{6,4},{8,10},{10,8},{12,14},{14,12},{16,18},{18,... | collective-permute-start | bytes 1572872 | tf_op jit(solution)/shard_map/ppermute | solution.py:78
  3.3 3.7 %collective-permute-start.1 = (bf16[2,256,512]{2,1,0:T(8,128)(2,1)S(1)}, bf16[2,256,512]{2,1,0:T(8,128)(2,1)S(1)}, u32[]{:S(2)}, u32[]{:S(2)}) collective-permute-start(bf16[2,256,512]{2,1,0:T(8,128)(2,1)S(1)} %get-tuple-element.49.refs_0_), channel_id=1, source_target_pairs={{0,2},{2,0},{4,6},{6,4},{8,10},{10,8},{12,14},{14,12},{16,18},{18,... | collective-permute-start | bytes 1572872 | tf_op jit(solution)/shard_map/ppermute | solution.py:78
  3.7 5.5 %collective-permute-start.2 = (bf16[2,256,512]{2,1,0:T(8,128)(2,1)S(1)}, bf16[2,256,512]{2,1,0:T(8,128)(2,1)S(1)}, u32[]{:S(2)}, u32[]{:S(2)}) collective-permute-start(bf16[2,256,512]{2,1,0:T(8,128)(2,1)S(1)} %get-tuple-element.50.refs_1_), channel_id=1, source_target_pairs={{0,2},{2,0},{4,6},{6,4},{8,10},{10,8},{12,14},{14,12},{16,18},{18,... | collective-permute-start | bytes 1572872 | tf_op jit(solution)/shard_map/ppermute | solution.py:78
  3.8 6.7 %collective-permute-start.3 = (bf16[2,256,512]{2,1,0:T(8,128)(2,1)S(1)}, bf16[2,256,512]{2,1,0:T(8,128)(2,1)S(1)}, u32[]{:S(2)}, u32[]{:S(2)}) collective-permute-start(bf16[2,256,512]{2,1,0:T(8,128)(2,1)S(1)} %get-tuple-element.51.refs_2_), channel_id=1, source_target_pairs={{0,2},{2,0},{4,6},{6,4},{8,10},{10,8},{12,14},{14,12},{16,18},{18,... | collective-permute-start | bytes 1572872 | tf_op jit(solution)/shard_map/ppermute | solution.py:78
  4.3 6.5 %collective-permute-start.4 = (bf16[2,256,512]{2,1,0:T(8,128)(2,1)S(1)}, bf16[2,256,512]{2,1,0:T(8,128)(2,1)S(1)}, u32[]{:S(2)}, u32[]{:S(2)}) collective-permute-start(bf16[2,256,512]{2,1,0:T(8,128)(2,1)S(1)} %get-tuple-element.45.end_ref.refs_8_.own_ref), channel_id=1, source_target_pairs={{0,2},{2,0},{4,6},{6,4},{8,10},{10,8},{12,14},{14,12},{16,18},{18,... | collective-permute-start | bytes 1572872 | tf_op jit(solution)/shard_map/ppermute | solution.py:78
  5.2 9.8 %copy-start.1 = (bf16[2,1,1,3,256,1536]{5,4,3,2,1,0:T(8,128)(2,1)S(1)}, bf16[2,1,1,3,256,1536]{5,4,3,2,1,0:T(8,128)(2,1)}, u32[]{:S(2)}) copy-start(bf16[2,1,1,3,256,1536]{5,4,3,2,1,0:T(8,128)(2,1)} %param.5) | copy-start | bytes 14155780
  6.4 16.2 %collective-permute-start.8 = (bf16[2,256,512]{2,1,0:T(8,128)(2,1)S(1)}, bf16[2,256,512]{2,1,0:T(8,128)(2,1)S(1)}, u32[]{:S(2)}, u32[]{:S(2)}) collective-permute-start(bf16[2,256,512]{2,1,0:T(8,128)(2,1)S(1)} %bitcast.13), channel_id=1, source_target_pairs={{0,2},{2,0},{4,6},{6,4},{8,10},{10,8},{12,14},{14,12},{16,18},{18,... | collective-permute-start | bytes 1572872 | tf_op jit(solution)/shard_map/ppermute | solution.py:78
  6.9 9.1 %collective-permute-start.9 = (bf16[2,128,512]{2,1,0:T(8,128)(2,1)S(1)}, bf16[2,128,512]{2,1,0:T(8,128)(2,1)S(1)}, u32[]{:S(2)}, u32[]{:S(2)}) collective-permute-start(bf16[2,128,512]{2,1,0:T(8,128)(2,1)S(1)} %get-tuple-element.61), channel_id=1, source_target_pairs={{0,1},{1,0},{2,3},{3,2},{4,5},{5,4},{6,7},{7,6},{8,9},{9,8},{10,11... | collective-permute-start | bytes 786440 | tf_op jit(solution)/shard_map/ppermute | solution.py:85
  9.3 7.8 %collective-permute-start.11 = (bf16[2,128,512]{2,1,0:T(8,128)(2,1)S(1)}, bf16[2,128,512]{2,1,0:T(8,128)(2,1)S(1)}, u32[]{:S(2)}, u32[]{:S(2)}) collective-permute-start(bf16[2,128,512]{2,1,0:T(8,128)(2,1)S(1)} %bitcast.15), channel_id=1, source_target_pairs={{0,4},{2,6},{4,0},{6,2},{8,12},{10,14},{12,8},{14,10},{16,20},{18,... | collective-permute-start | bytes 786440 | tf_op jit(solution)/shard_map/ppermute | solution.py:78
  10.5 10.7 %collective-permute-start.10 = (bf16[2,128,512]{2,1,0:T(8,128)(2,1)S(1)}, bf16[2,128,512]{2,1,0:T(8,128)(2,1)S(1)}, u32[]{:S(2)}, u32[]{:S(2)}) collective-permute-start(bf16[2,128,512]{2,1,0:T(8,128)(2,1)S(1)} %get-tuple-element.62), channel_id=1, source_target_pairs={{0,1},{1,0},{2,3},{3,2},{4,5},{5,4},{6,7},{7,6},{8,9},{9,8},{10,11... | collective-permute-start | bytes 786440 | tf_op jit(solution)/shard_map/ppermute | solution.py:85
  13.6 20.6 %collective-permute-start.5 = (bf16[2,128,1024]{2,1,0:T(8,128)(2,1)S(1)}, bf16[2,128,1024]{2,1,0:T(8,128)(2,1)S(1)}, u32[]{:S(2)}, u32[]{:S(2)}) collective-permute-start(bf16[2,128,1024]{2,1,0:T(8,128)(2,1)S(1)} %get-tuple-element.54), channel_id=1, source_target_pairs={{0,1},{1,0},{2,3},{3,2},{4,5},{5,4},{6,7},{7,6},{8,9},{9,8},{10,11... | collective-permute-start | bytes 1572872 | tf_op jit(solution)/shard_map/ppermute | solution.py:85
  16.0 7.3 %collective-permute-start.6 = (bf16[2,128,512]{2,1,0:T(8,128)(2,1)S(1)}, bf16[2,128,512]{2,1,0:T(8,128)(2,1)S(1)}, u32[]{:S(2)}, u32[]{:S(2)}) collective-permute-start(bf16[2,128,512]{2,1,0:T(8,128)(2,1)S(1)} %get-tuple-element.56), channel_id=1, source_target_pairs={{0,2},{2,0},{4,6},{6,4},{8,10},{10,8},{12,14},{14,12},{16,18},{18,... | collective-permute-start | bytes 786440 | tf_op jit(solution)/shard_map/ppermute | solution.py:78
  17.1 6.3 %collective-permute-start.7 = (bf16[2,128,512]{2,1,0:T(8,128)(2,1)S(1)}, bf16[2,128,512]{2,1,0:T(8,128)(2,1)S(1)}, u32[]{:S(2)}, u32[]{:S(2)}) collective-permute-start(bf16[2,128,512]{2,1,0:T(8,128)(2,1)S(1)} %get-tuple-element.57), channel_id=1, source_target_pairs={{0,2},{2,0},{4,6},{6,4},{8,10},{10,8},{12,14},{14,12},{16,18},{18,... | collective-permute-start | bytes 786440 | tf_op jit(solution)/shard_map/ppermute | solution.py:78
  21.2 3.5 %collective-permute-start.12 = (bf16[2,128,512]{2,1,0:T(8,128)(2,1)S(1)}, bf16[2,128,512]{2,1,0:T(8,128)(2,1)S(1)}, u32[]{:S(2)}, u32[]{:S(2)}) collective-permute-start(bf16[2,128,512]{2,1,0:T(8,128)(2,1)S(1)} %collective-permute-done.9.rest_0_), channel_id=1, source_target_pairs={{0,2},{2,0},{4,6},{6,4},{8,10},{10,8},{12,14},{14,12},{16,18},{18,... | collective-permute-start | bytes 786440 | tf_op jit(solution)/shard_map/ppermute | solution.py:78
  22.7 2.1 %collective-permute-start.13 = (bf16[2,128,512]{2,1,0:T(8,128)(2,1)S(1)}, bf16[2,128,512]{2,1,0:T(8,128)(2,1)S(1)}, u32[]{:S(2)}, u32[]{:S(2)}) collective-permute-start(bf16[2,128,512]{2,1,0:T(8,128)(2,1)S(1)} %collective-permute-done.10.rest_1_), channel_id=1, source_target_pairs={{0,2},{2,0},{4,6},{6,4},{8,10},{10,8},{12,14},{14,12},{16,18},{18,... | collective-permute-start | bytes 786440 | tf_op jit(solution)/shard_map/ppermute | solution.py:78
  25.9 5.2 %collective-permute-start.14 = (bf16[2,128,256]{2,1,0:T(8,128)(2,1)S(1)}, bf16[2,128,256]{2,1,0:T(8,128)(2,1)S(1)}, u32[]{:S(2)}, u32[]{:S(2)}) collective-permute-start(bf16[2,128,256]{2,1,0:T(8,128)(2,1)S(1)} %get-tuple-element.68), channel_id=1, source_target_pairs={{0,4},{2,6},{4,0},{6,2},{8,12},{10,14},{12,8},{14,10},{16,20},{18,... | collective-permute-start | bytes 393224 | tf_op jit(solution)/shard_map/ppermute | solution.py:78
  27.7 8.4 %collective-permute-start.18 = (bf16[2,128,512]{2,1,0:T(8,128)(2,1)S(1)}, bf16[2,128,512]{2,1,0:T(8,128)(2,1)S(1)}, u32[]{:S(2)}, u32[]{:S(2)}) collective-permute-start(bf16[2,128,512]{2,1,0:T(8,128)(2,1)S(1)} %bitcast.16), channel_id=1, source_target_pairs={{0,2},{2,0},{4,6},{6,4},{8,10},{10,8},{12,14},{14,12},{16,18},{18,... | collective-permute-start | bytes 786440 | tf_op jit(solution)/shard_map/ppermute | solution.py:78
  31.7 9.6 %collective-permute-start.20 = (bf16[2,128,768]{2,1,0:T(8,128)(2,1)S(1)}, bf16[2,128,768]{2,1,0:T(8,128)(2,1)S(1)}, u32[]{:S(2)}, u32[]{:S(2)}) collective-permute-start(bf16[2,128,768]{2,1,0:T(8,128)(2,1)S(1)} %shard_map.63.own_ref), channel_id=1, source_target_pairs={{0,4},{2,6},{4,0},{6,2},{8,12},{10,14},{12,8},{14,10},{16,20},{18,... | collective-permute-start | bytes 1179656 | tf_op jit(solution)/shard_map/ppermute | solution.py:78
  32.9 9.0 %collective-permute-start.21 = (bf16[2,128,768]{2,1,0:T(8,128)(2,1)S(1)}, bf16[2,128,768]{2,1,0:T(8,128)(2,1)S(1)}, u32[]{:S(2)}, u32[]{:S(2)}) collective-permute-start(bf16[2,128,768]{2,1,0:T(8,128)(2,1)S(1)} %shard_map.63.own_ref), channel_id=1, source_target_pairs={{0,1},{1,0},{2,3},{3,2},{4,5},{5,4},{6,7},{7,6},{8,9},{9,8},{10,11... | collective-permute-start | bytes 1179656 | tf_op jit(solution)/shard_map/ppermute | solution.py:85
  34.2 12.7 %collective-permute-start.15 = (bf16[2,128,1024]{2,1,0:T(8,128)(2,1)S(1)}, bf16[2,128,1024]{2,1,0:T(8,128)(2,1)S(1)}, u32[]{:S(2)}, u32[]{:S(2)}) collective-permute-start(bf16[2,128,1024]{2,1,0:T(8,128)(2,1)S(1)} %collective-permute-done.5.rest_4_.refs_0_), channel_id=1, source_target_pairs={{0,2},{2,0},{4,6},{6,4},{8,10},{10,8},{12,14},{14,12},{16,18},{18,... | collective-permute-start | bytes 1572872 | tf_op jit(solution)/shard_map/ppermute | solution.py:78
  36.1 1.9 %collective-permute-start.19 = (bf16[2,128,512]{2,1,0:T(8,128)(2,1)S(1)}, bf16[2,128,512]{2,1,0:T(8,128)(2,1)S(1)}, u32[]{:S(2)}, u32[]{:S(2)}) collective-permute-start(bf16[2,128,512]{2,1,0:T(8,128)(2,1)S(1)} %collective-permute-done.11.refs_1_), channel_id=1, source_target_pairs={{0,2},{2,0},{4,6},{6,4},{8,10},{10,8},{12,14},{14,12},{16,18},{18,... | collective-permute-start | bytes 786440 | tf_op jit(solution)/shard_map/ppermute | solution.py:78
  36.1 17.0 %collective-permute-start.16 = (bf16[2,128,1024]{2,1,0:T(8,128)(2,1)S(1)}, bf16[2,128,1024]{2,1,0:T(8,128)(2,1)S(1)}, u32[]{:S(2)}, u32[]{:S(2)}) collective-permute-start(bf16[2,128,1024]{2,1,0:T(8,128)(2,1)S(1)} %get-tuple-element.71), channel_id=1, source_target_pairs={{0,1},{1,0},{2,3},{3,2},{4,5},{5,4},{6,7},{7,6},{8,9},{9,8},{10,11... | collective-permute-start | bytes 1572872 | tf_op jit(solution)/shard_map/ppermute | solution.py:85
  42.0 13.7 %collective-permute-start.22 = (bf16[2,128,768]{2,1,0:T(8,128)(2,1)S(1)}, bf16[2,128,768]{2,1,0:T(8,128)(2,1)S(1)}, u32[]{:S(2)}, u32[]{:S(2)}) collective-permute-start(bf16[2,128,768]{2,1,0:T(8,128)(2,1)S(1)} %collective-permute-done.21.own_ref), channel_id=1, source_target_pairs={{0,4},{2,6},{4,0},{6,2},{8,12},{10,14},{12,8},{14,10},{16,20},{18,... | collective-permute-start | bytes 1179656 | tf_op jit(solution)/shard_map/ppermute | solution.py:78
  42.9 17.8 %collective-permute-start.23 = (bf16[2,128,1536]{2,1,0:T(8,128)(2,1)S(1)}, bf16[2,128,1536]{2,1,0:T(8,128)(2,1)S(1)}, u32[]{:S(2)}, u32[]{:S(2)}) collective-permute-start(bf16[2,128,1536]{2,1,0:T(8,128)(2,1)S(1)} %shard_map.67.refs_0_), channel_id=1, source_target_pairs={{0,2},{2,0},{4,6},{6,4},{8,10},{10,8},{12,14},{14,12},{16,18},{18,... | collective-permute-start | bytes 2359304 | tf_op jit(solution)/shard_map/ppermute | solution.py:78
  53.1 4.1 %collective-permute-start.17 = (bf16[2,128,1024]{2,1,0:T(8,128)(2,1)S(1)}, bf16[2,128,1024]{2,1,0:T(8,128)(2,1)S(1)}, u32[]{:S(2)}, u32[]{:S(2)}) collective-permute-start(bf16[2,128,1024]{2,1,0:T(8,128)(2,1)S(1)} %collective-permute-done.16.refs_2_), channel_id=1, source_target_pairs={{0,2},{2,0},{4,6},{6,4},{8,10},{10,8},{12,14},{14,12},{16,18},{18,... | collective-permute-start | bytes 1572872 | tf_op jit(solution)/shard_map/ppermute | solution.py:78
  56.4 4.3 %collective-permute-start.24 = (bf16[2,128,768]{2,1,0:T(8,128)(2,1)S(1)}, bf16[2,128,768]{2,1,0:T(8,128)(2,1)S(1)}, u32[]{:S(2)}, u32[]{:S(2)}) collective-permute-start(bf16[2,128,768]{2,1,0:T(8,128)(2,1)S(1)} %get-tuple-element.79.refs_1_), channel_id=1, source_target_pairs={{0,2},{2,0},{4,6},{6,4},{8,10},{10,8},{12,14},{14,12},{16,18},{18,... | collective-permute-start | bytes 1179656 | tf_op jit(solution)/shard_map/ppermute | solution.py:78
  56.4 4.2 %collective-permute-start.25 = (bf16[2,128,768]{2,1,0:T(8,128)(2,1)S(1)}, bf16[2,128,768]{2,1,0:T(8,128)(2,1)S(1)}, u32[]{:S(2)}, u32[]{:S(2)}) collective-permute-start(bf16[2,128,768]{2,1,0:T(8,128)(2,1)S(1)} %get-tuple-element.80.refs_2_), channel_id=1, source_target_pairs={{0,2},{2,0},{4,6},{6,4},{8,10},{10,8},{12,14},{14,12},{16,18},{18,... | collective-permute-start | bytes 1179656 | tf_op jit(solution)/shard_map/ppermute | solution.py:78

commit v16 on v15

--- a/solution.py
+++ b/solution.py
@@ -13,7 +13,7 @@
 JOIN_COST = 300000000
 SLOTS_COST = 0
 OWN_COST = 700_000_000
-SOLVED_COST = 800_000_000
+SOLVED_COST = 500_000_000
 KEEP_COST = 300_000_000
 
 

time: 64.6 us -> 63.8 us (0.988)
  waiting for transfers between devices: 12.5 us -> 11.5 us
    ppermute x5, waiting for transfers between devices: 5.23 us -> 4.33 us  [face_permute(): return lax.ppermute(array, ('box', 'face'), pairs)]
    ppermute x5, starting transfers between devices: 5.31 us -> 6.07 us  [face_permute(): return lax.ppermute(array, ('box', 'face'), pairs)]
  transfers between devices with their start and end apart: 26 -> 26, of which waited for: 6 -> 7; matrix products, arithmetic and copies ran while one was open for 0% -> 0% of each run, Pallas kernels for 30% -> 30%
where the time goes in v16:
time: 63.8 us; the launch traced here: 63.4 us
  starting transfers between devices  25.6 us (40%)
  Pallas kernels  23.4 us (37%)
  waiting for transfers between devices  11.5 us (18%)
  local copies, waits for them, and re-layouts  2.45 us (4%)
    pallas_call x15, Pallas kernels, call(): pl.pallas_call(kernel, in_specs=[pl.BlockSpec(memory_space=pltpu.SMEM)] +...  23.4 us
    ppermute x21, starting transfers between devices, box_permute(): return lax.ppermute(array, 'box', [(b, b ^ mask) for b in range(n_box)])  19.5 us
    ppermute x21, waiting for transfers between devices, box_permute(): return lax.ppermute(array, 'box', [(b, b ^ mask) for b in range(n_box)])  7.19 us
    ppermute x5, starting transfers between devices, face_permute(): return lax.ppermute(array, ('box', 'face'), pairs)  6.07 us
    ppermute x5, waiting for transfers between devices, face_permute(): return lax.ppermute(array, ('box', 'face'), pairs)  4.33 us
    unnamed x12, local copies, waits for them, and re-layouts  2.36 us
  transfers between devices with their start and end apart: 26, of which 7 were waited for; matrix products, arithmetic and copies ran while one was open for 0% of the time, Pallas kernels for 30%

profile of v16, /device:TPU:1, one launch (start us, length us, event | category | flops | bytes accessed | tf_op | source)
XLA Modules:
  0.0 63.4 jit_solution(11339093234253187989)
XLA Ops:
  0.0 0.1 stack.27.sc
  0.1 2.3 %copy-done = bf16[2,1,1,3,256,1536]{5,4,3,2,1,0:T(8,128)(2,1)S(1)} copy-done((bf16[2,1,1,3,256,1536]{5,4,3,2,1,0:T(8,128)(2,1)S(1)}, bf16[2,1,1,3,256,1536]{5,4,3,2,1,0:T(8,128)(2,1)}, u32[]{:S(2)}) %copy-start) | copy-done | bytes 4718616
  2.4 0.7 %shard_map.55 = (bf16[2,256,512]{2,1,0:T(8,128)(2,1)S(1)}, bf16[2,256,512]{2,1,0:T(8,128)(2,1)S(1)}, bf16[2,256,512]{2,1,0:T(8,128)(2,1)S(1)}, bf16[2,256,512]{2,1,0:T(8,128)(2,1)S(1)}, bf16[2,256,512]{2,1,0:T(8,128)(2,1)S(1)}) custom-call(s32[6]{0:T(128)S(1)} %stack.27.sc, bf16[2,3,256,1536]{3,2,1,0:T(8,128)(2,1)S(1)} %bitcast.11), custom_call_target="tpu_custom_call" | custom-call | tf_op jit(solution)/shard_map/pallas_call | solution.py:48
  3.2 0.1 collective-permute-start
  3.3 0.5 collective-permute-start.1
  3.7 0.1 collective-permute-start.2
  3.8 0.4 collective-permute-start.3
  4.3 0.1 collective-permute-start.4
  4.3 0.8 %shard_map.56 = (s32[1,512]{1,0:T(1,128)S(1)}, s32[512,1]{1,0:T(8,128)S(1)}) custom-call(s32[6]{0:T(128)S(1)} %stack.27.sc, s32[8,512]{1,0:T(8,128)S(1)} %bitcast.18, s32[4,512]{1,0:T(4,128)S(1)} %bitcast.19), custom_call_target="tpu_custom_call" | custom-call | tf_op jit(solution)/shard_map/pallas_call | solution.py:48
  5.2 1.3 %shard_map.57 = (bf16[2,256,512]{2,1,0:T(8,128)(2,1)S(1)}, bf16[2,128,512]{2,1,0:T(8,128)(2,1)S(1)}, bf16[2,128,512]{2,1,0:T(8,128)(2,1)S(1)}) custom-call(s32[6]{0:T(128)S(1)} %stack.27.sc, bf16[2,256,512]{2,1,0:T(8,128)(2,1)S(1)} %get-tuple-element.43.own_ref, bf16[2,256,512]{2,1,0:T(8,128)(2,1)S(1)} %collective-permute-done.sib_ref, ...), custom_call_target="tpu_custom_call" | custom-call | tf_op jit(solution)/shard_map/pallas_call | solution.py:48
  6.4 0.5 collective-permute-start.8
  6.9 2.3 %collective-permute-start.9 = (bf16[2,128,512]{2,1,0:T(8,128)(2,1)S(1)}, bf16[2,128,512]{2,1,0:T(8,128)(2,1)S(1)}, u32[]{:S(2)}, u32[]{:S(2)}) collective-permute-start(bf16[2,128,512]{2,1,0:T(8,128)(2,1)S(1)} %get-tuple-element.61), channel_id=1, source_target_pairs={{0,1},{1,0},{2,3},{3,2},{4,5},{5,4},{6,7},{7,6},{8,9},{9,8},{10,11... | collective-permute-start | bytes 786440 | tf_op jit(solution)/shard_map/ppermute | solution.py:85
  9.3 1.2 %collective-permute-start.11 = (bf16[2,128,512]{2,1,0:T(8,128)(2,1)S(1)}, bf16[2,128,512]{2,1,0:T(8,128)(2,1)S(1)}, u32[]{:S(2)}, u32[]{:S(2)}) collective-permute-start(bf16[2,128,512]{2,1,0:T(8,128)(2,1)S(1)} %bitcast.15), channel_id=1, source_target_pairs={{0,4},{2,6},{4,0},{6,2},{8,12},{10,14},{12,8},{14,10},{16,20},{18,... | collective-permute-start | bytes 786440 | tf_op jit(solution)/shard_map/ppermute | solution.py:78
  10.5 0.2 collective-permute-start.10
  10.7 1.1 %shard_map.58 = (bf16[2,128,1024]{2,1,0:T(8,128)(2,1)S(1)}, bf16[2,128,512]{2,1,0:T(8,128)(2,1)S(1)}, bf16[2,128,512]{2,1,0:T(8,128)(2,1)S(1)}, bf16[2,256,1536]{2,1,0:T(8,128)(2,1)S(1)}) custom-call(s32[6]{0:T(128)S(1)} %stack.27.sc, bf16[2,3,256,1536]{3,2,1,0:T(8,128)(2,1)S(1)} %bitcast.12, s32[1,512]{1,0:T(1,128)S(1)} %get-tuple-element.44.comp_ref.refs_6_), custom_call_target="tpu_custom_call" | custom-call | tf_op jit(solution)/shard_map/pallas_call | solution.py:48
  11.8 1.3 %collective-permute-start.6 = (bf16[2,128,512]{2,1,0:T(8,128)(2,1)S(1)}, bf16[2,128,512]{2,1,0:T(8,128)(2,1)S(1)}, u32[]{:S(2)}, u32[]{:S(2)}) collective-permute-start(bf16[2,128,512]{2,1,0:T(8,128)(2,1)S(1)} %get-tuple-element.56), channel_id=1, source_target_pairs={{0,2},{2,0},{4,6},{6,4},{8,10},{10,8},{12,14},{14,12},{16,18},{18,... | collective-permute-start | bytes 786440 | tf_op jit(solution)/shard_map/ppermute | solution.py:78
  13.2 2.4 %collective-permute-done.9.rest_0_ = bf16[2,128,512]{2,1,0:T(8,128)(2,1)S(1)} collective-permute-done((bf16[2,128,512]{2,1,0:T(8,128)(2,1)S(1)}, bf16[2,128,512]{2,1,0:T(8,128)(2,1)S(1)}, u32[]{:S(2)}, u32[]{:S(2)}) %collective-permute-start.9) | collective-permute-done | bytes 262176 | tf_op jit(solution)/shard_map/ppermute | solution.py:85
  15.6 1.5 %collective-permute-start.7 = (bf16[2,128,512]{2,1,0:T(8,128)(2,1)S(1)}, bf16[2,128,512]{2,1,0:T(8,128)(2,1)S(1)}, u32[]{:S(2)}, u32[]{:S(2)}) collective-permute-start(bf16[2,128,512]{2,1,0:T(8,128)(2,1)S(1)} %get-tuple-element.57), channel_id=1, source_target_pairs={{0,2},{2,0},{4,6},{6,4},{8,10},{10,8},{12,14},{14,12},{16,18},{18,... | collective-permute-start | bytes 786440 | tf_op jit(solution)/shard_map/ppermute | solution.py:78
  17.1 2.9 %shard_map.59 = (bf16[2,256,1536]{2,1,0:T(8,128)(2,1)S(1)}, bf16[2,128,1024]{2,1,0:T(8,128)(2,1)S(1)}, bf16[2,128,1024]{2,1,0:T(8,128)(2,1)S(1)}) custom-call(s32[6]{0:T(128)S(1)} %stack.27.sc, bf16[2,256,512]{2,1,0:T(8,128)(2,1)S(1)} %get-tuple-element.49.refs_0_, bf16[2,256,512]{2,1,0:T(8,128)(2,1)S(1)} %get-tuple-element.50.refs_1_, ...), custom_call_target="tpu_custom_call" | custom-call | tf_op jit(solution)/shard_map/pallas_call | solution.py:48
  19.9 1.9 %collective-permute-start.5 = (bf16[2,128,1024]{2,1,0:T(8,128)(2,1)S(1)}, bf16[2,128,1024]{2,1,0:T(8,128)(2,1)S(1)}, u32[]{:S(2)}, u32[]{:S(2)}) collective-permute-start(bf16[2,128,1024]{2,1,0:T(8,128)(2,1)S(1)} %get-tuple-element.54), channel_id=1, source_target_pairs={{0,1},{1,0},{2,3},{3,2},{4,5},{5,4},{6,7},{7,6},{8,9},{9,8},{10,11... | collective-permute-start | bytes 1572872 | tf_op jit(solution)/shard_map/ppermute | solution.py:85
  21.8 0.3 collective-permute-start.12
  22.1 0.2 collective-permute-start.13
  22.3 0.6 %shard_map.60.w_ref = bf16[2,512,512]{2,1,0:T(8,128)(2,1)S(1)} custom-call(s32[6]{0:T(128)S(1)} %stack.27.sc, bf16[2,256,512]{2,1,0:T(8,128)(2,1)S(1)} %bitcast.14, bf16[2,256,512]{2,1,0:T(8,128)(2,1)S(1)} %collective-permute-done.8.refs_1_), custom_call_target="tpu_custom_call" | custom-call | tf_op jit(solution)/shard_map/pallas_call | solution.py:48
  23.0 1.4 %shard_map.61 = (f32[2,128,1024]{2,1,0:T(8,128)S(1)}, bf16[2,128,512]{2,1,0:T(8,128)(2,1)S(1)}) custom-call(s32[6]{0:T(128)S(1)} %stack.27.sc, bf16[2,128,1024]{2,1,0:T(8,128)(2,1)S(1)} %get-tuple-element.55.keep_ref, bf16[2,128,512]{2,1,0:T(8,128)(2,1)S(1)} %collective-permute-done.6.couple_ref, bf16[2,128,512]{2,1,0:T(8,128)(2,1)S(1)} %collective-permute-done.7.slots_ref, ...), custom_call_target="tpu_custom_call" | custom-call | flops 700000000 | tf_op jit(solution)/shard_map/pallas_call | solution.py:48
  24.4 1.1 %shard_map.62 = (bf16[2,128,512]{2,1,0:T(8,128)(2,1)S(1)}, bf16[2,128,256]{2,1,0:T(8,128)(2,1)S(1)}, bf16[2,128,256]{2,1,0:T(8,128)(2,1)S(1)}) custom-call(s32[6]{0:T(128)S(1)} %stack.27.sc, f32[2,128,1024]{2,1,0:T(8,128)S(1)} %get-tuple-element.59.acc_ref, bf16[2,128,512]{2,1,0:T(8,128)(2,1)S(1)} %get-tuple-element.60.hid_ref, ...), custom_call_target="tpu_custom_call" | custom-call | tf_op jit(solution)/shard_map/pallas_call | solution.py:48
  25.5 1.3 %collective-permute-start.14 = (bf16[2,128,256]{2,1,0:T(8,128)(2,1)S(1)}, bf16[2,128,256]{2,1,0:T(8,128)(2,1)S(1)}, u32[]{:S(2)}, u32[]{:S(2)}) collective-permute-start(bf16[2,128,256]{2,1,0:T(8,128)(2,1)S(1)} %get-tuple-element.68), channel_id=1, source_target_pairs={{0,4},{2,6},{4,0},{6,2},{8,12},{10,14},{12,8},{14,10},{16,20},{18,... | collective-permute-start | bytes 393224 | tf_op jit(solution)/shard_map/ppermute | solution.py:78
  26.9 0.8 %collective-permute-start.18 = (bf16[2,128,512]{2,1,0:T(8,128)(2,1)S(1)}, bf16[2,128,512]{2,1,0:T(8,128)(2,1)S(1)}, u32[]{:S(2)}, u32[]{:S(2)}) collective-permute-start(bf16[2,128,512]{2,1,0:T(8,128)(2,1)S(1)} %bitcast.16), channel_id=1, source_target_pairs={{0,2},{2,0},{4,6},{6,4},{8,10},{10,8},{12,14},{14,12},{16,18},{18,... | collective-permute-start | bytes 786440 | tf_op jit(solution)/shard_map/ppermute | solution.py:78
  27.7 2.7 %collective-permute-done.14.x_ref = bf16[2,128,256]{2,1,0:T(8,128)(2,1)S(1)} collective-permute-done((bf16[2,128,256]{2,1,0:T(8,128)(2,1)S(1)}, bf16[2,128,256]{2,1,0:T(8,128)(2,1)S(1)}, u32[]{:S(2)}, u32[]{:S(2)}) %collective-permute-start.14) | collective-permute-done | bytes 131104 | tf_op jit(solution)/shard_map/ppermute | solution.py:78
  30.4 0.6 shard_map.63.own_ref
  30.9 1.1 %collective-permute-start.20 = (bf16[2,128,768]{2,1,0:T(8,128)(2,1)S(1)}, bf16[2,128,768]{2,1,0:T(8,128)(2,1)S(1)}, u32[]{:S(2)}, u32[]{:S(2)}) collective-permute-start(bf16[2,128,768]{2,1,0:T(8,128)(2,1)S(1)} %shard_map.63.own_ref), channel_id=1, source_target_pairs={{0,4},{2,6},{4,0},{6,2},{8,12},{10,14},{12,8},{14,10},{16,20},{18,... | collective-permute-start | bytes 1179656 | tf_op jit(solution)/shard_map/ppermute | solution.py:78
  32.1 1.2 %collective-permute-start.21 = (bf16[2,128,768]{2,1,0:T(8,128)(2,1)S(1)}, bf16[2,128,768]{2,1,0:T(8,128)(2,1)S(1)}, u32[]{:S(2)}, u32[]{:S(2)}) collective-permute-start(bf16[2,128,768]{2,1,0:T(8,128)(2,1)S(1)} %shard_map.63.own_ref), channel_id=1, source_target_pairs={{0,1},{1,0},{2,3},{3,2},{4,5},{5,4},{6,7},{7,6},{8,9},{9,8},{10,11... | collective-permute-start | bytes 1179656 | tf_op jit(solution)/shard_map/ppermute | solution.py:85
  33.3 0.1 collective-permute-done.5.rest_4_.refs_0_
  33.4 1.8 %collective-permute-start.15 = (bf16[2,128,1024]{2,1,0:T(8,128)(2,1)S(1)}, bf16[2,128,1024]{2,1,0:T(8,128)(2,1)S(1)}, u32[]{:S(2)}, u32[]{:S(2)}) collective-permute-start(bf16[2,128,1024]{2,1,0:T(8,128)(2,1)S(1)} %collective-permute-done.5.rest_4_.refs_0_), channel_id=1, source_target_pairs={{0,2},{2,0},{4,6},{6,4},{8,10},{10,8},{12,14},{14,12},{16,18},{18,... | collective-permute-start | bytes 1572872 | tf_op jit(solution)/shard_map/ppermute | solution.py:78
  35.2 0.4 collective-permute-start.16
  35.7 1.5 %collective-permute-done.19.refs_3_ = bf16[2,128,512]{2,1,0:T(8,128)(2,1)S(1)} collective-permute-done((bf16[2,128,512]{2,1,0:T(8,128)(2,1)S(1)}, bf16[2,128,512]{2,1,0:T(8,128)(2,1)S(1)}, u32[]{:S(2)}, u32[]{:S(2)}) %collective-permute-start.19) | collective-permute-done | bytes 262176 | tf_op jit(solution)/shard_map/ppermute | solution.py:78
  37.1 0.7 %shard_map.65.refs_6_ = bf16[2,512,512]{2,1,0:T(8,128)(2,1)S(1)} custom-call(s32[6]{0:T(128)S(1)} %stack.27.sc, bf16[2,128,512]{2,1,0:T(8,128)(2,1)S(1)} %bitcast.17, bf16[2,128,512]{2,1,0:T(8,128)(2,1)S(1)} %collective-permute-done.11.refs_1_, bf16[2,128,512]{2,1,0:T(8,128)(2,1)S(1)} %collective-permute-done.18.refs_2_, ...), custom_call_target="tpu_custom_call" | custom-call | tf_op jit(solution)/shard_map/pallas_call | solution.py:48
  37.8 2.6 %collective-permute-done.20.x_ref = bf16[2,128,768]{2,1,0:T(8,128)(2,1)S(1)} collective-permute-done((bf16[2,128,768]{2,1,0:T(8,128)(2,1)S(1)}, bf16[2,128,768]{2,1,0:T(8,128)(2,1)S(1)}, u32[]{:S(2)}, u32[]{:S(2)}) %collective-permute-start.20) | collective-permute-done | bytes 393248 | tf_op jit(solution)/shard_map/ppermute | solution.py:78
  40.5 0.6 shard_map.67.refs_0_
  41.1 0.9 %collective-permute-start.22 = (bf16[2,128,768]{2,1,0:T(8,128)(2,1)S(1)}, bf16[2,128,768]{2,1,0:T(8,128)(2,1)S(1)}, u32[]{:S(2)}, u32[]{:S(2)}) collective-permute-start(bf16[2,128,768]{2,1,0:T(8,128)(2,1)S(1)} %collective-permute-done.21.own_ref), channel_id=1, source_target_pairs={{0,4},{2,6},{4,0},{6,2},{8,12},{10,14},{12,8},{14,10},{16,20},{18,... | collective-permute-start | bytes 1179656 | tf_op jit(solution)/shard_map/ppermute | solution.py:78
  42.0 4.2 %collective-permute-start.23 = (bf16[2,128,1536]{2,1,0:T(8,128)(2,1)S(1)}, bf16[2,128,1536]{2,1,0:T(8,128)(2,1)S(1)}, u32[]{:S(2)}, u32[]{:S(2)}) collective-permute-start(bf16[2,128,1536]{2,1,0:T(8,128)(2,1)S(1)} %shard_map.67.refs_0_), channel_id=1, source_target_pairs={{0,2},{2,0},{4,6},{6,4},{8,10},{10,8},{12,14},{14,12},{16,18},{18,... | collective-permute-start | bytes 2359304 | tf_op jit(solution)/shard_map/ppermute | solution.py:78
  46.2 4.2 %shard_map.64.refs_5_ = bf16[2,512,1536]{2,1,0:T(8,128)(2,1)S(1)} custom-call(s32[6]{0:T(128)S(1)} %stack.27.sc, bf16[2,512,512]{2,1,0:T(8,128)(2,1)S(1)} %shard_map.60.w_ref, bf16[2,256,512]{2,1,0:T(8,128)(2,1)S(1)} %get-tuple-element.45.end_ref.refs_8_.own_ref, bf16[2,256,512]{2,1,0:T(8,128)(2,1)S(1)} %collective-permute-done.4.refs_9_.endsib_ref.sib_ref, ...), custom_call_target="tpu_custom_call" | custom-call | flops 500000000 | tf_op jit(solution)/shard_map/pallas_call | solution.py:48
  50.5 1.8 %collective-permute-done.16.refs_2_ = bf16[2,128,1024]{2,1,0:T(8,128)(2,1)S(1)} collective-permute-done((bf16[2,128,1024]{2,1,0:T(8,128)(2,1)S(1)}, bf16[2,128,1024]{2,1,0:T(8,128)(2,1)S(1)}, u32[]{:S(2)}, u32[]{:S(2)}) %collective-permute-start.16) | collective-permute-done | bytes 524320 | tf_op jit(solution)/shard_map/ppermute | solution.py:85
  52.3 2.6 %collective-permute-start.17 = (bf16[2,128,1024]{2,1,0:T(8,128)(2,1)S(1)}, bf16[2,128,1024]{2,1,0:T(8,128)(2,1)S(1)}, u32[]{:S(2)}, u32[]{:S(2)}) collective-permute-start(bf16[2,128,1024]{2,1,0:T(8,128)(2,1)S(1)} %collective-permute-done.16.refs_2_), channel_id=1, source_target_pairs={{0,2},{2,0},{4,6},{6,4},{8,10},{10,8},{12,14},{14,12},{16,18},{18,... | collective-permute-start | bytes 1572872 | tf_op jit(solution)/shard_map/ppermute | solution.py:78
  54.8 0.6 %shard_map.68 = (bf16[2,128,768]{2,1,0:T(8,128)(2,1)S(1)}, bf16[2,128,768]{2,1,0:T(8,128)(2,1)S(1)}) custom-call(s32[6]{0:T(128)S(1)} %stack.27.sc, bf16[2,128,768]{2,1,0:T(8,128)(2,1)S(1)} %collective-permute-done.21.own_ref, bf16[2,128,768]{2,1,0:T(8,128)(2,1)S(1)} %collective-permute-done.22.x_ref), custom_call_target="tpu_custom_call" | custom-call | tf_op jit(solution)/shard_map/pallas_call | solution.py:48
  55.6 0.5 collective-permute-start.25
  56.1 0.3 collective-permute-done.17.refs_3_
  56.4 3.4 %shard_map.66 = (bf16[2,512,512]{2,1,0:T(8,128)(2,1)S(1)}, bf16[512,512]{1,0:T(8,128)(2,1)S(1)}, bf16[512,512]{1,0:T(8,128)(2,1)S(1)}) custom-call(s32[6]{0:T(128)S(1)} %stack.27.sc, bf16[2,256,1536]{2,1,0:T(8,128)(2,1)S(1)} %get-tuple-element.48.end_ref, bf16[2,256,1536]{2,1,0:T(8,128)(2,1)S(1)} %get-tuple-element.53.kept_ref, ...), custom_call_target="tpu_custom_call" | custom-call | flops 300000000 | tf_op jit(solution)/shard_map/pallas_call | solution.py:48
  59.8 3.4 %shard_map.69 = bf16[2,1,256,1536]{3,2,1,0:T(8,128)(2,1)} custom-call(s32[6]{0:T(128)S(1)} %stack.27.sc, bf16[2,512,512]{2,1,0:T(8,128)(2,1)S(1)} %get-tuple-element.73.hid_ref, bf16[512,512]{1,0:T(8,128)(2,1)S(1)} %get-tuple-element.74.first_ref, bf16[512,512]{1,0:T(8,128)(2,1)S(1)} %get-tuple-element.75.slots_ref, ...), custom_call_target="tpu_custom_call" | custom-call | tf_op jit(solution)/shard_map/pallas_call | solution.py:48
  (32 shorter events, 0.1 us)
Async XLA Ops:
  0.0 4.3 %copy-start.4 = (s32[1,8,512]{2,1,0:T(8,128)S(1)}, s32[1,8,512]{2,1,0:T(8,128)}, u32[]{:S(2)}) copy-start(s32[1,8,512]{2,1,0:T(8,128)} %param.8) | copy-start | bytes 49156
  0.1 2.3 %copy-start = (bf16[2,1,1,3,256,1536]{5,4,3,2,1,0:T(8,128)(2,1)S(1)}, bf16[2,1,1,3,256,1536]{5,4,3,2,1,0:T(8,128)(2,1)}, u32[]{:S(2)}) copy-start(bf16[2,1,1,3,256,1536]{5,4,3,2,1,0:T(8,128)(2,1)} %param.5) | copy-start | bytes 14155780
  2.4 1.9 %copy-start.5 = (s32[1,4,512]{2,1,0:T(4,128)S(1)}, s32[1,4,512]{2,1,0:T(4,128)}, u32[]{:S(2)}) copy-start(s32[1,4,512]{2,1,0:T(4,128)} %param.9) | copy-start | bytes 24580
  2.4 8.3 %copy-start.1 = (bf16[2,1,1,3,256,1536]{5,4,3,2,1,0:T(8,128)(2,1)S(1)}, bf16[2,1,1,3,256,1536]{5,4,3,2,1,0:T(8,128)(2,1)}, u32[]{:S(2)}) copy-start(bf16[2,1,1,3,256,1536]{5,4,3,2,1,0:T(8,128)(2,1)} %param.5) | copy-start | bytes 14155780
  3.1 3.3 %copy-start.2 = (bf16[2,1,256,512]{3,2,1,0:T(8,128)(2,1)S(1)}, bf16[2,1,256,512]{3,2,1,0:T(8,128)(2,1)}, u32[]{:S(2)}) copy-start(bf16[2,1,256,512]{3,2,1,0:T(8,128)(2,1)} %param.6) | copy-start | bytes 1572868
  3.2 6.1 %copy-start.3 = (bf16[2,1,128,512]{3,2,1,0:T(8,128)(2,1)S(1)}, bf16[2,1,128,512]{3,2,1,0:T(8,128)(2,1)}, u32[]{:S(2)}) copy-start(bf16[2,1,128,512]{3,2,1,0:T(8,128)(2,1)} %param.7) | copy-start | bytes 786436
  3.2 2.0 %collective-permute-start = (bf16[2,256,512]{2,1,0:T(8,128)(2,1)S(1)}, bf16[2,256,512]{2,1,0:T(8,128)(2,1)S(1)}, u32[]{:S(2)}, u32[]{:S(2)}) collective-permute-start(bf16[2,256,512]{2,1,0:T(8,128)(2,1)S(1)} %get-tuple-element.43.own_ref), channel_id=1, source_target_pairs={{0,2},{2,0},{4,6},{6,4},{8,10},{10,8},{12,14},{14,12},{16,18},{18,... | collective-permute-start | bytes 1572872 | tf_op jit(solution)/shard_map/ppermute | solution.py:78
  3.3 3.6 %collective-permute-start.1 = (bf16[2,256,512]{2,1,0:T(8,128)(2,1)S(1)}, bf16[2,256,512]{2,1,0:T(8,128)(2,1)S(1)}, u32[]{:S(2)}, u32[]{:S(2)}) collective-permute-start(bf16[2,256,512]{2,1,0:T(8,128)(2,1)S(1)} %get-tuple-element.49.refs_0_), channel_id=1, source_target_pairs={{0,2},{2,0},{4,6},{6,4},{8,10},{10,8},{12,14},{14,12},{16,18},{18,... | collective-permute-start | bytes 1572872 | tf_op jit(solution)/shard_map/ppermute | solution.py:78
  3.7 5.5 %collective-permute-start.2 = (bf16[2,256,512]{2,1,0:T(8,128)(2,1)S(1)}, bf16[2,256,512]{2,1,0:T(8,128)(2,1)S(1)}, u32[]{:S(2)}, u32[]{:S(2)}) collective-permute-start(bf16[2,256,512]{2,1,0:T(8,128)(2,1)S(1)} %get-tuple-element.50.refs_1_), channel_id=1, source_target_pairs={{0,2},{2,0},{4,6},{6,4},{8,10},{10,8},{12,14},{14,12},{16,18},{18,... | collective-permute-start | bytes 1572872 | tf_op jit(solution)/shard_map/ppermute | solution.py:78
  3.8 6.7 %collective-permute-start.3 = (bf16[2,256,512]{2,1,0:T(8,128)(2,1)S(1)}, bf16[2,256,512]{2,1,0:T(8,128)(2,1)S(1)}, u32[]{:S(2)}, u32[]{:S(2)}) collective-permute-start(bf16[2,256,512]{2,1,0:T(8,128)(2,1)S(1)} %get-tuple-element.51.refs_2_), channel_id=1, source_target_pairs={{0,2},{2,0},{4,6},{6,4},{8,10},{10,8},{12,14},{14,12},{16,18},{18,... | collective-permute-start | bytes 1572872 | tf_op jit(solution)/shard_map/ppermute | solution.py:78
  4.3 7.6 %collective-permute-start.4 = (bf16[2,256,512]{2,1,0:T(8,128)(2,1)S(1)}, bf16[2,256,512]{2,1,0:T(8,128)(2,1)S(1)}, u32[]{:S(2)}, u32[]{:S(2)}) collective-permute-start(bf16[2,256,512]{2,1,0:T(8,128)(2,1)S(1)} %get-tuple-element.45.end_ref.refs_8_.own_ref), channel_id=1, source_target_pairs={{0,2},{2,0},{4,6},{6,4},{8,10},{10,8},{12,14},{14,12},{16,18},{18,... | collective-permute-start | bytes 1572872 | tf_op jit(solution)/shard_map/ppermute | solution.py:78
  6.4 15.7 %collective-permute-start.8 = (bf16[2,256,512]{2,1,0:T(8,128)(2,1)S(1)}, bf16[2,256,512]{2,1,0:T(8,128)(2,1)S(1)}, u32[]{:S(2)}, u32[]{:S(2)}) collective-permute-start(bf16[2,256,512]{2,1,0:T(8,128)(2,1)S(1)} %bitcast.13), channel_id=1, source_target_pairs={{0,2},{2,0},{4,6},{6,4},{8,10},{10,8},{12,14},{14,12},{16,18},{18,... | collective-permute-start | bytes 1572872 | tf_op jit(solution)/shard_map/ppermute | solution.py:78
  6.9 8.6 %collective-permute-start.9 = (bf16[2,128,512]{2,1,0:T(8,128)(2,1)S(1)}, bf16[2,128,512]{2,1,0:T(8,128)(2,1)S(1)}, u32[]{:S(2)}, u32[]{:S(2)}) collective-permute-start(bf16[2,128,512]{2,1,0:T(8,128)(2,1)S(1)} %get-tuple-element.61), channel_id=1, source_target_pairs={{0,1},{1,0},{2,3},{3,2},{4,5},{5,4},{6,7},{7,6},{8,9},{9,8},{10,11... | collective-permute-start | bytes 786440 | tf_op jit(solution)/shard_map/ppermute | solution.py:85
  9.3 10.7 %collective-permute-start.11 = (bf16[2,128,512]{2,1,0:T(8,128)(2,1)S(1)}, bf16[2,128,512]{2,1,0:T(8,128)(2,1)S(1)}, u32[]{:S(2)}, u32[]{:S(2)}) collective-permute-start(bf16[2,128,512]{2,1,0:T(8,128)(2,1)S(1)} %bitcast.15), channel_id=1, source_target_pairs={{0,4},{2,6},{4,0},{6,2},{8,12},{10,14},{12,8},{14,10},{16,20},{18,... | collective-permute-start | bytes 786440 | tf_op jit(solution)/shard_map/ppermute | solution.py:78
  10.5 11.3 %collective-permute-start.10 = (bf16[2,128,512]{2,1,0:T(8,128)(2,1)S(1)}, bf16[2,128,512]{2,1,0:T(8,128)(2,1)S(1)}, u32[]{:S(2)}, u32[]{:S(2)}) collective-permute-start(bf16[2,128,512]{2,1,0:T(8,128)(2,1)S(1)} %get-tuple-element.62), channel_id=1, source_target_pairs={{0,1},{1,0},{2,3},{3,2},{4,5},{5,4},{6,7},{7,6},{8,9},{9,8},{10,11... | collective-permute-start | bytes 786440 | tf_op jit(solution)/shard_map/ppermute | solution.py:85
  11.8 11.1 %collective-permute-start.6 = (bf16[2,128,512]{2,1,0:T(8,128)(2,1)S(1)}, bf16[2,128,512]{2,1,0:T(8,128)(2,1)S(1)}, u32[]{:S(2)}, u32[]{:S(2)}) collective-permute-start(bf16[2,128,512]{2,1,0:T(8,128)(2,1)S(1)} %get-tuple-element.56), channel_id=1, source_target_pairs={{0,2},{2,0},{4,6},{6,4},{8,10},{10,8},{12,14},{14,12},{16,18},{18,... | collective-permute-start | bytes 786440 | tf_op jit(solution)/shard_map/ppermute | solution.py:78
  15.6 7.4 %collective-permute-start.7 = (bf16[2,128,512]{2,1,0:T(8,128)(2,1)S(1)}, bf16[2,128,512]{2,1,0:T(8,128)(2,1)S(1)}, u32[]{:S(2)}, u32[]{:S(2)}) collective-permute-start(bf16[2,128,512]{2,1,0:T(8,128)(2,1)S(1)} %get-tuple-element.57), channel_id=1, source_target_pairs={{0,2},{2,0},{4,6},{6,4},{8,10},{10,8},{12,14},{14,12},{16,18},{18,... | collective-permute-start | bytes 786440 | tf_op jit(solution)/shard_map/ppermute | solution.py:78
  19.9 13.5 %collective-permute-start.5 = (bf16[2,128,1024]{2,1,0:T(8,128)(2,1)S(1)}, bf16[2,128,1024]{2,1,0:T(8,128)(2,1)S(1)}, u32[]{:S(2)}, u32[]{:S(2)}) collective-permute-start(bf16[2,128,1024]{2,1,0:T(8,128)(2,1)S(1)} %get-tuple-element.54), channel_id=1, source_target_pairs={{0,1},{1,0},{2,3},{3,2},{4,5},{5,4},{6,7},{7,6},{8,9},{9,8},{10,11... | collective-permute-start | bytes 1572872 | tf_op jit(solution)/shard_map/ppermute | solution.py:85
  21.8 2.6 %collective-permute-start.12 = (bf16[2,128,512]{2,1,0:T(8,128)(2,1)S(1)}, bf16[2,128,512]{2,1,0:T(8,128)(2,1)S(1)}, u32[]{:S(2)}, u32[]{:S(2)}) collective-permute-start(bf16[2,128,512]{2,1,0:T(8,128)(2,1)S(1)} %collective-permute-done.9.rest_0_), channel_id=1, source_target_pairs={{0,2},{2,0},{4,6},{6,4},{8,10},{10,8},{12,14},{14,12},{16,18},{18,... | collective-permute-start | bytes 786440 | tf_op jit(solution)/shard_map/ppermute | solution.py:78
  22.1 2.2 %collective-permute-start.13 = (bf16[2,128,512]{2,1,0:T(8,128)(2,1)S(1)}, bf16[2,128,512]{2,1,0:T(8,128)(2,1)S(1)}, u32[]{:S(2)}, u32[]{:S(2)}) collective-permute-start(bf16[2,128,512]{2,1,0:T(8,128)(2,1)S(1)} %collective-permute-done.10.rest_1_), channel_id=1, source_target_pairs={{0,2},{2,0},{4,6},{6,4},{8,10},{10,8},{12,14},{14,12},{16,18},{18,... | collective-permute-start | bytes 786440 | tf_op jit(solution)/shard_map/ppermute | solution.py:78
  25.5 4.8 %collective-permute-start.14 = (bf16[2,128,256]{2,1,0:T(8,128)(2,1)S(1)}, bf16[2,128,256]{2,1,0:T(8,128)(2,1)S(1)}, u32[]{:S(2)}, u32[]{:S(2)}) collective-permute-start(bf16[2,128,256]{2,1,0:T(8,128)(2,1)S(1)} %get-tuple-element.68), channel_id=1, source_target_pairs={{0,4},{2,6},{4,0},{6,2},{8,12},{10,14},{12,8},{14,10},{16,20},{18,... | collective-permute-start | bytes 393224 | tf_op jit(solution)/shard_map/ppermute | solution.py:78
  26.9 8.4 %collective-permute-start.18 = (bf16[2,128,512]{2,1,0:T(8,128)(2,1)S(1)}, bf16[2,128,512]{2,1,0:T(8,128)(2,1)S(1)}, u32[]{:S(2)}, u32[]{:S(2)}) collective-permute-start(bf16[2,128,512]{2,1,0:T(8,128)(2,1)S(1)} %bitcast.16), channel_id=1, source_target_pairs={{0,2},{2,0},{4,6},{6,4},{8,10},{10,8},{12,14},{14,12},{16,18},{18,... | collective-permute-start | bytes 786440 | tf_op jit(solution)/shard_map/ppermute | solution.py:78
  30.9 9.5 %collective-permute-start.20 = (bf16[2,128,768]{2,1,0:T(8,128)(2,1)S(1)}, bf16[2,128,768]{2,1,0:T(8,128)(2,1)S(1)}, u32[]{:S(2)}, u32[]{:S(2)}) collective-permute-start(bf16[2,128,768]{2,1,0:T(8,128)(2,1)S(1)} %shard_map.63.own_ref), channel_id=1, source_target_pairs={{0,4},{2,6},{4,0},{6,2},{8,12},{10,14},{12,8},{14,10},{16,20},{18,... | collective-permute-start | bytes 1179656 | tf_op jit(solution)/shard_map/ppermute | solution.py:78
  32.1 9.0 %collective-permute-start.21 = (bf16[2,128,768]{2,1,0:T(8,128)(2,1)S(1)}, bf16[2,128,768]{2,1,0:T(8,128)(2,1)S(1)}, u32[]{:S(2)}, u32[]{:S(2)}) collective-permute-start(bf16[2,128,768]{2,1,0:T(8,128)(2,1)S(1)} %shard_map.63.own_ref), channel_id=1, source_target_pairs={{0,1},{1,0},{2,3},{3,2},{4,5},{5,4},{6,7},{7,6},{8,9},{9,8},{10,11... | collective-permute-start | bytes 1179656 | tf_op jit(solution)/shard_map/ppermute | solution.py:85
  33.4 12.8 %collective-permute-start.15 = (bf16[2,128,1024]{2,1,0:T(8,128)(2,1)S(1)}, bf16[2,128,1024]{2,1,0:T(8,128)(2,1)S(1)}, u32[]{:S(2)}, u32[]{:S(2)}) collective-permute-start(bf16[2,128,1024]{2,1,0:T(8,128)(2,1)S(1)} %collective-permute-done.5.rest_4_.refs_0_), channel_id=1, source_target_pairs={{0,2},{2,0},{4,6},{6,4},{8,10},{10,8},{12,14},{14,12},{16,18},{18,... | collective-permute-start | bytes 1572872 | tf_op jit(solution)/shard_map/ppermute | solution.py:78
  35.2 1.9 %collective-permute-start.19 = (bf16[2,128,512]{2,1,0:T(8,128)(2,1)S(1)}, bf16[2,128,512]{2,1,0:T(8,128)(2,1)S(1)}, u32[]{:S(2)}, u32[]{:S(2)}) collective-permute-start(bf16[2,128,512]{2,1,0:T(8,128)(2,1)S(1)} %collective-permute-done.11.refs_1_), channel_id=1, source_target_pairs={{0,2},{2,0},{4,6},{6,4},{8,10},{10,8},{12,14},{14,12},{16,18},{18,... | collective-permute-start | bytes 786440 | tf_op jit(solution)/shard_map/ppermute | solution.py:78
  35.2 17.0 %collective-permute-start.16 = (bf16[2,128,1024]{2,1,0:T(8,128)(2,1)S(1)}, bf16[2,128,1024]{2,1,0:T(8,128)(2,1)S(1)}, u32[]{:S(2)}, u32[]{:S(2)}) collective-permute-start(bf16[2,128,1024]{2,1,0:T(8,128)(2,1)S(1)} %get-tuple-element.71), channel_id=1, source_target_pairs={{0,1},{1,0},{2,3},{3,2},{4,5},{5,4},{6,7},{7,6},{8,9},{9,8},{10,11... | collective-permute-start | bytes 1572872 | tf_op jit(solution)/shard_map/ppermute | solution.py:85
  41.1 13.8 %collective-permute-start.22 = (bf16[2,128,768]{2,1,0:T(8,128)(2,1)S(1)}, bf16[2,128,768]{2,1,0:T(8,128)(2,1)S(1)}, u32[]{:S(2)}, u32[]{:S(2)}) collective-permute-start(bf16[2,128,768]{2,1,0:T(8,128)(2,1)S(1)} %collective-permute-done.21.own_ref), channel_id=1, source_target_pairs={{0,4},{2,6},{4,0},{6,2},{8,12},{10,14},{12,8},{14,10},{16,20},{18,... | collective-permute-start | bytes 1179656 | tf_op jit(solution)/shard_map/ppermute | solution.py:78
  42.0 17.8 %collective-permute-start.23 = (bf16[2,128,1536]{2,1,0:T(8,128)(2,1)S(1)}, bf16[2,128,1536]{2,1,0:T(8,128)(2,1)S(1)}, u32[]{:S(2)}, u32[]{:S(2)}) collective-permute-start(bf16[2,128,1536]{2,1,0:T(8,128)(2,1)S(1)} %shard_map.67.refs_0_), channel_id=1, source_target_pairs={{0,2},{2,0},{4,6},{6,4},{8,10},{10,8},{12,14},{14,12},{16,18},{18,... | collective-permute-start | bytes 2359304 | tf_op jit(solution)/shard_map/ppermute | solution.py:78
  52.3 4.1 %collective-permute-start.17 = (bf16[2,128,1024]{2,1,0:T(8,128)(2,1)S(1)}, bf16[2,128,1024]{2,1,0:T(8,128)(2,1)S(1)}, u32[]{:S(2)}, u32[]{:S(2)}) collective-permute-start(bf16[2,128,1024]{2,1,0:T(8,128)(2,1)S(1)} %collective-permute-done.16.refs_2_), channel_id=1, source_target_pairs={{0,2},{2,0},{4,6},{6,4},{8,10},{10,8},{12,14},{14,12},{16,18},{18,... | collective-permute-start | bytes 1572872 | tf_op jit(solution)/shard_map/ppermute | solution.py:78
  55.5 4.3 %collective-permute-start.24 = (bf16[2,128,768]{2,1,0:T(8,128)(2,1)S(1)}, bf16[2,128,768]{2,1,0:T(8,128)(2,1)S(1)}, u32[]{:S(2)}, u32[]{:S(2)}) collective-permute-start(bf16[2,128,768]{2,1,0:T(8,128)(2,1)S(1)} %get-tuple-element.79.refs_1_), channel_id=1, source_target_pairs={{0,2},{2,0},{4,6},{6,4},{8,10},{10,8},{12,14},{14,12},{16,18},{18,... | collective-permute-start | bytes 1179656 | tf_op jit(solution)/shard_map/ppermute | solution.py:78
  55.6 4.2 %collective-permute-start.25 = (bf16[2,128,768]{2,1,0:T(8,128)(2,1)S(1)}, bf16[2,128,768]{2,1,0:T(8,128)(2,1)S(1)}, u32[]{:S(2)}, u32[]{:S(2)}) collective-permute-start(bf16[2,128,768]{2,1,0:T(8,128)(2,1)S(1)} %get-tuple-element.80.refs_2_), channel_id=1, source_target_pairs={{0,2},{2,0},{4,6},{6,4},{8,10},{10,8},{12,14},{14,12},{16,18},{18,... | collective-permute-start | bytes 1179656 | tf_op jit(solution)/shard_map/ppermute | solution.py:78

commit v17 on v16

--- a/solution.py
+++ b/solution.py
@@ -14,7 +14,8 @@
 SLOTS_COST = 0
 OWN_COST = 700_000_000
 SOLVED_COST = 500_000_000
-KEEP_COST = 300_000_000
+KEEP_COST = 0
+HALF_COST = 3_200_000_000
 
 
 def dot(first, second):
@@ -207,10 +208,10 @@
                     write(t, c, (dot(take_own, own) + dot(take_sib, sib)).astype(BF16))
 
         def write_far(s, t, c, picked):
-            if c < 2:
-                outs[s][t, :, c * k : (c + 1) * k] = picked
+            if c == 0:
+                outs[nf + s][t, :, k:] = picked
             else:
-                outs[nf + s][t, :, k:] = picked
+                outs[(c - 1) * 2 * nf + s][t] = picked
 
         def col_half(s):
             start = (f + n_face - s - 1) % n_face * fr + p * hr
@@ -237,9 +238,10 @@
 
     kept, *kept_out = call(
         rows_kernel, scalars, [*s_rows, *s_sib, comp, skel_col, end_own, end_sib],
-        [sds((2, fr, 3 * k), BF16)] + [sds((2, hr, 2 * k), BF16)] * (2 * nf),
-    )
-    mixed_far = [face_permute(a, i + 1) for i, a in enumerate(kept_out[nf:])]
+        [sds((2, fr, 3 * k), BF16)]
+        + [sds((2, hr, width), BF16) for width in (k, 2 * k, k) for _ in range(nf)],
+    )
+    mixed_far = [face_permute(a, i + 1) for i, a in enumerate(kept_out[nf : 2 * nf])]
 
     def piece(hidden, start, count):
         return stacked(hidden[0][:, start : start + count], hidden[1][:, start : start + count])
@@ -368,28 +370,33 @@
 
     ends_far = [face_permute(after(a, two_own), i + 1) for i, a in enumerate(kept_out[:nf])]
     ends_fwd = [box_permute(after(a, solved_one), 1) for a in ends_far]
+    slots_far = [face_permute(after(a, two_own), i + 1) for i, a in enumerate(kept_out[2 * nf :])]
     two_sib += [box_permute(a, 1) for a in two_rows[1:]]
+
+    def whole_rows(sc, out_ref, base, end_ref, kept_ref, pieces):
+        p, q = sc[0], sc[1]
+
+        @pl.when(p == q)
+        def _():
+            for _, _, cols, _ in pieces:
+                out_ref[:, :, cols] = end_ref[:, :, slice(cols.start + base, cols.stop + base)]
+
+        @pl.when(p != q)
+        def _():
+            for far, fwd, cols, source in pieces:
+                for take, parts in zip(halves(p), (far, fwd)):
+                    total = kept_ref[:, take, cols.start + base : cols.stop + base]
+                    for part in parts:
+                        total = total + part[:, :, source]
+                    out_ref[:, take, cols] = total
 
     def level_one_kernel(sc, end_ref, kept_ref, *refs):
         parts = [refs[i * nf : (i + 1) * nf] for i in range(4)]
-        col_ref, one_ref, w_ref, hid_out, first_out, slots_out, zs = refs[4 * nf :]
+        col_ref, one_ref, w_ref, hid_out, first_out, sub_out, zs = refs[4 * nf :]
         p, q, f = sc[0], sc[1], sc[2]
-
-        @pl.when(p == q)
-        def _():
-            zs[...] = end_ref[...]
-
-        @pl.when(p != q)
-        def _():
-            for h, take in enumerate(halves(p)):
-                for part, cols, source in (
-                    (parts[h], slice(2 * k, 3 * k), slice(k, 2 * k)), (parts[2 + h], slice(0, 2 * k), slice(0, 2 * k)),
-                ):
-                    total = kept_ref[:, take, cols]
-                    for ref in part:
-                        total = total + ref[:, :, source]
-                    zs[:, take, cols] = total
-
+        whole_rows(sc, zs, 0, end_ref, kept_ref, [
+            (parts[0], parts[1], slice(0, k), slice(k, 2 * k)), (parts[2], parts[3], slice(k, 2 * k), slice(0, k)),
+        ])
         slots = col_ref[pl.ds(pl.multiple_of(f * fr, fr), fr), :]
         right = jnp.where(slots >= k, 1, 0)
         right = jnp.where(p == q, p, right) > 0
@@ -400,31 +407,57 @@
         start = [
             jnp.concatenate([jnp.where(right, nothing, a) for a in lefts], axis=0),
             jnp.concatenate([jnp.where(right, a, nothing) for a in rights], axis=0),
-            flat(zs[:, :, 2 * k :]),
         ]
         merged = [
             (start[c].astype(F32) - dot(left, flat(one_ref[:, :, c * k : (c + 1) * k]))).astype(BF16)
-            for c in range(3)
+            for c in range(2)
         ]
+        sub_out[...] = dot(left, flat(one_ref[:, :, 2 * k :]))
         is_left = q == 0
         first_out[...] = jnp.where(is_left, merged[0], merged[1])
-        slots_out[...] = merged[2]
         couple = jnp.where(is_left, merged[1], merged[0])
         second = dot(stacked(couple[:fr], couple[fr:]), flat(w_ref[...])).astype(BF16)
         for s in range(n_face):
             hid_out[s] = piece((second[:fr], second[fr:]), s * fr, fr)
 
-    hid_two, first_two, slots_two = call(
+    hid_two, first_two, sub_one = call(
         level_one_kernel, scalars,
         [end_kept, kept, *mixed_far, *mixed_fwd, *ends_far, *ends_fwd, skel_col, solved_one, weight_two],
-        [sds((n_face, 2 * fr, 2 * fr), BF16), sds((2 * fr, k), BF16), sds((2 * fr, k), BF16)],
-        scratch=[pltpu.VMEM((2, fr, 3 * k), BF16)], cost=KEEP_COST,
-    )
-
-    def level_two_kernel(sc, hid_ref, first_ref, slots_ref, *refs):
+        [sds((n_face, 2 * fr, 2 * fr), BF16), sds((2 * fr, k), BF16), sds((2 * fr, k), F32)],
+        scratch=[pltpu.VMEM((2, fr, 2 * k), BF16)], cost=KEEP_COST,
+    )
+    slots_fwd = [box_permute(after(a, hid_two), 1) for a in slots_far]
+
+    def slots_half_kernel(sc, kept_ref, *refs):
+        mine, _ = halves(sc[0])
+        total = kept_ref[:, mine, 2 * k :]
+        for ref in refs[:nf]:
+            total = total + ref[...]
+        refs[nf][...] = total
+
+    (slots_half,) = call(
+        slots_half_kernel, after(scalars, hid_two), [kept, *slots_far], [sds((2, hr, k), BF16)], cost=HALF_COST
+    )
+
+    def level_two_kernel(sc, hid_ref, first_ref, sub_ref, end_ref, kept_ref, half_ref, *refs):
+        fwd, refs = refs[:nf], refs[nf:]
         mine, other = refs[: 1 + 2 * nf], refs[1 + 2 * nf : 2 + 4 * nf]
-        out_ref, rows, stage, sems = refs[2 + 4 * nf :]
-        q = sc[1]
+        out_ref, rows, slots, stage, sems = refs[2 + 4 * nf :]
+        p, q = sc[0], sc[1]
+
+        @pl.when(p == q)
+        def _():
+            slots[...] = end_ref[:, :, 2 * k :]
+
+        @pl.when(p != q)
+        def _():
+            own_rows, sib_rows = halves(p)
+            slots[:, own_rows, :] = half_ref[...]
+            total = kept_ref[:, sib_rows, 2 * k :]
+            for ref in fwd:
+                total = total + ref[...]
+            slots[:, sib_rows, :] = total
+
         left = jnp.concatenate([hid_ref[s] for s in range(n_face)], axis=1)
         for take, parts in zip(halves(sc[0]), (mine, other)):
             rows[0, :, take, :] = parts[0][...]
@@ -432,8 +465,9 @@
                 rows[1 + i // 2, :, take, i % 2 * 3 * half : (i % 2 + 1) * 3 * half] = ref[...]
         copies = []
         for c in range(3):
-            first = slots_ref[...]
-            if c < 2:
+            if c == 2:
+                first = (flat(slots[...]).astype(F32) - sub_ref[...]).astype(BF16)
+            else:
                 first = jnp.where(q == c, first_ref[...], jnp.zeros((2 * fr, k), BF16))
             right = rows[:, :, :, c * k : (c + 1) * k].reshape(n_face * 2 * fr, k)
             stage[c] = (first.astype(F32) - dot(left, right)).astype(BF16).reshape(2, fr, k)
@@ -446,9 +480,11 @@
             copy.wait()
 
     (out,) = call(
-        level_two_kernel, scalars, [hid_two, first_two, slots_two, *two_rows, *two_sib],
+        level_two_kernel, scalars,
+        [hid_two, first_two, sub_one, end_kept, kept, slots_half, *slots_fwd, *two_rows, *two_sib],
         [sds((2, 1, fr, 3 * k), BF16)], out_specs=[in_hbm],
-        scratch=[pltpu.VMEM((n_face, 2, fr, 3 * k), BF16), pltpu.VMEM((3, 2, fr, k), BF16),
+        scratch=[pltpu.VMEM((n_face, 2, fr, 3 * k), BF16), pltpu.VMEM((2, fr, k), BF16),
+                 pltpu.VMEM((3, 2, fr, k), BF16),
                  pltpu.SemaphoreType.DMA((3, 2))],
     )
     return out

time: 63.8 us -> 64.6 us (1.013)
  starting transfers between devices: 25.6 us -> 26.5 us
  waiting for transfers between devices: 11.5 us -> 10.8 us
    ppermute x5 -> x6, waiting for transfers between devices: 4.33 us -> 2.91 us  [face_permute(): return lax.ppermute(array, ('box', 'face'), pairs)]
    ppermute x5 -> x6, starting transfers between devices: 6.07 us -> 7.28 us  [face_permute(): return lax.ppermute(array, ('box', 'face'), pairs)]
    ppermute x21 -> x22, waiting for transfers between devices: 7.19 us -> 7.89 us  [box_permute(): return lax.ppermute(array, 'box', [(b, b ^ mask) for b in range(n_box)])]
    pallas_call x15 -> x16, Pallas kernels: 23.4 us -> 24 us  [call(): pl.pallas_call(kernel, in_specs=[pl.BlockSpec(memory_space=pltpu.SMEM)] +...]
    ppermute x21 -> x22, starting transfers between devices: 19.5 us -> 19.3 us  [box_permute(): return lax.ppermute(array, 'box', [(b, b ^ mask) for b in range(n_box)])]
  transfers between devices with their start and end apart: 26 -> 28, of which waited for: 7 -> 8; matrix products, arithmetic and copies ran while one was open for 0% -> 0% of each run, Pallas kernels for 30% -> 31%
where the time goes in v17:
time: 64.6 us; the launch traced here: 64.1 us
  starting transfers between devices  26.5 us (41%)
  Pallas kernels  24 us (37%)
  waiting for transfers between devices  10.8 us (17%)
  local copies, waits for them, and re-layouts  2.45 us (4%)
    pallas_call x16, Pallas kernels, call(): pl.pallas_call(kernel, in_specs=[pl.BlockSpec(memory_space=pltpu.SMEM)] +...  24 us
    ppermute x22, starting transfers between devices, box_permute(): return lax.ppermute(array, 'box', [(b, b ^ mask) for b in range(n_box)])  19.3 us
    ppermute x22, waiting for transfers between devices, box_permute(): return lax.ppermute(array, 'box', [(b, b ^ mask) for b in range(n_box)])  7.89 us
    ppermute x6, starting transfers between devices, face_permute(): return lax.ppermute(array, ('box', 'face'), pairs)  7.28 us
    ppermute x6, waiting for transfers between devices, face_permute(): return lax.ppermute(array, ('box', 'face'), pairs)  2.91 us
    unnamed x12, local copies, waits for them, and re-layouts  2.36 us
  transfers between devices with their start and end apart: 28, of which 8 were waited for; matrix products, arithmetic and copies ran while one was open for 0% of the time, Pallas kernels for 31%

profile of v17, /device:TPU:1, one launch (start us, length us, event | category | flops | bytes accessed | tf_op | source)
XLA Modules:
  0.0 64.1 jit_solution(3852284273275700185)
XLA Ops:
  0.1 2.3 %copy-done = bf16[2,1,1,3,256,1536]{5,4,3,2,1,0:T(8,128)(2,1)S(1)} copy-done((bf16[2,1,1,3,256,1536]{5,4,3,2,1,0:T(8,128)(2,1)S(1)}, bf16[2,1,1,3,256,1536]{5,4,3,2,1,0:T(8,128)(2,1)}, u32[]{:S(2)}) %copy-start) | copy-done | bytes 4718616
  2.4 0.7 %shard_map.55 = (bf16[2,256,512]{2,1,0:T(8,128)(2,1)S(1)}, bf16[2,256,512]{2,1,0:T(8,128)(2,1)S(1)}, bf16[2,256,512]{2,1,0:T(8,128)(2,1)S(1)}, bf16[2,256,512]{2,1,0:T(8,128)(2,1)S(1)}, bf16[2,256,512]{2,1,0:T(8,128)(2,1)S(1)}) custom-call(s32[6]{0:T(128)S(1)} %stack.27.sc, bf16[2,3,256,1536]{3,2,1,0:T(8,128)(2,1)S(1)} %bitcast.11), custom_call_target="tpu_custom_call" | custom-call | tf_op jit(solution)/shard_map/pallas_call | solution.py:49
  3.2 0.1 collective-permute-start
  3.3 0.5 collective-permute-start.1
  3.8 0.4 collective-permute-start.3
  4.3 0.8 %shard_map.56 = (s32[1,512]{1,0:T(1,128)S(1)}, s32[512,1]{1,0:T(8,128)S(1)}) custom-call(s32[6]{0:T(128)S(1)} %stack.27.sc, s32[8,512]{1,0:T(8,128)S(1)} %bitcast.18, s32[4,512]{1,0:T(4,128)S(1)} %bitcast.19), custom_call_target="tpu_custom_call" | custom-call | tf_op jit(solution)/shard_map/pallas_call | solution.py:49
  5.2 1.3 %shard_map.57 = (bf16[2,256,512]{2,1,0:T(8,128)(2,1)S(1)}, bf16[2,128,512]{2,1,0:T(8,128)(2,1)S(1)}, bf16[2,128,512]{2,1,0:T(8,128)(2,1)S(1)}) custom-call(s32[6]{0:T(128)S(1)} %stack.27.sc, bf16[2,256,512]{2,1,0:T(8,128)(2,1)S(1)} %get-tuple-element.47.own_ref, bf16[2,256,512]{2,1,0:T(8,128)(2,1)S(1)} %collective-permute-done.sib_ref, ...), custom_call_target="tpu_custom_call" | custom-call | tf_op jit(solution)/shard_map/pallas_call | solution.py:49
  6.4 0.5 collective-permute-start.8
  6.9 2.3 %collective-permute-start.9 = (bf16[2,128,512]{2,1,0:T(8,128)(2,1)S(1)}, bf16[2,128,512]{2,1,0:T(8,128)(2,1)S(1)}, u32[]{:S(2)}, u32[]{:S(2)}) collective-permute-start(bf16[2,128,512]{2,1,0:T(8,128)(2,1)S(1)} %get-tuple-element.65), channel_id=1, source_target_pairs={{0,1},{1,0},{2,3},{3,2},{4,5},{5,4},{6,7},{7,6},{8,9},{9,8},{10,11... | collective-permute-start | bytes 786440 | tf_op jit(solution)/shard_map/ppermute | solution.py:86
  9.3 1.2 %collective-permute-start.11 = (bf16[2,128,512]{2,1,0:T(8,128)(2,1)S(1)}, bf16[2,128,512]{2,1,0:T(8,128)(2,1)S(1)}, u32[]{:S(2)}, u32[]{:S(2)}) collective-permute-start(bf16[2,128,512]{2,1,0:T(8,128)(2,1)S(1)} %bitcast.15), channel_id=1, source_target_pairs={{0,4},{2,6},{4,0},{6,2},{8,12},{10,14},{12,8},{14,10},{16,20},{18,... | collective-permute-start | bytes 786440 | tf_op jit(solution)/shard_map/ppermute | solution.py:79
  10.5 0.2 collective-permute-start.10
  10.7 1.1 %shard_map.58 = (bf16[2,128,1024]{2,1,0:T(8,128)(2,1)S(1)}, bf16[2,128,512]{2,1,0:T(8,128)(2,1)S(1)}, bf16[2,128,512]{2,1,0:T(8,128)(2,1)S(1)}, bf16[2,256,1536]{2,1,0:T(8,128)(2,1)S(1)}) custom-call(s32[6]{0:T(128)S(1)} %stack.27.sc, bf16[2,3,256,1536]{3,2,1,0:T(8,128)(2,1)S(1)} %bitcast.12, s32[1,512]{1,0:T(1,128)S(1)} %get-tuple-element.48.comp_ref.refs_6_), custom_call_target="tpu_custom_call" | custom-call | tf_op jit(solution)/shard_map/pallas_call | solution.py:49
  11.8 1.3 %collective-permute-start.6 = (bf16[2,128,512]{2,1,0:T(8,128)(2,1)S(1)}, bf16[2,128,512]{2,1,0:T(8,128)(2,1)S(1)}, u32[]{:S(2)}, u32[]{:S(2)}) collective-permute-start(bf16[2,128,512]{2,1,0:T(8,128)(2,1)S(1)} %get-tuple-element.60), channel_id=1, source_target_pairs={{0,2},{2,0},{4,6},{6,4},{8,10},{10,8},{12,14},{14,12},{16,18},{18,... | collective-permute-start | bytes 786440 | tf_op jit(solution)/shard_map/ppermute | solution.py:79
  13.2 2.4 %collective-permute-done.9.rest_0_ = bf16[2,128,512]{2,1,0:T(8,128)(2,1)S(1)} collective-permute-done((bf16[2,128,512]{2,1,0:T(8,128)(2,1)S(1)}, bf16[2,128,512]{2,1,0:T(8,128)(2,1)S(1)}, u32[]{:S(2)}, u32[]{:S(2)}) %collective-permute-start.9) | collective-permute-done | bytes 262176 | tf_op jit(solution)/shard_map/ppermute | solution.py:86
  15.6 1.5 %collective-permute-start.7 = (bf16[2,128,512]{2,1,0:T(8,128)(2,1)S(1)}, bf16[2,128,512]{2,1,0:T(8,128)(2,1)S(1)}, u32[]{:S(2)}, u32[]{:S(2)}) collective-permute-start(bf16[2,128,512]{2,1,0:T(8,128)(2,1)S(1)} %get-tuple-element.61), channel_id=1, source_target_pairs={{0,2},{2,0},{4,6},{6,4},{8,10},{10,8},{12,14},{14,12},{16,18},{18,... | collective-permute-start | bytes 786440 | tf_op jit(solution)/shard_map/ppermute | solution.py:79
  17.1 2.9 %shard_map.59 = (bf16[2,256,1536]{2,1,0:T(8,128)(2,1)S(1)}, bf16[2,128,512]{2,1,0:T(8,128)(2,1)S(1)}, bf16[2,128,1024]{2,1,0:T(8,128)(2,1)S(1)}, bf16[2,128,512]{2,1,0:T(8,128)(2,1)S(1)}) custom-call(s32[6]{0:T(128)S(1)} %stack.27.sc, bf16[2,256,512]{2,1,0:T(8,128)(2,1)S(1)} %get-tuple-element.53.refs_0_, ...), custom_call_target="tpu_custom_call" | custom-call | tf_op jit(solution)/shard_map/pallas_call | solution.py:49
  19.9 1.9 %collective-permute-start.5 = (bf16[2,128,1024]{2,1,0:T(8,128)(2,1)S(1)}, bf16[2,128,1024]{2,1,0:T(8,128)(2,1)S(1)}, u32[]{:S(2)}, u32[]{:S(2)}) collective-permute-start(bf16[2,128,1024]{2,1,0:T(8,128)(2,1)S(1)} %get-tuple-element.58), channel_id=1, source_target_pairs={{0,1},{1,0},{2,3},{3,2},{4,5},{5,4},{6,7},{7,6},{8,9},{9,8},{10,11... | collective-permute-start | bytes 1572872 | tf_op jit(solution)/shard_map/ppermute | solution.py:86
  21.8 0.3 collective-permute-start.12
  22.1 0.2 collective-permute-start.13
  22.3 0.6 shard_map.60.w_ref
  23.0 1.4 %shard_map.61 = (f32[2,128,1024]{2,1,0:T(8,128)S(1)}, bf16[2,128,512]{2,1,0:T(8,128)(2,1)S(1)}) custom-call(s32[6]{0:T(128)S(1)} %stack.27.sc, bf16[2,128,1024]{2,1,0:T(8,128)(2,1)S(1)} %get-tuple-element.59.keep_ref, bf16[2,128,512]{2,1,0:T(8,128)(2,1)S(1)} %collective-permute-done.6.couple_ref, bf16[2,128,512]{2,1,0:T(8,128)(2,1)S(1)} %collective-permute-done.7.slots_ref, ...), custom_call_target="tpu_custom_call" | custom-call | flops 700000000 | tf_op jit(solution)/shard_map/pallas_call | solution.py:49
  24.4 1.1 %shard_map.62 = (bf16[2,128,512]{2,1,0:T(8,128)(2,1)S(1)}, bf16[2,128,256]{2,1,0:T(8,128)(2,1)S(1)}, bf16[2,128,256]{2,1,0:T(8,128)(2,1)S(1)}) custom-call(s32[6]{0:T(128)S(1)} %stack.27.sc, f32[2,128,1024]{2,1,0:T(8,128)S(1)} %get-tuple-element.63.acc_ref, bf16[2,128,512]{2,1,0:T(8,128)(2,1)S(1)} %get-tuple-element.64.hid_ref, ...), custom_call_target="tpu_custom_call" | custom-call | tf_op jit(solution)/shard_map/pallas_call | solution.py:49
  25.5 1.3 %collective-permute-start.14 = (bf16[2,128,256]{2,1,0:T(8,128)(2,1)S(1)}, bf16[2,128,256]{2,1,0:T(8,128)(2,1)S(1)}, u32[]{:S(2)}, u32[]{:S(2)}) collective-permute-start(bf16[2,128,256]{2,1,0:T(8,128)(2,1)S(1)} %get-tuple-element.72), channel_id=1, source_target_pairs={{0,4},{2,6},{4,0},{6,2},{8,12},{10,14},{12,8},{14,10},{16,20},{18,... | collective-permute-start | bytes 393224 | tf_op jit(solution)/shard_map/ppermute | solution.py:79
  26.9 3.5 %collective-permute-done.14.x_ref = bf16[2,128,256]{2,1,0:T(8,128)(2,1)S(1)} collective-permute-done((bf16[2,128,256]{2,1,0:T(8,128)(2,1)S(1)}, bf16[2,128,256]{2,1,0:T(8,128)(2,1)S(1)}, u32[]{:S(2)}, u32[]{:S(2)}) %collective-permute-start.14) | collective-permute-done | bytes 131104 | tf_op jit(solution)/shard_map/ppermute | solution.py:79
  30.4 0.6 shard_map.63.own_ref
  30.9 1.1 %collective-permute-start.22 = (bf16[2,128,768]{2,1,0:T(8,128)(2,1)S(1)}, bf16[2,128,768]{2,1,0:T(8,128)(2,1)S(1)}, u32[]{:S(2)}, u32[]{:S(2)}) collective-permute-start(bf16[2,128,768]{2,1,0:T(8,128)(2,1)S(1)} %shard_map.63.own_ref), channel_id=1, source_target_pairs={{0,4},{2,6},{4,0},{6,2},{8,12},{10,14},{12,8},{14,10},{16,20},{18,... | collective-permute-start | bytes 1179656 | tf_op jit(solution)/shard_map/ppermute | solution.py:79
  32.1 1.2 %collective-permute-start.23 = (bf16[2,128,768]{2,1,0:T(8,128)(2,1)S(1)}, bf16[2,128,768]{2,1,0:T(8,128)(2,1)S(1)}, u32[]{:S(2)}, u32[]{:S(2)}) collective-permute-start(bf16[2,128,768]{2,1,0:T(8,128)(2,1)S(1)} %shard_map.63.own_ref), channel_id=1, source_target_pairs={{0,1},{1,0},{2,3},{3,2},{4,5},{5,4},{6,7},{7,6},{8,9},{9,8},{10,11... | collective-permute-start | bytes 1179656 | tf_op jit(solution)/shard_map/ppermute | solution.py:86
  33.3 0.1 collective-permute-done.5.rest_4_.refs_0_
  33.4 1.8 %collective-permute-start.15 = (bf16[2,128,1024]{2,1,0:T(8,128)(2,1)S(1)}, bf16[2,128,1024]{2,1,0:T(8,128)(2,1)S(1)}, u32[]{:S(2)}, u32[]{:S(2)}) collective-permute-start(bf16[2,128,1024]{2,1,0:T(8,128)(2,1)S(1)} %collective-permute-done.5.rest_4_.refs_0_), channel_id=1, source_target_pairs={{0,2},{2,0},{4,6},{6,4},{8,10},{10,8},{12,14},{14,12},{16,18},{18,... | collective-permute-start | bytes 1572872 | tf_op jit(solution)/shard_map/ppermute | solution.py:79
  35.2 0.5 collective-permute-start.19
  35.7 1.4 %collective-permute-done.18.refs_2_ = bf16[2,128,512]{2,1,0:T(8,128)(2,1)S(1)} collective-permute-done((bf16[2,128,512]{2,1,0:T(8,128)(2,1)S(1)}, bf16[2,128,512]{2,1,0:T(8,128)(2,1)S(1)}, u32[]{:S(2)}, u32[]{:S(2)}) %collective-permute-start.18) | collective-permute-done | bytes 262176 | tf_op jit(solution)/shard_map/ppermute | solution.py:79
  37.1 0.3 collective-permute-start.16
  37.4 0.1 collective-permute-done.19.refs_3_
  37.5 0.7 %shard_map.65.refs_6_ = bf16[2,512,512]{2,1,0:T(8,128)(2,1)S(1)} custom-call(s32[6]{0:T(128)S(1)} %stack.27.sc, bf16[2,128,512]{2,1,0:T(8,128)(2,1)S(1)} %bitcast.17, bf16[2,128,512]{2,1,0:T(8,128)(2,1)S(1)} %collective-permute-done.11.refs_1_, bf16[2,128,512]{2,1,0:T(8,128)(2,1)S(1)} %collective-permute-done.18.refs_2_, ...), custom_call_target="tpu_custom_call" | custom-call | tf_op jit(solution)/shard_map/pallas_call | solution.py:49
  38.2 2.3 %collective-permute-done.22.x_ref = bf16[2,128,768]{2,1,0:T(8,128)(2,1)S(1)} collective-permute-done((bf16[2,128,768]{2,1,0:T(8,128)(2,1)S(1)}, bf16[2,128,768]{2,1,0:T(8,128)(2,1)S(1)}, u32[]{:S(2)}, u32[]{:S(2)}) %collective-permute-start.22) | collective-permute-done | bytes 393248 | tf_op jit(solution)/shard_map/ppermute | solution.py:79
  40.5 0.6 shard_map.68.refs_1_
  41.1 0.9 %collective-permute-start.24 = (bf16[2,128,768]{2,1,0:T(8,128)(2,1)S(1)}, bf16[2,128,768]{2,1,0:T(8,128)(2,1)S(1)}, u32[]{:S(2)}, u32[]{:S(2)}) collective-permute-start(bf16[2,128,768]{2,1,0:T(8,128)(2,1)S(1)} %collective-permute-done.23.own_ref), channel_id=1, source_target_pairs={{0,4},{2,6},{4,0},{6,2},{8,12},{10,14},{12,8},{14,10},{16,20},{18,... | collective-permute-start | bytes 1179656 | tf_op jit(solution)/shard_map/ppermute | solution.py:79
  42.0 4.2 %collective-permute-start.25 = (bf16[2,128,1536]{2,1,0:T(8,128)(2,1)S(1)}, bf16[2,128,1536]{2,1,0:T(8,128)(2,1)S(1)}, u32[]{:S(2)}, u32[]{:S(2)}) collective-permute-start(bf16[2,128,1536]{2,1,0:T(8,128)(2,1)S(1)} %shard_map.68.refs_1_), channel_id=1, source_target_pairs={{0,2},{2,0},{4,6},{6,4},{8,10},{10,8},{12,14},{14,12},{16,18},{18,... | collective-permute-start | bytes 2359304 | tf_op jit(solution)/shard_map/ppermute | solution.py:79
  46.2 4.2 %shard_map.64.refs_5_ = bf16[2,512,1536]{2,1,0:T(8,128)(2,1)S(1)} custom-call(s32[6]{0:T(128)S(1)} %stack.27.sc, bf16[2,512,512]{2,1,0:T(8,128)(2,1)S(1)} %shard_map.60.w_ref, bf16[2,256,512]{2,1,0:T(8,128)(2,1)S(1)} %get-tuple-element.49.end_ref.refs_8_.own_ref, bf16[2,256,512]{2,1,0:T(8,128)(2,1)S(1)} %collective-permute-done.4.refs_9_.endsib_ref.sib_ref, ...), custom_call_target="tpu_custom_call" | custom-call | flops 500000000 | tf_op jit(solution)/shard_map/pallas_call | solution.py:49
  50.6 1.3 %collective-permute-start.20 = (bf16[2,128,512]{2,1,0:T(8,128)(2,1)S(1)}, bf16[2,128,512]{2,1,0:T(8,128)(2,1)S(1)}, u32[]{:S(2)}, u32[]{:S(2)}) collective-permute-start(bf16[2,128,512]{2,1,0:T(8,128)(2,1)S(1)} %get-tuple-element.82), channel_id=1, source_target_pairs={{0,1},{1,0},{2,3},{3,2},{4,5},{5,4},{6,7},{7,6},{8,9},{9,8},{10,11... | collective-permute-start | bytes 786440 | tf_op jit(solution)/shard_map/ppermute | solution.py:86
  51.9 0.6 %shard_map.69 = (bf16[2,128,768]{2,1,0:T(8,128)(2,1)S(1)}, bf16[2,128,768]{2,1,0:T(8,128)(2,1)S(1)}) custom-call(s32[6]{0:T(128)S(1)} %stack.27.sc, bf16[2,128,768]{2,1,0:T(8,128)(2,1)S(1)} %collective-permute-done.23.own_ref, bf16[2,128,768]{2,1,0:T(8,128)(2,1)S(1)} %collective-permute-done.24.x_ref), custom_call_target="tpu_custom_call" | custom-call | tf_op jit(solution)/shard_map/pallas_call | solution.py:49
  52.6 1.7 %collective-permute-start.26 = (bf16[2,128,768]{2,1,0:T(8,128)(2,1)S(1)}, bf16[2,128,768]{2,1,0:T(8,128)(2,1)S(1)}, u32[]{:S(2)}, u32[]{:S(2)}) collective-permute-start(bf16[2,128,768]{2,1,0:T(8,128)(2,1)S(1)} %get-tuple-element.87.refs_2_), channel_id=1, source_target_pairs={{0,2},{2,0},{4,6},{6,4},{8,10},{10,8},{12,14},{14,12},{16,18},{18,... | collective-permute-start | bytes 1179656 | tf_op jit(solution)/shard_map/ppermute | solution.py:79
  54.3 3.3 %shard_map.66 = (bf16[2,512,512]{2,1,0:T(8,128)(2,1)S(1)}, bf16[512,512]{1,0:T(8,128)(2,1)S(1)}, f32[512,512]{1,0:T(8,128)S(1)}) custom-call(s32[6]{0:T(128)S(1)} %stack.27.sc, bf16[2,256,1536]{2,1,0:T(8,128)(2,1)S(1)} %get-tuple-element.52.end_ref, bf16[2,256,1536]{2,1,0:T(8,128)(2,1)S(1)} %get-tuple-element.57.kept_ref, ...), custom_call_target="tpu_custom_call" | custom-call | tf_op jit(solution)/shard_map/pallas_call | solution.py:49
  57.7 0.4 collective-permute-done.20.refs_0_
  58.1 1.3 %collective-permute-start.21 = (bf16[2,128,512]{2,1,0:T(8,128)(2,1)S(1)}, bf16[2,128,512]{2,1,0:T(8,128)(2,1)S(1)}, u32[]{:S(2)}, u32[]{:S(2)}) collective-permute-start(bf16[2,128,512]{2,1,0:T(8,128)(2,1)S(1)} %collective-permute-done.20.refs_0_), channel_id=1, source_target_pairs={{0,2},{2,0},{4,6},{6,4},{8,10},{10,8},{12,14},{14,12},{16,18},{18,... | collective-permute-start | bytes 786440 | tf_op jit(solution)/shard_map/ppermute | solution.py:79
  59.3 0.6 shard_map.67.half_ref
  59.9 0.6 collective-permute-done.21.refs_0_
  60.5 3.5 %shard_map.70 = bf16[2,1,256,1536]{3,2,1,0:T(8,128)(2,1)} custom-call(s32[6]{0:T(128)S(1)} %stack.27.sc, bf16[2,512,512]{2,1,0:T(8,128)(2,1)S(1)} %get-tuple-element.77.hid_ref, bf16[512,512]{1,0:T(8,128)(2,1)S(1)} %get-tuple-element.78.first_ref, f32[512,512]{1,0:T(8,128)S(1)} %get-tuple-element.79.sub_ref, ...), custom_call_target="tpu_custom_call" | custom-call | tf_op jit(solution)/shard_map/pallas_call | solution.py:49
  (37 shorter events, 0.5 us)
Async XLA Ops:
  0.0 4.3 %copy-start.4 = (s32[1,8,512]{2,1,0:T(8,128)S(1)}, s32[1,8,512]{2,1,0:T(8,128)}, u32[]{:S(2)}) copy-start(s32[1,8,512]{2,1,0:T(8,128)} %param.8) | copy-start | bytes 49156
  0.1 2.3 %copy-start = (bf16[2,1,1,3,256,1536]{5,4,3,2,1,0:T(8,128)(2,1)S(1)}, bf16[2,1,1,3,256,1536]{5,4,3,2,1,0:T(8,128)(2,1)}, u32[]{:S(2)}) copy-start(bf16[2,1,1,3,256,1536]{5,4,3,2,1,0:T(8,128)(2,1)} %param.5) | copy-start | bytes 14155780
  2.4 1.9 %copy-start.5 = (s32[1,4,512]{2,1,0:T(4,128)S(1)}, s32[1,4,512]{2,1,0:T(4,128)}, u32[]{:S(2)}) copy-start(s32[1,4,512]{2,1,0:T(4,128)} %param.9) | copy-start | bytes 24580
  2.4 8.3 %copy-start.1 = (bf16[2,1,1,3,256,1536]{5,4,3,2,1,0:T(8,128)(2,1)S(1)}, bf16[2,1,1,3,256,1536]{5,4,3,2,1,0:T(8,128)(2,1)}, u32[]{:S(2)}) copy-start(bf16[2,1,1,3,256,1536]{5,4,3,2,1,0:T(8,128)(2,1)} %param.5) | copy-start | bytes 14155780
  3.1 3.3 %copy-start.2 = (bf16[2,1,256,512]{3,2,1,0:T(8,128)(2,1)S(1)}, bf16[2,1,256,512]{3,2,1,0:T(8,128)(2,1)}, u32[]{:S(2)}) copy-start(bf16[2,1,256,512]{3,2,1,0:T(8,128)(2,1)} %param.6) | copy-start | bytes 1572868
  3.2 6.1 %copy-start.3 = (bf16[2,1,128,512]{3,2,1,0:T(8,128)(2,1)S(1)}, bf16[2,1,128,512]{3,2,1,0:T(8,128)(2,1)}, u32[]{:S(2)}) copy-start(bf16[2,1,128,512]{3,2,1,0:T(8,128)(2,1)} %param.7) | copy-start | bytes 786436
  3.2 2.0 %collective-permute-start = (bf16[2,256,512]{2,1,0:T(8,128)(2,1)S(1)}, bf16[2,256,512]{2,1,0:T(8,128)(2,1)S(1)}, u32[]{:S(2)}, u32[]{:S(2)}) collective-permute-start(bf16[2,256,512]{2,1,0:T(8,128)(2,1)S(1)} %get-tuple-element.47.own_ref), channel_id=1, source_target_pairs={{0,2},{2,0},{4,6},{6,4},{8,10},{10,8},{12,14},{14,12},{16,18},{18,... | collective-permute-start | bytes 1572872 | tf_op jit(solution)/shard_map/ppermute | solution.py:79
  3.3 3.6 %collective-permute-start.1 = (bf16[2,256,512]{2,1,0:T(8,128)(2,1)S(1)}, bf16[2,256,512]{2,1,0:T(8,128)(2,1)S(1)}, u32[]{:S(2)}, u32[]{:S(2)}) collective-permute-start(bf16[2,256,512]{2,1,0:T(8,128)(2,1)S(1)} %get-tuple-element.53.refs_0_), channel_id=1, source_target_pairs={{0,2},{2,0},{4,6},{6,4},{8,10},{10,8},{12,14},{14,12},{16,18},{18,... | collective-permute-start | bytes 1572872 | tf_op jit(solution)/shard_map/ppermute | solution.py:79
  3.7 5.5 %collective-permute-start.2 = (bf16[2,256,512]{2,1,0:T(8,128)(2,1)S(1)}, bf16[2,256,512]{2,1,0:T(8,128)(2,1)S(1)}, u32[]{:S(2)}, u32[]{:S(2)}) collective-permute-start(bf16[2,256,512]{2,1,0:T(8,128)(2,1)S(1)} %get-tuple-element.54.refs_1_), channel_id=1, source_target_pairs={{0,2},{2,0},{4,6},{6,4},{8,10},{10,8},{12,14},{14,12},{16,18},{18,... | collective-permute-start | bytes 1572872 | tf_op jit(solution)/shard_map/ppermute | solution.py:79
  3.8 6.7 %collective-permute-start.3 = (bf16[2,256,512]{2,1,0:T(8,128)(2,1)S(1)}, bf16[2,256,512]{2,1,0:T(8,128)(2,1)S(1)}, u32[]{:S(2)}, u32[]{:S(2)}) collective-permute-start(bf16[2,256,512]{2,1,0:T(8,128)(2,1)S(1)} %get-tuple-element.55.refs_2_), channel_id=1, source_target_pairs={{0,2},{2,0},{4,6},{6,4},{8,10},{10,8},{12,14},{14,12},{16,18},{18,... | collective-permute-start | bytes 1572872 | tf_op jit(solution)/shard_map/ppermute | solution.py:79
  4.3 7.6 %collective-permute-start.4 = (bf16[2,256,512]{2,1,0:T(8,128)(2,1)S(1)}, bf16[2,256,512]{2,1,0:T(8,128)(2,1)S(1)}, u32[]{:S(2)}, u32[]{:S(2)}) collective-permute-start(bf16[2,256,512]{2,1,0:T(8,128)(2,1)S(1)} %get-tuple-element.49.end_ref.refs_8_.own_ref), channel_id=1, source_target_pairs={{0,2},{2,0},{4,6},{6,4},{8,10},{10,8},{12,14},{14,12},{16,18},{18,... | collective-permute-start | bytes 1572872 | tf_op jit(solution)/shard_map/ppermute | solution.py:79
  6.4 15.7 %collective-permute-start.8 = (bf16[2,256,512]{2,1,0:T(8,128)(2,1)S(1)}, bf16[2,256,512]{2,1,0:T(8,128)(2,1)S(1)}, u32[]{:S(2)}, u32[]{:S(2)}) collective-permute-start(bf16[2,256,512]{2,1,0:T(8,128)(2,1)S(1)} %bitcast.13), channel_id=1, source_target_pairs={{0,2},{2,0},{4,6},{6,4},{8,10},{10,8},{12,14},{14,12},{16,18},{18,... | collective-permute-start | bytes 1572872 | tf_op jit(solution)/shard_map/ppermute | solution.py:79
  6.9 8.6 %collective-permute-start.9 = (bf16[2,128,512]{2,1,0:T(8,128)(2,1)S(1)}, bf16[2,128,512]{2,1,0:T(8,128)(2,1)S(1)}, u32[]{:S(2)}, u32[]{:S(2)}) collective-permute-start(bf16[2,128,512]{2,1,0:T(8,128)(2,1)S(1)} %get-tuple-element.65), channel_id=1, source_target_pairs={{0,1},{1,0},{2,3},{3,2},{4,5},{5,4},{6,7},{7,6},{8,9},{9,8},{10,11... | collective-permute-start | bytes 786440 | tf_op jit(solution)/shard_map/ppermute | solution.py:86
  9.3 10.7 %collective-permute-start.11 = (bf16[2,128,512]{2,1,0:T(8,128)(2,1)S(1)}, bf16[2,128,512]{2,1,0:T(8,128)(2,1)S(1)}, u32[]{:S(2)}, u32[]{:S(2)}) collective-permute-start(bf16[2,128,512]{2,1,0:T(8,128)(2,1)S(1)} %bitcast.15), channel_id=1, source_target_pairs={{0,4},{2,6},{4,0},{6,2},{8,12},{10,14},{12,8},{14,10},{16,20},{18,... | collective-permute-start | bytes 786440 | tf_op jit(solution)/shard_map/ppermute | solution.py:79
  10.5 11.3 %collective-permute-start.10 = (bf16[2,128,512]{2,1,0:T(8,128)(2,1)S(1)}, bf16[2,128,512]{2,1,0:T(8,128)(2,1)S(1)}, u32[]{:S(2)}, u32[]{:S(2)}) collective-permute-start(bf16[2,128,512]{2,1,0:T(8,128)(2,1)S(1)} %get-tuple-element.66), channel_id=1, source_target_pairs={{0,1},{1,0},{2,3},{3,2},{4,5},{5,4},{6,7},{7,6},{8,9},{9,8},{10,11... | collective-permute-start | bytes 786440 | tf_op jit(solution)/shard_map/ppermute | solution.py:86
  11.8 11.1 %collective-permute-start.6 = (bf16[2,128,512]{2,1,0:T(8,128)(2,1)S(1)}, bf16[2,128,512]{2,1,0:T(8,128)(2,1)S(1)}, u32[]{:S(2)}, u32[]{:S(2)}) collective-permute-start(bf16[2,128,512]{2,1,0:T(8,128)(2,1)S(1)} %get-tuple-element.60), channel_id=1, source_target_pairs={{0,2},{2,0},{4,6},{6,4},{8,10},{10,8},{12,14},{14,12},{16,18},{18,... | collective-permute-start | bytes 786440 | tf_op jit(solution)/shard_map/ppermute | solution.py:79
  15.6 7.4 %collective-permute-start.7 = (bf16[2,128,512]{2,1,0:T(8,128)(2,1)S(1)}, bf16[2,128,512]{2,1,0:T(8,128)(2,1)S(1)}, u32[]{:S(2)}, u32[]{:S(2)}) collective-permute-start(bf16[2,128,512]{2,1,0:T(8,128)(2,1)S(1)} %get-tuple-element.61), channel_id=1, source_target_pairs={{0,2},{2,0},{4,6},{6,4},{8,10},{10,8},{12,14},{14,12},{16,18},{18,... | collective-permute-start | bytes 786440 | tf_op jit(solution)/shard_map/ppermute | solution.py:79
  19.9 13.5 %collective-permute-start.5 = (bf16[2,128,1024]{2,1,0:T(8,128)(2,1)S(1)}, bf16[2,128,1024]{2,1,0:T(8,128)(2,1)S(1)}, u32[]{:S(2)}, u32[]{:S(2)}) collective-permute-start(bf16[2,128,1024]{2,1,0:T(8,128)(2,1)S(1)} %get-tuple-element.58), channel_id=1, source_target_pairs={{0,1},{1,0},{2,3},{3,2},{4,5},{5,4},{6,7},{7,6},{8,9},{9,8},{10,11... | collective-permute-start | bytes 1572872 | tf_op jit(solution)/shard_map/ppermute | solution.py:86
  21.8 2.6 %collective-permute-start.12 = (bf16[2,128,512]{2,1,0:T(8,128)(2,1)S(1)}, bf16[2,128,512]{2,1,0:T(8,128)(2,1)S(1)}, u32[]{:S(2)}, u32[]{:S(2)}) collective-permute-start(bf16[2,128,512]{2,1,0:T(8,128)(2,1)S(1)} %collective-permute-done.9.rest_0_), channel_id=1, source_target_pairs={{0,2},{2,0},{4,6},{6,4},{8,10},{10,8},{12,14},{14,12},{16,18},{18,... | collective-permute-start | bytes 786440 | tf_op jit(solution)/shard_map/ppermute | solution.py:79
  22.1 2.2 %collective-permute-start.13 = (bf16[2,128,512]{2,1,0:T(8,128)(2,1)S(1)}, bf16[2,128,512]{2,1,0:T(8,128)(2,1)S(1)}, u32[]{:S(2)}, u32[]{:S(2)}) collective-permute-start(bf16[2,128,512]{2,1,0:T(8,128)(2,1)S(1)} %collective-permute-done.10.rest_1_), channel_id=1, source_target_pairs={{0,2},{2,0},{4,6},{6,4},{8,10},{10,8},{12,14},{14,12},{16,18},{18,... | collective-permute-start | bytes 786440 | tf_op jit(solution)/shard_map/ppermute | solution.py:79
  25.5 4.8 %collective-permute-start.14 = (bf16[2,128,256]{2,1,0:T(8,128)(2,1)S(1)}, bf16[2,128,256]{2,1,0:T(8,128)(2,1)S(1)}, u32[]{:S(2)}, u32[]{:S(2)}) collective-permute-start(bf16[2,128,256]{2,1,0:T(8,128)(2,1)S(1)} %get-tuple-element.72), channel_id=1, source_target_pairs={{0,4},{2,6},{4,0},{6,2},{8,12},{10,14},{12,8},{14,10},{16,20},{18,... | collective-permute-start | bytes 393224 | tf_op jit(solution)/shard_map/ppermute | solution.py:79
  30.9 9.5 %collective-permute-start.22 = (bf16[2,128,768]{2,1,0:T(8,128)(2,1)S(1)}, bf16[2,128,768]{2,1,0:T(8,128)(2,1)S(1)}, u32[]{:S(2)}, u32[]{:S(2)}) collective-permute-start(bf16[2,128,768]{2,1,0:T(8,128)(2,1)S(1)} %shard_map.63.own_ref), channel_id=1, source_target_pairs={{0,4},{2,6},{4,0},{6,2},{8,12},{10,14},{12,8},{14,10},{16,20},{18,... | collective-permute-start | bytes 1179656 | tf_op jit(solution)/shard_map/ppermute | solution.py:79
  32.1 9.0 %collective-permute-start.23 = (bf16[2,128,768]{2,1,0:T(8,128)(2,1)S(1)}, bf16[2,128,768]{2,1,0:T(8,128)(2,1)S(1)}, u32[]{:S(2)}, u32[]{:S(2)}) collective-permute-start(bf16[2,128,768]{2,1,0:T(8,128)(2,1)S(1)} %shard_map.63.own_ref), channel_id=1, source_target_pairs={{0,1},{1,0},{2,3},{3,2},{4,5},{5,4},{6,7},{7,6},{8,9},{9,8},{10,11... | collective-permute-start | bytes 1179656 | tf_op jit(solution)/shard_map/ppermute | solution.py:86
  33.4 12.8 %collective-permute-start.15 = (bf16[2,128,1024]{2,1,0:T(8,128)(2,1)S(1)}, bf16[2,128,1024]{2,1,0:T(8,128)(2,1)S(1)}, u32[]{:S(2)}, u32[]{:S(2)}) collective-permute-start(bf16[2,128,1024]{2,1,0:T(8,128)(2,1)S(1)} %collective-permute-done.5.rest_4_.refs_0_), channel_id=1, source_target_pairs={{0,2},{2,0},{4,6},{6,4},{8,10},{10,8},{12,14},{14,12},{16,18},{18,... | collective-permute-start | bytes 1572872 | tf_op jit(solution)/shard_map/ppermute | solution.py:79
  35.2 1.9 %collective-permute-start.18 = (bf16[2,128,512]{2,1,0:T(8,128)(2,1)S(1)}, bf16[2,128,512]{2,1,0:T(8,128)(2,1)S(1)}, u32[]{:S(2)}, u32[]{:S(2)}) collective-permute-start(bf16[2,128,512]{2,1,0:T(8,128)(2,1)S(1)} %bitcast.16), channel_id=1, source_target_pairs={{0,2},{2,0},{4,6},{6,4},{8,10},{10,8},{12,14},{14,12},{16,18},{18,... | collective-permute-start | bytes 786440 | tf_op jit(solution)/shard_map/ppermute | solution.py:79
  35.2 2.3 %collective-permute-start.19 = (bf16[2,128,512]{2,1,0:T(8,128)(2,1)S(1)}, bf16[2,128,512]{2,1,0:T(8,128)(2,1)S(1)}, u32[]{:S(2)}, u32[]{:S(2)}) collective-permute-start(bf16[2,128,512]{2,1,0:T(8,128)(2,1)S(1)} %collective-permute-done.11.refs_1_), channel_id=1, source_target_pairs={{0,2},{2,0},{4,6},{6,4},{8,10},{10,8},{12,14},{14,12},{16,18},{18,... | collective-permute-start | bytes 786440 | tf_op jit(solution)/shard_map/ppermute | solution.py:79
  37.1 13.3 %collective-permute-start.16 = (bf16[2,128,512]{2,1,0:T(8,128)(2,1)S(1)}, bf16[2,128,512]{2,1,0:T(8,128)(2,1)S(1)}, u32[]{:S(2)}, u32[]{:S(2)}) collective-permute-start(bf16[2,128,512]{2,1,0:T(8,128)(2,1)S(1)} %get-tuple-element.75), channel_id=1, source_target_pairs={{0,1},{1,0},{2,3},{3,2},{4,5},{5,4},{6,7},{7,6},{8,9},{9,8},{10,11... | collective-permute-start | bytes 786440 | tf_op jit(solution)/shard_map/ppermute | solution.py:86
  41.1 10.8 %collective-permute-start.24 = (bf16[2,128,768]{2,1,0:T(8,128)(2,1)S(1)}, bf16[2,128,768]{2,1,0:T(8,128)(2,1)S(1)}, u32[]{:S(2)}, u32[]{:S(2)}) collective-permute-start(bf16[2,128,768]{2,1,0:T(8,128)(2,1)S(1)} %collective-permute-done.23.own_ref), channel_id=1, source_target_pairs={{0,4},{2,6},{4,0},{6,2},{8,12},{10,14},{12,8},{14,10},{16,20},{18,... | collective-permute-start | bytes 1179656 | tf_op jit(solution)/shard_map/ppermute | solution.py:79
  42.0 18.5 %collective-permute-start.25 = (bf16[2,128,1536]{2,1,0:T(8,128)(2,1)S(1)}, bf16[2,128,1536]{2,1,0:T(8,128)(2,1)S(1)}, u32[]{:S(2)}, u32[]{:S(2)}) collective-permute-start(bf16[2,128,1536]{2,1,0:T(8,128)(2,1)S(1)} %shard_map.68.refs_1_), channel_id=1, source_target_pairs={{0,2},{2,0},{4,6},{6,4},{8,10},{10,8},{12,14},{14,12},{16,18},{18,... | collective-permute-start | bytes 2359304 | tf_op jit(solution)/shard_map/ppermute | solution.py:79
  50.5 3.9 %collective-permute-start.17 = (bf16[2,128,512]{2,1,0:T(8,128)(2,1)S(1)}, bf16[2,128,512]{2,1,0:T(8,128)(2,1)S(1)}, u32[]{:S(2)}, u32[]{:S(2)}) collective-permute-start(bf16[2,128,512]{2,1,0:T(8,128)(2,1)S(1)} %collective-permute-done.16.refs_2_), channel_id=1, source_target_pairs={{0,2},{2,0},{4,6},{6,4},{8,10},{10,8},{12,14},{14,12},{16,18},{18,... | collective-permute-start | bytes 786440 | tf_op jit(solution)/shard_map/ppermute | solution.py:79
  50.6 7.5 %collective-permute-start.20 = (bf16[2,128,512]{2,1,0:T(8,128)(2,1)S(1)}, bf16[2,128,512]{2,1,0:T(8,128)(2,1)S(1)}, u32[]{:S(2)}, u32[]{:S(2)}) collective-permute-start(bf16[2,128,512]{2,1,0:T(8,128)(2,1)S(1)} %get-tuple-element.82), channel_id=1, source_target_pairs={{0,1},{1,0},{2,3},{3,2},{4,5},{5,4},{6,7},{7,6},{8,9},{9,8},{10,11... | collective-permute-start | bytes 786440 | tf_op jit(solution)/shard_map/ppermute | solution.py:86
  52.6 7.9 %collective-permute-start.26 = (bf16[2,128,768]{2,1,0:T(8,128)(2,1)S(1)}, bf16[2,128,768]{2,1,0:T(8,128)(2,1)S(1)}, u32[]{:S(2)}, u32[]{:S(2)}) collective-permute-start(bf16[2,128,768]{2,1,0:T(8,128)(2,1)S(1)} %get-tuple-element.87.refs_2_), channel_id=1, source_target_pairs={{0,2},{2,0},{4,6},{6,4},{8,10},{10,8},{12,14},{14,12},{16,18},{18,... | collective-permute-start | bytes 1179656 | tf_op jit(solution)/shard_map/ppermute | solution.py:79
  54.3 6.3 %collective-permute-start.27 = (bf16[2,128,768]{2,1,0:T(8,128)(2,1)S(1)}, bf16[2,128,768]{2,1,0:T(8,128)(2,1)S(1)}, u32[]{:S(2)}, u32[]{:S(2)}) collective-permute-start(bf16[2,128,768]{2,1,0:T(8,128)(2,1)S(1)} %get-tuple-element.88.refs_3_), channel_id=1, source_target_pairs={{0,2},{2,0},{4,6},{6,4},{8,10},{10,8},{12,14},{14,12},{16,18},{18,... | collective-permute-start | bytes 1179656 | tf_op jit(solution)/shard_map/ppermute | solution.py:79
  58.1 2.4 %collective-permute-start.21 = (bf16[2,128,512]{2,1,0:T(8,128)(2,1)S(1)}, bf16[2,128,512]{2,1,0:T(8,128)(2,1)S(1)}, u32[]{:S(2)}, u32[]{:S(2)}) collective-permute-start(bf16[2,128,512]{2,1,0:T(8,128)(2,1)S(1)} %collective-permute-done.20.refs_0_), channel_id=1, source_target_pairs={{0,2},{2,0},{4,6},{6,4},{8,10},{10,8},{12,14},{14,12},{16,18},{18,... | collective-permute-start | bytes 786440 | tf_op jit(solution)/shard_map/ppermute | solution.py:79

commit v18 on v16

--- a/solution.py
+++ b/solution.py
@@ -13,8 +13,8 @@
 JOIN_COST = 300000000
 SLOTS_COST = 0
 OWN_COST = 700_000_000
-SOLVED_COST = 500_000_000
-KEEP_COST = 300_000_000
+SOLVED_COST = 400_000_000
+KEEP_COST = 3_000_000_000
 
 
 def dot(first, second):
@@ -67,6 +67,7 @@
     nf = n_face - 1
     fr = leaf_maps.shape[4]
     hr = fr // 2
+    qr = hr // 2
     k = leaf_maps.shape[5] // 3
     half = k // 2
     leaf = leaf_maps[:, 0, 0]
@@ -192,7 +193,7 @@
         mine, _ = halves(p)
         rest = jnp.where(p == q, endsib_ref[:, mine, :], end_ref[:, mine, :])
         for s in range(nf):
-            outs[nf + s][:, :, :k] = rest
+            outs[2 * nf + s][:, :, :k] = rest
         pick_own = column_picker(comp_ref[...], p * k, k)
         pick_sib = column_picker(comp_ref[...], (1 - p) * k, k)
 
@@ -208,9 +209,10 @@
 
         def write_far(s, t, c, picked):
             if c < 2:
-                outs[s][t, :, c * k : (c + 1) * k] = picked
+                for j in range(2):
+                    outs[2 * s + j][t, :, c * k : (c + 1) * k] = picked[j * qr : (j + 1) * qr]
             else:
-                outs[nf + s][t, :, k:] = picked
+                outs[2 * nf + s][t, :, k:] = picked
 
         def col_half(s):
             start = (f + n_face - s - 1) % n_face * fr + p * hr
@@ -237,9 +239,9 @@
 
     kept, *kept_out = call(
         rows_kernel, scalars, [*s_rows, *s_sib, comp, skel_col, end_own, end_sib],
-        [sds((2, fr, 3 * k), BF16)] + [sds((2, hr, 2 * k), BF16)] * (2 * nf),
-    )
-    mixed_far = [face_permute(a, i + 1) for i, a in enumerate(kept_out[nf:])]
+        [sds((2, fr, 3 * k), BF16)] + [sds((2, qr, 2 * k), BF16)] * (2 * nf) + [sds((2, hr, 2 * k), BF16)] * nf,
+    )
+    mixed_far = [face_permute(a, i + 1) for i, a in enumerate(kept_out[2 * nf :])]
 
     def piece(hidden, start, count):
         return stacked(hidden[0][:, start : start + count], hidden[1][:, start : start + count])
@@ -366,13 +368,14 @@
         )
     two_sib = [box_permute(a, 1) for a in two_rows[:1]]
 
-    ends_far = [face_permute(after(a, two_own), i + 1) for i, a in enumerate(kept_out[:nf])]
+    ends_far = [face_permute(after(a, two_own), i // 2 + 1) for i, a in enumerate(kept_out[: 2 * nf])]
     ends_fwd = [box_permute(after(a, solved_one), 1) for a in ends_far]
     two_sib += [box_permute(a, 1) for a in two_rows[1:]]
 
     def level_one_kernel(sc, end_ref, kept_ref, *refs):
-        parts = [refs[i * nf : (i + 1) * nf] for i in range(4)]
-        col_ref, one_ref, w_ref, hid_out, first_out, slots_out, zs = refs[4 * nf :]
+        mixed = refs[:nf], refs[nf : 2 * nf]
+        ends = refs[2 * nf : 4 * nf], refs[4 * nf : 6 * nf]
+        col_ref, one_ref, w_ref, hid_out, first_out, slots_out, zs = refs[6 * nf :]
         p, q, f = sc[0], sc[1], sc[2]
 
         @pl.when(p == q)
@@ -382,13 +385,16 @@
         @pl.when(p != q)
         def _():
             for h, take in enumerate(halves(p)):
-                for part, cols, source in (
-                    (parts[h], slice(2 * k, 3 * k), slice(k, 2 * k)), (parts[2 + h], slice(0, 2 * k), slice(0, 2 * k)),
-                ):
-                    total = kept_ref[:, take, cols]
-                    for ref in part:
-                        total = total + ref[:, :, source]
-                    zs[:, take, cols] = total
+                total = kept_ref[:, take, 2 * k :]
+                for ref in mixed[h]:
+                    total = total + ref[:, :, k:]
+                zs[:, take, 2 * k :] = total
+                for j in range(2):
+                    take = pl.ds(pl.multiple_of((p ^ h) * hr + j * qr, qr), qr)
+                    total = kept_ref[:, take, : 2 * k]
+                    for ref in ends[h][j::2]:
+                        total = total + ref[...]
+                    zs[:, take, : 2 * k] = total
 
         slots = col_ref[pl.ds(pl.multiple_of(f * fr, fr), fr), :]
         right = jnp.where(slots >= k, 1, 0)

time: 63.8 us -> 63.3 us (level)
  waiting for transfers between devices: 11.5 us -> 9.45 us
  starting transfers between devices: 25.6 us -> 27.4 us
    ppermute x21 -> x22, waiting for transfers between devices: 7.19 us -> 6.03 us  [box_permute(): return lax.ppermute(array, 'box', [(b, b ^ mask) for b in range(n_box)])]
    ppermute x5 -> x6, starting transfers between devices: 6.07 us -> 7.17 us  [face_permute(): return lax.ppermute(array, ('box', 'face'), pairs)]
    ppermute x5 -> x6, waiting for transfers between devices: 4.33 us -> 3.42 us  [face_permute(): return lax.ppermute(array, ('box', 'face'), pairs)]
    ppermute x21 -> x22, starting transfers between devices: 19.5 us -> 20.2 us  [box_permute(): return lax.ppermute(array, 'box', [(b, b ^ mask) for b in range(n_box)])]
  transfers between devices with their start and end apart: 26 -> 28, of which waited for: 7 -> 7; matrix products, arithmetic and copies ran while one was open for 0% -> 0% of each run, Pallas kernels for 30% -> 31%
where the time goes in v18:
time: 63.3 us; the launch traced here: 63 us
  starting transfers between devices  27.4 us (43%)
  Pallas kernels  23.4 us (37%)
  waiting for transfers between devices  9.45 us (15%)
  local copies, waits for them, and re-layouts  2.45 us (4%)
    pallas_call x15, Pallas kernels, call(): pl.pallas_call(kernel, in_specs=[pl.BlockSpec(memory_space=pltpu.SMEM)] +...  23.4 us
    ppermute x22, starting transfers between devices, box_permute(): return lax.ppermute(array, 'box', [(b, b ^ mask) for b in range(n_box)])  20.2 us
    ppermute x6, starting transfers between devices, face_permute(): return lax.ppermute(array, ('box', 'face'), pairs)  7.17 us
    ppermute x22, waiting for transfers between devices, box_permute(): return lax.ppermute(array, 'box', [(b, b ^ mask) for b in range(n_box)])  6.03 us
    ppermute x6, waiting for transfers between devices, face_permute(): return lax.ppermute(array, ('box', 'face'), pairs)  3.42 us
    unnamed x12, local copies, waits for them, and re-layouts  2.36 us
  transfers between devices with their start and end apart: 28, of which 7 were waited for; matrix products, arithmetic and copies ran while one was open for 0% of the time, Pallas kernels for 31%

profile of v18, /device:TPU:1, one launch (start us, length us, event | category | flops | bytes accessed | tf_op | source)
XLA Modules:
  0.0 63.0 jit_solution(18146870112917738877)
XLA Ops:
  0.0 0.1 stack.27.sc
  0.1 2.3 %copy-done = bf16[2,1,1,3,256,1536]{5,4,3,2,1,0:T(8,128)(2,1)S(1)} copy-done((bf16[2,1,1,3,256,1536]{5,4,3,2,1,0:T(8,128)(2,1)S(1)}, bf16[2,1,1,3,256,1536]{5,4,3,2,1,0:T(8,128)(2,1)}, u32[]{:S(2)}) %copy-start) | copy-done | bytes 4718616
  2.4 0.7 %shard_map.55 = (bf16[2,256,512]{2,1,0:T(8,128)(2,1)S(1)}, bf16[2,256,512]{2,1,0:T(8,128)(2,1)S(1)}, bf16[2,256,512]{2,1,0:T(8,128)(2,1)S(1)}, bf16[2,256,512]{2,1,0:T(8,128)(2,1)S(1)}, bf16[2,256,512]{2,1,0:T(8,128)(2,1)S(1)}) custom-call(s32[6]{0:T(128)S(1)} %stack.27.sc, bf16[2,3,256,1536]{3,2,1,0:T(8,128)(2,1)S(1)} %bitcast.11), custom_call_target="tpu_custom_call" | custom-call | tf_op jit(solution)/shard_map/pallas_call | solution.py:48
  3.2 0.1 collective-permute-start
  3.3 0.5 collective-permute-start.1
  3.8 0.4 collective-permute-start.3
  4.3 0.8 %shard_map.56 = (s32[1,512]{1,0:T(1,128)S(1)}, s32[512,1]{1,0:T(8,128)S(1)}) custom-call(s32[6]{0:T(128)S(1)} %stack.27.sc, s32[8,512]{1,0:T(8,128)S(1)} %bitcast.18, s32[4,512]{1,0:T(4,128)S(1)} %bitcast.19), custom_call_target="tpu_custom_call" | custom-call | tf_op jit(solution)/shard_map/pallas_call | solution.py:48
  5.2 1.3 %shard_map.57 = (bf16[2,256,512]{2,1,0:T(8,128)(2,1)S(1)}, bf16[2,128,512]{2,1,0:T(8,128)(2,1)S(1)}, bf16[2,128,512]{2,1,0:T(8,128)(2,1)S(1)}) custom-call(s32[6]{0:T(128)S(1)} %stack.27.sc, bf16[2,256,512]{2,1,0:T(8,128)(2,1)S(1)} %get-tuple-element.46.own_ref, bf16[2,256,512]{2,1,0:T(8,128)(2,1)S(1)} %collective-permute-done.sib_ref, ...), custom_call_target="tpu_custom_call" | custom-call | tf_op jit(solution)/shard_map/pallas_call | solution.py:48
  6.4 0.5 collective-permute-start.8
  6.9 2.3 %collective-permute-start.9 = (bf16[2,128,512]{2,1,0:T(8,128)(2,1)S(1)}, bf16[2,128,512]{2,1,0:T(8,128)(2,1)S(1)}, u32[]{:S(2)}, u32[]{:S(2)}) collective-permute-start(bf16[2,128,512]{2,1,0:T(8,128)(2,1)S(1)} %get-tuple-element.64), channel_id=1, source_target_pairs={{0,1},{1,0},{2,3},{3,2},{4,5},{5,4},{6,7},{7,6},{8,9},{9,8},{10,11... | collective-permute-start | bytes 786440 | tf_op jit(solution)/shard_map/ppermute | solution.py:86
  9.3 1.2 %collective-permute-start.11 = (bf16[2,128,512]{2,1,0:T(8,128)(2,1)S(1)}, bf16[2,128,512]{2,1,0:T(8,128)(2,1)S(1)}, u32[]{:S(2)}, u32[]{:S(2)}) collective-permute-start(bf16[2,128,512]{2,1,0:T(8,128)(2,1)S(1)} %bitcast.15), channel_id=1, source_target_pairs={{0,4},{2,6},{4,0},{6,2},{8,12},{10,14},{12,8},{14,10},{16,20},{18,... | collective-permute-start | bytes 786440 | tf_op jit(solution)/shard_map/ppermute | solution.py:79
  10.5 0.2 collective-permute-start.10
  10.7 1.1 %shard_map.58 = (bf16[2,128,1024]{2,1,0:T(8,128)(2,1)S(1)}, bf16[2,128,512]{2,1,0:T(8,128)(2,1)S(1)}, bf16[2,128,512]{2,1,0:T(8,128)(2,1)S(1)}, bf16[2,256,1536]{2,1,0:T(8,128)(2,1)S(1)}) custom-call(s32[6]{0:T(128)S(1)} %stack.27.sc, bf16[2,3,256,1536]{3,2,1,0:T(8,128)(2,1)S(1)} %bitcast.12, s32[1,512]{1,0:T(1,128)S(1)} %get-tuple-element.47.comp_ref.refs_6_), custom_call_target="tpu_custom_call" | custom-call | tf_op jit(solution)/shard_map/pallas_call | solution.py:48
  11.8 1.3 %collective-permute-start.6 = (bf16[2,128,512]{2,1,0:T(8,128)(2,1)S(1)}, bf16[2,128,512]{2,1,0:T(8,128)(2,1)S(1)}, u32[]{:S(2)}, u32[]{:S(2)}) collective-permute-start(bf16[2,128,512]{2,1,0:T(8,128)(2,1)S(1)} %get-tuple-element.59), channel_id=1, source_target_pairs={{0,2},{2,0},{4,6},{6,4},{8,10},{10,8},{12,14},{14,12},{16,18},{18,... | collective-permute-start | bytes 786440 | tf_op jit(solution)/shard_map/ppermute | solution.py:79
  13.2 2.4 %collective-permute-done.9.rest_0_ = bf16[2,128,512]{2,1,0:T(8,128)(2,1)S(1)} collective-permute-done((bf16[2,128,512]{2,1,0:T(8,128)(2,1)S(1)}, bf16[2,128,512]{2,1,0:T(8,128)(2,1)S(1)}, u32[]{:S(2)}, u32[]{:S(2)}) %collective-permute-start.9) | collective-permute-done | bytes 262176 | tf_op jit(solution)/shard_map/ppermute | solution.py:86
  15.6 1.5 %collective-permute-start.7 = (bf16[2,128,512]{2,1,0:T(8,128)(2,1)S(1)}, bf16[2,128,512]{2,1,0:T(8,128)(2,1)S(1)}, u32[]{:S(2)}, u32[]{:S(2)}) collective-permute-start(bf16[2,128,512]{2,1,0:T(8,128)(2,1)S(1)} %get-tuple-element.60), channel_id=1, source_target_pairs={{0,2},{2,0},{4,6},{6,4},{8,10},{10,8},{12,14},{14,12},{16,18},{18,... | collective-permute-start | bytes 786440 | tf_op jit(solution)/shard_map/ppermute | solution.py:79
  17.1 2.9 %shard_map.59 = (bf16[2,256,1536]{2,1,0:T(8,128)(2,1)S(1)}, bf16[2,64,1024]{2,1,0:T(8,128)(2,1)S(1)}, bf16[2,64,1024]{2,1,0:T(8,128)(2,1)S(1)}, bf16[2,128,1024]{2,1,0:T(8,128)(2,1)S(1)}) custom-call(s32[6]{0:T(128)S(1)} %stack.27.sc, bf16[2,256,512]{2,1,0:T(8,128)(2,1)S(1)} %get-tuple-element.52.refs_0_, ...), custom_call_target="tpu_custom_call" | custom-call | tf_op jit(solution)/shard_map/pallas_call | solution.py:48
  19.9 1.9 %collective-permute-start.5 = (bf16[2,128,1024]{2,1,0:T(8,128)(2,1)S(1)}, bf16[2,128,1024]{2,1,0:T(8,128)(2,1)S(1)}, u32[]{:S(2)}, u32[]{:S(2)}) collective-permute-start(bf16[2,128,1024]{2,1,0:T(8,128)(2,1)S(1)} %get-tuple-element.57), channel_id=1, source_target_pairs={{0,1},{1,0},{2,3},{3,2},{4,5},{5,4},{6,7},{7,6},{8,9},{9,8},{10,11... | collective-permute-start | bytes 1572872 | tf_op jit(solution)/shard_map/ppermute | solution.py:86
  21.8 0.3 collective-permute-start.12
  22.1 0.2 collective-permute-start.13
  22.3 0.6 %shard_map.60.w_ref = bf16[2,512,512]{2,1,0:T(8,128)(2,1)S(1)} custom-call(s32[6]{0:T(128)S(1)} %stack.27.sc, bf16[2,256,512]{2,1,0:T(8,128)(2,1)S(1)} %bitcast.14, bf16[2,256,512]{2,1,0:T(8,128)(2,1)S(1)} %collective-permute-done.8.refs_1_), custom_call_target="tpu_custom_call" | custom-call | tf_op jit(solution)/shard_map/pallas_call | solution.py:48
  23.0 1.4 %shard_map.61 = (f32[2,128,1024]{2,1,0:T(8,128)S(1)}, bf16[2,128,512]{2,1,0:T(8,128)(2,1)S(1)}) custom-call(s32[6]{0:T(128)S(1)} %stack.27.sc, bf16[2,128,1024]{2,1,0:T(8,128)(2,1)S(1)} %get-tuple-element.58.keep_ref, bf16[2,128,512]{2,1,0:T(8,128)(2,1)S(1)} %collective-permute-done.6.couple_ref, bf16[2,128,512]{2,1,0:T(8,128)(2,1)S(1)} %collective-permute-done.7.slots_ref, ...), custom_call_target="tpu_custom_call" | custom-call | flops 700000000 | tf_op jit(solution)/shard_map/pallas_call | solution.py:48
  24.4 1.1 %shard_map.62 = (bf16[2,128,512]{2,1,0:T(8,128)(2,1)S(1)}, bf16[2,128,256]{2,1,0:T(8,128)(2,1)S(1)}, bf16[2,128,256]{2,1,0:T(8,128)(2,1)S(1)}) custom-call(s32[6]{0:T(128)S(1)} %stack.27.sc, f32[2,128,1024]{2,1,0:T(8,128)S(1)} %get-tuple-element.62.acc_ref, bf16[2,128,512]{2,1,0:T(8,128)(2,1)S(1)} %get-tuple-element.63.hid_ref, ...), custom_call_target="tpu_custom_call" | custom-call | tf_op jit(solution)/shard_map/pallas_call | solution.py:48
  25.5 1.3 %collective-permute-start.14 = (bf16[2,128,256]{2,1,0:T(8,128)(2,1)S(1)}, bf16[2,128,256]{2,1,0:T(8,128)(2,1)S(1)}, u32[]{:S(2)}, u32[]{:S(2)}) collective-permute-start(bf16[2,128,256]{2,1,0:T(8,128)(2,1)S(1)} %get-tuple-element.71), channel_id=1, source_target_pairs={{0,4},{2,6},{4,0},{6,2},{8,12},{10,14},{12,8},{14,10},{16,20},{18,... | collective-permute-start | bytes 393224 | tf_op jit(solution)/shard_map/ppermute | solution.py:79
  26.9 3.5 %collective-permute-done.14.x_ref = bf16[2,128,256]{2,1,0:T(8,128)(2,1)S(1)} collective-permute-done((bf16[2,128,256]{2,1,0:T(8,128)(2,1)S(1)}, bf16[2,128,256]{2,1,0:T(8,128)(2,1)S(1)}, u32[]{:S(2)}, u32[]{:S(2)}) %collective-permute-start.14) | collective-permute-done | bytes 131104 | tf_op jit(solution)/shard_map/ppermute | solution.py:79
  30.4 0.6 shard_map.63.own_ref
  30.9 1.1 %collective-permute-start.22 = (bf16[2,128,768]{2,1,0:T(8,128)(2,1)S(1)}, bf16[2,128,768]{2,1,0:T(8,128)(2,1)S(1)}, u32[]{:S(2)}, u32[]{:S(2)}) collective-permute-start(bf16[2,128,768]{2,1,0:T(8,128)(2,1)S(1)} %shard_map.63.own_ref), channel_id=1, source_target_pairs={{0,4},{2,6},{4,0},{6,2},{8,12},{10,14},{12,8},{14,10},{16,20},{18,... | collective-permute-start | bytes 1179656 | tf_op jit(solution)/shard_map/ppermute | solution.py:79
  32.1 1.2 %collective-permute-start.23 = (bf16[2,128,768]{2,1,0:T(8,128)(2,1)S(1)}, bf16[2,128,768]{2,1,0:T(8,128)(2,1)S(1)}, u32[]{:S(2)}, u32[]{:S(2)}) collective-permute-start(bf16[2,128,768]{2,1,0:T(8,128)(2,1)S(1)} %shard_map.63.own_ref), channel_id=1, source_target_pairs={{0,1},{1,0},{2,3},{3,2},{4,5},{5,4},{6,7},{7,6},{8,9},{9,8},{10,11... | collective-permute-start | bytes 1179656 | tf_op jit(solution)/shard_map/ppermute | solution.py:86
  33.3 0.1 collective-permute-done.5.rest_4_.refs_0_
  33.4 1.8 %collective-permute-start.15 = (bf16[2,128,1024]{2,1,0:T(8,128)(2,1)S(1)}, bf16[2,128,1024]{2,1,0:T(8,128)(2,1)S(1)}, u32[]{:S(2)}, u32[]{:S(2)}) collective-permute-start(bf16[2,128,1024]{2,1,0:T(8,128)(2,1)S(1)} %collective-permute-done.5.rest_4_.refs_0_), channel_id=1, source_target_pairs={{0,2},{2,0},{4,6},{6,4},{8,10},{10,8},{12,14},{14,12},{16,18},{18,... | collective-permute-start | bytes 1572872 | tf_op jit(solution)/shard_map/ppermute | solution.py:79
  35.2 0.5 collective-permute-start.21
  35.7 1.4 %collective-permute-done.20.refs_2_ = bf16[2,128,512]{2,1,0:T(8,128)(2,1)S(1)} collective-permute-done((bf16[2,128,512]{2,1,0:T(8,128)(2,1)S(1)}, bf16[2,128,512]{2,1,0:T(8,128)(2,1)S(1)}, u32[]{:S(2)}, u32[]{:S(2)}) %collective-permute-start.20) | collective-permute-done | bytes 262176 | tf_op jit(solution)/shard_map/ppermute | solution.py:79
  37.1 0.4 collective-permute-done.21.refs_3_
  37.5 0.7 %shard_map.65.refs_8_ = bf16[2,512,512]{2,1,0:T(8,128)(2,1)S(1)} custom-call(s32[6]{0:T(128)S(1)} %stack.27.sc, bf16[2,128,512]{2,1,0:T(8,128)(2,1)S(1)} %bitcast.17, bf16[2,128,512]{2,1,0:T(8,128)(2,1)S(1)} %collective-permute-done.11.refs_1_, bf16[2,128,512]{2,1,0:T(8,128)(2,1)S(1)} %collective-permute-done.20.refs_2_, ...), custom_call_target="tpu_custom_call" | custom-call | tf_op jit(solution)/shard_map/pallas_call | solution.py:48
  38.2 0.3 collective-permute-start.16
  38.5 1.2 %collective-permute-start.17 = (bf16[2,64,1024]{2,1,0:T(8,128)(2,1)S(1)}, bf16[2,64,1024]{2,1,0:T(8,128)(2,1)S(1)}, u32[]{:S(2)}, u32[]{:S(2)}) collective-permute-start(bf16[2,64,1024]{2,1,0:T(8,128)(2,1)S(1)} %get-tuple-element.76), channel_id=1, source_target_pairs={{0,1},{1,0},{2,3},{3,2},{4,5},{5,4},{6,7},{7,6},{8,9},{9,8},{10,11... | collective-permute-start | bytes 786440 | tf_op jit(solution)/shard_map/ppermute | solution.py:86
  39.7 0.7 %collective-permute-done.22.x_ref = bf16[2,128,768]{2,1,0:T(8,128)(2,1)S(1)} collective-permute-done((bf16[2,128,768]{2,1,0:T(8,128)(2,1)S(1)}, bf16[2,128,768]{2,1,0:T(8,128)(2,1)S(1)}, u32[]{:S(2)}, u32[]{:S(2)}) %collective-permute-start.22) | collective-permute-done | bytes 393248 | tf_op jit(solution)/shard_map/ppermute | solution.py:79
  40.4 0.6 shard_map.67.refs_0_
  41.1 0.9 %collective-permute-start.24 = (bf16[2,128,768]{2,1,0:T(8,128)(2,1)S(1)}, bf16[2,128,768]{2,1,0:T(8,128)(2,1)S(1)}, u32[]{:S(2)}, u32[]{:S(2)}) collective-permute-start(bf16[2,128,768]{2,1,0:T(8,128)(2,1)S(1)} %collective-permute-done.23.own_ref), channel_id=1, source_target_pairs={{0,4},{2,6},{4,0},{6,2},{8,12},{10,14},{12,8},{14,10},{16,20},{18,... | collective-permute-start | bytes 1179656 | tf_op jit(solution)/shard_map/ppermute | solution.py:79
  42.0 4.2 %collective-permute-start.25 = (bf16[2,128,1536]{2,1,0:T(8,128)(2,1)S(1)}, bf16[2,128,1536]{2,1,0:T(8,128)(2,1)S(1)}, u32[]{:S(2)}, u32[]{:S(2)}) collective-permute-start(bf16[2,128,1536]{2,1,0:T(8,128)(2,1)S(1)} %shard_map.67.refs_0_), channel_id=1, source_target_pairs={{0,2},{2,0},{4,6},{6,4},{8,10},{10,8},{12,14},{14,12},{16,18},{18,... | collective-permute-start | bytes 2359304 | tf_op jit(solution)/shard_map/ppermute | solution.py:79
  46.2 4.2 %shard_map.64.refs_7_ = bf16[2,512,1536]{2,1,0:T(8,128)(2,1)S(1)} custom-call(s32[6]{0:T(128)S(1)} %stack.27.sc, bf16[2,512,512]{2,1,0:T(8,128)(2,1)S(1)} %shard_map.60.w_ref, bf16[2,256,512]{2,1,0:T(8,128)(2,1)S(1)} %get-tuple-element.48.end_ref.refs_8_.own_ref, bf16[2,256,512]{2,1,0:T(8,128)(2,1)S(1)} %collective-permute-done.4.refs_9_.endsib_ref.sib_ref, ...), custom_call_target="tpu_custom_call" | custom-call | flops 400000000 | tf_op jit(solution)/shard_map/pallas_call | solution.py:48
  50.5 0.9 %collective-permute-start.18 = (bf16[2,64,1024]{2,1,0:T(8,128)(2,1)S(1)}, bf16[2,64,1024]{2,1,0:T(8,128)(2,1)S(1)}, u32[]{:S(2)}, u32[]{:S(2)}) collective-permute-start(bf16[2,64,1024]{2,1,0:T(8,128)(2,1)S(1)} %collective-permute-done.16.refs_2_), channel_id=1, source_target_pairs={{0,2},{2,0},{4,6},{6,4},{8,10},{10,8},{12,14},{14,12},{16,18},{18,... | collective-permute-start | bytes 786440 | tf_op jit(solution)/shard_map/ppermute | solution.py:79
  51.4 0.9 %collective-permute-done.17.refs_3_ = bf16[2,64,1024]{2,1,0:T(8,128)(2,1)S(1)} collective-permute-done((bf16[2,64,1024]{2,1,0:T(8,128)(2,1)S(1)}, bf16[2,64,1024]{2,1,0:T(8,128)(2,1)S(1)}, u32[]{:S(2)}, u32[]{:S(2)}) %collective-permute-start.17) | collective-permute-done | bytes 262176 | tf_op jit(solution)/shard_map/ppermute | solution.py:86
  52.3 2.6 %collective-permute-start.19 = (bf16[2,64,1024]{2,1,0:T(8,128)(2,1)S(1)}, bf16[2,64,1024]{2,1,0:T(8,128)(2,1)S(1)}, u32[]{:S(2)}, u32[]{:S(2)}) collective-permute-start(bf16[2,64,1024]{2,1,0:T(8,128)(2,1)S(1)} %collective-permute-done.17.refs_3_), channel_id=1, source_target_pairs={{0,2},{2,0},{4,6},{6,4},{8,10},{10,8},{12,14},{14,12},{16,18},{18,... | collective-permute-start | bytes 786440 | tf_op jit(solution)/shard_map/ppermute | solution.py:79
  54.8 0.6 %shard_map.68 = (bf16[2,128,768]{2,1,0:T(8,128)(2,1)S(1)}, bf16[2,128,768]{2,1,0:T(8,128)(2,1)S(1)}) custom-call(s32[6]{0:T(128)S(1)} %stack.27.sc, bf16[2,128,768]{2,1,0:T(8,128)(2,1)S(1)} %collective-permute-done.23.own_ref, bf16[2,128,768]{2,1,0:T(8,128)(2,1)S(1)} %collective-permute-done.24.x_ref), custom_call_target="tpu_custom_call" | custom-call | tf_op jit(solution)/shard_map/pallas_call | solution.py:48
  55.6 0.5 collective-permute-start.27
  56.1 3.4 %shard_map.66 = (bf16[2,512,512]{2,1,0:T(8,128)(2,1)S(1)}, bf16[512,512]{1,0:T(8,128)(2,1)S(1)}, bf16[512,512]{1,0:T(8,128)(2,1)S(1)}) custom-call(s32[6]{0:T(128)S(1)} %stack.27.sc, bf16[2,256,1536]{2,1,0:T(8,128)(2,1)S(1)} %get-tuple-element.51.end_ref, bf16[2,256,1536]{2,1,0:T(8,128)(2,1)S(1)} %get-tuple-element.56.kept_ref, ...), custom_call_target="tpu_custom_call" | custom-call | flops 3000000000 | tf_op jit(solution)/shard_map/pallas_call | solution.py:48
  59.5 3.4 %shard_map.69 = bf16[2,1,256,1536]{3,2,1,0:T(8,128)(2,1)} custom-call(s32[6]{0:T(128)S(1)} %stack.27.sc, bf16[2,512,512]{2,1,0:T(8,128)(2,1)S(1)} %get-tuple-element.79.hid_ref, bf16[512,512]{1,0:T(8,128)(2,1)S(1)} %get-tuple-element.80.first_ref, bf16[512,512]{1,0:T(8,128)(2,1)S(1)} %get-tuple-element.81.slots_ref, ...), custom_call_target="tpu_custom_call" | custom-call | tf_op jit(solution)/shard_map/pallas_call | solution.py:48
  (36 shorter events, 0.3 us)
Async XLA Ops:
  0.0 4.3 %copy-start.4 = (s32[1,8,512]{2,1,0:T(8,128)S(1)}, s32[1,8,512]{2,1,0:T(8,128)}, u32[]{:S(2)}) copy-start(s32[1,8,512]{2,1,0:T(8,128)} %param.8) | copy-start | bytes 49156
  0.1 2.3 %copy-start = (bf16[2,1,1,3,256,1536]{5,4,3,2,1,0:T(8,128)(2,1)S(1)}, bf16[2,1,1,3,256,1536]{5,4,3,2,1,0:T(8,128)(2,1)}, u32[]{:S(2)}) copy-start(bf16[2,1,1,3,256,1536]{5,4,3,2,1,0:T(8,128)(2,1)} %param.5) | copy-start | bytes 14155780
  2.4 1.9 %copy-start.5 = (s32[1,4,512]{2,1,0:T(4,128)S(1)}, s32[1,4,512]{2,1,0:T(4,128)}, u32[]{:S(2)}) copy-start(s32[1,4,512]{2,1,0:T(4,128)} %param.9) | copy-start | bytes 24580
  2.4 8.3 %copy-start.1 = (bf16[2,1,1,3,256,1536]{5,4,3,2,1,0:T(8,128)(2,1)S(1)}, bf16[2,1,1,3,256,1536]{5,4,3,2,1,0:T(8,128)(2,1)}, u32[]{:S(2)}) copy-start(bf16[2,1,1,3,256,1536]{5,4,3,2,1,0:T(8,128)(2,1)} %param.5) | copy-start | bytes 14155780
  3.1 3.3 %copy-start.2 = (bf16[2,1,256,512]{3,2,1,0:T(8,128)(2,1)S(1)}, bf16[2,1,256,512]{3,2,1,0:T(8,128)(2,1)}, u32[]{:S(2)}) copy-start(bf16[2,1,256,512]{3,2,1,0:T(8,128)(2,1)} %param.6) | copy-start | bytes 1572868
  3.2 6.1 %copy-start.3 = (bf16[2,1,128,512]{3,2,1,0:T(8,128)(2,1)S(1)}, bf16[2,1,128,512]{3,2,1,0:T(8,128)(2,1)}, u32[]{:S(2)}) copy-start(bf16[2,1,128,512]{3,2,1,0:T(8,128)(2,1)} %param.7) | copy-start | bytes 786436
  3.2 2.0 %collective-permute-start = (bf16[2,256,512]{2,1,0:T(8,128)(2,1)S(1)}, bf16[2,256,512]{2,1,0:T(8,128)(2,1)S(1)}, u32[]{:S(2)}, u32[]{:S(2)}) collective-permute-start(bf16[2,256,512]{2,1,0:T(8,128)(2,1)S(1)} %get-tuple-element.46.own_ref), channel_id=1, source_target_pairs={{0,2},{2,0},{4,6},{6,4},{8,10},{10,8},{12,14},{14,12},{16,18},{18,... | collective-permute-start | bytes 1572872 | tf_op jit(solution)/shard_map/ppermute | solution.py:79
  3.3 3.6 %collective-permute-start.1 = (bf16[2,256,512]{2,1,0:T(8,128)(2,1)S(1)}, bf16[2,256,512]{2,1,0:T(8,128)(2,1)S(1)}, u32[]{:S(2)}, u32[]{:S(2)}) collective-permute-start(bf16[2,256,512]{2,1,0:T(8,128)(2,1)S(1)} %get-tuple-element.52.refs_0_), channel_id=1, source_target_pairs={{0,2},{2,0},{4,6},{6,4},{8,10},{10,8},{12,14},{14,12},{16,18},{18,... | collective-permute-start | bytes 1572872 | tf_op jit(solution)/shard_map/ppermute | solution.py:79
  3.7 5.5 %collective-permute-start.2 = (bf16[2,256,512]{2,1,0:T(8,128)(2,1)S(1)}, bf16[2,256,512]{2,1,0:T(8,128)(2,1)S(1)}, u32[]{:S(2)}, u32[]{:S(2)}) collective-permute-start(bf16[2,256,512]{2,1,0:T(8,128)(2,1)S(1)} %get-tuple-element.53.refs_1_), channel_id=1, source_target_pairs={{0,2},{2,0},{4,6},{6,4},{8,10},{10,8},{12,14},{14,12},{16,18},{18,... | collective-permute-start | bytes 1572872 | tf_op jit(solution)/shard_map/ppermute | solution.py:79
  3.8 6.7 %collective-permute-start.3 = (bf16[2,256,512]{2,1,0:T(8,128)(2,1)S(1)}, bf16[2,256,512]{2,1,0:T(8,128)(2,1)S(1)}, u32[]{:S(2)}, u32[]{:S(2)}) collective-permute-start(bf16[2,256,512]{2,1,0:T(8,128)(2,1)S(1)} %get-tuple-element.54.refs_2_), channel_id=1, source_target_pairs={{0,2},{2,0},{4,6},{6,4},{8,10},{10,8},{12,14},{14,12},{16,18},{18,... | collective-permute-start | bytes 1572872 | tf_op jit(solution)/shard_map/ppermute | solution.py:79
  4.3 7.6 %collective-permute-start.4 = (bf16[2,256,512]{2,1,0:T(8,128)(2,1)S(1)}, bf16[2,256,512]{2,1,0:T(8,128)(2,1)S(1)}, u32[]{:S(2)}, u32[]{:S(2)}) collective-permute-start(bf16[2,256,512]{2,1,0:T(8,128)(2,1)S(1)} %get-tuple-element.48.end_ref.refs_8_.own_ref), channel_id=1, source_target_pairs={{0,2},{2,0},{4,6},{6,4},{8,10},{10,8},{12,14},{14,12},{16,18},{18,... | collective-permute-start | bytes 1572872 | tf_op jit(solution)/shard_map/ppermute | solution.py:79
  6.4 15.7 %collective-permute-start.8 = (bf16[2,256,512]{2,1,0:T(8,128)(2,1)S(1)}, bf16[2,256,512]{2,1,0:T(8,128)(2,1)S(1)}, u32[]{:S(2)}, u32[]{:S(2)}) collective-permute-start(bf16[2,256,512]{2,1,0:T(8,128)(2,1)S(1)} %bitcast.13), channel_id=1, source_target_pairs={{0,2},{2,0},{4,6},{6,4},{8,10},{10,8},{12,14},{14,12},{16,18},{18,... | collective-permute-start | bytes 1572872 | tf_op jit(solution)/shard_map/ppermute | solution.py:79
  6.9 8.6 %collective-permute-start.9 = (bf16[2,128,512]{2,1,0:T(8,128)(2,1)S(1)}, bf16[2,128,512]{2,1,0:T(8,128)(2,1)S(1)}, u32[]{:S(2)}, u32[]{:S(2)}) collective-permute-start(bf16[2,128,512]{2,1,0:T(8,128)(2,1)S(1)} %get-tuple-element.64), channel_id=1, source_target_pairs={{0,1},{1,0},{2,3},{3,2},{4,5},{5,4},{6,7},{7,6},{8,9},{9,8},{10,11... | collective-permute-start | bytes 786440 | tf_op jit(solution)/shard_map/ppermute | solution.py:86
  9.3 10.7 %collective-permute-start.11 = (bf16[2,128,512]{2,1,0:T(8,128)(2,1)S(1)}, bf16[2,128,512]{2,1,0:T(8,128)(2,1)S(1)}, u32[]{:S(2)}, u32[]{:S(2)}) collective-permute-start(bf16[2,128,512]{2,1,0:T(8,128)(2,1)S(1)} %bitcast.15), channel_id=1, source_target_pairs={{0,4},{2,6},{4,0},{6,2},{8,12},{10,14},{12,8},{14,10},{16,20},{18,... | collective-permute-start | bytes 786440 | tf_op jit(solution)/shard_map/ppermute | solution.py:79
  10.5 11.3 %collective-permute-start.10 = (bf16[2,128,512]{2,1,0:T(8,128)(2,1)S(1)}, bf16[2,128,512]{2,1,0:T(8,128)(2,1)S(1)}, u32[]{:S(2)}, u32[]{:S(2)}) collective-permute-start(bf16[2,128,512]{2,1,0:T(8,128)(2,1)S(1)} %get-tuple-element.65), channel_id=1, source_target_pairs={{0,1},{1,0},{2,3},{3,2},{4,5},{5,4},{6,7},{7,6},{8,9},{9,8},{10,11... | collective-permute-start | bytes 786440 | tf_op jit(solution)/shard_map/ppermute | solution.py:86
  11.8 11.1 %collective-permute-start.6 = (bf16[2,128,512]{2,1,0:T(8,128)(2,1)S(1)}, bf16[2,128,512]{2,1,0:T(8,128)(2,1)S(1)}, u32[]{:S(2)}, u32[]{:S(2)}) collective-permute-start(bf16[2,128,512]{2,1,0:T(8,128)(2,1)S(1)} %get-tuple-element.59), channel_id=1, source_target_pairs={{0,2},{2,0},{4,6},{6,4},{8,10},{10,8},{12,14},{14,12},{16,18},{18,... | collective-permute-start | bytes 786440 | tf_op jit(solution)/shard_map/ppermute | solution.py:79
  15.6 7.4 %collective-permute-start.7 = (bf16[2,128,512]{2,1,0:T(8,128)(2,1)S(1)}, bf16[2,128,512]{2,1,0:T(8,128)(2,1)S(1)}, u32[]{:S(2)}, u32[]{:S(2)}) collective-permute-start(bf16[2,128,512]{2,1,0:T(8,128)(2,1)S(1)} %get-tuple-element.60), channel_id=1, source_target_pairs={{0,2},{2,0},{4,6},{6,4},{8,10},{10,8},{12,14},{14,12},{16,18},{18,... | collective-permute-start | bytes 786440 | tf_op jit(solution)/shard_map/ppermute | solution.py:79
  19.9 13.5 %collective-permute-start.5 = (bf16[2,128,1024]{2,1,0:T(8,128)(2,1)S(1)}, bf16[2,128,1024]{2,1,0:T(8,128)(2,1)S(1)}, u32[]{:S(2)}, u32[]{:S(2)}) collective-permute-start(bf16[2,128,1024]{2,1,0:T(8,128)(2,1)S(1)} %get-tuple-element.57), channel_id=1, source_target_pairs={{0,1},{1,0},{2,3},{3,2},{4,5},{5,4},{6,7},{7,6},{8,9},{9,8},{10,11... | collective-permute-start | bytes 1572872 | tf_op jit(solution)/shard_map/ppermute | solution.py:86
  21.8 2.6 %collective-permute-start.12 = (bf16[2,128,512]{2,1,0:T(8,128)(2,1)S(1)}, bf16[2,128,512]{2,1,0:T(8,128)(2,1)S(1)}, u32[]{:S(2)}, u32[]{:S(2)}) collective-permute-start(bf16[2,128,512]{2,1,0:T(8,128)(2,1)S(1)} %collective-permute-done.9.rest_0_), channel_id=1, source_target_pairs={{0,2},{2,0},{4,6},{6,4},{8,10},{10,8},{12,14},{14,12},{16,18},{18,... | collective-permute-start | bytes 786440 | tf_op jit(solution)/shard_map/ppermute | solution.py:79
  22.1 2.2 %collective-permute-start.13 = (bf16[2,128,512]{2,1,0:T(8,128)(2,1)S(1)}, bf16[2,128,512]{2,1,0:T(8,128)(2,1)S(1)}, u32[]{:S(2)}, u32[]{:S(2)}) collective-permute-start(bf16[2,128,512]{2,1,0:T(8,128)(2,1)S(1)} %collective-permute-done.10.rest_1_), channel_id=1, source_target_pairs={{0,2},{2,0},{4,6},{6,4},{8,10},{10,8},{12,14},{14,12},{16,18},{18,... | collective-permute-start | bytes 786440 | tf_op jit(solution)/shard_map/ppermute | solution.py:79
  25.5 4.8 %collective-permute-start.14 = (bf16[2,128,256]{2,1,0:T(8,128)(2,1)S(1)}, bf16[2,128,256]{2,1,0:T(8,128)(2,1)S(1)}, u32[]{:S(2)}, u32[]{:S(2)}) collective-permute-start(bf16[2,128,256]{2,1,0:T(8,128)(2,1)S(1)} %get-tuple-element.71), channel_id=1, source_target_pairs={{0,4},{2,6},{4,0},{6,2},{8,12},{10,14},{12,8},{14,10},{16,20},{18,... | collective-permute-start | bytes 393224 | tf_op jit(solution)/shard_map/ppermute | solution.py:79
  30.9 9.5 %collective-permute-start.22 = (bf16[2,128,768]{2,1,0:T(8,128)(2,1)S(1)}, bf16[2,128,768]{2,1,0:T(8,128)(2,1)S(1)}, u32[]{:S(2)}, u32[]{:S(2)}) collective-permute-start(bf16[2,128,768]{2,1,0:T(8,128)(2,1)S(1)} %shard_map.63.own_ref), channel_id=1, source_target_pairs={{0,4},{2,6},{4,0},{6,2},{8,12},{10,14},{12,8},{14,10},{16,20},{18,... | collective-permute-start | bytes 1179656 | tf_op jit(solution)/shard_map/ppermute | solution.py:79
  32.1 9.0 %collective-permute-start.23 = (bf16[2,128,768]{2,1,0:T(8,128)(2,1)S(1)}, bf16[2,128,768]{2,1,0:T(8,128)(2,1)S(1)}, u32[]{:S(2)}, u32[]{:S(2)}) collective-permute-start(bf16[2,128,768]{2,1,0:T(8,128)(2,1)S(1)} %shard_map.63.own_ref), channel_id=1, source_target_pairs={{0,1},{1,0},{2,3},{3,2},{4,5},{5,4},{6,7},{7,6},{8,9},{9,8},{10,11... | collective-permute-start | bytes 1179656 | tf_op jit(solution)/shard_map/ppermute | solution.py:86
  33.4 12.8 %collective-permute-start.15 = (bf16[2,128,1024]{2,1,0:T(8,128)(2,1)S(1)}, bf16[2,128,1024]{2,1,0:T(8,128)(2,1)S(1)}, u32[]{:S(2)}, u32[]{:S(2)}) collective-permute-start(bf16[2,128,1024]{2,1,0:T(8,128)(2,1)S(1)} %collective-permute-done.5.rest_4_.refs_0_), channel_id=1, source_target_pairs={{0,2},{2,0},{4,6},{6,4},{8,10},{10,8},{12,14},{14,12},{16,18},{18,... | collective-permute-start | bytes 1572872 | tf_op jit(solution)/shard_map/ppermute | solution.py:79
  35.2 1.9 %collective-permute-start.20 = (bf16[2,128,512]{2,1,0:T(8,128)(2,1)S(1)}, bf16[2,128,512]{2,1,0:T(8,128)(2,1)S(1)}, u32[]{:S(2)}, u32[]{:S(2)}) collective-permute-start(bf16[2,128,512]{2,1,0:T(8,128)(2,1)S(1)} %bitcast.16), channel_id=1, source_target_pairs={{0,2},{2,0},{4,6},{6,4},{8,10},{10,8},{12,14},{14,12},{16,18},{18,... | collective-permute-start | bytes 786440 | tf_op jit(solution)/shard_map/ppermute | solution.py:79
  35.2 2.3 %collective-permute-start.21 = (bf16[2,128,512]{2,1,0:T(8,128)(2,1)S(1)}, bf16[2,128,512]{2,1,0:T(8,128)(2,1)S(1)}, u32[]{:S(2)}, u32[]{:S(2)}) collective-permute-start(bf16[2,128,512]{2,1,0:T(8,128)(2,1)S(1)} %collective-permute-done.11.refs_1_), channel_id=1, source_target_pairs={{0,2},{2,0},{4,6},{6,4},{8,10},{10,8},{12,14},{14,12},{16,18},{18,... | collective-permute-start | bytes 786440 | tf_op jit(solution)/shard_map/ppermute | solution.py:79
  38.2 12.3 %collective-permute-start.16 = (bf16[2,64,1024]{2,1,0:T(8,128)(2,1)S(1)}, bf16[2,64,1024]{2,1,0:T(8,128)(2,1)S(1)}, u32[]{:S(2)}, u32[]{:S(2)}) collective-permute-start(bf16[2,64,1024]{2,1,0:T(8,128)(2,1)S(1)} %get-tuple-element.74), channel_id=1, source_target_pairs={{0,1},{1,0},{2,3},{3,2},{4,5},{5,4},{6,7},{7,6},{8,9},{9,8},{10,11... | collective-permute-start | bytes 786440 | tf_op jit(solution)/shard_map/ppermute | solution.py:86
  38.5 13.7 %collective-permute-start.17 = (bf16[2,64,1024]{2,1,0:T(8,128)(2,1)S(1)}, bf16[2,64,1024]{2,1,0:T(8,128)(2,1)S(1)}, u32[]{:S(2)}, u32[]{:S(2)}) collective-permute-start(bf16[2,64,1024]{2,1,0:T(8,128)(2,1)S(1)} %get-tuple-element.76), channel_id=1, source_target_pairs={{0,1},{1,0},{2,3},{3,2},{4,5},{5,4},{6,7},{7,6},{8,9},{9,8},{10,11... | collective-permute-start | bytes 786440 | tf_op jit(solution)/shard_map/ppermute | solution.py:86
  41.1 13.8 %collective-permute-start.24 = (bf16[2,128,768]{2,1,0:T(8,128)(2,1)S(1)}, bf16[2,128,768]{2,1,0:T(8,128)(2,1)S(1)}, u32[]{:S(2)}, u32[]{:S(2)}) collective-permute-start(bf16[2,128,768]{2,1,0:T(8,128)(2,1)S(1)} %collective-permute-done.23.own_ref), channel_id=1, source_target_pairs={{0,4},{2,6},{4,0},{6,2},{8,12},{10,14},{12,8},{14,10},{16,20},{18,... | collective-permute-start | bytes 1179656 | tf_op jit(solution)/shard_map/ppermute | solution.py:79
  42.0 17.4 %collective-permute-start.25 = (bf16[2,128,1536]{2,1,0:T(8,128)(2,1)S(1)}, bf16[2,128,1536]{2,1,0:T(8,128)(2,1)S(1)}, u32[]{:S(2)}, u32[]{:S(2)}) collective-permute-start(bf16[2,128,1536]{2,1,0:T(8,128)(2,1)S(1)} %shard_map.67.refs_0_), channel_id=1, source_target_pairs={{0,2},{2,0},{4,6},{6,4},{8,10},{10,8},{12,14},{14,12},{16,18},{18,... | collective-permute-start | bytes 2359304 | tf_op jit(solution)/shard_map/ppermute | solution.py:79
  50.5 5.6 %collective-permute-start.18 = (bf16[2,64,1024]{2,1,0:T(8,128)(2,1)S(1)}, bf16[2,64,1024]{2,1,0:T(8,128)(2,1)S(1)}, u32[]{:S(2)}, u32[]{:S(2)}) collective-permute-start(bf16[2,64,1024]{2,1,0:T(8,128)(2,1)S(1)} %collective-permute-done.16.refs_2_), channel_id=1, source_target_pairs={{0,2},{2,0},{4,6},{6,4},{8,10},{10,8},{12,14},{14,12},{16,18},{18,... | collective-permute-start | bytes 786440 | tf_op jit(solution)/shard_map/ppermute | solution.py:79
  52.3 3.8 %collective-permute-start.19 = (bf16[2,64,1024]{2,1,0:T(8,128)(2,1)S(1)}, bf16[2,64,1024]{2,1,0:T(8,128)(2,1)S(1)}, u32[]{:S(2)}, u32[]{:S(2)}) collective-permute-start(bf16[2,64,1024]{2,1,0:T(8,128)(2,1)S(1)} %collective-permute-done.17.refs_3_), channel_id=1, source_target_pairs={{0,2},{2,0},{4,6},{6,4},{8,10},{10,8},{12,14},{14,12},{16,18},{18,... | collective-permute-start | bytes 786440 | tf_op jit(solution)/shard_map/ppermute | solution.py:79
  55.5 4.0 %collective-permute-start.26 = (bf16[2,128,768]{2,1,0:T(8,128)(2,1)S(1)}, bf16[2,128,768]{2,1,0:T(8,128)(2,1)S(1)}, u32[]{:S(2)}, u32[]{:S(2)}) collective-permute-start(bf16[2,128,768]{2,1,0:T(8,128)(2,1)S(1)} %get-tuple-element.85.refs_1_), channel_id=1, source_target_pairs={{0,2},{2,0},{4,6},{6,4},{8,10},{10,8},{12,14},{14,12},{16,18},{18,... | collective-permute-start | bytes 1179656 | tf_op jit(solution)/shard_map/ppermute | solution.py:79
  55.6 3.9 %collective-permute-start.27 = (bf16[2,128,768]{2,1,0:T(8,128)(2,1)S(1)}, bf16[2,128,768]{2,1,0:T(8,128)(2,1)S(1)}, u32[]{:S(2)}, u32[]{:S(2)}) collective-permute-start(bf16[2,128,768]{2,1,0:T(8,128)(2,1)S(1)} %get-tuple-element.86.refs_2_), channel_id=1, source_target_pairs={{0,2},{2,0},{4,6},{6,4},{8,10},{10,8},{12,14},{14,12},{16,18},{18,... | collective-permute-start | bytes 1179656 | tf_op jit(solution)/shard_map/ppermute | solution.py:79

commit v19 on v18

--- a/solution.py
+++ b/solution.py
@@ -355,22 +355,11 @@
     two_shape = [sds((2, hr, 3 * k), BF16)]
     two_rows = call(join_kernel, after(scalars, weight_two), [two_own, two_x], two_shape, cost=JOIN_COST)
     two_xy = [box_permute(after(a, *two_rows), 2) for a in two_y]
-
-    def join_far_kernel(sc, own_ref, x_ref, *refs):
-        join_kernel(sc, own_ref, x_ref, refs[-1])
-        for h in range(2):
-            refs[h][...] = refs[-1][:, :, h * 3 * half : (h + 1) * 3 * half]
-
-    for own, other in zip(two_y, two_xy):
-        two_rows += call(
-            join_far_kernel, after(scalars, solved_one), [own, other], [sds((2, hr, 3 * half), BF16)] * 2,
-            scratch=[pltpu.VMEM((2, hr, 3 * k), BF16)],
-        )
-    two_sib = [box_permute(a, 1) for a in two_rows[:1]]
+    two_rows = [*two_rows, *(a for pair in zip(two_y, two_xy) for a in pair)]
+    two_sib = [box_permute(a, 1) for a in two_rows]
 
     ends_far = [face_permute(after(a, two_own), i // 2 + 1) for i, a in enumerate(kept_out[: 2 * nf])]
     ends_fwd = [box_permute(after(a, solved_one), 1) for a in ends_far]
-    two_sib += [box_permute(a, 1) for a in two_rows[1:]]
 
     def level_one_kernel(sc, end_ref, kept_ref, *refs):
         mixed = refs[:nf], refs[nf : 2 * nf]
@@ -435,7 +424,9 @@
         for take, parts in zip(halves(sc[0]), (mine, other)):
             rows[0, :, take, :] = parts[0][...]
             for i, ref in enumerate(parts[1:]):
-                rows[1 + i // 2, :, take, i % 2 * 3 * half : (i % 2 + 1) * 3 * half] = ref[...]
+                which = q ^ (i % 2)
+                rows[1 + i // 2, :, take, pl.ds(pl.multiple_of(which * k, k), k)] = ref[:, :, :k]
+                rows[1 + i // 2, :, take, pl.ds(pl.multiple_of(2 * k + which * half, half), half)] = ref[:, :, k:]
         copies = []
         for c in range(3):
             first = slots_ref[...]

time: 63.3 us -> 63.3 us (level)
  Pallas kernels: 23.4 us -> 22.7 us
  waiting for transfers between devices: 9.45 us -> 10.1 us
    pallas_call x15 -> x14, Pallas kernels: 23.4 us -> 22.7 us  [call(): pl.pallas_call(kernel, in_specs=[pl.BlockSpec(memory_space=pltpu.SMEM)] +...]
    ppermute x22, waiting for transfers between devices: 6.03 us -> 6.67 us  [box_permute(): return lax.ppermute(array, 'box', [(b, b ^ mask) for b in range(n_box)])]
  transfers between devices with their start and end apart: 28 -> 28, of which waited for: 7 -> 8; matrix products, arithmetic and copies ran while one was open for 0% -> 0% of each run, Pallas kernels for 31% -> 30%
where the time goes in v19:
time: 63.3 us; the launch traced here: 63 us
  starting transfers between devices  27.3 us (43%)
  Pallas kernels  22.7 us (36%)
  waiting for transfers between devices  10.1 us (16%)
  local copies, waits for them, and re-layouts  2.45 us (4%)
    pallas_call x14, Pallas kernels, call(): pl.pallas_call(kernel, in_specs=[pl.BlockSpec(memory_space=pltpu.SMEM)] +...  22.7 us
    ppermute x22, starting transfers between devices, box_permute(): return lax.ppermute(array, 'box', [(b, b ^ mask) for b in range(n_box)])  20.2 us
    ppermute x6, starting transfers between devices, face_permute(): return lax.ppermute(array, ('box', 'face'), pairs)  7.17 us
    ppermute x22, waiting for transfers between devices, box_permute(): return lax.ppermute(array, 'box', [(b, b ^ mask) for b in range(n_box)])  6.67 us
    ppermute x6, waiting for transfers between devices, face_permute(): return lax.ppermute(array, ('box', 'face'), pairs)  3.42 us
    unnamed x12, local copies, waits for them, and re-layouts  2.36 us
  transfers between devices with their start and end apart: 28, of which 8 were waited for; matrix products, arithmetic and copies ran while one was open for 0% of the time, Pallas kernels for 30%

profile of v19, /device:TPU:1, one launch (start us, length us, event | category | flops | bytes accessed | tf_op | source)
XLA Modules:
  0.0 63.0 jit_solution(11199591685247480300)
XLA Ops:
  0.0 0.1 stack.27.sc
  0.1 2.3 %copy-done = bf16[2,1,1,3,256,1536]{5,4,3,2,1,0:T(8,128)(2,1)S(1)} copy-done((bf16[2,1,1,3,256,1536]{5,4,3,2,1,0:T(8,128)(2,1)S(1)}, bf16[2,1,1,3,256,1536]{5,4,3,2,1,0:T(8,128)(2,1)}, u32[]{:S(2)}) %copy-start) | copy-done | bytes 4718616
  2.4 0.7 %shard_map.55 = (bf16[2,256,512]{2,1,0:T(8,128)(2,1)S(1)}, bf16[2,256,512]{2,1,0:T(8,128)(2,1)S(1)}, bf16[2,256,512]{2,1,0:T(8,128)(2,1)S(1)}, bf16[2,256,512]{2,1,0:T(8,128)(2,1)S(1)}, bf16[2,256,512]{2,1,0:T(8,128)(2,1)S(1)}) custom-call(s32[6]{0:T(128)S(1)} %stack.27.sc, bf16[2,3,256,1536]{3,2,1,0:T(8,128)(2,1)S(1)} %bitcast.11), custom_call_target="tpu_custom_call" | custom-call | tf_op jit(solution)/shard_map/pallas_call | solution.py:48
  3.2 0.1 collective-permute-start
  3.3 0.5 collective-permute-start.1
  3.8 0.4 collective-permute-start.3
  4.3 0.8 %shard_map.56 = (s32[1,512]{1,0:T(1,128)S(1)}, s32[512,1]{1,0:T(8,128)S(1)}) custom-call(s32[6]{0:T(128)S(1)} %stack.27.sc, s32[8,512]{1,0:T(8,128)S(1)} %bitcast.18, s32[4,512]{1,0:T(4,128)S(1)} %bitcast.19), custom_call_target="tpu_custom_call" | custom-call | tf_op jit(solution)/shard_map/pallas_call | solution.py:48
  5.2 1.3 %shard_map.57 = (bf16[2,256,512]{2,1,0:T(8,128)(2,1)S(1)}, bf16[2,128,512]{2,1,0:T(8,128)(2,1)S(1)}, bf16[2,128,512]{2,1,0:T(8,128)(2,1)S(1)}) custom-call(s32[6]{0:T(128)S(1)} %stack.27.sc, bf16[2,256,512]{2,1,0:T(8,128)(2,1)S(1)} %get-tuple-element.43.own_ref, bf16[2,256,512]{2,1,0:T(8,128)(2,1)S(1)} %collective-permute-done.sib_ref, ...), custom_call_target="tpu_custom_call" | custom-call | tf_op jit(solution)/shard_map/pallas_call | solution.py:48
  6.4 0.5 collective-permute-start.8
  6.9 2.3 %collective-permute-start.9 = (bf16[2,128,512]{2,1,0:T(8,128)(2,1)S(1)}, bf16[2,128,512]{2,1,0:T(8,128)(2,1)S(1)}, u32[]{:S(2)}, u32[]{:S(2)}) collective-permute-start(bf16[2,128,512]{2,1,0:T(8,128)(2,1)S(1)} %get-tuple-element.61), channel_id=1, source_target_pairs={{0,1},{1,0},{2,3},{3,2},{4,5},{5,4},{6,7},{7,6},{8,9},{9,8},{10,11... | collective-permute-start | bytes 786440 | tf_op jit(solution)/shard_map/ppermute | solution.py:86
  9.3 1.2 %collective-permute-start.11 = (bf16[2,128,512]{2,1,0:T(8,128)(2,1)S(1)}, bf16[2,128,512]{2,1,0:T(8,128)(2,1)S(1)}, u32[]{:S(2)}, u32[]{:S(2)}) collective-permute-start(bf16[2,128,512]{2,1,0:T(8,128)(2,1)S(1)} %bitcast.15), channel_id=1, source_target_pairs={{0,4},{2,6},{4,0},{6,2},{8,12},{10,14},{12,8},{14,10},{16,20},{18,... | collective-permute-start | bytes 786440 | tf_op jit(solution)/shard_map/ppermute | solution.py:79
  10.5 0.2 collective-permute-start.10
  10.7 1.1 %shard_map.58 = (bf16[2,128,1024]{2,1,0:T(8,128)(2,1)S(1)}, bf16[2,128,512]{2,1,0:T(8,128)(2,1)S(1)}, bf16[2,128,512]{2,1,0:T(8,128)(2,1)S(1)}, bf16[2,256,1536]{2,1,0:T(8,128)(2,1)S(1)}) custom-call(s32[6]{0:T(128)S(1)} %stack.27.sc, bf16[2,3,256,1536]{3,2,1,0:T(8,128)(2,1)S(1)} %bitcast.12, s32[1,512]{1,0:T(1,128)S(1)} %get-tuple-element.44.comp_ref.refs_6_), custom_call_target="tpu_custom_call" | custom-call | tf_op jit(solution)/shard_map/pallas_call | solution.py:48
  11.8 1.3 %collective-permute-start.6 = (bf16[2,128,512]{2,1,0:T(8,128)(2,1)S(1)}, bf16[2,128,512]{2,1,0:T(8,128)(2,1)S(1)}, u32[]{:S(2)}, u32[]{:S(2)}) collective-permute-start(bf16[2,128,512]{2,1,0:T(8,128)(2,1)S(1)} %get-tuple-element.56), channel_id=1, source_target_pairs={{0,2},{2,0},{4,6},{6,4},{8,10},{10,8},{12,14},{14,12},{16,18},{18,... | collective-permute-start | bytes 786440 | tf_op jit(solution)/shard_map/ppermute | solution.py:79
  13.2 2.4 %collective-permute-done.9.rest_0_ = bf16[2,128,512]{2,1,0:T(8,128)(2,1)S(1)} collective-permute-done((bf16[2,128,512]{2,1,0:T(8,128)(2,1)S(1)}, bf16[2,128,512]{2,1,0:T(8,128)(2,1)S(1)}, u32[]{:S(2)}, u32[]{:S(2)}) %collective-permute-start.9) | collective-permute-done | bytes 262176 | tf_op jit(solution)/shard_map/ppermute | solution.py:86
  15.6 1.5 %collective-permute-start.7 = (bf16[2,128,512]{2,1,0:T(8,128)(2,1)S(1)}, bf16[2,128,512]{2,1,0:T(8,128)(2,1)S(1)}, u32[]{:S(2)}, u32[]{:S(2)}) collective-permute-start(bf16[2,128,512]{2,1,0:T(8,128)(2,1)S(1)} %get-tuple-element.57), channel_id=1, source_target_pairs={{0,2},{2,0},{4,6},{6,4},{8,10},{10,8},{12,14},{14,12},{16,18},{18,... | collective-permute-start | bytes 786440 | tf_op jit(solution)/shard_map/ppermute | solution.py:79
  17.1 2.9 %shard_map.59 = (bf16[2,256,1536]{2,1,0:T(8,128)(2,1)S(1)}, bf16[2,64,1024]{2,1,0:T(8,128)(2,1)S(1)}, bf16[2,64,1024]{2,1,0:T(8,128)(2,1)S(1)}, bf16[2,128,1024]{2,1,0:T(8,128)(2,1)S(1)}) custom-call(s32[6]{0:T(128)S(1)} %stack.27.sc, bf16[2,256,512]{2,1,0:T(8,128)(2,1)S(1)} %get-tuple-element.49.refs_0_, ...), custom_call_target="tpu_custom_call" | custom-call | tf_op jit(solution)/shard_map/pallas_call | solution.py:48
  19.9 1.9 %collective-permute-start.5 = (bf16[2,128,1024]{2,1,0:T(8,128)(2,1)S(1)}, bf16[2,128,1024]{2,1,0:T(8,128)(2,1)S(1)}, u32[]{:S(2)}, u32[]{:S(2)}) collective-permute-start(bf16[2,128,1024]{2,1,0:T(8,128)(2,1)S(1)} %get-tuple-element.54), channel_id=1, source_target_pairs={{0,1},{1,0},{2,3},{3,2},{4,5},{5,4},{6,7},{7,6},{8,9},{9,8},{10,11... | collective-permute-start | bytes 1572872 | tf_op jit(solution)/shard_map/ppermute | solution.py:86
  21.8 0.3 collective-permute-start.12
  22.1 0.2 collective-permute-start.13
  22.3 0.6 %shard_map.60.w_ref = bf16[2,512,512]{2,1,0:T(8,128)(2,1)S(1)} custom-call(s32[6]{0:T(128)S(1)} %stack.27.sc, bf16[2,256,512]{2,1,0:T(8,128)(2,1)S(1)} %bitcast.14, bf16[2,256,512]{2,1,0:T(8,128)(2,1)S(1)} %collective-permute-done.8.refs_1_), custom_call_target="tpu_custom_call" | custom-call | tf_op jit(solution)/shard_map/pallas_call | solution.py:48
  23.0 1.4 %shard_map.61 = (f32[2,128,1024]{2,1,0:T(8,128)S(1)}, bf16[2,128,512]{2,1,0:T(8,128)(2,1)S(1)}) custom-call(s32[6]{0:T(128)S(1)} %stack.27.sc, bf16[2,128,1024]{2,1,0:T(8,128)(2,1)S(1)} %get-tuple-element.55.keep_ref, bf16[2,128,512]{2,1,0:T(8,128)(2,1)S(1)} %collective-permute-done.6.couple_ref, bf16[2,128,512]{2,1,0:T(8,128)(2,1)S(1)} %collective-permute-done.7.slots_ref, ...), custom_call_target="tpu_custom_call" | custom-call | flops 700000000 | tf_op jit(solution)/shard_map/pallas_call | solution.py:48
  24.4 1.1 %shard_map.62 = (bf16[2,128,512]{2,1,0:T(8,128)(2,1)S(1)}, bf16[2,128,256]{2,1,0:T(8,128)(2,1)S(1)}, bf16[2,128,256]{2,1,0:T(8,128)(2,1)S(1)}) custom-call(s32[6]{0:T(128)S(1)} %stack.27.sc, f32[2,128,1024]{2,1,0:T(8,128)S(1)} %get-tuple-element.59.acc_ref, bf16[2,128,512]{2,1,0:T(8,128)(2,1)S(1)} %get-tuple-element.60.hid_ref, ...), custom_call_target="tpu_custom_call" | custom-call | tf_op jit(solution)/shard_map/pallas_call | solution.py:48
  25.5 1.3 %collective-permute-start.14 = (bf16[2,128,256]{2,1,0:T(8,128)(2,1)S(1)}, bf16[2,128,256]{2,1,0:T(8,128)(2,1)S(1)}, u32[]{:S(2)}, u32[]{:S(2)}) collective-permute-start(bf16[2,128,256]{2,1,0:T(8,128)(2,1)S(1)} %get-tuple-element.68), channel_id=1, source_target_pairs={{0,4},{2,6},{4,0},{6,2},{8,12},{10,14},{12,8},{14,10},{16,20},{18,... | collective-permute-start | bytes 393224 | tf_op jit(solution)/shard_map/ppermute | solution.py:79
  26.9 3.5 %collective-permute-done.14.x_ref = bf16[2,128,256]{2,1,0:T(8,128)(2,1)S(1)} collective-permute-done((bf16[2,128,256]{2,1,0:T(8,128)(2,1)S(1)}, bf16[2,128,256]{2,1,0:T(8,128)(2,1)S(1)}, u32[]{:S(2)}, u32[]{:S(2)}) %collective-permute-start.14) | collective-permute-done | bytes 131104 | tf_op jit(solution)/shard_map/ppermute | solution.py:79
  30.4 0.6 shard_map.63.own_ref
  30.9 1.1 %collective-permute-start.22 = (bf16[2,128,768]{2,1,0:T(8,128)(2,1)S(1)}, bf16[2,128,768]{2,1,0:T(8,128)(2,1)S(1)}, u32[]{:S(2)}, u32[]{:S(2)}) collective-permute-start(bf16[2,128,768]{2,1,0:T(8,128)(2,1)S(1)} %shard_map.63.own_ref), channel_id=1, source_target_pairs={{0,4},{2,6},{4,0},{6,2},{8,12},{10,14},{12,8},{14,10},{16,20},{18,... | collective-permute-start | bytes 1179656 | tf_op jit(solution)/shard_map/ppermute | solution.py:79
  32.1 1.2 %collective-permute-start.23 = (bf16[2,128,768]{2,1,0:T(8,128)(2,1)S(1)}, bf16[2,128,768]{2,1,0:T(8,128)(2,1)S(1)}, u32[]{:S(2)}, u32[]{:S(2)}) collective-permute-start(bf16[2,128,768]{2,1,0:T(8,128)(2,1)S(1)} %shard_map.63.own_ref), channel_id=1, source_target_pairs={{0,1},{1,0},{2,3},{3,2},{4,5},{5,4},{6,7},{7,6},{8,9},{9,8},{10,11... | collective-permute-start | bytes 1179656 | tf_op jit(solution)/shard_map/ppermute | solution.py:86
  33.3 0.1 collective-permute-done.5.rest_4_.refs_0_
  33.4 1.8 %collective-permute-start.15 = (bf16[2,128,1024]{2,1,0:T(8,128)(2,1)S(1)}, bf16[2,128,1024]{2,1,0:T(8,128)(2,1)S(1)}, u32[]{:S(2)}, u32[]{:S(2)}) collective-permute-start(bf16[2,128,1024]{2,1,0:T(8,128)(2,1)S(1)} %collective-permute-done.5.rest_4_.refs_0_), channel_id=1, source_target_pairs={{0,2},{2,0},{4,6},{6,4},{8,10},{10,8},{12,14},{14,12},{16,18},{18,... | collective-permute-start | bytes 1572872 | tf_op jit(solution)/shard_map/ppermute | solution.py:79
  35.2 0.5 collective-permute-start.21
  35.7 1.4 %collective-permute-done.20.refs_2_ = bf16[2,128,512]{2,1,0:T(8,128)(2,1)S(1)} collective-permute-done((bf16[2,128,512]{2,1,0:T(8,128)(2,1)S(1)}, bf16[2,128,512]{2,1,0:T(8,128)(2,1)S(1)}, u32[]{:S(2)}, u32[]{:S(2)}) %collective-permute-start.20) | collective-permute-done | bytes 262176 | tf_op jit(solution)/shard_map/ppermute | solution.py:79
  37.1 0.4 collective-permute-done.21.refs_3_
  37.5 0.7 %shard_map.65.refs_8_ = bf16[2,512,512]{2,1,0:T(8,128)(2,1)S(1)} custom-call(s32[6]{0:T(128)S(1)} %stack.27.sc, bf16[2,128,512]{2,1,0:T(8,128)(2,1)S(1)} %bitcast.17, bf16[2,128,512]{2,1,0:T(8,128)(2,1)S(1)} %collective-permute-done.11.refs_1_, bf16[2,128,512]{2,1,0:T(8,128)(2,1)S(1)} %collective-permute-done.20.refs_2_, ...), custom_call_target="tpu_custom_call" | custom-call | tf_op jit(solution)/shard_map/pallas_call | solution.py:48
  38.2 0.3 collective-permute-start.16
  38.5 1.2 %collective-permute-start.17 = (bf16[2,64,1024]{2,1,0:T(8,128)(2,1)S(1)}, bf16[2,64,1024]{2,1,0:T(8,128)(2,1)S(1)}, u32[]{:S(2)}, u32[]{:S(2)}) collective-permute-start(bf16[2,64,1024]{2,1,0:T(8,128)(2,1)S(1)} %get-tuple-element.73), channel_id=1, source_target_pairs={{0,1},{1,0},{2,3},{3,2},{4,5},{5,4},{6,7},{7,6},{8,9},{9,8},{10,11... | collective-permute-start | bytes 786440 | tf_op jit(solution)/shard_map/ppermute | solution.py:86
  39.7 0.7 %collective-permute-done.22.x_ref = bf16[2,128,768]{2,1,0:T(8,128)(2,1)S(1)} collective-permute-done((bf16[2,128,768]{2,1,0:T(8,128)(2,1)S(1)}, bf16[2,128,768]{2,1,0:T(8,128)(2,1)S(1)}, u32[]{:S(2)}, u32[]{:S(2)}) %collective-permute-start.22) | collective-permute-done | bytes 393248 | tf_op jit(solution)/shard_map/ppermute | solution.py:79
  40.4 0.6 shard_map.67.refs_0_
  41.0 2.1 %collective-permute-start.25 = (bf16[2,128,1536]{2,1,0:T(8,128)(2,1)S(1)}, bf16[2,128,1536]{2,1,0:T(8,128)(2,1)S(1)}, u32[]{:S(2)}, u32[]{:S(2)}) collective-permute-start(bf16[2,128,1536]{2,1,0:T(8,128)(2,1)S(1)} %shard_map.67.refs_0_), channel_id=1, source_target_pairs={{0,2},{2,0},{4,6},{6,4},{8,10},{10,8},{12,14},{14,12},{16,18},{18,... | collective-permute-start | bytes 2359304 | tf_op jit(solution)/shard_map/ppermute | solution.py:79
  43.2 1.1 %collective-permute-start.24 = (bf16[2,128,768]{2,1,0:T(8,128)(2,1)S(1)}, bf16[2,128,768]{2,1,0:T(8,128)(2,1)S(1)}, u32[]{:S(2)}, u32[]{:S(2)}) collective-permute-start(bf16[2,128,768]{2,1,0:T(8,128)(2,1)S(1)} %collective-permute-done.23.refs_1_), channel_id=1, source_target_pairs={{0,4},{2,6},{4,0},{6,2},{8,12},{10,14},{12,8},{14,10},{16,20},{18,... | collective-permute-start | bytes 1179656 | tf_op jit(solution)/shard_map/ppermute | solution.py:79
  44.3 4.2 %shard_map.64.refs_7_ = bf16[2,512,1536]{2,1,0:T(8,128)(2,1)S(1)} custom-call(s32[6]{0:T(128)S(1)} %stack.27.sc, bf16[2,512,512]{2,1,0:T(8,128)(2,1)S(1)} %shard_map.60.w_ref, bf16[2,256,512]{2,1,0:T(8,128)(2,1)S(1)} %get-tuple-element.45.end_ref.refs_8_.own_ref, bf16[2,256,512]{2,1,0:T(8,128)(2,1)S(1)} %collective-permute-done.4.refs_9_.endsib_ref.sib_ref, ...), custom_call_target="tpu_custom_call" | custom-call | flops 400000000 | tf_op jit(solution)/shard_map/pallas_call | solution.py:48
  48.5 2.9 %collective-permute-start.18 = (bf16[2,64,1024]{2,1,0:T(8,128)(2,1)S(1)}, bf16[2,64,1024]{2,1,0:T(8,128)(2,1)S(1)}, u32[]{:S(2)}, u32[]{:S(2)}) collective-permute-start(bf16[2,64,1024]{2,1,0:T(8,128)(2,1)S(1)} %collective-permute-done.16.refs_2_), channel_id=1, source_target_pairs={{0,2},{2,0},{4,6},{6,4},{8,10},{10,8},{12,14},{14,12},{16,18},{18,... | collective-permute-start | bytes 786440 | tf_op jit(solution)/shard_map/ppermute | solution.py:79
  51.4 0.9 %collective-permute-done.17.refs_3_ = bf16[2,64,1024]{2,1,0:T(8,128)(2,1)S(1)} collective-permute-done((bf16[2,64,1024]{2,1,0:T(8,128)(2,1)S(1)}, bf16[2,64,1024]{2,1,0:T(8,128)(2,1)S(1)}, u32[]{:S(2)}, u32[]{:S(2)}) %collective-permute-start.17) | collective-permute-done | bytes 262176 | tf_op jit(solution)/shard_map/ppermute | solution.py:86
  52.3 2.6 %collective-permute-start.19 = (bf16[2,64,1024]{2,1,0:T(8,128)(2,1)S(1)}, bf16[2,64,1024]{2,1,0:T(8,128)(2,1)S(1)}, u32[]{:S(2)}, u32[]{:S(2)}) collective-permute-start(bf16[2,64,1024]{2,1,0:T(8,128)(2,1)S(1)} %collective-permute-done.17.refs_3_), channel_id=1, source_target_pairs={{0,2},{2,0},{4,6},{6,4},{8,10},{10,8},{12,14},{14,12},{16,18},{18,... | collective-permute-start | bytes 786440 | tf_op jit(solution)/shard_map/ppermute | solution.py:79
  54.8 0.5 collective-permute-start.27
  55.4 0.6 %collective-permute-done.19.refs_5_ = bf16[2,64,1024]{2,1,0:T(8,128)(2,1)S(1)} collective-permute-done((bf16[2,64,1024]{2,1,0:T(8,128)(2,1)S(1)}, bf16[2,64,1024]{2,1,0:T(8,128)(2,1)S(1)}, u32[]{:S(2)}, u32[]{:S(2)}) %collective-permute-start.19) | collective-permute-done | bytes 262176 | tf_op jit(solution)/shard_map/ppermute | solution.py:79
  56.0 3.4 %shard_map.66 = (bf16[2,512,512]{2,1,0:T(8,128)(2,1)S(1)}, bf16[512,512]{1,0:T(8,128)(2,1)S(1)}, bf16[512,512]{1,0:T(8,128)(2,1)S(1)}) custom-call(s32[6]{0:T(128)S(1)} %stack.27.sc, bf16[2,256,1536]{2,1,0:T(8,128)(2,1)S(1)} %get-tuple-element.48.end_ref, bf16[2,256,1536]{2,1,0:T(8,128)(2,1)S(1)} %get-tuple-element.53.kept_ref, ...), custom_call_target="tpu_custom_call" | custom-call | flops 3000000000 | tf_op jit(solution)/shard_map/pallas_call | solution.py:48
  59.4 3.4 %shard_map.68 = bf16[2,1,256,1536]{3,2,1,0:T(8,128)(2,1)} custom-call(s32[6]{0:T(128)S(1)} %stack.27.sc, bf16[2,512,512]{2,1,0:T(8,128)(2,1)S(1)} %get-tuple-element.76.hid_ref, bf16[512,512]{1,0:T(8,128)(2,1)S(1)} %get-tuple-element.77.first_ref, bf16[512,512]{1,0:T(8,128)(2,1)S(1)} %get-tuple-element.78.slots_ref, ...), custom_call_target="tpu_custom_call" | custom-call | tf_op jit(solution)/shard_map/pallas_call | solution.py:48
  (35 shorter events, 0.2 us)
Async XLA Ops:
  0.0 4.3 %copy-start.4 = (s32[1,8,512]{2,1,0:T(8,128)S(1)}, s32[1,8,512]{2,1,0:T(8,128)}, u32[]{:S(2)}) copy-start(s32[1,8,512]{2,1,0:T(8,128)} %param.8) | copy-start | bytes 49156
  0.1 2.3 %copy-start = (bf16[2,1,1,3,256,1536]{5,4,3,2,1,0:T(8,128)(2,1)S(1)}, bf16[2,1,1,3,256,1536]{5,4,3,2,1,0:T(8,128)(2,1)}, u32[]{:S(2)}) copy-start(bf16[2,1,1,3,256,1536]{5,4,3,2,1,0:T(8,128)(2,1)} %param.5) | copy-start | bytes 14155780
  2.4 1.9 %copy-start.5 = (s32[1,4,512]{2,1,0:T(4,128)S(1)}, s32[1,4,512]{2,1,0:T(4,128)}, u32[]{:S(2)}) copy-start(s32[1,4,512]{2,1,0:T(4,128)} %param.9) | copy-start | bytes 24580
  2.4 8.3 %copy-start.1 = (bf16[2,1,1,3,256,1536]{5,4,3,2,1,0:T(8,128)(2,1)S(1)}, bf16[2,1,1,3,256,1536]{5,4,3,2,1,0:T(8,128)(2,1)}, u32[]{:S(2)}) copy-start(bf16[2,1,1,3,256,1536]{5,4,3,2,1,0:T(8,128)(2,1)} %param.5) | copy-start | bytes 14155780
  3.1 3.3 %copy-start.2 = (bf16[2,1,256,512]{3,2,1,0:T(8,128)(2,1)S(1)}, bf16[2,1,256,512]{3,2,1,0:T(8,128)(2,1)}, u32[]{:S(2)}) copy-start(bf16[2,1,256,512]{3,2,1,0:T(8,128)(2,1)} %param.6) | copy-start | bytes 1572868
  3.2 6.1 %copy-start.3 = (bf16[2,1,128,512]{3,2,1,0:T(8,128)(2,1)S(1)}, bf16[2,1,128,512]{3,2,1,0:T(8,128)(2,1)}, u32[]{:S(2)}) copy-start(bf16[2,1,128,512]{3,2,1,0:T(8,128)(2,1)} %param.7) | copy-start | bytes 786436
  3.2 2.0 %collective-permute-start = (bf16[2,256,512]{2,1,0:T(8,128)(2,1)S(1)}, bf16[2,256,512]{2,1,0:T(8,128)(2,1)S(1)}, u32[]{:S(2)}, u32[]{:S(2)}) collective-permute-start(bf16[2,256,512]{2,1,0:T(8,128)(2,1)S(1)} %get-tuple-element.43.own_ref), channel_id=1, source_target_pairs={{0,2},{2,0},{4,6},{6,4},{8,10},{10,8},{12,14},{14,12},{16,18},{18,... | collective-permute-start | bytes 1572872 | tf_op jit(solution)/shard_map/ppermute | solution.py:79
  3.3 3.6 %collective-permute-start.1 = (bf16[2,256,512]{2,1,0:T(8,128)(2,1)S(1)}, bf16[2,256,512]{2,1,0:T(8,128)(2,1)S(1)}, u32[]{:S(2)}, u32[]{:S(2)}) collective-permute-start(bf16[2,256,512]{2,1,0:T(8,128)(2,1)S(1)} %get-tuple-element.49.refs_0_), channel_id=1, source_target_pairs={{0,2},{2,0},{4,6},{6,4},{8,10},{10,8},{12,14},{14,12},{16,18},{18,... | collective-permute-start | bytes 1572872 | tf_op jit(solution)/shard_map/ppermute | solution.py:79
  3.7 5.5 %collective-permute-start.2 = (bf16[2,256,512]{2,1,0:T(8,128)(2,1)S(1)}, bf16[2,256,512]{2,1,0:T(8,128)(2,1)S(1)}, u32[]{:S(2)}, u32[]{:S(2)}) collective-permute-start(bf16[2,256,512]{2,1,0:T(8,128)(2,1)S(1)} %get-tuple-element.50.refs_1_), channel_id=1, source_target_pairs={{0,2},{2,0},{4,6},{6,4},{8,10},{10,8},{12,14},{14,12},{16,18},{18,... | collective-permute-start | bytes 1572872 | tf_op jit(solution)/shard_map/ppermute | solution.py:79
  3.8 6.7 %collective-permute-start.3 = (bf16[2,256,512]{2,1,0:T(8,128)(2,1)S(1)}, bf16[2,256,512]{2,1,0:T(8,128)(2,1)S(1)}, u32[]{:S(2)}, u32[]{:S(2)}) collective-permute-start(bf16[2,256,512]{2,1,0:T(8,128)(2,1)S(1)} %get-tuple-element.51.refs_2_), channel_id=1, source_target_pairs={{0,2},{2,0},{4,6},{6,4},{8,10},{10,8},{12,14},{14,12},{16,18},{18,... | collective-permute-start | bytes 1572872 | tf_op jit(solution)/shard_map/ppermute | solution.py:79
  4.3 7.6 %collective-permute-start.4 = (bf16[2,256,512]{2,1,0:T(8,128)(2,1)S(1)}, bf16[2,256,512]{2,1,0:T(8,128)(2,1)S(1)}, u32[]{:S(2)}, u32[]{:S(2)}) collective-permute-start(bf16[2,256,512]{2,1,0:T(8,128)(2,1)S(1)} %get-tuple-element.45.end_ref.refs_8_.own_ref), channel_id=1, source_target_pairs={{0,2},{2,0},{4,6},{6,4},{8,10},{10,8},{12,14},{14,12},{16,18},{18,... | collective-permute-start | bytes 1572872 | tf_op jit(solution)/shard_map/ppermute | solution.py:79
  6.4 15.7 %collective-permute-start.8 = (bf16[2,256,512]{2,1,0:T(8,128)(2,1)S(1)}, bf16[2,256,512]{2,1,0:T(8,128)(2,1)S(1)}, u32[]{:S(2)}, u32[]{:S(2)}) collective-permute-start(bf16[2,256,512]{2,1,0:T(8,128)(2,1)S(1)} %bitcast.13), channel_id=1, source_target_pairs={{0,2},{2,0},{4,6},{6,4},{8,10},{10,8},{12,14},{14,12},{16,18},{18,... | collective-permute-start | bytes 1572872 | tf_op jit(solution)/shard_map/ppermute | solution.py:79
  6.9 8.6 %collective-permute-start.9 = (bf16[2,128,512]{2,1,0:T(8,128)(2,1)S(1)}, bf16[2,128,512]{2,1,0:T(8,128)(2,1)S(1)}, u32[]{:S(2)}, u32[]{:S(2)}) collective-permute-start(bf16[2,128,512]{2,1,0:T(8,128)(2,1)S(1)} %get-tuple-element.61), channel_id=1, source_target_pairs={{0,1},{1,0},{2,3},{3,2},{4,5},{5,4},{6,7},{7,6},{8,9},{9,8},{10,11... | collective-permute-start | bytes 786440 | tf_op jit(solution)/shard_map/ppermute | solution.py:86
  9.3 10.7 %collective-permute-start.11 = (bf16[2,128,512]{2,1,0:T(8,128)(2,1)S(1)}, bf16[2,128,512]{2,1,0:T(8,128)(2,1)S(1)}, u32[]{:S(2)}, u32[]{:S(2)}) collective-permute-start(bf16[2,128,512]{2,1,0:T(8,128)(2,1)S(1)} %bitcast.15), channel_id=1, source_target_pairs={{0,4},{2,6},{4,0},{6,2},{8,12},{10,14},{12,8},{14,10},{16,20},{18,... | collective-permute-start | bytes 786440 | tf_op jit(solution)/shard_map/ppermute | solution.py:79
  10.5 11.3 %collective-permute-start.10 = (bf16[2,128,512]{2,1,0:T(8,128)(2,1)S(1)}, bf16[2,128,512]{2,1,0:T(8,128)(2,1)S(1)}, u32[]{:S(2)}, u32[]{:S(2)}) collective-permute-start(bf16[2,128,512]{2,1,0:T(8,128)(2,1)S(1)} %get-tuple-element.62), channel_id=1, source_target_pairs={{0,1},{1,0},{2,3},{3,2},{4,5},{5,4},{6,7},{7,6},{8,9},{9,8},{10,11... | collective-permute-start | bytes 786440 | tf_op jit(solution)/shard_map/ppermute | solution.py:86
  11.8 11.1 %collective-permute-start.6 = (bf16[2,128,512]{2,1,0:T(8,128)(2,1)S(1)}, bf16[2,128,512]{2,1,0:T(8,128)(2,1)S(1)}, u32[]{:S(2)}, u32[]{:S(2)}) collective-permute-start(bf16[2,128,512]{2,1,0:T(8,128)(2,1)S(1)} %get-tuple-element.56), channel_id=1, source_target_pairs={{0,2},{2,0},{4,6},{6,4},{8,10},{10,8},{12,14},{14,12},{16,18},{18,... | collective-permute-start | bytes 786440 | tf_op jit(solution)/shard_map/ppermute | solution.py:79
  15.6 7.4 %collective-permute-start.7 = (bf16[2,128,512]{2,1,0:T(8,128)(2,1)S(1)}, bf16[2,128,512]{2,1,0:T(8,128)(2,1)S(1)}, u32[]{:S(2)}, u32[]{:S(2)}) collective-permute-start(bf16[2,128,512]{2,1,0:T(8,128)(2,1)S(1)} %get-tuple-element.57), channel_id=1, source_target_pairs={{0,2},{2,0},{4,6},{6,4},{8,10},{10,8},{12,14},{14,12},{16,18},{18,... | collective-permute-start | bytes 786440 | tf_op jit(solution)/shard_map/ppermute | solution.py:79
  19.9 13.5 %collective-permute-start.5 = (bf16[2,128,1024]{2,1,0:T(8,128)(2,1)S(1)}, bf16[2,128,1024]{2,1,0:T(8,128)(2,1)S(1)}, u32[]{:S(2)}, u32[]{:S(2)}) collective-permute-start(bf16[2,128,1024]{2,1,0:T(8,128)(2,1)S(1)} %get-tuple-element.54), channel_id=1, source_target_pairs={{0,1},{1,0},{2,3},{3,2},{4,5},{5,4},{6,7},{7,6},{8,9},{9,8},{10,11... | collective-permute-start | bytes 1572872 | tf_op jit(solution)/shard_map/ppermute | solution.py:86
  21.8 2.6 %collective-permute-start.12 = (bf16[2,128,512]{2,1,0:T(8,128)(2,1)S(1)}, bf16[2,128,512]{2,1,0:T(8,128)(2,1)S(1)}, u32[]{:S(2)}, u32[]{:S(2)}) collective-permute-start(bf16[2,128,512]{2,1,0:T(8,128)(2,1)S(1)} %collective-permute-done.9.rest_0_), channel_id=1, source_target_pairs={{0,2},{2,0},{4,6},{6,4},{8,10},{10,8},{12,14},{14,12},{16,18},{18,... | collective-permute-start | bytes 786440 | tf_op jit(solution)/shard_map/ppermute | solution.py:79
  22.1 2.2 %collective-permute-start.13 = (bf16[2,128,512]{2,1,0:T(8,128)(2,1)S(1)}, bf16[2,128,512]{2,1,0:T(8,128)(2,1)S(1)}, u32[]{:S(2)}, u32[]{:S(2)}) collective-permute-start(bf16[2,128,512]{2,1,0:T(8,128)(2,1)S(1)} %collective-permute-done.10.rest_1_), channel_id=1, source_target_pairs={{0,2},{2,0},{4,6},{6,4},{8,10},{10,8},{12,14},{14,12},{16,18},{18,... | collective-permute-start | bytes 786440 | tf_op jit(solution)/shard_map/ppermute | solution.py:79
  25.5 4.8 %collective-permute-start.14 = (bf16[2,128,256]{2,1,0:T(8,128)(2,1)S(1)}, bf16[2,128,256]{2,1,0:T(8,128)(2,1)S(1)}, u32[]{:S(2)}, u32[]{:S(2)}) collective-permute-start(bf16[2,128,256]{2,1,0:T(8,128)(2,1)S(1)} %get-tuple-element.68), channel_id=1, source_target_pairs={{0,4},{2,6},{4,0},{6,2},{8,12},{10,14},{12,8},{14,10},{16,20},{18,... | collective-permute-start | bytes 393224 | tf_op jit(solution)/shard_map/ppermute | solution.py:79
  30.9 9.5 %collective-permute-start.22 = (bf16[2,128,768]{2,1,0:T(8,128)(2,1)S(1)}, bf16[2,128,768]{2,1,0:T(8,128)(2,1)S(1)}, u32[]{:S(2)}, u32[]{:S(2)}) collective-permute-start(bf16[2,128,768]{2,1,0:T(8,128)(2,1)S(1)} %shard_map.63.own_ref), channel_id=1, source_target_pairs={{0,4},{2,6},{4,0},{6,2},{8,12},{10,14},{12,8},{14,10},{16,20},{18,... | collective-permute-start | bytes 1179656 | tf_op jit(solution)/shard_map/ppermute | solution.py:79
  32.1 11.1 %collective-permute-start.23 = (bf16[2,128,768]{2,1,0:T(8,128)(2,1)S(1)}, bf16[2,128,768]{2,1,0:T(8,128)(2,1)S(1)}, u32[]{:S(2)}, u32[]{:S(2)}) collective-permute-start(bf16[2,128,768]{2,1,0:T(8,128)(2,1)S(1)} %shard_map.63.own_ref), channel_id=1, source_target_pairs={{0,1},{1,0},{2,3},{3,2},{4,5},{5,4},{6,7},{7,6},{8,9},{9,8},{10,11... | collective-permute-start | bytes 1179656 | tf_op jit(solution)/shard_map/ppermute | solution.py:86
  33.4 10.9 %collective-permute-start.15 = (bf16[2,128,1024]{2,1,0:T(8,128)(2,1)S(1)}, bf16[2,128,1024]{2,1,0:T(8,128)(2,1)S(1)}, u32[]{:S(2)}, u32[]{:S(2)}) collective-permute-start(bf16[2,128,1024]{2,1,0:T(8,128)(2,1)S(1)} %collective-permute-done.5.rest_4_.refs_0_), channel_id=1, source_target_pairs={{0,2},{2,0},{4,6},{6,4},{8,10},{10,8},{12,14},{14,12},{16,18},{18,... | collective-permute-start | bytes 1572872 | tf_op jit(solution)/shard_map/ppermute | solution.py:79
  35.2 1.9 %collective-permute-start.20 = (bf16[2,128,512]{2,1,0:T(8,128)(2,1)S(1)}, bf16[2,128,512]{2,1,0:T(8,128)(2,1)S(1)}, u32[]{:S(2)}, u32[]{:S(2)}) collective-permute-start(bf16[2,128,512]{2,1,0:T(8,128)(2,1)S(1)} %bitcast.16), channel_id=1, source_target_pairs={{0,2},{2,0},{4,6},{6,4},{8,10},{10,8},{12,14},{14,12},{16,18},{18,... | collective-permute-start | bytes 786440 | tf_op jit(solution)/shard_map/ppermute | solution.py:79
  35.2 2.3 %collective-permute-start.21 = (bf16[2,128,512]{2,1,0:T(8,128)(2,1)S(1)}, bf16[2,128,512]{2,1,0:T(8,128)(2,1)S(1)}, u32[]{:S(2)}, u32[]{:S(2)}) collective-permute-start(bf16[2,128,512]{2,1,0:T(8,128)(2,1)S(1)} %collective-permute-done.11.refs_1_), channel_id=1, source_target_pairs={{0,2},{2,0},{4,6},{6,4},{8,10},{10,8},{12,14},{14,12},{16,18},{18,... | collective-permute-start | bytes 786440 | tf_op jit(solution)/shard_map/ppermute | solution.py:79
  38.2 10.3 %collective-permute-start.16 = (bf16[2,64,1024]{2,1,0:T(8,128)(2,1)S(1)}, bf16[2,64,1024]{2,1,0:T(8,128)(2,1)S(1)}, u32[]{:S(2)}, u32[]{:S(2)}) collective-permute-start(bf16[2,64,1024]{2,1,0:T(8,128)(2,1)S(1)} %get-tuple-element.71), channel_id=1, source_target_pairs={{0,1},{1,0},{2,3},{3,2},{4,5},{5,4},{6,7},{7,6},{8,9},{9,8},{10,11... | collective-permute-start | bytes 786440 | tf_op jit(solution)/shard_map/ppermute | solution.py:86
  38.5 13.7 %collective-permute-start.17 = (bf16[2,64,1024]{2,1,0:T(8,128)(2,1)S(1)}, bf16[2,64,1024]{2,1,0:T(8,128)(2,1)S(1)}, u32[]{:S(2)}, u32[]{:S(2)}) collective-permute-start(bf16[2,64,1024]{2,1,0:T(8,128)(2,1)S(1)} %get-tuple-element.73), channel_id=1, source_target_pairs={{0,1},{1,0},{2,3},{3,2},{4,5},{5,4},{6,7},{7,6},{8,9},{9,8},{10,11... | collective-permute-start | bytes 786440 | tf_op jit(solution)/shard_map/ppermute | solution.py:86
  41.0 18.3 %collective-permute-start.25 = (bf16[2,128,1536]{2,1,0:T(8,128)(2,1)S(1)}, bf16[2,128,1536]{2,1,0:T(8,128)(2,1)S(1)}, u32[]{:S(2)}, u32[]{:S(2)}) collective-permute-start(bf16[2,128,1536]{2,1,0:T(8,128)(2,1)S(1)} %shard_map.67.refs_0_), channel_id=1, source_target_pairs={{0,2},{2,0},{4,6},{6,4},{8,10},{10,8},{12,14},{14,12},{16,18},{18,... | collective-permute-start | bytes 2359304 | tf_op jit(solution)/shard_map/ppermute | solution.py:79
  43.2 11.6 %collective-permute-start.24 = (bf16[2,128,768]{2,1,0:T(8,128)(2,1)S(1)}, bf16[2,128,768]{2,1,0:T(8,128)(2,1)S(1)}, u32[]{:S(2)}, u32[]{:S(2)}) collective-permute-start(bf16[2,128,768]{2,1,0:T(8,128)(2,1)S(1)} %collective-permute-done.23.refs_1_), channel_id=1, source_target_pairs={{0,4},{2,6},{4,0},{6,2},{8,12},{10,14},{12,8},{14,10},{16,20},{18,... | collective-permute-start | bytes 1179656 | tf_op jit(solution)/shard_map/ppermute | solution.py:79
  48.5 6.8 %collective-permute-start.18 = (bf16[2,64,1024]{2,1,0:T(8,128)(2,1)S(1)}, bf16[2,64,1024]{2,1,0:T(8,128)(2,1)S(1)}, u32[]{:S(2)}, u32[]{:S(2)}) collective-permute-start(bf16[2,64,1024]{2,1,0:T(8,128)(2,1)S(1)} %collective-permute-done.16.refs_2_), channel_id=1, source_target_pairs={{0,2},{2,0},{4,6},{6,4},{8,10},{10,8},{12,14},{14,12},{16,18},{18,... | collective-permute-start | bytes 786440 | tf_op jit(solution)/shard_map/ppermute | solution.py:79
  52.3 3.7 %collective-permute-start.19 = (bf16[2,64,1024]{2,1,0:T(8,128)(2,1)S(1)}, bf16[2,64,1024]{2,1,0:T(8,128)(2,1)S(1)}, u32[]{:S(2)}, u32[]{:S(2)}) collective-permute-start(bf16[2,64,1024]{2,1,0:T(8,128)(2,1)S(1)} %collective-permute-done.17.refs_3_), channel_id=1, source_target_pairs={{0,2},{2,0},{4,6},{6,4},{8,10},{10,8},{12,14},{14,12},{16,18},{18,... | collective-permute-start | bytes 786440 | tf_op jit(solution)/shard_map/ppermute | solution.py:79
  54.8 4.5 %collective-permute-start.26 = (bf16[2,128,768]{2,1,0:T(8,128)(2,1)S(1)}, bf16[2,128,768]{2,1,0:T(8,128)(2,1)S(1)}, u32[]{:S(2)}, u32[]{:S(2)}) collective-permute-start(bf16[2,128,768]{2,1,0:T(8,128)(2,1)S(1)} %collective-permute-done.23.refs_1_), channel_id=1, source_target_pairs={{0,2},{2,0},{4,6},{6,4},{8,10},{10,8},{12,14},{14,12},{16,18},{18,... | collective-permute-start | bytes 1179656 | tf_op jit(solution)/shard_map/ppermute | solution.py:79
  54.8 4.5 %collective-permute-start.27 = (bf16[2,128,768]{2,1,0:T(8,128)(2,1)S(1)}, bf16[2,128,768]{2,1,0:T(8,128)(2,1)S(1)}, u32[]{:S(2)}, u32[]{:S(2)}) collective-permute-start(bf16[2,128,768]{2,1,0:T(8,128)(2,1)S(1)} %collective-permute-done.24.refs_2_), channel_id=1, source_target_pairs={{0,2},{2,0},{4,6},{6,4},{8,10},{10,8},{12,14},{14,12},{16,18},{18,... | collective-permute-start | bytes 1179656 | tf_op jit(solution)/shard_map/ppermute | solution.py:79

commit v20 on v19

--- a/solution.py
+++ b/solution.py
@@ -319,12 +319,25 @@
             right = rows[:, :, :, cols].reshape(n_face * 2 * fr, k)
             out_ref[:, :, cols] = dot(left, right).astype(BF16).reshape(2, k, k)
 
-    def weighted_one_kernel(sc, w_ref, own_ref, sib_ref, side_ref, *rest):
+    def weighted_one_kernel(sc, w_ref, own_ref, sib_ref, side_ref, end_ref, kept_ref, *rest):
         refs = [rest[i * nf : (i + 1) * nf] for i in range(6)]
         far, fwd = rest[: 2 * nf], rest[2 * nf : 4 * nf]
-        out_ref, rows = rest[6 * nf :]
+        out_ref, slots_out, rows = rest[6 * nf :]
         p, q = sc[0], sc[1]
         is_end = p == q
+
+        @pl.when(is_end)
+        def _():
+            slots_out[...] = end_ref[:, :, 2 * k :]
+
+        @pl.when(p != q)
+        def _():
+            for take, parts in zip(halves(p), refs[4:]):
+                total = kept_ref[:, take, 2 * k :]
+                for ref in parts:
+                    total = total + ref[:, :, k:]
+                slots_out[:, take, :] = total
+
         first_cols = pl.ds(pl.multiple_of(q * k, k), k)
         rest_cols = pl.ds(pl.multiple_of((1 - q) * k, k), k)
         rows[0, :, :, pl.ds(pl.multiple_of(p * k, k), k)] = own_ref[...]
@@ -340,10 +353,11 @@
                 rows[s + 1, :, take, rest_cols] = parts[s][:, :, :k]
         weighted(w_ref, rows, out_ref)
 
-    (solved_one,) = call(
+    solved_one, slot_rows = call(
         weighted_one_kernel, scalars,
-        [weight_one, end_own, end_sib, side, *first_far, *first_fwd, *mixed_far, *mixed_fwd],
-        [sds((2, k, 3 * k), BF16)], scratch=[pltpu.VMEM((n_face, 2, fr, 3 * k), BF16)], cost=SOLVED_COST,
+        [weight_one, end_own, end_sib, side, end_kept, kept, *first_far, *first_fwd, *mixed_far, *mixed_fwd],
+        [sds((2, k, 3 * k), BF16), sds((2, fr, k), BF16)],
+        scratch=[pltpu.VMEM((n_face, 2, fr, 3 * k), BF16)], cost=SOLVED_COST,
     )
 
     def join_kernel(sc, own_ref, x_ref, out_ref):
@@ -362,28 +376,24 @@
     ends_fwd = [box_permute(after(a, solved_one), 1) for a in ends_far]
 
     def level_one_kernel(sc, end_ref, kept_ref, *refs):
-        mixed = refs[:nf], refs[nf : 2 * nf]
-        ends = refs[2 * nf : 4 * nf], refs[4 * nf : 6 * nf]
-        col_ref, one_ref, w_ref, hid_out, first_out, slots_out, zs = refs[6 * nf :]
+        slot_ref, refs = refs[0], refs[1:]
+        ends = refs[: 2 * nf], refs[2 * nf : 4 * nf]
+        col_ref, one_ref, w_ref, hid_out, first_out, slots_out, zs = refs[4 * nf :]
         p, q, f = sc[0], sc[1], sc[2]
 
         @pl.when(p == q)
         def _():
-            zs[...] = end_ref[...]
+            zs[...] = end_ref[:, :, : 2 * k]
 
         @pl.when(p != q)
         def _():
-            for h, take in enumerate(halves(p)):
-                total = kept_ref[:, take, 2 * k :]
-                for ref in mixed[h]:
-                    total = total + ref[:, :, k:]
-                zs[:, take, 2 * k :] = total
+            for h in range(2):
                 for j in range(2):
                     take = pl.ds(pl.multiple_of((p ^ h) * hr + j * qr, qr), qr)
                     total = kept_ref[:, take, : 2 * k]
                     for ref in ends[h][j::2]:
                         total = total + ref[...]
-                    zs[:, take, : 2 * k] = total
+                    zs[:, take, :] = total
 
         slots = col_ref[pl.ds(pl.multiple_of(f * fr, fr), fr), :]
         right = jnp.where(slots >= k, 1, 0)
@@ -395,7 +405,7 @@
         start = [
             jnp.concatenate([jnp.where(right, nothing, a) for a in lefts], axis=0),
             jnp.concatenate([jnp.where(right, a, nothing) for a in rights], axis=0),
-            flat(zs[:, :, 2 * k :]),
+            flat(slot_ref[...]),
         ]
         merged = [
             (start[c].astype(F32) - dot(left, flat(one_ref[:, :, c * k : (c + 1) * k]))).astype(BF16)
@@ -411,9 +421,9 @@
 
     hid_two, first_two, slots_two = call(
         level_one_kernel, scalars,
-        [end_kept, kept, *mixed_far, *mixed_fwd, *ends_far, *ends_fwd, skel_col, solved_one, weight_two],
+        [end_kept, kept, slot_rows, *ends_far, *ends_fwd, skel_col, solved_one, weight_two],
         [sds((n_face, 2 * fr, 2 * fr), BF16), sds((2 * fr, k), BF16), sds((2 * fr, k), BF16)],
-        scratch=[pltpu.VMEM((2, fr, 3 * k), BF16)], cost=KEEP_COST,
+        scratch=[pltpu.VMEM((2, fr, 2 * k), BF16)], cost=KEEP_COST,
     )
 
     def level_two_kernel(sc, hid_ref, first_ref, slots_ref, *refs):

time: 63.3 us -> 63.3 us (level)
  no operation moved by 1% of the time
where the time goes in v20:
time: 63.3 us; the launch traced here: 62.9 us
  starting transfers between devices  27.1 us (43%)
  Pallas kernels  22.8 us (36%)
  waiting for transfers between devices  10.2 us (16%)
  local copies, waits for them, and re-layouts  2.45 us (4%)
    pallas_call x14, Pallas kernels, call(): pl.pallas_call(kernel, in_specs=[pl.BlockSpec(memory_space=pltpu.SMEM)] +...  22.8 us
    ppermute x22, starting transfers between devices, box_permute(): return lax.ppermute(array, 'box', [(b, b ^ mask) for b in range(n_box)])  20 us
    ppermute x6, starting transfers between devices, face_permute(): return lax.ppermute(array, ('box', 'face'), pairs)  7.18 us
    ppermute x22, waiting for transfers between devices, box_permute(): return lax.ppermute(array, 'box', [(b, b ^ mask) for b in range(n_box)])  6.78 us
    ppermute x6, waiting for transfers between devices, face_permute(): return lax.ppermute(array, ('box', 'face'), pairs)  3.42 us
    unnamed x12, local copies, waits for them, and re-layouts  2.36 us
  transfers between devices with their start and end apart: 28, of which 8 were waited for; matrix products, arithmetic and copies ran while one was open for 0% of the time, Pallas kernels for 30%

profile of v20, /device:TPU:1, one launch (start us, length us, event | category | flops | bytes accessed | tf_op | source)
XLA Modules:
  0.0 62.9 jit_solution(4511313409173872993)
XLA Ops:
  0.0 0.1 stack.27.sc
  0.1 2.3 %copy-done = bf16[2,1,1,3,256,1536]{5,4,3,2,1,0:T(8,128)(2,1)S(1)} copy-done((bf16[2,1,1,3,256,1536]{5,4,3,2,1,0:T(8,128)(2,1)S(1)}, bf16[2,1,1,3,256,1536]{5,4,3,2,1,0:T(8,128)(2,1)}, u32[]{:S(2)}) %copy-start) | copy-done | bytes 4718616
  2.4 0.7 %shard_map.55 = (bf16[2,256,512]{2,1,0:T(8,128)(2,1)S(1)}, bf16[2,256,512]{2,1,0:T(8,128)(2,1)S(1)}, bf16[2,256,512]{2,1,0:T(8,128)(2,1)S(1)}, bf16[2,256,512]{2,1,0:T(8,128)(2,1)S(1)}, bf16[2,256,512]{2,1,0:T(8,128)(2,1)S(1)}) custom-call(s32[6]{0:T(128)S(1)} %stack.27.sc, bf16[2,3,256,1536]{3,2,1,0:T(8,128)(2,1)S(1)} %bitcast.11), custom_call_target="tpu_custom_call" | custom-call | tf_op jit(solution)/shard_map/pallas_call | solution.py:48
  3.2 0.1 collective-permute-start
  3.3 0.5 collective-permute-start.1
  3.8 0.4 collective-permute-start.3
  4.3 0.8 %shard_map.56 = (s32[1,512]{1,0:T(1,128)S(1)}, s32[512,1]{1,0:T(8,128)S(1)}) custom-call(s32[6]{0:T(128)S(1)} %stack.27.sc, s32[8,512]{1,0:T(8,128)S(1)} %bitcast.18, s32[4,512]{1,0:T(4,128)S(1)} %bitcast.19), custom_call_target="tpu_custom_call" | custom-call | tf_op jit(solution)/shard_map/pallas_call | solution.py:48
  5.2 1.3 %shard_map.57 = (bf16[2,256,512]{2,1,0:T(8,128)(2,1)S(1)}, bf16[2,128,512]{2,1,0:T(8,128)(2,1)S(1)}, bf16[2,128,512]{2,1,0:T(8,128)(2,1)S(1)}) custom-call(s32[6]{0:T(128)S(1)} %stack.27.sc, bf16[2,256,512]{2,1,0:T(8,128)(2,1)S(1)} %get-tuple-element.45.own_ref, bf16[2,256,512]{2,1,0:T(8,128)(2,1)S(1)} %collective-permute-done.sib_ref, ...), custom_call_target="tpu_custom_call" | custom-call | tf_op jit(solution)/shard_map/pallas_call | solution.py:48
  6.4 0.5 collective-permute-start.5
  6.9 2.3 %collective-permute-start.6 = (bf16[2,128,512]{2,1,0:T(8,128)(2,1)S(1)}, bf16[2,128,512]{2,1,0:T(8,128)(2,1)S(1)}, u32[]{:S(2)}, u32[]{:S(2)}) collective-permute-start(bf16[2,128,512]{2,1,0:T(8,128)(2,1)S(1)} %get-tuple-element.57), channel_id=1, source_target_pairs={{0,1},{1,0},{2,3},{3,2},{4,5},{5,4},{6,7},{7,6},{8,9},{9,8},{10,11... | collective-permute-start | bytes 786440 | tf_op jit(solution)/shard_map/ppermute | solution.py:86
  9.3 1.2 %collective-permute-start.8 = (bf16[2,128,512]{2,1,0:T(8,128)(2,1)S(1)}, bf16[2,128,512]{2,1,0:T(8,128)(2,1)S(1)}, u32[]{:S(2)}, u32[]{:S(2)}) collective-permute-start(bf16[2,128,512]{2,1,0:T(8,128)(2,1)S(1)} %bitcast.15), channel_id=1, source_target_pairs={{0,4},{2,6},{4,0},{6,2},{8,12},{10,14},{12,8},{14,10},{16,20},{18,... | collective-permute-start | bytes 786440 | tf_op jit(solution)/shard_map/ppermute | solution.py:79
  10.5 0.2 collective-permute-start.7
  10.7 1.1 %shard_map.58 = (bf16[2,128,1024]{2,1,0:T(8,128)(2,1)S(1)}, bf16[2,128,512]{2,1,0:T(8,128)(2,1)S(1)}, bf16[2,128,512]{2,1,0:T(8,128)(2,1)S(1)}, bf16[2,256,1536]{2,1,0:T(8,128)(2,1)S(1)}) custom-call(s32[6]{0:T(128)S(1)} %stack.27.sc, bf16[2,3,256,1536]{3,2,1,0:T(8,128)(2,1)S(1)} %bitcast.12, s32[1,512]{1,0:T(1,128)S(1)} %get-tuple-element.46.comp_ref.refs_6_), custom_call_target="tpu_custom_call" | custom-call | tf_op jit(solution)/shard_map/pallas_call | solution.py:48
  11.8 1.3 %collective-permute-start.12 = (bf16[2,128,512]{2,1,0:T(8,128)(2,1)S(1)}, bf16[2,128,512]{2,1,0:T(8,128)(2,1)S(1)}, u32[]{:S(2)}, u32[]{:S(2)}) collective-permute-start(bf16[2,128,512]{2,1,0:T(8,128)(2,1)S(1)} %get-tuple-element.64), channel_id=1, source_target_pairs={{0,2},{2,0},{4,6},{6,4},{8,10},{10,8},{12,14},{14,12},{16,18},{18,... | collective-permute-start | bytes 786440 | tf_op jit(solution)/shard_map/ppermute | solution.py:79
  13.2 2.4 %collective-permute-done.6.rest_0_ = bf16[2,128,512]{2,1,0:T(8,128)(2,1)S(1)} collective-permute-done((bf16[2,128,512]{2,1,0:T(8,128)(2,1)S(1)}, bf16[2,128,512]{2,1,0:T(8,128)(2,1)S(1)}, u32[]{:S(2)}, u32[]{:S(2)}) %collective-permute-start.6) | collective-permute-done | bytes 262176 | tf_op jit(solution)/shard_map/ppermute | solution.py:86
  15.6 1.5 %collective-permute-start.13 = (bf16[2,128,512]{2,1,0:T(8,128)(2,1)S(1)}, bf16[2,128,512]{2,1,0:T(8,128)(2,1)S(1)}, u32[]{:S(2)}, u32[]{:S(2)}) collective-permute-start(bf16[2,128,512]{2,1,0:T(8,128)(2,1)S(1)} %get-tuple-element.65), channel_id=1, source_target_pairs={{0,2},{2,0},{4,6},{6,4},{8,10},{10,8},{12,14},{14,12},{16,18},{18,... | collective-permute-start | bytes 786440 | tf_op jit(solution)/shard_map/ppermute | solution.py:79
  17.1 2.9 %shard_map.59 = (bf16[2,256,1536]{2,1,0:T(8,128)(2,1)S(1)}, bf16[2,64,1024]{2,1,0:T(8,128)(2,1)S(1)}, bf16[2,64,1024]{2,1,0:T(8,128)(2,1)S(1)}, bf16[2,128,1024]{2,1,0:T(8,128)(2,1)S(1)}) custom-call(s32[6]{0:T(128)S(1)} %stack.27.sc, bf16[2,256,512]{2,1,0:T(8,128)(2,1)S(1)} %get-tuple-element.51.refs_0_, ...), custom_call_target="tpu_custom_call" | custom-call | tf_op jit(solution)/shard_map/pallas_call | solution.py:48
  20.0 1.9 %collective-permute-start.11 = (bf16[2,128,1024]{2,1,0:T(8,128)(2,1)S(1)}, bf16[2,128,1024]{2,1,0:T(8,128)(2,1)S(1)}, u32[]{:S(2)}, u32[]{:S(2)}) collective-permute-start(bf16[2,128,1024]{2,1,0:T(8,128)(2,1)S(1)} %get-tuple-element.62), channel_id=1, source_target_pairs={{0,1},{1,0},{2,3},{3,2},{4,5},{5,4},{6,7},{7,6},{8,9},{9,8},{10,11... | collective-permute-start | bytes 1572872 | tf_op jit(solution)/shard_map/ppermute | solution.py:86
  21.8 0.3 collective-permute-start.9
  22.1 0.2 collective-permute-start.10
  22.3 0.6 %shard_map.60.w_ref = bf16[2,512,512]{2,1,0:T(8,128)(2,1)S(1)} custom-call(s32[6]{0:T(128)S(1)} %stack.27.sc, bf16[2,256,512]{2,1,0:T(8,128)(2,1)S(1)} %bitcast.14, bf16[2,256,512]{2,1,0:T(8,128)(2,1)S(1)} %collective-permute-done.5.refs_1_), custom_call_target="tpu_custom_call" | custom-call | tf_op jit(solution)/shard_map/pallas_call | solution.py:48
  23.0 1.4 %shard_map.61 = (f32[2,128,1024]{2,1,0:T(8,128)S(1)}, bf16[2,128,512]{2,1,0:T(8,128)(2,1)S(1)}) custom-call(s32[6]{0:T(128)S(1)} %stack.27.sc, bf16[2,128,1024]{2,1,0:T(8,128)(2,1)S(1)} %get-tuple-element.63.keep_ref, bf16[2,128,512]{2,1,0:T(8,128)(2,1)S(1)} %collective-permute-done.12.couple_ref, ...), custom_call_target="tpu_custom_call" | custom-call | flops 700000000 | tf_op jit(solution)/shard_map/pallas_call | solution.py:48
  24.4 1.1 %shard_map.62 = (bf16[2,128,512]{2,1,0:T(8,128)(2,1)S(1)}, bf16[2,128,256]{2,1,0:T(8,128)(2,1)S(1)}, bf16[2,128,256]{2,1,0:T(8,128)(2,1)S(1)}) custom-call(s32[6]{0:T(128)S(1)} %stack.27.sc, f32[2,128,1024]{2,1,0:T(8,128)S(1)} %get-tuple-element.66.acc_ref, bf16[2,128,512]{2,1,0:T(8,128)(2,1)S(1)} %get-tuple-element.67.hid_ref, ...), custom_call_target="tpu_custom_call" | custom-call | tf_op jit(solution)/shard_map/pallas_call | solution.py:48
  25.6 1.3 %collective-permute-start.14 = (bf16[2,128,256]{2,1,0:T(8,128)(2,1)S(1)}, bf16[2,128,256]{2,1,0:T(8,128)(2,1)S(1)}, u32[]{:S(2)}, u32[]{:S(2)}) collective-permute-start(bf16[2,128,256]{2,1,0:T(8,128)(2,1)S(1)} %get-tuple-element.70), channel_id=1, source_target_pairs={{0,4},{2,6},{4,0},{6,2},{8,12},{10,14},{12,8},{14,10},{16,20},{18,... | collective-permute-start | bytes 393224 | tf_op jit(solution)/shard_map/ppermute | solution.py:79
  26.9 3.5 %collective-permute-done.14.x_ref = bf16[2,128,256]{2,1,0:T(8,128)(2,1)S(1)} collective-permute-done((bf16[2,128,256]{2,1,0:T(8,128)(2,1)S(1)}, bf16[2,128,256]{2,1,0:T(8,128)(2,1)S(1)}, u32[]{:S(2)}, u32[]{:S(2)}) %collective-permute-start.14) | collective-permute-done | bytes 131104 | tf_op jit(solution)/shard_map/ppermute | solution.py:79
  30.4 0.6 shard_map.63.own_ref
  31.0 1.1 %collective-permute-start.22 = (bf16[2,128,768]{2,1,0:T(8,128)(2,1)S(1)}, bf16[2,128,768]{2,1,0:T(8,128)(2,1)S(1)}, u32[]{:S(2)}, u32[]{:S(2)}) collective-permute-start(bf16[2,128,768]{2,1,0:T(8,128)(2,1)S(1)} %shard_map.63.own_ref), channel_id=1, source_target_pairs={{0,4},{2,6},{4,0},{6,2},{8,12},{10,14},{12,8},{14,10},{16,20},{18,... | collective-permute-start | bytes 1179656 | tf_op jit(solution)/shard_map/ppermute | solution.py:79
  32.1 1.2 %collective-permute-start.23 = (bf16[2,128,768]{2,1,0:T(8,128)(2,1)S(1)}, bf16[2,128,768]{2,1,0:T(8,128)(2,1)S(1)}, u32[]{:S(2)}, u32[]{:S(2)}) collective-permute-start(bf16[2,128,768]{2,1,0:T(8,128)(2,1)S(1)} %shard_map.63.own_ref), channel_id=1, source_target_pairs={{0,1},{1,0},{2,3},{3,2},{4,5},{5,4},{6,7},{7,6},{8,9},{9,8},{10,11... | collective-permute-start | bytes 1179656 | tf_op jit(solution)/shard_map/ppermute | solution.py:86
  33.3 0.1 collective-permute-done.11.rest_4_
  33.4 1.8 %collective-permute-start.15 = (bf16[2,128,1024]{2,1,0:T(8,128)(2,1)S(1)}, bf16[2,128,1024]{2,1,0:T(8,128)(2,1)S(1)}, u32[]{:S(2)}, u32[]{:S(2)}) collective-permute-start(bf16[2,128,1024]{2,1,0:T(8,128)(2,1)S(1)} %collective-permute-done.11.rest_4_), channel_id=1, source_target_pairs={{0,2},{2,0},{4,6},{6,4},{8,10},{10,8},{12,14},{14,12},{16,18},{18,... | collective-permute-start | bytes 1572872 | tf_op jit(solution)/shard_map/ppermute | solution.py:79
  35.2 0.5 collective-permute-start.21
  35.7 1.4 %collective-permute-done.20.refs_2_ = bf16[2,128,512]{2,1,0:T(8,128)(2,1)S(1)} collective-permute-done((bf16[2,128,512]{2,1,0:T(8,128)(2,1)S(1)}, bf16[2,128,512]{2,1,0:T(8,128)(2,1)S(1)}, u32[]{:S(2)}, u32[]{:S(2)}) %collective-permute-start.20) | collective-permute-done | bytes 262176 | tf_op jit(solution)/shard_map/ppermute | solution.py:79
  37.1 0.4 collective-permute-done.21.refs_3_
  37.5 0.7 %shard_map.65.refs_7_ = bf16[2,512,512]{2,1,0:T(8,128)(2,1)S(1)} custom-call(s32[6]{0:T(128)S(1)} %stack.27.sc, bf16[2,128,512]{2,1,0:T(8,128)(2,1)S(1)} %bitcast.17, bf16[2,128,512]{2,1,0:T(8,128)(2,1)S(1)} %collective-permute-done.8.refs_1_, bf16[2,128,512]{2,1,0:T(8,128)(2,1)S(1)} %collective-permute-done.20.refs_2_, ...), custom_call_target="tpu_custom_call" | custom-call | tf_op jit(solution)/shard_map/pallas_call | solution.py:48
  38.2 0.4 collective-permute-start.16
  38.5 1.2 %collective-permute-start.17 = (bf16[2,64,1024]{2,1,0:T(8,128)(2,1)S(1)}, bf16[2,64,1024]{2,1,0:T(8,128)(2,1)S(1)}, u32[]{:S(2)}, u32[]{:S(2)}) collective-permute-start(bf16[2,64,1024]{2,1,0:T(8,128)(2,1)S(1)} %get-tuple-element.76), channel_id=1, source_target_pairs={{0,1},{1,0},{2,3},{3,2},{4,5},{5,4},{6,7},{7,6},{8,9},{9,8},{10,11... | collective-permute-start | bytes 786440 | tf_op jit(solution)/shard_map/ppermute | solution.py:86
  39.7 0.8 %collective-permute-done.22.x_ref = bf16[2,128,768]{2,1,0:T(8,128)(2,1)S(1)} collective-permute-done((bf16[2,128,768]{2,1,0:T(8,128)(2,1)S(1)}, bf16[2,128,768]{2,1,0:T(8,128)(2,1)S(1)}, u32[]{:S(2)}, u32[]{:S(2)}) %collective-permute-start.22) | collective-permute-done | bytes 393248 | tf_op jit(solution)/shard_map/ppermute | solution.py:79
  40.5 0.6 shard_map.67.refs_0_
  41.1 2.1 %collective-permute-start.25 = (bf16[2,128,1536]{2,1,0:T(8,128)(2,1)S(1)}, bf16[2,128,1536]{2,1,0:T(8,128)(2,1)S(1)}, u32[]{:S(2)}, u32[]{:S(2)}) collective-permute-start(bf16[2,128,1536]{2,1,0:T(8,128)(2,1)S(1)} %shard_map.67.refs_0_), channel_id=1, source_target_pairs={{0,2},{2,0},{4,6},{6,4},{8,10},{10,8},{12,14},{14,12},{16,18},{18,... | collective-permute-start | bytes 2359304 | tf_op jit(solution)/shard_map/ppermute | solution.py:79
  43.2 1.0 %collective-permute-start.24 = (bf16[2,128,768]{2,1,0:T(8,128)(2,1)S(1)}, bf16[2,128,768]{2,1,0:T(8,128)(2,1)S(1)}, u32[]{:S(2)}, u32[]{:S(2)}) collective-permute-start(bf16[2,128,768]{2,1,0:T(8,128)(2,1)S(1)} %collective-permute-done.23.refs_1_), channel_id=1, source_target_pairs={{0,4},{2,6},{4,0},{6,2},{8,12},{10,14},{12,8},{14,10},{16,20},{18,... | collective-permute-start | bytes 1179656 | tf_op jit(solution)/shard_map/ppermute | solution.py:79
  44.3 4.3 %shard_map.64 = (bf16[2,512,1536]{2,1,0:T(8,128)(2,1)S(1)}, bf16[2,256,512]{2,1,0:T(8,128)(2,1)S(1)}) custom-call(s32[6]{0:T(128)S(1)} %stack.27.sc, bf16[2,512,512]{2,1,0:T(8,128)(2,1)S(1)} %shard_map.60.w_ref, bf16[2,256,512]{2,1,0:T(8,128)(2,1)S(1)} %get-tuple-element.47.end_ref.refs_8_.own_ref, ...), custom_call_target="tpu_custom_call" | custom-call | flops 400000000 | tf_op jit(solution)/shard_map/pallas_call | solution.py:48
  48.6 2.8 %collective-permute-start.18 = (bf16[2,64,1024]{2,1,0:T(8,128)(2,1)S(1)}, bf16[2,64,1024]{2,1,0:T(8,128)(2,1)S(1)}, u32[]{:S(2)}, u32[]{:S(2)}) collective-permute-start(bf16[2,64,1024]{2,1,0:T(8,128)(2,1)S(1)} %collective-permute-done.16.refs_1_), channel_id=1, source_target_pairs={{0,2},{2,0},{4,6},{6,4},{8,10},{10,8},{12,14},{14,12},{16,18},{18,... | collective-permute-start | bytes 786440 | tf_op jit(solution)/shard_map/ppermute | solution.py:79
  51.4 0.9 %collective-permute-done.17.refs_2_ = bf16[2,64,1024]{2,1,0:T(8,128)(2,1)S(1)} collective-permute-done((bf16[2,64,1024]{2,1,0:T(8,128)(2,1)S(1)}, bf16[2,64,1024]{2,1,0:T(8,128)(2,1)S(1)}, u32[]{:S(2)}, u32[]{:S(2)}) %collective-permute-start.17) | collective-permute-done | bytes 262176 | tf_op jit(solution)/shard_map/ppermute | solution.py:86
  52.3 2.6 %collective-permute-start.19 = (bf16[2,64,1024]{2,1,0:T(8,128)(2,1)S(1)}, bf16[2,64,1024]{2,1,0:T(8,128)(2,1)S(1)}, u32[]{:S(2)}, u32[]{:S(2)}) collective-permute-start(bf16[2,64,1024]{2,1,0:T(8,128)(2,1)S(1)} %collective-permute-done.17.refs_2_), channel_id=1, source_target_pairs={{0,2},{2,0},{4,6},{6,4},{8,10},{10,8},{12,14},{14,12},{16,18},{18,... | collective-permute-start | bytes 786440 | tf_op jit(solution)/shard_map/ppermute | solution.py:79
  54.8 0.5 collective-permute-start.27
  55.4 0.6 %collective-permute-done.19.refs_4_ = bf16[2,64,1024]{2,1,0:T(8,128)(2,1)S(1)} collective-permute-done((bf16[2,64,1024]{2,1,0:T(8,128)(2,1)S(1)}, bf16[2,64,1024]{2,1,0:T(8,128)(2,1)S(1)}, u32[]{:S(2)}, u32[]{:S(2)}) %collective-permute-start.19) | collective-permute-done | bytes 262176 | tf_op jit(solution)/shard_map/ppermute | solution.py:79
  56.0 3.3 %shard_map.66 = (bf16[2,512,512]{2,1,0:T(8,128)(2,1)S(1)}, bf16[512,512]{1,0:T(8,128)(2,1)S(1)}, bf16[512,512]{1,0:T(8,128)(2,1)S(1)}) custom-call(s32[6]{0:T(128)S(1)} %stack.27.sc, bf16[2,256,1536]{2,1,0:T(8,128)(2,1)S(1)} %get-tuple-element.50.end_ref, bf16[2,256,1536]{2,1,0:T(8,128)(2,1)S(1)} %get-tuple-element.55.kept_ref, ...), custom_call_target="tpu_custom_call" | custom-call | flops 3000000000 | tf_op jit(solution)/shard_map/pallas_call | solution.py:48
  59.4 3.4 %shard_map.68 = bf16[2,1,256,1536]{3,2,1,0:T(8,128)(2,1)} custom-call(s32[6]{0:T(128)S(1)} %stack.27.sc, bf16[2,512,512]{2,1,0:T(8,128)(2,1)S(1)} %get-tuple-element.80.hid_ref, bf16[512,512]{1,0:T(8,128)(2,1)S(1)} %get-tuple-element.81.first_ref, bf16[512,512]{1,0:T(8,128)(2,1)S(1)} %get-tuple-element.82.slots_ref, ...), custom_call_target="tpu_custom_call" | custom-call | tf_op jit(solution)/shard_map/pallas_call | solution.py:48
  (35 shorter events, 0.2 us)
Async XLA Ops:
  0.0 4.3 %copy-start.4 = (s32[1,8,512]{2,1,0:T(8,128)S(1)}, s32[1,8,512]{2,1,0:T(8,128)}, u32[]{:S(2)}) copy-start(s32[1,8,512]{2,1,0:T(8,128)} %param.8) | copy-start | bytes 49156
  0.1 2.3 %copy-start = (bf16[2,1,1,3,256,1536]{5,4,3,2,1,0:T(8,128)(2,1)S(1)}, bf16[2,1,1,3,256,1536]{5,4,3,2,1,0:T(8,128)(2,1)}, u32[]{:S(2)}) copy-start(bf16[2,1,1,3,256,1536]{5,4,3,2,1,0:T(8,128)(2,1)} %param.5) | copy-start | bytes 14155780
  2.4 1.9 %copy-start.5 = (s32[1,4,512]{2,1,0:T(4,128)S(1)}, s32[1,4,512]{2,1,0:T(4,128)}, u32[]{:S(2)}) copy-start(s32[1,4,512]{2,1,0:T(4,128)} %param.9) | copy-start | bytes 24580
  2.4 8.3 %copy-start.1 = (bf16[2,1,1,3,256,1536]{5,4,3,2,1,0:T(8,128)(2,1)S(1)}, bf16[2,1,1,3,256,1536]{5,4,3,2,1,0:T(8,128)(2,1)}, u32[]{:S(2)}) copy-start(bf16[2,1,1,3,256,1536]{5,4,3,2,1,0:T(8,128)(2,1)} %param.5) | copy-start | bytes 14155780
  3.1 3.3 %copy-start.2 = (bf16[2,1,256,512]{3,2,1,0:T(8,128)(2,1)S(1)}, bf16[2,1,256,512]{3,2,1,0:T(8,128)(2,1)}, u32[]{:S(2)}) copy-start(bf16[2,1,256,512]{3,2,1,0:T(8,128)(2,1)} %param.6) | copy-start | bytes 1572868
  3.2 6.1 %copy-start.3 = (bf16[2,1,128,512]{3,2,1,0:T(8,128)(2,1)S(1)}, bf16[2,1,128,512]{3,2,1,0:T(8,128)(2,1)}, u32[]{:S(2)}) copy-start(bf16[2,1,128,512]{3,2,1,0:T(8,128)(2,1)} %param.7) | copy-start | bytes 786436
  3.2 2.0 %collective-permute-start = (bf16[2,256,512]{2,1,0:T(8,128)(2,1)S(1)}, bf16[2,256,512]{2,1,0:T(8,128)(2,1)S(1)}, u32[]{:S(2)}, u32[]{:S(2)}) collective-permute-start(bf16[2,256,512]{2,1,0:T(8,128)(2,1)S(1)} %get-tuple-element.45.own_ref), channel_id=1, source_target_pairs={{0,2},{2,0},{4,6},{6,4},{8,10},{10,8},{12,14},{14,12},{16,18},{18,... | collective-permute-start | bytes 1572872 | tf_op jit(solution)/shard_map/ppermute | solution.py:79
  3.3 3.6 %collective-permute-start.1 = (bf16[2,256,512]{2,1,0:T(8,128)(2,1)S(1)}, bf16[2,256,512]{2,1,0:T(8,128)(2,1)S(1)}, u32[]{:S(2)}, u32[]{:S(2)}) collective-permute-start(bf16[2,256,512]{2,1,0:T(8,128)(2,1)S(1)} %get-tuple-element.51.refs_0_), channel_id=1, source_target_pairs={{0,2},{2,0},{4,6},{6,4},{8,10},{10,8},{12,14},{14,12},{16,18},{18,... | collective-permute-start | bytes 1572872 | tf_op jit(solution)/shard_map/ppermute | solution.py:79
  3.7 5.5 %collective-permute-start.2 = (bf16[2,256,512]{2,1,0:T(8,128)(2,1)S(1)}, bf16[2,256,512]{2,1,0:T(8,128)(2,1)S(1)}, u32[]{:S(2)}, u32[]{:S(2)}) collective-permute-start(bf16[2,256,512]{2,1,0:T(8,128)(2,1)S(1)} %get-tuple-element.52.refs_1_), channel_id=1, source_target_pairs={{0,2},{2,0},{4,6},{6,4},{8,10},{10,8},{12,14},{14,12},{16,18},{18,... | collective-permute-start | bytes 1572872 | tf_op jit(solution)/shard_map/ppermute | solution.py:79
  3.8 6.7 %collective-permute-start.3 = (bf16[2,256,512]{2,1,0:T(8,128)(2,1)S(1)}, bf16[2,256,512]{2,1,0:T(8,128)(2,1)S(1)}, u32[]{:S(2)}, u32[]{:S(2)}) collective-permute-start(bf16[2,256,512]{2,1,0:T(8,128)(2,1)S(1)} %get-tuple-element.53.refs_2_), channel_id=1, source_target_pairs={{0,2},{2,0},{4,6},{6,4},{8,10},{10,8},{12,14},{14,12},{16,18},{18,... | collective-permute-start | bytes 1572872 | tf_op jit(solution)/shard_map/ppermute | solution.py:79
  4.3 7.6 %collective-permute-start.4 = (bf16[2,256,512]{2,1,0:T(8,128)(2,1)S(1)}, bf16[2,256,512]{2,1,0:T(8,128)(2,1)S(1)}, u32[]{:S(2)}, u32[]{:S(2)}) collective-permute-start(bf16[2,256,512]{2,1,0:T(8,128)(2,1)S(1)} %get-tuple-element.47.end_ref.refs_8_.own_ref), channel_id=1, source_target_pairs={{0,2},{2,0},{4,6},{6,4},{8,10},{10,8},{12,14},{14,12},{16,18},{18,... | collective-permute-start | bytes 1572872 | tf_op jit(solution)/shard_map/ppermute | solution.py:79
  6.4 15.7 %collective-permute-start.5 = (bf16[2,256,512]{2,1,0:T(8,128)(2,1)S(1)}, bf16[2,256,512]{2,1,0:T(8,128)(2,1)S(1)}, u32[]{:S(2)}, u32[]{:S(2)}) collective-permute-start(bf16[2,256,512]{2,1,0:T(8,128)(2,1)S(1)} %bitcast.13), channel_id=1, source_target_pairs={{0,2},{2,0},{4,6},{6,4},{8,10},{10,8},{12,14},{14,12},{16,18},{18,... | collective-permute-start | bytes 1572872 | tf_op jit(solution)/shard_map/ppermute | solution.py:79
  6.9 8.6 %collective-permute-start.6 = (bf16[2,128,512]{2,1,0:T(8,128)(2,1)S(1)}, bf16[2,128,512]{2,1,0:T(8,128)(2,1)S(1)}, u32[]{:S(2)}, u32[]{:S(2)}) collective-permute-start(bf16[2,128,512]{2,1,0:T(8,128)(2,1)S(1)} %get-tuple-element.57), channel_id=1, source_target_pairs={{0,1},{1,0},{2,3},{3,2},{4,5},{5,4},{6,7},{7,6},{8,9},{9,8},{10,11... | collective-permute-start | bytes 786440 | tf_op jit(solution)/shard_map/ppermute | solution.py:86
  9.3 10.7 %collective-permute-start.8 = (bf16[2,128,512]{2,1,0:T(8,128)(2,1)S(1)}, bf16[2,128,512]{2,1,0:T(8,128)(2,1)S(1)}, u32[]{:S(2)}, u32[]{:S(2)}) collective-permute-start(bf16[2,128,512]{2,1,0:T(8,128)(2,1)S(1)} %bitcast.15), channel_id=1, source_target_pairs={{0,4},{2,6},{4,0},{6,2},{8,12},{10,14},{12,8},{14,10},{16,20},{18,... | collective-permute-start | bytes 786440 | tf_op jit(solution)/shard_map/ppermute | solution.py:79
  10.5 11.3 %collective-permute-start.7 = (bf16[2,128,512]{2,1,0:T(8,128)(2,1)S(1)}, bf16[2,128,512]{2,1,0:T(8,128)(2,1)S(1)}, u32[]{:S(2)}, u32[]{:S(2)}) collective-permute-start(bf16[2,128,512]{2,1,0:T(8,128)(2,1)S(1)} %get-tuple-element.58), channel_id=1, source_target_pairs={{0,1},{1,0},{2,3},{3,2},{4,5},{5,4},{6,7},{7,6},{8,9},{9,8},{10,11... | collective-permute-start | bytes 786440 | tf_op jit(solution)/shard_map/ppermute | solution.py:86
  11.8 11.1 %collective-permute-start.12 = (bf16[2,128,512]{2,1,0:T(8,128)(2,1)S(1)}, bf16[2,128,512]{2,1,0:T(8,128)(2,1)S(1)}, u32[]{:S(2)}, u32[]{:S(2)}) collective-permute-start(bf16[2,128,512]{2,1,0:T(8,128)(2,1)S(1)} %get-tuple-element.64), channel_id=1, source_target_pairs={{0,2},{2,0},{4,6},{6,4},{8,10},{10,8},{12,14},{14,12},{16,18},{18,... | collective-permute-start | bytes 786440 | tf_op jit(solution)/shard_map/ppermute | solution.py:79
  15.6 7.4 %collective-permute-start.13 = (bf16[2,128,512]{2,1,0:T(8,128)(2,1)S(1)}, bf16[2,128,512]{2,1,0:T(8,128)(2,1)S(1)}, u32[]{:S(2)}, u32[]{:S(2)}) collective-permute-start(bf16[2,128,512]{2,1,0:T(8,128)(2,1)S(1)} %get-tuple-element.65), channel_id=1, source_target_pairs={{0,2},{2,0},{4,6},{6,4},{8,10},{10,8},{12,14},{14,12},{16,18},{18,... | collective-permute-start | bytes 786440 | tf_op jit(solution)/shard_map/ppermute | solution.py:79
  20.0 13.4 %collective-permute-start.11 = (bf16[2,128,1024]{2,1,0:T(8,128)(2,1)S(1)}, bf16[2,128,1024]{2,1,0:T(8,128)(2,1)S(1)}, u32[]{:S(2)}, u32[]{:S(2)}) collective-permute-start(bf16[2,128,1024]{2,1,0:T(8,128)(2,1)S(1)} %get-tuple-element.62), channel_id=1, source_target_pairs={{0,1},{1,0},{2,3},{3,2},{4,5},{5,4},{6,7},{7,6},{8,9},{9,8},{10,11... | collective-permute-start | bytes 1572872 | tf_op jit(solution)/shard_map/ppermute | solution.py:86
  21.8 2.6 %collective-permute-start.9 = (bf16[2,128,512]{2,1,0:T(8,128)(2,1)S(1)}, bf16[2,128,512]{2,1,0:T(8,128)(2,1)S(1)}, u32[]{:S(2)}, u32[]{:S(2)}) collective-permute-start(bf16[2,128,512]{2,1,0:T(8,128)(2,1)S(1)} %collective-permute-done.6.rest_0_), channel_id=1, source_target_pairs={{0,2},{2,0},{4,6},{6,4},{8,10},{10,8},{12,14},{14,12},{16,18},{18,... | collective-permute-start | bytes 786440 | tf_op jit(solution)/shard_map/ppermute | solution.py:79
  22.1 2.3 %collective-permute-start.10 = (bf16[2,128,512]{2,1,0:T(8,128)(2,1)S(1)}, bf16[2,128,512]{2,1,0:T(8,128)(2,1)S(1)}, u32[]{:S(2)}, u32[]{:S(2)}) collective-permute-start(bf16[2,128,512]{2,1,0:T(8,128)(2,1)S(1)} %collective-permute-done.7.rest_1_), channel_id=1, source_target_pairs={{0,2},{2,0},{4,6},{6,4},{8,10},{10,8},{12,14},{14,12},{16,18},{18,... | collective-permute-start | bytes 786440 | tf_op jit(solution)/shard_map/ppermute | solution.py:79
  25.6 4.8 %collective-permute-start.14 = (bf16[2,128,256]{2,1,0:T(8,128)(2,1)S(1)}, bf16[2,128,256]{2,1,0:T(8,128)(2,1)S(1)}, u32[]{:S(2)}, u32[]{:S(2)}) collective-permute-start(bf16[2,128,256]{2,1,0:T(8,128)(2,1)S(1)} %get-tuple-element.70), channel_id=1, source_target_pairs={{0,4},{2,6},{4,0},{6,2},{8,12},{10,14},{12,8},{14,10},{16,20},{18,... | collective-permute-start | bytes 393224 | tf_op jit(solution)/shard_map/ppermute | solution.py:79
  31.0 9.5 %collective-permute-start.22 = (bf16[2,128,768]{2,1,0:T(8,128)(2,1)S(1)}, bf16[2,128,768]{2,1,0:T(8,128)(2,1)S(1)}, u32[]{:S(2)}, u32[]{:S(2)}) collective-permute-start(bf16[2,128,768]{2,1,0:T(8,128)(2,1)S(1)} %shard_map.63.own_ref), channel_id=1, source_target_pairs={{0,4},{2,6},{4,0},{6,2},{8,12},{10,14},{12,8},{14,10},{16,20},{18,... | collective-permute-start | bytes 1179656 | tf_op jit(solution)/shard_map/ppermute | solution.py:79
  32.1 11.2 %collective-permute-start.23 = (bf16[2,128,768]{2,1,0:T(8,128)(2,1)S(1)}, bf16[2,128,768]{2,1,0:T(8,128)(2,1)S(1)}, u32[]{:S(2)}, u32[]{:S(2)}) collective-permute-start(bf16[2,128,768]{2,1,0:T(8,128)(2,1)S(1)} %shard_map.63.own_ref), channel_id=1, source_target_pairs={{0,1},{1,0},{2,3},{3,2},{4,5},{5,4},{6,7},{7,6},{8,9},{9,8},{10,11... | collective-permute-start | bytes 1179656 | tf_op jit(solution)/shard_map/ppermute | solution.py:86
  33.4 10.9 %collective-permute-start.15 = (bf16[2,128,1024]{2,1,0:T(8,128)(2,1)S(1)}, bf16[2,128,1024]{2,1,0:T(8,128)(2,1)S(1)}, u32[]{:S(2)}, u32[]{:S(2)}) collective-permute-start(bf16[2,128,1024]{2,1,0:T(8,128)(2,1)S(1)} %collective-permute-done.11.rest_4_), channel_id=1, source_target_pairs={{0,2},{2,0},{4,6},{6,4},{8,10},{10,8},{12,14},{14,12},{16,18},{18,... | collective-permute-start | bytes 1572872 | tf_op jit(solution)/shard_map/ppermute | solution.py:79
  35.2 1.9 %collective-permute-start.20 = (bf16[2,128,512]{2,1,0:T(8,128)(2,1)S(1)}, bf16[2,128,512]{2,1,0:T(8,128)(2,1)S(1)}, u32[]{:S(2)}, u32[]{:S(2)}) collective-permute-start(bf16[2,128,512]{2,1,0:T(8,128)(2,1)S(1)} %bitcast.16), channel_id=1, source_target_pairs={{0,2},{2,0},{4,6},{6,4},{8,10},{10,8},{12,14},{14,12},{16,18},{18,... | collective-permute-start | bytes 786440 | tf_op jit(solution)/shard_map/ppermute | solution.py:79
  35.2 2.3 %collective-permute-start.21 = (bf16[2,128,512]{2,1,0:T(8,128)(2,1)S(1)}, bf16[2,128,512]{2,1,0:T(8,128)(2,1)S(1)}, u32[]{:S(2)}, u32[]{:S(2)}) collective-permute-start(bf16[2,128,512]{2,1,0:T(8,128)(2,1)S(1)} %collective-permute-done.8.refs_1_), channel_id=1, source_target_pairs={{0,2},{2,0},{4,6},{6,4},{8,10},{10,8},{12,14},{14,12},{16,18},{18,... | collective-permute-start | bytes 786440 | tf_op jit(solution)/shard_map/ppermute | solution.py:79
  38.2 10.4 %collective-permute-start.16 = (bf16[2,64,1024]{2,1,0:T(8,128)(2,1)S(1)}, bf16[2,64,1024]{2,1,0:T(8,128)(2,1)S(1)}, u32[]{:S(2)}, u32[]{:S(2)}) collective-permute-start(bf16[2,64,1024]{2,1,0:T(8,128)(2,1)S(1)} %get-tuple-element.74), channel_id=1, source_target_pairs={{0,1},{1,0},{2,3},{3,2},{4,5},{5,4},{6,7},{7,6},{8,9},{9,8},{10,11... | collective-permute-start | bytes 786440 | tf_op jit(solution)/shard_map/ppermute | solution.py:86
  38.5 13.7 %collective-permute-start.17 = (bf16[2,64,1024]{2,1,0:T(8,128)(2,1)S(1)}, bf16[2,64,1024]{2,1,0:T(8,128)(2,1)S(1)}, u32[]{:S(2)}, u32[]{:S(2)}) collective-permute-start(bf16[2,64,1024]{2,1,0:T(8,128)(2,1)S(1)} %get-tuple-element.76), channel_id=1, source_target_pairs={{0,1},{1,0},{2,3},{3,2},{4,5},{5,4},{6,7},{7,6},{8,9},{9,8},{10,11... | collective-permute-start | bytes 786440 | tf_op jit(solution)/shard_map/ppermute | solution.py:86
  41.1 18.2 %collective-permute-start.25 = (bf16[2,128,1536]{2,1,0:T(8,128)(2,1)S(1)}, bf16[2,128,1536]{2,1,0:T(8,128)(2,1)S(1)}, u32[]{:S(2)}, u32[]{:S(2)}) collective-permute-start(bf16[2,128,1536]{2,1,0:T(8,128)(2,1)S(1)} %shard_map.67.refs_0_), channel_id=1, source_target_pairs={{0,2},{2,0},{4,6},{6,4},{8,10},{10,8},{12,14},{14,12},{16,18},{18,... | collective-permute-start | bytes 2359304 | tf_op jit(solution)/shard_map/ppermute | solution.py:79
  43.2 11.6 %collective-permute-start.24 = (bf16[2,128,768]{2,1,0:T(8,128)(2,1)S(1)}, bf16[2,128,768]{2,1,0:T(8,128)(2,1)S(1)}, u32[]{:S(2)}, u32[]{:S(2)}) collective-permute-start(bf16[2,128,768]{2,1,0:T(8,128)(2,1)S(1)} %collective-permute-done.23.refs_1_), channel_id=1, source_target_pairs={{0,4},{2,6},{4,0},{6,2},{8,12},{10,14},{12,8},{14,10},{16,20},{18,... | collective-permute-start | bytes 1179656 | tf_op jit(solution)/shard_map/ppermute | solution.py:79
  48.6 6.8 %collective-permute-start.18 = (bf16[2,64,1024]{2,1,0:T(8,128)(2,1)S(1)}, bf16[2,64,1024]{2,1,0:T(8,128)(2,1)S(1)}, u32[]{:S(2)}, u32[]{:S(2)}) collective-permute-start(bf16[2,64,1024]{2,1,0:T(8,128)(2,1)S(1)} %collective-permute-done.16.refs_1_), channel_id=1, source_target_pairs={{0,2},{2,0},{4,6},{6,4},{8,10},{10,8},{12,14},{14,12},{16,18},{18,... | collective-permute-start | bytes 786440 | tf_op jit(solution)/shard_map/ppermute | solution.py:79
  52.3 3.7 %collective-permute-start.19 = (bf16[2,64,1024]{2,1,0:T(8,128)(2,1)S(1)}, bf16[2,64,1024]{2,1,0:T(8,128)(2,1)S(1)}, u32[]{:S(2)}, u32[]{:S(2)}) collective-permute-start(bf16[2,64,1024]{2,1,0:T(8,128)(2,1)S(1)} %collective-permute-done.17.refs_2_), channel_id=1, source_target_pairs={{0,2},{2,0},{4,6},{6,4},{8,10},{10,8},{12,14},{14,12},{16,18},{18,... | collective-permute-start | bytes 786440 | tf_op jit(solution)/shard_map/ppermute | solution.py:79
  54.8 4.5 %collective-permute-start.26 = (bf16[2,128,768]{2,1,0:T(8,128)(2,1)S(1)}, bf16[2,128,768]{2,1,0:T(8,128)(2,1)S(1)}, u32[]{:S(2)}, u32[]{:S(2)}) collective-permute-start(bf16[2,128,768]{2,1,0:T(8,128)(2,1)S(1)} %collective-permute-done.23.refs_1_), channel_id=1, source_target_pairs={{0,2},{2,0},{4,6},{6,4},{8,10},{10,8},{12,14},{14,12},{16,18},{18,... | collective-permute-start | bytes 1179656 | tf_op jit(solution)/shard_map/ppermute | solution.py:79
  54.8 4.5 %collective-permute-start.27 = (bf16[2,128,768]{2,1,0:T(8,128)(2,1)S(1)}, bf16[2,128,768]{2,1,0:T(8,128)(2,1)S(1)}, u32[]{:S(2)}, u32[]{:S(2)}) collective-permute-start(bf16[2,128,768]{2,1,0:T(8,128)(2,1)S(1)} %collective-permute-done.24.refs_2_), channel_id=1, source_target_pairs={{0,2},{2,0},{4,6},{6,4},{8,10},{10,8},{12,14},{14,12},{16,18},{18,... | collective-permute-start | bytes 1179656 | tf_op jit(solution)/shard_map/ppermute | solution.py:79

commit v21 on v19

--- a/solution.py
+++ b/solution.py
@@ -356,10 +356,11 @@
     two_rows = call(join_kernel, after(scalars, weight_two), [two_own, two_x], two_shape, cost=JOIN_COST)
     two_xy = [box_permute(after(a, *two_rows), 2) for a in two_y]
     two_rows = [*two_rows, *(a for pair in zip(two_y, two_xy) for a in pair)]
-    two_sib = [box_permute(a, 1) for a in two_rows]
+    two_sib = [box_permute(two_rows[0], 1)]
 
     ends_far = [face_permute(after(a, two_own), i // 2 + 1) for i, a in enumerate(kept_out[: 2 * nf])]
     ends_fwd = [box_permute(after(a, solved_one), 1) for a in ends_far]
+    two_sib += [box_permute(after(a, *ends_fwd), 1) for a in two_rows[1:]]
 
     def level_one_kernel(sc, end_ref, kept_ref, *refs):
         mixed = refs[:nf], refs[nf : 2 * nf]

time: 63.3 us -> 67.1 us (1.060)
  waiting for transfers between devices: 10.1 us -> 18.8 us
  starting transfers between devices: 27.3 us -> 22.4 us
    ppermute x6, waiting for transfers between devices: 3.42 us -> 8.75 us  [face_permute(): return lax.ppermute(array, ('box', 'face'), pairs)]
    ppermute x22, starting transfers between devices: 20.2 us -> 15.8 us  [box_permute(): return lax.ppermute(array, 'box', [(b, b ^ mask) for b in range(n_box)])]
    ppermute x22, waiting for transfers between devices: 6.67 us -> 10 us  [box_permute(): return lax.ppermute(array, 'box', [(b, b ^ mask) for b in range(n_box)])]
  transfers between devices with their start and end apart: 28 -> 28, of which waited for: 8 -> 7; matrix products, arithmetic and copies ran while one was open for 0% -> 0% of each run, Pallas kernels for 30% -> 28%
where the time goes in v21:
time: 67.1 us; the launch traced here: 66.7 us
  Pallas kernels  22.7 us (34%)
  starting transfers between devices  22.4 us (33%)
  waiting for transfers between devices  18.8 us (28%)
  local copies, waits for them, and re-layouts  2.45 us (4%)
    pallas_call x14, Pallas kernels, call(): pl.pallas_call(kernel, in_specs=[pl.BlockSpec(memory_space=pltpu.SMEM)] +...  22.7 us
    ppermute x22, starting transfers between devices, box_permute(): return lax.ppermute(array, 'box', [(b, b ^ mask) for b in range(n_box)])  15.8 us
    ppermute x22, waiting for transfers between devices, box_permute(): return lax.ppermute(array, 'box', [(b, b ^ mask) for b in range(n_box)])  10 us
    ppermute x6, waiting for transfers between devices, face_permute(): return lax.ppermute(array, ('box', 'face'), pairs)  8.75 us
    ppermute x6, starting transfers between devices, face_permute(): return lax.ppermute(array, ('box', 'face'), pairs)  6.56 us
    unnamed x12, local copies, waits for them, and re-layouts  2.36 us
  transfers between devices with their start and end apart: 28, of which 7 were waited for; matrix products, arithmetic and copies ran while one was open for 0% of the time, Pallas kernels for 28%

profile of v21, /device:TPU:1, one launch (start us, length us, event | category | flops | bytes accessed | tf_op | source)
XLA Modules:
  0.0 66.7 jit_solution(17205697104835989905)
XLA Ops:
  0.0 0.1 stack.27.sc
  0.1 2.3 %copy-done = bf16[2,1,1,3,256,1536]{5,4,3,2,1,0:T(8,128)(2,1)S(1)} copy-done((bf16[2,1,1,3,256,1536]{5,4,3,2,1,0:T(8,128)(2,1)S(1)}, bf16[2,1,1,3,256,1536]{5,4,3,2,1,0:T(8,128)(2,1)}, u32[]{:S(2)}) %copy-start) | copy-done | bytes 4718616
  2.4 0.7 %shard_map.55 = (bf16[2,256,512]{2,1,0:T(8,128)(2,1)S(1)}, bf16[2,256,512]{2,1,0:T(8,128)(2,1)S(1)}, bf16[2,256,512]{2,1,0:T(8,128)(2,1)S(1)}, bf16[2,256,512]{2,1,0:T(8,128)(2,1)S(1)}, bf16[2,256,512]{2,1,0:T(8,128)(2,1)S(1)}) custom-call(s32[6]{0:T(128)S(1)} %stack.27.sc, bf16[2,3,256,1536]{3,2,1,0:T(8,128)(2,1)S(1)} %bitcast.11), custom_call_target="tpu_custom_call" | custom-call | tf_op jit(solution)/shard_map/pallas_call | solution.py:48
  3.2 0.1 collective-permute-start
  3.3 0.5 collective-permute-start.1
  3.8 0.4 collective-permute-start.3
  4.3 0.8 %shard_map.56 = (s32[1,512]{1,0:T(1,128)S(1)}, s32[512,1]{1,0:T(8,128)S(1)}) custom-call(s32[6]{0:T(128)S(1)} %stack.27.sc, s32[8,512]{1,0:T(8,128)S(1)} %bitcast.18, s32[4,512]{1,0:T(4,128)S(1)} %bitcast.19), custom_call_target="tpu_custom_call" | custom-call | tf_op jit(solution)/shard_map/pallas_call | solution.py:48
  5.2 1.3 %shard_map.57 = (bf16[2,256,512]{2,1,0:T(8,128)(2,1)S(1)}, bf16[2,128,512]{2,1,0:T(8,128)(2,1)S(1)}, bf16[2,128,512]{2,1,0:T(8,128)(2,1)S(1)}) custom-call(s32[6]{0:T(128)S(1)} %stack.27.sc, bf16[2,256,512]{2,1,0:T(8,128)(2,1)S(1)} %get-tuple-element.45.own_ref, bf16[2,256,512]{2,1,0:T(8,128)(2,1)S(1)} %collective-permute-done.sib_ref, ...), custom_call_target="tpu_custom_call" | custom-call | tf_op jit(solution)/shard_map/pallas_call | solution.py:48
  6.4 0.5 collective-permute-start.8
  6.9 2.3 %collective-permute-start.9 = (bf16[2,128,512]{2,1,0:T(8,128)(2,1)S(1)}, bf16[2,128,512]{2,1,0:T(8,128)(2,1)S(1)}, u32[]{:S(2)}, u32[]{:S(2)}) collective-permute-start(bf16[2,128,512]{2,1,0:T(8,128)(2,1)S(1)} %get-tuple-element.63), channel_id=1, source_target_pairs={{0,1},{1,0},{2,3},{3,2},{4,5},{5,4},{6,7},{7,6},{8,9},{9,8},{10,11... | collective-permute-start | bytes 786440 | tf_op jit(solution)/shard_map/ppermute | solution.py:86
  9.3 1.2 %collective-permute-start.11 = (bf16[2,128,512]{2,1,0:T(8,128)(2,1)S(1)}, bf16[2,128,512]{2,1,0:T(8,128)(2,1)S(1)}, u32[]{:S(2)}, u32[]{:S(2)}) collective-permute-start(bf16[2,128,512]{2,1,0:T(8,128)(2,1)S(1)} %bitcast.15), channel_id=1, source_target_pairs={{0,4},{2,6},{4,0},{6,2},{8,12},{10,14},{12,8},{14,10},{16,20},{18,... | collective-permute-start | bytes 786440 | tf_op jit(solution)/shard_map/ppermute | solution.py:79
  10.5 0.2 collective-permute-start.10
  10.7 2.9 %shard_map.59 = (bf16[2,256,1536]{2,1,0:T(8,128)(2,1)S(1)}, bf16[2,64,1024]{2,1,0:T(8,128)(2,1)S(1)}, bf16[2,64,1024]{2,1,0:T(8,128)(2,1)S(1)}, bf16[2,128,1024]{2,1,0:T(8,128)(2,1)S(1)}) custom-call(s32[6]{0:T(128)S(1)} %stack.27.sc, bf16[2,256,512]{2,1,0:T(8,128)(2,1)S(1)} %get-tuple-element.51.refs_0_, ...), custom_call_target="tpu_custom_call" | custom-call | tf_op jit(solution)/shard_map/pallas_call | solution.py:48
  13.6 1.3 %collective-permute-start.5 = (bf16[2,128,1024]{2,1,0:T(8,128)(2,1)S(1)}, bf16[2,128,1024]{2,1,0:T(8,128)(2,1)S(1)}, u32[]{:S(2)}, u32[]{:S(2)}) collective-permute-start(bf16[2,128,1024]{2,1,0:T(8,128)(2,1)S(1)} %get-tuple-element.56), channel_id=1, source_target_pairs={{0,1},{1,0},{2,3},{3,2},{4,5},{5,4},{6,7},{7,6},{8,9},{9,8},{10,11... | collective-permute-start | bytes 1572872 | tf_op jit(solution)/shard_map/ppermute | solution.py:86
  14.9 1.1 %shard_map.58 = (bf16[2,128,1024]{2,1,0:T(8,128)(2,1)S(1)}, bf16[2,128,512]{2,1,0:T(8,128)(2,1)S(1)}, bf16[2,128,512]{2,1,0:T(8,128)(2,1)S(1)}, bf16[2,256,1536]{2,1,0:T(8,128)(2,1)S(1)}) custom-call(s32[6]{0:T(128)S(1)} %stack.27.sc, bf16[2,3,256,1536]{3,2,1,0:T(8,128)(2,1)S(1)} %bitcast.12, s32[1,512]{1,0:T(1,128)S(1)} %get-tuple-element.46.comp_ref.refs_6_), custom_call_target="tpu_custom_call" | custom-call | tf_op jit(solution)/shard_map/pallas_call | solution.py:48
  16.0 1.0 %collective-permute-start.6 = (bf16[2,128,512]{2,1,0:T(8,128)(2,1)S(1)}, bf16[2,128,512]{2,1,0:T(8,128)(2,1)S(1)}, u32[]{:S(2)}, u32[]{:S(2)}) collective-permute-start(bf16[2,128,512]{2,1,0:T(8,128)(2,1)S(1)} %get-tuple-element.58), channel_id=1, source_target_pairs={{0,2},{2,0},{4,6},{6,4},{8,10},{10,8},{12,14},{14,12},{16,18},{18,... | collective-permute-start | bytes 786440 | tf_op jit(solution)/shard_map/ppermute | solution.py:79
  17.1 0.9 %collective-permute-start.7 = (bf16[2,128,512]{2,1,0:T(8,128)(2,1)S(1)}, bf16[2,128,512]{2,1,0:T(8,128)(2,1)S(1)}, u32[]{:S(2)}, u32[]{:S(2)}) collective-permute-start(bf16[2,128,512]{2,1,0:T(8,128)(2,1)S(1)} %get-tuple-element.59), channel_id=1, source_target_pairs={{0,2},{2,0},{4,6},{6,4},{8,10},{10,8},{12,14},{14,12},{16,18},{18,... | collective-permute-start | bytes 786440 | tf_op jit(solution)/shard_map/ppermute | solution.py:79
  18.0 3.2 %collective-permute-done.10.rest_1_ = bf16[2,128,512]{2,1,0:T(8,128)(2,1)S(1)} collective-permute-done((bf16[2,128,512]{2,1,0:T(8,128)(2,1)S(1)}, bf16[2,128,512]{2,1,0:T(8,128)(2,1)S(1)}, u32[]{:S(2)}, u32[]{:S(2)}) %collective-permute-start.10) | collective-permute-done | bytes 262176 | tf_op jit(solution)/shard_map/ppermute | solution.py:86
  21.2 1.5 %collective-permute-start.12 = (bf16[2,128,512]{2,1,0:T(8,128)(2,1)S(1)}, bf16[2,128,512]{2,1,0:T(8,128)(2,1)S(1)}, u32[]{:S(2)}, u32[]{:S(2)}) collective-permute-start(bf16[2,128,512]{2,1,0:T(8,128)(2,1)S(1)} %collective-permute-done.9.rest_0_), channel_id=1, source_target_pairs={{0,2},{2,0},{4,6},{6,4},{8,10},{10,8},{12,14},{14,12},{16,18},{18,... | collective-permute-start | bytes 786440 | tf_op jit(solution)/shard_map/ppermute | solution.py:79
  22.7 0.6 shard_map.60.w_ref
  23.4 1.4 %shard_map.61 = (f32[2,128,1024]{2,1,0:T(8,128)S(1)}, bf16[2,128,512]{2,1,0:T(8,128)(2,1)S(1)}) custom-call(s32[6]{0:T(128)S(1)} %stack.27.sc, bf16[2,128,1024]{2,1,0:T(8,128)(2,1)S(1)} %get-tuple-element.57.keep_ref, bf16[2,128,512]{2,1,0:T(8,128)(2,1)S(1)} %collective-permute-done.6.couple_ref, bf16[2,128,512]{2,1,0:T(8,128)(2,1)S(1)} %collective-permute-done.7.slots_ref, ...), custom_call_target="tpu_custom_call" | custom-call | flops 700000000 | tf_op jit(solution)/shard_map/pallas_call | solution.py:48
  24.8 1.1 %shard_map.62 = (bf16[2,128,512]{2,1,0:T(8,128)(2,1)S(1)}, bf16[2,128,256]{2,1,0:T(8,128)(2,1)S(1)}, bf16[2,128,256]{2,1,0:T(8,128)(2,1)S(1)}) custom-call(s32[6]{0:T(128)S(1)} %stack.27.sc, f32[2,128,1024]{2,1,0:T(8,128)S(1)} %get-tuple-element.61.acc_ref, bf16[2,128,512]{2,1,0:T(8,128)(2,1)S(1)} %get-tuple-element.62.hid_ref, ...), custom_call_target="tpu_custom_call" | custom-call | tf_op jit(solution)/shard_map/pallas_call | solution.py:48
  25.9 1.8 %collective-permute-start.14 = (bf16[2,128,256]{2,1,0:T(8,128)(2,1)S(1)}, bf16[2,128,256]{2,1,0:T(8,128)(2,1)S(1)}, u32[]{:S(2)}, u32[]{:S(2)}) collective-permute-start(bf16[2,128,256]{2,1,0:T(8,128)(2,1)S(1)} %get-tuple-element.70), channel_id=1, source_target_pairs={{0,4},{2,6},{4,0},{6,2},{8,12},{10,14},{12,8},{14,10},{16,20},{18,... | collective-permute-start | bytes 393224 | tf_op jit(solution)/shard_map/ppermute | solution.py:79
  27.7 3.4 %collective-permute-done.14.x_ref = bf16[2,128,256]{2,1,0:T(8,128)(2,1)S(1)} collective-permute-done((bf16[2,128,256]{2,1,0:T(8,128)(2,1)S(1)}, bf16[2,128,256]{2,1,0:T(8,128)(2,1)S(1)}, u32[]{:S(2)}, u32[]{:S(2)}) %collective-permute-start.14) | collective-permute-done | bytes 131104 | tf_op jit(solution)/shard_map/ppermute | solution.py:79
  31.2 0.6 shard_map.63.own_ref
  31.7 0.7 %collective-permute-done.5.rest_4_.refs_0_ = bf16[2,128,1024]{2,1,0:T(8,128)(2,1)S(1)} collective-permute-done((bf16[2,128,1024]{2,1,0:T(8,128)(2,1)S(1)}, bf16[2,128,1024]{2,1,0:T(8,128)(2,1)S(1)}, u32[]{:S(2)}, u32[]{:S(2)}) %collective-permute-start.5) | collective-permute-done | bytes 524320 | tf_op jit(solution)/shard_map/ppermute | solution.py:86
  32.4 0.9 %collective-permute-start.15 = (bf16[2,128,1024]{2,1,0:T(8,128)(2,1)S(1)}, bf16[2,128,1024]{2,1,0:T(8,128)(2,1)S(1)}, u32[]{:S(2)}, u32[]{:S(2)}) collective-permute-start(bf16[2,128,1024]{2,1,0:T(8,128)(2,1)S(1)} %collective-permute-done.5.rest_4_.refs_0_), channel_id=1, source_target_pairs={{0,2},{2,0},{4,6},{6,4},{8,10},{10,8},{12,14},{14,12},{16,18},{18,... | collective-permute-start | bytes 1572872 | tf_op jit(solution)/shard_map/ppermute | solution.py:79
  33.4 1.4 %collective-permute-start.22 = (bf16[2,128,768]{2,1,0:T(8,128)(2,1)S(1)}, bf16[2,128,768]{2,1,0:T(8,128)(2,1)S(1)}, u32[]{:S(2)}, u32[]{:S(2)}) collective-permute-start(bf16[2,128,768]{2,1,0:T(8,128)(2,1)S(1)} %shard_map.63.own_ref), channel_id=1, source_target_pairs={{0,4},{2,6},{4,0},{6,2},{8,12},{10,14},{12,8},{14,10},{16,20},{18,... | collective-permute-start | bytes 1179656 | tf_op jit(solution)/shard_map/ppermute | solution.py:79
  34.8 0.3 collective-permute-start.20
  35.1 0.2 collective-permute-start.21
  35.3 1.2 %collective-permute-start.23 = (bf16[2,128,768]{2,1,0:T(8,128)(2,1)S(1)}, bf16[2,128,768]{2,1,0:T(8,128)(2,1)S(1)}, u32[]{:S(2)}, u32[]{:S(2)}) collective-permute-start(bf16[2,128,768]{2,1,0:T(8,128)(2,1)S(1)} %shard_map.63.own_ref), channel_id=1, source_target_pairs={{0,1},{1,0},{2,3},{3,2},{4,5},{5,4},{6,7},{7,6},{8,9},{9,8},{10,11... | collective-permute-start | bytes 1179656 | tf_op jit(solution)/shard_map/ppermute | solution.py:86
  36.6 1.0 %collective-permute-start.16 = (bf16[2,64,1024]{2,1,0:T(8,128)(2,1)S(1)}, bf16[2,64,1024]{2,1,0:T(8,128)(2,1)S(1)}, u32[]{:S(2)}, u32[]{:S(2)}) collective-permute-start(bf16[2,64,1024]{2,1,0:T(8,128)(2,1)S(1)} %get-tuple-element.73), channel_id=1, source_target_pairs={{0,1},{1,0},{2,3},{3,2},{4,5},{5,4},{6,7},{7,6},{8,9},{9,8},{10,11... | collective-permute-start | bytes 786440 | tf_op jit(solution)/shard_map/ppermute | solution.py:86
  37.6 0.4 collective-permute-start.17
  38.0 0.7 shard_map.65.refs_8_
  38.7 5.4 %collective-permute-done.22.x_ref = bf16[2,128,768]{2,1,0:T(8,128)(2,1)S(1)} collective-permute-done((bf16[2,128,768]{2,1,0:T(8,128)(2,1)S(1)}, bf16[2,128,768]{2,1,0:T(8,128)(2,1)S(1)}, u32[]{:S(2)}, u32[]{:S(2)}) %collective-permute-start.22) | collective-permute-done | bytes 393248 | tf_op jit(solution)/shard_map/ppermute | solution.py:79
  44.1 0.6 shard_map.67.refs_0_
  44.7 1.0 %collective-permute-done.23.refs_1_ = bf16[2,128,768]{2,1,0:T(8,128)(2,1)S(1)} collective-permute-done((bf16[2,128,768]{2,1,0:T(8,128)(2,1)S(1)}, bf16[2,128,768]{2,1,0:T(8,128)(2,1)S(1)}, u32[]{:S(2)}, u32[]{:S(2)}) %collective-permute-start.23) | collective-permute-done | bytes 393248 | tf_op jit(solution)/shard_map/ppermute | solution.py:86
  45.8 0.5 collective-permute-start.24
  46.2 1.6 %collective-permute-start.25 = (bf16[2,128,1536]{2,1,0:T(8,128)(2,1)S(1)}, bf16[2,128,1536]{2,1,0:T(8,128)(2,1)S(1)}, u32[]{:S(2)}, u32[]{:S(2)}) collective-permute-start(bf16[2,128,1536]{2,1,0:T(8,128)(2,1)S(1)} %shard_map.67.refs_0_), channel_id=1, source_target_pairs={{0,2},{2,0},{4,6},{6,4},{8,10},{10,8},{12,14},{14,12},{16,18},{18,... | collective-permute-start | bytes 2359304 | tf_op jit(solution)/shard_map/ppermute | solution.py:79
  47.9 4.2 %shard_map.64.refs_7_ = bf16[2,512,1536]{2,1,0:T(8,128)(2,1)S(1)} custom-call(s32[6]{0:T(128)S(1)} %stack.27.sc, bf16[2,512,512]{2,1,0:T(8,128)(2,1)S(1)} %shard_map.60.w_ref, bf16[2,256,512]{2,1,0:T(8,128)(2,1)S(1)} %get-tuple-element.47.end_ref.refs_8_.own_ref, bf16[2,256,512]{2,1,0:T(8,128)(2,1)S(1)} %collective-permute-done.4.refs_9_.endsib_ref.sib_ref, ...), custom_call_target="tpu_custom_call" | custom-call | flops 400000000 | tf_op jit(solution)/shard_map/pallas_call | solution.py:48
  52.1 1.1 %collective-permute-start.18 = (bf16[2,64,1024]{2,1,0:T(8,128)(2,1)S(1)}, bf16[2,64,1024]{2,1,0:T(8,128)(2,1)S(1)}, u32[]{:S(2)}, u32[]{:S(2)}) collective-permute-start(bf16[2,64,1024]{2,1,0:T(8,128)(2,1)S(1)} %collective-permute-done.16.refs_2_), channel_id=1, source_target_pairs={{0,2},{2,0},{4,6},{6,4},{8,10},{10,8},{12,14},{14,12},{16,18},{18,... | collective-permute-start | bytes 786440 | tf_op jit(solution)/shard_map/ppermute | solution.py:79
  53.2 3.8 %collective-permute-done.17.refs_3_ = bf16[2,64,1024]{2,1,0:T(8,128)(2,1)S(1)} collective-permute-done((bf16[2,64,1024]{2,1,0:T(8,128)(2,1)S(1)}, bf16[2,64,1024]{2,1,0:T(8,128)(2,1)S(1)}, u32[]{:S(2)}, u32[]{:S(2)}) %collective-permute-start.17) | collective-permute-done | bytes 262176 | tf_op jit(solution)/shard_map/ppermute | solution.py:86
  57.0 1.1 %collective-permute-start.19 = (bf16[2,64,1024]{2,1,0:T(8,128)(2,1)S(1)}, bf16[2,64,1024]{2,1,0:T(8,128)(2,1)S(1)}, u32[]{:S(2)}, u32[]{:S(2)}) collective-permute-start(bf16[2,64,1024]{2,1,0:T(8,128)(2,1)S(1)} %collective-permute-done.17.refs_3_), channel_id=1, source_target_pairs={{0,2},{2,0},{4,6},{6,4},{8,10},{10,8},{12,14},{14,12},{16,18},{18,... | collective-permute-start | bytes 786440 | tf_op jit(solution)/shard_map/ppermute | solution.py:79
  58.1 1.2 %collective-permute-done.19.refs_5_ = bf16[2,64,1024]{2,1,0:T(8,128)(2,1)S(1)} collective-permute-done((bf16[2,64,1024]{2,1,0:T(8,128)(2,1)S(1)}, bf16[2,64,1024]{2,1,0:T(8,128)(2,1)S(1)}, u32[]{:S(2)}, u32[]{:S(2)}) %collective-permute-start.19) | collective-permute-done | bytes 262176 | tf_op jit(solution)/shard_map/ppermute | solution.py:79
  59.3 0.4 collective-permute-start.26
  59.6 0.1 collective-permute-start.27
  59.8 3.4 %shard_map.66 = (bf16[2,512,512]{2,1,0:T(8,128)(2,1)S(1)}, bf16[512,512]{1,0:T(8,128)(2,1)S(1)}, bf16[512,512]{1,0:T(8,128)(2,1)S(1)}) custom-call(s32[6]{0:T(128)S(1)} %stack.27.sc, bf16[2,256,1536]{2,1,0:T(8,128)(2,1)S(1)} %get-tuple-element.50.end_ref, bf16[2,256,1536]{2,1,0:T(8,128)(2,1)S(1)} %get-tuple-element.55.kept_ref, ...), custom_call_target="tpu_custom_call" | custom-call | flops 3000000000 | tf_op jit(solution)/shard_map/pallas_call | solution.py:48
  63.2 3.4 %shard_map.68 = bf16[2,1,256,1536]{3,2,1,0:T(8,128)(2,1)} custom-call(s32[6]{0:T(128)S(1)} %stack.27.sc, bf16[2,512,512]{2,1,0:T(8,128)(2,1)S(1)} %get-tuple-element.78.hid_ref, bf16[512,512]{1,0:T(8,128)(2,1)S(1)} %get-tuple-element.79.first_ref, bf16[512,512]{1,0:T(8,128)(2,1)S(1)} %get-tuple-element.80.slots_ref, ...), custom_call_target="tpu_custom_call" | custom-call | tf_op jit(solution)/shard_map/pallas_call | solution.py:48
  (35 shorter events, 0.2 us)
Async XLA Ops:
  0.1 2.3 %copy-start = (bf16[2,1,1,3,256,1536]{5,4,3,2,1,0:T(8,128)(2,1)S(1)}, bf16[2,1,1,3,256,1536]{5,4,3,2,1,0:T(8,128)(2,1)}, u32[]{:S(2)}) copy-start(bf16[2,1,1,3,256,1536]{5,4,3,2,1,0:T(8,128)(2,1)} %param.5) | copy-start | bytes 14155780
  2.4 1.9 %copy-start.4 = (s32[1,8,512]{2,1,0:T(8,128)S(1)}, s32[1,8,512]{2,1,0:T(8,128)}, u32[]{:S(2)}) copy-start(s32[1,8,512]{2,1,0:T(8,128)} %param.8) | copy-start | bytes 49156
  2.4 1.9 %copy-start.5 = (s32[1,4,512]{2,1,0:T(4,128)S(1)}, s32[1,4,512]{2,1,0:T(4,128)}, u32[]{:S(2)}) copy-start(s32[1,4,512]{2,1,0:T(4,128)} %param.9) | copy-start | bytes 24580
  3.1 3.3 %copy-start.2 = (bf16[2,1,256,512]{3,2,1,0:T(8,128)(2,1)S(1)}, bf16[2,1,256,512]{3,2,1,0:T(8,128)(2,1)}, u32[]{:S(2)}) copy-start(bf16[2,1,256,512]{3,2,1,0:T(8,128)(2,1)} %param.6) | copy-start | bytes 1572868
  3.2 6.1 %copy-start.3 = (bf16[2,1,128,512]{3,2,1,0:T(8,128)(2,1)S(1)}, bf16[2,1,128,512]{3,2,1,0:T(8,128)(2,1)}, u32[]{:S(2)}) copy-start(bf16[2,1,128,512]{3,2,1,0:T(8,128)(2,1)} %param.7) | copy-start | bytes 786436
  3.2 2.0 %collective-permute-start = (bf16[2,256,512]{2,1,0:T(8,128)(2,1)S(1)}, bf16[2,256,512]{2,1,0:T(8,128)(2,1)S(1)}, u32[]{:S(2)}, u32[]{:S(2)}) collective-permute-start(bf16[2,256,512]{2,1,0:T(8,128)(2,1)S(1)} %get-tuple-element.45.own_ref), channel_id=1, source_target_pairs={{0,2},{2,0},{4,6},{6,4},{8,10},{10,8},{12,14},{14,12},{16,18},{18,... | collective-permute-start | bytes 1572872 | tf_op jit(solution)/shard_map/ppermute | solution.py:79
  3.3 3.7 %collective-permute-start.1 = (bf16[2,256,512]{2,1,0:T(8,128)(2,1)S(1)}, bf16[2,256,512]{2,1,0:T(8,128)(2,1)S(1)}, u32[]{:S(2)}, u32[]{:S(2)}) collective-permute-start(bf16[2,256,512]{2,1,0:T(8,128)(2,1)S(1)} %get-tuple-element.51.refs_0_), channel_id=1, source_target_pairs={{0,2},{2,0},{4,6},{6,4},{8,10},{10,8},{12,14},{14,12},{16,18},{18,... | collective-permute-start | bytes 1572872 | tf_op jit(solution)/shard_map/ppermute | solution.py:79
  3.7 5.5 %collective-permute-start.2 = (bf16[2,256,512]{2,1,0:T(8,128)(2,1)S(1)}, bf16[2,256,512]{2,1,0:T(8,128)(2,1)S(1)}, u32[]{:S(2)}, u32[]{:S(2)}) collective-permute-start(bf16[2,256,512]{2,1,0:T(8,128)(2,1)S(1)} %get-tuple-element.52.refs_1_), channel_id=1, source_target_pairs={{0,2},{2,0},{4,6},{6,4},{8,10},{10,8},{12,14},{14,12},{16,18},{18,... | collective-permute-start | bytes 1572872 | tf_op jit(solution)/shard_map/ppermute | solution.py:79
  3.8 6.7 %collective-permute-start.3 = (bf16[2,256,512]{2,1,0:T(8,128)(2,1)S(1)}, bf16[2,256,512]{2,1,0:T(8,128)(2,1)S(1)}, u32[]{:S(2)}, u32[]{:S(2)}) collective-permute-start(bf16[2,256,512]{2,1,0:T(8,128)(2,1)S(1)} %get-tuple-element.53.refs_2_), channel_id=1, source_target_pairs={{0,2},{2,0},{4,6},{6,4},{8,10},{10,8},{12,14},{14,12},{16,18},{18,... | collective-permute-start | bytes 1572872 | tf_op jit(solution)/shard_map/ppermute | solution.py:79
  4.3 6.5 %collective-permute-start.4 = (bf16[2,256,512]{2,1,0:T(8,128)(2,1)S(1)}, bf16[2,256,512]{2,1,0:T(8,128)(2,1)S(1)}, u32[]{:S(2)}, u32[]{:S(2)}) collective-permute-start(bf16[2,256,512]{2,1,0:T(8,128)(2,1)S(1)} %get-tuple-element.47.end_ref.refs_8_.own_ref), channel_id=1, source_target_pairs={{0,2},{2,0},{4,6},{6,4},{8,10},{10,8},{12,14},{14,12},{16,18},{18,... | collective-permute-start | bytes 1572872 | tf_op jit(solution)/shard_map/ppermute | solution.py:79
  5.2 9.7 %copy-start.1 = (bf16[2,1,1,3,256,1536]{5,4,3,2,1,0:T(8,128)(2,1)S(1)}, bf16[2,1,1,3,256,1536]{5,4,3,2,1,0:T(8,128)(2,1)}, u32[]{:S(2)}) copy-start(bf16[2,1,1,3,256,1536]{5,4,3,2,1,0:T(8,128)(2,1)} %param.5) | copy-start | bytes 14155780
  6.4 16.2 %collective-permute-start.8 = (bf16[2,256,512]{2,1,0:T(8,128)(2,1)S(1)}, bf16[2,256,512]{2,1,0:T(8,128)(2,1)S(1)}, u32[]{:S(2)}, u32[]{:S(2)}) collective-permute-start(bf16[2,256,512]{2,1,0:T(8,128)(2,1)S(1)} %bitcast.13), channel_id=1, source_target_pairs={{0,2},{2,0},{4,6},{6,4},{8,10},{10,8},{12,14},{14,12},{16,18},{18,... | collective-permute-start | bytes 1572872 | tf_op jit(solution)/shard_map/ppermute | solution.py:79
  6.9 9.1 %collective-permute-start.9 = (bf16[2,128,512]{2,1,0:T(8,128)(2,1)S(1)}, bf16[2,128,512]{2,1,0:T(8,128)(2,1)S(1)}, u32[]{:S(2)}, u32[]{:S(2)}) collective-permute-start(bf16[2,128,512]{2,1,0:T(8,128)(2,1)S(1)} %get-tuple-element.63), channel_id=1, source_target_pairs={{0,1},{1,0},{2,3},{3,2},{4,5},{5,4},{6,7},{7,6},{8,9},{9,8},{10,11... | collective-permute-start | bytes 786440 | tf_op jit(solution)/shard_map/ppermute | solution.py:86
  9.3 7.8 %collective-permute-start.11 = (bf16[2,128,512]{2,1,0:T(8,128)(2,1)S(1)}, bf16[2,128,512]{2,1,0:T(8,128)(2,1)S(1)}, u32[]{:S(2)}, u32[]{:S(2)}) collective-permute-start(bf16[2,128,512]{2,1,0:T(8,128)(2,1)S(1)} %bitcast.15), channel_id=1, source_target_pairs={{0,4},{2,6},{4,0},{6,2},{8,12},{10,14},{12,8},{14,10},{16,20},{18,... | collective-permute-start | bytes 786440 | tf_op jit(solution)/shard_map/ppermute | solution.py:79
  10.5 10.7 %collective-permute-start.10 = (bf16[2,128,512]{2,1,0:T(8,128)(2,1)S(1)}, bf16[2,128,512]{2,1,0:T(8,128)(2,1)S(1)}, u32[]{:S(2)}, u32[]{:S(2)}) collective-permute-start(bf16[2,128,512]{2,1,0:T(8,128)(2,1)S(1)} %get-tuple-element.64), channel_id=1, source_target_pairs={{0,1},{1,0},{2,3},{3,2},{4,5},{5,4},{6,7},{7,6},{8,9},{9,8},{10,11... | collective-permute-start | bytes 786440 | tf_op jit(solution)/shard_map/ppermute | solution.py:86
  13.6 18.8 %collective-permute-start.5 = (bf16[2,128,1024]{2,1,0:T(8,128)(2,1)S(1)}, bf16[2,128,1024]{2,1,0:T(8,128)(2,1)S(1)}, u32[]{:S(2)}, u32[]{:S(2)}) collective-permute-start(bf16[2,128,1024]{2,1,0:T(8,128)(2,1)S(1)} %get-tuple-element.56), channel_id=1, source_target_pairs={{0,1},{1,0},{2,3},{3,2},{4,5},{5,4},{6,7},{7,6},{8,9},{9,8},{10,11... | collective-permute-start | bytes 1572872 | tf_op jit(solution)/shard_map/ppermute | solution.py:86
  16.0 7.3 %collective-permute-start.6 = (bf16[2,128,512]{2,1,0:T(8,128)(2,1)S(1)}, bf16[2,128,512]{2,1,0:T(8,128)(2,1)S(1)}, u32[]{:S(2)}, u32[]{:S(2)}) collective-permute-start(bf16[2,128,512]{2,1,0:T(8,128)(2,1)S(1)} %get-tuple-element.58), channel_id=1, source_target_pairs={{0,2},{2,0},{4,6},{6,4},{8,10},{10,8},{12,14},{14,12},{16,18},{18,... | collective-permute-start | bytes 786440 | tf_op jit(solution)/shard_map/ppermute | solution.py:79
  17.1 6.3 %collective-permute-start.7 = (bf16[2,128,512]{2,1,0:T(8,128)(2,1)S(1)}, bf16[2,128,512]{2,1,0:T(8,128)(2,1)S(1)}, u32[]{:S(2)}, u32[]{:S(2)}) collective-permute-start(bf16[2,128,512]{2,1,0:T(8,128)(2,1)S(1)} %get-tuple-element.59), channel_id=1, source_target_pairs={{0,2},{2,0},{4,6},{6,4},{8,10},{10,8},{12,14},{14,12},{16,18},{18,... | collective-permute-start | bytes 786440 | tf_op jit(solution)/shard_map/ppermute | solution.py:79
  21.2 3.5 %collective-permute-start.12 = (bf16[2,128,512]{2,1,0:T(8,128)(2,1)S(1)}, bf16[2,128,512]{2,1,0:T(8,128)(2,1)S(1)}, u32[]{:S(2)}, u32[]{:S(2)}) collective-permute-start(bf16[2,128,512]{2,1,0:T(8,128)(2,1)S(1)} %collective-permute-done.9.rest_0_), channel_id=1, source_target_pairs={{0,2},{2,0},{4,6},{6,4},{8,10},{10,8},{12,14},{14,12},{16,18},{18,... | collective-permute-start | bytes 786440 | tf_op jit(solution)/shard_map/ppermute | solution.py:79
  22.7 2.1 %collective-permute-start.13 = (bf16[2,128,512]{2,1,0:T(8,128)(2,1)S(1)}, bf16[2,128,512]{2,1,0:T(8,128)(2,1)S(1)}, u32[]{:S(2)}, u32[]{:S(2)}) collective-permute-start(bf16[2,128,512]{2,1,0:T(8,128)(2,1)S(1)} %collective-permute-done.10.rest_1_), channel_id=1, source_target_pairs={{0,2},{2,0},{4,6},{6,4},{8,10},{10,8},{12,14},{14,12},{16,18},{18,... | collective-permute-start | bytes 786440 | tf_op jit(solution)/shard_map/ppermute | solution.py:79
  25.9 5.2 %collective-permute-start.14 = (bf16[2,128,256]{2,1,0:T(8,128)(2,1)S(1)}, bf16[2,128,256]{2,1,0:T(8,128)(2,1)S(1)}, u32[]{:S(2)}, u32[]{:S(2)}) collective-permute-start(bf16[2,128,256]{2,1,0:T(8,128)(2,1)S(1)} %get-tuple-element.70), channel_id=1, source_target_pairs={{0,4},{2,6},{4,0},{6,2},{8,12},{10,14},{12,8},{14,10},{16,20},{18,... | collective-permute-start | bytes 393224 | tf_op jit(solution)/shard_map/ppermute | solution.py:79
  32.4 15.4 %collective-permute-start.15 = (bf16[2,128,1024]{2,1,0:T(8,128)(2,1)S(1)}, bf16[2,128,1024]{2,1,0:T(8,128)(2,1)S(1)}, u32[]{:S(2)}, u32[]{:S(2)}) collective-permute-start(bf16[2,128,1024]{2,1,0:T(8,128)(2,1)S(1)} %collective-permute-done.5.rest_4_.refs_0_), channel_id=1, source_target_pairs={{0,2},{2,0},{4,6},{6,4},{8,10},{10,8},{12,14},{14,12},{16,18},{18,... | collective-permute-start | bytes 1572872 | tf_op jit(solution)/shard_map/ppermute | solution.py:79
  33.4 10.7 %collective-permute-start.22 = (bf16[2,128,768]{2,1,0:T(8,128)(2,1)S(1)}, bf16[2,128,768]{2,1,0:T(8,128)(2,1)S(1)}, u32[]{:S(2)}, u32[]{:S(2)}) collective-permute-start(bf16[2,128,768]{2,1,0:T(8,128)(2,1)S(1)} %shard_map.63.own_ref), channel_id=1, source_target_pairs={{0,4},{2,6},{4,0},{6,2},{8,12},{10,14},{12,8},{14,10},{16,20},{18,... | collective-permute-start | bytes 1179656 | tf_op jit(solution)/shard_map/ppermute | solution.py:79
  34.8 1.8 %collective-permute-start.20 = (bf16[2,128,512]{2,1,0:T(8,128)(2,1)S(1)}, bf16[2,128,512]{2,1,0:T(8,128)(2,1)S(1)}, u32[]{:S(2)}, u32[]{:S(2)}) collective-permute-start(bf16[2,128,512]{2,1,0:T(8,128)(2,1)S(1)} %bitcast.16), channel_id=1, source_target_pairs={{0,2},{2,0},{4,6},{6,4},{8,10},{10,8},{12,14},{14,12},{16,18},{18,... | collective-permute-start | bytes 786440 | tf_op jit(solution)/shard_map/ppermute | solution.py:79
  35.1 2.5 %collective-permute-start.21 = (bf16[2,128,512]{2,1,0:T(8,128)(2,1)S(1)}, bf16[2,128,512]{2,1,0:T(8,128)(2,1)S(1)}, u32[]{:S(2)}, u32[]{:S(2)}) collective-permute-start(bf16[2,128,512]{2,1,0:T(8,128)(2,1)S(1)} %collective-permute-done.11.refs_1_), channel_id=1, source_target_pairs={{0,2},{2,0},{4,6},{6,4},{8,10},{10,8},{12,14},{14,12},{16,18},{18,... | collective-permute-start | bytes 786440 | tf_op jit(solution)/shard_map/ppermute | solution.py:79
  35.3 10.4 %collective-permute-start.23 = (bf16[2,128,768]{2,1,0:T(8,128)(2,1)S(1)}, bf16[2,128,768]{2,1,0:T(8,128)(2,1)S(1)}, u32[]{:S(2)}, u32[]{:S(2)}) collective-permute-start(bf16[2,128,768]{2,1,0:T(8,128)(2,1)S(1)} %shard_map.63.own_ref), channel_id=1, source_target_pairs={{0,1},{1,0},{2,3},{3,2},{4,5},{5,4},{6,7},{7,6},{8,9},{9,8},{10,11... | collective-permute-start | bytes 1179656 | tf_op jit(solution)/shard_map/ppermute | solution.py:86
  36.6 15.5 %collective-permute-start.16 = (bf16[2,64,1024]{2,1,0:T(8,128)(2,1)S(1)}, bf16[2,64,1024]{2,1,0:T(8,128)(2,1)S(1)}, u32[]{:S(2)}, u32[]{:S(2)}) collective-permute-start(bf16[2,64,1024]{2,1,0:T(8,128)(2,1)S(1)} %get-tuple-element.73), channel_id=1, source_target_pairs={{0,1},{1,0},{2,3},{3,2},{4,5},{5,4},{6,7},{7,6},{8,9},{9,8},{10,11... | collective-permute-start | bytes 786440 | tf_op jit(solution)/shard_map/ppermute | solution.py:86
  37.6 19.4 %collective-permute-start.17 = (bf16[2,64,1024]{2,1,0:T(8,128)(2,1)S(1)}, bf16[2,64,1024]{2,1,0:T(8,128)(2,1)S(1)}, u32[]{:S(2)}, u32[]{:S(2)}) collective-permute-start(bf16[2,64,1024]{2,1,0:T(8,128)(2,1)S(1)} %get-tuple-element.75), channel_id=1, source_target_pairs={{0,1},{1,0},{2,3},{3,2},{4,5},{5,4},{6,7},{7,6},{8,9},{9,8},{10,11... | collective-permute-start | bytes 786440 | tf_op jit(solution)/shard_map/ppermute | solution.py:86
  45.8 13.9 %collective-permute-start.24 = (bf16[2,128,768]{2,1,0:T(8,128)(2,1)S(1)}, bf16[2,128,768]{2,1,0:T(8,128)(2,1)S(1)}, u32[]{:S(2)}, u32[]{:S(2)}) collective-permute-start(bf16[2,128,768]{2,1,0:T(8,128)(2,1)S(1)} %collective-permute-done.23.refs_1_), channel_id=1, source_target_pairs={{0,4},{2,6},{4,0},{6,2},{8,12},{10,14},{12,8},{14,10},{16,20},{18,... | collective-permute-start | bytes 1179656 | tf_op jit(solution)/shard_map/ppermute | solution.py:79
  46.2 16.9 %collective-permute-start.25 = (bf16[2,128,1536]{2,1,0:T(8,128)(2,1)S(1)}, bf16[2,128,1536]{2,1,0:T(8,128)(2,1)S(1)}, u32[]{:S(2)}, u32[]{:S(2)}) collective-permute-start(bf16[2,128,1536]{2,1,0:T(8,128)(2,1)S(1)} %shard_map.67.refs_0_), channel_id=1, source_target_pairs={{0,2},{2,0},{4,6},{6,4},{8,10},{10,8},{12,14},{14,12},{16,18},{18,... | collective-permute-start | bytes 2359304 | tf_op jit(solution)/shard_map/ppermute | solution.py:79
  52.1 6.0 %collective-permute-start.18 = (bf16[2,64,1024]{2,1,0:T(8,128)(2,1)S(1)}, bf16[2,64,1024]{2,1,0:T(8,128)(2,1)S(1)}, u32[]{:S(2)}, u32[]{:S(2)}) collective-permute-start(bf16[2,64,1024]{2,1,0:T(8,128)(2,1)S(1)} %collective-permute-done.16.refs_2_), channel_id=1, source_target_pairs={{0,2},{2,0},{4,6},{6,4},{8,10},{10,8},{12,14},{14,12},{16,18},{18,... | collective-permute-start | bytes 786440 | tf_op jit(solution)/shard_map/ppermute | solution.py:79
  57.0 2.3 %collective-permute-start.19 = (bf16[2,64,1024]{2,1,0:T(8,128)(2,1)S(1)}, bf16[2,64,1024]{2,1,0:T(8,128)(2,1)S(1)}, u32[]{:S(2)}, u32[]{:S(2)}) collective-permute-start(bf16[2,64,1024]{2,1,0:T(8,128)(2,1)S(1)} %collective-permute-done.17.refs_3_), channel_id=1, source_target_pairs={{0,2},{2,0},{4,6},{6,4},{8,10},{10,8},{12,14},{14,12},{16,18},{18,... | collective-permute-start | bytes 786440 | tf_op jit(solution)/shard_map/ppermute | solution.py:79
  59.3 3.9 %collective-permute-start.26 = (bf16[2,128,768]{2,1,0:T(8,128)(2,1)S(1)}, bf16[2,128,768]{2,1,0:T(8,128)(2,1)S(1)}, u32[]{:S(2)}, u32[]{:S(2)}) collective-permute-start(bf16[2,128,768]{2,1,0:T(8,128)(2,1)S(1)} %collective-permute-done.23.refs_1_), channel_id=1, source_target_pairs={{0,2},{2,0},{4,6},{6,4},{8,10},{10,8},{12,14},{14,12},{16,18},{18,... | collective-permute-start | bytes 1179656 | tf_op jit(solution)/shard_map/ppermute | solution.py:79
  59.6 3.5 %collective-permute-start.27 = (bf16[2,128,768]{2,1,0:T(8,128)(2,1)S(1)}, bf16[2,128,768]{2,1,0:T(8,128)(2,1)S(1)}, u32[]{:S(2)}, u32[]{:S(2)}) collective-permute-start(bf16[2,128,768]{2,1,0:T(8,128)(2,1)S(1)} %collective-permute-done.24.refs_2_), channel_id=1, source_target_pairs={{0,2},{2,0},{4,6},{6,4},{8,10},{10,8},{12,14},{14,12},{16,18},{18,... | collective-permute-start | bytes 1179656 | tf_op jit(solution)/shard_map/ppermute | solution.py:79
